TPU v7x, 32 devices: a whole 2x2x4 slice. The times are simulated.
32 devices in a mesh: rep: 2 (over core), section: 2 (over y), exp: 8 (over z, x).
Axes of the slice: x: 2, y: 2, z: 4, core: 2. Of those that a mesh axis runs over, the one named last changes fastest.
Arguments:
- row_codes: bfloat16 [2, 1024, 2048], P('section', ('rep', 'exp')), may hold values from -448 to 448
- block_exponents: int32 [2, 1024, 16], P('section', ('rep', 'exp')), may hold values from -10 to -6
- routes: int32 [2, 1024, 8], P('section', ('rep', 'exp')), may hold values from 0 to 15, all different within a row; in each aligned block of 64 rows (0 to 63, 64 to 127, ..., all dimensions but the last counted through in order) at most 48 rows name the same one
- route_weight: float32 [2, 1024, 8], P('section', ('rep', 'exp')), may hold values from 0.02 to 0.3
- out_grad: bfloat16 [2, 1024, 2048], P('section', ('rep', 'exp')), may hold values from -6 to 6
- gate_weight: bfloat16 [2, 16, 384, 2048], P('section', 'exp', 'rep'), may hold values from -0.125 to 0.125
- up_weight: bfloat16 [2, 16, 384, 2048], P('section', 'exp', 'rep'), may hold values from -0.125 to 0.125
- down_weight: bfloat16 [2, 16, 384, 2048], P('section', 'exp', 'rep'), may hold values from -0.3125 to 0.3125
Outputs:
- next_rows: bfloat16 [2, 1024, 2048], P('section', ('rep', 'exp'))
- prev_grads: bfloat16 [2, 1024, 2048], P('section', ('rep', 'exp'))
- gate_weight_grad: bfloat16 [2, 16, 384, 2048], P('section', 'exp', 'rep')
- up_weight_grad: bfloat16 [2, 16, 384, 2048], P('section', 'exp', 'rep')
- down_weight_grad: bfloat16 [2, 16, 384, 2048], P('section', 'exp', 'rep')
Inputs may be any that keep to these rules, and one draw needn't show every extreme that they name: `routes`: the 8 experts of a token differ. In the 64 rows of one device of a layer no expert is named by more than 48 rows, a bound that some of them reach.
All inputs are finite; a program needn't handle non-finite values.
Results may differ from a plain program's by a relative error of at most 0.0065.
Values may be sent and summed in bfloat16 or wider, within the bound.
No kernel may reach another device: no remote copies, remote signals or barrier semaphores. Data moves between devices by JAX's collectives and lax.ppermute only.
A program may use at most 128 MiB of HBM per device.

v0:
```python
import jax
import jax.numpy as jnp
from jax import lax
from jax.sharding import PartitionSpec as P


def from_behind(value, axis, by):
    peers = lax.axis_size(axis)
    return lax.ppermute(value, axis, [(i, (i + by) % peers) for i in range(peers)])


def dequantize(code_rows, exponent_rows):
    dims_of = code_rows.shape
    blocks = code_rows.astype(jnp.float32).reshape(dims_of[:-1] + (dims_of[-1] // 128, 128))
    scales = jnp.exp2(exponent_rows.astype(jnp.float32))[..., None]
    return (blocks * scales).reshape(dims_of).astype(jnp.bfloat16)


def expert_forward(arrived, weights):
    gate_full, up_full, down_full = weights
    gate_act = jnp.einsum("secd,efd->secf", arrived, gate_full, preferred_element_type=jnp.float32)
    up_act = jnp.einsum("secd,efd->secf", arrived, up_full, preferred_element_type=jnp.float32)
    sigmoid_gate = jax.nn.sigmoid(gate_act)
    swish = gate_act * sigmoid_gate
    hidden = (swish * up_act).astype(jnp.bfloat16)
    output = jnp.einsum(
        "secf,efd->secd", hidden, down_full, preferred_element_type=jnp.float32
    ).astype(jnp.bfloat16)
    return (output, (gate_act, up_act, sigmoid_gate, swish, hidden))


def expert_backward(arrived, gated_grad, saved, weights):
    gate_full, up_full, down_full = weights
    gate_act, up_act, sigmoid_gate, swish, hidden = saved
    hidden_grad = jnp.einsum(
        "secd,efd->secf", gated_grad, down_full, preferred_element_type=jnp.float32
    )
    gate_grad = (
        hidden_grad * up_act * sigmoid_gate * (1.0 + gate_act * (1.0 - sigmoid_gate))
    ).astype(jnp.bfloat16)
    up_grad = (hidden_grad * swish).astype(jnp.bfloat16)
    input_grad = (
        jnp.einsum("secf,efd->secd", gate_grad, gate_full, preferred_element_type=jnp.float32)
        + jnp.einsum("secf,efd->secd", up_grad, up_full, preferred_element_type=jnp.float32)
    ).astype(jnp.bfloat16)
    gate_total = jnp.einsum(
        "secf,secd->efd", gate_grad, arrived, preferred_element_type=jnp.float32
    )
    up_total = jnp.einsum("secf,secd->efd", up_grad, arrived, preferred_element_type=jnp.float32)
    down_total = jnp.einsum(
        "secf,secd->efd", hidden, gated_grad, preferred_element_type=jnp.float32
    )
    return (input_grad, gate_total, up_total, down_total)


def shards(
    row_codes, block_exponents, routes, route_weight, out_grad, gate_weight, up_weight, down_weight
):
    token_count = row_codes.shape[1]
    model_width = row_codes.shape[2]
    block_count = block_exponents.shape[2]
    top_count = routes.shape[2]
    groups = lax.axis_size("exp")
    local_experts = gate_weight.shape[1]
    expert_total = groups * local_experts
    assigns = token_count * top_count
    mean_load = assigns // expert_total
    capacity = mean_load + assigns // (2 * expert_total)
    flat_ids = routes[0].reshape(-1)
    one_hot = (flat_ids[:, None] == jnp.arange(expert_total, dtype=jnp.int32)[None, :]).astype(
        jnp.int32
    )
    running = jnp.cumsum(one_hot, axis=0)
    slot_index = jnp.sum(running * one_hot, axis=1) - 1
    place = flat_ids * capacity + slot_index
    source = (
        jnp.full((expert_total * capacity,), assigns, jnp.int32)
        .at[place]
        .set(jnp.arange(assigns, dtype=jnp.int32))
    )
    filled = source < assigns
    safe_source = jnp.minimum(source, assigns - 1)
    token_of = safe_source // top_count
    zero_value = jnp.zeros((), jnp.bfloat16)
    buffer_dims = (groups, local_experts, capacity)
    codes_send = jnp.where(filled[:, None], row_codes[0][token_of], zero_value).reshape(
        buffer_dims + (model_width,)
    )
    exps_send = (
        jnp.where(filled[:, None], block_exponents[0][token_of], 0)
        .astype(jnp.bfloat16)
        .reshape(buffer_dims + (block_count,))
    )
    weight_flat = route_weight[0].reshape(-1)
    gated_send = (
        jnp.where(
            filled[:, None],
            weight_flat[safe_source][:, None] * out_grad[0][token_of].astype(jnp.float32),
            0.0,
        )
        .astype(jnp.bfloat16)
        .reshape(buffer_dims + (model_width,))
    )
    gathered = (
        lax.all_gather(gate_weight, "rep", axis=2, tiled=True),
        lax.all_gather(up_weight, "rep", axis=2, tiled=True),
        lax.all_gather(down_weight, "rep", axis=2, tiled=True),
    )
    weights = (gathered[0][0], gathered[1][0], gathered[2][0])
    codes_in, exps_in = (
        lax.all_to_all(codes_send, "exp", split_axis=0, concat_axis=0, tiled=True),
        lax.all_to_all(exps_send, "exp", split_axis=0, concat_axis=0, tiled=True),
    )
    arrived = dequantize(codes_in, exps_in)
    output, saved = expert_forward(arrived, weights)
    output_back = lax.all_to_all(output, "exp", split_axis=0, concat_axis=0, tiled=True)
    gated_in = lax.all_to_all(gated_send, "exp", split_axis=0, concat_axis=0, tiled=True)
    input_grad, gate_total, up_total, down_total = expert_backward(
        arrived, gated_in, saved, weights
    )
    grad_back = lax.all_to_all(input_grad, "exp", split_axis=0, concat_axis=0, tiled=True)
    per_output = output_back.reshape(expert_total * capacity, model_width)[place].reshape(
        token_count, top_count, model_width
    )
    per_grad = grad_back.reshape(expert_total * capacity, model_width)[place].reshape(
        token_count, top_count, model_width
    )
    home_rows = dequantize(row_codes[0], block_exponents[0])
    layer_out = (
        home_rows.astype(jnp.float32)
        + jnp.sum(route_weight[0][:, :, None] * per_output.astype(jnp.float32), axis=1)
    ).astype(jnp.bfloat16)
    layer_back = (
        out_grad[0].astype(jnp.float32) + jnp.sum(per_grad.astype(jnp.float32), axis=1)
    ).astype(jnp.bfloat16)
    next_rows = from_behind(layer_out[None], "section", 1)
    prev_grads = from_behind(layer_back[None], "section", -1)
    summed = (
        lax.psum_scatter(
            gate_total[None].astype(jnp.bfloat16), "rep", scatter_dimension=2, tiled=True
        ).astype(jnp.float32),
        lax.psum_scatter(
            up_total[None].astype(jnp.bfloat16), "rep", scatter_dimension=2, tiled=True
        ).astype(jnp.float32),
        lax.psum_scatter(
            down_total[None].astype(jnp.bfloat16), "rep", scatter_dimension=2, tiled=True
        ).astype(jnp.float32),
    )
    return (
        next_rows,
        prev_grads,
        summed[0].astype(jnp.bfloat16),
        summed[1].astype(jnp.bfloat16),
        summed[2].astype(jnp.bfloat16),
    )


def solution(mesh):
    return jax.shard_map(
        shards,
        mesh=mesh,
        in_specs=(
            P("section", ("rep", "exp"), None),
            P("section", ("rep", "exp"), None),
            P("section", ("rep", "exp"), None),
            P("section", ("rep", "exp"), None),
            P("section", ("rep", "exp"), None),
            P("section", "exp", "rep", None),
            P("section", "exp", "rep", None),
            P("section", "exp", "rep", None),
        ),
        out_specs=(
            P("section", ("rep", "exp"), None),
            P("section", ("rep", "exp"), None),
            P("section", "exp", "rep", None),
            P("section", "exp", "rep", None),
            P("section", "exp", "rep", None),
        ),
        check_vma=False,
    )
```

profile of v0, /device:TPU:0, one launch (start us, length us, event | category | flops | bytes accessed | tf_op | source)
XLA Modules:
  0.0 375.7 jit_solution(15829424576845240646)
XLA Ops:
  7.2 0.7 broadcast_multiply_fusion
  7.9 0.8 copy.34
  8.7 0.1 eq.25
  8.8 0.1 eq.29
  8.9 0.1 copy.33
  8.9 0.1 mul.91
  9.1 1.2 reduce-window.6
  10.2 0.2 slice_reduce_fusion
  10.5 0.1 fusion.47
  10.6 2.4 scatter_custom_fusion
  13.1 0.8 copy.31
  13.9 1.6 gather_fusion.1
  15.5 0.1 copy.37
  15.6 0.1 broadcast_in_dim.40
  15.7 0.7 reshape.198
  16.5 7.3 %all-to-all-start.1 = ((bf16[8,2,768]{2,1,0:T(2,128)(2,1)}), bf16[8,2,768]{2,1,0:T(2,128)(2,1)S(1)}, u32[]{:S(2)}, u32[]{:S(2)}) async-start(bf16[8,2,768]{2,1,0:T(2,128)(2,1)} %reshape.198), calls=%async_computation.1 | async-start | bytes 49152 | tf_op jit(solution)/shard_map/all_to_all | solution.py:112
  23.7 4.2 %gather_fusion = bf16[768,2048]{1,0:T(8,128)(2,1)} fusion(bf16[64,2048]{1,0:T(8,128)(2,1)S(1)} %bitcast.121, s32[1024]{0:T(1024)S(1)} %get-tuple-element.11), kind=kCustom, calls=%fused_computation | custom fusion | bytes 6294528 | tf_op jit(solution)/shard_map/gather | solution.py:86
  28.0 3.9 %broadcast_select_fusion = bf16[8,2,48,2048]{3,2,1,0:T(8,128)(2,1)} fusion(bf16[8,2,48,2048]{3,2,1,0:T(8,128)(2,1)} %bitcast.125, pred[8,2,48]{2,1,0:T(4,128)(4,1)S(1)} %broadcast_in_dim.40), kind=kLoop, calls=%fused_computation.29 | loop fusion | flops 1572864 | bytes 6292224 | tf_op jit(solution)/shard_map/jit(_where)/select_n | solution.py:86
  31.9 6.0 %all-to-all-start = ((bf16[8,2,48,2048]{3,2,1,0:T(8,128)(2,1)}), bf16[8,2,48,2048]{3,2,1,0:T(8,128)(2,1)}, u32[]{:S(2)}, u32[]{:S(2)}) async-start(bf16[8,2,48,2048]{3,2,1,0:T(8,128)(2,1)} %broadcast_select_fusion), calls=%async_computation | async-start | bytes 6291456 | tf_op jit(solution)/shard_map/all_to_all | solution.py:111
  37.9 0.7 all-gather.4.cloned.1.call-update
  38.6 0.7 all-gather.6.cloned.1.call-update
  39.4 4.2 %gather_fusion.4 = bf16[768,2048]{1,0:T(8,128)(2,1)} fusion(bf16[64,2048]{1,0:T(8,128)(2,1)S(1)} %bitcast.122, s32[1024]{0:T(1024)S(1)} %get-tuple-element.11), kind=kCustom, calls=%fused_computation.4 | custom fusion | bytes 6294528 | tf_op jit(solution)/shard_map/gather | solution.py:98
  43.6 0.1 copy.42
  43.7 0.1 reshape_squeeze.4
  43.8 5.0 %gather_fusion.3 = f32[768]{0:T(1024)S(1)} fusion(f32[512]{0:T(512)S(1)} %reshape_squeeze.4, s32[1024]{0:T(1024)S(1)} %get-tuple-element.10), kind=kCustom, calls=%fused_computation.3 | custom fusion | bytes 9216 | tf_op jit(solution)/shard_map/gather | solution.py:98
  48.9 4.9 %fusion.1 = bf16[8,2,48,2048]{3,2,1,0:T(8,128)(2,1)} fusion(bf16[8,2,48,2048]{3,2,1,0:T(8,128)(2,1)} %bitcast.124, f32[8,2,48]{2,1,0:T(2,128)S(1)} %mul.99, pred[8,2,48]{2,1,0:T(4,128)(4,1)S(1)} %broadcast_in_dim.40), kind=kLoop, calls=%fused_computation.9 | loop fusion | flops 6291456 | bytes 6295296 | tf_op jit(solution)/shard_map/convert_element_type | solution.py:101
  53.7 54.4 %all-to-all-done = bf16[8,2,48,2048]{3,2,1,0:T(8,128)(2,1)} async-done(((bf16[8,2,48,2048]{3,2,1,0:T(8,128)(2,1)}), bf16[8,2,48,2048]{3,2,1,0:T(8,128)(2,1)}, u32[]{:S(2)}, u32[]{:S(2)}) %all-to-all-start) | async-done | bytes 3145760 | tf_op jit(solution)/shard_map/all_to_all | solution.py:111
  108.1 4.5 %all-to-all-start.3 = ((bf16[8,2,48,2048]{3,2,1,0:T(8,128)(2,1)}), bf16[8,2,48,2048]{3,2,1,0:T(8,128)(2,1)}, u32[]{:S(2)}, u32[]{:S(2)}) async-start(bf16[8,2,48,2048]{3,2,1,0:T(8,128)(2,1)} %fusion.1), calls=%async_computation.3 | async-start | bytes 6291456 | tf_op jit(solution)/shard_map/all_to_all | solution.py:117
  112.6 0.7 all-gather.8.cloned.1.call-update
  113.3 0.2 reduce-scatter.4.cloned.1.call-start
  113.6 0.1 reshape.199
  113.7 0.2 copy.38
  113.9 3.8 %mul.93 = f32[8,2,48,16,128]{4,3,2,1,0:T(8,128)} broadcast(f32[8,2,48,16]{3,2,1,0:T(8,128)S(1)} %copy.38), dimensions={0,1,2,3} | broadcast | bytes 6340608 | tf_op jit(solution)/shard_map/mul | solution.py:16
  117.7 7.2 %mul.94 = f32[8,2,48,2048]{3,2,1,0:T(8,128)} reshape(f32[8,2,48,16,128]{4,3,2,1,0:T(8,128)} %mul.93) | data formatting | bytes 12582912 | tf_op jit(solution)/shard_map/mul | solution.py:16
  124.9 7.1 %multiply_convert_fusion = bf16[8,2,48,2048]{3,2,1,0:T(8,128)(2,1)} fusion(f32[8,2,48,2048]{3,2,1,0:T(8,128)} %mul.94, bf16[8,2,48,2048]{3,2,1,0:T(8,128)(2,1)} %all-to-all-done), kind=kLoop, calls=%fused_computation.14 | loop fusion | flops 4718592 | bytes 12582912 | tf_op jit(solution)/shard_map/convert_element_type | solution.py:16
  132.0 4.6 %fusion.33 = f32[8,2,48,384]{3,2,0,1:T(8,128)S(1)} fusion(bf16[1,2,384,2048]{3,2,1,0:T(8,128)(2,1)} %all-gather.4.cloned.1.call-done, bf16[8,2,48,2048]{3,2,1,0:T(8,128)(2,1)} %multiply_convert_fusion), kind=kOutput, calls=%fused_computation.42 | convolution fusion | flops 1207959552 | bytes 7471104 | tf_op jit(solution)/shard_map/secd,efd->secf/dot_general | solution.py:21
  136.7 5.7 %fusion.38 = f32[8,2,48,384]{3,2,0,1:T(8,128)} fusion(bf16[1,2,384,2048]{3,2,1,0:T(8,128)(2,1)} %all-gather.6.cloned.1.call-done, bf16[8,2,48,2048]{3,2,1,0:T(8,128)(2,1)} %multiply_convert_fusion), kind=kOutput, calls=%fused_computation.43 | convolution fusion | flops 1207959552 | bytes 7471104 | tf_op jit(solution)/shard_map/secd,efd->secf/dot_general | solution.py:22
  142.4 40.4 %all-to-all-done.3 = bf16[8,2,48,2048]{3,2,1,0:T(8,128)(2,1)} async-done(((bf16[8,2,48,2048]{3,2,1,0:T(8,128)(2,1)}), bf16[8,2,48,2048]{3,2,1,0:T(8,128)(2,1)}, u32[]{:S(2)}, u32[]{:S(2)}) %all-to-all-start.3) | async-done | bytes 3145760 | tf_op jit(solution)/shard_map/all_to_all | solution.py:117
  182.8 5.4 %multiply_convert_fusion.1 = (bf16[8,2,48,384]{3,2,0,1:T(8,128)(2,1)S(1)}, bf16[8,2,48,384]{3,2,0,1:T(8,128)(2,1)S(1)}, bf16[8,2,48,384]{3,2,0,1:T(8,128)(2,1)S(1)}) fusion(f32[8,2,48,384]{3,2,0,1:T(8,128)S(1)} %fusion.33, f32[8,2,48,384]{3,2,0,1:T(8,128)} %fusion.38, bf16[1,2,384,2048]{3,2,1,0:T(8,128)(2,1)} %all-gather.8.cloned.1.call-done, ...), kind=kOutput, calls=%fused_computation.44 | convolution fusion | flops 1212383232 | bytes 10420224 | tf_op jit(solution)/shard_map/secd,efd->secf/dot_general | solution.py:35
  188.2 3.5 fusion.16
  191.8 5.5 %fusion.17 = bf16[1,2,384,2048]{3,2,1,0:T(8,128)(2,1)} fusion(bf16[8,2,48,384]{3,2,0,1:T(8,128)(2,1)S(1)} %get-tuple-element.5, bf16[8,2,48,2048]{3,2,1,0:T(8,128)(2,1)} %multiply_convert_fusion), kind=kOutput, calls=%fused_computation.32 | convolution fusion | flops 1209532416 | bytes 6881280 | tf_op jit(solution)/shard_map/secf,secd->efd/dot_general | solution.py:49
  197.3 4.0 %fusion.19 = bf16[8,2,48,2048]{3,2,0,1:T(8,128)(2,1)S(1)} fusion(bf16[8,2,48,384]{3,2,0,1:T(8,128)(2,1)S(1)} %get-tuple-element.7, bf16[1,2,384,2048]{3,2,1,0:T(8,128)(2,1)} %all-gather.8.cloned.1.call-done), kind=kOutput, calls=%fused_computation.34 | convolution fusion | flops 1209532416 | bytes 6881280 | tf_op jit(solution)/shard_map/secf,efd->secd/dot_general | solution.py:26
  201.3 2.1 copy.41
  203.4 4.7 %all-to-all-start.2 = ((bf16[8,2,48,2048]{3,2,1,0:T(8,128)(2,1)}), bf16[8,2,48,2048]{3,2,1,0:T(8,128)(2,1)}, u32[]{:S(2)}, u32[]{:S(2)}) async-start(bf16[8,2,48,2048]{3,2,1,0:T(8,128)(2,1)} %copy.41), calls=%async_computation.2 | async-start | bytes 6291456 | tf_op jit(solution)/shard_map/all_to_all | solution.py:116
  208.0 3.8 %fusion.6 = f32[2,8,48,2048]{3,2,1,0:T(8,128)S(1)} fusion(bf16[8,2,48,384]{3,2,0,1:T(8,128)(2,1)S(1)} %get-tuple-element.6, bf16[1,2,384,2048]{3,2,1,0:T(8,128)(2,1)} %all-gather.4.cloned.1.call-done), kind=kOutput, calls=%fused_computation.22 | convolution fusion | flops 1207959552 | bytes 10027008 | tf_op jit(solution)/shard_map/secf,efd->secd/dot_general | solution.py:43
  211.9 1.8 fusion.13
  213.7 2.0 copy.44
  215.8 62.5 %all-to-all-done.2 = bf16[8,2,48,2048]{3,2,1,0:T(8,128)(2,1)} async-done(((bf16[8,2,48,2048]{3,2,1,0:T(8,128)(2,1)}), bf16[8,2,48,2048]{3,2,1,0:T(8,128)(2,1)}, u32[]{:S(2)}, u32[]{:S(2)}) %all-to-all-start.2) | async-done | bytes 3145760 | tf_op jit(solution)/shard_map/all_to_all | solution.py:116
  278.3 4.4 %all-to-all-start.4 = ((bf16[8,2,48,2048]{3,2,1,0:T(8,128)(2,1)}), bf16[8,2,48,2048]{3,2,1,0:T(8,128)(2,1)}, u32[]{:S(2)}, u32[]{:S(2)}) async-start(bf16[8,2,48,2048]{3,2,1,0:T(8,128)(2,1)} %copy.44), calls=%async_computation.4 | async-start | bytes 6291456 | tf_op jit(solution)/shard_map/all_to_all | solution.py:121
  282.8 5.4 %fusion.18 = bf16[1,2,384,2048]{3,2,1,0:T(8,128)(2,1)} fusion(bf16[8,2,48,384]{3,2,0,1:T(8,128)(2,1)S(1)} %get-tuple-element.7, bf16[8,2,48,2048]{3,2,1,0:T(8,128)(2,1)} %all-to-all-done.3), kind=kOutput, calls=%fused_computation.33 | convolution fusion | flops 1209532416 | bytes 6881280 | tf_op jit(solution)/shard_map/secf,secd->efd/dot_general | solution.py:50
  288.2 0.1 copy.32
  288.3 0.2 mul.84
  288.5 0.1 mul.85
  288.6 6.7 %gather_fusion.2 = bf16[512,2048]{1,0:T(8,128)(2,1)S(1)} fusion(bf16[768,2048]{1,0:T(8,128)(2,1)} %bitcast.20, s32[1024]{0:T(1024)S(1)} %pad_clamp_fusion.1), kind=kCustom, calls=%fused_computation.2 | custom fusion | bytes 4196352 | tf_op jit(solution)/shard_map/gather | solution.py:122
  295.3 1.8 fusion.2
  297.2 0.1 fusion.45
  297.3 1.6 collective-permute-start
  298.9 53.9 %all-to-all-done.4 = bf16[8,2,48,2048]{3,2,1,0:T(8,128)(2,1)} async-done(((bf16[8,2,48,2048]{3,2,1,0:T(8,128)(2,1)}), bf16[8,2,48,2048]{3,2,1,0:T(8,128)(2,1)}, u32[]{:S(2)}, u32[]{:S(2)}) %all-to-all-start.4) | async-done | bytes 3145760 | tf_op jit(solution)/shard_map/all_to_all | solution.py:121
  352.8 6.7 %gather_fusion.5 = bf16[512,2048]{1,0:T(8,128)(2,1)S(1)} fusion(bf16[768,2048]{1,0:T(8,128)(2,1)} %bitcast.30, s32[1024]{0:T(1024)S(1)} %pad_clamp_fusion.1), kind=kCustom, calls=%fused_computation.5 | custom fusion | bytes 4196352 | tf_op jit(solution)/shard_map/gather | solution.py:125
  359.5 1.4 convert_reduce_fusion
  361.0 1.6 collective-permute-start.1
  362.6 4.8 %collective-permute-done.1 = bf16[1,64,2048]{2,1,0:T(8,128)(2,1)S(1)} collective-permute-done((bf16[1,64,2048]{2,1,0:T(8,128)(2,1)S(1)}, bf16[1,64,2048]{2,1,0:T(8,128)(2,1)S(1)}, u32[]{:S(2)}, u32[]{:S(2)}) %collective-permute-start.1) | collective-permute-done | bytes 262176 | tf_op jit(solution)/shard_map/ppermute | solution.py:9
  367.4 0.7 copy.78
  368.1 0.7 copy.79
  (41 shorter events, 0.6 us)
Async XLA Ops:
  7.2 16.6 %copy-start = (bf16[1,64,2048]{2,1,0:T(8,128)(2,1)S(1)}, bf16[1,64,2048]{2,1,0:T(8,128)(2,1)}, u32[]{:S(2)}) copy-start(bf16[1,64,2048]{2,1,0:T(8,128)(2,1)} %param.8) | copy-start | bytes 786436
  16.5 15.4 %all-to-all-start.1 = ((bf16[8,2,768]{2,1,0:T(2,128)(2,1)}), bf16[8,2,768]{2,1,0:T(2,128)(2,1)S(1)}, u32[]{:S(2)}, u32[]{:S(2)}) async-start(bf16[8,2,768]{2,1,0:T(2,128)(2,1)} %reshape.198), calls=%async_computation.1 | async-start | bytes 49152 | tf_op jit(solution)/shard_map/all_to_all | solution.py:112
  31.9 76.2 %all-to-all-start = ((bf16[8,2,48,2048]{3,2,1,0:T(8,128)(2,1)}), bf16[8,2,48,2048]{3,2,1,0:T(8,128)(2,1)}, u32[]{:S(2)}, u32[]{:S(2)}) async-start(bf16[8,2,48,2048]{3,2,1,0:T(8,128)(2,1)} %broadcast_select_fusion), calls=%async_computation | async-start | bytes 6291456 | tf_op jit(solution)/shard_map/all_to_all | solution.py:111
  37.9 1.5 copy-start.1
  37.9 94.2 %all-gather.4.cloned.1.call-start = ((), (), s32[]{:S(2)}) async-start(), calls=%async_computation.8 | async-start | bytes 4718592 | tf_op jit(solution)/shard_map/all_gather | solution.py:105
  38.6 98.1 %all-gather.6.cloned.1.call-start = ((), (), s32[]{:S(2)}) async-start(), calls=%async_computation.9 | async-start | bytes 4718592 | tf_op jit(solution)/shard_map/all_gather | solution.py:106
  39.4 4.3 %copy-start.4 = (f32[1,64,8]{1,2,0:T(8,128)S(1)}, f32[1,64,8]{1,2,0:T(8,128)}, u32[]{:S(2)}) copy-start(f32[1,64,8]{1,2,0:T(8,128)} %param.11) | copy-start | bytes 6148
  108.1 74.7 %all-to-all-start.3 = ((bf16[8,2,48,2048]{3,2,1,0:T(8,128)(2,1)}), bf16[8,2,48,2048]{3,2,1,0:T(8,128)(2,1)}, u32[]{:S(2)}, u32[]{:S(2)}) async-start(bf16[8,2,48,2048]{3,2,1,0:T(8,128)(2,1)} %fusion.1), calls=%async_computation.3 | async-start | bytes 6291456 | tf_op jit(solution)/shard_map/all_to_all | solution.py:117
  112.6 29.8 %all-gather.8.cloned.1.call-start = ((), (), s32[]{:S(2)}) async-start(), calls=%async_computation.10 | async-start | bytes 4718592 | tf_op jit(solution)/shard_map/all_gather | solution.py:107
  113.3 254.1 %reduce-scatter.4.cloned.1.call-start = ((), (), s32[]{:S(2)}) async-start(), calls=%async_computation.11 | async-start | bytes 4718592 | tf_op jit(solution)/shard_map/reduce_scatter | solution.py:139
  182.8 5.4 %copy-start.3 = (bf16[8,2,48,2048]{3,2,1,0:T(8,128)(2,1)S(1)}, bf16[8,2,48,2048]{3,2,1,0:T(8,128)(2,1)}, u32[]{:S(2)}) copy-start(bf16[8,2,48,2048]{3,2,1,0:T(8,128)(2,1)} %multiply_convert_fusion) | copy-start | bytes 9437188
  191.7 175.7 %reduce-scatter.6.cloned.1.call-start = ((), (), s32[]{:S(2)}) async-start(), calls=%async_computation.12 | async-start | bytes 4718592 | tf_op jit(solution)/shard_map/reduce_scatter | solution.py:142
  203.4 74.9 %all-to-all-start.2 = ((bf16[8,2,48,2048]{3,2,1,0:T(8,128)(2,1)}), bf16[8,2,48,2048]{3,2,1,0:T(8,128)(2,1)}, u32[]{:S(2)}, u32[]{:S(2)}) async-start(bf16[8,2,48,2048]{3,2,1,0:T(8,128)(2,1)} %copy.41), calls=%async_computation.2 | async-start | bytes 6291456 | tf_op jit(solution)/shard_map/all_to_all | solution.py:116
  208.0 3.8 %copy-start.2 = (bf16[1,2,384,2048]{3,2,1,0:T(8,128)(2,1)S(1)}, bf16[1,2,384,2048]{3,2,1,0:T(8,128)(2,1)}, u32[]{:S(2)}) copy-start(bf16[1,2,384,2048]{3,2,1,0:T(8,128)(2,1)} %all-gather.6.cloned.1.call-done) | copy-start | bytes 9437188
  278.3 74.5 %all-to-all-start.4 = ((bf16[8,2,48,2048]{3,2,1,0:T(8,128)(2,1)}), bf16[8,2,48,2048]{3,2,1,0:T(8,128)(2,1)}, u32[]{:S(2)}, u32[]{:S(2)}) async-start(bf16[8,2,48,2048]{3,2,1,0:T(8,128)(2,1)} %copy.44), calls=%async_computation.4 | async-start | bytes 6291456 | tf_op jit(solution)/shard_map/all_to_all | solution.py:121
  282.7 84.7 %reduce-scatter.8.cloned.1.call-start = ((), (), s32[]{:S(2)}) async-start(), calls=%async_computation.13 | async-start | bytes 4718592 | tf_op jit(solution)/shard_map/reduce_scatter | solution.py:145
  297.3 65.3 %collective-permute-start = (bf16[1,64,2048]{2,1,0:T(8,128)(2,1)S(1)}, bf16[1,64,2048]{2,1,0:T(8,128)(2,1)S(1)}, u32[]{:S(2)}, u32[]{:S(2)}) collective-permute-start(bf16[1,64,2048]{2,1,0:T(8,128)(2,1)S(1)} %fusion.45), channel_id=1, source_target_pairs={{0,8},{8,0},{1,9},{9,1},{2,10},{10,2},{3,11},{11,3},{4,12},{12,4},... | collective-permute-start | bytes 786440 | tf_op jit(solution)/shard_map/ppermute | solution.py:9
  361.0 6.4 %collective-permute-start.1 = (bf16[1,64,2048]{2,1,0:T(8,128)(2,1)S(1)}, bf16[1,64,2048]{2,1,0:T(8,128)(2,1)S(1)}, u32[]{:S(2)}, u32[]{:S(2)}) collective-permute-start(bf16[1,64,2048]{2,1,0:T(8,128)(2,1)S(1)} %fusion.44), channel_id=1, source_target_pairs={{0,8},{8,0},{1,9},{9,1},{2,10},{10,2},{3,11},{11,3},{4,12},{12,4},... | collective-permute-start | bytes 786440 | tf_op jit(solution)/shard_map/ppermute | solution.py:9
Sparse Core Ops, SparseCore 0:
  40.2 13.5 all-gather.3
  55.4 13.2 all-gather.5
  115.0 13.4 all-gather.7
  191.9 9.9 reduce-scatter.3
  204.6 12.0 reduce-scatter.5
  288.3 12.2 reduce-scatter.7
where the time goes:
time: 377 us; the launch traced here: 376 us
  waiting for transfers between devices  218 us (58%)
  local copies, waits for them, and re-layouts  51.5 us (14%)
  matrix products  39.7 us (11%)
  starting transfers between devices  30.5 us (8%)
  other arithmetic  21.4 us (6%)
  between operations  14.4 us (4%)
    all_to_all x1, waiting for transfers between devices, shards(): lax.all_to_all(output, 'exp', split_axis=0, concat_axis=0, tiled=True)  62.5 us
    all_to_all x1, waiting for transfers between devices, shards(): lax.all_to_all(codes_send, 'exp', split_axis=0, concat_axis=0, tiled=True)  54.4 us
    all_to_all x1, waiting for transfers between devices, shards(): lax.all_to_all(input_grad, 'exp', split_axis=0, concat_axis=0, tiled=True)  53.9 us
    all_to_all x1, waiting for transfers between devices, shards(): lax.all_to_all(gated_send, 'exp', split_axis=0, concat_axis=0, tiled=True)  40.4 us
    mul x4, local copies, waits for them, and re-layouts, dequantize(): return (blocks * scales).reshape(dims_of).astype(jnp.bfloat16)  11.3 us
  transfers between devices with their start and end apart: 13, of which 5 were waited for; matrix products, arithmetic and copies ran while one was open for 25% of the time, Pallas kernels for 0%

commit v1 on v0

v1 whole, which is shorter than its diff:
```python
import jax
import jax.numpy as jnp
from jax import lax
from jax.sharding import PartitionSpec as P


def from_behind(value, axis, by):
    peers = lax.axis_size(axis)
    return lax.ppermute(value, axis, [(i, (i + by) % peers) for i in range(peers)])


def dequantize(code_rows, exponent_rows):
    scales = jnp.exp2(exponent_rows.astype(jnp.float32))
    scales = jnp.repeat(scales, code_rows.shape[-1] // exponent_rows.shape[-1], axis=-1)
    return (code_rows.astype(jnp.float32) * scales).astype(jnp.bfloat16)


def dot(a, b, dims):
    return lax.dot_general(a, b, (dims, ((), ())), preferred_element_type=jnp.float32)


def shards(
    row_codes, block_exponents, routes, route_weight, out_grad, gate_weight, up_weight, down_weight
):
    token_count, model_width = row_codes.shape[1:]
    local_experts, half_units = gate_weight.shape[1:3]
    units = half_units * lax.axis_size("rep")
    experts = lax.axis_size("exp") * local_experts
    home_rows = dequantize(row_codes[0], block_exponents[0])
    table = jnp.sum(
        jnp.where(
            routes[0][:, :, None] == jnp.arange(experts, dtype=jnp.int32)[None, None, :],
            route_weight[0][:, :, None],
            0.0,
        ),
        axis=1,
    )
    rows = lax.all_gather(home_rows, "exp", axis=0, tiled=True)
    all_tables = lax.all_gather(table, "exp", axis=0, tiled=True)
    weights = [
        lax.all_gather(w[0], "rep", axis=1, tiled=True).reshape(local_experts * units, model_width)
        for w in (gate_weight, up_weight, down_weight)
    ]
    gate_full, up_full, down_full = weights
    grads = lax.all_gather(out_grad[0], "exp", axis=0, tiled=True)
    mine = lax.dynamic_slice_in_dim(
        all_tables, lax.axis_index("exp") * local_experts, local_experts, axis=1
    )
    scale = jnp.repeat(mine, units, axis=1)
    last, first = ((1,), (1,)), ((0,), (0,))
    gate_act = dot(rows, gate_full, last)
    up_act = dot(rows, up_full, last)
    sigmoid_gate = jax.nn.sigmoid(gate_act)
    swish = gate_act * sigmoid_gate
    hidden = (swish * up_act * scale).astype(jnp.bfloat16)
    output = dot(hidden, down_full, ((1,), (0,))).astype(jnp.bfloat16)
    output_sum = lax.psum_scatter(output, "exp", scatter_dimension=0, tiled=True)
    hidden_grad = dot(grads, down_full, last) * scale
    gate_grad = (
        hidden_grad * up_act * sigmoid_gate * (1.0 + gate_act * (1.0 - sigmoid_gate))
    ).astype(jnp.bfloat16)
    up_grad = (hidden_grad * swish).astype(jnp.bfloat16)
    input_grad = (
        dot(gate_grad, gate_full, ((1,), (0,))) + dot(up_grad, up_full, ((1,), (0,)))
    ).astype(jnp.bfloat16)
    input_sum = lax.psum_scatter(input_grad, "exp", scatter_dimension=0, tiled=True)
    shape = (1, local_experts, units, model_width)
    totals = [
        lax.psum_scatter(
            dot(a, b, first).astype(jnp.bfloat16).reshape(shape),
            "rep",
            scatter_dimension=2,
            tiled=True,
        )
        for a, b in ((gate_grad, rows), (up_grad, rows), (hidden, grads))
    ]
    layer_out = (home_rows.astype(jnp.float32) + output_sum.astype(jnp.float32)).astype(jnp.bfloat16)
    layer_back = (out_grad[0].astype(jnp.float32) + input_sum.astype(jnp.float32)).astype(
        jnp.bfloat16
    )
    next_rows = from_behind(layer_out[None], "section", 1)
    prev_grads = from_behind(layer_back[None], "section", -1)
    return (next_rows, prev_grads, totals[0], totals[1], totals[2])


def solution(mesh):
    tokens = P("section", ("rep", "exp"), None)
    weights = P("section", "exp", "rep", None)
    return jax.shard_map(
        shards,
        mesh=mesh,
        in_specs=(tokens,) * 5 + (weights,) * 3,
        out_specs=(tokens,) * 2 + (weights,) * 3,
        check_vma=False,
    )
```

time: 377 us -> 355 us (0.942)
  local copies, waits for them, and re-layouts: 51.5 us -> 7.66 us
  waiting for transfers between devices: 218 us -> 257 us
  blocking collectives: 0 us -> 32.4 us
  starting transfers between devices: 30.5 us -> 3.68 us
  other arithmetic: 21.4 us -> 3.64 us
    all_to_all x5 -> x0, waiting for transfers between devices: 211 us -> none  [the longest x1 62.5 us: shards(): lax.all_to_all(output, 'exp', split_axis=0, concat_axis=0, tiled=True)]
    reduce_scatter x3 -> x5, waiting for transfers between devices: 0.01 us -> 147 us  [the longest x1 67.5 us: shards(): lax.psum_scatter(input_grad, 'exp', scatter_dimension=0, tiled=True)]
    all_gather x3 -> x5, waiting for transfers between devices: 0.02 us -> 102 us  [the longest x1 52.5 us: shards(): grads = lax.all_gather(out_grad[0], 'exp', axis=0, tiled=True)]
    all_gather x0 -> x1, blocking collectives: none -> 32.4 us  [shards(): all_tables = lax.all_gather(table, 'exp', axis=0, tiled=True)]
    gather x7 -> x0, local copies, waits for them, and re-layouts: 28.6 us -> none  [the longest x1 6.7 us: shards(): output_back.reshape(expert_total * capacity, model_width)[place]]
    all_to_all x5 -> x0, starting transfers between devices: 26.8 us -> none  [the longest x1 7.25 us: shards(): lax.all_to_all(exps_send, 'exp', split_axis=0, concat_axis=0, tiled=True)]
    mul x8 -> x0, local copies, waits for them, and re-layouts: 11.7 us -> none  [the longest x4 11.3 us: dequantize(): return (blocks * scales).reshape(dims_of).astype(jnp.bfloat16)]
    convert_element_type x5 -> x1, other arithmetic: 12.1 us -> 0.89 us  [dequantize(): return (code_rows.astype(jnp.float32) * scales).astype(jnp.bfloat16)]
  transfers between devices with their start and end apart: 13 -> 12, of which waited for: 5 -> 10; matrix products, arithmetic and copies ran while one was open for 25% -> 9% of each run, Pallas kernels for 0% -> 0%
where the time goes in v1:
time: 355 us
  waiting for transfers between devices  257 us (72%)
  matrix products  36.5 us (10%)
  blocking collectives  32.4 us (9%)
  between operations  14.3 us (4%)
  local copies, waits for them, and re-layouts  7.66 us (2%)
  starting transfers between devices  3.68 us (1%)
  other arithmetic  3.64 us (1%)
    reduce_scatter x1, waiting for transfers between devices, shards(): lax.psum_scatter(input_grad, 'exp', scatter_dimension=0, tiled=True)  67.5 us
    all_gather x1, waiting for transfers between devices, shards(): grads = lax.all_gather(out_grad[0], 'exp', axis=0, tiled=True)  52.5 us
    reduce_scatter x1, waiting for transfers between devices, shards(): lax.psum_scatter(output, 'exp', scatter_dimension=0, tiled=True)  44.8 us
    dot_general x9, matrix products, dot(): lax.dot_general(a, b, (dims, ((), ())), preferred_element_type=jnp.float32)  36.5 us
    reduce_scatter x3, waiting for transfers between devices, shards(): lax.psum_scatter(dot(a, b, first).astype(jnp.bfloat16).reshape(shape), 'r...  35.1 us
    all_gather x1, waiting for transfers between devices, shards(): rows = lax.all_gather(home_rows, 'exp', axis=0, tiled=True)  32.5 us
    all_gather x1, blocking collectives, shards(): all_tables = lax.all_gather(table, 'exp', axis=0, tiled=True)  32.4 us
    all_gather x3, waiting for transfers between devices, shards(): lax.all_gather(w[0], 'rep', axis=1, tiled=True)  17.1 us
  transfers between devices with their start and end apart: 12, of which 10 were waited for; matrix products, arithmetic and copies ran while one was open for 9% of the time, Pallas kernels for 0%

profile of v1, /device:TPU:0, one launch (start us, length us, event | category | flops | bytes accessed | tf_op | source)
XLA Modules:
  0.0 355.0 jit_solution(635339150714821790)
XLA Ops:
  7.2 0.0 all-gather.15.cloned.1.call-start
  7.2 0.7 all-gather.15.cloned.1.call-update
  7.9 0.0 all-gather.11.cloned.1.call-start
  8.0 0.7 exponential_bitcast_fusion
  8.7 0.1 copy.24
  8.7 0.2 broadcast_in_dim.27
  9.0 0.9 fusion.7
  9.9 0.0 all-gather.11.cloned.1.call-update
  9.9 0.0 all-gather.13.cloned.1.call-start
  9.9 0.7 all-gather.13.cloned.1.call-update
  10.6 0.0 all-gather.17.cloned.1.call-start
  10.7 0.5 all-gather.17.cloned.1.call-update
  11.2 0.0 all-gather.19.cloned.1.call-start
  11.2 0.5 all-gather.19.cloned.1.call-update
  11.8 0.0 reduce-scatter.6.cloned.1.call-start
  11.9 32.4 %all-gather.4 = f32[8,64,16]{1,2,0:T(8,128)S(1)} all-gather(f32[1,64,16]{1,2,0:T(8,128)S(1)} %bitcast.61), channel_id=1, replica_groups=mesh['rep'=2,'section'=2,'exp'=8] {'exp'}, dimensions={0}, use_global_device_ids=true | all-gather | bytes 36864 | tf_op jit(solution)/shard_map/all_gather | solution.py:39
  44.3 0.1 reshape.60
  44.4 0.1 copy.26
  44.5 0.6 broadcast_in_dim.31
  45.1 0.1 copy.28
  45.2 0.0 all-gather.15.cloned.1.call-done
  45.3 32.5 %all-gather.11.cloned.1.call-done = bf16[512,2048]{1,0:T(8,128)(2,1)} async-done(((bf16[64,2048]{1,0:T(8,128)(2,1)}), bf16[512,2048]{1,0:T(8,128)(2,1)}) %all-gather.11.cloned.1.call-update) | async-done | bytes 2097168 | tf_op jit(solution)/shard_map/all_gather | solution.py:38
  77.8 4.3 %fusion.12 = f32[512,768]{1,0:T(8,128)S(1)} fusion(bf16[512,2048]{1,0:T(8,128)(2,1)} %all-gather.11.cloned.1.call-done, bf16[768,2048]{1,0:T(8,128)(2,1)} %bitcast.64), kind=kOutput, calls=%fused_computation.26 | convolution fusion | flops 1610612736 | bytes 6815744 | tf_op jit(solution)/shard_map/dot_general | solution.py:19
  82.1 7.8 %all-gather.13.cloned.1.call-done = bf16[1,2,384,2048]{3,2,1,0:T(8,128)(2,1)} async-done(((bf16[1,2,192,2048]{3,2,1,0:T(8,128)(2,1)}), bf16[1,2,384,2048]{3,2,1,0:T(8,128)(2,1)}) %all-gather.13.cloned.1.call-update) | async-done | bytes 3145744 | tf_op jit(solution)/shard_map/all_gather | solution.py:41
  90.0 5.5 %fusion.11 = f32[512,768]{1,0:T(8,128)} fusion(bf16[512,2048]{1,0:T(8,128)(2,1)} %all-gather.11.cloned.1.call-done, bf16[768,2048]{1,0:T(8,128)(2,1)} %bitcast.66), kind=kOutput, calls=%fused_computation.25 | convolution fusion | flops 1610612736 | bytes 6815744 | tf_op jit(solution)/shard_map/dot_general | solution.py:19
  95.5 9.2 %all-gather.17.cloned.1.call-done = bf16[1,2,384,2048]{3,2,1,0:T(8,128)(2,1)} async-done(((bf16[1,2,192,2048]{3,2,1,0:T(8,128)(2,1)}), bf16[1,2,384,2048]{3,2,1,0:T(8,128)(2,1)}) %all-gather.17.cloned.1.call-update) | async-done | bytes 3145744 | tf_op jit(solution)/shard_map/all_gather | solution.py:41
  104.7 52.5 %all-gather.19.cloned.1.call-done = bf16[1,512,2048]{2,1,0:T(8,128)(2,1)} async-done(((bf16[1,64,2048]{2,1,0:T(8,128)(2,1)}), bf16[1,512,2048]{2,1,0:T(8,128)(2,1)}) %all-gather.19.cloned.1.call-update) | async-done | bytes 2097168 | tf_op jit(solution)/shard_map/all_gather | solution.py:45
  157.2 6.7 %multiply_convert_fusion = (bf16[512,768]{1,0:T(8,128)(2,1)}, bf16[512,768]{1,0:T(8,128)(2,1)}, bf16[512,768]{1,0:T(8,128)(2,1)S(1)}) fusion(f32[512,768]{1,0:T(8,128)} %fusion.11, f32[512,768]{1,0:T(8,128)S(1)} %fusion.12, f32[512,768]{1,0:T(8,128)S(1)} %bitcast.60, bf16[768,2048]{1,0:T(8,128)(2,1)} %bitcast.68, ...), kind=kOutput, calls=%fused_computation.8 | convolution fusion | flops 1617297408 | bytes 12320768 | tf_op jit(solution)/shard_map/dot_general | solution.py:19
  163.9 0.9 copy-done.13
  164.7 0.0 copy-done.7
  164.7 3.1 convolution_convert_fusion.3
  167.8 0.0 reduce-scatter.6.cloned.1.call-update
  167.9 0.0 reduce-scatter.8.cloned.1.call-start
  167.9 0.0 copy-start.10
  167.9 3.1 fusion.13
  171.0 0.0 copy-start.14
  171.1 3.2 add_convert_fusion
  174.2 0.0 reduce-scatter.8.cloned.1.call-update
  174.3 0.2 reduce-scatter.14.cloned.1.call-start
  174.5 1.3 copy-done.9
  175.8 3.6 %convolution_convert_fusion = bf16[768,2048]{1,0:T(8,128)(2,1)} fusion(bf16[512,768]{1,0:T(8,128)(2,1)S(1)} %copy-done.14, bf16[1,512,2048]{2,1,0:T(8,128)(2,1)S(1)} %copy-done.9), kind=kOutput, calls=%fused_computation.1 | convolution fusion | flops 1612185600 | bytes 6029312 | tf_op jit(solution)/shard_map/dot_general | solution.py:19
  179.4 0.0 reduce-scatter.14.cloned.1.call-update
  179.4 0.0 reduce-scatter.12.cloned.1.call-start
  179.5 1.5 copy-done.8
  181.0 0.2 copy-done.11
  181.2 3.5 convolution_convert_fusion.1
  184.6 0.0 reduce-scatter.12.cloned.1.call-update
  184.7 0.0 reduce-scatter.10.cloned.1.call-start
  184.7 1.1 copy-done.12
  185.8 3.6 %convolution_convert_fusion.2 = bf16[768,2048]{1,0:T(8,128)(2,1)} fusion(bf16[512,768]{1,0:T(8,128)(2,1)S(1)} %copy-done.12, bf16[512,2048]{1,0:T(8,128)(2,1)S(1)} %copy-done.8), kind=kOutput, calls=%fused_computation.3 | convolution fusion | flops 1612185600 | bytes 6029312 | tf_op jit(solution)/shard_map/dot_general | solution.py:19
  189.3 0.0 reduce-scatter.10.cloned.1.call-update
  189.4 44.8 %reduce-scatter.6.cloned.1.call-done = bf16[64,2048]{1,0:T(8,128)(2,1)} async-done(((bf16[512,2048]{1,0:T(8,128)(2,1)}), bf16[64,2048]{1,0:T(8,128)(2,1)}) %reduce-scatter.6.cloned.1.call-update) | async-done | bytes 262160 | tf_op jit(solution)/shard_map/reduce_scatter | solution.py:57
  234.2 1.0 fusion.9
  235.2 1.5 collective-permute-start
  236.8 67.5 %reduce-scatter.8.cloned.1.call-done = bf16[64,2048]{1,0:T(8,128)(2,1)} async-done(((bf16[512,2048]{1,0:T(8,128)(2,1)}), bf16[64,2048]{1,0:T(8,128)(2,1)}) %reduce-scatter.8.cloned.1.call-update) | async-done | bytes 262160 | tf_op jit(solution)/shard_map/reduce_scatter | solution.py:66
  304.2 1.0 fusion.10
  305.3 1.6 collective-permute-start.1
  306.8 0.0 collective-permute-done
  306.8 4.9 %collective-permute-done.1 = bf16[1,64,2048]{2,1,0:T(8,128)(2,1)S(1)} collective-permute-done((bf16[1,64,2048]{2,1,0:T(8,128)(2,1)S(1)}, bf16[1,64,2048]{2,1,0:T(8,128)(2,1)S(1)}, u32[]{:S(2)}, u32[]{:S(2)}) %collective-permute-start.1) | collective-permute-done | bytes 262176 | tf_op jit(solution)/shard_map/ppermute | solution.py:9
  311.7 5.3 %reduce-scatter.14.cloned.1.call-done = bf16[1,2,192,2048]{3,2,1,0:T(8,128)(2,1)} async-done(((bf16[1,2,384,2048]{3,2,1,0:T(8,128)(2,1)}), bf16[1,2,192,2048]{3,2,1,0:T(8,128)(2,1)}) %reduce-scatter.14.cloned.1.call-update) | async-done | bytes 1572880 | tf_op jit(solution)/shard_map/reduce_scatter | solution.py:69
  317.0 15.0 %reduce-scatter.12.cloned.1.call-done = bf16[1,2,192,2048]{3,2,1,0:T(8,128)(2,1)} async-done(((bf16[1,2,384,2048]{3,2,1,0:T(8,128)(2,1)}), bf16[1,2,192,2048]{3,2,1,0:T(8,128)(2,1)}) %reduce-scatter.12.cloned.1.call-update) | async-done | bytes 1572880 | tf_op jit(solution)/shard_map/reduce_scatter | solution.py:69
  332.0 14.7 %reduce-scatter.10.cloned.1.call-done = bf16[1,2,192,2048]{3,2,1,0:T(8,128)(2,1)} async-done(((bf16[1,2,384,2048]{3,2,1,0:T(8,128)(2,1)}), bf16[1,2,192,2048]{3,2,1,0:T(8,128)(2,1)}) %reduce-scatter.10.cloned.1.call-update) | async-done | bytes 1572880 | tf_op jit(solution)/shard_map/reduce_scatter | solution.py:69
  346.8 0.7 copy.32
  347.5 0.7 copy.33
  (25 shorter events, 0.1 us)
Async XLA Ops:
  7.2 1.8 copy-start.2
  7.2 38.1 %all-gather.15.cloned.1.call-start = ((), (), s32[]{:S(2)}) async-start(), calls=%async_computation.12 | async-start | bytes 4718592 | tf_op jit(solution)/shard_map/all_gather | solution.py:41
  7.9 69.9 %all-gather.11.cloned.1.call-start = ((), (), s32[]{:S(2)}) async-start(), calls=%async_computation.5 | async-start | bytes 2359296 | tf_op jit(solution)/shard_map/all_gather | solution.py:38
  9.8 2.0 copy-start.3
  9.8 2.0 copy-start.4
  9.9 80.1 %all-gather.13.cloned.1.call-start = ((), (), s32[]{:S(2)}) async-start(), calls=%async_computation.11 | async-start | bytes 4718592 | tf_op jit(solution)/shard_map/all_gather | solution.py:41
  10.6 94.1 %all-gather.17.cloned.1.call-start = ((), (), s32[]{:S(2)}) async-start(), calls=%async_computation.13 | async-start | bytes 4718592 | tf_op jit(solution)/shard_map/all_gather | solution.py:41
  11.2 146.0 %all-gather.19.cloned.1.call-start = ((), (), s32[]{:S(2)}) async-start(), calls=%async_computation.14 | async-start | bytes 2359296 | tf_op jit(solution)/shard_map/all_gather | solution.py:45
  11.8 222.4 %reduce-scatter.6.cloned.1.call-start = ((), (), s32[]{:S(2)}) async-start(), calls=%async_computation.6 | async-start | bytes 2359296 | tf_op jit(solution)/shard_map/reduce_scatter | solution.py:57
  157.2 7.6 %copy-start.7 = (bf16[1,2,384,2048]{3,2,1,0:T(8,128)(2,1)S(1)}, bf16[1,2,384,2048]{3,2,1,0:T(8,128)(2,1)}, u32[]{:S(2)}) copy-start(bf16[1,2,384,2048]{3,2,1,0:T(8,128)(2,1)} %all-gather.17.cloned.1.call-done) | copy-start | bytes 9437188
  163.8 0.9 copy-start.13
  164.7 3.2 copy-start.6
  167.9 136.4 %reduce-scatter.8.cloned.1.call-start = ((), (), s32[]{:S(2)}) async-start(), calls=%async_computation.7 | async-start | bytes 2359296 | tf_op jit(solution)/shard_map/reduce_scatter | solution.py:66
  167.9 3.1 copy-start.5
  167.9 3.1 copy-start.10
  171.0 3.4 copy-start.14
  174.2 1.6 copy-start.9
  174.3 142.8 %reduce-scatter.14.cloned.1.call-start = ((), (), s32[]{:S(2)}) async-start(), calls=%async_computation.10 | async-start | bytes 4718592 | tf_op jit(solution)/shard_map/reduce_scatter | solution.py:69
  179.4 1.6 copy-start.8
  179.4 1.8 copy-start.11
  179.4 152.6 %reduce-scatter.12.cloned.1.call-start = ((), (), s32[]{:S(2)}) async-start(), calls=%async_computation.9 | async-start | bytes 4718592 | tf_op jit(solution)/shard_map/reduce_scatter | solution.py:69
  184.6 1.1 copy-start.12
  184.7 162.1 %reduce-scatter.10.cloned.1.call-start = ((), (), s32[]{:S(2)}) async-start(), calls=%async_computation.8 | async-start | bytes 4718592 | tf_op jit(solution)/shard_map/reduce_scatter | solution.py:69
  189.3 44.9 %copy-start = (bf16[64,2048]{1,0:T(8,128)(2,1)S(1)}, bf16[64,2048]{1,0:T(8,128)(2,1)}, u32[]{:S(2)}) copy-start(bf16[64,2048]{1,0:T(8,128)(2,1)} %fusion.7) | copy-start | bytes 786436
  189.3 114.9 %copy-start.1 = (bf16[1,64,2048]{2,1,0:T(8,128)(2,1)S(1)}, bf16[1,64,2048]{2,1,0:T(8,128)(2,1)}, u32[]{:S(2)}) copy-start(bf16[1,64,2048]{2,1,0:T(8,128)(2,1)} %param.12) | copy-start | bytes 786436
  235.2 71.6 %collective-permute-start = (bf16[1,64,2048]{2,1,0:T(8,128)(2,1)S(1)}, bf16[1,64,2048]{2,1,0:T(8,128)(2,1)S(1)}, u32[]{:S(2)}, u32[]{:S(2)}) collective-permute-start(bf16[1,64,2048]{2,1,0:T(8,128)(2,1)S(1)} %fusion.9), channel_id=1, source_target_pairs={{0,8},{8,0},{1,9},{9,1},{2,10},{10,2},{3,11},{11,3},{4,12},{12,4},... | collective-permute-start | bytes 786440 | tf_op jit(solution)/shard_map/ppermute | solution.py:9
  305.3 6.4 %collective-permute-start.1 = (bf16[1,64,2048]{2,1,0:T(8,128)(2,1)S(1)}, bf16[1,64,2048]{2,1,0:T(8,128)(2,1)S(1)}, u32[]{:S(2)}, u32[]{:S(2)}) collective-permute-start(bf16[1,64,2048]{2,1,0:T(8,128)(2,1)S(1)} %fusion.10), channel_id=1, source_target_pairs={{0,8},{8,0},{1,9},{9,1},{2,10},{10,2},{3,11},{11,3},{4,12},{12,4},... | collective-permute-start | bytes 786440 | tf_op jit(solution)/shard_map/ppermute | solution.py:9
Sparse Core Ops, SparseCore 0:
  9.6 14.8 all-gather.14
  27.1 50.6 all-gather.10
  79.3 10.6 all-gather.12
  91.4 13.2 all-gather.16
  106.7 50.4 all-gather.18
  168.0 66.1 reduce-scatter.5
  237.7 66.4 reduce-scatter.7
  307.1 9.9 reduce-scatter.13
  319.9 12.0 reduce-scatter.11
  334.7 12.0 reduce-scatter.9

commit v2 on v1

v2 whole, which is shorter than its diff:
```python
import functools
import jax
import jax.numpy as jnp
from jax import lax
from jax.experimental import pallas as pl
from jax.experimental.pallas import tpu as pltpu
from jax.sharding import PartitionSpec as P

F32 = jnp.float32
BF16 = jnp.bfloat16
VMEM_BYTES = 40 * 2**20


def ring_order(peers):
    width = 1
    while 8 * width * width <= peers:
        width *= 2
    depth = peers // width
    if width == 1 or depth % 2:
        return list(range(peers))
    order = [z * width for z in range(depth)]
    for back, z in enumerate(reversed(range(depth))):
        columns = list(range(1, width))
        order += [z * width + x for x in (columns if back % 2 == 0 else reversed(columns))]
    return order


def ring_shift(value, by):
    peers = lax.axis_size("exp")
    order = ring_order(peers)
    pairs = []
    for rep in range(lax.axis_size("rep")):
        step = by if rep % 2 == 0 else -by
        for spot in range(peers):
            pairs.append((rep * peers + order[spot], rep * peers + order[(spot + step) % peers]))
    return lax.ppermute(value, ("rep", "exp"), pairs)


def from_behind(value, axis, by):
    peers = lax.axis_size(axis)
    return lax.ppermute(value, axis, [(i, (i + by) % peers) for i in range(peers)])


def dot(a, b, dims):
    return lax.dot_general(a, b, (dims, ((), ())), preferred_element_type=F32)


def whole():
    return pl.BlockSpec(memory_space=pltpu.VMEM)


def turned(value):
    rows, columns = value.shape
    wide = jnp.concatenate([value, jnp.zeros((rows, 128 - columns), F32)], axis=1)
    return wide.T[:columns]


def pack_kernel(experts, codes_ref, exps_ref, routes_ref, weight_ref, grad_ref, out_ref):
    tokens, width = codes_ref.shape
    blocks = exps_ref.shape[0]
    scales = jnp.exp2(exps_ref[...].astype(F32))
    scales = turned(jnp.concatenate([scales, jnp.zeros((128 - blocks, tokens), F32)], axis=0))
    per = width // blocks
    for b in range(blocks):
        cols = slice(b * per, (b + 1) * per)
        out_ref[:, cols] = (codes_ref[:, cols].astype(F32) * scales[:, b : b + 1]).astype(BF16)
    out_ref[:, width : 2 * width] = grad_ref[...]
    expert = lax.broadcasted_iota(jnp.int32, (experts, tokens), 0)
    table = jnp.zeros((experts, tokens), F32)
    for k in range(routes_ref.shape[0]):
        table += jnp.where(routes_ref[k : k + 1, :] == expert, weight_ref[k : k + 1, :], 0.0)
    high = table.astype(BF16).astype(F32)
    middle = (table - high).astype(BF16).astype(F32)
    low = table - high - middle
    extra = out_ref.shape[1] - 2 * width
    parts = [high, middle, low]
    if extra > 3 * experts:
        parts.append(jnp.zeros((extra - 3 * experts, tokens), F32))
    out_ref[:, 2 * width :] = turned(jnp.concatenate(parts, axis=0)).astype(BF16)


def expert_kernel(count, experts, local_experts, width, first_ref, *refs):
    blocks = refs[:count]
    weights = refs[count : count + 6]
    outs = refs[count + 6 : 2 * count + 6]
    gate_out, up_out, hidden_out, buffer, rows, sems = refs[2 * count + 6 :]
    half = weights[0].shape[0]
    units = 2 * half
    copies = []
    for i in range(6):
        kind, side = divmod(i, 2)
        copies.append(
            pltpu.make_async_copy(
                weights[side * 3 + kind], buffer.at[kind, pl.ds(side * half, half)], sems.at[i]
            )
        )
    for copy in copies:
        copy.start()
    tokens = blocks[0].shape[0]
    lanes = blocks[0].shape[1] - 2 * width
    scales = []
    lane = lax.broadcasted_iota(jnp.int32, (tokens, lanes), 1)
    expert_of = lax.rem(lane, experts)
    for i, block in enumerate(blocks):
        rows[0, i * tokens : (i + 1) * tokens, :] = block[:, :width]
        rows[1, i * tokens : (i + 1) * tokens, :] = block[:, width : 2 * width]
        table = block[:, 2 * width :].astype(F32)
        scales.append(
            [
                jnp.sum(
                    jnp.where(expert_of == first_ref[0] + e, table, 0.0), axis=1, keepdims=True
                )
                for e in range(local_experts)
            ]
        )
    scales = [
        jnp.concatenate([s[e] for s in scales], axis=0) for e in range(local_experts)
    ]
    for copy in copies:
        copy.wait()
    tile = 256
    last = ((1,), (1,))
    plain = ((1,), (0,))

    def hidden_tile(j, carry):
        at = pl.ds(pl.multiple_of(j * tile, tile), tile)
        gate = dot(rows[0], buffer[0, at, :], last)
        up = dot(rows[0], buffer[1, at, :], last)
        back = dot(rows[1], buffer[2, at, :], last)
        unit = lax.rem(j * tile + lax.broadcasted_iota(jnp.int32, (1, tile), 1), half)
        scale = jnp.broadcast_to(scales[0], gate.shape)
        for e in range(1, local_experts):
            scale = jnp.where(unit >= e * (half // local_experts), scales[e], scale)
        sig = 1.0 / (1.0 + jnp.exp(-gate))
        swish = gate * sig
        back = back * scale
        hidden_out[:, at] = (swish * up * scale).astype(BF16)
        gate_out[:, at] = (back * up * sig * (1.0 + gate * (1.0 - sig))).astype(BF16)
        up_out[:, at] = (back * swish).astype(BF16)
        return carry

    lax.fori_loop(0, units // tile, hidden_tile, 0)

    def column_tile(n, carry):
        at = pl.ds(pl.multiple_of(n * tile, tile), tile)
        later = pl.ds(pl.multiple_of(width + n * tile, tile), tile)
        output = dot(hidden_out[...], buffer[2, :, at], plain).astype(BF16)
        grad = (
            dot(gate_out[...], buffer[0, :, at], plain) + dot(up_out[...], buffer[1, :, at], plain)
        ).astype(BF16)
        for i, out in enumerate(outs):
            out[:, at] = output[i * tokens : (i + 1) * tokens]
            out[:, later] = grad[i * tokens : (i + 1) * tokens]
        return carry

    lax.fori_loop(0, width // tile, column_tile, 0)


def expert_call(blocks, weights, first, experts, local_experts, width):
    count = len(blocks)
    tokens = blocks[0].shape[0]
    half = weights[0].shape[0]
    rows = count * tokens
    saved = jax.ShapeDtypeStruct((rows, 2 * half), BF16)
    results = pl.pallas_call(
        functools.partial(expert_kernel, count, experts, local_experts, width),
        out_shape=[jax.ShapeDtypeStruct((tokens, 2 * width), BF16)] * count + [saved] * 3,
        in_specs=[pl.BlockSpec(memory_space=pltpu.SMEM)]
        + [whole()] * count
        + [pl.BlockSpec(memory_space=pl.ANY)] * 6,
        out_specs=[whole()] * (count + 3),
        scratch_shapes=[
            pltpu.VMEM((3, 2 * half, width), BF16),
            pltpu.VMEM((2, rows, width), BF16),
            pltpu.SemaphoreType.DMA((6,)),
        ],
        compiler_params=pltpu.CompilerParams(vmem_limit_bytes=VMEM_BYTES),
        cost_estimate=pl.CostEstimate(
            flops=6 * 2 * rows * 2 * half * width,
            bytes_accessed=12 * half * width + 8 * rows * width,
            transcendentals=rows * 2 * half,
        ),
        name="expert_rows",
    )(first, *blocks, *weights)
    return results[:count], results[count:]


def weight_kernel(groups, count, has_received, *refs):
    rows = refs[:count]
    grads = refs[count : 2 * count]
    refs = refs[2 * count :]
    saved = [refs[g * 3 : g * 3 + 3] for g in range(groups)]
    refs = refs[groups * 3 :]
    received = refs[:3] if has_received else None
    outs = refs[-4:-1]
    across = refs[-1]

    @pl.when(pl.program_id(0) == 0)
    def _():
        for kind in range(3):
            start = 0
            for group in saved:
                size = group[kind].shape[0]
                across[kind, :, start : start + size] = group[kind][...].T
                start += size

    right = [
        jnp.concatenate([r[...] for r in rows], axis=0),
        jnp.concatenate([r[...] for r in grads], axis=0),
    ]
    for kind in range(3):
        total = dot(across[kind], right[kind // 2], ((1,), (0,)))
        if has_received:
            total = total + received[kind][...].astype(F32)
        outs[kind][...] = total.astype(BF16)


def weight_call(blocks, saved, side, received, width):
    tokens = blocks[0].shape[0]
    count = len(blocks)
    half = saved[0][0].shape[1] // 2
    tile = 256
    steps = width // tile
    block = lambda offset: pl.BlockSpec((tokens, tile), lambda n: (0, n + offset))
    column = pl.BlockSpec((half, tile), lambda n: (0, n))
    total = tokens * count
    specs = [block(0)] * count + [block(steps)] * count
    args = list(blocks) * 2
    for group in saved:
        specs += [pl.BlockSpec((g.shape[0], half), lambda n: (0, side)) for g in group]
        args += list(group)
    if received is not None:
        specs += [column] * 3
        args += list(received)
    return pl.pallas_call(
        functools.partial(weight_kernel, len(saved), count, received is not None),
        grid=(steps,),
        out_shape=[jax.ShapeDtypeStruct((half, width), BF16)] * 3,
        in_specs=specs,
        out_specs=[column] * 3,
        scratch_shapes=[pltpu.VMEM((3, half, total), BF16)],
        compiler_params=pltpu.CompilerParams(vmem_limit_bytes=VMEM_BYTES),
        cost_estimate=pl.CostEstimate(
            flops=3 * 2 * total * half * width,
            bytes_accessed=4 * total * width + 12 * half * width,
            transcendentals=0,
        ),
        name="weight_grads",
    )(*args)


def add(a, b):
    return (a.astype(F32) + b.astype(F32)).astype(BF16)


def shards(
    row_codes, block_exponents, routes, route_weight, out_grad, gate_weight, up_weight, down_weight
):
    tokens, width = row_codes.shape[1:]
    local_experts, half_units = gate_weight.shape[1:3]
    half = local_experts * half_units
    peers = lax.axis_size("exp")
    experts = peers * local_experts
    lanes = -(-3 * experts // 128) * 128
    own = [w.reshape(half, width) for w in (gate_weight, up_weight, down_weight)]
    other = [from_behind(w, "rep", 1) for w in own]
    weights = own + other
    first = (lax.axis_index("exp") * local_experts).astype(jnp.int32).reshape(1)
    home = pl.pallas_call(
        functools.partial(pack_kernel, experts),
        out_shape=jax.ShapeDtypeStruct((tokens, 2 * width + lanes), BF16),
        in_specs=[whole()] * 5,
        out_specs=whole(),
        name="pack_rows",
    )(row_codes[0], block_exponents[0].T, routes[0].T, route_weight[0].T, out_grad[0])

    ahead, behind = peers // 2, peers // 2 - 1
    near, far = [home], [home]
    arrived = [("home", 0, home)]
    for k in range(1, ahead + 1):
        near.append(ring_shift(near[-1], 1))
        arrived.append(("near", k, near[k]))
        if k <= behind:
            far.append(ring_shift(far[-1], -1))
            arrived.append(("far", k, far[k]))
    groups = [arrived[i : i + 4] for i in range(0, len(arrived) - 1, 4)]
    if len(groups[-1]) > 1 and groups[-1][-1] is arrived[-1]:
        groups[-1] = groups[-1][:-1]
    groups.append(arrived[-1:])
    partial, saved = {}, []
    for group in groups:
        outs, kept = expert_call(
            [g[2] for g in group], weights, first, experts, local_experts, width
        )
        saved.append(kept)
        for (name, k, _), out in zip(group, outs):
            partial[name, k] = out

    blocks = [g[2] for group in groups for g in group]
    given = weight_call(blocks, saved, 1, None, width)
    received = [from_behind(g, "rep", 1) for g in given]

    near_sum, far_sum = partial["near", ahead], partial["far", behind] if behind else None
    for k in range(ahead, 0, -1):
        near_sum = ring_shift(near_sum, -1)
        if k > 1:
            near_sum = add(near_sum, partial["near", k - 1])
        if k <= behind:
            far_sum = ring_shift(far_sum, 1)
            if k > 1:
                far_sum = add(far_sum, partial["far", k - 1])
    total = home[:, : 2 * width].astype(F32) + partial["home", 0].astype(F32)
    total = total + near_sum.astype(F32)
    if behind:
        total = total + far_sum.astype(F32)
    total = total.astype(BF16)
    next_rows = from_behind(total[None, :, :width], "section", 1)
    prev_grads = from_behind(total[None, :, width:], "section", -1)
    totals = weight_call(blocks, saved, 0, received, width)
    shape = (1, local_experts, half_units, width)
    return (next_rows, prev_grads) + tuple(t.reshape(shape) for t in totals)


def solution(mesh):
    tokens = P("section", ("rep", "exp"), None)
    weights = P("section", "exp", "rep", None)
    return jax.shard_map(
        shards,
        mesh=mesh,
        in_specs=(tokens,) * 5 + (weights,) * 3,
        out_specs=(tokens,) * 2 + (weights,) * 3,
        check_vma=False,
    )
```

time: 355 us -> 145 us (0.41)
  waiting for transfers between devices: 257 us -> 61.4 us
  Pallas kernels: 0 us -> 50.1 us
  matrix products: 36.5 us -> 0 us
  blocking collectives: 32.4 us -> 0 us
  starting transfers between devices: 3.68 us -> 26.2 us
  between operations: 14.3 us -> 0.74 us
    reduce_scatter x5 -> x0, waiting for transfers between devices: 147 us -> none  [the longest x1 67.5 us: shards(): lax.psum_scatter(input_grad, 'exp', scatter_dimension=0, tiled=True)]
    all_gather x5 -> x0, waiting for transfers between devices: 102 us -> none  [the longest x1 52.5 us: shards(): grads = lax.all_gather(out_grad[0], 'exp', axis=0, tiled=True)]
    ppermute x0 -> x14, waiting for transfers between devices: none -> 56.6 us  [ring_shift(): return lax.ppermute(value, ('rep', 'exp'), pairs)]
    pallas_call x0 -> x6, Pallas kernels: none -> 50.1 us  [the longest x3 27.9 us: expert_call(): pl.pallas_call(functools.partial(expert_kernel, count, experts, local_exp...]
    dot_general x9 -> x0, matrix products: 36.5 us -> none  [dot(): lax.dot_general(a, b, (dims, ((), ())), preferred_element_type=jnp.float32)]
    all_gather x1 -> x0, blocking collectives: 32.4 us -> none  [shards(): all_tables = lax.all_gather(table, 'exp', axis=0, tiled=True)]
    ppermute x0 -> x14, starting transfers between devices: none -> 22.8 us  [ring_shift(): return lax.ppermute(value, ('rep', 'exp'), pairs)]
  transfers between devices with their start and end apart: 12 -> 22, of which waited for: 10 -> 10; matrix products, arithmetic and copies ran while one was open for 9% -> 1% of each run, Pallas kernels for 0% -> 33%
where the time goes in v2:
time: 145 us
  waiting for transfers between devices  61.4 us (42%)
  Pallas kernels  50.1 us (35%)
  starting transfers between devices  26.2 us (18%)
  local copies, waits for them, and re-layouts  5.67 us (4%)
    ppermute x14, waiting for transfers between devices, ring_shift(): return lax.ppermute(value, ('rep', 'exp'), pairs)  56.6 us
    pallas_call x3, Pallas kernels, expert_call(): pl.pallas_call(functools.partial(expert_kernel, count, experts, local_exp...  27.9 us
    ppermute x14, starting transfers between devices, ring_shift(): return lax.ppermute(value, ('rep', 'exp'), pairs)  22.8 us
    pallas_call x2, Pallas kernels, weight_call(): pl.pallas_call(functools.partial(weight_kernel, len(saved), count, receiv...  19.9 us
    unnamed x10, local copies, waits for them, and re-layouts  5.63 us
    ppermute x8, waiting for transfers between devices, from_behind(): lax.ppermute(value, axis, [(i, (i + by) % peers) for i in range(peers)])  4.77 us
    ppermute x8, starting transfers between devices, from_behind(): lax.ppermute(value, axis, [(i, (i + by) % peers) for i in range(peers)])  3.4 us
  transfers between devices with their start and end apart: 22, of which 10 were waited for; matrix products, arithmetic and copies ran while one was open for 1% of the time, Pallas kernels for 33%

profile of v2, /device:TPU:0, one launch (start us, length us, event | category | flops | bytes accessed | tf_op | source)
XLA Modules:
  0.0 145.0 jit_solution(18005413896407385829)
XLA Ops:
  0.6 2.2 %pack_rows.1.refs_0_.refs_8_ = bf16[64,4224]{1,0:T(8,128)(2,1)} custom-call(bf16[64,2048]{1,0:T(8,128)(2,1)} %bitcast.34, s32[16,64]{1,0:T(8,128)} %bitcast.36, s32[8,64]{1,0:T(8,128)} %bitcast.37, f32[8,64]{1,0:T(8,128)} %bitcast.38, bf16[64,2048]{1,0:T(8,128)(2,1)} %bitcast.35), custom_call_target="tpu_custom_call" | custom-call | tf_op jit(solution)/shard_map/pack_rows/pallas_call | solution.py:269
  2.8 3.0 %collective-permute-start = (bf16[64,4224]{1,0:T(8,128)(2,1)}, bf16[64,4224]{1,0:T(8,128)(2,1)S(1)}, u32[]{:S(2)}, u32[]{:S(2)}) collective-permute-start(bf16[64,4224]{1,0:T(8,128)(2,1)} %pack_rows.1.refs_0_.refs_8_), channel_id=1, source_target_pairs={{0,2},{2,4},{4,6},{6,7},{7,5},{5,3},{3,1},{1,0},{16,17},{18,16},{2... | collective-permute-start | bytes 1622024 | tf_op jit(solution)/shard_map/ppermute | solution.py:36
  5.9 7.5 %collective-permute-done.refs_1_.refs_9_ = bf16[64,4224]{1,0:T(8,128)(2,1)S(1)} collective-permute-done((bf16[64,4224]{1,0:T(8,128)(2,1)}, bf16[64,4224]{1,0:T(8,128)(2,1)S(1)}, u32[]{:S(2)}, u32[]{:S(2)}) %collective-permute-start) | collective-permute-done | bytes 540704 | tf_op jit(solution)/shard_map/ppermute | solution.py:36
  13.3 2.1 %collective-permute-start.2 = (bf16[64,4224]{1,0:T(8,128)(2,1)S(1)}, bf16[64,4224]{1,0:T(8,128)(2,1)S(1)}, u32[]{:S(2)}, u32[]{:S(2)}) collective-permute-start(bf16[64,4224]{1,0:T(8,128)(2,1)S(1)} %collective-permute-done.refs_1_.refs_9_), channel_id=1, source_target_pairs={{0,2},{2,4},{4,6},{6,7},{7,5},{5,3},{3,1},{1,0},{16,17},{18,16},{2... | collective-permute-start | bytes 1622024 | tf_op jit(solution)/shard_map/ppermute | solution.py:36
  15.4 0.0 collective-permute-start.3
  15.4 0.5 collective-permute-start.4
  15.9 0.0 collective-permute-start.5
  15.9 0.2 collective-permute-start.1
  16.1 10.1 %collective-permute-done.2.refs_3_.refs_11_ = bf16[64,4224]{1,0:T(8,128)(2,1)S(1)} collective-permute-done((bf16[64,4224]{1,0:T(8,128)(2,1)S(1)}, bf16[64,4224]{1,0:T(8,128)(2,1)S(1)}, u32[]{:S(2)}, u32[]{:S(2)}) %collective-permute-start.2) | collective-permute-done | bytes 540704 | tf_op jit(solution)/shard_map/ppermute | solution.py:36
  26.2 2.5 %collective-permute-start.6 = (bf16[64,4224]{1,0:T(8,128)(2,1)S(1)}, bf16[64,4224]{1,0:T(8,128)(2,1)S(1)}, u32[]{:S(2)}, u32[]{:S(2)}) collective-permute-start(bf16[64,4224]{1,0:T(8,128)(2,1)S(1)} %collective-permute-done.2.refs_3_.refs_11_), channel_id=1, source_target_pairs={{0,2},{2,4},{4,6},{6,7},{7,5},{5,3},{3,1},{1,0},{16,17},{18,16},{2... | collective-permute-start | bytes 1622024 | tf_op jit(solution)/shard_map/ppermute | solution.py:36
  28.7 0.0 collective-permute-done.1.refs_2_.refs_10_
  28.7 1.3 collective-permute-start.9
  30.0 12.7 %collective-permute-done.6.refs_1_.refs_5_.refs_13_ = bf16[64,4224]{1,0:T(8,128)(2,1)S(1)} collective-permute-done((bf16[64,4224]{1,0:T(8,128)(2,1)S(1)}, bf16[64,4224]{1,0:T(8,128)(2,1)S(1)}, u32[]{:S(2)}, u32[]{:S(2)}) %collective-permute-start.6) | collective-permute-done | bytes 540704 | tf_op jit(solution)/shard_map/ppermute | solution.py:36
  42.8 0.3 collective-permute-start.7
  43.1 0.0 collective-permute-done.9.refs_0_.refs_4_.refs_12_
  43.1 1.7 %collective-permute-start.10 = (bf16[64,4224]{1,0:T(8,128)(2,1)S(1)}, bf16[64,4224]{1,0:T(8,128)(2,1)S(1)}, u32[]{:S(2)}, u32[]{:S(2)}) collective-permute-start(bf16[64,4224]{1,0:T(8,128)(2,1)S(1)} %collective-permute-done.9.refs_0_.refs_4_.refs_12_), channel_id=1, source_target_pairs={{0,1},{2,0},{4,2},{6,4},{7,6},{5,7},{3,5},{1,3},{16,18},{18,20},{2... | collective-permute-start | bytes 1622024 | tf_op jit(solution)/shard_map/ppermute | solution.py:36
  44.8 0.0 collective-permute-done.3.refs_7_.refs_4_.refs_6_
  44.8 0.0 collective-permute-done.4.refs_8_.refs_5_.refs_7_
  44.8 0.0 collective-permute-done.5.refs_9_.refs_6_.refs_8_
  44.8 12.0 %collective-permute-done.7.refs_0_.refs_7_.refs_15_ = bf16[64,4224]{1,0:T(8,128)(2,1)S(1)} collective-permute-done((bf16[64,4224]{1,0:T(8,128)(2,1)S(1)}, bf16[64,4224]{1,0:T(8,128)(2,1)S(1)}, u32[]{:S(2)}, u32[]{:S(2)}) %collective-permute-start.7) | collective-permute-done | bytes 540704 | tf_op jit(solution)/shard_map/ppermute | solution.py:36
  56.8 0.0 copy-start.1
  56.8 1.4 copy-done.1
  58.2 0.0 copy-start.2
  58.2 1.4 copy-done.2
  59.6 1.4 copy-done.3
  61.0 8.7 %expert_rows.4 = (bf16[64,4096]{1,0:T(8,128)(2,1)S(1)}, bf16[64,768]{1,0:T(8,128)(2,1)S(1)}, bf16[64,768]{1,0:T(8,128)(2,1)S(1)}, bf16[64,768]{1,0:T(8,128)(2,1)S(1)}) custom-call(s32[1]{0:T(128)} %bitcast.8.first_ref, bf16[64,4224]{1,0:T(8,128)(2,1)S(1)} %collective-permute-done.7.refs_0_.refs_7_.refs_15_, bf16[384,2048]{1,0:T(8,128)(2,1)S(1)} %bitcast.23, ...), custom_call_target="tpu_custom_call" | custom-call | flops 1207959552 | bytes 10485760 | tf_op jit(solution)/shard_map/expert_rows/pallas_call | solution.py:165
  69.7 1.5 %collective-permute-start.8 = (bf16[64,4096]{1,0:T(8,128)(2,1)S(1)}, bf16[64,4096]{1,0:T(8,128)(2,1)S(1)}, u32[]{:S(2)}, u32[]{:S(2)}) collective-permute-start(bf16[64,4096]{1,0:T(8,128)(2,1)S(1)} %get-tuple-element.29), channel_id=1, source_target_pairs={{0,1},{2,0},{4,2},{6,4},{7,6},{5,7},{3,5},{1,3},{16,18},{18,20},{2... | collective-permute-start | bytes 1572872 | tf_op jit(solution)/shard_map/ppermute | solution.py:36
  71.2 0.0 copy-done
  71.2 9.6 %expert_rows.3 = (bf16[64,4096]{1,0:T(8,128)(2,1)S(1)}, bf16[64,4096]{1,0:T(8,128)(2,1)S(1)}, bf16[64,4096]{1,0:T(8,128)(2,1)S(1)}, bf16[64,4096]{1,0:T(8,128)(2...) custom-call(s32[1]{0:T(128)} %bitcast.8.first_ref, ...), custom_call_target="tpu_custom_call" | custom-call | flops 4831838208 | bytes 13631488 | tf_op jit(solution)/shard_map/expert_rows/pallas_call | solution.py:165
  80.9 0.0 collective-permute-done.10.refs_2_.refs_6_.refs_14_
  80.9 9.6 %expert_rows.5 = (bf16[64,4096]{1,0:T(8,128)(2,1)S(1)}, bf16[64,4096]{1,0:T(8,128)(2,1)S(1)}, bf16[64,4096]{1,0:T(8,128)(2,1)S(1)}, bf16[192,768]{1,0:T(8,128)(2...) custom-call(s32[1]{0:T(128)} %bitcast.8.first_ref, ...), custom_call_target="tpu_custom_call" | custom-call | flops 3623878656 | bytes 12582912 | tf_op jit(solution)/shard_map/expert_rows/pallas_call | solution.py:165
  90.5 0.6 collective-permute-start.14
  91.1 0.0 collective-permute-done.8
  91.1 0.1 add_convert_fusion.5
  91.2 1.5 %collective-permute-start.11 = (bf16[64,4096]{1,0:T(8,128)(2,1)S(1)}, bf16[64,4096]{1,0:T(8,128)(2,1)S(1)}, u32[]{:S(2)}, u32[]{:S(2)}) collective-permute-start(bf16[64,4096]{1,0:T(8,128)(2,1)S(1)} %add_convert_fusion.5), channel_id=1, source_target_pairs={{0,1},{2,0},{4,2},{6,4},{7,6},{5,7},{3,5},{1,3},{16,18},{18,20},{2... | collective-permute-start | bytes 1572872 | tf_op jit(solution)/shard_map/ppermute | solution.py:36
  92.8 8.7 %collective-permute-done.14 = bf16[64,4096]{1,0:T(8,128)(2,1)S(1)} collective-permute-done((bf16[64,4096]{1,0:T(8,128)(2,1)S(1)}, bf16[64,4096]{1,0:T(8,128)(2,1)S(1)}, u32[]{:S(2)}, u32[]{:S(2)}) %collective-permute-start.14) | collective-permute-done | bytes 524320 | tf_op jit(solution)/shard_map/ppermute | solution.py:36
  101.5 0.1 add_convert_fusion.2
  101.6 1.6 %collective-permute-start.15 = (bf16[64,4096]{1,0:T(8,128)(2,1)S(1)}, bf16[64,4096]{1,0:T(8,128)(2,1)S(1)}, u32[]{:S(2)}, u32[]{:S(2)}) collective-permute-start(bf16[64,4096]{1,0:T(8,128)(2,1)S(1)} %add_convert_fusion.2), channel_id=1, source_target_pairs={{0,2},{2,4},{4,6},{6,7},{7,5},{5,3},{3,1},{1,0},{16,17},{18,16},{2... | collective-permute-start | bytes 1572872 | tf_op jit(solution)/shard_map/ppermute | solution.py:36
  103.2 0.5 collective-permute-done.11
  103.6 0.1 add_convert_fusion.4
  103.8 2.5 %collective-permute-start.12 = (bf16[64,4096]{1,0:T(8,128)(2,1)S(1)}, bf16[64,4096]{1,0:T(8,128)(2,1)S(1)}, u32[]{:S(2)}, u32[]{:S(2)}) collective-permute-start(bf16[64,4096]{1,0:T(8,128)(2,1)S(1)} %add_convert_fusion.4), channel_id=1, source_target_pairs={{0,1},{2,0},{4,2},{6,4},{7,6},{5,7},{3,5},{1,3},{16,18},{18,20},{2... | collective-permute-start | bytes 1572872 | tf_op jit(solution)/shard_map/ppermute | solution.py:36
  106.3 5.2 %collective-permute-done.15 = bf16[64,4096]{1,0:T(8,128)(2,1)S(1)} collective-permute-done((bf16[64,4096]{1,0:T(8,128)(2,1)S(1)}, bf16[64,4096]{1,0:T(8,128)(2,1)S(1)}, u32[]{:S(2)}, u32[]{:S(2)}) %collective-permute-start.15) | collective-permute-done | bytes 524320 | tf_op jit(solution)/shard_map/ppermute | solution.py:36
  111.5 0.1 add_convert_fusion.1
  111.7 1.8 %collective-permute-start.16 = (bf16[64,4096]{1,0:T(8,128)(2,1)S(1)}, bf16[64,4096]{1,0:T(8,128)(2,1)S(1)}, u32[]{:S(2)}, u32[]{:S(2)}) collective-permute-start(bf16[64,4096]{1,0:T(8,128)(2,1)S(1)} %add_convert_fusion.1), channel_id=1, source_target_pairs={{0,2},{2,4},{4,6},{6,7},{7,5},{5,3},{3,1},{1,0},{16,17},{18,16},{2... | collective-permute-start | bytes 1572872 | tf_op jit(solution)/shard_map/ppermute | solution.py:36
  113.5 0.0 collective-permute-done.12
  113.5 0.1 add_convert_fusion.3
  113.6 2.0 %collective-permute-start.13 = (bf16[64,4096]{1,0:T(8,128)(2,1)S(1)}, bf16[64,4096]{1,0:T(8,128)(2,1)S(1)}, u32[]{:S(2)}, u32[]{:S(2)}) collective-permute-start(bf16[64,4096]{1,0:T(8,128)(2,1)S(1)} %add_convert_fusion.3), channel_id=1, source_target_pairs={{0,1},{2,0},{4,2},{6,4},{7,6},{5,7},{3,5},{1,3},{16,18},{18,20},{2... | collective-permute-start | bytes 1572872 | tf_op jit(solution)/shard_map/ppermute | solution.py:36
  115.7 9.4 %weight_grads.2 = (bf16[384,2048]{1,0:T(8,128)(2,1)S(1)}, bf16[384,2048]{1,0:T(8,128)(2,1)S(1)}, bf16[384,2048]{1,0:T(8,128)(2,1)S(1)}) custom-call(bf16[64,4224]{1,0:T(8,128)(2,1)S(1)} %copy-done, bf16[64,4224]{1,0:T(8,128)(2,1)S(1)} %collective-permute-done.refs_1_.refs_9_, bf16[64,4224]{1,0:T(8,128)(2,1)S(1)} %collective-permute-done.1.refs_2_.refs_10_, ...), custom_call_target="tpu_custom_call" | custom-call | flops 2415919104 | bytes 13631488 | tf_op jit(solution)/shard_map/weight_grads/pallas_call | solution.py:235
  125.1 0.1 collective-permute-start.19
  125.2 0.5 collective-permute-start.20
  125.7 0.1 collective-permute-start.21
  125.8 0.0 collective-permute-done.16
  125.8 0.0 collective-permute-done.13
  125.8 0.3 add_convert_fusion
  126.1 2.2 %collective-permute-start.18 = (bf16[1,64,2048]{2,1,0:T(8,128)(2,1)S(1)}, bf16[1,64,2048]{2,1,0:T(8,128)(2,1)S(1)}, u32[]{:S(2)}, u32[]{:S(2)}) collective-permute-start(bf16[1,64,2048]{2,1,0:T(8,128)(2,1)S(1)} %get-tuple-element.51), channel_id=1, source_target_pairs={{0,8},{8,0},{1,9},{9,1},{2,10},{10,2},{3,11},{11,3},{4,12},{12,4},... | collective-permute-start | bytes 786440 | tf_op jit(solution)/shard_map/ppermute | solution.py:41
  128.2 0.1 collective-permute-start.17
  128.3 0.3 collective-permute-done.19.refs_25_
  128.6 2.2 %collective-permute-done.20.refs_26_ = bf16[384,2048]{1,0:T(8,128)(2,1)S(1)} collective-permute-done((bf16[384,2048]{1,0:T(8,128)(2,1)S(1)}, bf16[384,2048]{1,0:T(8,128)(2,1)S(1)}, u32[]{:S(2)}, u32[]{:S(2)}) %collective-permute-start.20) | collective-permute-done | bytes 1572896 | tf_op jit(solution)/shard_map/ppermute | solution.py:41
  130.8 2.2 %collective-permute-done.21.refs_27_ = bf16[384,2048]{1,0:T(8,128)(2,1)S(1)} collective-permute-done((bf16[384,2048]{1,0:T(8,128)(2,1)S(1)}, bf16[384,2048]{1,0:T(8,128)(2,1)S(1)}, u32[]{:S(2)}, u32[]{:S(2)}) %collective-permute-start.21) | collective-permute-done | bytes 1572896 | tf_op jit(solution)/shard_map/ppermute | solution.py:41
  133.1 10.5 %weight_grads.3 = (bf16[384,2048]{1,0:T(8,128)(2,1)}, bf16[384,2048]{1,0:T(8,128)(2,1)}, bf16[384,2048]{1,0:T(8,128)(2,1)}) custom-call(bf16[64,4224]{1,0:T(8,128)(2,1)S(1)} %copy-done, bf16[64,4224]{1,0:T(8,128)(2,1)S(1)} %collective-permute-done.refs_1_.refs_9_, bf16[64,4224]{1,0:T(8,128)(2,1)S(1)} %collective-permute-done.1.refs_2_.refs_10_, ...), custom_call_target="tpu_custom_call" | custom-call | flops 2415919104 | bytes 13631488 | tf_op jit(solution)/shard_map/weight_grads/pallas_call | solution.py:235
  143.6 0.0 collective-permute-done.18
  143.6 0.0 collective-permute-done.17
  143.6 0.7 copy.15
  144.3 0.7 copy.16
  (3 shorter events, 0.0 us)
Async XLA Ops:
  2.8 10.5 %collective-permute-start = (bf16[64,4224]{1,0:T(8,128)(2,1)}, bf16[64,4224]{1,0:T(8,128)(2,1)S(1)}, u32[]{:S(2)}, u32[]{:S(2)}) collective-permute-start(bf16[64,4224]{1,0:T(8,128)(2,1)} %pack_rows.1.refs_0_.refs_8_), channel_id=1, source_target_pairs={{0,2},{2,4},{4,6},{6,7},{7,5},{5,3},{3,1},{1,0},{16,17},{18,16},{2... | collective-permute-start | bytes 1622024 | tf_op jit(solution)/shard_map/ppermute | solution.py:36
  13.3 12.9 %collective-permute-start.2 = (bf16[64,4224]{1,0:T(8,128)(2,1)S(1)}, bf16[64,4224]{1,0:T(8,128)(2,1)S(1)}, u32[]{:S(2)}, u32[]{:S(2)}) collective-permute-start(bf16[64,4224]{1,0:T(8,128)(2,1)S(1)} %collective-permute-done.refs_1_.refs_9_), channel_id=1, source_target_pairs={{0,2},{2,4},{4,6},{6,7},{7,5},{5,3},{3,1},{1,0},{16,17},{18,16},{2... | collective-permute-start | bytes 1622024 | tf_op jit(solution)/shard_map/ppermute | solution.py:36
  15.4 29.4 %collective-permute-start.3 = (bf16[384,2048]{1,0:T(8,128)(2,1)}, bf16[384,2048]{1,0:T(8,128)(2,1)}, u32[]{:S(2)}, u32[]{:S(2)}) collective-permute-start(bf16[384,2048]{1,0:T(8,128)(2,1)} %bitcast.22), channel_id=1, source_target_pairs={{0,16},{16,0},{1,17},{17,1},{2,18},{18,2},{3,19},{19,3},{4,20},{20... | collective-permute-start | bytes 4718600 | tf_op jit(solution)/shard_map/ppermute | solution.py:41
  15.4 29.4 %collective-permute-start.4 = (bf16[384,2048]{1,0:T(8,128)(2,1)}, bf16[384,2048]{1,0:T(8,128)(2,1)}, u32[]{:S(2)}, u32[]{:S(2)}) collective-permute-start(bf16[384,2048]{1,0:T(8,128)(2,1)} %bitcast.26), channel_id=1, source_target_pairs={{0,16},{16,0},{1,17},{17,1},{2,18},{18,2},{3,19},{19,3},{4,20},{20... | collective-permute-start | bytes 4718600 | tf_op jit(solution)/shard_map/ppermute | solution.py:41
  15.9 28.9 %collective-permute-start.5 = (bf16[384,2048]{1,0:T(8,128)(2,1)}, bf16[384,2048]{1,0:T(8,128)(2,1)}, u32[]{:S(2)}, u32[]{:S(2)}) collective-permute-start(bf16[384,2048]{1,0:T(8,128)(2,1)} %bitcast.30), channel_id=1, source_target_pairs={{0,16},{16,0},{1,17},{17,1},{2,18},{18,2},{3,19},{19,3},{4,20},{20... | collective-permute-start | bytes 4718600 | tf_op jit(solution)/shard_map/ppermute | solution.py:41
  15.9 12.7 %collective-permute-start.1 = (bf16[64,4224]{1,0:T(8,128)(2,1)}, bf16[64,4224]{1,0:T(8,128)(2,1)S(1)}, u32[]{:S(2)}, u32[]{:S(2)}) collective-permute-start(bf16[64,4224]{1,0:T(8,128)(2,1)} %pack_rows.1.refs_0_.refs_8_), channel_id=1, source_target_pairs={{0,1},{2,0},{4,2},{6,4},{7,6},{5,7},{3,5},{1,3},{16,18},{18,20},{2... | collective-permute-start | bytes 1622024 | tf_op jit(solution)/shard_map/ppermute | solution.py:36
  26.2 16.6 %collective-permute-start.6 = (bf16[64,4224]{1,0:T(8,128)(2,1)S(1)}, bf16[64,4224]{1,0:T(8,128)(2,1)S(1)}, u32[]{:S(2)}, u32[]{:S(2)}) collective-permute-start(bf16[64,4224]{1,0:T(8,128)(2,1)S(1)} %collective-permute-done.2.refs_3_.refs_11_), channel_id=1, source_target_pairs={{0,2},{2,4},{4,6},{6,7},{7,5},{5,3},{3,1},{1,0},{16,17},{18,16},{2... | collective-permute-start | bytes 1622024 | tf_op jit(solution)/shard_map/ppermute | solution.py:36
  28.7 14.4 %collective-permute-start.9 = (bf16[64,4224]{1,0:T(8,128)(2,1)S(1)}, bf16[64,4224]{1,0:T(8,128)(2,1)S(1)}, u32[]{:S(2)}, u32[]{:S(2)}) collective-permute-start(bf16[64,4224]{1,0:T(8,128)(2,1)S(1)} %collective-permute-done.1.refs_2_.refs_10_), channel_id=1, source_target_pairs={{0,1},{2,0},{4,2},{6,4},{7,6},{5,7},{3,5},{1,3},{16,18},{18,20},{2... | collective-permute-start | bytes 1622024 | tf_op jit(solution)/shard_map/ppermute | solution.py:36
  42.8 14.0 %collective-permute-start.7 = (bf16[64,4224]{1,0:T(8,128)(2,1)S(1)}, bf16[64,4224]{1,0:T(8,128)(2,1)S(1)}, u32[]{:S(2)}, u32[]{:S(2)}) collective-permute-start(bf16[64,4224]{1,0:T(8,128)(2,1)S(1)} %collective-permute-done.6.refs_1_.refs_5_.refs_13_), channel_id=1, source_target_pairs={{0,2},{2,4},{4,6},{6,7},{7,5},{5,3},{3,1},{1,0},{16,17},{18,16},{2... | collective-permute-start | bytes 1622024 | tf_op jit(solution)/shard_map/ppermute | solution.py:36
  43.1 37.8 %collective-permute-start.10 = (bf16[64,4224]{1,0:T(8,128)(2,1)S(1)}, bf16[64,4224]{1,0:T(8,128)(2,1)S(1)}, u32[]{:S(2)}, u32[]{:S(2)}) collective-permute-start(bf16[64,4224]{1,0:T(8,128)(2,1)S(1)} %collective-permute-done.9.refs_0_.refs_4_.refs_12_), channel_id=1, source_target_pairs={{0,1},{2,0},{4,2},{6,4},{7,6},{5,7},{3,5},{1,3},{16,18},{18,20},{2... | collective-permute-start | bytes 1622024 | tf_op jit(solution)/shard_map/ppermute | solution.py:36
  56.8 1.4 copy-start.1
  58.2 1.4 copy-start.2
  59.6 1.4 copy-start.3
  61.0 10.3 %copy-start = (bf16[64,4224]{1,0:T(8,128)(2,1)S(1)}, bf16[64,4224]{1,0:T(8,128)(2,1)}, u32[]{:S(2)}) copy-start(bf16[64,4224]{1,0:T(8,128)(2,1)} %pack_rows.1.refs_0_.refs_8_) | copy-start | bytes 1622020
  69.7 21.4 %collective-permute-start.8 = (bf16[64,4096]{1,0:T(8,128)(2,1)S(1)}, bf16[64,4096]{1,0:T(8,128)(2,1)S(1)}, u32[]{:S(2)}, u32[]{:S(2)}) collective-permute-start(bf16[64,4096]{1,0:T(8,128)(2,1)S(1)} %get-tuple-element.29), channel_id=1, source_target_pairs={{0,1},{2,0},{4,2},{6,4},{7,6},{5,7},{3,5},{1,3},{16,18},{18,20},{2... | collective-permute-start | bytes 1572872 | tf_op jit(solution)/shard_map/ppermute | solution.py:36
  90.5 11.0 %collective-permute-start.14 = (bf16[64,4096]{1,0:T(8,128)(2,1)S(1)}, bf16[64,4096]{1,0:T(8,128)(2,1)S(1)}, u32[]{:S(2)}, u32[]{:S(2)}) collective-permute-start(bf16[64,4096]{1,0:T(8,128)(2,1)S(1)} %get-tuple-element.33), channel_id=1, source_target_pairs={{0,2},{2,4},{4,6},{6,7},{7,5},{5,3},{3,1},{1,0},{16,17},{18,16},{2... | collective-permute-start | bytes 1572872 | tf_op jit(solution)/shard_map/ppermute | solution.py:36
  91.2 12.4 %collective-permute-start.11 = (bf16[64,4096]{1,0:T(8,128)(2,1)S(1)}, bf16[64,4096]{1,0:T(8,128)(2,1)S(1)}, u32[]{:S(2)}, u32[]{:S(2)}) collective-permute-start(bf16[64,4096]{1,0:T(8,128)(2,1)S(1)} %add_convert_fusion.5), channel_id=1, source_target_pairs={{0,1},{2,0},{4,2},{6,4},{7,6},{5,7},{3,5},{1,3},{16,18},{18,20},{2... | collective-permute-start | bytes 1572872 | tf_op jit(solution)/shard_map/ppermute | solution.py:36
  101.6 9.9 %collective-permute-start.15 = (bf16[64,4096]{1,0:T(8,128)(2,1)S(1)}, bf16[64,4096]{1,0:T(8,128)(2,1)S(1)}, u32[]{:S(2)}, u32[]{:S(2)}) collective-permute-start(bf16[64,4096]{1,0:T(8,128)(2,1)S(1)} %add_convert_fusion.2), channel_id=1, source_target_pairs={{0,2},{2,4},{4,6},{6,7},{7,5},{5,3},{3,1},{1,0},{16,17},{18,16},{2... | collective-permute-start | bytes 1572872 | tf_op jit(solution)/shard_map/ppermute | solution.py:36
  103.8 9.7 %collective-permute-start.12 = (bf16[64,4096]{1,0:T(8,128)(2,1)S(1)}, bf16[64,4096]{1,0:T(8,128)(2,1)S(1)}, u32[]{:S(2)}, u32[]{:S(2)}) collective-permute-start(bf16[64,4096]{1,0:T(8,128)(2,1)S(1)} %add_convert_fusion.4), channel_id=1, source_target_pairs={{0,1},{2,0},{4,2},{6,4},{7,6},{5,7},{3,5},{1,3},{16,18},{18,20},{2... | collective-permute-start | bytes 1572872 | tf_op jit(solution)/shard_map/ppermute | solution.py:36
  111.7 14.1 %collective-permute-start.16 = (bf16[64,4096]{1,0:T(8,128)(2,1)S(1)}, bf16[64,4096]{1,0:T(8,128)(2,1)S(1)}, u32[]{:S(2)}, u32[]{:S(2)}) collective-permute-start(bf16[64,4096]{1,0:T(8,128)(2,1)S(1)} %add_convert_fusion.1), channel_id=1, source_target_pairs={{0,2},{2,4},{4,6},{6,7},{7,5},{5,3},{3,1},{1,0},{16,17},{18,16},{2... | collective-permute-start | bytes 1572872 | tf_op jit(solution)/shard_map/ppermute | solution.py:36
  113.6 12.1 %collective-permute-start.13 = (bf16[64,4096]{1,0:T(8,128)(2,1)S(1)}, bf16[64,4096]{1,0:T(8,128)(2,1)S(1)}, u32[]{:S(2)}, u32[]{:S(2)}) collective-permute-start(bf16[64,4096]{1,0:T(8,128)(2,1)S(1)} %add_convert_fusion.3), channel_id=1, source_target_pairs={{0,1},{2,0},{4,2},{6,4},{7,6},{5,7},{3,5},{1,3},{16,18},{18,20},{2... | collective-permute-start | bytes 1572872 | tf_op jit(solution)/shard_map/ppermute | solution.py:36
  125.1 3.5 %collective-permute-start.19 = (bf16[384,2048]{1,0:T(8,128)(2,1)S(1)}, bf16[384,2048]{1,0:T(8,128)(2,1)S(1)}, u32[]{:S(2)}, u32[]{:S(2)}) collective-permute-start(bf16[384,2048]{1,0:T(8,128)(2,1)S(1)} %get-tuple-element.45), channel_id=1, source_target_pairs={{0,16},{16,0},{1,17},{17,1},{2,18},{18,2},{3,19},{19,3},{4,20},{20... | collective-permute-start | bytes 4718600 | tf_op jit(solution)/shard_map/ppermute | solution.py:41
  125.2 5.6 %collective-permute-start.20 = (bf16[384,2048]{1,0:T(8,128)(2,1)S(1)}, bf16[384,2048]{1,0:T(8,128)(2,1)S(1)}, u32[]{:S(2)}, u32[]{:S(2)}) collective-permute-start(bf16[384,2048]{1,0:T(8,128)(2,1)S(1)} %get-tuple-element.46), channel_id=1, source_target_pairs={{0,16},{16,0},{1,17},{17,1},{2,18},{18,2},{3,19},{19,3},{4,20},{20... | collective-permute-start | bytes 4718600 | tf_op jit(solution)/shard_map/ppermute | solution.py:41
  125.7 7.4 %collective-permute-start.21 = (bf16[384,2048]{1,0:T(8,128)(2,1)S(1)}, bf16[384,2048]{1,0:T(8,128)(2,1)S(1)}, u32[]{:S(2)}, u32[]{:S(2)}) collective-permute-start(bf16[384,2048]{1,0:T(8,128)(2,1)S(1)} %get-tuple-element.47), channel_id=1, source_target_pairs={{0,16},{16,0},{1,17},{17,1},{2,18},{18,2},{3,19},{19,3},{4,20},{20... | collective-permute-start | bytes 4718600 | tf_op jit(solution)/shard_map/ppermute | solution.py:41
  126.1 17.5 %collective-permute-start.18 = (bf16[1,64,2048]{2,1,0:T(8,128)(2,1)S(1)}, bf16[1,64,2048]{2,1,0:T(8,128)(2,1)S(1)}, u32[]{:S(2)}, u32[]{:S(2)}) collective-permute-start(bf16[1,64,2048]{2,1,0:T(8,128)(2,1)S(1)} %get-tuple-element.51), channel_id=1, source_target_pairs={{0,8},{8,0},{1,9},{9,1},{2,10},{10,2},{3,11},{11,3},{4,12},{12,4},... | collective-permute-start | bytes 786440 | tf_op jit(solution)/shard_map/ppermute | solution.py:41
  128.2 15.3 %collective-permute-start.17 = (bf16[1,64,2048]{2,1,0:T(8,128)(2,1)S(1)}, bf16[1,64,2048]{2,1,0:T(8,128)(2,1)S(1)}, u32[]{:S(2)}, u32[]{:S(2)}) collective-permute-start(bf16[1,64,2048]{2,1,0:T(8,128)(2,1)S(1)} %get-tuple-element.52), channel_id=1, source_target_pairs={{0,8},{8,0},{1,9},{9,1},{2,10},{10,2},{3,11},{11,3},{4,12},{12,4},... | collective-permute-start | bytes 786440 | tf_op jit(solution)/shard_map/ppermute | solution.py:41

commit v3 on v2

--- a/solution.py
+++ b/solution.py
@@ -8,7 +8,7 @@
 
 F32 = jnp.float32
 BF16 = jnp.bfloat16
-VMEM_BYTES = 40 * 2**20
+VMEM_BYTES = 60 * 2**20
 
 
 def ring_order(peers):
@@ -79,11 +79,26 @@
     out_ref[:, 2 * width :] = turned(jnp.concatenate(parts, axis=0)).astype(BF16)
 
 
+def row_copies(blocks, rows, width, sems, offset):
+    tokens = blocks[0].shape[0]
+    copies = []
+    for i, block in enumerate(blocks):
+        for part in range(2):
+            copies.append(
+                pltpu.make_async_copy(
+                    block.at[:, pl.ds(part * width, width)],
+                    rows.at[part, pl.ds(i * tokens, tokens)],
+                    sems.at[offset + 2 * i + part],
+                )
+            )
+    return copies
+
+
 def expert_kernel(count, experts, local_experts, width, first_ref, *refs):
     blocks = refs[:count]
     weights = refs[count : count + 6]
     outs = refs[count + 6 : 2 * count + 6]
-    gate_out, up_out, hidden_out, buffer, rows, sems = refs[2 * count + 6 :]
+    gate_out, up_out, hidden_out, rows, tables, buffer, gates, slopes, sems = refs[2 * count + 6 :]
     half = weights[0].shape[0]
     units = 2 * half
     copies = []
@@ -94,18 +109,24 @@
                 weights[side * 3 + kind], buffer.at[kind, pl.ds(side * half, half)], sems.at[i]
             )
         )
-    for copy in copies:
-        copy.start()
     tokens = blocks[0].shape[0]
     lanes = blocks[0].shape[1] - 2 * width
-    scales = []
-    lane = lax.broadcasted_iota(jnp.int32, (tokens, lanes), 1)
-    expert_of = lax.rem(lane, experts)
+    loads = row_copies(blocks, rows, width, sems, 6)
     for i, block in enumerate(blocks):
-        rows[0, i * tokens : (i + 1) * tokens, :] = block[:, :width]
-        rows[1, i * tokens : (i + 1) * tokens, :] = block[:, width : 2 * width]
-        table = block[:, 2 * width :].astype(F32)
-        scales.append(
+        loads.append(
+            pltpu.make_async_copy(
+                block.at[:, pl.ds(2 * width, lanes)], tables.at[i], sems.at[6 + 2 * count + i]
+            )
+        )
+    for copy in copies[:2] + loads + copies[2:]:
+        copy.start()
+    for copy in loads:
+        copy.wait()
+    parts = []
+    expert_of = lax.rem(lax.broadcasted_iota(jnp.int32, (tokens, lanes), 1), experts)
+    for i in range(count):
+        table = tables[i].astype(F32)
+        parts.append(
             [
                 jnp.sum(
                     jnp.where(expert_of == first_ref[0] + e, table, 0.0), axis=1, keepdims=True
@@ -113,33 +134,40 @@
                 for e in range(local_experts)
             ]
         )
-    scales = [
-        jnp.concatenate([s[e] for s in scales], axis=0) for e in range(local_experts)
-    ]
-    for copy in copies:
-        copy.wait()
+    scales = [jnp.concatenate([s[e] for s in parts], axis=0) for e in range(local_experts)]
     tile = 256
     last = ((1,), (1,))
     plain = ((1,), (0,))
-
-    def hidden_tile(j, carry):
-        at = pl.ds(pl.multiple_of(j * tile, tile), tile)
-        gate = dot(rows[0], buffer[0, at, :], last)
-        up = dot(rows[0], buffer[1, at, :], last)
-        back = dot(rows[1], buffer[2, at, :], last)
-        unit = lax.rem(j * tile + lax.broadcasted_iota(jnp.int32, (1, tile), 1), half)
-        scale = jnp.broadcast_to(scales[0], gate.shape)
+    tiles = [slice(j * tile, (j + 1) * tile) for j in range(units // tile)]
+
+    def scale_of(at, shape):
+        unit = lax.rem(at.start + lax.broadcasted_iota(jnp.int32, (1, tile), 1), half)
+        scale = jnp.broadcast_to(scales[0], shape)
         for e in range(1, local_experts):
             scale = jnp.where(unit >= e * (half // local_experts), scales[e], scale)
+        return scale
+
+    copies[0].wait()
+    copies[1].wait()
+    for at in tiles:
+        gates[:, at] = dot(rows[0], buffer[0, at, :], last)
+    copies[2].wait()
+    copies[3].wait()
+    for at in tiles:
+        gate = gates[:, at]
+        up = dot(rows[0], buffer[1, at, :], last)
         sig = 1.0 / (1.0 + jnp.exp(-gate))
         swish = gate * sig
-        back = back * scale
+        scale = scale_of(at, gate.shape)
         hidden_out[:, at] = (swish * up * scale).astype(BF16)
-        gate_out[:, at] = (back * up * sig * (1.0 + gate * (1.0 - sig))).astype(BF16)
-        up_out[:, at] = (back * swish).astype(BF16)
-        return carry
-
-    lax.fori_loop(0, units // tile, hidden_tile, 0)
+        gates[:, at] = swish * scale
+        slopes[:, at] = up * sig * (1.0 + gate * (1.0 - sig)) * scale
+    copies[4].wait()
+    copies[5].wait()
+    for at in tiles:
+        back = dot(rows[1], buffer[2, at, :], last)
+        gate_out[:, at] = (back * slopes[:, at]).astype(BF16)
+        up_out[:, at] = (back * gates[:, at]).astype(BF16)
 
     def column_tile(n, carry):
         at = pl.ds(pl.multiple_of(n * tile, tile), tile)
@@ -153,7 +181,7 @@
             out[:, later] = grad[i * tokens : (i + 1) * tokens]
         return carry
 
-    lax.fori_loop(0, width // tile, column_tile, 0)
+    lax.fori_loop(0, width // tile, column_tile, 0, unroll=2)
 
 
 def expert_call(blocks, weights, first, experts, local_experts, width):
@@ -164,15 +192,18 @@
     saved = jax.ShapeDtypeStruct((rows, 2 * half), BF16)
     results = pl.pallas_call(
         functools.partial(expert_kernel, count, experts, local_experts, width),
-        out_shape=[jax.ShapeDtypeStruct((tokens, 2 * width), BF16)] * count + [saved] * 3,
+        out_shape=[jax.ShapeDtypeStruct((tokens, 2 * width), BF16)] * count
+        + [saved] * 3,
         in_specs=[pl.BlockSpec(memory_space=pltpu.SMEM)]
-        + [whole()] * count
-        + [pl.BlockSpec(memory_space=pl.ANY)] * 6,
+        + [pl.BlockSpec(memory_space=pl.ANY)] * (count + 6),
         out_specs=[whole()] * (count + 3),
         scratch_shapes=[
+            pltpu.VMEM((2, rows, width), BF16),
+            pltpu.VMEM((count, tokens, blocks[0].shape[1] - 2 * width), BF16),
             pltpu.VMEM((3, 2 * half, width), BF16),
-            pltpu.VMEM((2, rows, width), BF16),
-            pltpu.SemaphoreType.DMA((6,)),
+            pltpu.VMEM((rows, 2 * half), F32),
+            pltpu.VMEM((rows, 2 * half), F32),
+            pltpu.SemaphoreType.DMA((6 + 3 * count,)),
         ],
         compiler_params=pltpu.CompilerParams(vmem_limit_bytes=VMEM_BYTES),
         cost_estimate=pl.CostEstimate(
@@ -186,59 +217,61 @@
 
 
 def weight_kernel(groups, count, has_received, *refs):
-    rows = refs[:count]
-    grads = refs[count : 2 * count]
-    refs = refs[2 * count :]
-    saved = [refs[g * 3 : g * 3 + 3] for g in range(groups)]
-    refs = refs[groups * 3 :]
+    blocks = refs[:count]
+    kept = [refs[count + g * 3 : count + g * 3 + 3] for g in range(groups)]
+    refs = refs[count + groups * 3 :]
     received = refs[:3] if has_received else None
-    outs = refs[-4:-1]
-    across = refs[-1]
+    outs = refs[-6:-3]
+    across, rows, sems = refs[-3:]
+    tile = outs[0].shape[1]
+    copies = row_copies(blocks, rows, rows.shape[2], sems, 0)
 
     @pl.when(pl.program_id(0) == 0)
     def _():
+        for copy in copies:
+            copy.start()
         for kind in range(3):
             start = 0
-            for group in saved:
+            for group in kept:
                 size = group[kind].shape[0]
                 across[kind, :, start : start + size] = group[kind][...].T
                 start += size
-
-    right = [
-        jnp.concatenate([r[...] for r in rows], axis=0),
-        jnp.concatenate([r[...] for r in grads], axis=0),
-    ]
+        for copy in copies:
+            copy.wait()
+
+    at = pl.ds(pl.multiple_of(pl.program_id(0) * tile, tile), tile)
     for kind in range(3):
-        total = dot(across[kind], right[kind // 2], ((1,), (0,)))
+        total = dot(across[kind], rows[kind // 2, :, at], ((1,), (0,)))
         if has_received:
             total = total + received[kind][...].astype(F32)
         outs[kind][...] = total.astype(BF16)
 
 
-def weight_call(blocks, saved, side, received, width):
-    tokens = blocks[0].shape[0]
-    count = len(blocks)
-    half = saved[0][0].shape[1] // 2
-    tile = 256
+def weight_call(blocks, kept, side, received, width):
+    half = kept[0][0].shape[1] // 2
+    tile = 512
     steps = width // tile
-    block = lambda offset: pl.BlockSpec((tokens, tile), lambda n: (0, n + offset))
     column = pl.BlockSpec((half, tile), lambda n: (0, n))
-    total = tokens * count
-    specs = [block(0)] * count + [block(steps)] * count
-    args = list(blocks) * 2
-    for group in saved:
+    total = len(blocks) * blocks[0].shape[0]
+    specs = [pl.BlockSpec(memory_space=pl.ANY)] * len(blocks)
+    args = list(blocks)
+    for group in kept:
         specs += [pl.BlockSpec((g.shape[0], half), lambda n: (0, side)) for g in group]
         args += list(group)
     if received is not None:
         specs += [column] * 3
         args += list(received)
     return pl.pallas_call(
-        functools.partial(weight_kernel, len(saved), count, received is not None),
+        functools.partial(weight_kernel, len(kept), len(blocks), received is not None),
         grid=(steps,),
         out_shape=[jax.ShapeDtypeStruct((half, width), BF16)] * 3,
         in_specs=specs,
         out_specs=[column] * 3,
-        scratch_shapes=[pltpu.VMEM((3, half, total), BF16)],
+        scratch_shapes=[
+            pltpu.VMEM((3, half, total), BF16),
+            pltpu.VMEM((2, total, width), BF16),
+            pltpu.SemaphoreType.DMA((2 * len(blocks),)),
+        ],
         compiler_params=pltpu.CompilerParams(vmem_limit_bytes=VMEM_BYTES),
         cost_estimate=pl.CostEstimate(
             flops=3 * 2 * total * half * width,
@@ -274,51 +307,64 @@
         name="pack_rows",
     )(row_codes[0], block_exponents[0].T, routes[0].T, route_weight[0].T, out_grad[0])
 
+    tie = lax.optimization_barrier
     ahead, behind = peers // 2, peers // 2 - 1
     near, far = [home], [home]
-    arrived = [("home", 0, home)]
+    partial, kept, blocks = {}, [], []
+
+    def expert_rows(names):
+        held = [(near if name == "near" else far)[k] for name, k in names]
+        outs, saved = expert_call(held, weights, first, experts, local_experts, width)
+        for name, out in zip(names, outs):
+            partial[name] = out
+        kept.append(saved)
+        blocks.extend(held)
+
+    waiting = [("near", 0)]
     for k in range(1, ahead + 1):
-        near.append(ring_shift(near[-1], 1))
-        arrived.append(("near", k, near[k]))
+        near.append(ring_shift(near[k - 1], 1))
         if k <= behind:
-            far.append(ring_shift(far[-1], -1))
-            arrived.append(("far", k, far[k]))
-    groups = [arrived[i : i + 4] for i in range(0, len(arrived) - 1, 4)]
-    if len(groups[-1]) > 1 and groups[-1][-1] is arrived[-1]:
-        groups[-1] = groups[-1][:-1]
-    groups.append(arrived[-1:])
-    partial, saved = {}, []
-    for group in groups:
-        outs, kept = expert_call(
-            [g[2] for g in group], weights, first, experts, local_experts, width
-        )
-        saved.append(kept)
-        for (name, k, _), out in zip(group, outs):
-            partial[name, k] = out
-
-    blocks = [g[2] for group in groups for g in group]
-    given = weight_call(blocks, saved, 1, None, width)
-    received = [from_behind(g, "rep", 1) for g in given]
-
-    near_sum, far_sum = partial["near", ahead], partial["far", behind] if behind else None
-    for k in range(ahead, 0, -1):
+            far.append(ring_shift(far[k - 1], -1))
+        done = None
+        if len(waiting) >= 4:
+            expert_rows(waiting[:4])
+            done, waiting = kept[-1], waiting[4:]
+        if k <= behind:
+            near[k], far[k], done = tie((near[k], far[k], done))
+            waiting += [("near", k), ("far", k)]
+        else:
+            expert_rows([name for name in waiting if name[0] == "far"])
+            waiting = [name for name in waiting if name[0] == "near"]
+            near[k], done = tie((near[k], kept[-1]))
+            waiting.append(("near", k))
+        if done is not None:
+            kept[-1] = done
+    far_sum = ring_shift(partial["far", behind], 1)
+    expert_rows(waiting)
+    far_sum, near_sum = tie((far_sum, partial["near", ahead]))
+    given = received = totals = None
+    for k in range(ahead, 1, -1):
         near_sum = ring_shift(near_sum, -1)
-        if k > 1:
+        left = k - 2
+        if left >= 1:
+            far_sum = ring_shift(add(far_sum, partial["far", left]), 1)
+        if k == ahead:
+            given = weight_call(blocks, kept, 1, None, width)
+            near_sum, far_sum, given = tie((near_sum, far_sum, given))
+            received = [from_behind(g, "rep", 1) for g in given]
+        elif k == ahead - 1:
+            totals = weight_call(blocks, kept, 0, received, width)
+            near_sum, far_sum, totals = tie((near_sum, far_sum, totals))
+        if k > 2:
             near_sum = add(near_sum, partial["near", k - 1])
-        if k <= behind:
-            far_sum = ring_shift(far_sum, 1)
-            if k > 1:
-                far_sum = add(far_sum, partial["far", k - 1])
-    total = home[:, : 2 * width].astype(F32) + partial["home", 0].astype(F32)
-    total = total + near_sum.astype(F32)
-    if behind:
-        total = total + far_sum.astype(F32)
-    total = total.astype(BF16)
-    next_rows = from_behind(total[None, :, :width], "section", 1)
-    prev_grads = from_behind(total[None, :, width:], "section", -1)
-    totals = weight_call(blocks, saved, 0, received, width)
+    results = []
+    for part, axis_step in ((slice(0, width), 1), (slice(width, 2 * width), -1)):
+        arrived = ring_shift(add(near_sum[:, part], partial["near", 1][:, part]), -1)
+        total = home[:, part].astype(F32) + partial["near", 0][:, part].astype(F32)
+        total = total + far_sum[:, part].astype(F32) + arrived.astype(F32)
+        results.append(from_behind(total.astype(BF16)[None], "section", axis_step))
     shape = (1, local_experts, half_units, width)
-    return (next_rows, prev_grads) + tuple(t.reshape(shape) for t in totals)
+    return tuple(results) + tuple(t.reshape(shape) for t in totals)
 
 
 def solution(mesh):

time: 145 us -> 142 us (0.979)
  starting transfers between devices: 26.2 us -> 19.2 us
  other arithmetic: 0.9 us -> 5.76 us
    ppermute x14 -> x15, waiting for transfers between devices: 56.6 us -> 48 us  [ring_shift(): return lax.ppermute(value, ('rep', 'exp'), pairs)]
    ppermute x8, waiting for transfers between devices: 4.77 us -> 13 us  [from_behind(): lax.ppermute(value, axis, [(i, (i + by) % peers) for i in range(peers)])]
    ppermute x14 -> x15, starting transfers between devices: 22.8 us -> 15.6 us  [ring_shift(): return lax.ppermute(value, ('rep', 'exp'), pairs)]
    convert_element_type x5, other arithmetic: 0.64 us -> 4.44 us  [add(): return (a.astype(F32) + b.astype(F32)).astype(BF16)]
    pallas_call x2, Pallas kernels: 19.9 us -> 16.5 us  [weight_call(): pl.pallas_call(functools.partial(weight_kernel, len(kept), len(blocks), r...]
    pallas_call x3, Pallas kernels: 27.9 us -> 30.4 us  [expert_call(): pl.pallas_call(functools.partial(expert_kernel, count, experts, local_exp...]
    unnamed x10 -> x38, local copies, waits for them, and re-layouts: 5.63 us -> 5.91 us
  transfers between devices with their start and end apart: 22 -> 23, of which waited for: 10 -> 11; matrix products, arithmetic and copies ran while one was open for 1% -> 2% of each run, Pallas kernels for 33% -> 35%
where the time goes in v3:
time: 142 us
  waiting for transfers between devices  61 us (43%)
  Pallas kernels  49.2 us (35%)
  starting transfers between devices  19.2 us (14%)
  local copies, waits for them, and re-layouts  5.91 us (4%)
  other arithmetic  5.76 us (4%)
    ppermute x15, waiting for transfers between devices, ring_shift(): return lax.ppermute(value, ('rep', 'exp'), pairs)  48 us
    pallas_call x3, Pallas kernels, expert_call(): pl.pallas_call(functools.partial(expert_kernel, count, experts, local_exp...  30.4 us
    pallas_call x2, Pallas kernels, weight_call(): pl.pallas_call(functools.partial(weight_kernel, len(kept), len(blocks), r...  16.5 us
    ppermute x15, starting transfers between devices, ring_shift(): return lax.ppermute(value, ('rep', 'exp'), pairs)  15.6 us
    ppermute x8, waiting for transfers between devices, from_behind(): lax.ppermute(value, axis, [(i, (i + by) % peers) for i in range(peers)])  13 us
    unnamed x38, local copies, waits for them, and re-layouts  5.91 us
    convert_element_type x5, other arithmetic, add(): return (a.astype(F32) + b.astype(F32)).astype(BF16)  4.44 us
    ppermute x8, starting transfers between devices, from_behind(): lax.ppermute(value, axis, [(i, (i + by) % peers) for i in range(peers)])  3.63 us
  transfers between devices with their start and end apart: 23, of which 11 were waited for; matrix products, arithmetic and copies ran while one was open for 2% of the time, Pallas kernels for 35%

profile of v3, /device:TPU:0, one launch (start us, length us, event | category | flops | bytes accessed | tf_op | source)
XLA Modules:
  0.0 141.9 jit_solution(10248532527426098732)
XLA Ops:
  0.6 0.5 collective-permute-start.4
  1.2 0.1 collective-permute-start.5
  1.2 0.4 collective-permute-start.6
  1.7 2.2 %pack_rows.1.refs_0_ = bf16[64,4224]{1,0:T(8,128)(2,1)} custom-call(bf16[64,2048]{1,0:T(8,128)(2,1)} %bitcast.34, s32[16,64]{1,0:T(8,128)} %bitcast.36, s32[8,64]{1,0:T(8,128)} %bitcast.37, f32[8,64]{1,0:T(8,128)} %bitcast.38, bf16[64,2048]{1,0:T(8,128)(2,1)} %bitcast.35), custom_call_target="tpu_custom_call" | custom-call | tf_op jit(solution)/shard_map/pack_rows/pallas_call | solution.py:302
  3.9 2.6 %collective-permute-start.1 = (bf16[64,4224]{1,0:T(8,128)(2,1)}, bf16[64,4224]{1,0:T(8,128)(2,1)S(1)}, u32[]{:S(2)}, u32[]{:S(2)}) collective-permute-start(bf16[64,4224]{1,0:T(8,128)(2,1)} %pack_rows.1.refs_0_), channel_id=1, source_target_pairs={{0,1},{2,0},{4,2},{6,4},{7,6},{5,7},{3,5},{1,3},{16,18},{18,20},{2... | collective-permute-start | bytes 1622024 | tf_op jit(solution)/shard_map/ppermute | solution.py:36
  6.5 0.1 collective-permute-start
  6.6 12.5 %collective-permute-done.1.refs_2_ = bf16[64,4224]{1,0:T(8,128)(2,1)S(1)} collective-permute-done((bf16[64,4224]{1,0:T(8,128)(2,1)}, bf16[64,4224]{1,0:T(8,128)(2,1)S(1)}, u32[]{:S(2)}, u32[]{:S(2)}) %collective-permute-start.1) | collective-permute-done | bytes 540704 | tf_op jit(solution)/shard_map/ppermute | solution.py:36
  19.1 0.5 collective-permute-done.refs_1_
  19.5 1.8 %collective-permute-start.2 = (bf16[64,4224]{1,0:T(8,128)(2,1)S(1)}, bf16[64,4224]{1,0:T(8,128)(2,1)}, u32[]{:S(2)}, u32[]{:S(2)}) collective-permute-start(bf16[64,4224]{1,0:T(8,128)(2,1)S(1)} %collective-permute-done.refs_1_), channel_id=1, source_target_pairs={{0,2},{2,4},{4,6},{6,7},{7,5},{5,3},{3,1},{1,0},{16,17},{18,16},{2... | collective-permute-start | bytes 1622024 | tf_op jit(solution)/shard_map/ppermute | solution.py:36
  21.4 0.8 collective-permute-start.3
  22.2 12.2 %collective-permute-done.2.refs_3_ = bf16[64,4224]{1,0:T(8,128)(2,1)} collective-permute-done((bf16[64,4224]{1,0:T(8,128)(2,1)S(1)}, bf16[64,4224]{1,0:T(8,128)(2,1)}, u32[]{:S(2)}, u32[]{:S(2)}) %collective-permute-start.2) | collective-permute-done | bytes 540704 | tf_op jit(solution)/shard_map/ppermute | solution.py:36
  34.5 1.7 %collective-permute-start.7 = (bf16[64,4224]{1,0:T(8,128)(2,1)}, bf16[64,4224]{1,0:T(8,128)(2,1)}, u32[]{:S(2)}, u32[]{:S(2)}) collective-permute-start(bf16[64,4224]{1,0:T(8,128)(2,1)} %collective-permute-done.2.refs_3_), channel_id=1, source_target_pairs={{0,2},{2,4},{4,6},{6,7},{7,5},{5,3},{3,1},{1,0},{16,17},{18,16},{2... | collective-permute-start | bytes 1622024 | tf_op jit(solution)/shard_map/ppermute | solution.py:36
  36.1 0.5 collective-permute-start.8
  36.7 0.0 collective-permute-done.4.refs_7_.refs_5_
  36.7 0.0 collective-permute-done.5.refs_8_.refs_6_
  36.7 0.0 copy-start.1
  36.7 1.1 copy-done
  37.8 0.5 copy-done.1
  38.3 11.3 %expert_rows.3 = (bf16[64,4096]{1,0:T(8,128)(2,1)}, bf16[64,4096]{1,0:T(8,128)(2,1)}, bf16[64,4096]{1,0:T(8,128)(2,1)}, bf16[64,4096]{1,0:T(8,128)(2,1)}, bf16[2...) custom-call(s32[1]{0:T(128)} %bitcast.8.first_ref, bf16[64,4224]{1,0:T(8,128)(2,1)} %pack_rows.1.refs_0_, ...), custom_call_target="tpu_custom_call" | custom-call | flops 4831838208 | bytes 13631488 | tf_op jit(solution)/shard_map/expert_rows/pallas_call | solution.py:193
  49.7 0.0 collective-permute-done.8.refs_1_.refs_5_
  49.7 1.6 %collective-permute-start.10 = (bf16[64,4224]{1,0:T(8,128)(2,1)}, bf16[64,4224]{1,0:T(8,128)(2,1)S(1)}, u32[]{:S(2)}, u32[]{:S(2)}) collective-permute-start(bf16[64,4224]{1,0:T(8,128)(2,1)} %collective-permute-done.7.refs_0_.refs_6_), channel_id=1, source_target_pairs={{0,2},{2,4},{4,6},{6,7},{7,5},{5,3},{3,1},{1,0},{16,17},{18,16},{2... | collective-permute-start | bytes 1622024 | tf_op jit(solution)/shard_map/ppermute | solution.py:36
  51.2 9.5 %expert_rows.4 = (bf16[64,4096]{1,0:T(8,128)(2,1)}, bf16[64,4096]{1,0:T(8,128)(2,1)}, bf16[128,768]{1,0:T(8,128)(2,1)}, bf16[128,768]{1,0:T(8,128)(2,1)}, bf16[128,768]{1,0:T(8,128)(2,1)}) custom-call(s32[1]{0:T(128)} %bitcast.8.first_ref, bf16[64,4224]{1,0:T(8,128)(2,1)} %collective-permute-done.3.refs_0_.refs_4_, ...), custom_call_target="tpu_custom_call" | custom-call | flops 2415919104 | bytes 11534336 | tf_op jit(solution)/shard_map/expert_rows/pallas_call | solution.py:193
  60.8 1.7 %collective-permute-start.9 = (bf16[64,4096]{1,0:T(8,128)(2,1)}, bf16[64,4096]{1,0:T(8,128)(2,1)S(1)}, u32[]{:S(2)}, u32[]{:S(2)}) collective-permute-start(bf16[64,4096]{1,0:T(8,128)(2,1)} %get-tuple-element.62), channel_id=1, source_target_pairs={{0,2},{2,4},{4,6},{6,7},{7,5},{5,3},{3,1},{1,0},{16,17},{18,16},{2... | collective-permute-start | bytes 1572872 | tf_op jit(solution)/shard_map/ppermute | solution.py:36
  62.5 0.0 collective-permute-done.10.refs_1_.refs_7_
  62.5 0.8 copy-done.3
  63.3 9.5 %expert_rows.5 = (bf16[64,4096]{1,0:T(8,128)(2,1)}, bf16[64,4096]{1,0:T(8,128)(2,1)}, bf16[128,768]{1,0:T(8,128)(2,1)}, bf16[128,768]{1,0:T(8,128)(2,1)}, bf16[128,768]{1,0:T(8,128)(2,1)}) custom-call(s32[1]{0:T(128)} %bitcast.8.first_ref, bf16[64,4224]{1,0:T(8,128)(2,1)} %collective-permute-done.7.refs_0_.refs_6_, bf16[64,4224]{1,0:T(8,128)(2,1)} %copy-done.3, ...), custom_call_target="tpu_custom_call" | custom-call | flops 2415919104 | bytes 11534336 | tf_op jit(solution)/shard_map/expert_rows/pallas_call | solution.py:193
  72.8 0.0 copy-start.17
  72.8 0.0 collective-permute-done.9
  72.9 0.1 add_convert_fusion.3
  73.0 1.6 %collective-permute-start.12 = (bf16[64,4096]{1,0:T(8,128)(2,1)S(1)}, bf16[64,4096]{1,0:T(8,128)(2,1)S(1)}, u32[]{:S(2)}, u32[]{:S(2)}) collective-permute-start(bf16[64,4096]{1,0:T(8,128)(2,1)S(1)} %add_convert_fusion.3), channel_id=1, source_target_pairs={{0,2},{2,4},{4,6},{6,7},{7,5},{5,3},{3,1},{1,0},{16,17},{18,16},{2... | collective-permute-start | bytes 1572872 | tf_op jit(solution)/shard_map/ppermute | solution.py:36
  74.6 0.4 collective-permute-start.11
  75.1 7.7 %weight_grads.2 = (bf16[384,2048]{1,0:T(8,128)(2,1)}, bf16[384,2048]{1,0:T(8,128)(2,1)}, bf16[384,2048]{1,0:T(8,128)(2,1)}) custom-call(bf16[64,4224]{1,0:T(8,128)(2,1)} %pack_rows.1.refs_0_, bf16[64,4224]{1,0:T(8,128)(2,1)} %copy-done.7, bf16[64,4224]{1,0:T(8,128)(2,1)} %copy-done.6, bf16[64,4224]{1,0:T(8,128)(2,1)} %collective-permute-done.2.refs_3_, ...), custom_call_target="tpu_custom_call" | custom-call | flops 2415919104 | bytes 13631488 | tf_op jit(solution)/shard_map/weight_grads/pallas_call | solution.py:264
  82.8 5.0 %collective-permute-done.12 = bf16[64,4096]{1,0:T(8,128)(2,1)S(1)} collective-permute-done((bf16[64,4096]{1,0:T(8,128)(2,1)S(1)}, bf16[64,4096]{1,0:T(8,128)(2,1)S(1)}, u32[]{:S(2)}, u32[]{:S(2)}) %collective-permute-start.12) | collective-permute-done | bytes 524320 | tf_op jit(solution)/shard_map/ppermute | solution.py:36
  87.8 0.0 collective-permute-done.11
  87.8 0.8 copy-done.15
  88.6 0.2 copy-done.13
  88.8 0.0 collective-permute-start.15
  88.8 0.5 collective-permute-start.16
  89.3 0.0 collective-permute-start.17
  89.3 1.9 %add_convert_fusion.1 = bf16[64,4096]{1,0:T(8,128)(2,1)} fusion(bf16[64,4096]{1,0:T(8,128)(2,1)S(1)} %copy-done.11, bf16[64,4096]{1,0:T(8,128)(2,1)} %copy-done.15), kind=kLoop, calls=%fused_computation.1 | loop fusion | flops 1048576 | bytes 1572864 | tf_op jit(solution)/shard_map/convert_element_type | solution.py:286
  91.3 0.9 collective-permute-start.14
  92.2 1.0 add_convert_fusion.2
  93.2 1.1 collective-permute-start.13
  94.3 0.0 collective-permute-done.15.refs_17_
  94.3 2.6 %collective-permute-done.16.refs_18_ = bf16[384,2048]{1,0:T(8,128)(2,1)S(1)} collective-permute-done((bf16[384,2048]{1,0:T(8,128)(2,1)}, bf16[384,2048]{1,0:T(8,128)(2,1)S(1)}, u32[]{:S(2)}, u32[]{:S(2)}) %collective-permute-start.16) | collective-permute-done | bytes 1572896 | tf_op jit(solution)/shard_map/ppermute | solution.py:41
  96.9 0.1 collective-permute-done.17.refs_19_
  97.1 1.0 copy-done.5
  98.1 8.8 %weight_grads.3 = (bf16[384,2048]{1,0:T(8,128)(2,1)}, bf16[384,2048]{1,0:T(8,128)(2,1)}, bf16[384,2048]{1,0:T(8,128)(2,1)}) custom-call(bf16[64,4224]{1,0:T(8,128)(2,1)} %pack_rows.1.refs_0_, bf16[64,4224]{1,0:T(8,128)(2,1)} %copy-done.7, bf16[64,4224]{1,0:T(8,128)(2,1)} %copy-done.6, bf16[64,4224]{1,0:T(8,128)(2,1)} %collective-permute-done.2.refs_3_, ...), custom_call_target="tpu_custom_call" | custom-call | flops 2415919104 | bytes 13631488 | tf_op jit(solution)/shard_map/weight_grads/pallas_call | solution.py:264
  106.9 0.0 collective-permute-done.14
  107.0 1.3 add_convert_fusion
  108.3 0.1 collective-permute-start.18
  108.3 9.2 %collective-permute-done.18 = bf16[64,4096]{1,0:T(8,128)(2,1)S(1)} collective-permute-done((bf16[64,4096]{1,0:T(8,128)(2,1)S(1)}, bf16[64,4096]{1,0:T(8,128)(2,1)S(1)}, u32[]{:S(2)}, u32[]{:S(2)}) %collective-permute-start.18) | collective-permute-done | bytes 524320 | tf_op jit(solution)/shard_map/ppermute | solution.py:36
  117.5 0.1 add_convert_fusion.5
  117.6 0.1 collective-permute-start.21
  117.7 0.6 collective-permute-start.19
  118.3 5.8 %collective-permute-done.21 = bf16[64,2048]{1,0:T(8,128)(2,1)S(1)} collective-permute-done((bf16[64,2048]{1,0:T(8,128)(2,1)S(1)}, bf16[64,2048]{1,0:T(8,128)(2,1)S(1)}, u32[]{:S(2)}, u32[]{:S(2)}) %collective-permute-start.21) | collective-permute-done | bytes 262176 | tf_op jit(solution)/shard_map/ppermute | solution.py:36
  124.1 2.8 %collective-permute-done.19 = bf16[64,2048]{1,0:T(8,128)(2,1)S(1)} collective-permute-done((bf16[64,2048]{1,0:T(8,128)(2,1)S(1)}, bf16[64,2048]{1,0:T(8,128)(2,1)S(1)}, u32[]{:S(2)}, u32[]{:S(2)}) %collective-permute-start.19) | collective-permute-done | bytes 262176 | tf_op jit(solution)/shard_map/ppermute | solution.py:36
  126.9 1.3 fusion.1
  128.2 1.6 %collective-permute-start.22 = (bf16[1,64,2048]{2,1,0:T(8,128)(2,1)S(1)}, bf16[1,64,2048]{2,1,0:T(8,128)(2,1)S(1)}, u32[]{:S(2)}, u32[]{:S(2)}) collective-permute-start(bf16[1,64,2048]{2,1,0:T(8,128)(2,1)S(1)} %get-tuple-element.101), channel_id=1, source_target_pairs={{0,8},{8,0},{1,9},{9,1},{2,10},{10,2},{3,11},{11,3},{4,12},{12,4},... | collective-permute-start | bytes 786440 | tf_op jit(solution)/shard_map/ppermute | solution.py:41
  129.8 0.5 collective-permute-start.20
  130.3 7.2 %collective-permute-done.22 = bf16[1,64,2048]{2,1,0:T(8,128)(2,1)S(1)} collective-permute-done((bf16[1,64,2048]{2,1,0:T(8,128)(2,1)S(1)}, bf16[1,64,2048]{2,1,0:T(8,128)(2,1)S(1)}, u32[]{:S(2)}, u32[]{:S(2)}) %collective-permute-start.22) | collective-permute-done | bytes 262176 | tf_op jit(solution)/shard_map/ppermute | solution.py:41
  137.5 3.0 %collective-permute-done.20 = bf16[1,64,2048]{2,1,0:T(8,128)(2,1)S(1)} collective-permute-done((bf16[1,64,2048]{2,1,0:T(8,128)(2,1)S(1)}, bf16[1,64,2048]{2,1,0:T(8,128)(2,1)S(1)}, u32[]{:S(2)}, u32[]{:S(2)}) %collective-permute-start.20) | collective-permute-done | bytes 262176 | tf_op jit(solution)/shard_map/ppermute | solution.py:41
  140.5 0.7 copy.15
  141.2 0.7 copy.16
  (32 shorter events, 0.1 us)
Async XLA Ops:
  0.6 36.0 %collective-permute-start.4 = (bf16[384,2048]{1,0:T(8,128)(2,1)}, bf16[384,2048]{1,0:T(8,128)(2,1)S(1)}, u32[]{:S(2)}, u32[]{:S(2)}) collective-permute-start(bf16[384,2048]{1,0:T(8,128)(2,1)} %bitcast.22), channel_id=1, source_target_pairs={{0,16},{16,0},{1,17},{17,1},{2,18},{18,2},{3,19},{19,3},{4,20},{20... | collective-permute-start | bytes 4718600 | tf_op jit(solution)/shard_map/ppermute | solution.py:41
  1.2 35.5 %collective-permute-start.5 = (bf16[384,2048]{1,0:T(8,128)(2,1)}, bf16[384,2048]{1,0:T(8,128)(2,1)S(1)}, u32[]{:S(2)}, u32[]{:S(2)}) collective-permute-start(bf16[384,2048]{1,0:T(8,128)(2,1)} %bitcast.26), channel_id=1, source_target_pairs={{0,16},{16,0},{1,17},{17,1},{2,18},{18,2},{3,19},{19,3},{4,20},{20... | collective-permute-start | bytes 4718600 | tf_op jit(solution)/shard_map/ppermute | solution.py:41
  1.2 35.5 %collective-permute-start.6 = (bf16[384,2048]{1,0:T(8,128)(2,1)}, bf16[384,2048]{1,0:T(8,128)(2,1)}, u32[]{:S(2)}, u32[]{:S(2)}) collective-permute-start(bf16[384,2048]{1,0:T(8,128)(2,1)} %bitcast.30), channel_id=1, source_target_pairs={{0,16},{16,0},{1,17},{17,1},{2,18},{18,2},{3,19},{19,3},{4,20},{20... | collective-permute-start | bytes 4718600 | tf_op jit(solution)/shard_map/ppermute | solution.py:41
  3.9 15.1 %collective-permute-start.1 = (bf16[64,4224]{1,0:T(8,128)(2,1)}, bf16[64,4224]{1,0:T(8,128)(2,1)S(1)}, u32[]{:S(2)}, u32[]{:S(2)}) collective-permute-start(bf16[64,4224]{1,0:T(8,128)(2,1)} %pack_rows.1.refs_0_), channel_id=1, source_target_pairs={{0,1},{2,0},{4,2},{6,4},{7,6},{5,7},{3,5},{1,3},{16,18},{18,20},{2... | collective-permute-start | bytes 1622024 | tf_op jit(solution)/shard_map/ppermute | solution.py:36
  6.5 13.1 %collective-permute-start = (bf16[64,4224]{1,0:T(8,128)(2,1)}, bf16[64,4224]{1,0:T(8,128)(2,1)S(1)}, u32[]{:S(2)}, u32[]{:S(2)}) collective-permute-start(bf16[64,4224]{1,0:T(8,128)(2,1)} %pack_rows.1.refs_0_), channel_id=1, source_target_pairs={{0,2},{2,4},{4,6},{6,7},{7,5},{5,3},{3,1},{1,0},{16,17},{18,16},{2... | collective-permute-start | bytes 1622024 | tf_op jit(solution)/shard_map/ppermute | solution.py:36
  19.0 2.3 %copy-start.6 = (bf16[64,4224]{1,0:T(8,128)(2,1)}, bf16[64,4224]{1,0:T(8,128)(2,1)S(1)}, u32[]{:S(2)}) copy-start(bf16[64,4224]{1,0:T(8,128)(2,1)S(1)} %collective-permute-done.1.refs_2_) | copy-start | bytes 1622020
  19.5 14.9 %copy-start.7 = (bf16[64,4224]{1,0:T(8,128)(2,1)}, bf16[64,4224]{1,0:T(8,128)(2,1)S(1)}, u32[]{:S(2)}) copy-start(bf16[64,4224]{1,0:T(8,128)(2,1)S(1)} %collective-permute-done.refs_1_) | copy-start | bytes 1622020
  19.5 14.9 %collective-permute-start.2 = (bf16[64,4224]{1,0:T(8,128)(2,1)S(1)}, bf16[64,4224]{1,0:T(8,128)(2,1)}, u32[]{:S(2)}, u32[]{:S(2)}) collective-permute-start(bf16[64,4224]{1,0:T(8,128)(2,1)S(1)} %collective-permute-done.refs_1_), channel_id=1, source_target_pairs={{0,2},{2,4},{4,6},{6,7},{7,5},{5,3},{3,1},{1,0},{16,17},{18,16},{2... | collective-permute-start | bytes 1622024 | tf_op jit(solution)/shard_map/ppermute | solution.py:36
  21.4 13.1 %collective-permute-start.3 = (bf16[64,4224]{1,0:T(8,128)(2,1)S(1)}, bf16[64,4224]{1,0:T(8,128)(2,1)}, u32[]{:S(2)}, u32[]{:S(2)}) collective-permute-start(bf16[64,4224]{1,0:T(8,128)(2,1)S(1)} %collective-permute-done.1.refs_2_), channel_id=1, source_target_pairs={{0,1},{2,0},{4,2},{6,4},{7,6},{5,7},{3,5},{1,3},{16,18},{18,20},{2... | collective-permute-start | bytes 1622024 | tf_op jit(solution)/shard_map/ppermute | solution.py:36
  34.5 15.2 %collective-permute-start.7 = (bf16[64,4224]{1,0:T(8,128)(2,1)}, bf16[64,4224]{1,0:T(8,128)(2,1)}, u32[]{:S(2)}, u32[]{:S(2)}) collective-permute-start(bf16[64,4224]{1,0:T(8,128)(2,1)} %collective-permute-done.2.refs_3_), channel_id=1, source_target_pairs={{0,2},{2,4},{4,6},{6,7},{7,5},{5,3},{3,1},{1,0},{16,17},{18,16},{2... | collective-permute-start | bytes 1622024 | tf_op jit(solution)/shard_map/ppermute | solution.py:36
  36.1 13.5 %collective-permute-start.8 = (bf16[64,4224]{1,0:T(8,128)(2,1)}, bf16[64,4224]{1,0:T(8,128)(2,1)}, u32[]{:S(2)}, u32[]{:S(2)}) collective-permute-start(bf16[64,4224]{1,0:T(8,128)(2,1)} %collective-permute-done.3.refs_0_.refs_4_), channel_id=1, source_target_pairs={{0,1},{2,0},{4,2},{6,4},{7,6},{5,7},{3,5},{1,3},{16,18},{18,20},{2... | collective-permute-start | bytes 1622024 | tf_op jit(solution)/shard_map/ppermute | solution.py:36
  36.7 1.1 copy-start
  36.7 1.7 %copy-start.1 = (bf16[384,2048]{1,0:T(8,128)(2,1)}, bf16[384,2048]{1,0:T(8,128)(2,1)S(1)}, u32[]{:S(2)}) copy-start(bf16[384,2048]{1,0:T(8,128)(2,1)S(1)} %collective-permute-done.5.refs_8_.refs_6_) | copy-start | bytes 4718596
  49.7 12.8 %collective-permute-start.10 = (bf16[64,4224]{1,0:T(8,128)(2,1)}, bf16[64,4224]{1,0:T(8,128)(2,1)S(1)}, u32[]{:S(2)}, u32[]{:S(2)}) collective-permute-start(bf16[64,4224]{1,0:T(8,128)(2,1)} %collective-permute-done.7.refs_0_.refs_6_), channel_id=1, source_target_pairs={{0,2},{2,4},{4,6},{6,7},{7,5},{5,3},{3,1},{1,0},{16,17},{18,16},{2... | collective-permute-start | bytes 1622024 | tf_op jit(solution)/shard_map/ppermute | solution.py:36
  60.8 12.1 %collective-permute-start.9 = (bf16[64,4096]{1,0:T(8,128)(2,1)}, bf16[64,4096]{1,0:T(8,128)(2,1)S(1)}, u32[]{:S(2)}, u32[]{:S(2)}) collective-permute-start(bf16[64,4096]{1,0:T(8,128)(2,1)} %get-tuple-element.62), channel_id=1, source_target_pairs={{0,2},{2,4},{4,6},{6,7},{7,5},{5,3},{3,1},{1,0},{16,17},{18,16},{2... | collective-permute-start | bytes 1572872 | tf_op jit(solution)/shard_map/ppermute | solution.py:36
  62.5 0.8 copy-start.3
  63.3 9.6 %copy-start.16 = (bf16[64,4096]{1,0:T(8,128)(2,1)S(1)}, bf16[64,4096]{1,0:T(8,128)(2,1)}, u32[]{:S(2)}) copy-start(bf16[64,4096]{1,0:T(8,128)(2,1)} %get-tuple-element.71) | copy-start | bytes 1572868
  72.8 1.8 %copy-start.17 = (bf16[64,4096]{1,0:T(8,128)(2,1)S(1)}, bf16[64,4096]{1,0:T(8,128)(2,1)}, u32[]{:S(2)}) copy-start(bf16[64,4096]{1,0:T(8,128)(2,1)} %get-tuple-element.69) | copy-start | bytes 1572868
  73.0 14.8 %collective-permute-start.12 = (bf16[64,4096]{1,0:T(8,128)(2,1)S(1)}, bf16[64,4096]{1,0:T(8,128)(2,1)S(1)}, u32[]{:S(2)}, u32[]{:S(2)}) collective-permute-start(bf16[64,4096]{1,0:T(8,128)(2,1)S(1)} %add_convert_fusion.3), channel_id=1, source_target_pairs={{0,2},{2,4},{4,6},{6,7},{7,5},{5,3},{3,1},{1,0},{16,17},{18,16},{2... | collective-permute-start | bytes 1572872 | tf_op jit(solution)/shard_map/ppermute | solution.py:36
  74.6 13.2 %collective-permute-start.11 = (bf16[64,4096]{1,0:T(8,128)(2,1)S(1)}, bf16[64,4096]{1,0:T(8,128)(2,1)S(1)}, u32[]{:S(2)}, u32[]{:S(2)}) collective-permute-start(bf16[64,4096]{1,0:T(8,128)(2,1)S(1)} %copy-done.17), channel_id=1, source_target_pairs={{0,1},{2,0},{4,2},{6,4},{7,6},{5,7},{3,5},{1,3},{16,18},{18,20},{2... | collective-permute-start | bytes 1572872 | tf_op jit(solution)/shard_map/ppermute | solution.py:36
  75.1 14.3 %copy-start.11 = (bf16[64,4096]{1,0:T(8,128)(2,1)S(1)}, bf16[64,4096]{1,0:T(8,128)(2,1)}, u32[]{:S(2)}) copy-start(bf16[64,4096]{1,0:T(8,128)(2,1)} %get-tuple-element.87) | copy-start | bytes 1572868
  82.8 9.4 %copy-start.12 = (bf16[64,4096]{1,0:T(8,128)(2,1)S(1)}, bf16[64,4096]{1,0:T(8,128)(2,1)}, u32[]{:S(2)}) copy-start(bf16[64,4096]{1,0:T(8,128)(2,1)} %get-tuple-element.85) | copy-start | bytes 1572868
  87.8 0.8 copy-start.15
  87.8 1.0 copy-start.13
  88.8 3.4 %copy-start.14 = (bf16[64,4096]{1,0:T(8,128)(2,1)S(1)}, bf16[64,4096]{1,0:T(8,128)(2,1)}, u32[]{:S(2)}) copy-start(bf16[64,4096]{1,0:T(8,128)(2,1)} %copy-done.13) | copy-start | bytes 1572868
  88.8 5.5 %collective-permute-start.15 = (bf16[384,2048]{1,0:T(8,128)(2,1)}, bf16[384,2048]{1,0:T(8,128)(2,1)S(1)}, u32[]{:S(2)}, u32[]{:S(2)}) collective-permute-start(bf16[384,2048]{1,0:T(8,128)(2,1)} %get-tuple-element.88), channel_id=1, source_target_pairs={{0,16},{16,0},{1,17},{17,1},{2,18},{18,2},{3,19},{19,3},{4,20},{20... | collective-permute-start | bytes 4718600 | tf_op jit(solution)/shard_map/ppermute | solution.py:41
  88.8 8.1 %collective-permute-start.16 = (bf16[384,2048]{1,0:T(8,128)(2,1)}, bf16[384,2048]{1,0:T(8,128)(2,1)S(1)}, u32[]{:S(2)}, u32[]{:S(2)}) collective-permute-start(bf16[384,2048]{1,0:T(8,128)(2,1)} %get-tuple-element.89), channel_id=1, source_target_pairs={{0,16},{16,0},{1,17},{17,1},{2,18},{18,2},{3,19},{19,3},{4,20},{20... | collective-permute-start | bytes 4718600 | tf_op jit(solution)/shard_map/ppermute | solution.py:41
  89.3 7.7 %collective-permute-start.17 = (bf16[384,2048]{1,0:T(8,128)(2,1)}, bf16[384,2048]{1,0:T(8,128)(2,1)}, u32[]{:S(2)}, u32[]{:S(2)}) collective-permute-start(bf16[384,2048]{1,0:T(8,128)(2,1)} %get-tuple-element.90), channel_id=1, source_target_pairs={{0,16},{16,0},{1,17},{17,1},{2,18},{18,2},{3,19},{19,3},{4,20},{20... | collective-permute-start | bytes 4718600 | tf_op jit(solution)/shard_map/ppermute | solution.py:41
  91.3 15.7 %collective-permute-start.14 = (bf16[64,4096]{1,0:T(8,128)(2,1)}, bf16[64,4096]{1,0:T(8,128)(2,1)}, u32[]{:S(2)}, u32[]{:S(2)}) collective-permute-start(bf16[64,4096]{1,0:T(8,128)(2,1)} %add_convert_fusion.1), channel_id=1, source_target_pairs={{0,2},{2,4},{4,6},{6,7},{7,5},{5,3},{3,1},{1,0},{16,17},{18,16},{2... | collective-permute-start | bytes 1572872 | tf_op jit(solution)/shard_map/ppermute | solution.py:36
  93.2 13.8 %copy-start.10 = (bf16[64,4096]{1,0:T(8,128)(2,1)S(1)}, bf16[64,4096]{1,0:T(8,128)(2,1)}, u32[]{:S(2)}) copy-start(bf16[64,4096]{1,0:T(8,128)(2,1)} %get-tuple-element.96) | copy-start | bytes 1572868
  93.2 13.8 %collective-permute-start.13 = (bf16[64,4096]{1,0:T(8,128)(2,1)}, bf16[64,4096]{1,0:T(8,128)(2,1)}, u32[]{:S(2)}, u32[]{:S(2)}) collective-permute-start(bf16[64,4096]{1,0:T(8,128)(2,1)} %add_convert_fusion.2), channel_id=1, source_target_pairs={{0,1},{2,0},{4,2},{6,4},{7,6},{5,7},{3,5},{1,3},{16,18},{18,20},{2... | collective-permute-start | bytes 1572872 | tf_op jit(solution)/shard_map/ppermute | solution.py:36
  94.3 2.8 %copy-start.4 = (bf16[384,2048]{1,0:T(8,128)(2,1)}, bf16[384,2048]{1,0:T(8,128)(2,1)S(1)}, u32[]{:S(2)}) copy-start(bf16[384,2048]{1,0:T(8,128)(2,1)S(1)} %collective-permute-done.15.refs_17_) | copy-start | bytes 4718596
  96.9 1.2 copy-start.5
  106.9 10.6 %copy-start.9 = (bf16[64,4096]{1,0:T(8,128)(2,1)S(1)}, bf16[64,4096]{1,0:T(8,128)(2,1)}, u32[]{:S(2)}) copy-start(bf16[64,4096]{1,0:T(8,128)(2,1)} %get-tuple-element.97) | copy-start | bytes 1572868
  107.0 19.9 %copy-start.2 = (bf16[64,4224]{1,0:T(8,128)(2,1)S(1)}, bf16[64,4224]{1,0:T(8,128)(2,1)}, u32[]{:S(2)}) copy-start(bf16[64,4224]{1,0:T(8,128)(2,1)} %pack_rows.1.refs_0_) | copy-start | bytes 1622020
  107.0 19.9 %copy-start.8 = (bf16[64,4096]{1,0:T(8,128)(2,1)S(1)}, bf16[64,4096]{1,0:T(8,128)(2,1)}, u32[]{:S(2)}) copy-start(bf16[64,4096]{1,0:T(8,128)(2,1)} %get-tuple-element.56) | copy-start | bytes 1572868
  108.3 9.2 %collective-permute-start.18 = (bf16[64,4096]{1,0:T(8,128)(2,1)S(1)}, bf16[64,4096]{1,0:T(8,128)(2,1)S(1)}, u32[]{:S(2)}, u32[]{:S(2)}) collective-permute-start(bf16[64,4096]{1,0:T(8,128)(2,1)S(1)} %add_convert_fusion), channel_id=1, source_target_pairs={{0,1},{2,0},{4,2},{6,4},{7,6},{5,7},{3,5},{1,3},{16,18},{18,20},{2... | collective-permute-start | bytes 1572872 | tf_op jit(solution)/shard_map/ppermute | solution.py:36
  117.6 6.4 %collective-permute-start.21 = (bf16[64,2048]{1,0:T(8,128)(2,1)S(1)}, bf16[64,2048]{1,0:T(8,128)(2,1)S(1)}, u32[]{:S(2)}, u32[]{:S(2)}) collective-permute-start(bf16[64,2048]{1,0:T(8,128)(2,1)S(1)} %get-tuple-element.103), channel_id=1, source_target_pairs={{0,1},{2,0},{4,2},{6,4},{7,6},{5,7},{3,5},{1,3},{16,18},{18,20},{2... | collective-permute-start | bytes 786440 | tf_op jit(solution)/shard_map/ppermute | solution.py:36
  117.7 9.2 %collective-permute-start.19 = (bf16[64,2048]{1,0:T(8,128)(2,1)S(1)}, bf16[64,2048]{1,0:T(8,128)(2,1)S(1)}, u32[]{:S(2)}, u32[]{:S(2)}) collective-permute-start(bf16[64,2048]{1,0:T(8,128)(2,1)S(1)} %get-tuple-element.104), channel_id=1, source_target_pairs={{0,1},{2,0},{4,2},{6,4},{7,6},{5,7},{3,5},{1,3},{16,18},{18,20},{2... | collective-permute-start | bytes 786440 | tf_op jit(solution)/shard_map/ppermute | solution.py:36
  128.2 9.3 %collective-permute-start.22 = (bf16[1,64,2048]{2,1,0:T(8,128)(2,1)S(1)}, bf16[1,64,2048]{2,1,0:T(8,128)(2,1)S(1)}, u32[]{:S(2)}, u32[]{:S(2)}) collective-permute-start(bf16[1,64,2048]{2,1,0:T(8,128)(2,1)S(1)} %get-tuple-element.101), channel_id=1, source_target_pairs={{0,8},{8,0},{1,9},{9,1},{2,10},{10,2},{3,11},{11,3},{4,12},{12,4},... | collective-permute-start | bytes 786440 | tf_op jit(solution)/shard_map/ppermute | solution.py:41
  129.8 10.7 %collective-permute-start.20 = (bf16[1,64,2048]{2,1,0:T(8,128)(2,1)S(1)}, bf16[1,64,2048]{2,1,0:T(8,128)(2,1)S(1)}, u32[]{:S(2)}, u32[]{:S(2)}) collective-permute-start(bf16[1,64,2048]{2,1,0:T(8,128)(2,1)S(1)} %get-tuple-element.102), channel_id=1, source_target_pairs={{0,8},{8,0},{1,9},{9,1},{2,10},{10,2},{3,11},{11,3},{4,12},{12,4},... | collective-permute-start | bytes 786440 | tf_op jit(solution)/shard_map/ppermute | solution.py:41

commit v4 on v3

v4 whole, which is shorter than its diff:
```python
import functools
import jax
import jax.numpy as jnp
from jax import lax
from jax.experimental import pallas as pl
from jax.experimental.pallas import tpu as pltpu
from jax.sharding import PartitionSpec as P

F32 = jnp.float32
BF16 = jnp.bfloat16
VMEM_BYTES = 60 * 2**20


def ring_order(peers):
    width = 1
    while 8 * width * width <= peers:
        width *= 2
    depth = peers // width
    if width == 1 or depth % 2:
        return list(range(peers))
    order = [z * width for z in range(depth)]
    for back, z in enumerate(reversed(range(depth))):
        columns = list(range(1, width))
        order += [z * width + x for x in (columns if back % 2 == 0 else reversed(columns))]
    return order


def ring_shift(value, by):
    peers = lax.axis_size("exp")
    order = ring_order(peers)
    pairs = []
    for rep in range(lax.axis_size("rep")):
        step = by if rep % 2 == 0 else -by
        for spot in range(peers):
            pairs.append((rep * peers + order[spot], rep * peers + order[(spot + step) % peers]))
    return lax.ppermute(value, ("rep", "exp"), pairs)


def from_behind(value, axis, by):
    peers = lax.axis_size(axis)
    return lax.ppermute(value, axis, [(i, (i + by) % peers) for i in range(peers)])


def dot(a, b, dims):
    return lax.dot_general(a, b, (dims, ((), ())), preferred_element_type=F32)


def whole():
    return pl.BlockSpec(memory_space=pltpu.VMEM)


def turned(value):
    rows, columns = value.shape
    wide = jnp.concatenate([value, jnp.zeros((rows, 128 - columns), F32)], axis=1)
    return wide.T[:columns]


def pack_kernel(experts, codes_ref, exps_ref, routes_ref, weight_ref, out_ref):
    tokens, width = codes_ref.shape
    blocks = exps_ref.shape[0]
    scales = jnp.exp2(exps_ref[...].astype(F32))
    scales = turned(jnp.concatenate([scales, jnp.zeros((128 - blocks, tokens), F32)], axis=0))
    per = width // blocks
    for b in range(blocks):
        cols = slice(b * per, (b + 1) * per)
        out_ref[:, cols] = (codes_ref[:, cols].astype(F32) * scales[:, b : b + 1]).astype(BF16)
    expert = lax.broadcasted_iota(jnp.int32, (experts, tokens), 0)
    table = jnp.zeros((experts, tokens), F32)
    for k in range(routes_ref.shape[0]):
        table += jnp.where(routes_ref[k : k + 1, :] == expert, weight_ref[k : k + 1, :], 0.0)
    high = table.astype(BF16).astype(F32)
    middle = (table - high).astype(BF16).astype(F32)
    low = table - high - middle
    extra = out_ref.shape[1] - width
    parts = [high, middle, low]
    if extra > 3 * experts:
        parts.append(jnp.zeros((extra - 3 * experts, tokens), F32))
    out_ref[:, width:] = turned(jnp.concatenate(parts, axis=0)).astype(BF16)


def row_copies(blocks, rows, sems, offset):
    tokens = blocks[0].shape[0]
    return [
        pltpu.make_async_copy(
            block.at[:, pl.ds(0, rows.shape[1])],
            rows.at[pl.ds(i * tokens, tokens)],
            sems.at[offset + i],
        )
        for i, block in enumerate(blocks)
    ]


def weight_copies(weights, buffer, sems):
    half = weights[0].shape[0]
    return [
        pltpu.make_async_copy(
            weights[side * 3 + kind],
            buffer.at[kind, pl.ds(side * half, half)],
            sems.at[2 * kind + side],
        )
        for kind in range(3)
        for side in range(2)
    ]


LAST = ((1,), (1,))
PLAIN = ((1,), (0,))
TILE = 256


def columns_of(width, body):
    def step(n, carry):
        body(pl.ds(pl.multiple_of(n * TILE, TILE), TILE))
        return carry

    lax.fori_loop(0, width // TILE, step, 0, unroll=2)


def forward_kernel(count, experts, local_experts, first_ref, *refs):
    blocks = refs[:count]
    weights = refs[count : count + 6]
    outs = refs[count + 6 : 2 * count + 6]
    hidden_out, swish_out, slope_out, rows, tables, buffer, left, sems = refs[2 * count + 6 :]
    units, width = buffer.shape[1:]
    tokens, lanes = blocks[0].shape[0], tables.shape[1]
    copies = weight_copies(weights, buffer, sems)
    loads = row_copies(blocks, rows, sems, 6)
    for i, block in enumerate(blocks):
        loads.append(
            pltpu.make_async_copy(
                block.at[:, pl.ds(width, lanes)],
                tables.at[pl.ds(i * tokens, tokens)],
                sems.at[6 + count + i],
            )
        )
    for copy in copies[:2] + loads + copies[2:]:
        copy.start()
    for copy in loads + copies[:2]:
        copy.wait()
    gate = dot(buffer[0], rows[...], LAST)
    table = tables[...].astype(F32).T
    expert_of = lax.rem(lax.broadcasted_iota(jnp.int32, table.shape, 0), experts)
    scales = [
        jnp.sum(jnp.where(expert_of == first_ref[0] + e, table, 0.0), axis=0, keepdims=True)
        for e in range(local_experts)
    ]
    half = units // 2
    unit = lax.rem(lax.broadcasted_iota(jnp.int32, (units, 1), 0), half)
    scale = scales[0]
    for e in range(1, local_experts):
        scale = jnp.where(unit >= e * (half // local_experts), scales[e], scale)
    copies[2].wait()
    copies[3].wait()
    up = dot(buffer[1], rows[...], LAST)
    sig = 1.0 / (1.0 + jnp.exp(-gate))
    swish = gate * sig
    weighted = swish * scale
    hidden = (weighted * up).astype(BF16)
    hidden_out[...] = hidden
    swish_out[...] = weighted
    slope_out[...] = up * sig * (1.0 + gate * (1.0 - sig)) * scale
    left[...] = hidden.T
    copies[4].wait()
    copies[5].wait()

    def column(at):
        output = dot(left[...], buffer[2, :, at], PLAIN).astype(BF16)
        for i, out in enumerate(outs):
            out[:, at] = output[i * tokens : (i + 1) * tokens]

    columns_of(width, column)


def backward_kernel(count, *refs):
    blocks = refs[:count]
    swish_ref, slope_ref = refs[count : count + 2]
    weights = refs[count + 2 : count + 8]
    outs = refs[count + 8 : 2 * count + 8]
    gate_out, up_out, rows, buffer, gate_left, up_left, sems = refs[2 * count + 8 :]
    width = buffer.shape[2]
    tokens = blocks[0].shape[0]
    copies = weight_copies(weights, buffer, sems)
    loads = row_copies(blocks, rows, sems, 6)
    for copy in copies[4:] + loads + copies[:4]:
        copy.start()
    for copy in loads + copies[4:]:
        copy.wait()
    back = dot(buffer[2], rows[...], LAST)
    gate_grad = (back * slope_ref[...]).astype(BF16)
    up_grad = (back * swish_ref[...]).astype(BF16)
    gate_out[...] = gate_grad
    up_out[...] = up_grad
    gate_left[...] = gate_grad.T
    up_left[...] = up_grad.T
    for copy in copies[:4]:
        copy.wait()

    def column(at):
        grad = dot(gate_left[...], buffer[0, :, at], PLAIN)
        grad = (grad + dot(up_left[...], buffer[1, :, at], PLAIN)).astype(BF16)
        for i, out in enumerate(outs):
            out[:, at] = grad[i * tokens : (i + 1) * tokens]

    columns_of(width, column)


def forward_call(blocks, weights, first, experts, local_experts, width):
    count, (tokens, wide) = len(blocks), blocks[0].shape
    units, rows = 2 * weights[0].shape[0], count * tokens
    results = pl.pallas_call(
        functools.partial(forward_kernel, count, experts, local_experts),
        out_shape=[jax.ShapeDtypeStruct((tokens, width), BF16)] * count
        + [jax.ShapeDtypeStruct((units, rows), BF16)]
        + [jax.ShapeDtypeStruct((units, rows), F32)] * 2,
        in_specs=[pl.BlockSpec(memory_space=pltpu.SMEM)]
        + [pl.BlockSpec(memory_space=pl.ANY)] * (count + 6),
        out_specs=[whole()] * (count + 3),
        scratch_shapes=[
            pltpu.VMEM((rows, width), BF16),
            pltpu.VMEM((rows, wide - width), BF16),
            pltpu.VMEM((3, units, width), BF16),
            pltpu.VMEM((rows, units), BF16),
            pltpu.SemaphoreType.DMA((6 + 2 * count,)),
        ],
        compiler_params=pltpu.CompilerParams(vmem_limit_bytes=VMEM_BYTES),
        cost_estimate=pl.CostEstimate(
            flops=3 * 2 * rows * units * width,
            bytes_accessed=6 * units * width + 4 * rows * width,
            transcendentals=rows * units,
        ),
        name="expert_forward",
    )(first, *blocks, *weights)
    return results[:count], results[count:]


def backward_call(blocks, saved, weights, width):
    count, tokens = len(blocks), blocks[0].shape[0]
    units, rows = 2 * weights[0].shape[0], count * tokens
    results = pl.pallas_call(
        functools.partial(backward_kernel, count),
        out_shape=[jax.ShapeDtypeStruct((tokens, width), BF16)] * count
        + [jax.ShapeDtypeStruct((units, rows), BF16)] * 2,
        in_specs=[pl.BlockSpec(memory_space=pl.ANY)] * count
        + [whole()] * 2
        + [pl.BlockSpec(memory_space=pl.ANY)] * 6,
        out_specs=[whole()] * (count + 2),
        scratch_shapes=[
            pltpu.VMEM((rows, width), BF16),
            pltpu.VMEM((3, units, width), BF16),
            pltpu.VMEM((rows, units), BF16),
            pltpu.VMEM((rows, units), BF16),
            pltpu.SemaphoreType.DMA((6 + count,)),
        ],
        compiler_params=pltpu.CompilerParams(vmem_limit_bytes=VMEM_BYTES),
        cost_estimate=pl.CostEstimate(
            flops=3 * 2 * rows * units * width,
            bytes_accessed=6 * units * width + 4 * rows * width,
            transcendentals=0,
        ),
        name="expert_backward",
    )(*blocks, *saved, *weights)
    return results[:count], results[count:]


def weight_kernel(groups, count, *refs):
    blocks = [refs[:count], refs[count : 2 * count]]
    kept = [refs[2 * count + g * 3 : 2 * count + g * 3 + 3] for g in range(groups)]
    outs = refs[-9:-3]
    across, rows, sems = refs[-3:]
    half, tile = outs[0].shape
    copies = row_copies(blocks[0], rows.at[0], sems, 0)
    copies += row_copies(blocks[1], rows.at[1], sems, count)

    @pl.when(pl.program_id(0) == 0)
    def _():
        for copy in copies:
            copy.start()
        for kind in range(3):
            start = 0
            for group in kept:
                size = group[kind].shape[1]
                across[kind, :, start : start + size] = group[kind][...]
                start += size
        for copy in copies:
            copy.wait()

    at = pl.ds(pl.multiple_of(pl.program_id(0) * tile, tile), tile)
    for kind in range(3):
        total = dot(across[kind], rows[kind // 2, :, at], PLAIN).astype(BF16)
        outs[kind][...] = total[:half]
        outs[3 + kind][...] = total[half:]


def weight_call(row_blocks, grad_blocks, kept, width):
    count = len(row_blocks)
    units = kept[0][0].shape[0]
    half, tile = units // 2, 2 * TILE
    total = count * row_blocks[0].shape[0]
    results = pl.pallas_call(
        functools.partial(weight_kernel, len(kept), count),
        grid=(width // tile,),
        out_shape=[jax.ShapeDtypeStruct((half, width), BF16)] * 6,
        in_specs=[pl.BlockSpec(memory_space=pl.ANY)] * (2 * count) + [whole()] * (3 * len(kept)),
        out_specs=[pl.BlockSpec((half, tile), lambda n: (0, n))] * 6,
        scratch_shapes=[
            pltpu.VMEM((3, units, total), BF16),
            pltpu.VMEM((2, total, width), BF16),
            pltpu.SemaphoreType.DMA((2 * count,)),
        ],
        compiler_params=pltpu.CompilerParams(vmem_limit_bytes=VMEM_BYTES),
        cost_estimate=pl.CostEstimate(
            flops=3 * 2 * total * units * width,
            bytes_accessed=4 * total * width + 12 * half * width,
            transcendentals=0,
        ),
        name="weight_grads",
    )(*row_blocks, *grad_blocks, *[k for group in kept for k in group])
    return results[:3], results[3:]


def add(a, b):
    return (a.astype(F32) + b.astype(F32)).astype(BF16)


def shards(
    row_codes, block_exponents, routes, route_weight, out_grad, gate_weight, up_weight, down_weight
):
    tokens, width = row_codes.shape[1:]
    local_experts, half_units = gate_weight.shape[1:3]
    half = local_experts * half_units
    peers = lax.axis_size("exp")
    experts = peers * local_experts
    lanes = -(-3 * experts // 128) * 128
    own = [w.reshape(half, width) for w in (gate_weight, up_weight, down_weight)]
    other = [from_behind(w, "rep", 1) for w in own]
    weights = own + other
    first = (lax.axis_index("exp") * local_experts).astype(jnp.int32).reshape(1)
    home = pl.pallas_call(
        functools.partial(pack_kernel, experts),
        out_shape=jax.ShapeDtypeStruct((tokens, width + lanes), BF16),
        in_specs=[whole()] * 4,
        out_specs=whole(),
        name="pack_rows",
    )(row_codes[0], block_exponents[0].T, routes[0].T, route_weight[0].T)

    tie = lax.optimization_barrier
    ahead, behind = peers // 2, peers // 2 - 1
    names = [("near", 0)]
    for k in range(1, ahead + 1):
        names += [("near", k), ("far", k)]
    names = names[: 2 * ahead]
    groups = [names[i : i + 4] for i in range(0, len(names), 4)]
    rows = {("near", 0): home, ("far", 0): home}
    grads = {("near", 0): out_grad[0], ("far", 0): out_grad[0]}
    outputs, back, saved, kept = {}, {}, [], []

    def spread(held, k, work):
        for name, step in (("near", 1), ("far", -1)):
            if (name, k) in names:
                held[name, k] = ring_shift(held[name, k - 1], step)
        done = work()
        here = [name for name in (("near", k), ("far", k)) if name in names]
        tied, done = tie(([held[name] for name in here], done))
        held.update(zip(here, tied))
        return done

    def forward(g):
        outs, keep = forward_call(
            [rows[name] for name in groups[g]], weights, first, experts, local_experts, width
        )
        outputs.update(zip(groups[g], outs))
        saved.append(keep)
        return keep

    def backward(g):
        outs, keep = backward_call(
            [grads[name] for name in groups[g]], saved[g][1:], weights, width
        )
        back.update(zip(groups[g], outs))
        kept.append([keep[0], keep[1], saved[g][0]])
        return keep

    for k in range(1, ahead + 1):
        for held, work, got in ((rows, forward, saved), (grads, backward, kept)):
            ready = k % 2 == 1 and k > 1
            done = spread(held, k, lambda: work(k // 2 - 1) if ready else None)
    forward(len(groups) - 1)
    backward(len(groups) - 1)

    def collect(partial, k, sums):
        near, far = sums
        near = ring_shift(partial["near", ahead] if near is None else near, -1)
        if k > 1:
            far = ring_shift(partial["far", behind] if far is None else far, 1)
        return near, far

    def join(partial, k, sums):
        near, far = sums
        if k > 1:
            near = add(near, partial["near", k - 1])
        if k > 2:
            far = add(far, partial["far", k - 2])
        return near, far

    out_sums = back_sums = (None, None)
    own = other_half = received = totals = None
    for k in range(ahead, 0, -1):
        out_sums = collect(outputs, k, out_sums)
        back_sums = collect(back, k, back_sums)
        if k == ahead:
            own, other_half = weight_call(
                [rows[name] for group in groups for name in group],
                [grads[name] for group in groups for name in group],
                kept,
                width,
            )
            back_sums, own, other_half = tie((back_sums, own, other_half))
            received = [from_behind(g, "rep", 1) for g in other_half]
        elif k == ahead - 1:
            totals = [add(a, b) for a, b in zip(own, received)]
            back_sums, totals = tie((back_sums, totals))
        out_sums = join(outputs, k, out_sums)
        back_sums = join(back, k, back_sums)
    results = []
    for base, partial, sums, step in (
        (home[:, :width], outputs, out_sums, 1),
        (out_grad[0], back, back_sums, -1),
    ):
        total = base.astype(F32) + partial["near", 0].astype(F32)
        total = total + sums[0].astype(F32) + sums[1].astype(F32)
        results.append(from_behind(total.astype(BF16)[None], "section", step))
    shape = (1, local_experts, half_units, width)
    return tuple(results) + tuple(t.reshape(shape) for t in totals)


def solution(mesh):
    tokens = P("section", ("rep", "exp"), None)
    weights = P("section", "exp", "rep", None)
    return jax.shard_map(
        shards,
        mesh=mesh,
        in_specs=(tokens,) * 5 + (weights,) * 3,
        out_specs=(tokens,) * 2 + (weights,) * 3,
        check_vma=False,
    )
```

time: 142 us -> 153 us (1.077)
  starting transfers between devices: 19.2 us -> 37.9 us
  waiting for transfers between devices: 61 us -> 55.2 us
  local copies, waits for them, and re-layouts: 5.91 us -> 3.81 us
    ppermute x15 -> x28, starting transfers between devices: 15.6 us -> 31.4 us  [ring_shift(): return lax.ppermute(value, ('rep', 'exp'), pairs)]
    ppermute x8, waiting for transfers between devices: 13 us -> 4.43 us  [from_behind(): lax.ppermute(value, axis, [(i, (i + by) % peers) for i in range(peers)])]
    ppermute x8, starting transfers between devices: 3.63 us -> 6.45 us  [from_behind(): lax.ppermute(value, axis, [(i, (i + by) % peers) for i in range(peers)])]
    ppermute x15 -> x28, waiting for transfers between devices: 48 us -> 50.7 us  [ring_shift(): return lax.ppermute(value, ('rep', 'exp'), pairs)]
    unnamed x38 -> x60, local copies, waits for them, and re-layouts: 5.91 us -> 3.81 us
    convert_element_type x5 -> x13, other arithmetic: 4.44 us -> 5.92 us  [add(): return (a.astype(F32) + b.astype(F32)).astype(BF16)]
  transfers between devices with their start and end apart: 23 -> 36, of which waited for: 11 -> 14; matrix products, arithmetic and copies ran while one was open for 2% -> 4% of each run, Pallas kernels for 35% -> 26%
where the time goes in v4:
time: 153 us
  waiting for transfers between devices  55.2 us (36%)
  Pallas kernels  48.9 us (32%)
  starting transfers between devices  37.9 us (25%)
  other arithmetic  6.2 us (4%)
  local copies, waits for them, and re-layouts  3.81 us (2%)
    ppermute x28, waiting for transfers between devices, ring_shift(): return lax.ppermute(value, ('rep', 'exp'), pairs)  50.7 us
    ppermute x28, starting transfers between devices, ring_shift(): return lax.ppermute(value, ('rep', 'exp'), pairs)  31.4 us
    pallas_call x2, Pallas kernels, backward_call(): pl.pallas_call(functools.partial(backward_kernel, count), out_shape=[jax....  18.1 us
    pallas_call x2, Pallas kernels, forward_call(): pl.pallas_call(functools.partial(forward_kernel, count, experts, local_ex...  18 us
    pallas_call x1, Pallas kernels, weight_call(): pl.pallas_call(functools.partial(weight_kernel, len(kept), count), grid=(...  10.6 us
    ppermute x8, starting transfers between devices, from_behind(): lax.ppermute(value, axis, [(i, (i + by) % peers) for i in range(peers)])  6.45 us
    convert_element_type x13, other arithmetic, add(): return (a.astype(F32) + b.astype(F32)).astype(BF16)  5.92 us
    ppermute x8, waiting for transfers between devices, from_behind(): lax.ppermute(value, axis, [(i, (i + by) % peers) for i in range(peers)])  4.43 us
  transfers between devices with their start and end apart: 36, of which 14 were waited for; matrix products, arithmetic and copies ran while one was open for 4% of the time, Pallas kernels for 26%

profile of v4, /device:TPU:0, one launch (start us, length us, event | category | flops | bytes accessed | tf_op | source)
XLA Modules:
  0.0 152.9 jit_solution(18258319063759200068)
XLA Ops:
  0.6 0.5 collective-permute-start.4
  1.1 0.1 collective-permute-start.5
  1.2 0.4 collective-permute-start.6
  1.7 2.1 %pack_rows.1.refs_0_ = bf16[64,2176]{1,0:T(8,128)(2,1)} custom-call(bf16[64,2048]{1,0:T(8,128)(2,1)} %bitcast.45, s32[16,64]{1,0:T(8,128)} %bitcast.46, s32[8,64]{1,0:T(8,128)} %bitcast.47, f32[8,64]{1,0:T(8,128)} %bitcast.48), custom_call_target="tpu_custom_call" | custom-call | tf_op jit(solution)/shard_map/pack_rows/pallas_call | solution.py:338
  3.7 2.6 %collective-permute-start.1 = (bf16[64,2176]{1,0:T(8,128)(2,1)}, bf16[64,2176]{1,0:T(8,128)(2,1)S(1)}, u32[]{:S(2)}, u32[]{:S(2)}) collective-permute-start(bf16[64,2176]{1,0:T(8,128)(2,1)} %pack_rows.1.refs_0_), channel_id=1, source_target_pairs={{0,1},{2,0},{4,2},{6,4},{7,6},{5,7},{3,5},{1,3},{16,18},{18,20},{2... | collective-permute-start | bytes 835592 | tf_op jit(solution)/shard_map/ppermute | solution.py:36
  6.3 0.1 collective-permute-start
  6.4 6.9 %collective-permute-done.1.refs_2_ = bf16[64,2176]{1,0:T(8,128)(2,1)S(1)} collective-permute-done((bf16[64,2176]{1,0:T(8,128)(2,1)}, bf16[64,2176]{1,0:T(8,128)(2,1)S(1)}, u32[]{:S(2)}, u32[]{:S(2)}) %collective-permute-start.1) | collective-permute-done | bytes 278560 | tf_op jit(solution)/shard_map/ppermute | solution.py:36
  13.3 2.4 %collective-permute-start.19 = (bf16[64,2048]{1,0:T(8,128)(2,1)}, bf16[64,2048]{1,0:T(8,128)(2,1)S(1)}, u32[]{:S(2)}, u32[]{:S(2)}) collective-permute-start(bf16[64,2048]{1,0:T(8,128)(2,1)} %bitcast.41), channel_id=1, source_target_pairs={{0,1},{2,0},{4,2},{6,4},{7,6},{5,7},{3,5},{1,3},{16,18},{18,20},{2... | collective-permute-start | bytes 786440 | tf_op jit(solution)/shard_map/ppermute | solution.py:36
  15.6 6.8 %collective-permute-done.19.refs_2_.refs_10_ = bf16[64,2048]{1,0:T(8,128)(2,1)S(1)} collective-permute-done((bf16[64,2048]{1,0:T(8,128)(2,1)}, bf16[64,2048]{1,0:T(8,128)(2,1)S(1)}, u32[]{:S(2)}, u32[]{:S(2)}) %collective-permute-start.19) | collective-permute-done | bytes 262176 | tf_op jit(solution)/shard_map/ppermute | solution.py:36
  22.4 2.0 %collective-permute-start.2 = (bf16[64,2176]{1,0:T(8,128)(2,1)S(1)}, bf16[64,2176]{1,0:T(8,128)(2,1)}, u32[]{:S(2)}, u32[]{:S(2)}) collective-permute-start(bf16[64,2176]{1,0:T(8,128)(2,1)S(1)} %collective-permute-done.refs_1_), channel_id=1, source_target_pairs={{0,2},{2,4},{4,6},{6,7},{7,5},{5,3},{3,1},{1,0},{16,17},{18,16},{2... | collective-permute-start | bytes 835592 | tf_op jit(solution)/shard_map/ppermute | solution.py:36
  24.4 0.4 collective-permute-start.3
  24.9 6.4 %collective-permute-done.2.refs_3_ = bf16[64,2176]{1,0:T(8,128)(2,1)} collective-permute-done((bf16[64,2176]{1,0:T(8,128)(2,1)S(1)}, bf16[64,2176]{1,0:T(8,128)(2,1)}, u32[]{:S(2)}, u32[]{:S(2)}) %collective-permute-start.2) | collective-permute-done | bytes 278560 | tf_op jit(solution)/shard_map/ppermute | solution.py:36
  31.3 1.7 %collective-permute-start.20 = (bf16[64,2048]{1,0:T(8,128)(2,1)S(1)}, bf16[64,2048]{1,0:T(8,128)(2,1)S(1)}, u32[]{:S(2)}, u32[]{:S(2)}) collective-permute-start(bf16[64,2048]{1,0:T(8,128)(2,1)S(1)} %collective-permute-done.18.refs_1_.refs_9_), channel_id=1, source_target_pairs={{0,2},{2,4},{4,6},{6,7},{7,5},{5,3},{3,1},{1,0},{16,17},{18,16},{2... | collective-permute-start | bytes 786440 | tf_op jit(solution)/shard_map/ppermute | solution.py:36
  32.9 0.5 collective-permute-done.3.refs_0_.refs_4_
  33.4 0.2 collective-permute-start.21
  33.6 4.8 %collective-permute-done.20.refs_3_.refs_11_ = bf16[64,2048]{1,0:T(8,128)(2,1)S(1)} collective-permute-done((bf16[64,2048]{1,0:T(8,128)(2,1)S(1)}, bf16[64,2048]{1,0:T(8,128)(2,1)S(1)}, u32[]{:S(2)}, u32[]{:S(2)}) %collective-permute-start.20) | collective-permute-done | bytes 262176 | tf_op jit(solution)/shard_map/ppermute | solution.py:36
  38.4 1.7 %collective-permute-start.7 = (bf16[64,2176]{1,0:T(8,128)(2,1)}, bf16[64,2176]{1,0:T(8,128)(2,1)}, u32[]{:S(2)}, u32[]{:S(2)}) collective-permute-start(bf16[64,2176]{1,0:T(8,128)(2,1)} %collective-permute-done.2.refs_3_), channel_id=1, source_target_pairs={{0,2},{2,4},{4,6},{6,7},{7,5},{5,3},{3,1},{1,0},{16,17},{18,16},{2... | collective-permute-start | bytes 835592 | tf_op jit(solution)/shard_map/ppermute | solution.py:36
  40.1 2.4 %collective-permute-done.21.refs_0_.refs_12_ = bf16[64,2048]{1,0:T(8,128)(2,1)S(1)} collective-permute-done((bf16[64,2048]{1,0:T(8,128)(2,1)S(1)}, bf16[64,2048]{1,0:T(8,128)(2,1)S(1)}, u32[]{:S(2)}, u32[]{:S(2)}) %collective-permute-start.21) | collective-permute-done | bytes 262176 | tf_op jit(solution)/shard_map/ppermute | solution.py:36
  42.5 0.2 collective-permute-start.8
  42.8 0.5 copy-done.21
  43.3 2.0 %collective-permute-start.22 = (bf16[64,2048]{1,0:T(8,128)(2,1)}, bf16[64,2048]{1,0:T(8,128)(2,1)S(1)}, u32[]{:S(2)}, u32[]{:S(2)}) collective-permute-start(bf16[64,2048]{1,0:T(8,128)(2,1)} %copy-done.20), channel_id=1, source_target_pairs={{0,2},{2,4},{4,6},{6,7},{7,5},{5,3},{3,1},{1,0},{16,17},{18,16},{2... | collective-permute-start | bytes 786440 | tf_op jit(solution)/shard_map/ppermute | solution.py:36
  45.3 1.1 copy-done.1
  46.4 9.0 %expert_forward.2 = (bf16[64,2048]{1,0:T(8,128)(2,1)}, bf16[64,2048]{1,0:T(8,128)(2,1)}, bf16[64,2048]{1,0:T(8,128)(2,1)}, bf16[64,2048]{1,0:T(8,128)(2,1)}, bf1...) custom-call(s32[1]{0:T(128)} %bitcast.7.first_ref, bf16[64,2176]{1,0:T(8,128)(2,1)} %pack_rows.1.refs_0_, ...), custom_call_target="tpu_custom_call" | custom-call | flops 2415919104 | bytes 11534336 | tf_op jit(solution)/shard_map/expert_forward/pallas_call | solution.py:210
  55.4 2.1 %collective-permute-start.9 = (bf16[64,2176]{1,0:T(8,128)(2,1)}, bf16[64,2176]{1,0:T(8,128)(2,1)S(1)}, u32[]{:S(2)}, u32[]{:S(2)}) collective-permute-start(bf16[64,2176]{1,0:T(8,128)(2,1)} %collective-permute-done.7.refs_1_.refs_5_), channel_id=1, source_target_pairs={{0,2},{2,4},{4,6},{6,7},{7,5},{5,3},{3,1},{1,0},{16,17},{18,16},{2... | collective-permute-start | bytes 835592 | tf_op jit(solution)/shard_map/ppermute | solution.py:36
  57.5 9.1 %expert_backward.2 = (bf16[64,2048]{1,0:T(8,128)(2,1)}, bf16[64,2048]{1,0:T(8,128)(2,1)}, bf16[64,2048]{1,0:T(8,128)(2,1)}, bf16[64,2048]{1,0:T(8,128)(2,1)}, bf...) custom-call(bf16[64,2048]{1,0:T(8,128)(2,1)} %bitcast.43, bf16[64,2048]{1,0:T(8,128)(2,1)} %copy-done.19, ...), custom_call_target="tpu_custom_call" | custom-call | flops 2415919104 | bytes 11534336 | tf_op jit(solution)/shard_map/expert_backward/pallas_call | solution.py:239
  66.7 1.5 collective-permute-start.24
  68.1 5.0 %collective-permute-done.24.refs_3_.refs_15_ = bf16[64,2048]{1,0:T(8,128)(2,1)S(1)} collective-permute-done((bf16[64,2048]{1,0:T(8,128)(2,1)S(1)}, bf16[64,2048]{1,0:T(8,128)(2,1)S(1)}, u32[]{:S(2)}, u32[]{:S(2)}) %collective-permute-start.24) | collective-permute-done | bytes 262176 | tf_op jit(solution)/shard_map/ppermute | solution.py:36
  73.1 0.7 copy-done.9
  73.8 9.0 %expert_forward.3 = (bf16[64,2048]{1,0:T(8,128)(2,1)}, bf16[64,2048]{1,0:T(8,128)(2,1)}, bf16[64,2048]{1,0:T(8,128)(2,1)}, bf16[64,2048]{1,0:T(8,128)(2,1)}, bf1...) custom-call(s32[1]{0:T(128)} %bitcast.7.first_ref, ...), custom_call_target="tpu_custom_call" | custom-call | flops 2415919104 | bytes 11534336 | tf_op jit(solution)/shard_map/expert_forward/pallas_call | solution.py:210
  83.0 2.0 %collective-permute-start.14 = (bf16[64,2048]{1,0:T(8,128)(2,1)}, bf16[64,2048]{1,0:T(8,128)(2,1)S(1)}, u32[]{:S(2)}, u32[]{:S(2)}) collective-permute-start(bf16[64,2048]{1,0:T(8,128)(2,1)} %get-tuple-element.76), channel_id=1, source_target_pairs={{0,2},{2,4},{4,6},{6,7},{7,5},{5,3},{3,1},{1,0},{16,17},{18,16},{2... | collective-permute-start | bytes 786440 | tf_op jit(solution)/shard_map/ppermute | solution.py:36
  85.0 9.0 %expert_backward.3 = (bf16[64,2048]{1,0:T(8,128)(2,1)}, bf16[64,2048]{1,0:T(8,128)(2,1)}, bf16[64,2048]{1,0:T(8,128)(2,1)}, bf16[64,2048]{1,0:T(8,128)(2,1)}, bf...) custom-call(bf16[64,2048]{1,0:T(8,128)(2,1)} %copy-done.21, bf16[64,2048]{1,0:T(8,128)(2,1)} %copy-done.22, ...), custom_call_target="tpu_custom_call" | custom-call | flops 2415919104 | bytes 11534336 | tf_op jit(solution)/shard_map/expert_backward/pallas_call | solution.py:239
  94.0 0.1 collective-permute-start.25
  94.1 2.0 %collective-permute-start.26 = (bf16[64,2048]{1,0:T(8,128)(2,1)}, bf16[64,2048]{1,0:T(8,128)(2,1)S(1)}, u32[]{:S(2)}, u32[]{:S(2)}) collective-permute-start(bf16[64,2048]{1,0:T(8,128)(2,1)} %get-tuple-element.91), channel_id=1, source_target_pairs={{0,2},{2,4},{4,6},{6,7},{7,5},{5,3},{3,1},{1,0},{16,17},{18,16},{2... | collective-permute-start | bytes 786440 | tf_op jit(solution)/shard_map/ppermute | solution.py:36
  96.1 10.6 %weight_grads.1 = (bf16[384,2048]{1,0:T(8,128)(2,1)}, bf16[384,2048]{1,0:T(8,128)(2,1)}, bf16[384,2048]{1,0:T(8,128)(2,1)}, bf16[384,2048]{1,0:T(8,128)(2,1)}, b...) custom-call(bf16[64,2176]{1,0:T(8,128)(2,1)} %pack_rows.1.refs_0_, bf16[64,2176]{1,0:T(8,128)(2,1)} %copy-done.8, ...), custom_call_target="tpu_custom_call" | custom-call | flops 4831838208 | bytes 13631488 | tf_op jit(solution)/shard_map/weight_grads/pallas_call | solution.py:299
  106.9 0.1 collective-permute-start.11
  107.1 2.0 %collective-permute-start.15 = (bf16[64,2048]{1,0:T(8,128)(2,1)S(1)}, bf16[64,2048]{1,0:T(8,128)(2,1)S(1)}, u32[]{:S(2)}, u32[]{:S(2)}) collective-permute-start(bf16[64,2048]{1,0:T(8,128)(2,1)S(1)} %add_convert_fusion.11), channel_id=1, source_target_pairs={{0,2},{2,4},{4,6},{6,7},{7,5},{5,3},{3,1},{1,0},{16,17},{18,16},{2... | collective-permute-start | bytes 786440 | tf_op jit(solution)/shard_map/ppermute | solution.py:36
  109.2 1.5 collective-permute-start.28
  110.7 0.9 collective-permute-start.27
  111.6 1.7 %collective-permute-done.11 = bf16[64,2048]{1,0:T(8,128)(2,1)S(1)} collective-permute-done((bf16[64,2048]{1,0:T(8,128)(2,1)S(1)}, bf16[64,2048]{1,0:T(8,128)(2,1)S(1)}, u32[]{:S(2)}, u32[]{:S(2)}) %collective-permute-start.11) | collective-permute-done | bytes 262176 | tf_op jit(solution)/shard_map/ppermute | solution.py:36
  113.3 0.1 add_convert_fusion.13
  113.4 0.1 collective-permute-done.15
  113.5 0.9 collective-permute-start.12
  114.3 0.1 add_convert_fusion.10
  114.4 5.7 %collective-permute-done.12 = bf16[64,2048]{1,0:T(8,128)(2,1)S(1)} collective-permute-done((bf16[64,2048]{1,0:T(8,128)(2,1)S(1)}, bf16[64,2048]{1,0:T(8,128)(2,1)S(1)}, u32[]{:S(2)}, u32[]{:S(2)}) %collective-permute-start.12) | collective-permute-done | bytes 262176 | tf_op jit(solution)/shard_map/ppermute | solution.py:36
  120.1 1.6 %collective-permute-start.31 = (bf16[384,2048]{1,0:T(8,128)(2,1)S(1)}, bf16[384,2048]{1,0:T(8,128)(2,1)S(1)}, u32[]{:S(2)}, u32[]{:S(2)}) collective-permute-start(bf16[384,2048]{1,0:T(8,128)(2,1)S(1)} %copy-done.28), channel_id=1, source_target_pairs={{0,16},{16,0},{1,17},{17,1},{2,18},{18,2},{3,19},{19,3},{4,20},{20... | collective-permute-start | bytes 4718600 | tf_op jit(solution)/shard_map/ppermute | solution.py:41
  121.8 2.0 %collective-permute-start.16 = (bf16[64,2048]{1,0:T(8,128)(2,1)S(1)}, bf16[64,2048]{1,0:T(8,128)(2,1)S(1)}, u32[]{:S(2)}, u32[]{:S(2)}) collective-permute-start(bf16[64,2048]{1,0:T(8,128)(2,1)S(1)} %add_convert_fusion.10), channel_id=1, source_target_pairs={{0,2},{2,4},{4,6},{6,7},{7,5},{5,3},{3,1},{1,0},{16,17},{18,16},{2... | collective-permute-start | bytes 786440 | tf_op jit(solution)/shard_map/ppermute | solution.py:36
  123.8 1.8 %add_convert_fusion.2 = bf16[384,2048]{1,0:T(8,128)(2,1)} fusion(bf16[384,2048]{1,0:T(8,128)(2,1)S(1)} %collective-permute-done.29, bf16[384,2048]{1,0:T(8,128)(2,1)S(1)} %copy-done.5), kind=kLoop, calls=%fused_computation.2 | loop fusion | flops 3145728 | bytes 4718592 | tf_op jit(solution)/shard_map/convert_element_type | solution.py:322
  125.6 0.1 collective-permute-start.13
  125.7 1.8 %add_convert_fusion.1 = bf16[384,2048]{1,0:T(8,128)(2,1)} fusion(bf16[384,2048]{1,0:T(8,128)(2,1)S(1)} %collective-permute-done.30, bf16[384,2048]{1,0:T(8,128)(2,1)S(1)} %copy-done.4), kind=kLoop, calls=%fused_computation.1 | loop fusion | flops 3145728 | bytes 4718592 | tf_op jit(solution)/shard_map/convert_element_type | solution.py:322
  127.4 1.8 %add_convert_fusion = bf16[384,2048]{1,0:T(8,128)(2,1)} fusion(bf16[384,2048]{1,0:T(8,128)(2,1)S(1)} %collective-permute-done.31, bf16[384,2048]{1,0:T(8,128)(2,1)S(1)} %copy-done.3), kind=kLoop, calls=%fused_computation | loop fusion | flops 3145728 | bytes 4718592 | tf_op jit(solution)/shard_map/convert_element_type | solution.py:322
  129.3 0.9 collective-permute-start.32
  130.3 1.2 collective-permute-start.34
  131.5 6.7 %collective-permute-done.32 = bf16[64,2048]{1,0:T(8,128)(2,1)S(1)} collective-permute-done((bf16[64,2048]{1,0:T(8,128)(2,1)S(1)}, bf16[64,2048]{1,0:T(8,128)(2,1)S(1)}, u32[]{:S(2)}, u32[]{:S(2)}) %collective-permute-start.32) | collective-permute-done | bytes 262176 | tf_op jit(solution)/shard_map/ppermute | solution.py:36
  138.3 0.1 add_convert_fusion.5
  138.3 0.9 collective-permute-start.33
  139.3 0.1 fusion
  139.4 1.6 %collective-permute-start.17 = (bf16[1,64,2048]{2,1,0:T(8,128)(2,1)S(1)}, bf16[1,64,2048]{2,1,0:T(8,128)(2,1)S(1)}, u32[]{:S(2)}, u32[]{:S(2)}) collective-permute-start(bf16[1,64,2048]{2,1,0:T(8,128)(2,1)S(1)} %fusion), channel_id=1, source_target_pairs={{0,8},{8,0},{1,9},{9,1},{2,10},{10,2},{3,11},{11,3},{4,12},{12,4},... | collective-permute-start | bytes 786440 | tf_op jit(solution)/shard_map/ppermute | solution.py:41
  141.1 3.7 %collective-permute-done.33 = bf16[64,2048]{1,0:T(8,128)(2,1)S(1)} collective-permute-done((bf16[64,2048]{1,0:T(8,128)(2,1)S(1)}, bf16[64,2048]{1,0:T(8,128)(2,1)S(1)}, u32[]{:S(2)}, u32[]{:S(2)}) %collective-permute-start.33) | collective-permute-done | bytes 262176 | tf_op jit(solution)/shard_map/ppermute | solution.py:36
  144.8 0.1 fusion.1
  144.9 2.2 %collective-permute-start.35 = (bf16[1,64,2048]{2,1,0:T(8,128)(2,1)S(1)}, bf16[1,64,2048]{2,1,0:T(8,128)(2,1)S(1)}, u32[]{:S(2)}, u32[]{:S(2)}) collective-permute-start(bf16[1,64,2048]{2,1,0:T(8,128)(2,1)S(1)} %fusion.1), channel_id=1, source_target_pairs={{0,8},{8,0},{1,9},{9,1},{2,10},{10,2},{3,11},{11,3},{4,12},{12,4},... | collective-permute-start | bytes 786440 | tf_op jit(solution)/shard_map/ppermute | solution.py:41
  147.1 1.3 collective-permute-done.17
  148.4 3.1 %collective-permute-done.35 = bf16[1,64,2048]{2,1,0:T(8,128)(2,1)S(1)} collective-permute-done((bf16[1,64,2048]{2,1,0:T(8,128)(2,1)S(1)}, bf16[1,64,2048]{2,1,0:T(8,128)(2,1)S(1)}, u32[]{:S(2)}, u32[]{:S(2)}) %collective-permute-start.35) | collective-permute-done | bytes 262176 | tf_op jit(solution)/shard_map/ppermute | solution.py:41
  151.5 0.7 copy.15
  152.2 0.7 copy.16
  (89 shorter events, 0.7 us)
Async XLA Ops:
  0.6 42.6 %collective-permute-start.4 = (bf16[384,2048]{1,0:T(8,128)(2,1)}, bf16[384,2048]{1,0:T(8,128)(2,1)S(1)}, u32[]{:S(2)}, u32[]{:S(2)}) collective-permute-start(bf16[384,2048]{1,0:T(8,128)(2,1)} %bitcast.23), channel_id=1, source_target_pairs={{0,16},{16,0},{1,17},{17,1},{2,18},{18,2},{3,19},{19,3},{4,20},{20... | collective-permute-start | bytes 4718600 | tf_op jit(solution)/shard_map/ppermute | solution.py:41
  1.1 44.1 %collective-permute-start.5 = (bf16[384,2048]{1,0:T(8,128)(2,1)}, bf16[384,2048]{1,0:T(8,128)(2,1)S(1)}, u32[]{:S(2)}, u32[]{:S(2)}) collective-permute-start(bf16[384,2048]{1,0:T(8,128)(2,1)} %bitcast.28), channel_id=1, source_target_pairs={{0,16},{16,0},{1,17},{17,1},{2,18},{18,2},{3,19},{19,3},{4,20},{20... | collective-permute-start | bytes 4718600 | tf_op jit(solution)/shard_map/ppermute | solution.py:41
  1.2 44.1 %collective-permute-start.6 = (bf16[384,2048]{1,0:T(8,128)(2,1)}, bf16[384,2048]{1,0:T(8,128)(2,1)}, u32[]{:S(2)}, u32[]{:S(2)}) collective-permute-start(bf16[384,2048]{1,0:T(8,128)(2,1)} %bitcast.33), channel_id=1, source_target_pairs={{0,16},{16,0},{1,17},{17,1},{2,18},{18,2},{3,19},{19,3},{4,20},{20... | collective-permute-start | bytes 4718600 | tf_op jit(solution)/shard_map/ppermute | solution.py:41
  3.7 9.5 %collective-permute-start.1 = (bf16[64,2176]{1,0:T(8,128)(2,1)}, bf16[64,2176]{1,0:T(8,128)(2,1)S(1)}, u32[]{:S(2)}, u32[]{:S(2)}) collective-permute-start(bf16[64,2176]{1,0:T(8,128)(2,1)} %pack_rows.1.refs_0_), channel_id=1, source_target_pairs={{0,1},{2,0},{4,2},{6,4},{7,6},{5,7},{3,5},{1,3},{16,18},{18,20},{2... | collective-permute-start | bytes 835592 | tf_op jit(solution)/shard_map/ppermute | solution.py:36
  6.3 9.3 %collective-permute-start = (bf16[64,2176]{1,0:T(8,128)(2,1)}, bf16[64,2176]{1,0:T(8,128)(2,1)S(1)}, u32[]{:S(2)}, u32[]{:S(2)}) collective-permute-start(bf16[64,2176]{1,0:T(8,128)(2,1)} %pack_rows.1.refs_0_), channel_id=1, source_target_pairs={{0,2},{2,4},{4,6},{6,7},{7,5},{5,3},{3,1},{1,0},{16,17},{18,16},{2... | collective-permute-start | bytes 835592 | tf_op jit(solution)/shard_map/ppermute | solution.py:36
  13.2 32.0 %copy-start.7 = (bf16[64,2176]{1,0:T(8,128)(2,1)}, bf16[64,2176]{1,0:T(8,128)(2,1)S(1)}, u32[]{:S(2)}) copy-start(bf16[64,2176]{1,0:T(8,128)(2,1)S(1)} %collective-permute-done.1.refs_2_) | copy-start | bytes 835588
  13.3 9.2 %collective-permute-start.19 = (bf16[64,2048]{1,0:T(8,128)(2,1)}, bf16[64,2048]{1,0:T(8,128)(2,1)S(1)}, u32[]{:S(2)}, u32[]{:S(2)}) collective-permute-start(bf16[64,2048]{1,0:T(8,128)(2,1)} %bitcast.41), channel_id=1, source_target_pairs={{0,1},{2,0},{4,2},{6,4},{7,6},{5,7},{3,5},{1,3},{16,18},{18,20},{2... | collective-permute-start | bytes 786440 | tf_op jit(solution)/shard_map/ppermute | solution.py:36
  15.6 17.8 %copy-start.8 = (bf16[64,2176]{1,0:T(8,128)(2,1)}, bf16[64,2176]{1,0:T(8,128)(2,1)S(1)}, u32[]{:S(2)}) copy-start(bf16[64,2176]{1,0:T(8,128)(2,1)S(1)} %collective-permute-done.refs_1_) | copy-start | bytes 835588
  15.6 8.8 %collective-permute-start.18 = (bf16[64,2048]{1,0:T(8,128)(2,1)}, bf16[64,2048]{1,0:T(8,128)(2,1)S(1)}, u32[]{:S(2)}, u32[]{:S(2)}) collective-permute-start(bf16[64,2048]{1,0:T(8,128)(2,1)} %bitcast.42), channel_id=1, source_target_pairs={{0,2},{2,4},{4,6},{6,7},{7,5},{5,3},{3,1},{1,0},{16,17},{18,16},{2... | collective-permute-start | bytes 786440 | tf_op jit(solution)/shard_map/ppermute | solution.py:36
  22.4 11.2 %copy-start.17 = (bf16[64,2048]{1,0:T(8,128)(2,1)}, bf16[64,2048]{1,0:T(8,128)(2,1)S(1)}, u32[]{:S(2)}) copy-start(bf16[64,2048]{1,0:T(8,128)(2,1)S(1)} %collective-permute-done.19.refs_2_.refs_10_) | copy-start | bytes 786436
  22.4 8.8 %collective-permute-start.2 = (bf16[64,2176]{1,0:T(8,128)(2,1)S(1)}, bf16[64,2176]{1,0:T(8,128)(2,1)}, u32[]{:S(2)}, u32[]{:S(2)}) collective-permute-start(bf16[64,2176]{1,0:T(8,128)(2,1)S(1)} %collective-permute-done.refs_1_), channel_id=1, source_target_pairs={{0,2},{2,4},{4,6},{6,7},{7,5},{5,3},{3,1},{1,0},{16,17},{18,16},{2... | collective-permute-start | bytes 835592 | tf_op jit(solution)/shard_map/ppermute | solution.py:36
  24.4 18.1 %copy-start.19 = (bf16[64,2048]{1,0:T(8,128)(2,1)}, bf16[64,2048]{1,0:T(8,128)(2,1)S(1)}, u32[]{:S(2)}) copy-start(bf16[64,2048]{1,0:T(8,128)(2,1)S(1)} %collective-permute-done.18.refs_1_.refs_9_) | copy-start | bytes 786436
  24.4 9.0 %collective-permute-start.3 = (bf16[64,2176]{1,0:T(8,128)(2,1)S(1)}, bf16[64,2176]{1,0:T(8,128)(2,1)}, u32[]{:S(2)}, u32[]{:S(2)}) collective-permute-start(bf16[64,2176]{1,0:T(8,128)(2,1)S(1)} %collective-permute-done.1.refs_2_), channel_id=1, source_target_pairs={{0,1},{2,0},{4,2},{6,4},{7,6},{5,7},{3,5},{1,3},{16,18},{18,20},{2... | collective-permute-start | bytes 835592 | tf_op jit(solution)/shard_map/ppermute | solution.py:36
  31.3 7.2 %collective-permute-start.20 = (bf16[64,2048]{1,0:T(8,128)(2,1)S(1)}, bf16[64,2048]{1,0:T(8,128)(2,1)S(1)}, u32[]{:S(2)}, u32[]{:S(2)}) collective-permute-start(bf16[64,2048]{1,0:T(8,128)(2,1)S(1)} %collective-permute-done.18.refs_1_.refs_9_), channel_id=1, source_target_pairs={{0,2},{2,4},{4,6},{6,7},{7,5},{5,3},{3,1},{1,0},{16,17},{18,16},{2... | collective-permute-start | bytes 786440 | tf_op jit(solution)/shard_map/ppermute | solution.py:36
  33.4 9.1 %collective-permute-start.21 = (bf16[64,2048]{1,0:T(8,128)(2,1)S(1)}, bf16[64,2048]{1,0:T(8,128)(2,1)S(1)}, u32[]{:S(2)}, u32[]{:S(2)}) collective-permute-start(bf16[64,2048]{1,0:T(8,128)(2,1)S(1)} %collective-permute-done.19.refs_2_.refs_10_), channel_id=1, source_target_pairs={{0,1},{2,0},{4,2},{6,4},{7,6},{5,7},{3,5},{1,3},{16,18},{18,20},{2... | collective-permute-start | bytes 786440 | tf_op jit(solution)/shard_map/ppermute | solution.py:36
  38.4 4.4 %copy-start.20 = (bf16[64,2048]{1,0:T(8,128)(2,1)}, bf16[64,2048]{1,0:T(8,128)(2,1)S(1)}, u32[]{:S(2)}) copy-start(bf16[64,2048]{1,0:T(8,128)(2,1)S(1)} %collective-permute-done.20.refs_3_.refs_11_) | copy-start | bytes 786436
  38.4 17.0 %collective-permute-start.7 = (bf16[64,2176]{1,0:T(8,128)(2,1)}, bf16[64,2176]{1,0:T(8,128)(2,1)}, u32[]{:S(2)}, u32[]{:S(2)}) collective-permute-start(bf16[64,2176]{1,0:T(8,128)(2,1)} %collective-permute-done.2.refs_3_), channel_id=1, source_target_pairs={{0,2},{2,4},{4,6},{6,7},{7,5},{5,3},{3,1},{1,0},{16,17},{18,16},{2... | collective-permute-start | bytes 835592 | tf_op jit(solution)/shard_map/ppermute | solution.py:36
  42.5 12.9 %collective-permute-start.8 = (bf16[64,2176]{1,0:T(8,128)(2,1)}, bf16[64,2176]{1,0:T(8,128)(2,1)}, u32[]{:S(2)}, u32[]{:S(2)}) collective-permute-start(bf16[64,2176]{1,0:T(8,128)(2,1)} %collective-permute-done.3.refs_0_.refs_4_), channel_id=1, source_target_pairs={{0,1},{2,0},{4,2},{6,4},{7,6},{5,7},{3,5},{1,3},{16,18},{18,20},{2... | collective-permute-start | bytes 835592 | tf_op jit(solution)/shard_map/ppermute | solution.py:36
  43.3 2.0 %copy-start = (bf16[384,2048]{1,0:T(8,128)(2,1)}, bf16[384,2048]{1,0:T(8,128)(2,1)S(1)}, u32[]{:S(2)}) copy-start(bf16[384,2048]{1,0:T(8,128)(2,1)S(1)} %collective-permute-done.4.refs_7_.refs_9_) | copy-start | bytes 4718596
  43.3 23.4 %collective-permute-start.22 = (bf16[64,2048]{1,0:T(8,128)(2,1)}, bf16[64,2048]{1,0:T(8,128)(2,1)S(1)}, u32[]{:S(2)}, u32[]{:S(2)}) collective-permute-start(bf16[64,2048]{1,0:T(8,128)(2,1)} %copy-done.20), channel_id=1, source_target_pairs={{0,2},{2,4},{4,6},{6,7},{7,5},{5,3},{3,1},{1,0},{16,17},{18,16},{2... | collective-permute-start | bytes 786440 | tf_op jit(solution)/shard_map/ppermute | solution.py:36
  45.2 1.1 copy-start.1
  45.2 21.4 %collective-permute-start.23 = (bf16[64,2048]{1,0:T(8,128)(2,1)}, bf16[64,2048]{1,0:T(8,128)(2,1)}, u32[]{:S(2)}, u32[]{:S(2)}) collective-permute-start(bf16[64,2048]{1,0:T(8,128)(2,1)} %copy-done.21), channel_id=1, source_target_pairs={{0,1},{2,0},{4,2},{6,4},{7,6},{5,7},{3,5},{1,3},{16,18},{18,20},{2... | collective-permute-start | bytes 786440 | tf_op jit(solution)/shard_map/ppermute | solution.py:36
  55.4 17.7 %collective-permute-start.9 = (bf16[64,2176]{1,0:T(8,128)(2,1)}, bf16[64,2176]{1,0:T(8,128)(2,1)S(1)}, u32[]{:S(2)}, u32[]{:S(2)}) collective-permute-start(bf16[64,2176]{1,0:T(8,128)(2,1)} %collective-permute-done.7.refs_1_.refs_5_), channel_id=1, source_target_pairs={{0,2},{2,4},{4,6},{6,7},{7,5},{5,3},{3,1},{1,0},{16,17},{18,16},{2... | collective-permute-start | bytes 835592 | tf_op jit(solution)/shard_map/ppermute | solution.py:36
  66.6 16.2 %copy-start.22 = (bf16[64,2048]{1,0:T(8,128)(2,1)}, bf16[64,2048]{1,0:T(8,128)(2,1)S(1)}, u32[]{:S(2)}) copy-start(bf16[64,2048]{1,0:T(8,128)(2,1)S(1)} %collective-permute-done.22.refs_1_.refs_13_) | copy-start | bytes 786436
  66.7 6.4 %collective-permute-start.24 = (bf16[64,2048]{1,0:T(8,128)(2,1)S(1)}, bf16[64,2048]{1,0:T(8,128)(2,1)S(1)}, u32[]{:S(2)}, u32[]{:S(2)}) collective-permute-start(bf16[64,2048]{1,0:T(8,128)(2,1)S(1)} %collective-permute-done.22.refs_1_.refs_13_), channel_id=1, source_target_pairs={{0,2},{2,4},{4,6},{6,7},{7,5},{5,3},{3,1},{1,0},{16,17},{18,16},{2... | collective-permute-start | bytes 786440 | tf_op jit(solution)/shard_map/ppermute | solution.py:36
  73.1 9.8 %copy-start.26 = (bf16[64,2048]{1,0:T(8,128)(2,1)}, bf16[64,2048]{1,0:T(8,128)(2,1)S(1)}, u32[]{:S(2)}) copy-start(bf16[64,2048]{1,0:T(8,128)(2,1)S(1)} %collective-permute-done.24.refs_3_.refs_15_) | copy-start | bytes 786436
  73.1 0.7 copy-start.9
  82.9 23.9 %collective-permute-start.10 = (bf16[64,2048]{1,0:T(8,128)(2,1)}, bf16[64,2048]{1,0:T(8,128)(2,1)S(1)}, u32[]{:S(2)}, u32[]{:S(2)}) collective-permute-start(bf16[64,2048]{1,0:T(8,128)(2,1)} %get-tuple-element.72), channel_id=1, source_target_pairs={{0,1},{2,0},{4,2},{6,4},{7,6},{5,7},{3,5},{1,3},{16,18},{18,20},{2... | collective-permute-start | bytes 786440 | tf_op jit(solution)/shard_map/ppermute | solution.py:36
  83.0 24.0 %collective-permute-start.14 = (bf16[64,2048]{1,0:T(8,128)(2,1)}, bf16[64,2048]{1,0:T(8,128)(2,1)S(1)}, u32[]{:S(2)}, u32[]{:S(2)}) collective-permute-start(bf16[64,2048]{1,0:T(8,128)(2,1)} %get-tuple-element.76), channel_id=1, source_target_pairs={{0,2},{2,4},{4,6},{6,7},{7,5},{5,3},{3,1},{1,0},{16,17},{18,16},{2... | collective-permute-start | bytes 786440 | tf_op jit(solution)/shard_map/ppermute | solution.py:36
  94.0 15.1 %collective-permute-start.25 = (bf16[64,2048]{1,0:T(8,128)(2,1)}, bf16[64,2048]{1,0:T(8,128)(2,1)S(1)}, u32[]{:S(2)}, u32[]{:S(2)}) collective-permute-start(bf16[64,2048]{1,0:T(8,128)(2,1)} %get-tuple-element.90), channel_id=1, source_target_pairs={{0,1},{2,0},{4,2},{6,4},{7,6},{5,7},{3,5},{1,3},{16,18},{18,20},{2... | collective-permute-start | bytes 786440 | tf_op jit(solution)/shard_map/ppermute | solution.py:36
  94.1 15.0 %collective-permute-start.26 = (bf16[64,2048]{1,0:T(8,128)(2,1)}, bf16[64,2048]{1,0:T(8,128)(2,1)S(1)}, u32[]{:S(2)}, u32[]{:S(2)}) collective-permute-start(bf16[64,2048]{1,0:T(8,128)(2,1)} %get-tuple-element.91), channel_id=1, source_target_pairs={{0,2},{2,4},{4,6},{6,7},{7,5},{5,3},{3,1},{1,0},{16,17},{18,16},{2... | collective-permute-start | bytes 786440 | tf_op jit(solution)/shard_map/ppermute | solution.py:36
  96.1 10.7 %copy-start.27 = (bf16[64,2048]{1,0:T(8,128)(2,1)S(1)}, bf16[64,2048]{1,0:T(8,128)(2,1)}, u32[]{:S(2)}) copy-start(bf16[64,2048]{1,0:T(8,128)(2,1)} %get-tuple-element.73) | copy-start | bytes 786436
  96.1 10.9 %copy-start.25 = (bf16[64,2048]{1,0:T(8,128)(2,1)S(1)}, bf16[64,2048]{1,0:T(8,128)(2,1)}, u32[]{:S(2)}) copy-start(bf16[64,2048]{1,0:T(8,128)(2,1)} %get-tuple-element.77) | copy-start | bytes 786436
  106.7 2.3 %copy-start.24 = (bf16[64,2048]{1,0:T(8,128)(2,1)S(1)}, bf16[64,2048]{1,0:T(8,128)(2,1)}, u32[]{:S(2)}) copy-start(bf16[64,2048]{1,0:T(8,128)(2,1)} %get-tuple-element.104) | copy-start | bytes 786436
  106.8 3.9 %copy-start.23 = (bf16[64,2048]{1,0:T(8,128)(2,1)S(1)}, bf16[64,2048]{1,0:T(8,128)(2,1)}, u32[]{:S(2)}) copy-start(bf16[64,2048]{1,0:T(8,128)(2,1)} %get-tuple-element.102) | copy-start | bytes 786436
  106.8 6.5 %copy-start.18 = (bf16[64,2048]{1,0:T(8,128)(2,1)S(1)}, bf16[64,2048]{1,0:T(8,128)(2,1)}, u32[]{:S(2)}) copy-start(bf16[64,2048]{1,0:T(8,128)(2,1)} %get-tuple-element.74) | copy-start | bytes 786436
  106.9 6.4 %collective-permute-start.11 = (bf16[64,2048]{1,0:T(8,128)(2,1)S(1)}, bf16[64,2048]{1,0:T(8,128)(2,1)S(1)}, u32[]{:S(2)}, u32[]{:S(2)}) collective-permute-start(bf16[64,2048]{1,0:T(8,128)(2,1)S(1)} %add_convert_fusion.14), channel_id=1, source_target_pairs={{0,1},{2,0},{4,2},{6,4},{7,6},{5,7},{3,5},{1,3},{16,18},{18,20},{2... | collective-permute-start | bytes 786440 | tf_op jit(solution)/shard_map/ppermute | solution.py:36
  107.0 7.4 %copy-start.16 = (bf16[64,2048]{1,0:T(8,128)(2,1)S(1)}, bf16[64,2048]{1,0:T(8,128)(2,1)}, u32[]{:S(2)}) copy-start(bf16[64,2048]{1,0:T(8,128)(2,1)} %get-tuple-element.78) | copy-start | bytes 786436
  107.1 6.4 %collective-permute-start.15 = (bf16[64,2048]{1,0:T(8,128)(2,1)S(1)}, bf16[64,2048]{1,0:T(8,128)(2,1)S(1)}, u32[]{:S(2)}, u32[]{:S(2)}) collective-permute-start(bf16[64,2048]{1,0:T(8,128)(2,1)S(1)} %add_convert_fusion.11), channel_id=1, source_target_pairs={{0,2},{2,4},{4,6},{6,7},{7,5},{5,3},{3,1},{1,0},{16,17},{18,16},{2... | collective-permute-start | bytes 786440 | tf_op jit(solution)/shard_map/ppermute | solution.py:36
  109.1 11.0 %copy-start.28 = (bf16[384,2048]{1,0:T(8,128)(2,1)S(1)}, bf16[384,2048]{1,0:T(8,128)(2,1)}, u32[]{:S(2)}) copy-start(bf16[384,2048]{1,0:T(8,128)(2,1)} %get-tuple-element.110) | copy-start | bytes 4718596
  109.1 12.6 %copy-start.15 = (bf16[64,2048]{1,0:T(8,128)(2,1)S(1)}, bf16[64,2048]{1,0:T(8,128)(2,1)}, u32[]{:S(2)}) copy-start(bf16[64,2048]{1,0:T(8,128)(2,1)} %get-tuple-element.75) | copy-start | bytes 786436
  109.2 20.0 %collective-permute-start.28 = (bf16[64,2048]{1,0:T(8,128)(2,1)S(1)}, bf16[64,2048]{1,0:T(8,128)(2,1)S(1)}, u32[]{:S(2)}, u32[]{:S(2)}) collective-permute-start(bf16[64,2048]{1,0:T(8,128)(2,1)S(1)} %add_convert_fusion.7), channel_id=1, source_target_pairs={{0,2},{2,4},{4,6},{6,7},{7,5},{5,3},{3,1},{1,0},{16,17},{18,16},{2... | collective-permute-start | bytes 786440 | tf_op jit(solution)/shard_map/ppermute | solution.py:36
  110.6 11.2 %collective-permute-start.29 = (bf16[384,2048]{1,0:T(8,128)(2,1)}, bf16[384,2048]{1,0:T(8,128)(2,1)S(1)}, u32[]{:S(2)}, u32[]{:S(2)}) collective-permute-start(bf16[384,2048]{1,0:T(8,128)(2,1)} %get-tuple-element.106), channel_id=1, source_target_pairs={{0,16},{16,0},{1,17},{17,1},{2,18},{18,2},{3,19},{19,3},{4,20},{20... | collective-permute-start | bytes 4718600 | tf_op jit(solution)/shard_map/ppermute | solution.py:41
  110.6 13.2 %copy-start.5 = (bf16[384,2048]{1,0:T(8,128)(2,1)S(1)}, bf16[384,2048]{1,0:T(8,128)(2,1)}, u32[]{:S(2)}) copy-start(bf16[384,2048]{1,0:T(8,128)(2,1)} %get-tuple-element.105) | copy-start | bytes 4718596
  110.7 18.5 %collective-permute-start.27 = (bf16[64,2048]{1,0:T(8,128)(2,1)S(1)}, bf16[64,2048]{1,0:T(8,128)(2,1)S(1)}, u32[]{:S(2)}, u32[]{:S(2)}) collective-permute-start(bf16[64,2048]{1,0:T(8,128)(2,1)S(1)} %add_convert_fusion.8), channel_id=1, source_target_pairs={{0,1},{2,0},{4,2},{6,4},{7,6},{5,7},{3,5},{1,3},{16,18},{18,20},{2... | collective-permute-start | bytes 786440 | tf_op jit(solution)/shard_map/ppermute | solution.py:36
  113.3 12.3 %collective-permute-start.30 = (bf16[384,2048]{1,0:T(8,128)(2,1)}, bf16[384,2048]{1,0:T(8,128)(2,1)S(1)}, u32[]{:S(2)}, u32[]{:S(2)}) collective-permute-start(bf16[384,2048]{1,0:T(8,128)(2,1)} %get-tuple-element.108), channel_id=1, source_target_pairs={{0,16},{16,0},{1,17},{17,1},{2,18},{18,2},{3,19},{19,3},{4,20},{20... | collective-permute-start | bytes 4718600 | tf_op jit(solution)/shard_map/ppermute | solution.py:41
  113.5 6.6 %collective-permute-start.12 = (bf16[64,2048]{1,0:T(8,128)(2,1)S(1)}, bf16[64,2048]{1,0:T(8,128)(2,1)S(1)}, u32[]{:S(2)}, u32[]{:S(2)}) collective-permute-start(bf16[64,2048]{1,0:T(8,128)(2,1)S(1)} %add_convert_fusion.13), channel_id=1, source_target_pairs={{0,1},{2,0},{4,2},{6,4},{7,6},{5,7},{3,5},{1,3},{16,18},{18,20},{2... | collective-permute-start | bytes 786440 | tf_op jit(solution)/shard_map/ppermute | solution.py:36
  120.1 7.3 %collective-permute-start.31 = (bf16[384,2048]{1,0:T(8,128)(2,1)S(1)}, bf16[384,2048]{1,0:T(8,128)(2,1)S(1)}, u32[]{:S(2)}, u32[]{:S(2)}) collective-permute-start(bf16[384,2048]{1,0:T(8,128)(2,1)S(1)} %copy-done.28), channel_id=1, source_target_pairs={{0,16},{16,0},{1,17},{17,1},{2,18},{18,2},{3,19},{19,3},{4,20},{20... | collective-permute-start | bytes 4718600 | tf_op jit(solution)/shard_map/ppermute | solution.py:41
  121.8 3.9 %copy-start.4 = (bf16[384,2048]{1,0:T(8,128)(2,1)S(1)}, bf16[384,2048]{1,0:T(8,128)(2,1)}, u32[]{:S(2)}) copy-start(bf16[384,2048]{1,0:T(8,128)(2,1)} %get-tuple-element.107) | copy-start | bytes 4718596
  121.8 17.5 %collective-permute-start.16 = (bf16[64,2048]{1,0:T(8,128)(2,1)S(1)}, bf16[64,2048]{1,0:T(8,128)(2,1)S(1)}, u32[]{:S(2)}, u32[]{:S(2)}) collective-permute-start(bf16[64,2048]{1,0:T(8,128)(2,1)S(1)} %add_convert_fusion.10), channel_id=1, source_target_pairs={{0,2},{2,4},{4,6},{6,7},{7,5},{5,3},{3,1},{1,0},{16,17},{18,16},{2... | collective-permute-start | bytes 786440 | tf_op jit(solution)/shard_map/ppermute | solution.py:36
  125.6 1.8 %copy-start.3 = (bf16[384,2048]{1,0:T(8,128)(2,1)S(1)}, bf16[384,2048]{1,0:T(8,128)(2,1)}, u32[]{:S(2)}) copy-start(bf16[384,2048]{1,0:T(8,128)(2,1)} %get-tuple-element.109) | copy-start | bytes 4718596
  125.6 13.7 %collective-permute-start.13 = (bf16[64,2048]{1,0:T(8,128)(2,1)S(1)}, bf16[64,2048]{1,0:T(8,128)(2,1)S(1)}, u32[]{:S(2)}, u32[]{:S(2)}) collective-permute-start(bf16[64,2048]{1,0:T(8,128)(2,1)S(1)} %add_convert_fusion.12), channel_id=1, source_target_pairs={{0,1},{2,0},{4,2},{6,4},{7,6},{5,7},{3,5},{1,3},{16,18},{18,20},{2... | collective-permute-start | bytes 786440 | tf_op jit(solution)/shard_map/ppermute | solution.py:36
  127.4 1.8 %copy-start.14 = (bf16[64,2048]{1,0:T(8,128)(2,1)S(1)}, bf16[64,2048]{1,0:T(8,128)(2,1)}, u32[]{:S(2)}) copy-start(bf16[64,2048]{1,0:T(8,128)(2,1)} %get-tuple-element.112) | copy-start | bytes 786436
  127.4 2.8 %copy-start.13 = (bf16[64,2048]{1,0:T(8,128)(2,1)S(1)}, bf16[64,2048]{1,0:T(8,128)(2,1)}, u32[]{:S(2)}) copy-start(bf16[64,2048]{1,0:T(8,128)(2,1)} %get-tuple-element.115) | copy-start | bytes 786436
  129.2 9.1 %copy-start.12 = (bf16[64,2048]{1,0:T(8,128)(2,1)S(1)}, bf16[64,2048]{1,0:T(8,128)(2,1)}, u32[]{:S(2)}) copy-start(bf16[64,2048]{1,0:T(8,128)(2,1)} %get-tuple-element.113) | copy-start | bytes 786436
  129.2 10.1 %copy-start.2 = (bf16[64,2176]{1,0:T(8,128)(2,1)S(1)}, bf16[64,2176]{1,0:T(8,128)(2,1)}, u32[]{:S(2)}) copy-start(bf16[64,2176]{1,0:T(8,128)(2,1)} %pack_rows.1.refs_0_) | copy-start | bytes 835588
  129.2 10.1 %copy-start.10 = (bf16[64,2048]{1,0:T(8,128)(2,1)S(1)}, bf16[64,2048]{1,0:T(8,128)(2,1)}, u32[]{:S(2)}) copy-start(bf16[64,2048]{1,0:T(8,128)(2,1)} %get-tuple-element.65) | copy-start | bytes 786436
  129.3 15.5 %copy-start.6 = (bf16[1,64,2048]{2,1,0:T(8,128)(2,1)S(1)}, bf16[1,64,2048]{2,1,0:T(8,128)(2,1)}, u32[]{:S(2)}) copy-start(bf16[1,64,2048]{2,1,0:T(8,128)(2,1)} %param.12) | copy-start | bytes 786436
  129.3 15.5 %copy-start.11 = (bf16[64,2048]{1,0:T(8,128)(2,1)S(1)}, bf16[64,2048]{1,0:T(8,128)(2,1)}, u32[]{:S(2)}) copy-start(bf16[64,2048]{1,0:T(8,128)(2,1)} %get-tuple-element.82) | copy-start | bytes 786436
  129.3 8.9 %collective-permute-start.32 = (bf16[64,2048]{1,0:T(8,128)(2,1)S(1)}, bf16[64,2048]{1,0:T(8,128)(2,1)S(1)}, u32[]{:S(2)}, u32[]{:S(2)}) collective-permute-start(bf16[64,2048]{1,0:T(8,128)(2,1)S(1)} %add_convert_fusion.6), channel_id=1, source_target_pairs={{0,1},{2,0},{4,2},{6,4},{7,6},{5,7},{3,5},{1,3},{16,18},{18,20},{2... | collective-permute-start | bytes 786440 | tf_op jit(solution)/shard_map/ppermute | solution.py:36
  130.3 10.8 %collective-permute-start.34 = (bf16[64,2048]{1,0:T(8,128)(2,1)S(1)}, bf16[64,2048]{1,0:T(8,128)(2,1)S(1)}, u32[]{:S(2)}, u32[]{:S(2)}) collective-permute-start(bf16[64,2048]{1,0:T(8,128)(2,1)S(1)} %add_convert_fusion.4), channel_id=1, source_target_pairs={{0,2},{2,4},{4,6},{6,7},{7,5},{5,3},{3,1},{1,0},{16,17},{18,16},{2... | collective-permute-start | bytes 786440 | tf_op jit(solution)/shard_map/ppermute | solution.py:36
  138.3 6.4 %collective-permute-start.33 = (bf16[64,2048]{1,0:T(8,128)(2,1)S(1)}, bf16[64,2048]{1,0:T(8,128)(2,1)S(1)}, u32[]{:S(2)}, u32[]{:S(2)}) collective-permute-start(bf16[64,2048]{1,0:T(8,128)(2,1)S(1)} %add_convert_fusion.5), channel_id=1, source_target_pairs={{0,1},{2,0},{4,2},{6,4},{7,6},{5,7},{3,5},{1,3},{16,18},{18,20},{2... | collective-permute-start | bytes 786440 | tf_op jit(solution)/shard_map/ppermute | solution.py:36
  139.4 9.0 %collective-permute-start.17 = (bf16[1,64,2048]{2,1,0:T(8,128)(2,1)S(1)}, bf16[1,64,2048]{2,1,0:T(8,128)(2,1)S(1)}, u32[]{:S(2)}, u32[]{:S(2)}) collective-permute-start(bf16[1,64,2048]{2,1,0:T(8,128)(2,1)S(1)} %fusion), channel_id=1, source_target_pairs={{0,8},{8,0},{1,9},{9,1},{2,10},{10,2},{3,11},{11,3},{4,12},{12,4},... | collective-permute-start | bytes 786440 | tf_op jit(solution)/shard_map/ppermute | solution.py:41
  144.9 6.6 %collective-permute-start.35 = (bf16[1,64,2048]{2,1,0:T(8,128)(2,1)S(1)}, bf16[1,64,2048]{2,1,0:T(8,128)(2,1)S(1)}, u32[]{:S(2)}, u32[]{:S(2)}) collective-permute-start(bf16[1,64,2048]{2,1,0:T(8,128)(2,1)S(1)} %fusion.1), channel_id=1, source_target_pairs={{0,8},{8,0},{1,9},{9,1},{2,10},{10,2},{3,11},{11,3},{4,12},{12,4},... | collective-permute-start | bytes 786440 | tf_op jit(solution)/shard_map/ppermute | solution.py:41
  (1 other events, 0.7 us)

commit v5 on v1

v5 whole, which is shorter than its diff:
```python
import functools
import jax
import jax.numpy as jnp
from jax import lax
from jax.experimental import pallas as pl
from jax.experimental.pallas import tpu as pltpu
from jax.sharding import PartitionSpec as P

F32 = jnp.float32
BF16 = jnp.bfloat16


def vmem(peers):
    return (30 if peers <= 8 else 60) * 2**20


def ring_order(peers):
    width = 1
    while 8 * width * width <= peers:
        width *= 2
    depth = peers // width
    if width == 1 or depth % 2:
        return list(range(peers))
    order = [z * width for z in range(depth)]
    for back, z in enumerate(reversed(range(depth))):
        columns = list(range(1, width))
        order += [z * width + x for x in (columns if back % 2 == 0 else reversed(columns))]
    return order


def ring_shift(value, by):
    peers = lax.axis_size("exp")
    order = ring_order(peers)
    pairs = []
    for rep in range(lax.axis_size("rep")):
        step = by if rep % 2 == 0 else -by
        for spot in range(peers):
            pairs.append((rep * peers + order[spot], rep * peers + order[(spot + step) % peers]))
    return lax.ppermute(value, ("rep", "exp"), pairs)


def from_behind(value, axis, by):
    peers = lax.axis_size(axis)
    return lax.ppermute(value, axis, [(i, (i + by) % peers) for i in range(peers)])


def dot(a, b, dims):
    return lax.dot_general(a, b, (dims, ((), ())), preferred_element_type=F32)


def whole():
    return pl.BlockSpec(memory_space=pltpu.VMEM)


def turned(value):
    rows, columns = value.shape
    wide = jnp.concatenate([value, jnp.zeros((rows, 128 - columns), F32)], axis=1)
    return wide.T[:columns]


def pack_kernel(experts, codes_ref, exps_ref, routes_ref, weight_ref, grad_ref, out_ref):
    tokens, width = codes_ref.shape
    blocks = exps_ref.shape[0]
    scales = jnp.exp2(exps_ref[...].astype(F32))
    scales = turned(jnp.concatenate([scales, jnp.zeros((128 - blocks, tokens), F32)], axis=0))
    per = width // blocks
    for b in range(blocks):
        cols = slice(b * per, (b + 1) * per)
        out_ref[:, cols] = (codes_ref[:, cols].astype(F32) * scales[:, b : b + 1]).astype(BF16)
    expert = lax.broadcasted_iota(jnp.int32, (experts, tokens), 0)
    table = jnp.zeros((experts, tokens), F32)
    for k in range(routes_ref.shape[0]):
        table += jnp.where(routes_ref[k : k + 1, :] == expert, weight_ref[k : k + 1, :], 0.0)
    high = table.astype(BF16).astype(F32)
    middle = (table - high).astype(BF16).astype(F32)
    low = table - high - middle
    out_ref[:, width : 2 * width] = grad_ref[...]
    extra = out_ref.shape[1] - 2 * width
    parts = [high, middle, low]
    if extra > 3 * experts:
        parts.append(jnp.zeros((extra - 3 * experts, tokens), F32))
    out_ref[:, 2 * width :] = turned(jnp.concatenate(parts, axis=0)).astype(BF16)


LAST = ((1,), (1,))
PLAIN = ((1,), (0,))
TILE = 256


def columns_of(width, body):
    def step(n, carry):
        body(n * TILE)
        return carry

    lax.fori_loop(0, width // TILE, step, 0, unroll=2)


def span(start):
    return pl.ds(pl.multiple_of(start, TILE), TILE)


def load_kernel(*refs):
    count = len(refs) // 2
    copies = [
        pltpu.make_async_copy(refs[i], refs[count + i], refs[-1].at[i]) for i in range(count)
    ]
    for copy in copies:
        copy.start()
    for copy in copies:
        copy.wait()


def load_call(weights):
    return pl.pallas_call(
        load_kernel,
        out_shape=[jax.ShapeDtypeStruct(w.shape, w.dtype) for w in weights],
        in_specs=[pl.BlockSpec(memory_space=pl.ANY)] * len(weights),
        out_specs=[whole()] * len(weights),
        scratch_shapes=[pltpu.SemaphoreType.DMA((len(weights),))],
        cost_estimate=pl.CostEstimate(flops=0, bytes_accessed=10**7, transcendentals=0),
        name="load_weights",
    )(*weights)


def expert_kernel(count, experts, local_experts, first_ref, *refs):
    blocks = refs[:count]
    weights = refs[count : count + 6]
    outs = refs[count + 6 : 2 * count + 6]
    saved = refs[2 * count + 6 : 2 * count + 9]
    rows, left = refs[2 * count + 9 :]
    half, width = weights[0].shape
    tokens = blocks[0].shape[0]
    tables = []
    for i, block in enumerate(blocks):
        rows[0, i * tokens : (i + 1) * tokens] = block[:, :width]
        rows[1, i * tokens : (i + 1) * tokens] = block[:, width : 2 * width]
        tables.append(block[:, 2 * width :].astype(F32))
    table = jnp.concatenate(tables, axis=0).T
    expert_of = lax.rem(lax.broadcasted_iota(jnp.int32, table.shape, 0), experts)
    scales = [
        jnp.sum(jnp.where(expert_of == first_ref[0] + e, table, 0.0), axis=0, keepdims=True)
        for e in range(local_experts)
    ]
    unit = lax.broadcasted_iota(jnp.int32, (half, 1), 0)
    scale = scales[0]
    for e in range(1, local_experts):
        scale = jnp.where(unit >= e * (half // local_experts), scales[e], scale)
    for side in range(2):
        at = slice(side * half, (side + 1) * half)
        gate = dot(weights[3 * side][...], rows[0], LAST)
        up = dot(weights[3 * side + 1][...], rows[0], LAST)
        back = dot(weights[3 * side + 2][...], rows[1], LAST) * scale
        sig = 1.0 / (1.0 + jnp.exp(-gate))
        swish = gate * sig
        results = (
            back * up * sig * (1.0 + gate * (1.0 - sig)),
            back * swish,
            swish * up * scale,
        )
        for kind, result in enumerate(results):
            result = result.astype(BF16)
            saved[kind][at, :] = result
            left[kind, :, at] = result.T

    def column(start):
        at, later = span(start), span(width + start)
        right = [
            jnp.concatenate([weights[kind][:, at], weights[3 + kind][:, at]], axis=0)
            for kind in range(3)
        ]
        output = dot(left[2], right[2], PLAIN).astype(BF16)
        grad = (dot(left[0], right[0], PLAIN) + dot(left[1], right[1], PLAIN)).astype(BF16)
        for i, out in enumerate(outs):
            out[:, at] = output[i * tokens : (i + 1) * tokens]
            out[:, later] = grad[i * tokens : (i + 1) * tokens]

    columns_of(width, column)


def expert_call(blocks, weights, first, experts, local_experts):
    count, tokens = len(blocks), blocks[0].shape[0]
    half, width = weights[0].shape
    units, rows = 2 * half, count * tokens
    results = pl.pallas_call(
        functools.partial(expert_kernel, count, experts, local_experts),
        out_shape=[jax.ShapeDtypeStruct((tokens, 2 * width), BF16)] * count
        + [jax.ShapeDtypeStruct((units, rows), BF16)] * 3,
        in_specs=[pl.BlockSpec(memory_space=pltpu.SMEM)] + [whole()] * (count + 6),
        out_specs=[whole()] * (count + 3),
        scratch_shapes=[
            pltpu.VMEM((2, rows, width), BF16),
            pltpu.VMEM((3, rows, units), BF16),
        ],
        compiler_params=pltpu.CompilerParams(vmem_limit_bytes=vmem(experts // local_experts)),
        cost_estimate=pl.CostEstimate(
            flops=6 * 2 * rows * units * width,
            bytes_accessed=6 * units * width + 8 * rows * width,
            transcendentals=rows * units,
        ),
        name="expert_rows",
    )(first, *blocks, *weights)
    return results[:count], results[count:]


def weight_kernel(groups, count, *refs):
    blocks = refs[:count]
    kept = [refs[count + g * 3 : count + g * 3 + 3] for g in range(groups)]
    outs, across = refs[-7:-1], refs[-1]
    half, width = outs[0].shape
    for kind in range(3):
        start = 0
        for group in kept:
            size = group[kind].shape[1]
            across[kind, :, start : start + size] = group[kind][...]
            start += size

    def column(start):
        at, later = span(start), span(width + start)
        right = [
            jnp.concatenate([b[:, at] for b in blocks], axis=0),
            jnp.concatenate([b[:, later] for b in blocks], axis=0),
        ]
        for kind in range(3):
            total = dot(across[kind], right[kind // 2], PLAIN).astype(BF16)
            outs[kind][:, at] = total[:half]
            outs[3 + kind][:, at] = total[half:]

    columns_of(width, column)


def weight_call(blocks, kept, width, peers):
    count = len(blocks)
    units = kept[0][0].shape[0]
    half, total = units // 2, count * blocks[0].shape[0]
    results = pl.pallas_call(
        functools.partial(weight_kernel, len(kept), count),
        out_shape=[jax.ShapeDtypeStruct((half, width), BF16)] * 6,
        in_specs=[whole()] * (count + 3 * len(kept)),
        out_specs=[whole()] * 6,
        scratch_shapes=[pltpu.VMEM((3, units, total), BF16)],
        compiler_params=pltpu.CompilerParams(vmem_limit_bytes=vmem(peers)),
        cost_estimate=pl.CostEstimate(
            flops=3 * 2 * total * units * width,
            bytes_accessed=4 * total * width + 12 * half * width,
            transcendentals=0,
        ),
        name="weight_grads",
    )(*blocks, *[k for group in kept for k in group])
    return results[:3], results[3:]


def add(a, b):
    return (a.astype(F32) + b.astype(F32)).astype(BF16)


def shards(
    row_codes, block_exponents, routes, route_weight, out_grad, gate_weight, up_weight, down_weight
):
    tokens, width = row_codes.shape[1:]
    local_experts, half_units = gate_weight.shape[1:3]
    half = local_experts * half_units
    peers = lax.axis_size("exp")
    experts = peers * local_experts
    lanes = -(-3 * experts // 128) * 128
    shards_of = [w.reshape(half, width) for w in (gate_weight, up_weight, down_weight)]
    other = [from_behind(w, "rep", 1) for w in shards_of]
    own = load_call(shards_of)
    weights = list(own) + other
    first = (lax.axis_index("exp") * local_experts).astype(jnp.int32).reshape(1)
    home = pl.pallas_call(
        functools.partial(pack_kernel, experts),
        out_shape=jax.ShapeDtypeStruct((tokens, 2 * width + lanes), BF16),
        in_specs=[whole()] * 5,
        out_specs=whole(),
        name="pack_rows",
    )(row_codes[0], block_exponents[0].T, routes[0].T, route_weight[0].T, out_grad[0])

    tie = lax.optimization_barrier
    ahead, behind = peers // 2, peers // 2 - 1
    names = [("near", 0)]
    for k in range(1, ahead + 1):
        names += [("near", k), ("far", k)]
    names = names[: 2 * ahead]
    groups = [names[i : i + 4] for i in range(0, len(names) - 4, 4)]
    groups.append([name for name in names[-4:] if name[0] == "far"])
    groups.append([name for name in names[-4:] if name[0] == "near"])
    held = {("near", 0): home, ("far", 0): tie((home, own))[0]}
    partial, kept = {}, []

    def work(group):
        outs, saved = expert_call(
            [held[name] for name in group], weights, first, experts, local_experts
        )
        partial.update(zip(group, outs))
        kept.append(saved)

    for k in range(1, ahead + 1):
        held["near", k] = ring_shift(held["near", k - 1], 1)
        if k <= behind:
            held["far", k] = ring_shift(held["far", k - 1], -1)
        if k % 2 == 1 and k > 1:
            work(groups[(k - 3) // 2])
            held["near", k], kept[-1] = tie((held["near", k], kept[-1]))
    work(groups[-2])
    far_sum = ring_shift(partial["far", behind], 1)
    held["near", ahead], kept[-1] = tie((held["near", ahead], kept[-1]))
    work(groups[-1])
    far_sum, near_sum = tie((far_sum, partial["near", ahead]))
    own_total = received = totals = None
    blocks = [held[name] for group in groups for name in group]
    for k in range(ahead, 1, -1):
        near_sum = ring_shift(near_sum, -1)
        left = k - 2
        if left >= 1:
            far_sum = ring_shift(add(far_sum, partial["far", left]), 1)
        if k == ahead:
            own_total, other_total = weight_call(blocks, kept, width, peers)
            near_sum, far_sum, own_total, other_total = tie(
                (near_sum, far_sum, own_total, other_total)
            )
            received = [from_behind(g, "rep", 1) for g in other_total]
        elif k == ahead - 1:
            totals = [add(a, b) for a, b in zip(own_total, received)]
            near_sum, far_sum, totals = tie((near_sum, far_sum, totals))
        if k > 2:
            near_sum = add(near_sum, partial["near", k - 1])
    results = []
    for part, step in ((slice(0, width), 1), (slice(width, 2 * width), -1)):
        arrived = ring_shift(add(near_sum[:, part], partial["near", 1][:, part]), -1)
        total = home[:, part].astype(F32) + partial["near", 0][:, part].astype(F32)
        total = total + far_sum[:, part].astype(F32) + arrived.astype(F32)
        results.append(from_behind(total.astype(BF16)[None], "section", step))
    shape = (1, local_experts, half_units, width)
    return tuple(results) + tuple(t.reshape(shape) for t in totals)


def solution(mesh):
    tokens = P("section", ("rep", "exp"), None)
    weights = P("section", "exp", "rep", None)
    return jax.shard_map(
        shards,
        mesh=mesh,
        in_specs=(tokens,) * 5 + (weights,) * 3,
        out_specs=(tokens,) * 2 + (weights,) * 3,
        check_vma=False,
    )
```

time: 355 us -> 134 us (0.38)
  waiting for transfers between devices: 257 us -> 62.4 us
  matrix products: 36.5 us -> 0 us
  Pallas kernels: 0 us -> 35.5 us
  blocking collectives: 32.4 us -> 0 us
  starting transfers between devices: 3.68 us -> 20 us
  between operations: 14.3 us -> 0.8 us
    reduce_scatter x5 -> x0, waiting for transfers between devices: 147 us -> none  [the longest x1 67.5 us: shards(): lax.psum_scatter(input_grad, 'exp', scatter_dimension=0, tiled=True)]
    all_gather x5 -> x0, waiting for transfers between devices: 102 us -> none  [the longest x1 52.5 us: shards(): grads = lax.all_gather(out_grad[0], 'exp', axis=0, tiled=True)]
    ppermute x0 -> x15, waiting for transfers between devices: none -> 50.3 us  [ring_shift(): return lax.ppermute(value, ('rep', 'exp'), pairs)]
    dot_general x9 -> x0, matrix products: 36.5 us -> none  [dot(): lax.dot_general(a, b, (dims, ((), ())), preferred_element_type=jnp.float32)]
    pallas_call x0 -> x6, Pallas kernels: none -> 35.5 us  [the longest x3 21.1 us: expert_call(): pl.pallas_call(functools.partial(expert_kernel, count, experts, local_exp...]
    all_gather x1 -> x0, blocking collectives: 32.4 us -> none  [shards(): all_tables = lax.all_gather(table, 'exp', axis=0, tiled=True)]
    ppermute x0 -> x15, starting transfers between devices: none -> 16.4 us  [ring_shift(): return lax.ppermute(value, ('rep', 'exp'), pairs)]
    ppermute x2 -> x8, waiting for transfers between devices: 4.89 us -> 12.1 us  [from_behind(): lax.ppermute(value, axis, [(i, (i + by) % peers) for i in range(peers)])]
  transfers between devices with their start and end apart: 12 -> 23, of which waited for: 10 -> 16; matrix products, arithmetic and copies ran while one was open for 9% -> 4% of each run, Pallas kernels for 0% -> 27%
where the time goes in v5:
time: 134 us
  waiting for transfers between devices  62.4 us (47%)
  Pallas kernels  35.5 us (26%)
  starting transfers between devices  20 us (15%)
  local copies, waits for them, and re-layouts  8.57 us (6%)
  other arithmetic  6.27 us (5%)
    ppermute x15, waiting for transfers between devices, ring_shift(): return lax.ppermute(value, ('rep', 'exp'), pairs)  50.3 us
    pallas_call x3, Pallas kernels, expert_call(): pl.pallas_call(functools.partial(expert_kernel, count, experts, local_exp...  21.1 us
    ppermute x15, starting transfers between devices, ring_shift(): return lax.ppermute(value, ('rep', 'exp'), pairs)  16.4 us
    ppermute x8, waiting for transfers between devices, from_behind(): lax.ppermute(value, axis, [(i, (i + by) % peers) for i in range(peers)])  12.1 us
    unnamed x24, local copies, waits for them, and re-layouts  8.57 us
    pallas_call x1, Pallas kernels, weight_call(): pl.pallas_call(functools.partial(weight_kernel, len(kept), count), out_sh...  7.59 us
    convert_element_type x8, other arithmetic, add(): return (a.astype(F32) + b.astype(F32)).astype(BF16)  5.99 us
    pallas_call x1, Pallas kernels, load_call(): pl.pallas_call(load_kernel, out_shape=[jax.ShapeDtypeStruct(w.shape, w.dt...  4.56 us
  transfers between devices with their start and end apart: 23, of which 16 were waited for; matrix products, arithmetic and copies ran while one was open for 4% of the time, Pallas kernels for 27%

profile of v5, /device:TPU:0, one launch (start us, length us, event | category | flops | bytes accessed | tf_op | source)
XLA Modules:
  0.0 133.6 jit_solution(15389680278574209174)
XLA Ops:
  0.6 0.5 collective-permute-start.3
  1.2 0.1 collective-permute-start.4
  1.2 0.4 collective-permute-start.5
  1.7 2.2 %pack_rows.1.refs_0_ = bf16[64,4224]{1,0:T(8,128)(2,1)} custom-call(bf16[64,2048]{1,0:T(8,128)(2,1)} %bitcast.31, s32[16,64]{1,0:T(8,128)} %bitcast.33, s32[8,64]{1,0:T(8,128)} %bitcast.34, f32[8,64]{1,0:T(8,128)} %bitcast.35, bf16[64,2048]{1,0:T(8,128)(2,1)} %bitcast.32), custom_call_target="tpu_custom_call" | custom-call | tf_op jit(solution)/shard_map/pack_rows/pallas_call | solution.py:270
  3.9 2.7 %collective-permute-start = (bf16[64,4224]{1,0:T(8,128)(2,1)}, bf16[64,4224]{1,0:T(8,128)(2,1)}, u32[]{:S(2)}, u32[]{:S(2)}) collective-permute-start(bf16[64,4224]{1,0:T(8,128)(2,1)} %pack_rows.1.refs_0_), channel_id=1, source_target_pairs={{0,2},{2,4},{4,6},{6,7},{7,5},{5,3},{3,1},{1,0},{16,17},{18,16},{2... | collective-permute-start | bytes 1622024 | tf_op jit(solution)/shard_map/ppermute | solution.py:39
  6.5 4.6 %load_weights.1 = (bf16[384,2048]{1,0:T(8,128)(2,1)}, bf16[384,2048]{1,0:T(8,128)(2,1)}, bf16[384,2048]{1,0:T(8,128)(2,1)}) custom-call(bf16[384,2048]{1,0:T(8,128)(2,1)} %bitcast.23, bf16[384,2048]{1,0:T(8,128)(2,1)} %bitcast.25, bf16[384,2048]{1,0:T(8,128)(2,1)} %bitcast.27), custom_call_target="tpu_custom_call" | custom-call | bytes 10000000 | tf_op jit(solution)/shard_map/load_weights/pallas_call | solution.py:114
  11.1 0.1 collective-permute-start.1
  11.2 4.2 %collective-permute-done.refs_1_ = bf16[64,4224]{1,0:T(8,128)(2,1)} collective-permute-done((bf16[64,4224]{1,0:T(8,128)(2,1)}, bf16[64,4224]{1,0:T(8,128)(2,1)}, u32[]{:S(2)}, u32[]{:S(2)}) %collective-permute-start) | collective-permute-done | bytes 540704 | tf_op jit(solution)/shard_map/ppermute | solution.py:39
  15.4 2.5 %collective-permute-start.2 = (bf16[64,4224]{1,0:T(8,128)(2,1)}, bf16[64,4224]{1,0:T(8,128)(2,1)}, u32[]{:S(2)}, u32[]{:S(2)}) collective-permute-start(bf16[64,4224]{1,0:T(8,128)(2,1)} %collective-permute-done.refs_1_), channel_id=1, source_target_pairs={{0,2},{2,4},{4,6},{6,7},{7,5},{5,3},{3,1},{1,0},{16,17},{18,16},{2... | collective-permute-start | bytes 1622024 | tf_op jit(solution)/shard_map/ppermute | solution.py:39
  17.8 6.7 %collective-permute-done.1.refs_2_ = bf16[64,4224]{1,0:T(8,128)(2,1)S(1)} collective-permute-done((bf16[64,4224]{1,0:T(8,128)(2,1)}, bf16[64,4224]{1,0:T(8,128)(2,1)S(1)}, u32[]{:S(2)}, u32[]{:S(2)}) %collective-permute-start.1) | collective-permute-done | bytes 540704 | tf_op jit(solution)/shard_map/ppermute | solution.py:39
  24.5 0.0 collective-permute-start.6
  24.5 0.8 copy-done.8
  25.4 2.7 %collective-permute-done.2.refs_3_ = bf16[64,4224]{1,0:T(8,128)(2,1)} collective-permute-done((bf16[64,4224]{1,0:T(8,128)(2,1)}, bf16[64,4224]{1,0:T(8,128)(2,1)}, u32[]{:S(2)}, u32[]{:S(2)}) %collective-permute-start.2) | collective-permute-done | bytes 540704 | tf_op jit(solution)/shard_map/ppermute | solution.py:39
  28.0 2.5 %collective-permute-start.9 = (bf16[64,4224]{1,0:T(8,128)(2,1)}, bf16[64,4224]{1,0:T(8,128)(2,1)}, u32[]{:S(2)}, u32[]{:S(2)}) collective-permute-start(bf16[64,4224]{1,0:T(8,128)(2,1)} %collective-permute-done.2.refs_3_), channel_id=1, source_target_pairs={{0,2},{2,4},{4,6},{6,7},{7,5},{5,3},{3,1},{1,0},{16,17},{18,16},{2... | collective-permute-start | bytes 1622024 | tf_op jit(solution)/shard_map/ppermute | solution.py:39
  30.5 7.8 %collective-permute-done.6.refs_0_.refs_4_ = bf16[64,4224]{1,0:T(8,128)(2,1)} collective-permute-done((bf16[64,4224]{1,0:T(8,128)(2,1)S(1)}, bf16[64,4224]{1,0:T(8,128)(2,1)}, u32[]{:S(2)}, u32[]{:S(2)}) %collective-permute-start.6) | collective-permute-done | bytes 540704 | tf_op jit(solution)/shard_map/ppermute | solution.py:39
  38.3 0.0 collective-permute-start.7
  38.3 0.0 collective-permute-done.3.refs_7_.refs_5_
  38.3 0.0 collective-permute-done.4.refs_8_.refs_6_
  38.3 0.0 copy-start
  38.3 1.4 %copy-done = bf16[384,2048]{1,0:T(8,128)(2,1)S(1)} copy-done((bf16[384,2048]{1,0:T(8,128)(2,1)S(1)}, bf16[384,2048]{1,0:T(8,128)(2,1)}, u32[]{:S(2)}) %copy-start) | copy-done | bytes 1572888
  39.7 1.4 %copy-done.2 = bf16[384,2048]{1,0:T(8,128)(2,1)S(1)} copy-done((bf16[384,2048]{1,0:T(8,128)(2,1)S(1)}, bf16[384,2048]{1,0:T(8,128)(2,1)}, u32[]{:S(2)}) %copy-start.2) | copy-done | bytes 1572888
  41.1 1.4 %copy-done.4 = bf16[384,2048]{1,0:T(8,128)(2,1)S(1)} copy-done((bf16[384,2048]{1,0:T(8,128)(2,1)S(1)}, bf16[384,2048]{1,0:T(8,128)(2,1)}, u32[]{:S(2)}) %copy-start.4) | copy-done | bytes 1572888
  42.5 1.0 copy-done.6
  43.6 1.0 copy-done.9
  44.6 8.2 %expert_rows.3 = (bf16[64,4096]{1,0:T(8,128)(2,1)S(1)}, bf16[64,4096]{1,0:T(8,128)(2,1)S(1)}, bf16[64,4096]{1,0:T(8,128)(2,1)S(1)}, bf16[64,4096]{1,0:T(8,128)(2...) custom-call(s32[1]{0:T(128)} %bitcast.8.first_ref, ...), custom_call_target="tpu_custom_call" | custom-call | flops 4831838208 | bytes 13631488 | tf_op jit(solution)/shard_map/expert_rows/pallas_call | solution.py:184
  52.8 0.0 collective-permute-done.9.refs_0_.refs_6_
  52.8 2.1 %collective-permute-start.10 = (bf16[64,4224]{1,0:T(8,128)(2,1)}, bf16[64,4224]{1,0:T(8,128)(2,1)S(1)}, u32[]{:S(2)}, u32[]{:S(2)}) collective-permute-start(bf16[64,4224]{1,0:T(8,128)(2,1)} %collective-permute-done.9.refs_0_.refs_6_), channel_id=1, source_target_pairs={{0,2},{2,4},{4,6},{6,7},{7,5},{5,3},{3,1},{1,0},{16,17},{18,16},{2... | collective-permute-start | bytes 1622024 | tf_op jit(solution)/shard_map/ppermute | solution.py:39
  54.9 0.0 collective-permute-done.7.refs_1_.refs_5_
  54.9 6.5 %expert_rows.4 = (bf16[64,4096]{1,0:T(8,128)(2,1)S(1)}, bf16[64,4096]{1,0:T(8,128)(2,1)S(1)}, bf16[768,128]{1,0:T(8,128)(2,1)S(1)}, bf16[768,128]{1,0:T(8,128)(2,1)S(1)}, bf16[768,128]{1,0:T(8,128)(2,1)S(1)}) custom-call(s32[1]{0:T(128)} %bitcast.8.first_ref, bf16[64,4224]{1,0:T(8,128)(2,1)} %collective-permute-done.6.refs_0_.refs_4_, ...), custom_call_target="tpu_custom_call" | custom-call | flops 2415919104 | bytes 11534336 | tf_op jit(solution)/shard_map/expert_rows/pallas_call | solution.py:184
  61.5 1.3 collective-permute-start.8
  62.8 6.4 %expert_rows.5 = (bf16[64,4096]{1,0:T(8,128)(2,1)S(1)}, bf16[64,4096]{1,0:T(8,128)(2,1)S(1)}, bf16[768,128]{1,0:T(8,128)(2,1)S(1)}, bf16[768,128]{1,0:T(8,128)(2,1)S(1)}, bf16[768,128]{1,0:T(8,128)(2,1)S(1)}) custom-call(s32[1]{0:T(128)} %bitcast.8.first_ref, bf16[64,4224]{1,0:T(8,128)(2,1)} %collective-permute-done.9.refs_0_.refs_6_, ...), custom_call_target="tpu_custom_call" | custom-call | flops 2415919104 | bytes 11534336 | tf_op jit(solution)/shard_map/expert_rows/pallas_call | solution.py:184
  69.2 4.9 %collective-permute-done.8 = bf16[64,4096]{1,0:T(8,128)(2,1)S(1)} collective-permute-done((bf16[64,4096]{1,0:T(8,128)(2,1)S(1)}, bf16[64,4096]{1,0:T(8,128)(2,1)S(1)}, u32[]{:S(2)}, u32[]{:S(2)}) %collective-permute-start.8) | collective-permute-done | bytes 524320 | tf_op jit(solution)/shard_map/ppermute | solution.py:39
  74.1 0.1 add_convert_fusion.6
  74.2 2.3 %collective-permute-start.12 = (bf16[64,4096]{1,0:T(8,128)(2,1)S(1)}, bf16[64,4096]{1,0:T(8,128)(2,1)S(1)}, u32[]{:S(2)}, u32[]{:S(2)}) collective-permute-start(bf16[64,4096]{1,0:T(8,128)(2,1)S(1)} %add_convert_fusion.6), channel_id=1, source_target_pairs={{0,2},{2,4},{4,6},{6,7},{7,5},{5,3},{3,1},{1,0},{16,17},{18,16},{2... | collective-permute-start | bytes 1572872 | tf_op jit(solution)/shard_map/ppermute | solution.py:39
  76.5 7.6 %weight_grads.1 = (bf16[384,2048]{1,0:T(8,128)(2,1)S(1)}, bf16[384,2048]{1,0:T(8,128)(2,1)S(1)}, bf16[384,2048]{1,0:T(8,128)(2,1)S(1)}, bf16[384,2048]{1,0:T(8,1...) custom-call(bf16[64,4224]{1,0:T(8,128)(2,1)S(1)} %copy-done.7, ...), custom_call_target="tpu_custom_call" | custom-call | flops 4831838208 | bytes 13631488 | tf_op jit(solution)/shard_map/weight_grads/pallas_call | solution.py:235
  84.1 1.6 %collective-permute-done.11 = bf16[64,4096]{1,0:T(8,128)(2,1)S(1)} collective-permute-done((bf16[64,4096]{1,0:T(8,128)(2,1)S(1)}, bf16[64,4096]{1,0:T(8,128)(2,1)S(1)}, u32[]{:S(2)}, u32[]{:S(2)}) %collective-permute-start.11) | collective-permute-done | bytes 524320 | tf_op jit(solution)/shard_map/ppermute | solution.py:39
  85.6 0.5 collective-permute-start.16
  86.1 0.1 add_convert_fusion.4
  86.3 1.7 %collective-permute-start.14 = (bf16[64,4096]{1,0:T(8,128)(2,1)S(1)}, bf16[64,4096]{1,0:T(8,128)(2,1)S(1)}, u32[]{:S(2)}, u32[]{:S(2)}) collective-permute-start(bf16[64,4096]{1,0:T(8,128)(2,1)S(1)} %add_convert_fusion.4), channel_id=1, source_target_pairs={{0,2},{2,4},{4,6},{6,7},{7,5},{5,3},{3,1},{1,0},{16,17},{18,16},{2... | collective-permute-start | bytes 1572872 | tf_op jit(solution)/shard_map/ppermute | solution.py:39
  88.0 0.1 add_convert_fusion.5
  88.1 0.6 collective-permute-start.13
  88.7 0.3 collective-permute-done.15
  89.0 1.8 %add_convert_fusion.2 = bf16[384,2048]{1,0:T(8,128)(2,1)} fusion(bf16[384,2048]{1,0:T(8,128)(2,1)S(1)} %collective-permute-done.15, bf16[384,2048]{1,0:T(8,128)(2,1)S(1)} %get-tuple-element.92), kind=kLoop, calls=%fused_computation.2 | loop fusion | flops 3145728 | bytes 4718592 | tf_op jit(solution)/shard_map/convert_element_type | solution.py:253
  90.9 0.4 collective-permute-done.16
  91.3 1.8 %add_convert_fusion.1 = bf16[384,2048]{1,0:T(8,128)(2,1)} fusion(bf16[384,2048]{1,0:T(8,128)(2,1)S(1)} %collective-permute-done.16, bf16[384,2048]{1,0:T(8,128)(2,1)S(1)} %get-tuple-element.94), kind=kLoop, calls=%fused_computation.1 | loop fusion | flops 3145728 | bytes 4718592 | tf_op jit(solution)/shard_map/convert_element_type | solution.py:253
  93.1 0.4 collective-permute-done.17
  93.5 1.7 %add_convert_fusion = bf16[384,2048]{1,0:T(8,128)(2,1)} fusion(bf16[384,2048]{1,0:T(8,128)(2,1)S(1)} %collective-permute-done.17, bf16[384,2048]{1,0:T(8,128)(2,1)S(1)} %get-tuple-element.96), kind=kLoop, calls=%fused_computation | loop fusion | flops 3145728 | bytes 4718592 | tf_op jit(solution)/shard_map/convert_element_type | solution.py:253
  95.3 4.2 %collective-permute-done.14 = bf16[64,4096]{1,0:T(8,128)(2,1)S(1)} collective-permute-done((bf16[64,4096]{1,0:T(8,128)(2,1)S(1)}, bf16[64,4096]{1,0:T(8,128)(2,1)S(1)}, u32[]{:S(2)}, u32[]{:S(2)}) %collective-permute-start.14) | collective-permute-done | bytes 524320 | tf_op jit(solution)/shard_map/ppermute | solution.py:39
  99.5 0.7 collective-permute-done.13
  100.2 0.1 add_convert_fusion.3
  100.3 0.3 collective-permute-start.18
  100.6 8.9 %collective-permute-done.18 = bf16[64,4096]{1,0:T(8,128)(2,1)S(1)} collective-permute-done((bf16[64,4096]{1,0:T(8,128)(2,1)S(1)}, bf16[64,4096]{1,0:T(8,128)(2,1)S(1)}, u32[]{:S(2)}, u32[]{:S(2)}) %collective-permute-start.18) | collective-permute-done | bytes 524320 | tf_op jit(solution)/shard_map/ppermute | solution.py:39
  109.5 0.1 add_convert_fusion.8
  109.7 0.3 collective-permute-start.21
  110.0 0.1 collective-permute-start.19
  110.1 6.0 %collective-permute-done.21 = bf16[64,2048]{1,0:T(8,128)(2,1)S(1)} collective-permute-done((bf16[64,2048]{1,0:T(8,128)(2,1)S(1)}, bf16[64,2048]{1,0:T(8,128)(2,1)S(1)}, u32[]{:S(2)}, u32[]{:S(2)}) %collective-permute-start.21) | collective-permute-done | bytes 262176 | tf_op jit(solution)/shard_map/ppermute | solution.py:39
  116.1 2.8 %collective-permute-done.19 = bf16[64,2048]{1,0:T(8,128)(2,1)S(1)} collective-permute-done((bf16[64,2048]{1,0:T(8,128)(2,1)S(1)}, bf16[64,2048]{1,0:T(8,128)(2,1)S(1)}, u32[]{:S(2)}, u32[]{:S(2)}) %collective-permute-start.19) | collective-permute-done | bytes 262176 | tf_op jit(solution)/shard_map/ppermute | solution.py:39
  118.9 0.3 fusion.1
  119.2 1.6 %collective-permute-start.22 = (bf16[1,64,2048]{2,1,0:T(8,128)(2,1)S(1)}, bf16[1,64,2048]{2,1,0:T(8,128)(2,1)S(1)}, u32[]{:S(2)}, u32[]{:S(2)}) collective-permute-start(bf16[1,64,2048]{2,1,0:T(8,128)(2,1)S(1)} %get-tuple-element.105), channel_id=1, source_target_pairs={{0,8},{8,0},{1,9},{9,1},{2,10},{10,2},{3,11},{11,3},{4,12},{12,4},... | collective-permute-start | bytes 786440 | tf_op jit(solution)/shard_map/ppermute | solution.py:44
  120.8 0.5 collective-permute-start.20
  121.3 7.2 %collective-permute-done.22 = bf16[1,64,2048]{2,1,0:T(8,128)(2,1)S(1)} collective-permute-done((bf16[1,64,2048]{2,1,0:T(8,128)(2,1)S(1)}, bf16[1,64,2048]{2,1,0:T(8,128)(2,1)S(1)}, u32[]{:S(2)}, u32[]{:S(2)}) %collective-permute-start.22) | collective-permute-done | bytes 262176 | tf_op jit(solution)/shard_map/ppermute | solution.py:44
  128.5 3.7 %collective-permute-done.20 = bf16[1,64,2048]{2,1,0:T(8,128)(2,1)S(1)} collective-permute-done((bf16[1,64,2048]{2,1,0:T(8,128)(2,1)S(1)}, bf16[1,64,2048]{2,1,0:T(8,128)(2,1)S(1)}, u32[]{:S(2)}, u32[]{:S(2)}) %collective-permute-start.20) | collective-permute-done | bytes 262176 | tf_op jit(solution)/shard_map/ppermute | solution.py:44
  132.1 0.7 copy.15
  132.8 0.7 copy.16
  (21 shorter events, 0.0 us)
Async XLA Ops:
  0.6 37.6 %collective-permute-start.3 = (bf16[384,2048]{1,0:T(8,128)(2,1)}, bf16[384,2048]{1,0:T(8,128)(2,1)S(1)}, u32[]{:S(2)}, u32[]{:S(2)}) collective-permute-start(bf16[384,2048]{1,0:T(8,128)(2,1)} %bitcast.22), channel_id=1, source_target_pairs={{0,16},{16,0},{1,17},{17,1},{2,18},{18,2},{3,19},{19,3},{4,20},{20... | collective-permute-start | bytes 4718600 | tf_op jit(solution)/shard_map/ppermute | solution.py:44
  1.2 37.1 %collective-permute-start.4 = (bf16[384,2048]{1,0:T(8,128)(2,1)}, bf16[384,2048]{1,0:T(8,128)(2,1)S(1)}, u32[]{:S(2)}, u32[]{:S(2)}) collective-permute-start(bf16[384,2048]{1,0:T(8,128)(2,1)} %bitcast.24), channel_id=1, source_target_pairs={{0,16},{16,0},{1,17},{17,1},{2,18},{18,2},{3,19},{19,3},{4,20},{20... | collective-permute-start | bytes 4718600 | tf_op jit(solution)/shard_map/ppermute | solution.py:44
  1.2 37.0 %collective-permute-start.5 = (bf16[384,2048]{1,0:T(8,128)(2,1)}, bf16[384,2048]{1,0:T(8,128)(2,1)}, u32[]{:S(2)}, u32[]{:S(2)}) collective-permute-start(bf16[384,2048]{1,0:T(8,128)(2,1)} %bitcast.26), channel_id=1, source_target_pairs={{0,16},{16,0},{1,17},{17,1},{2,18},{18,2},{3,19},{19,3},{4,20},{20... | collective-permute-start | bytes 4718600 | tf_op jit(solution)/shard_map/ppermute | solution.py:44
  3.9 11.5 %collective-permute-start = (bf16[64,4224]{1,0:T(8,128)(2,1)}, bf16[64,4224]{1,0:T(8,128)(2,1)}, u32[]{:S(2)}, u32[]{:S(2)}) collective-permute-start(bf16[64,4224]{1,0:T(8,128)(2,1)} %pack_rows.1.refs_0_), channel_id=1, source_target_pairs={{0,2},{2,4},{4,6},{6,7},{7,5},{5,3},{3,1},{1,0},{16,17},{18,16},{2... | collective-permute-start | bytes 1622024 | tf_op jit(solution)/shard_map/ppermute | solution.py:39
  11.1 13.4 %collective-permute-start.1 = (bf16[64,4224]{1,0:T(8,128)(2,1)}, bf16[64,4224]{1,0:T(8,128)(2,1)S(1)}, u32[]{:S(2)}, u32[]{:S(2)}) collective-permute-start(bf16[64,4224]{1,0:T(8,128)(2,1)} %pack_rows.1.refs_0_), channel_id=1, source_target_pairs={{0,1},{2,0},{4,2},{6,4},{7,6},{5,7},{3,5},{1,3},{16,18},{18,20},{2... | collective-permute-start | bytes 1622024 | tf_op jit(solution)/shard_map/ppermute | solution.py:39
  15.4 12.7 %collective-permute-start.2 = (bf16[64,4224]{1,0:T(8,128)(2,1)}, bf16[64,4224]{1,0:T(8,128)(2,1)}, u32[]{:S(2)}, u32[]{:S(2)}) collective-permute-start(bf16[64,4224]{1,0:T(8,128)(2,1)} %collective-permute-done.refs_1_), channel_id=1, source_target_pairs={{0,2},{2,4},{4,6},{6,7},{7,5},{5,3},{3,1},{1,0},{16,17},{18,16},{2... | collective-permute-start | bytes 1622024 | tf_op jit(solution)/shard_map/ppermute | solution.py:39
  24.5 13.7 %collective-permute-start.6 = (bf16[64,4224]{1,0:T(8,128)(2,1)S(1)}, bf16[64,4224]{1,0:T(8,128)(2,1)}, u32[]{:S(2)}, u32[]{:S(2)}) collective-permute-start(bf16[64,4224]{1,0:T(8,128)(2,1)S(1)} %collective-permute-done.1.refs_2_), channel_id=1, source_target_pairs={{0,1},{2,0},{4,2},{6,4},{7,6},{5,7},{3,5},{1,3},{16,18},{18,20},{2... | collective-permute-start | bytes 1622024 | tf_op jit(solution)/shard_map/ppermute | solution.py:39
  24.5 0.8 copy-start.8
  28.0 24.8 %collective-permute-start.9 = (bf16[64,4224]{1,0:T(8,128)(2,1)}, bf16[64,4224]{1,0:T(8,128)(2,1)}, u32[]{:S(2)}, u32[]{:S(2)}) collective-permute-start(bf16[64,4224]{1,0:T(8,128)(2,1)} %collective-permute-done.2.refs_3_), channel_id=1, source_target_pairs={{0,2},{2,4},{4,6},{6,7},{7,5},{5,3},{3,1},{1,0},{16,17},{18,16},{2... | collective-permute-start | bytes 1622024 | tf_op jit(solution)/shard_map/ppermute | solution.py:39
  38.3 16.6 %collective-permute-start.7 = (bf16[64,4224]{1,0:T(8,128)(2,1)}, bf16[64,4224]{1,0:T(8,128)(2,1)}, u32[]{:S(2)}, u32[]{:S(2)}) collective-permute-start(bf16[64,4224]{1,0:T(8,128)(2,1)} %collective-permute-done.6.refs_0_.refs_4_), channel_id=1, source_target_pairs={{0,1},{2,0},{4,2},{6,4},{7,6},{5,7},{3,5},{1,3},{16,18},{18,20},{2... | collective-permute-start | bytes 1622024 | tf_op jit(solution)/shard_map/ppermute | solution.py:39
  38.3 1.4 %copy-start = (bf16[384,2048]{1,0:T(8,128)(2,1)S(1)}, bf16[384,2048]{1,0:T(8,128)(2,1)}, u32[]{:S(2)}) copy-start(bf16[384,2048]{1,0:T(8,128)(2,1)} %get-tuple-element.55.refs_4_.refs_2_) | copy-start | bytes 4718596
  39.7 1.4 %copy-start.2 = (bf16[384,2048]{1,0:T(8,128)(2,1)S(1)}, bf16[384,2048]{1,0:T(8,128)(2,1)}, u32[]{:S(2)}) copy-start(bf16[384,2048]{1,0:T(8,128)(2,1)} %get-tuple-element.56.refs_5_.refs_3_) | copy-start | bytes 4718596
  41.1 1.4 %copy-start.4 = (bf16[384,2048]{1,0:T(8,128)(2,1)S(1)}, bf16[384,2048]{1,0:T(8,128)(2,1)}, u32[]{:S(2)}) copy-start(bf16[384,2048]{1,0:T(8,128)(2,1)} %get-tuple-element.57.refs_6_.refs_4_) | copy-start | bytes 4718596
  42.5 1.0 copy-start.6
  43.6 1.0 copy-start.9
  44.6 10.3 %copy-start.1 = (bf16[384,2048]{1,0:T(8,128)(2,1)S(1)}, bf16[384,2048]{1,0:T(8,128)(2,1)}, u32[]{:S(2)}) copy-start(bf16[384,2048]{1,0:T(8,128)(2,1)} %get-tuple-element.55.refs_4_.refs_2_) | copy-start | bytes 4718596
  44.6 10.3 %copy-start.3 = (bf16[384,2048]{1,0:T(8,128)(2,1)S(1)}, bf16[384,2048]{1,0:T(8,128)(2,1)}, u32[]{:S(2)}) copy-start(bf16[384,2048]{1,0:T(8,128)(2,1)} %get-tuple-element.56.refs_5_.refs_3_) | copy-start | bytes 4718596
  44.6 10.3 %copy-start.5 = (bf16[384,2048]{1,0:T(8,128)(2,1)S(1)}, bf16[384,2048]{1,0:T(8,128)(2,1)}, u32[]{:S(2)}) copy-start(bf16[384,2048]{1,0:T(8,128)(2,1)} %get-tuple-element.57.refs_6_.refs_4_) | copy-start | bytes 4718596
  52.8 10.0 %collective-permute-start.10 = (bf16[64,4224]{1,0:T(8,128)(2,1)}, bf16[64,4224]{1,0:T(8,128)(2,1)S(1)}, u32[]{:S(2)}, u32[]{:S(2)}) collective-permute-start(bf16[64,4224]{1,0:T(8,128)(2,1)} %collective-permute-done.9.refs_0_.refs_6_), channel_id=1, source_target_pairs={{0,2},{2,4},{4,6},{6,7},{7,5},{5,3},{3,1},{1,0},{16,17},{18,16},{2... | collective-permute-start | bytes 1622024 | tf_op jit(solution)/shard_map/ppermute | solution.py:39
  61.5 12.6 %collective-permute-start.8 = (bf16[64,4096]{1,0:T(8,128)(2,1)S(1)}, bf16[64,4096]{1,0:T(8,128)(2,1)S(1)}, u32[]{:S(2)}, u32[]{:S(2)}) collective-permute-start(bf16[64,4096]{1,0:T(8,128)(2,1)S(1)} %get-tuple-element.60), channel_id=1, source_target_pairs={{0,2},{2,4},{4,6},{6,7},{7,5},{5,3},{3,1},{1,0},{16,17},{18,16},{2... | collective-permute-start | bytes 1572872 | tf_op jit(solution)/shard_map/ppermute | solution.py:39
  69.1 7.3 %copy-start.7 = (bf16[64,4224]{1,0:T(8,128)(2,1)S(1)}, bf16[64,4224]{1,0:T(8,128)(2,1)}, u32[]{:S(2)}) copy-start(bf16[64,4224]{1,0:T(8,128)(2,1)} %pack_rows.1.refs_0_) | copy-start | bytes 1622020
  69.2 7.3 %copy-start.10 = (bf16[64,4224]{1,0:T(8,128)(2,1)S(1)}, bf16[64,4224]{1,0:T(8,128)(2,1)}, u32[]{:S(2)}) copy-start(bf16[64,4224]{1,0:T(8,128)(2,1)} %copy-done.8) | copy-start | bytes 1622020
  74.2 9.9 %collective-permute-start.12 = (bf16[64,4096]{1,0:T(8,128)(2,1)S(1)}, bf16[64,4096]{1,0:T(8,128)(2,1)S(1)}, u32[]{:S(2)}, u32[]{:S(2)}) collective-permute-start(bf16[64,4096]{1,0:T(8,128)(2,1)S(1)} %add_convert_fusion.6), channel_id=1, source_target_pairs={{0,2},{2,4},{4,6},{6,7},{7,5},{5,3},{3,1},{1,0},{16,17},{18,16},{2... | collective-permute-start | bytes 1572872 | tf_op jit(solution)/shard_map/ppermute | solution.py:39
  76.5 9.2 %collective-permute-start.11 = (bf16[64,4096]{1,0:T(8,128)(2,1)S(1)}, bf16[64,4096]{1,0:T(8,128)(2,1)S(1)}, u32[]{:S(2)}, u32[]{:S(2)}) collective-permute-start(bf16[64,4096]{1,0:T(8,128)(2,1)S(1)} %get-tuple-element.70), channel_id=1, source_target_pairs={{0,1},{2,0},{4,2},{6,4},{7,6},{5,7},{3,5},{1,3},{16,18},{18,20},{2... | collective-permute-start | bytes 1572872 | tf_op jit(solution)/shard_map/ppermute | solution.py:39
  85.6 3.4 %collective-permute-start.15 = (bf16[384,2048]{1,0:T(8,128)(2,1)S(1)}, bf16[384,2048]{1,0:T(8,128)(2,1)S(1)}, u32[]{:S(2)}, u32[]{:S(2)}) collective-permute-start(bf16[384,2048]{1,0:T(8,128)(2,1)S(1)} %get-tuple-element.93), channel_id=1, source_target_pairs={{0,16},{16,0},{1,17},{17,1},{2,18},{18,2},{3,19},{19,3},{4,20},{20... | collective-permute-start | bytes 4718600 | tf_op jit(solution)/shard_map/ppermute | solution.py:44
  85.6 5.7 %collective-permute-start.16 = (bf16[384,2048]{1,0:T(8,128)(2,1)S(1)}, bf16[384,2048]{1,0:T(8,128)(2,1)S(1)}, u32[]{:S(2)}, u32[]{:S(2)}) collective-permute-start(bf16[384,2048]{1,0:T(8,128)(2,1)S(1)} %get-tuple-element.95), channel_id=1, source_target_pairs={{0,16},{16,0},{1,17},{17,1},{2,18},{18,2},{3,19},{19,3},{4,20},{20... | collective-permute-start | bytes 4718600 | tf_op jit(solution)/shard_map/ppermute | solution.py:44
  86.3 13.2 %collective-permute-start.14 = (bf16[64,4096]{1,0:T(8,128)(2,1)S(1)}, bf16[64,4096]{1,0:T(8,128)(2,1)S(1)}, u32[]{:S(2)}, u32[]{:S(2)}) collective-permute-start(bf16[64,4096]{1,0:T(8,128)(2,1)S(1)} %add_convert_fusion.4), channel_id=1, source_target_pairs={{0,2},{2,4},{4,6},{6,7},{7,5},{5,3},{3,1},{1,0},{16,17},{18,16},{2... | collective-permute-start | bytes 1572872 | tf_op jit(solution)/shard_map/ppermute | solution.py:39
  88.0 5.6 %collective-permute-start.17 = (bf16[384,2048]{1,0:T(8,128)(2,1)S(1)}, bf16[384,2048]{1,0:T(8,128)(2,1)S(1)}, u32[]{:S(2)}, u32[]{:S(2)}) collective-permute-start(bf16[384,2048]{1,0:T(8,128)(2,1)S(1)} %get-tuple-element.97), channel_id=1, source_target_pairs={{0,16},{16,0},{1,17},{17,1},{2,18},{18,2},{3,19},{19,3},{4,20},{20... | collective-permute-start | bytes 4718600 | tf_op jit(solution)/shard_map/ppermute | solution.py:44
  88.1 12.0 %collective-permute-start.13 = (bf16[64,4096]{1,0:T(8,128)(2,1)S(1)}, bf16[64,4096]{1,0:T(8,128)(2,1)S(1)}, u32[]{:S(2)}, u32[]{:S(2)}) collective-permute-start(bf16[64,4096]{1,0:T(8,128)(2,1)S(1)} %add_convert_fusion.5), channel_id=1, source_target_pairs={{0,1},{2,0},{4,2},{6,4},{7,6},{5,7},{3,5},{1,3},{16,18},{18,20},{2... | collective-permute-start | bytes 1572872 | tf_op jit(solution)/shard_map/ppermute | solution.py:39
  100.3 9.2 %collective-permute-start.18 = (bf16[64,4096]{1,0:T(8,128)(2,1)S(1)}, bf16[64,4096]{1,0:T(8,128)(2,1)S(1)}, u32[]{:S(2)}, u32[]{:S(2)}) collective-permute-start(bf16[64,4096]{1,0:T(8,128)(2,1)S(1)} %add_convert_fusion.3), channel_id=1, source_target_pairs={{0,1},{2,0},{4,2},{6,4},{7,6},{5,7},{3,5},{1,3},{16,18},{18,20},{2... | collective-permute-start | bytes 1572872 | tf_op jit(solution)/shard_map/ppermute | solution.py:39
  109.7 6.4 %collective-permute-start.21 = (bf16[64,2048]{1,0:T(8,128)(2,1)S(1)}, bf16[64,2048]{1,0:T(8,128)(2,1)S(1)}, u32[]{:S(2)}, u32[]{:S(2)}) collective-permute-start(bf16[64,2048]{1,0:T(8,128)(2,1)S(1)} %get-tuple-element.107), channel_id=1, source_target_pairs={{0,1},{2,0},{4,2},{6,4},{7,6},{5,7},{3,5},{1,3},{16,18},{18,20},{2... | collective-permute-start | bytes 786440 | tf_op jit(solution)/shard_map/ppermute | solution.py:39
  110.0 8.9 %collective-permute-start.19 = (bf16[64,2048]{1,0:T(8,128)(2,1)S(1)}, bf16[64,2048]{1,0:T(8,128)(2,1)S(1)}, u32[]{:S(2)}, u32[]{:S(2)}) collective-permute-start(bf16[64,2048]{1,0:T(8,128)(2,1)S(1)} %get-tuple-element.108), channel_id=1, source_target_pairs={{0,1},{2,0},{4,2},{6,4},{7,6},{5,7},{3,5},{1,3},{16,18},{18,20},{2... | collective-permute-start | bytes 786440 | tf_op jit(solution)/shard_map/ppermute | solution.py:39
  119.2 9.3 %collective-permute-start.22 = (bf16[1,64,2048]{2,1,0:T(8,128)(2,1)S(1)}, bf16[1,64,2048]{2,1,0:T(8,128)(2,1)S(1)}, u32[]{:S(2)}, u32[]{:S(2)}) collective-permute-start(bf16[1,64,2048]{2,1,0:T(8,128)(2,1)S(1)} %get-tuple-element.105), channel_id=1, source_target_pairs={{0,8},{8,0},{1,9},{9,1},{2,10},{10,2},{3,11},{11,3},{4,12},{12,4},... | collective-permute-start | bytes 786440 | tf_op jit(solution)/shard_map/ppermute | solution.py:44
  120.8 11.4 %collective-permute-start.20 = (bf16[1,64,2048]{2,1,0:T(8,128)(2,1)S(1)}, bf16[1,64,2048]{2,1,0:T(8,128)(2,1)S(1)}, u32[]{:S(2)}, u32[]{:S(2)}) collective-permute-start(bf16[1,64,2048]{2,1,0:T(8,128)(2,1)S(1)} %get-tuple-element.106), channel_id=1, source_target_pairs={{0,8},{8,0},{1,9},{9,1},{2,10},{10,2},{3,11},{11,3},{4,12},{12,4},... | collective-permute-start | bytes 786440 | tf_op jit(solution)/shard_map/ppermute | solution.py:44

commit v6 on v5

--- a/solution.py
+++ b/solution.py
@@ -11,7 +11,7 @@
 
 
 def vmem(peers):
-    return (30 if peers <= 8 else 60) * 2**20
+    return (24 if peers <= 8 else 60) * 2**20
 
 
 def ring_order(peers):
@@ -28,15 +28,18 @@
     return order
 
 
-def ring_shift(value, by):
-    peers = lax.axis_size("exp")
+def ring_shift(value, by, sections=0):
+    peers, layers = lax.axis_size("exp"), lax.axis_size("section")
     order = ring_order(peers)
     pairs = []
     for rep in range(lax.axis_size("rep")):
         step = by if rep % 2 == 0 else -by
-        for spot in range(peers):
-            pairs.append((rep * peers + order[spot], rep * peers + order[(spot + step) % peers]))
-    return lax.ppermute(value, ("rep", "exp"), pairs)
+        for layer in range(layers):
+            source = (rep * layers + layer) * peers
+            target = (rep * layers + (layer + sections) % layers) * peers
+            for spot in range(peers):
+                pairs.append((source + order[spot], target + order[(spot + step) % peers]))
+    return lax.ppermute(value, ("rep", "section", "exp"), pairs)
 
 
 def from_behind(value, axis, by):
@@ -117,7 +120,10 @@
         in_specs=[pl.BlockSpec(memory_space=pl.ANY)] * len(weights),
         out_specs=[whole()] * len(weights),
         scratch_shapes=[pltpu.SemaphoreType.DMA((len(weights),))],
-        cost_estimate=pl.CostEstimate(flops=0, bytes_accessed=10**7, transcendentals=0),
+        compiler_params=pltpu.CompilerParams(vmem_limit_bytes=8 * 2**20),
+        cost_estimate=pl.CostEstimate(
+            flops=0, bytes_accessed=sum(4 * w.size for w in weights), transcendentals=0
+        ),
         name="load_weights",
     )(*weights)
 
@@ -264,7 +270,7 @@
     lanes = -(-3 * experts // 128) * 128
     shards_of = [w.reshape(half, width) for w in (gate_weight, up_weight, down_weight)]
     other = [from_behind(w, "rep", 1) for w in shards_of]
-    own = load_call(shards_of)
+    own = load_call(shards_of[:1]) + load_call(shards_of[1:])
     weights = list(own) + other
     first = (lax.axis_index("exp") * local_experts).astype(jnp.int32).reshape(1)
     home = pl.pallas_call(
@@ -272,6 +278,7 @@
         out_shape=jax.ShapeDtypeStruct((tokens, 2 * width + lanes), BF16),
         in_specs=[whole()] * 5,
         out_specs=whole(),
+        compiler_params=pltpu.CompilerParams(vmem_limit_bytes=8 * 2**20),
         name="pack_rows",
     )(row_codes[0], block_exponents[0].T, routes[0].T, route_weight[0].T, out_grad[0])
 
@@ -284,7 +291,7 @@
     groups = [names[i : i + 4] for i in range(0, len(names) - 4, 4)]
     groups.append([name for name in names[-4:] if name[0] == "far"])
     groups.append([name for name in names[-4:] if name[0] == "near"])
-    held = {("near", 0): home, ("far", 0): tie((home, own))[0]}
+    held = {("near", 0): home, ("far", 0): tie((home, own[0]))[0]}
     partial, kept = {}, []
 
     def work(group):
@@ -298,6 +305,9 @@
         held["near", k] = ring_shift(held["near", k - 1], 1)
         if k <= behind:
             held["far", k] = ring_shift(held["far", k - 1], -1)
+        if k == 1:
+            held["near", 1], own = tie((held["near", 1], own))
+            weights[:3] = own
         if k % 2 == 1 and k > 1:
             work(groups[(k - 3) // 2])
             held["near", k], kept[-1] = tie((held["near", k], kept[-1]))
@@ -305,31 +315,44 @@
     far_sum = ring_shift(partial["far", behind], 1)
     held["near", ahead], kept[-1] = tie((held["near", ahead], kept[-1]))
     work(groups[-1])
-    far_sum, near_sum = tie((far_sum, partial["near", ahead]))
-    own_total = received = totals = None
+    both = (slice(0, width), slice(width, 2 * width))
+    near_sum = partial["near", ahead]
+    own_total = other_total = None
     blocks = [held[name] for group in groups for name in group]
+    steps = (1, -1)
+    finals = []
+    for part, step in zip(both, steps):
+        kept_here = add(home[:, part], partial["near", 0][:, part])
+        finals.append([from_behind(kept_here, "section", step)])
     for k in range(ahead, 1, -1):
         near_sum = ring_shift(near_sum, -1)
         left = k - 2
-        if left >= 1:
+        if left > 1:
+            far_done = far_sum
             far_sum = ring_shift(add(far_sum, partial["far", left]), 1)
-        if k == ahead:
+            near_sum, _ = tie((near_sum, far_done))
+        if k == 3:
             own_total, other_total = weight_call(blocks, kept, width, peers)
-            near_sum, far_sum, own_total, other_total = tie(
-                (near_sum, far_sum, own_total, other_total)
-            )
-            received = [from_behind(g, "rep", 1) for g in other_total]
-        elif k == ahead - 1:
-            totals = [add(a, b) for a, b in zip(own_total, received)]
-            near_sum, far_sum, totals = tie((near_sum, far_sum, totals))
-        if k > 2:
+            here = [final[0] for final in finals]
+            near_sum, own_total, other_total, _ = tie((near_sum, own_total, other_total, here))
+            near_sum = add(near_sum, partial["near", 2])
+            for final, part, step in zip(finals, both, steps):
+                last = add(far_sum[:, part], partial["far", 1][:, part])
+                final.append(ring_shift(last, 1, step))
+        elif k == 2:
+            here = [final[1] for final in finals]
+            near_sum, other_total, _ = tie((near_sum, other_total, here))
+        else:
             near_sum = add(near_sum, partial["near", k - 1])
+    for final, part, step in zip(finals, both, steps):
+        final.append(ring_shift(add(near_sum[:, part], partial["near", 1][:, part]), -1, step))
+    received = [from_behind(g, "rep", 1) for g in other_total]
+    totals = [add(a, b) for a, b in zip(own_total, received)]
     results = []
-    for part, step in ((slice(0, width), 1), (slice(width, 2 * width), -1)):
-        arrived = ring_shift(add(near_sum[:, part], partial["near", 1][:, part]), -1)
-        total = home[:, part].astype(F32) + partial["near", 0][:, part].astype(F32)
-        total = total + far_sum[:, part].astype(F32) + arrived.astype(F32)
-        results.append(from_behind(total.astype(BF16)[None], "section", step))
+    for final in finals:
+        if results:
+            final, _ = tie((final, results[0]))
+        results.append(sum(f.astype(F32) for f in final).astype(BF16)[None])
     shape = (1, local_experts, half_units, width)
     return tuple(results) + tuple(t.reshape(shape) for t in totals)
 

time: 134 us -> 126 us (0.940)
  waiting for transfers between devices: 62.4 us -> 45.6 us
  local copies, waits for them, and re-layouts: 8.57 us -> 15 us
  starting transfers between devices: 20 us -> 25.8 us
  Pallas kernels: 35.5 us -> 30.4 us
  other arithmetic: 6.27 us -> 7.62 us
    ppermute x8, waiting for transfers between devices: 12.1 us -> 0.02 us  [from_behind(): lax.ppermute(value, axis, [(i, (i + by) % peers) for i in range(peers)])]
    unnamed x24 -> x36, local copies, waits for them, and re-layouts: 8.57 us -> 15 us
    ppermute x15 -> x16, waiting for transfers between devices: 50.3 us -> 45.6 us  [ring_shift(): return lax.ppermute(value, ('rep', 'section', 'exp'), pairs)]
    ppermute x15 -> x16, starting transfers between devices: 16.4 us -> 21.1 us  [ring_shift(): return lax.ppermute(value, ('rep', 'section', 'exp'), pairs)]
    pallas_call x1 -> x2, Pallas kernels: 4.56 us -> 0.35 us  [load_call(): pl.pallas_call(load_kernel, out_shape=[jax.ShapeDtypeStruct(w.shape, w.dt...]
    pallas_call x1, Pallas kernels: 2.21 us -> 0.33 us  [shards(): pl.pallas_call(functools.partial(pack_kernel, experts), out_shape=jax.Sha...]
    convert_element_type x8 -> x9, other arithmetic: 5.99 us -> 6.01 us  [add(): return (a.astype(F32) + b.astype(F32)).astype(BF16)]
  transfers between devices with their start and end apart: 23 -> 24, of which waited for: 16 -> 8; matrix products, arithmetic and copies ran while one was open for 4% -> 5% of each run, Pallas kernels for 27% -> 24%
where the time goes in v6:
time: 126 us; the launch traced here: 125 us
  waiting for transfers between devices  45.6 us (36%)
  Pallas kernels  30.4 us (24%)
  starting transfers between devices  25.8 us (20%)
  local copies, waits for them, and re-layouts  15 us (12%)
  other arithmetic  7.62 us (6%)
    ppermute x16, waiting for transfers between devices, ring_shift(): return lax.ppermute(value, ('rep', 'section', 'exp'), pairs)  45.6 us
    pallas_call x3, Pallas kernels, expert_call(): pl.pallas_call(functools.partial(expert_kernel, count, experts, local_exp...  22.3 us
    ppermute x16, starting transfers between devices, ring_shift(): return lax.ppermute(value, ('rep', 'section', 'exp'), pairs)  21.1 us
    unnamed x36, local copies, waits for them, and re-layouts  15 us
    pallas_call x1, Pallas kernels, weight_call(): pl.pallas_call(functools.partial(weight_kernel, len(kept), count), out_sh...  7.43 us
    convert_element_type x9, other arithmetic, add(): return (a.astype(F32) + b.astype(F32)).astype(BF16)  6.01 us
    ppermute x8, starting transfers between devices, from_behind(): lax.ppermute(value, axis, [(i, (i + by) % peers) for i in range(peers)])  4.67 us
  transfers between devices with their start and end apart: 24, of which 8 were waited for; matrix products, arithmetic and copies ran while one was open for 5% of the time, Pallas kernels for 24%

profile of v6, /device:TPU:0, one launch (start us, length us, event | category | flops | bytes accessed | tf_op | source)
XLA Modules:
  0.0 125.2 jit_solution(4042210219790394589)
XLA Ops:
  0.6 0.5 collective-permute-start.3
  1.2 0.1 collective-permute-start.4
  1.2 0.4 collective-permute-start.5
  1.7 0.9 copy-done.10
  2.6 0.9 copy-done.11
  3.6 0.7 copy-done.12
  4.3 0.7 copy-done.13
  4.9 0.7 copy-done.14
  5.6 0.3 pack_rows.1.refs_0_
  6.0 0.0 copy-start.5
  6.0 2.7 %collective-permute-start = (bf16[64,4224]{1,0:T(8,128)(2,1)S(1)}, bf16[64,4224]{1,0:T(8,128)(2,1)S(1)}, u32[]{:S(2)}, u32[]{:S(2)}) collective-permute-start(bf16[64,4224]{1,0:T(8,128)(2,1)S(1)} %pack_rows.1.refs_0_), channel_id=1, source_target_pairs={{0,2},{2,4},{4,6},{6,7},{7,5},{5,3},{3,1},{1,0},{8,10},{10,12},{12... | collective-permute-start | bytes 1622024 | tf_op jit(solution)/shard_map/ppermute | solution.py:42
  8.7 1.4 %copy-done.7 = bf16[1,2,192,2048]{3,2,1,0:T(8,128)(2,1)S(1)} copy-done((bf16[1,2,192,2048]{3,2,1,0:T(8,128)(2,1)S(1)}, bf16[1,2,192,2048]{3,2,1,0:T(8,128)(2,1)}, u32[]{:S(2)}) %copy-start.7) | copy-done | bytes 1572888
  10.1 0.1 load_weights.2.refs_4_.refs_2_
  10.2 0.1 collective-permute-start.1
  10.3 1.2 copy-done.8
  11.5 0.5 copy-done.9
  12.0 0.2 load_weights.3
  12.2 0.0 copy-start
  12.2 1.1 copy-done
  13.4 1.1 copy-done.3
  14.5 5.6 %collective-permute-done.refs_1_ = bf16[64,4224]{1,0:T(8,128)(2,1)S(1)} collective-permute-done((bf16[64,4224]{1,0:T(8,128)(2,1)S(1)}, bf16[64,4224]{1,0:T(8,128)(2,1)S(1)}, u32[]{:S(2)}, u32[]{:S(2)}) %collective-permute-start) | collective-permute-done | bytes 540704 | tf_op jit(solution)/shard_map/ppermute | solution.py:42
  20.1 2.5 %collective-permute-start.2 = (bf16[64,4224]{1,0:T(8,128)(2,1)S(1)}, bf16[64,4224]{1,0:T(8,128)(2,1)}, u32[]{:S(2)}, u32[]{:S(2)}) collective-permute-start(bf16[64,4224]{1,0:T(8,128)(2,1)S(1)} %collective-permute-done.refs_1_), channel_id=1, source_target_pairs={{0,2},{2,4},{4,6},{6,7},{7,5},{5,3},{3,1},{1,0},{8,10},{10,12},{12... | collective-permute-start | bytes 1622024 | tf_op jit(solution)/shard_map/ppermute | solution.py:42
  22.6 0.8 copy-done.15
  23.4 11.2 %collective-permute-done.2.refs_3_ = bf16[64,4224]{1,0:T(8,128)(2,1)} collective-permute-done((bf16[64,4224]{1,0:T(8,128)(2,1)S(1)}, bf16[64,4224]{1,0:T(8,128)(2,1)}, u32[]{:S(2)}, u32[]{:S(2)}) %collective-permute-start.2) | collective-permute-done | bytes 540704 | tf_op jit(solution)/shard_map/ppermute | solution.py:42
  34.6 2.6 %collective-permute-start.12 = (bf16[64,4224]{1,0:T(8,128)(2,1)}, bf16[64,4224]{1,0:T(8,128)(2,1)}, u32[]{:S(2)}, u32[]{:S(2)}) collective-permute-start(bf16[64,4224]{1,0:T(8,128)(2,1)} %collective-permute-done.2.refs_3_), channel_id=1, source_target_pairs={{0,2},{2,4},{4,6},{6,7},{7,5},{5,3},{3,1},{1,0},{8,10},{10,12},{12... | collective-permute-start | bytes 1622024 | tf_op jit(solution)/shard_map/ppermute | solution.py:42
  37.3 1.4 %copy-done.1 = bf16[384,2048]{1,0:T(8,128)(2,1)S(1)} copy-done((bf16[384,2048]{1,0:T(8,128)(2,1)S(1)}, bf16[384,2048]{1,0:T(8,128)(2,1)}, u32[]{:S(2)}) %copy-start.1) | copy-done | bytes 1572888
  38.7 1.4 %copy-done.4 = bf16[384,2048]{1,0:T(8,128)(2,1)S(1)} copy-done((bf16[384,2048]{1,0:T(8,128)(2,1)S(1)}, bf16[384,2048]{1,0:T(8,128)(2,1)}, u32[]{:S(2)}) %copy-start.4) | copy-done | bytes 1572888
  40.1 1.0 copy-done.6
  41.1 1.0 copy-done.16
  42.2 8.6 %expert_rows.3 = (bf16[64,4096]{1,0:T(8,128)(2,1)S(1)}, bf16[64,4096]{1,0:T(8,128)(2,1)S(1)}, bf16[64,4096]{1,0:T(8,128)(2,1)S(1)}, bf16[64,4096]{1,0:T(8,128)(2...) custom-call(s32[1]{0:T(128)} %bitcast.8.first_ref, ...), custom_call_target="tpu_custom_call" | custom-call | flops 4831838208 | bytes 13631488 | tf_op jit(solution)/shard_map/expert_rows/pallas_call | solution.py:190
  50.8 2.1 %collective-permute-start.13 = (bf16[64,4224]{1,0:T(8,128)(2,1)}, bf16[64,4224]{1,0:T(8,128)(2,1)S(1)}, u32[]{:S(2)}, u32[]{:S(2)}) collective-permute-start(bf16[64,4224]{1,0:T(8,128)(2,1)} %collective-permute-done.12.refs_0_.refs_6_), channel_id=1, source_target_pairs={{0,2},{2,4},{4,6},{6,7},{7,5},{5,3},{3,1},{1,0},{8,10},{10,12},{12... | collective-permute-start | bytes 1622024 | tf_op jit(solution)/shard_map/ppermute | solution.py:42
  52.9 6.8 %expert_rows.4 = (bf16[64,4096]{1,0:T(8,128)(2,1)S(1)}, bf16[64,4096]{1,0:T(8,128)(2,1)S(1)}, bf16[768,128]{1,0:T(8,128)(2,1)S(1)}, bf16[768,128]{1,0:T(8,128)(2,1)S(1)}, bf16[768,128]{1,0:T(8,128)(2,1)S(1)}) custom-call(s32[1]{0:T(128)} %bitcast.8.first_ref, bf16[64,4224]{1,0:T(8,128)(2,1)} %collective-permute-done.7.refs_0_.refs_4_, ...), custom_call_target="tpu_custom_call" | custom-call | flops 2415919104 | bytes 11534336 | tf_op jit(solution)/shard_map/expert_rows/pallas_call | solution.py:190
  59.7 1.6 %collective-permute-start.9 = (bf16[64,4096]{1,0:T(8,128)(2,1)S(1)}, bf16[64,4096]{1,0:T(8,128)(2,1)S(1)}, u32[]{:S(2)}, u32[]{:S(2)}) collective-permute-start(bf16[64,4096]{1,0:T(8,128)(2,1)S(1)} %get-tuple-element.66), channel_id=1, source_target_pairs={{0,2},{2,4},{4,6},{6,7},{7,5},{5,3},{3,1},{1,0},{8,10},{10,12},{12... | collective-permute-start | bytes 1572872 | tf_op jit(solution)/shard_map/ppermute | solution.py:42
  61.3 6.8 %expert_rows.5 = (bf16[64,4096]{1,0:T(8,128)(2,1)S(1)}, bf16[64,4096]{1,0:T(8,128)(2,1)S(1)}, bf16[768,128]{1,0:T(8,128)(2,1)S(1)}, bf16[768,128]{1,0:T(8,128)(2,1)S(1)}, bf16[768,128]{1,0:T(8,128)(2,1)S(1)}) custom-call(s32[1]{0:T(128)} %bitcast.8.first_ref, bf16[64,4224]{1,0:T(8,128)(2,1)} %collective-permute-done.12.refs_0_.refs_6_, ...), custom_call_target="tpu_custom_call" | custom-call | flops 2415919104 | bytes 11534336 | tf_op jit(solution)/shard_map/expert_rows/pallas_call | solution.py:190
  68.2 0.5 collective-permute-start.14
  68.7 0.1 add_convert_fusion.11
  68.8 1.6 %collective-permute-start.16 = (bf16[64,2048]{1,0:T(8,128)(2,1)S(1)}, bf16[64,2048]{1,0:T(8,128)(2,1)S(1)}, u32[]{:S(2)}, u32[]{:S(2)}) collective-permute-start(bf16[64,2048]{1,0:T(8,128)(2,1)S(1)} %get-tuple-element.111), channel_id=1, source_target_pairs={{0,8},{8,0},{1,9},{9,1},{2,10},{10,2},{3,11},{11,3},{4,12},{12,4},... | collective-permute-start | bytes 786440 | tf_op jit(solution)/shard_map/ppermute | solution.py:47
  70.4 0.5 collective-permute-start.6
  70.9 6.5 %collective-permute-done.14 = bf16[64,4096]{1,0:T(8,128)(2,1)S(1)} collective-permute-done((bf16[64,4096]{1,0:T(8,128)(2,1)S(1)}, bf16[64,4096]{1,0:T(8,128)(2,1)S(1)}, u32[]{:S(2)}, u32[]{:S(2)}) %collective-permute-start.14) | collective-permute-done | bytes 524320 | tf_op jit(solution)/shard_map/ppermute | solution.py:42
  77.4 0.1 add_convert_fusion.4
  77.5 0.5 collective-permute-start.15
  78.1 0.1 add_convert_fusion.5
  78.2 1.6 %collective-permute-start.10 = (bf16[64,4096]{1,0:T(8,128)(2,1)S(1)}, bf16[64,4096]{1,0:T(8,128)(2,1)S(1)}, u32[]{:S(2)}, u32[]{:S(2)}) collective-permute-start(bf16[64,4096]{1,0:T(8,128)(2,1)S(1)} %add_convert_fusion.5), channel_id=1, source_target_pairs={{0,2},{2,4},{4,6},{6,7},{7,5},{5,3},{3,1},{1,0},{8,10},{10,12},{12... | collective-permute-start | bytes 1572872 | tf_op jit(solution)/shard_map/ppermute | solution.py:42
  79.8 7.4 %weight_grads.1 = (bf16[384,2048]{1,0:T(8,128)(2,1)S(1)}, bf16[384,2048]{1,0:T(8,128)(2,1)S(1)}, bf16[384,2048]{1,0:T(8,128)(2,1)S(1)}, bf16[384,2048]{1,0:T(8,1...) custom-call(bf16[64,4224]{1,0:T(8,128)(2,1)S(1)} %copy-done.6, ...), custom_call_target="tpu_custom_call" | custom-call | flops 4831838208 | bytes 13631488 | tf_op jit(solution)/shard_map/weight_grads/pallas_call | solution.py:241
  87.3 3.2 %collective-permute-done.15 = bf16[64,4096]{1,0:T(8,128)(2,1)S(1)} collective-permute-done((bf16[64,4096]{1,0:T(8,128)(2,1)S(1)}, bf16[64,4096]{1,0:T(8,128)(2,1)S(1)}, u32[]{:S(2)}, u32[]{:S(2)}) %collective-permute-start.15) | collective-permute-done | bytes 524320 | tf_op jit(solution)/shard_map/ppermute | solution.py:42
  90.5 0.1 add_convert_fusion.3
  90.6 0.5 collective-permute-start.17
  91.1 0.1 add_convert_fusion.10
  91.2 2.6 %collective-permute-start.18 = (bf16[64,2048]{1,0:T(8,128)(2,1)S(1)}, bf16[64,2048]{1,0:T(8,128)(2,1)S(1)}, u32[]{:S(2)}, u32[]{:S(2)}) collective-permute-start(bf16[64,2048]{1,0:T(8,128)(2,1)S(1)} %get-tuple-element.115), channel_id=1, source_target_pairs={{0,10},{2,12},{4,14},{6,15},{7,13},{5,11},{3,9},{1,8},{8,2},{10,4}... | collective-permute-start | bytes 786440 | tf_op jit(solution)/shard_map/ppermute | solution.py:42
  93.8 1.6 %collective-permute-start.11 = (bf16[64,2048]{1,0:T(8,128)(2,1)S(1)}, bf16[64,2048]{1,0:T(8,128)(2,1)S(1)}, u32[]{:S(2)}, u32[]{:S(2)}) collective-permute-start(bf16[64,2048]{1,0:T(8,128)(2,1)S(1)} %get-tuple-element.116), channel_id=1, source_target_pairs={{0,10},{2,12},{4,14},{6,15},{7,13},{5,11},{3,9},{1,8},{8,2},{10,4}... | collective-permute-start | bytes 786440 | tf_op jit(solution)/shard_map/ppermute | solution.py:42
  95.4 5.1 %collective-permute-done.18 = bf16[64,2048]{1,0:T(8,128)(2,1)S(1)} collective-permute-done((bf16[64,2048]{1,0:T(8,128)(2,1)S(1)}, bf16[64,2048]{1,0:T(8,128)(2,1)S(1)}, u32[]{:S(2)}, u32[]{:S(2)}) %collective-permute-start.18) | collective-permute-done | bytes 262176 | tf_op jit(solution)/shard_map/ppermute | solution.py:42
  100.5 3.2 %collective-permute-done.11 = bf16[64,2048]{1,0:T(8,128)(2,1)S(1)} collective-permute-done((bf16[64,2048]{1,0:T(8,128)(2,1)S(1)}, bf16[64,2048]{1,0:T(8,128)(2,1)S(1)}, u32[]{:S(2)}, u32[]{:S(2)}) %collective-permute-start.11) | collective-permute-done | bytes 262176 | tf_op jit(solution)/shard_map/ppermute | solution.py:42
  103.8 0.1 add_convert_fusion.7
  103.9 2.1 %collective-permute-start.19 = (bf16[64,2048]{1,0:T(8,128)(2,1)S(1)}, bf16[64,2048]{1,0:T(8,128)(2,1)S(1)}, u32[]{:S(2)}, u32[]{:S(2)}) collective-permute-start(bf16[64,2048]{1,0:T(8,128)(2,1)S(1)} %get-tuple-element.114), channel_id=1, source_target_pairs={{0,9},{2,8},{4,10},{6,12},{7,14},{5,15},{3,13},{1,11},{8,1},{10,0}... | collective-permute-start | bytes 786440 | tf_op jit(solution)/shard_map/ppermute | solution.py:42
  106.0 1.0 collective-permute-start.22
  107.0 0.1 collective-permute-start.20
  107.1 0.6 collective-permute-start.23
  107.7 6.3 %collective-permute-done.19 = bf16[64,2048]{1,0:T(8,128)(2,1)S(1)} collective-permute-done((bf16[64,2048]{1,0:T(8,128)(2,1)S(1)}, bf16[64,2048]{1,0:T(8,128)(2,1)S(1)}, u32[]{:S(2)}, u32[]{:S(2)}) %collective-permute-start.19) | collective-permute-done | bytes 262176 | tf_op jit(solution)/shard_map/ppermute | solution.py:42
  114.0 0.8 fusion
  114.8 4.4 %collective-permute-done.20 = bf16[64,2048]{1,0:T(8,128)(2,1)S(1)} collective-permute-done((bf16[64,2048]{1,0:T(8,128)(2,1)S(1)}, bf16[64,2048]{1,0:T(8,128)(2,1)S(1)}, u32[]{:S(2)}, u32[]{:S(2)}) %collective-permute-start.20) | collective-permute-done | bytes 262176 | tf_op jit(solution)/shard_map/ppermute | solution.py:42
  119.2 0.8 fusion.1
  120.0 1.7 %add_convert_fusion.2 = bf16[384,2048]{1,0:T(8,128)(2,1)} fusion(bf16[384,2048]{1,0:T(8,128)(2,1)S(1)} %collective-permute-done.21, bf16[384,2048]{1,0:T(8,128)(2,1)S(1)} %get-tuple-element.105), kind=kLoop, calls=%fused_computation.2 | loop fusion | flops 3145728 | bytes 4718592 | tf_op jit(solution)/shard_map/convert_element_type | solution.py:259
  121.7 1.7 %add_convert_fusion.1 = bf16[384,2048]{1,0:T(8,128)(2,1)} fusion(bf16[384,2048]{1,0:T(8,128)(2,1)S(1)} %collective-permute-done.22, bf16[384,2048]{1,0:T(8,128)(2,1)S(1)} %get-tuple-element.107), kind=kLoop, calls=%fused_computation.1 | loop fusion | flops 3145728 | bytes 4718592 | tf_op jit(solution)/shard_map/convert_element_type | solution.py:259
  123.5 1.7 %add_convert_fusion = bf16[384,2048]{1,0:T(8,128)(2,1)} fusion(bf16[384,2048]{1,0:T(8,128)(2,1)S(1)} %collective-permute-done.23, bf16[384,2048]{1,0:T(8,128)(2,1)S(1)} %get-tuple-element.109), kind=kLoop, calls=%fused_computation | loop fusion | flops 3145728 | bytes 4718592 | tf_op jit(solution)/shard_map/convert_element_type | solution.py:259
  (38 shorter events, 0.1 us)
Async XLA Ops:
  0.6 36.6 %collective-permute-start.3 = (bf16[384,2048]{1,0:T(8,128)(2,1)}, bf16[384,2048]{1,0:T(8,128)(2,1)S(1)}, u32[]{:S(2)}, u32[]{:S(2)}) collective-permute-start(bf16[384,2048]{1,0:T(8,128)(2,1)} %bitcast.22), channel_id=1, source_target_pairs={{0,16},{16,0},{1,17},{17,1},{2,18},{18,2},{3,19},{19,3},{4,20},{20... | collective-permute-start | bytes 4718600 | tf_op jit(solution)/shard_map/ppermute | solution.py:47
  1.2 36.1 %collective-permute-start.4 = (bf16[384,2048]{1,0:T(8,128)(2,1)}, bf16[384,2048]{1,0:T(8,128)(2,1)}, u32[]{:S(2)}, u32[]{:S(2)}) collective-permute-start(bf16[384,2048]{1,0:T(8,128)(2,1)} %bitcast.24), channel_id=1, source_target_pairs={{0,16},{16,0},{1,17},{17,1},{2,18},{18,2},{3,19},{19,3},{4,20},{20... | collective-permute-start | bytes 4718600 | tf_op jit(solution)/shard_map/ppermute | solution.py:47
  1.2 36.0 %collective-permute-start.5 = (bf16[384,2048]{1,0:T(8,128)(2,1)}, bf16[384,2048]{1,0:T(8,128)(2,1)}, u32[]{:S(2)}, u32[]{:S(2)}) collective-permute-start(bf16[384,2048]{1,0:T(8,128)(2,1)} %bitcast.26), channel_id=1, source_target_pairs={{0,16},{16,0},{1,17},{17,1},{2,18},{18,2},{3,19},{19,3},{4,20},{20... | collective-permute-start | bytes 4718600 | tf_op jit(solution)/shard_map/ppermute | solution.py:47
  1.7 0.9 copy-start.10
  2.6 0.9 copy-start.11
  3.6 0.7 copy-start.12
  4.3 0.7 copy-start.13
  4.9 0.7 copy-start.14
  6.0 6.2 %copy-start.5 = (bf16[64,4224]{1,0:T(8,128)(2,1)}, bf16[64,4224]{1,0:T(8,128)(2,1)S(1)}, u32[]{:S(2)}) copy-start(bf16[64,4224]{1,0:T(8,128)(2,1)S(1)} %pack_rows.1.refs_0_) | copy-start | bytes 1622020
  6.0 14.1 %collective-permute-start = (bf16[64,4224]{1,0:T(8,128)(2,1)S(1)}, bf16[64,4224]{1,0:T(8,128)(2,1)S(1)}, u32[]{:S(2)}, u32[]{:S(2)}) collective-permute-start(bf16[64,4224]{1,0:T(8,128)(2,1)S(1)} %pack_rows.1.refs_0_), channel_id=1, source_target_pairs={{0,2},{2,4},{4,6},{6,7},{7,5},{5,3},{3,1},{1,0},{8,10},{10,12},{12... | collective-permute-start | bytes 1622024 | tf_op jit(solution)/shard_map/ppermute | solution.py:42
  8.7 1.4 %copy-start.7 = (bf16[1,2,192,2048]{3,2,1,0:T(8,128)(2,1)S(1)}, bf16[1,2,192,2048]{3,2,1,0:T(8,128)(2,1)}, u32[]{:S(2)}) copy-start(bf16[1,2,192,2048]{3,2,1,0:T(8,128)(2,1)} %param.13) | copy-start | bytes 4718596
  10.1 1.4 %copy-start.8 = (bf16[1,2,192,2048]{3,2,1,0:T(8,128)(2,1)S(1)}, bf16[1,2,192,2048]{3,2,1,0:T(8,128)(2,1)}, u32[]{:S(2)}) copy-start(bf16[1,2,192,2048]{3,2,1,0:T(8,128)(2,1)} %param.14) | copy-start | bytes 4718596
  10.1 1.9 %copy-start.9 = (bf16[1,2,192,2048]{3,2,1,0:T(8,128)(2,1)S(1)}, bf16[1,2,192,2048]{3,2,1,0:T(8,128)(2,1)}, u32[]{:S(2)}) copy-start(bf16[1,2,192,2048]{3,2,1,0:T(8,128)(2,1)} %param.15) | copy-start | bytes 4718596
  10.2 13.2 %collective-permute-start.1 = (bf16[64,4224]{1,0:T(8,128)(2,1)S(1)}, bf16[64,4224]{1,0:T(8,128)(2,1)}, u32[]{:S(2)}, u32[]{:S(2)}) collective-permute-start(bf16[64,4224]{1,0:T(8,128)(2,1)S(1)} %pack_rows.1.refs_0_), channel_id=1, source_target_pairs={{0,1},{2,0},{4,2},{6,4},{7,6},{5,7},{3,5},{1,3},{8,9},{10,8},{12,1... | collective-permute-start | bytes 1622024 | tf_op jit(solution)/shard_map/ppermute | solution.py:42
  12.2 1.1 copy-start
  13.4 1.1 copy-start.3
  20.1 14.5 %collective-permute-start.2 = (bf16[64,4224]{1,0:T(8,128)(2,1)S(1)}, bf16[64,4224]{1,0:T(8,128)(2,1)}, u32[]{:S(2)}, u32[]{:S(2)}) collective-permute-start(bf16[64,4224]{1,0:T(8,128)(2,1)S(1)} %collective-permute-done.refs_1_), channel_id=1, source_target_pairs={{0,2},{2,4},{4,6},{6,7},{7,5},{5,3},{3,1},{1,0},{8,10},{10,12},{12... | collective-permute-start | bytes 1622024 | tf_op jit(solution)/shard_map/ppermute | solution.py:42
  22.6 0.8 copy-start.15
  23.4 13.8 %collective-permute-start.7 = (bf16[64,4224]{1,0:T(8,128)(2,1)}, bf16[64,4224]{1,0:T(8,128)(2,1)}, u32[]{:S(2)}, u32[]{:S(2)}) collective-permute-start(bf16[64,4224]{1,0:T(8,128)(2,1)} %collective-permute-done.1.refs_2_), channel_id=1, source_target_pairs={{0,1},{2,0},{4,2},{6,4},{7,6},{5,7},{3,5},{1,3},{8,9},{10,8},{12,1... | collective-permute-start | bytes 1622024 | tf_op jit(solution)/shard_map/ppermute | solution.py:42
  34.6 16.2 %collective-permute-start.12 = (bf16[64,4224]{1,0:T(8,128)(2,1)}, bf16[64,4224]{1,0:T(8,128)(2,1)}, u32[]{:S(2)}, u32[]{:S(2)}) collective-permute-start(bf16[64,4224]{1,0:T(8,128)(2,1)} %collective-permute-done.2.refs_3_), channel_id=1, source_target_pairs={{0,2},{2,4},{4,6},{6,7},{7,5},{5,3},{3,1},{1,0},{8,10},{10,12},{12... | collective-permute-start | bytes 1622024 | tf_op jit(solution)/shard_map/ppermute | solution.py:42
  37.2 15.7 %collective-permute-start.8 = (bf16[64,4224]{1,0:T(8,128)(2,1)}, bf16[64,4224]{1,0:T(8,128)(2,1)S(1)}, u32[]{:S(2)}, u32[]{:S(2)}) collective-permute-start(bf16[64,4224]{1,0:T(8,128)(2,1)} %collective-permute-done.7.refs_0_.refs_4_), channel_id=1, source_target_pairs={{0,1},{2,0},{4,2},{6,4},{7,6},{5,7},{3,5},{1,3},{8,9},{10,8},{12,1... | collective-permute-start | bytes 1622024 | tf_op jit(solution)/shard_map/ppermute | solution.py:42
  37.2 1.4 %copy-start.1 = (bf16[384,2048]{1,0:T(8,128)(2,1)S(1)}, bf16[384,2048]{1,0:T(8,128)(2,1)}, u32[]{:S(2)}) copy-start(bf16[384,2048]{1,0:T(8,128)(2,1)} %copy-done) | copy-start | bytes 4718596
  38.7 1.4 %copy-start.4 = (bf16[384,2048]{1,0:T(8,128)(2,1)S(1)}, bf16[384,2048]{1,0:T(8,128)(2,1)}, u32[]{:S(2)}) copy-start(bf16[384,2048]{1,0:T(8,128)(2,1)} %copy-done.3) | copy-start | bytes 4718596
  40.1 1.0 copy-start.6
  41.1 1.0 copy-start.16
  42.2 10.7 %copy-start.2 = (bf16[384,2048]{1,0:T(8,128)(2,1)S(1)}, bf16[384,2048]{1,0:T(8,128)(2,1)}, u32[]{:S(2)}) copy-start(bf16[384,2048]{1,0:T(8,128)(2,1)} %copy-done) | copy-start | bytes 4718596
  50.8 10.5 %collective-permute-start.13 = (bf16[64,4224]{1,0:T(8,128)(2,1)}, bf16[64,4224]{1,0:T(8,128)(2,1)S(1)}, u32[]{:S(2)}, u32[]{:S(2)}) collective-permute-start(bf16[64,4224]{1,0:T(8,128)(2,1)} %collective-permute-done.12.refs_0_.refs_6_), channel_id=1, source_target_pairs={{0,2},{2,4},{4,6},{6,7},{7,5},{5,3},{3,1},{1,0},{8,10},{10,12},{12... | collective-permute-start | bytes 1622024 | tf_op jit(solution)/shard_map/ppermute | solution.py:42
  59.7 11.2 %collective-permute-start.9 = (bf16[64,4096]{1,0:T(8,128)(2,1)S(1)}, bf16[64,4096]{1,0:T(8,128)(2,1)S(1)}, u32[]{:S(2)}, u32[]{:S(2)}) collective-permute-start(bf16[64,4096]{1,0:T(8,128)(2,1)S(1)} %get-tuple-element.66), channel_id=1, source_target_pairs={{0,2},{2,4},{4,6},{6,7},{7,5},{5,3},{3,1},{1,0},{8,10},{10,12},{12... | collective-permute-start | bytes 1572872 | tf_op jit(solution)/shard_map/ppermute | solution.py:42
  68.2 9.2 %collective-permute-start.14 = (bf16[64,4096]{1,0:T(8,128)(2,1)S(1)}, bf16[64,4096]{1,0:T(8,128)(2,1)S(1)}, u32[]{:S(2)}, u32[]{:S(2)}) collective-permute-start(bf16[64,4096]{1,0:T(8,128)(2,1)S(1)} %get-tuple-element.77), channel_id=1, source_target_pairs={{0,1},{2,0},{4,2},{6,4},{7,6},{5,7},{3,5},{1,3},{8,9},{10,8},{12,1... | collective-permute-start | bytes 1572872 | tf_op jit(solution)/shard_map/ppermute | solution.py:42
  68.8 18.4 %collective-permute-start.16 = (bf16[64,2048]{1,0:T(8,128)(2,1)S(1)}, bf16[64,2048]{1,0:T(8,128)(2,1)S(1)}, u32[]{:S(2)}, u32[]{:S(2)}) collective-permute-start(bf16[64,2048]{1,0:T(8,128)(2,1)S(1)} %get-tuple-element.111), channel_id=1, source_target_pairs={{0,8},{8,0},{1,9},{9,1},{2,10},{10,2},{3,11},{11,3},{4,12},{12,4},... | collective-permute-start | bytes 786440 | tf_op jit(solution)/shard_map/ppermute | solution.py:47
  70.4 16.9 %collective-permute-start.6 = (bf16[64,2048]{1,0:T(8,128)(2,1)S(1)}, bf16[64,2048]{1,0:T(8,128)(2,1)S(1)}, u32[]{:S(2)}, u32[]{:S(2)}) collective-permute-start(bf16[64,2048]{1,0:T(8,128)(2,1)S(1)} %get-tuple-element.112), channel_id=1, source_target_pairs={{0,8},{8,0},{1,9},{9,1},{2,10},{10,2},{3,11},{11,3},{4,12},{12,4},... | collective-permute-start | bytes 786440 | tf_op jit(solution)/shard_map/ppermute | solution.py:47
  77.4 2.4 %copy-start.17 = (bf16[64,4224]{1,0:T(8,128)(2,1)S(1)}, bf16[64,4224]{1,0:T(8,128)(2,1)}, u32[]{:S(2)}) copy-start(bf16[64,4224]{1,0:T(8,128)(2,1)} %copy-done.15) | copy-start | bytes 1622020
  77.5 12.9 %collective-permute-start.15 = (bf16[64,4096]{1,0:T(8,128)(2,1)S(1)}, bf16[64,4096]{1,0:T(8,128)(2,1)S(1)}, u32[]{:S(2)}, u32[]{:S(2)}) collective-permute-start(bf16[64,4096]{1,0:T(8,128)(2,1)S(1)} %add_convert_fusion.4), channel_id=1, source_target_pairs={{0,1},{2,0},{4,2},{6,4},{7,6},{5,7},{3,5},{1,3},{8,9},{10,8},{12,1... | collective-permute-start | bytes 1572872 | tf_op jit(solution)/shard_map/ppermute | solution.py:42
  78.2 12.9 %collective-permute-start.10 = (bf16[64,4096]{1,0:T(8,128)(2,1)S(1)}, bf16[64,4096]{1,0:T(8,128)(2,1)S(1)}, u32[]{:S(2)}, u32[]{:S(2)}) collective-permute-start(bf16[64,4096]{1,0:T(8,128)(2,1)S(1)} %add_convert_fusion.5), channel_id=1, source_target_pairs={{0,2},{2,4},{4,6},{6,7},{7,5},{5,3},{3,1},{1,0},{8,10},{10,12},{12... | collective-permute-start | bytes 1572872 | tf_op jit(solution)/shard_map/ppermute | solution.py:42
  90.6 13.2 %collective-permute-start.17 = (bf16[64,4096]{1,0:T(8,128)(2,1)S(1)}, bf16[64,4096]{1,0:T(8,128)(2,1)S(1)}, u32[]{:S(2)}, u32[]{:S(2)}) collective-permute-start(bf16[64,4096]{1,0:T(8,128)(2,1)S(1)} %add_convert_fusion.3), channel_id=1, source_target_pairs={{0,1},{2,0},{4,2},{6,4},{7,6},{5,7},{3,5},{1,3},{8,9},{10,8},{12,1... | collective-permute-start | bytes 1572872 | tf_op jit(solution)/shard_map/ppermute | solution.py:42
  91.2 9.3 %collective-permute-start.18 = (bf16[64,2048]{1,0:T(8,128)(2,1)S(1)}, bf16[64,2048]{1,0:T(8,128)(2,1)S(1)}, u32[]{:S(2)}, u32[]{:S(2)}) collective-permute-start(bf16[64,2048]{1,0:T(8,128)(2,1)S(1)} %get-tuple-element.115), channel_id=1, source_target_pairs={{0,10},{2,12},{4,14},{6,15},{7,13},{5,11},{3,9},{1,8},{8,2},{10,4}... | collective-permute-start | bytes 786440 | tf_op jit(solution)/shard_map/ppermute | solution.py:42
  93.8 9.9 %collective-permute-start.11 = (bf16[64,2048]{1,0:T(8,128)(2,1)S(1)}, bf16[64,2048]{1,0:T(8,128)(2,1)S(1)}, u32[]{:S(2)}, u32[]{:S(2)}) collective-permute-start(bf16[64,2048]{1,0:T(8,128)(2,1)S(1)} %get-tuple-element.116), channel_id=1, source_target_pairs={{0,10},{2,12},{4,14},{6,15},{7,13},{5,11},{3,9},{1,8},{8,2},{10,4}... | collective-permute-start | bytes 786440 | tf_op jit(solution)/shard_map/ppermute | solution.py:42
  103.8 16.2 %collective-permute-start.21 = (bf16[384,2048]{1,0:T(8,128)(2,1)S(1)}, bf16[384,2048]{1,0:T(8,128)(2,1)S(1)}, u32[]{:S(2)}, u32[]{:S(2)}) collective-permute-start(bf16[384,2048]{1,0:T(8,128)(2,1)S(1)} %get-tuple-element.106), channel_id=1, source_target_pairs={{0,16},{16,0},{1,17},{17,1},{2,18},{18,2},{3,19},{19,3},{4,20},{20... | collective-permute-start | bytes 4718600 | tf_op jit(solution)/shard_map/ppermute | solution.py:47
  103.9 10.1 %collective-permute-start.19 = (bf16[64,2048]{1,0:T(8,128)(2,1)S(1)}, bf16[64,2048]{1,0:T(8,128)(2,1)S(1)}, u32[]{:S(2)}, u32[]{:S(2)}) collective-permute-start(bf16[64,2048]{1,0:T(8,128)(2,1)S(1)} %get-tuple-element.114), channel_id=1, source_target_pairs={{0,9},{2,8},{4,10},{6,12},{7,14},{5,15},{3,13},{1,11},{8,1},{10,0}... | collective-permute-start | bytes 786440 | tf_op jit(solution)/shard_map/ppermute | solution.py:42
  106.0 15.8 %collective-permute-start.22 = (bf16[384,2048]{1,0:T(8,128)(2,1)S(1)}, bf16[384,2048]{1,0:T(8,128)(2,1)S(1)}, u32[]{:S(2)}, u32[]{:S(2)}) collective-permute-start(bf16[384,2048]{1,0:T(8,128)(2,1)S(1)} %get-tuple-element.108), channel_id=1, source_target_pairs={{0,16},{16,0},{1,17},{17,1},{2,18},{18,2},{3,19},{19,3},{4,20},{20... | collective-permute-start | bytes 4718600 | tf_op jit(solution)/shard_map/ppermute | solution.py:47
  107.0 12.2 %collective-permute-start.20 = (bf16[64,2048]{1,0:T(8,128)(2,1)S(1)}, bf16[64,2048]{1,0:T(8,128)(2,1)S(1)}, u32[]{:S(2)}, u32[]{:S(2)}) collective-permute-start(bf16[64,2048]{1,0:T(8,128)(2,1)S(1)} %get-tuple-element.113), channel_id=1, source_target_pairs={{0,9},{2,8},{4,10},{6,12},{7,14},{5,15},{3,13},{1,11},{8,1},{10,0}... | collective-permute-start | bytes 786440 | tf_op jit(solution)/shard_map/ppermute | solution.py:42
  107.1 16.4 %collective-permute-start.23 = (bf16[384,2048]{1,0:T(8,128)(2,1)S(1)}, bf16[384,2048]{1,0:T(8,128)(2,1)S(1)}, u32[]{:S(2)}, u32[]{:S(2)}) collective-permute-start(bf16[384,2048]{1,0:T(8,128)(2,1)S(1)} %get-tuple-element.110), channel_id=1, source_target_pairs={{0,16},{16,0},{1,17},{17,1},{2,18},{18,2},{3,19},{19,3},{4,20},{20... | collective-permute-start | bytes 4718600 | tf_op jit(solution)/shard_map/ppermute | solution.py:47

commit v7 on v6

--- a/solution.py
+++ b/solution.py
@@ -128,7 +128,7 @@
     )(*weights)
 
 
-def expert_kernel(count, experts, local_experts, first_ref, *refs):
+def expert_kernel(count, experts, local_experts, *refs):
     blocks = refs[:count]
     weights = refs[count : count + 6]
     outs = refs[count + 6 : 2 * count + 6]
@@ -143,8 +143,9 @@
         tables.append(block[:, 2 * width :].astype(F32))
     table = jnp.concatenate(tables, axis=0).T
     expert_of = lax.rem(lax.broadcasted_iota(jnp.int32, table.shape, 0), experts)
+    first = lax.axis_index("exp") * local_experts
     scales = [
-        jnp.sum(jnp.where(expert_of == first_ref[0] + e, table, 0.0), axis=0, keepdims=True)
+        jnp.sum(jnp.where(expert_of == first + e, table, 0.0), axis=0, keepdims=True)
         for e in range(local_experts)
     ]
     unit = lax.broadcasted_iota(jnp.int32, (half, 1), 0)
@@ -183,7 +184,7 @@
     columns_of(width, column)
 
 
-def expert_call(blocks, weights, first, experts, local_experts):
+def expert_call(blocks, weights, experts, local_experts):
     count, tokens = len(blocks), blocks[0].shape[0]
     half, width = weights[0].shape
     units, rows = 2 * half, count * tokens
@@ -191,7 +192,7 @@
         functools.partial(expert_kernel, count, experts, local_experts),
         out_shape=[jax.ShapeDtypeStruct((tokens, 2 * width), BF16)] * count
         + [jax.ShapeDtypeStruct((units, rows), BF16)] * 3,
-        in_specs=[pl.BlockSpec(memory_space=pltpu.SMEM)] + [whole()] * (count + 6),
+        in_specs=[whole()] * (count + 6),
         out_specs=[whole()] * (count + 3),
         scratch_shapes=[
             pltpu.VMEM((2, rows, width), BF16),
@@ -204,7 +205,7 @@
             transcendentals=rows * units,
         ),
         name="expert_rows",
-    )(first, *blocks, *weights)
+    )(*blocks, *weights)
     return results[:count], results[count:]
 
 
@@ -270,19 +271,19 @@
     lanes = -(-3 * experts // 128) * 128
     shards_of = [w.reshape(half, width) for w in (gate_weight, up_weight, down_weight)]
     other = [from_behind(w, "rep", 1) for w in shards_of]
-    own = load_call(shards_of[:1]) + load_call(shards_of[1:])
-    weights = list(own) + other
-    first = (lax.axis_index("exp") * local_experts).astype(jnp.int32).reshape(1)
     home = pl.pallas_call(
         functools.partial(pack_kernel, experts),
         out_shape=jax.ShapeDtypeStruct((tokens, 2 * width + lanes), BF16),
         in_specs=[whole()] * 5,
         out_specs=whole(),
-        compiler_params=pltpu.CompilerParams(vmem_limit_bytes=8 * 2**20),
+        compiler_params=pltpu.CompilerParams(vmem_limit_bytes=60 * 2**20),
         name="pack_rows",
     )(row_codes[0], block_exponents[0].T, routes[0].T, route_weight[0].T, out_grad[0])
 
     tie = lax.optimization_barrier
+    shards_of = tie((home, shards_of))[1]
+    own = load_call(shards_of[:1]) + load_call(shards_of[1:])
+    weights = list(own) + other
     ahead, behind = peers // 2, peers // 2 - 1
     names = [("near", 0)]
     for k in range(1, ahead + 1):
@@ -296,7 +297,7 @@
 
     def work(group):
         outs, saved = expert_call(
-            [held[name] for name in group], weights, first, experts, local_experts
+            [held[name] for name in group], weights, experts, local_experts
         )
         partial.update(zip(group, outs))
         kept.append(saved)
@@ -317,7 +318,7 @@
     work(groups[-1])
     both = (slice(0, width), slice(width, 2 * width))
     near_sum = partial["near", ahead]
-    own_total = other_total = None
+    own_total = received = None
     blocks = [held[name] for group in groups for name in group]
     steps = (1, -1)
     finals = []
@@ -336,23 +337,22 @@
             here = [final[0] for final in finals]
             near_sum, own_total, other_total, _ = tie((near_sum, own_total, other_total, here))
             near_sum = add(near_sum, partial["near", 2])
-            for final, part, step in zip(finals, both, steps):
-                last = add(far_sum[:, part], partial["far", 1][:, part])
+            lasts = [add(far_sum[:, part], partial["far", 1][:, part]) for part in both]
+            near_sum, lasts = tie((near_sum, lasts))
+            for final, last, step in zip(finals, lasts, steps):
                 final.append(ring_shift(last, 1, step))
         elif k == 2:
             here = [final[1] for final in finals]
             near_sum, other_total, _ = tie((near_sum, other_total, here))
-        else:
+            received = [from_behind(g, "rep", 1) for g in other_total]
+        elif k > 2:
             near_sum = add(near_sum, partial["near", k - 1])
-    for final, part, step in zip(finals, both, steps):
-        final.append(ring_shift(add(near_sum[:, part], partial["near", 1][:, part]), -1, step))
-    received = [from_behind(g, "rep", 1) for g in other_total]
+    lasts = [add(near_sum[:, part], partial["near", 1][:, part]) for part in both]
+    for final, last, step in zip(finals, lasts, steps):
+        final.append(ring_shift(last, -1, step))
     totals = [add(a, b) for a, b in zip(own_total, received)]
-    results = []
-    for final in finals:
-        if results:
-            final, _ = tie((final, results[0]))
-        results.append(sum(f.astype(F32) for f in final).astype(BF16)[None])
+    finals, totals = tie((finals, totals))
+    results = [sum(f.astype(F32) for f in final).astype(BF16)[None] for final in finals]
     shape = (1, local_experts, half_units, width)
     return tuple(results) + tuple(t.reshape(shape) for t in totals)
 

time: 126 us -> 117 us (0.929)
  local copies, waits for them, and re-layouts: 15 us -> 4.03 us
  waiting for transfers between devices: 45.6 us -> 49.7 us
  Pallas kernels: 30.4 us -> 28.6 us
    unnamed x36 -> x8, local copies, waits for them, and re-layouts: 15 us -> 4.03 us
    ppermute x16, waiting for transfers between devices: 45.6 us -> 49.7 us  [ring_shift(): return lax.ppermute(value, ('rep', 'section', 'exp'), pairs)]
    pallas_call x3, Pallas kernels: 22.3 us -> 20.2 us  [expert_call(): pl.pallas_call(functools.partial(expert_kernel, count, experts, local_exp...]
    pallas_call x1, Pallas kernels: 0.33 us -> 2.21 us  [shards(): pl.pallas_call(functools.partial(pack_kernel, experts), out_shape=jax.Sha...]
    ppermute x16, starting transfers between devices: 21.1 us -> 23 us  [ring_shift(): return lax.ppermute(value, ('rep', 'section', 'exp'), pairs)]
    pallas_call x1, Pallas kernels: 7.43 us -> 5.87 us  [weight_call(): pl.pallas_call(functools.partial(weight_kernel, len(kept), count), out_sh...]
  transfers between devices with their start and end apart: 24 -> 24, of which waited for: 8 -> 9; matrix products, arithmetic and copies ran while one was open for 5% -> 5% of each run, Pallas kernels for 24% -> 24%
where the time goes in v7:
time: 117 us
  waiting for transfers between devices  49.7 us (42%)
  Pallas kernels  28.6 us (24%)
  starting transfers between devices  26.6 us (23%)
  other arithmetic  7.15 us (6%)
  local copies, waits for them, and re-layouts  4.03 us (3%)
    ppermute x16, waiting for transfers between devices, ring_shift(): return lax.ppermute(value, ('rep', 'section', 'exp'), pairs)  49.7 us
    ppermute x16, starting transfers between devices, ring_shift(): return lax.ppermute(value, ('rep', 'section', 'exp'), pairs)  23 us
    pallas_call x3, Pallas kernels, expert_call(): pl.pallas_call(functools.partial(expert_kernel, count, experts, local_exp...  20.2 us
    convert_element_type x9, other arithmetic, add(): return (a.astype(F32) + b.astype(F32)).astype(BF16)  6.12 us
    pallas_call x1, Pallas kernels, weight_call(): pl.pallas_call(functools.partial(weight_kernel, len(kept), count), out_sh...  5.87 us
    unnamed x8, local copies, waits for them, and re-layouts  4.03 us
    ppermute x8, starting transfers between devices, from_behind(): lax.ppermute(value, axis, [(i, (i + by) % peers) for i in range(peers)])  3.63 us
  transfers between devices with their start and end apart: 24, of which 9 were waited for; matrix products, arithmetic and copies ran while one was open for 5% of the time, Pallas kernels for 24%

profile of v7, /device:TPU:0, one launch (start us, length us, event | category | flops | bytes accessed | tf_op | source)
XLA Modules:
  0.0 116.9 jit_solution(14403092563826761551)
XLA Ops:
  0.6 0.5 collective-permute-start.3
  1.2 0.1 collective-permute-start.4
  1.2 0.4 collective-permute-start.5
  1.7 2.2 %pack_rows.1.refs_0_ = bf16[64,4224]{1,0:T(8,128)(2,1)} custom-call(bf16[64,2048]{1,0:T(8,128)(2,1)} %bitcast.30, s32[16,64]{1,0:T(8,128)} %bitcast.32, s32[8,64]{1,0:T(8,128)} %bitcast.33, f32[8,64]{1,0:T(8,128)} %bitcast.34, bf16[64,2048]{1,0:T(8,128)(2,1)} %bitcast.31), custom_call_target="tpu_custom_call" | custom-call | tf_op jit(solution)/shard_map/pack_rows/pallas_call | solution.py:274
  3.9 2.7 %collective-permute-start = (bf16[64,4224]{1,0:T(8,128)(2,1)}, bf16[64,4224]{1,0:T(8,128)(2,1)S(1)}, u32[]{:S(2)}, u32[]{:S(2)}) collective-permute-start(bf16[64,4224]{1,0:T(8,128)(2,1)} %pack_rows.1.refs_0_), channel_id=1, source_target_pairs={{0,2},{2,4},{4,6},{6,7},{7,5},{5,3},{3,1},{1,0},{8,10},{10,12},{12... | collective-permute-start | bytes 1622024 | tf_op jit(solution)/shard_map/ppermute | solution.py:42
  6.5 1.4 %copy-done.1 = bf16[1,2,192,2048]{3,2,1,0:T(8,128)(2,1)S(1)} copy-done((bf16[1,2,192,2048]{3,2,1,0:T(8,128)(2,1)S(1)}, bf16[1,2,192,2048]{3,2,1,0:T(8,128)(2,1)}, u32[]{:S(2)}) %copy-start.1) | copy-done | bytes 1572888
  7.9 0.1 load_weights.2.refs_4_.refs_2_
  8.1 0.1 collective-permute-start.1
  8.1 1.2 %copy-done.2 = bf16[1,2,192,2048]{3,2,1,0:T(8,128)(2,1)S(1)} copy-done((bf16[1,2,192,2048]{3,2,1,0:T(8,128)(2,1)S(1)}, bf16[1,2,192,2048]{3,2,1,0:T(8,128)(2,1)}, u32[]{:S(2)}) %copy-start.2) | copy-done | bytes 1572888
  9.3 1.4 %copy-done.3 = bf16[1,2,192,2048]{3,2,1,0:T(8,128)(2,1)S(1)} copy-done((bf16[1,2,192,2048]{3,2,1,0:T(8,128)(2,1)S(1)}, bf16[1,2,192,2048]{3,2,1,0:T(8,128)(2,1)}, u32[]{:S(2)}) %copy-start.3) | copy-done | bytes 1572888
  10.8 0.2 load_weights.3
  11.0 7.6 %collective-permute-done.refs_1_ = bf16[64,4224]{1,0:T(8,128)(2,1)S(1)} collective-permute-done((bf16[64,4224]{1,0:T(8,128)(2,1)}, bf16[64,4224]{1,0:T(8,128)(2,1)S(1)}, u32[]{:S(2)}, u32[]{:S(2)}) %collective-permute-start) | collective-permute-done | bytes 540704 | tf_op jit(solution)/shard_map/ppermute | solution.py:42
  18.6 2.4 %collective-permute-start.2 = (bf16[64,4224]{1,0:T(8,128)(2,1)S(1)}, bf16[64,4224]{1,0:T(8,128)(2,1)S(1)}, u32[]{:S(2)}, u32[]{:S(2)}) collective-permute-start(bf16[64,4224]{1,0:T(8,128)(2,1)S(1)} %collective-permute-done.refs_1_), channel_id=1, source_target_pairs={{0,2},{2,4},{4,6},{6,7},{7,5},{5,3},{3,1},{1,0},{8,10},{10,12},{12... | collective-permute-start | bytes 1622024 | tf_op jit(solution)/shard_map/ppermute | solution.py:42
  21.0 0.0 collective-permute-done.1.refs_2_
  21.0 0.3 collective-permute-start.9
  21.3 12.4 %collective-permute-done.2.refs_3_ = bf16[64,4224]{1,0:T(8,128)(2,1)S(1)} collective-permute-done((bf16[64,4224]{1,0:T(8,128)(2,1)S(1)}, bf16[64,4224]{1,0:T(8,128)(2,1)S(1)}, u32[]{:S(2)}, u32[]{:S(2)}) %collective-permute-start.2) | collective-permute-done | bytes 540704 | tf_op jit(solution)/shard_map/ppermute | solution.py:42
  33.6 2.5 %collective-permute-start.7 = (bf16[64,4224]{1,0:T(8,128)(2,1)S(1)}, bf16[64,4224]{1,0:T(8,128)(2,1)S(1)}, u32[]{:S(2)}, u32[]{:S(2)}) collective-permute-start(bf16[64,4224]{1,0:T(8,128)(2,1)S(1)} %collective-permute-done.2.refs_3_), channel_id=1, source_target_pairs={{0,2},{2,4},{4,6},{6,7},{7,5},{5,3},{3,1},{1,0},{8,10},{10,12},{12... | collective-permute-start | bytes 1622024 | tf_op jit(solution)/shard_map/ppermute | solution.py:42
  36.1 0.0 collective-permute-done.9.refs_0_.refs_4_
  36.1 0.0 collective-permute-start.10
  36.1 0.0 collective-permute-done.3.refs_7_.refs_5_
  36.1 0.0 collective-permute-done.4.refs_8_.refs_6_
  36.1 0.0 collective-permute-done.5.refs_9_.refs_7_
  36.1 7.7 %expert_rows.3 = (bf16[64,4096]{1,0:T(8,128)(2,1)S(1)}, bf16[64,4096]{1,0:T(8,128)(2,1)S(1)}, bf16[64,4096]{1,0:T(8,128)(2,1)S(1)}, bf16[64,4096]{1,0:T(8,128)(2...) custom-call(bf16[64,4224]{1,0:T(8,128)(2,1)S(1)} %copy-done, ...), custom_call_target="tpu_custom_call" | custom-call | flops 4831838208 | bytes 13631488 | tf_op jit(solution)/shard_map/expert_rows/pallas_call | solution.py:191
  43.9 4.1 %collective-permute-done.7.refs_0_.refs_6_ = bf16[64,4224]{1,0:T(8,128)(2,1)S(1)} collective-permute-done((bf16[64,4224]{1,0:T(8,128)(2,1)S(1)}, bf16[64,4224]{1,0:T(8,128)(2,1)S(1)}, u32[]{:S(2)}, u32[]{:S(2)}) %collective-permute-start.7) | collective-permute-done | bytes 540704 | tf_op jit(solution)/shard_map/ppermute | solution.py:42
  48.0 2.4 %collective-permute-start.8 = (bf16[64,4224]{1,0:T(8,128)(2,1)S(1)}, bf16[64,4224]{1,0:T(8,128)(2,1)S(1)}, u32[]{:S(2)}, u32[]{:S(2)}) collective-permute-start(bf16[64,4224]{1,0:T(8,128)(2,1)S(1)} %collective-permute-done.7.refs_0_.refs_6_), channel_id=1, source_target_pairs={{0,2},{2,4},{4,6},{6,7},{7,5},{5,3},{3,1},{1,0},{8,10},{10,12},{12... | collective-permute-start | bytes 1622024 | tf_op jit(solution)/shard_map/ppermute | solution.py:42
  50.4 0.0 collective-permute-done.10.refs_1_.refs_5_
  50.4 6.2 %expert_rows.4 = (bf16[64,4096]{1,0:T(8,128)(2,1)S(1)}, bf16[64,4096]{1,0:T(8,128)(2,1)S(1)}, bf16[768,128]{1,0:T(8,128)(2,1)S(1)}, bf16[768,128]{1,0:T(8,128)(2,1)S(1)}, bf16[768,128]{1,0:T(8,128)(2,1)S(1)}) custom-call(bf16[64,4224]{1,0:T(8,128)(2,1)S(1)} %collective-permute-done.9.refs_0_.refs_4_, ...), custom_call_target="tpu_custom_call" | custom-call | flops 2415919104 | bytes 11534336 | tf_op jit(solution)/shard_map/expert_rows/pallas_call | solution.py:191
  56.6 1.4 %collective-permute-start.12 = (bf16[64,4096]{1,0:T(8,128)(2,1)S(1)}, bf16[64,4096]{1,0:T(8,128)(2,1)S(1)}, u32[]{:S(2)}, u32[]{:S(2)}) collective-permute-start(bf16[64,4096]{1,0:T(8,128)(2,1)S(1)} %get-tuple-element.90), channel_id=1, source_target_pairs={{0,2},{2,4},{4,6},{6,7},{7,5},{5,3},{3,1},{1,0},{8,10},{10,12},{12... | collective-permute-start | bytes 1572872 | tf_op jit(solution)/shard_map/ppermute | solution.py:42
  58.0 0.1 add_convert_fusion.12
  58.1 1.6 %collective-permute-start.14 = (bf16[64,2048]{1,0:T(8,128)(2,1)S(1)}, bf16[64,2048]{1,0:T(8,128)(2,1)S(1)}, u32[]{:S(2)}, u32[]{:S(2)}) collective-permute-start(bf16[64,2048]{1,0:T(8,128)(2,1)S(1)} %get-tuple-element.135), channel_id=1, source_target_pairs={{0,8},{8,0},{1,9},{9,1},{2,10},{10,2},{3,11},{11,3},{4,12},{12,4},... | collective-permute-start | bytes 786440 | tf_op jit(solution)/shard_map/ppermute | solution.py:47
  59.7 0.5 collective-permute-start.6
  60.2 0.0 collective-permute-done.8.refs_1_.refs_7_
  60.2 6.2 %expert_rows.5 = (bf16[64,4096]{1,0:T(8,128)(2,1)S(1)}, bf16[64,4096]{1,0:T(8,128)(2,1)S(1)}, bf16[768,128]{1,0:T(8,128)(2,1)S(1)}, bf16[768,128]{1,0:T(8,128)(2,1)S(1)}, bf16[768,128]{1,0:T(8,128)(2,1)S(1)}) custom-call(bf16[64,4224]{1,0:T(8,128)(2,1)S(1)} %collective-permute-done.7.refs_0_.refs_6_, ...), custom_call_target="tpu_custom_call" | custom-call | flops 2415919104 | bytes 11534336 | tf_op jit(solution)/shard_map/expert_rows/pallas_call | solution.py:191
  66.4 0.8 collective-permute-start.11
  67.2 0.0 collective-permute-done.12
  67.2 0.1 add_convert_fusion.3
  67.3 1.4 %collective-permute-start.15 = (bf16[64,4096]{1,0:T(8,128)(2,1)S(1)}, bf16[64,4096]{1,0:T(8,128)(2,1)S(1)}, u32[]{:S(2)}, u32[]{:S(2)}) collective-permute-start(bf16[64,4096]{1,0:T(8,128)(2,1)S(1)} %add_convert_fusion.3), channel_id=1, source_target_pairs={{0,2},{2,4},{4,6},{6,7},{7,5},{5,3},{3,1},{1,0},{8,10},{10,12},{12... | collective-permute-start | bytes 1572872 | tf_op jit(solution)/shard_map/ppermute | solution.py:42
  68.7 8.9 %collective-permute-done.11 = bf16[64,4096]{1,0:T(8,128)(2,1)S(1)} collective-permute-done((bf16[64,4096]{1,0:T(8,128)(2,1)S(1)}, bf16[64,4096]{1,0:T(8,128)(2,1)S(1)}, u32[]{:S(2)}, u32[]{:S(2)}) %collective-permute-start.11) | collective-permute-done | bytes 524320 | tf_op jit(solution)/shard_map/ppermute | solution.py:42
  77.6 0.1 add_convert_fusion.5
  77.8 0.9 collective-permute-start.13
  78.6 5.9 %weight_grads.1 = (bf16[384,2048]{1,0:T(8,128)(2,1)S(1)}, bf16[384,2048]{1,0:T(8,128)(2,1)S(1)}, bf16[384,2048]{1,0:T(8,128)(2,1)S(1)}, bf16[384,2048]{1,0:T(8,1...) custom-call(bf16[64,4224]{1,0:T(8,128)(2,1)S(1)} %copy-done, ...), custom_call_target="tpu_custom_call" | custom-call | flops 4831838208 | bytes 13631488 | tf_op jit(solution)/shard_map/weight_grads/pallas_call | solution.py:242
  84.5 0.0 collective-permute-done.15
  84.5 0.1 add_convert_fusion.10
  84.7 0.0 collective-permute-done.14
  84.7 0.0 collective-permute-done.6
  84.7 2.3 %collective-permute-done.13 = bf16[64,4096]{1,0:T(8,128)(2,1)S(1)} collective-permute-done((bf16[64,4096]{1,0:T(8,128)(2,1)S(1)}, bf16[64,4096]{1,0:T(8,128)(2,1)S(1)}, u32[]{:S(2)}, u32[]{:S(2)}) %collective-permute-start.13) | collective-permute-done | bytes 524320 | tf_op jit(solution)/shard_map/ppermute | solution.py:42
  87.0 0.1 add_convert_fusion.4
  87.1 0.9 collective-permute-start.17
  88.0 2.0 %collective-permute-start.16 = (bf16[64,2048]{1,0:T(8,128)(2,1)S(1)}, bf16[64,2048]{1,0:T(8,128)(2,1)S(1)}, u32[]{:S(2)}, u32[]{:S(2)}) collective-permute-start(bf16[64,2048]{1,0:T(8,128)(2,1)S(1)} %get-tuple-element.112), channel_id=1, source_target_pairs={{0,10},{2,12},{4,14},{6,15},{7,13},{5,11},{3,9},{1,8},{8,2},{10,4}... | collective-permute-start | bytes 786440 | tf_op jit(solution)/shard_map/ppermute | solution.py:42
  90.0 1.8 %collective-permute-start.18 = (bf16[64,2048]{1,0:T(8,128)(2,1)S(1)}, bf16[64,2048]{1,0:T(8,128)(2,1)S(1)}, u32[]{:S(2)}, u32[]{:S(2)}) collective-permute-start(bf16[64,2048]{1,0:T(8,128)(2,1)S(1)} %get-tuple-element.117), channel_id=1, source_target_pairs={{0,10},{2,12},{4,14},{6,15},{7,13},{5,11},{3,9},{1,8},{8,2},{10,4}... | collective-permute-start | bytes 786440 | tf_op jit(solution)/shard_map/ppermute | solution.py:42
  91.8 5.3 %collective-permute-done.16 = bf16[64,2048]{1,0:T(8,128)(2,1)S(1)} collective-permute-done((bf16[64,2048]{1,0:T(8,128)(2,1)S(1)}, bf16[64,2048]{1,0:T(8,128)(2,1)S(1)}, u32[]{:S(2)}, u32[]{:S(2)}) %collective-permute-start.16) | collective-permute-done | bytes 262176 | tf_op jit(solution)/shard_map/ppermute | solution.py:42
  97.1 2.8 %collective-permute-done.18 = bf16[64,2048]{1,0:T(8,128)(2,1)S(1)} collective-permute-done((bf16[64,2048]{1,0:T(8,128)(2,1)S(1)}, bf16[64,2048]{1,0:T(8,128)(2,1)S(1)}, u32[]{:S(2)}, u32[]{:S(2)}) %collective-permute-start.18) | collective-permute-done | bytes 262176 | tf_op jit(solution)/shard_map/ppermute | solution.py:42
  99.9 0.5 collective-permute-start.22
  100.4 0.0 collective-permute-start.23
  100.4 0.1 add_convert_fusion.8
  100.6 2.4 %collective-permute-start.20 = (bf16[64,2048]{1,0:T(8,128)(2,1)S(1)}, bf16[64,2048]{1,0:T(8,128)(2,1)S(1)}, u32[]{:S(2)}, u32[]{:S(2)}) collective-permute-start(bf16[64,2048]{1,0:T(8,128)(2,1)S(1)} %get-tuple-element.137), channel_id=1, source_target_pairs={{0,9},{2,8},{4,10},{6,12},{7,14},{5,15},{3,13},{1,11},{8,1},{10,0}... | collective-permute-start | bytes 786440 | tf_op jit(solution)/shard_map/ppermute | solution.py:42
  103.0 1.3 %collective-permute-start.19 = (bf16[64,2048]{1,0:T(8,128)(2,1)S(1)}, bf16[64,2048]{1,0:T(8,128)(2,1)S(1)}, u32[]{:S(2)}, u32[]{:S(2)}) collective-permute-start(bf16[64,2048]{1,0:T(8,128)(2,1)S(1)} %get-tuple-element.138), channel_id=1, source_target_pairs={{0,9},{2,8},{4,10},{6,12},{7,14},{5,15},{3,13},{1,11},{8,1},{10,0}... | collective-permute-start | bytes 786440 | tf_op jit(solution)/shard_map/ppermute | solution.py:42
  104.3 1.8 %add_convert_fusion.2 = bf16[384,2048]{1,0:T(8,128)(2,1)} fusion(bf16[384,2048]{1,0:T(8,128)(2,1)S(1)} %collective-permute-done.21, bf16[384,2048]{1,0:T(8,128)(2,1)S(1)} %get-tuple-element.120), kind=kLoop, calls=%fused_computation.2 | loop fusion | flops 3145728 | bytes 4718592 | tf_op jit(solution)/shard_map/convert_element_type | solution.py:260
  106.1 1.8 %add_convert_fusion.1 = bf16[384,2048]{1,0:T(8,128)(2,1)} fusion(bf16[384,2048]{1,0:T(8,128)(2,1)S(1)} %collective-permute-done.22, bf16[384,2048]{1,0:T(8,128)(2,1)S(1)} %get-tuple-element.122), kind=kLoop, calls=%fused_computation.1 | loop fusion | flops 3145728 | bytes 4718592 | tf_op jit(solution)/shard_map/convert_element_type | solution.py:260
  107.9 0.0 collective-permute-done.23
  107.9 1.7 %add_convert_fusion = bf16[384,2048]{1,0:T(8,128)(2,1)} fusion(bf16[384,2048]{1,0:T(8,128)(2,1)S(1)} %collective-permute-done.23, bf16[384,2048]{1,0:T(8,128)(2,1)S(1)} %get-tuple-element.124), kind=kLoop, calls=%fused_computation | loop fusion | flops 3145728 | bytes 4718592 | tf_op jit(solution)/shard_map/convert_element_type | solution.py:260
  109.6 1.1 collective-permute-done.20
  110.7 5.2 %collective-permute-done.19 = bf16[64,2048]{1,0:T(8,128)(2,1)S(1)} collective-permute-done((bf16[64,2048]{1,0:T(8,128)(2,1)S(1)}, bf16[64,2048]{1,0:T(8,128)(2,1)S(1)}, u32[]{:S(2)}, u32[]{:S(2)}) %collective-permute-start.19) | collective-permute-done | bytes 262176 | tf_op jit(solution)/shard_map/ppermute | solution.py:42
  115.9 1.0 fusion
  (9 shorter events, 0.0 us)
Async XLA Ops:
  0.6 35.5 %collective-permute-start.3 = (bf16[384,2048]{1,0:T(8,128)(2,1)}, bf16[384,2048]{1,0:T(8,128)(2,1)S(1)}, u32[]{:S(2)}, u32[]{:S(2)}) collective-permute-start(bf16[384,2048]{1,0:T(8,128)(2,1)} %bitcast.21), channel_id=1, source_target_pairs={{0,16},{16,0},{1,17},{17,1},{2,18},{18,2},{3,19},{19,3},{4,20},{20... | collective-permute-start | bytes 4718600 | tf_op jit(solution)/shard_map/ppermute | solution.py:47
  1.2 35.0 %collective-permute-start.4 = (bf16[384,2048]{1,0:T(8,128)(2,1)}, bf16[384,2048]{1,0:T(8,128)(2,1)S(1)}, u32[]{:S(2)}, u32[]{:S(2)}) collective-permute-start(bf16[384,2048]{1,0:T(8,128)(2,1)} %bitcast.23), channel_id=1, source_target_pairs={{0,16},{16,0},{1,17},{17,1},{2,18},{18,2},{3,19},{19,3},{4,20},{20... | collective-permute-start | bytes 4718600 | tf_op jit(solution)/shard_map/ppermute | solution.py:47
  1.2 34.9 %collective-permute-start.5 = (bf16[384,2048]{1,0:T(8,128)(2,1)}, bf16[384,2048]{1,0:T(8,128)(2,1)}, u32[]{:S(2)}, u32[]{:S(2)}) collective-permute-start(bf16[384,2048]{1,0:T(8,128)(2,1)} %bitcast.25), channel_id=1, source_target_pairs={{0,16},{16,0},{1,17},{17,1},{2,18},{18,2},{3,19},{19,3},{4,20},{20... | collective-permute-start | bytes 4718600 | tf_op jit(solution)/shard_map/ppermute | solution.py:47
  3.9 4.2 %copy-start = (bf16[64,4224]{1,0:T(8,128)(2,1)S(1)}, bf16[64,4224]{1,0:T(8,128)(2,1)}, u32[]{:S(2)}) copy-start(bf16[64,4224]{1,0:T(8,128)(2,1)} %pack_rows.1.refs_0_) | copy-start | bytes 1622020
  3.9 14.7 %collective-permute-start = (bf16[64,4224]{1,0:T(8,128)(2,1)}, bf16[64,4224]{1,0:T(8,128)(2,1)S(1)}, u32[]{:S(2)}, u32[]{:S(2)}) collective-permute-start(bf16[64,4224]{1,0:T(8,128)(2,1)} %pack_rows.1.refs_0_), channel_id=1, source_target_pairs={{0,2},{2,4},{4,6},{6,7},{7,5},{5,3},{3,1},{1,0},{8,10},{10,12},{12... | collective-permute-start | bytes 1622024 | tf_op jit(solution)/shard_map/ppermute | solution.py:42
  6.5 1.4 %copy-start.1 = (bf16[1,2,192,2048]{3,2,1,0:T(8,128)(2,1)S(1)}, bf16[1,2,192,2048]{3,2,1,0:T(8,128)(2,1)}, u32[]{:S(2)}) copy-start(bf16[1,2,192,2048]{3,2,1,0:T(8,128)(2,1)} %param.13) | copy-start | bytes 4718596
  7.9 1.4 %copy-start.2 = (bf16[1,2,192,2048]{3,2,1,0:T(8,128)(2,1)S(1)}, bf16[1,2,192,2048]{3,2,1,0:T(8,128)(2,1)}, u32[]{:S(2)}) copy-start(bf16[1,2,192,2048]{3,2,1,0:T(8,128)(2,1)} %param.14) | copy-start | bytes 4718596
  8.1 12.9 %collective-permute-start.1 = (bf16[64,4224]{1,0:T(8,128)(2,1)S(1)}, bf16[64,4224]{1,0:T(8,128)(2,1)S(1)}, u32[]{:S(2)}, u32[]{:S(2)}) collective-permute-start(bf16[64,4224]{1,0:T(8,128)(2,1)S(1)} %copy-done), channel_id=1, source_target_pairs={{0,1},{2,0},{4,2},{6,4},{7,6},{5,7},{3,5},{1,3},{8,9},{10,8},{12,1... | collective-permute-start | bytes 1622024 | tf_op jit(solution)/shard_map/ppermute | solution.py:42
  9.3 1.4 %copy-start.3 = (bf16[1,2,192,2048]{3,2,1,0:T(8,128)(2,1)S(1)}, bf16[1,2,192,2048]{3,2,1,0:T(8,128)(2,1)}, u32[]{:S(2)}) copy-start(bf16[1,2,192,2048]{3,2,1,0:T(8,128)(2,1)} %param.15) | copy-start | bytes 4718596
  18.6 15.0 %collective-permute-start.2 = (bf16[64,4224]{1,0:T(8,128)(2,1)S(1)}, bf16[64,4224]{1,0:T(8,128)(2,1)S(1)}, u32[]{:S(2)}, u32[]{:S(2)}) collective-permute-start(bf16[64,4224]{1,0:T(8,128)(2,1)S(1)} %collective-permute-done.refs_1_), channel_id=1, source_target_pairs={{0,2},{2,4},{4,6},{6,7},{7,5},{5,3},{3,1},{1,0},{8,10},{10,12},{12... | collective-permute-start | bytes 1622024 | tf_op jit(solution)/shard_map/ppermute | solution.py:42
  21.0 15.1 %collective-permute-start.9 = (bf16[64,4224]{1,0:T(8,128)(2,1)S(1)}, bf16[64,4224]{1,0:T(8,128)(2,1)S(1)}, u32[]{:S(2)}, u32[]{:S(2)}) collective-permute-start(bf16[64,4224]{1,0:T(8,128)(2,1)S(1)} %collective-permute-done.1.refs_2_), channel_id=1, source_target_pairs={{0,1},{2,0},{4,2},{6,4},{7,6},{5,7},{3,5},{1,3},{8,9},{10,8},{12,1... | collective-permute-start | bytes 1622024 | tf_op jit(solution)/shard_map/ppermute | solution.py:42
  33.6 14.4 %collective-permute-start.7 = (bf16[64,4224]{1,0:T(8,128)(2,1)S(1)}, bf16[64,4224]{1,0:T(8,128)(2,1)S(1)}, u32[]{:S(2)}, u32[]{:S(2)}) collective-permute-start(bf16[64,4224]{1,0:T(8,128)(2,1)S(1)} %collective-permute-done.2.refs_3_), channel_id=1, source_target_pairs={{0,2},{2,4},{4,6},{6,7},{7,5},{5,3},{3,1},{1,0},{8,10},{10,12},{12... | collective-permute-start | bytes 1622024 | tf_op jit(solution)/shard_map/ppermute | solution.py:42
  36.1 14.3 %collective-permute-start.10 = (bf16[64,4224]{1,0:T(8,128)(2,1)S(1)}, bf16[64,4224]{1,0:T(8,128)(2,1)S(1)}, u32[]{:S(2)}, u32[]{:S(2)}) collective-permute-start(bf16[64,4224]{1,0:T(8,128)(2,1)S(1)} %collective-permute-done.9.refs_0_.refs_4_), channel_id=1, source_target_pairs={{0,1},{2,0},{4,2},{6,4},{7,6},{5,7},{3,5},{1,3},{8,9},{10,8},{12,1... | collective-permute-start | bytes 1622024 | tf_op jit(solution)/shard_map/ppermute | solution.py:42
  48.0 12.2 %collective-permute-start.8 = (bf16[64,4224]{1,0:T(8,128)(2,1)S(1)}, bf16[64,4224]{1,0:T(8,128)(2,1)S(1)}, u32[]{:S(2)}, u32[]{:S(2)}) collective-permute-start(bf16[64,4224]{1,0:T(8,128)(2,1)S(1)} %collective-permute-done.7.refs_0_.refs_6_), channel_id=1, source_target_pairs={{0,2},{2,4},{4,6},{6,7},{7,5},{5,3},{3,1},{1,0},{8,10},{10,12},{12... | collective-permute-start | bytes 1622024 | tf_op jit(solution)/shard_map/ppermute | solution.py:42
  56.6 10.6 %collective-permute-start.12 = (bf16[64,4096]{1,0:T(8,128)(2,1)S(1)}, bf16[64,4096]{1,0:T(8,128)(2,1)S(1)}, u32[]{:S(2)}, u32[]{:S(2)}) collective-permute-start(bf16[64,4096]{1,0:T(8,128)(2,1)S(1)} %get-tuple-element.90), channel_id=1, source_target_pairs={{0,2},{2,4},{4,6},{6,7},{7,5},{5,3},{3,1},{1,0},{8,10},{10,12},{12... | collective-permute-start | bytes 1572872 | tf_op jit(solution)/shard_map/ppermute | solution.py:42
  58.1 26.5 %collective-permute-start.14 = (bf16[64,2048]{1,0:T(8,128)(2,1)S(1)}, bf16[64,2048]{1,0:T(8,128)(2,1)S(1)}, u32[]{:S(2)}, u32[]{:S(2)}) collective-permute-start(bf16[64,2048]{1,0:T(8,128)(2,1)S(1)} %get-tuple-element.135), channel_id=1, source_target_pairs={{0,8},{8,0},{1,9},{9,1},{2,10},{10,2},{3,11},{11,3},{4,12},{12,4},... | collective-permute-start | bytes 786440 | tf_op jit(solution)/shard_map/ppermute | solution.py:47
  59.7 25.0 %collective-permute-start.6 = (bf16[64,2048]{1,0:T(8,128)(2,1)S(1)}, bf16[64,2048]{1,0:T(8,128)(2,1)S(1)}, u32[]{:S(2)}, u32[]{:S(2)}) collective-permute-start(bf16[64,2048]{1,0:T(8,128)(2,1)S(1)} %get-tuple-element.136), channel_id=1, source_target_pairs={{0,8},{8,0},{1,9},{9,1},{2,10},{10,2},{3,11},{11,3},{4,12},{12,4},... | collective-permute-start | bytes 786440 | tf_op jit(solution)/shard_map/ppermute | solution.py:47
  66.4 11.2 %collective-permute-start.11 = (bf16[64,4096]{1,0:T(8,128)(2,1)S(1)}, bf16[64,4096]{1,0:T(8,128)(2,1)S(1)}, u32[]{:S(2)}, u32[]{:S(2)}) collective-permute-start(bf16[64,4096]{1,0:T(8,128)(2,1)S(1)} %get-tuple-element.89), channel_id=1, source_target_pairs={{0,1},{2,0},{4,2},{6,4},{7,6},{5,7},{3,5},{1,3},{8,9},{10,8},{12,1... | collective-permute-start | bytes 1572872 | tf_op jit(solution)/shard_map/ppermute | solution.py:42
  67.3 17.2 %collective-permute-start.15 = (bf16[64,4096]{1,0:T(8,128)(2,1)S(1)}, bf16[64,4096]{1,0:T(8,128)(2,1)S(1)}, u32[]{:S(2)}, u32[]{:S(2)}) collective-permute-start(bf16[64,4096]{1,0:T(8,128)(2,1)S(1)} %add_convert_fusion.3), channel_id=1, source_target_pairs={{0,2},{2,4},{4,6},{6,7},{7,5},{5,3},{3,1},{1,0},{8,10},{10,12},{12... | collective-permute-start | bytes 1572872 | tf_op jit(solution)/shard_map/ppermute | solution.py:42
  77.8 9.2 %collective-permute-start.13 = (bf16[64,4096]{1,0:T(8,128)(2,1)S(1)}, bf16[64,4096]{1,0:T(8,128)(2,1)S(1)}, u32[]{:S(2)}, u32[]{:S(2)}) collective-permute-start(bf16[64,4096]{1,0:T(8,128)(2,1)S(1)} %add_convert_fusion.5), channel_id=1, source_target_pairs={{0,1},{2,0},{4,2},{6,4},{7,6},{5,7},{3,5},{1,3},{8,9},{10,8},{12,1... | collective-permute-start | bytes 1572872 | tf_op jit(solution)/shard_map/ppermute | solution.py:42
  87.1 12.8 %collective-permute-start.17 = (bf16[64,4096]{1,0:T(8,128)(2,1)S(1)}, bf16[64,4096]{1,0:T(8,128)(2,1)S(1)}, u32[]{:S(2)}, u32[]{:S(2)}) collective-permute-start(bf16[64,4096]{1,0:T(8,128)(2,1)S(1)} %add_convert_fusion.4), channel_id=1, source_target_pairs={{0,1},{2,0},{4,2},{6,4},{7,6},{5,7},{3,5},{1,3},{8,9},{10,8},{12,1... | collective-permute-start | bytes 1572872 | tf_op jit(solution)/shard_map/ppermute | solution.py:42
  88.0 9.1 %collective-permute-start.16 = (bf16[64,2048]{1,0:T(8,128)(2,1)S(1)}, bf16[64,2048]{1,0:T(8,128)(2,1)S(1)}, u32[]{:S(2)}, u32[]{:S(2)}) collective-permute-start(bf16[64,2048]{1,0:T(8,128)(2,1)S(1)} %get-tuple-element.112), channel_id=1, source_target_pairs={{0,10},{2,12},{4,14},{6,15},{7,13},{5,11},{3,9},{1,8},{8,2},{10,4}... | collective-permute-start | bytes 786440 | tf_op jit(solution)/shard_map/ppermute | solution.py:42
  90.0 9.9 %collective-permute-start.18 = (bf16[64,2048]{1,0:T(8,128)(2,1)S(1)}, bf16[64,2048]{1,0:T(8,128)(2,1)S(1)}, u32[]{:S(2)}, u32[]{:S(2)}) collective-permute-start(bf16[64,2048]{1,0:T(8,128)(2,1)S(1)} %get-tuple-element.117), channel_id=1, source_target_pairs={{0,10},{2,12},{4,14},{6,15},{7,13},{5,11},{3,9},{1,8},{8,2},{10,4}... | collective-permute-start | bytes 786440 | tf_op jit(solution)/shard_map/ppermute | solution.py:42
  99.9 4.3 %collective-permute-start.21 = (bf16[384,2048]{1,0:T(8,128)(2,1)S(1)}, bf16[384,2048]{1,0:T(8,128)(2,1)S(1)}, u32[]{:S(2)}, u32[]{:S(2)}) collective-permute-start(bf16[384,2048]{1,0:T(8,128)(2,1)S(1)} %get-tuple-element.121), channel_id=1, source_target_pairs={{0,16},{16,0},{1,17},{17,1},{2,18},{18,2},{3,19},{19,3},{4,20},{20... | collective-permute-start | bytes 4718600 | tf_op jit(solution)/shard_map/ppermute | solution.py:47
  99.9 6.1 %collective-permute-start.22 = (bf16[384,2048]{1,0:T(8,128)(2,1)S(1)}, bf16[384,2048]{1,0:T(8,128)(2,1)S(1)}, u32[]{:S(2)}, u32[]{:S(2)}) collective-permute-start(bf16[384,2048]{1,0:T(8,128)(2,1)S(1)} %get-tuple-element.123), channel_id=1, source_target_pairs={{0,16},{16,0},{1,17},{17,1},{2,18},{18,2},{3,19},{19,3},{4,20},{20... | collective-permute-start | bytes 4718600 | tf_op jit(solution)/shard_map/ppermute | solution.py:47
  100.4 7.5 %collective-permute-start.23 = (bf16[384,2048]{1,0:T(8,128)(2,1)S(1)}, bf16[384,2048]{1,0:T(8,128)(2,1)S(1)}, u32[]{:S(2)}, u32[]{:S(2)}) collective-permute-start(bf16[384,2048]{1,0:T(8,128)(2,1)S(1)} %get-tuple-element.125), channel_id=1, source_target_pairs={{0,16},{16,0},{1,17},{17,1},{2,18},{18,2},{3,19},{19,3},{4,20},{20... | collective-permute-start | bytes 4718600 | tf_op jit(solution)/shard_map/ppermute | solution.py:47
  100.6 10.1 %collective-permute-start.20 = (bf16[64,2048]{1,0:T(8,128)(2,1)S(1)}, bf16[64,2048]{1,0:T(8,128)(2,1)S(1)}, u32[]{:S(2)}, u32[]{:S(2)}) collective-permute-start(bf16[64,2048]{1,0:T(8,128)(2,1)S(1)} %get-tuple-element.137), channel_id=1, source_target_pairs={{0,9},{2,8},{4,10},{6,12},{7,14},{5,15},{3,13},{1,11},{8,1},{10,0}... | collective-permute-start | bytes 786440 | tf_op jit(solution)/shard_map/ppermute | solution.py:42
  103.0 12.9 %collective-permute-start.19 = (bf16[64,2048]{1,0:T(8,128)(2,1)S(1)}, bf16[64,2048]{1,0:T(8,128)(2,1)S(1)}, u32[]{:S(2)}, u32[]{:S(2)}) collective-permute-start(bf16[64,2048]{1,0:T(8,128)(2,1)S(1)} %get-tuple-element.138), channel_id=1, source_target_pairs={{0,9},{2,8},{4,10},{6,12},{7,14},{5,15},{3,13},{1,11},{8,1},{10,0}... | collective-permute-start | bytes 786440 | tf_op jit(solution)/shard_map/ppermute | solution.py:42

commit v8 on v7

--- a/solution.py
+++ b/solution.py
@@ -292,7 +292,7 @@
     groups = [names[i : i + 4] for i in range(0, len(names) - 4, 4)]
     groups.append([name for name in names[-4:] if name[0] == "far"])
     groups.append([name for name in names[-4:] if name[0] == "near"])
-    held = {("near", 0): home, ("far", 0): tie((home, own[0]))[0]}
+    held = {("near", 0): home, ("far", 0): tie((home, own))[0]}
     partial, kept = {}, []
 
     def work(group):
@@ -322,8 +322,9 @@
     blocks = [held[name] for group in groups for name in group]
     steps = (1, -1)
     finals = []
+    here, near_sum = tie((partial["near", 0], near_sum))
     for part, step in zip(both, steps):
-        kept_here = add(home[:, part], partial["near", 0][:, part])
+        kept_here = add(home[:, part], here[:, part])
         finals.append([from_behind(kept_here, "section", step)])
     for k in range(ahead, 1, -1):
         near_sum = ring_shift(near_sum, -1)
@@ -336,11 +337,11 @@
             own_total, other_total = weight_call(blocks, kept, width, peers)
             here = [final[0] for final in finals]
             near_sum, own_total, other_total, _ = tie((near_sum, own_total, other_total, here))
-            near_sum = add(near_sum, partial["near", 2])
             lasts = [add(far_sum[:, part], partial["far", 1][:, part]) for part in both]
-            near_sum, lasts = tie((near_sum, lasts))
             for final, last, step in zip(finals, lasts, steps):
                 final.append(ring_shift(last, 1, step))
+            near_sum, _ = tie((near_sum, lasts))
+            near_sum = add(near_sum, partial["near", 2])
         elif k == 2:
             here = [final[1] for final in finals]
             near_sum, other_total, _ = tie((near_sum, other_total, here))

time: 117 us -> 116 us (level)
  starting transfers between devices: 26.6 us -> 25.4 us
    ppermute x16, starting transfers between devices: 23 us -> 21.4 us  [ring_shift(): return lax.ppermute(value, ('rep', 'section', 'exp'), pairs)]
  transfers between devices with their start and end apart: 24 -> 24, of which waited for: 9 -> 15; matrix products, arithmetic and copies ran while one was open for 5% -> 5% of each run, Pallas kernels for 24% -> 25%
where the time goes in v8:
time: 116 us
  waiting for transfers between devices  50.3 us (43%)
  Pallas kernels  28.6 us (25%)
  starting transfers between devices  25.4 us (22%)
  other arithmetic  7.15 us (6%)
  local copies, waits for them, and re-layouts  3.97 us (3%)
    ppermute x16, waiting for transfers between devices, ring_shift(): return lax.ppermute(value, ('rep', 'section', 'exp'), pairs)  49.7 us
    ppermute x16, starting transfers between devices, ring_shift(): return lax.ppermute(value, ('rep', 'section', 'exp'), pairs)  21.4 us
    pallas_call x3, Pallas kernels, expert_call(): pl.pallas_call(functools.partial(expert_kernel, count, experts, local_exp...  20.1 us
    convert_element_type x9, other arithmetic, add(): return (a.astype(F32) + b.astype(F32)).astype(BF16)  6.11 us
    pallas_call x1, Pallas kernels, weight_call(): pl.pallas_call(functools.partial(weight_kernel, len(kept), count), out_sh...  5.88 us
    ppermute x8, starting transfers between devices, from_behind(): lax.ppermute(value, axis, [(i, (i + by) % peers) for i in range(peers)])  4 us
    unnamed x8, local copies, waits for them, and re-layouts  3.97 us
  transfers between devices with their start and end apart: 24, of which 15 were waited for; matrix products, arithmetic and copies ran while one was open for 5% of the time, Pallas kernels for 25%

profile of v8, /device:TPU:0, one launch (start us, length us, event | category | flops | bytes accessed | tf_op | source)
XLA Modules:
  0.0 116.2 jit_solution(5062882970287628888)
XLA Ops:
  0.6 0.5 collective-permute-start.3
  1.2 0.1 collective-permute-start.4
  1.2 0.4 collective-permute-start.5
  1.7 2.2 %pack_rows.1.refs_0_ = bf16[64,4224]{1,0:T(8,128)(2,1)} custom-call(bf16[64,2048]{1,0:T(8,128)(2,1)} %bitcast.30, s32[16,64]{1,0:T(8,128)} %bitcast.32, s32[8,64]{1,0:T(8,128)} %bitcast.33, f32[8,64]{1,0:T(8,128)} %bitcast.34, bf16[64,2048]{1,0:T(8,128)(2,1)} %bitcast.31), custom_call_target="tpu_custom_call" | custom-call | tf_op jit(solution)/shard_map/pack_rows/pallas_call | solution.py:274
  3.9 2.7 %collective-permute-start = (bf16[64,4224]{1,0:T(8,128)(2,1)}, bf16[64,4224]{1,0:T(8,128)(2,1)S(1)}, u32[]{:S(2)}, u32[]{:S(2)}) collective-permute-start(bf16[64,4224]{1,0:T(8,128)(2,1)} %pack_rows.1.refs_0_), channel_id=1, source_target_pairs={{0,2},{2,4},{4,6},{6,7},{7,5},{5,3},{3,1},{1,0},{8,10},{10,12},{12... | collective-permute-start | bytes 1622024 | tf_op jit(solution)/shard_map/ppermute | solution.py:42
  6.5 1.4 %copy-done.1 = bf16[1,2,192,2048]{3,2,1,0:T(8,128)(2,1)S(1)} copy-done((bf16[1,2,192,2048]{3,2,1,0:T(8,128)(2,1)S(1)}, bf16[1,2,192,2048]{3,2,1,0:T(8,128)(2,1)}, u32[]{:S(2)}) %copy-start.1) | copy-done | bytes 1572888
  7.9 0.1 load_weights.2.refs_4_.refs_2_
  8.1 1.3 %copy-done.2 = bf16[1,2,192,2048]{3,2,1,0:T(8,128)(2,1)S(1)} copy-done((bf16[1,2,192,2048]{3,2,1,0:T(8,128)(2,1)S(1)}, bf16[1,2,192,2048]{3,2,1,0:T(8,128)(2,1)}, u32[]{:S(2)}) %copy-start.2) | copy-done | bytes 1572888
  9.3 0.5 copy-done.3
  9.8 0.2 load_weights.3
  10.1 0.8 copy-done
  10.9 0.0 collective-permute-start.1
  10.9 5.0 %collective-permute-done.refs_1_ = bf16[64,4224]{1,0:T(8,128)(2,1)S(1)} collective-permute-done((bf16[64,4224]{1,0:T(8,128)(2,1)}, bf16[64,4224]{1,0:T(8,128)(2,1)S(1)}, u32[]{:S(2)}, u32[]{:S(2)}) %collective-permute-start) | collective-permute-done | bytes 540704 | tf_op jit(solution)/shard_map/ppermute | solution.py:42
  15.8 2.4 %collective-permute-start.2 = (bf16[64,4224]{1,0:T(8,128)(2,1)S(1)}, bf16[64,4224]{1,0:T(8,128)(2,1)S(1)}, u32[]{:S(2)}, u32[]{:S(2)}) collective-permute-start(bf16[64,4224]{1,0:T(8,128)(2,1)S(1)} %collective-permute-done.refs_1_), channel_id=1, source_target_pairs={{0,2},{2,4},{4,6},{6,7},{7,5},{5,3},{3,1},{1,0},{8,10},{10,12},{12... | collective-permute-start | bytes 1622024 | tf_op jit(solution)/shard_map/ppermute | solution.py:42
  18.2 5.4 %collective-permute-done.1.refs_2_ = bf16[64,4224]{1,0:T(8,128)(2,1)S(1)} collective-permute-done((bf16[64,4224]{1,0:T(8,128)(2,1)S(1)}, bf16[64,4224]{1,0:T(8,128)(2,1)S(1)}, u32[]{:S(2)}, u32[]{:S(2)}) %collective-permute-start.1) | collective-permute-done | bytes 540704 | tf_op jit(solution)/shard_map/ppermute | solution.py:42
  23.6 0.0 collective-permute-start.8
  23.6 4.6 %collective-permute-done.2.refs_3_ = bf16[64,4224]{1,0:T(8,128)(2,1)S(1)} collective-permute-done((bf16[64,4224]{1,0:T(8,128)(2,1)S(1)}, bf16[64,4224]{1,0:T(8,128)(2,1)S(1)}, u32[]{:S(2)}, u32[]{:S(2)}) %collective-permute-start.2) | collective-permute-done | bytes 540704 | tf_op jit(solution)/shard_map/ppermute | solution.py:42
  28.2 2.5 %collective-permute-start.6 = (bf16[64,4224]{1,0:T(8,128)(2,1)S(1)}, bf16[64,4224]{1,0:T(8,128)(2,1)S(1)}, u32[]{:S(2)}, u32[]{:S(2)}) collective-permute-start(bf16[64,4224]{1,0:T(8,128)(2,1)S(1)} %collective-permute-done.2.refs_3_), channel_id=1, source_target_pairs={{0,2},{2,4},{4,6},{6,7},{7,5},{5,3},{3,1},{1,0},{8,10},{10,12},{12... | collective-permute-start | bytes 1622024 | tf_op jit(solution)/shard_map/ppermute | solution.py:42
  30.7 6.5 %collective-permute-done.8.refs_0_.refs_4_ = bf16[64,4224]{1,0:T(8,128)(2,1)S(1)} collective-permute-done((bf16[64,4224]{1,0:T(8,128)(2,1)S(1)}, bf16[64,4224]{1,0:T(8,128)(2,1)S(1)}, u32[]{:S(2)}, u32[]{:S(2)}) %collective-permute-start.8) | collective-permute-done | bytes 540704 | tf_op jit(solution)/shard_map/ppermute | solution.py:42
  37.1 0.0 collective-permute-start.9
  37.1 0.0 collective-permute-done.3.refs_7_.refs_5_
  37.1 7.7 %expert_rows.3 = (bf16[64,4096]{1,0:T(8,128)(2,1)S(1)}, bf16[64,4096]{1,0:T(8,128)(2,1)S(1)}, bf16[64,4096]{1,0:T(8,128)(2,1)S(1)}, bf16[64,4096]{1,0:T(8,128)(2...) custom-call(bf16[64,4224]{1,0:T(8,128)(2,1)S(1)} %copy-done, ...), custom_call_target="tpu_custom_call" | custom-call | flops 4831838208 | bytes 13631488 | tf_op jit(solution)/shard_map/expert_rows/pallas_call | solution.py:191
  44.9 0.0 collective-permute-done.6.refs_0_.refs_6_
  44.9 2.1 %collective-permute-start.7 = (bf16[64,4224]{1,0:T(8,128)(2,1)S(1)}, bf16[64,4224]{1,0:T(8,128)(2,1)S(1)}, u32[]{:S(2)}, u32[]{:S(2)}) collective-permute-start(bf16[64,4224]{1,0:T(8,128)(2,1)S(1)} %collective-permute-done.6.refs_0_.refs_6_), channel_id=1, source_target_pairs={{0,2},{2,4},{4,6},{6,7},{7,5},{5,3},{3,1},{1,0},{8,10},{10,12},{12... | collective-permute-start | bytes 1622024 | tf_op jit(solution)/shard_map/ppermute | solution.py:42
  46.9 2.3 %collective-permute-done.9.refs_1_.refs_5_ = bf16[64,4224]{1,0:T(8,128)(2,1)S(1)} collective-permute-done((bf16[64,4224]{1,0:T(8,128)(2,1)S(1)}, bf16[64,4224]{1,0:T(8,128)(2,1)S(1)}, u32[]{:S(2)}, u32[]{:S(2)}) %collective-permute-start.9) | collective-permute-done | bytes 540704 | tf_op jit(solution)/shard_map/ppermute | solution.py:42
  49.2 6.2 %expert_rows.4 = (bf16[64,4096]{1,0:T(8,128)(2,1)S(1)}, bf16[64,4096]{1,0:T(8,128)(2,1)S(1)}, bf16[768,128]{1,0:T(8,128)(2,1)S(1)}, bf16[768,128]{1,0:T(8,128)(2,1)S(1)}, bf16[768,128]{1,0:T(8,128)(2,1)S(1)}) custom-call(bf16[64,4224]{1,0:T(8,128)(2,1)S(1)} %collective-permute-done.8.refs_0_.refs_4_, ...), custom_call_target="tpu_custom_call" | custom-call | flops 2415919104 | bytes 11534336 | tf_op jit(solution)/shard_map/expert_rows/pallas_call | solution.py:191
  55.4 2.0 %collective-permute-start.11 = (bf16[64,4096]{1,0:T(8,128)(2,1)S(1)}, bf16[64,4096]{1,0:T(8,128)(2,1)S(1)}, u32[]{:S(2)}, u32[]{:S(2)}) collective-permute-start(bf16[64,4096]{1,0:T(8,128)(2,1)S(1)} %get-tuple-element.91), channel_id=1, source_target_pairs={{0,2},{2,4},{4,6},{6,7},{7,5},{5,3},{3,1},{1,0},{8,10},{10,12},{12... | collective-permute-start | bytes 1572872 | tf_op jit(solution)/shard_map/ppermute | solution.py:42
  57.4 6.2 %expert_rows.5 = (bf16[64,4096]{1,0:T(8,128)(2,1)S(1)}, bf16[64,4096]{1,0:T(8,128)(2,1)S(1)}, bf16[768,128]{1,0:T(8,128)(2,1)S(1)}, bf16[768,128]{1,0:T(8,128)(2,1)S(1)}, bf16[768,128]{1,0:T(8,128)(2,1)S(1)}) custom-call(bf16[64,4224]{1,0:T(8,128)(2,1)S(1)} %collective-permute-done.6.refs_0_.refs_6_, ...), custom_call_target="tpu_custom_call" | custom-call | flops 2415919104 | bytes 11534336 | tf_op jit(solution)/shard_map/expert_rows/pallas_call | solution.py:191
  63.6 0.2 collective-permute-start.14
  63.8 4.2 %collective-permute-done.11 = bf16[64,4096]{1,0:T(8,128)(2,1)S(1)} collective-permute-done((bf16[64,4096]{1,0:T(8,128)(2,1)S(1)}, bf16[64,4096]{1,0:T(8,128)(2,1)S(1)}, u32[]{:S(2)}, u32[]{:S(2)}) %collective-permute-start.11) | collective-permute-done | bytes 524320 | tf_op jit(solution)/shard_map/ppermute | solution.py:42
  68.0 0.1 add_convert_fusion.5
  68.1 2.1 %collective-permute-start.12 = (bf16[64,4096]{1,0:T(8,128)(2,1)S(1)}, bf16[64,4096]{1,0:T(8,128)(2,1)S(1)}, u32[]{:S(2)}, u32[]{:S(2)}) collective-permute-start(bf16[64,4096]{1,0:T(8,128)(2,1)S(1)} %add_convert_fusion.5), channel_id=1, source_target_pairs={{0,2},{2,4},{4,6},{6,7},{7,5},{5,3},{3,1},{1,0},{8,10},{10,12},{12... | collective-permute-start | bytes 1572872 | tf_op jit(solution)/shard_map/ppermute | solution.py:42
  70.3 0.1 add_convert_fusion.11
  70.4 1.6 %collective-permute-start.16 = (bf16[64,2048]{1,0:T(8,128)(2,1)S(1)}, bf16[64,2048]{1,0:T(8,128)(2,1)S(1)}, u32[]{:S(2)}, u32[]{:S(2)}) collective-permute-start(bf16[64,2048]{1,0:T(8,128)(2,1)S(1)} %get-tuple-element.135), channel_id=1, source_target_pairs={{0,8},{8,0},{1,9},{9,1},{2,10},{10,2},{3,11},{11,3},{4,12},{12,4},... | collective-permute-start | bytes 786440 | tf_op jit(solution)/shard_map/ppermute | solution.py:47
  72.0 0.5 collective-permute-start.10
  72.5 1.7 %collective-permute-done.14 = bf16[64,4096]{1,0:T(8,128)(2,1)S(1)} collective-permute-done((bf16[64,4096]{1,0:T(8,128)(2,1)S(1)}, bf16[64,4096]{1,0:T(8,128)(2,1)S(1)}, u32[]{:S(2)}, u32[]{:S(2)}) %collective-permute-start.14) | collective-permute-done | bytes 524320 | tf_op jit(solution)/shard_map/ppermute | solution.py:42
  74.1 0.1 add_convert_fusion.4
  74.3 0.3 collective-permute-start.15
  74.6 5.9 %weight_grads.1 = (bf16[384,2048]{1,0:T(8,128)(2,1)S(1)}, bf16[384,2048]{1,0:T(8,128)(2,1)S(1)}, bf16[384,2048]{1,0:T(8,128)(2,1)S(1)}, bf16[384,2048]{1,0:T(8,1...) custom-call(bf16[64,4224]{1,0:T(8,128)(2,1)S(1)} %copy-done, ...), custom_call_target="tpu_custom_call" | custom-call | flops 4831838208 | bytes 13631488 | tf_op jit(solution)/shard_map/weight_grads/pallas_call | solution.py:242
  80.5 1.0 collective-permute-done.12
  81.5 0.1 add_convert_fusion.10
  81.6 0.0 collective-permute-done.16
  81.6 0.0 collective-permute-done.10
  81.6 1.9 %collective-permute-done.15 = bf16[64,4096]{1,0:T(8,128)(2,1)S(1)} collective-permute-done((bf16[64,4096]{1,0:T(8,128)(2,1)S(1)}, bf16[64,4096]{1,0:T(8,128)(2,1)S(1)}, u32[]{:S(2)}, u32[]{:S(2)}) %collective-permute-start.15) | collective-permute-done | bytes 524320 | tf_op jit(solution)/shard_map/ppermute | solution.py:42
  83.5 0.1 add_convert_fusion.3
  83.6 0.3 collective-permute-start.17
  84.0 2.7 %collective-permute-start.18 = (bf16[64,2048]{1,0:T(8,128)(2,1)S(1)}, bf16[64,2048]{1,0:T(8,128)(2,1)S(1)}, u32[]{:S(2)}, u32[]{:S(2)}) collective-permute-start(bf16[64,2048]{1,0:T(8,128)(2,1)S(1)} %get-tuple-element.139), channel_id=1, source_target_pairs={{0,10},{2,12},{4,14},{6,15},{7,13},{5,11},{3,9},{1,8},{8,2},{10,4}... | collective-permute-start | bytes 786440 | tf_op jit(solution)/shard_map/ppermute | solution.py:42
  86.7 1.5 %collective-permute-start.13 = (bf16[64,2048]{1,0:T(8,128)(2,1)S(1)}, bf16[64,2048]{1,0:T(8,128)(2,1)S(1)}, u32[]{:S(2)}, u32[]{:S(2)}) collective-permute-start(bf16[64,2048]{1,0:T(8,128)(2,1)S(1)} %get-tuple-element.140), channel_id=1, source_target_pairs={{0,10},{2,12},{4,14},{6,15},{7,13},{5,11},{3,9},{1,8},{8,2},{10,4}... | collective-permute-start | bytes 786440 | tf_op jit(solution)/shard_map/ppermute | solution.py:42
  88.2 5.9 %collective-permute-done.18 = bf16[64,2048]{1,0:T(8,128)(2,1)S(1)} collective-permute-done((bf16[64,2048]{1,0:T(8,128)(2,1)S(1)}, bf16[64,2048]{1,0:T(8,128)(2,1)S(1)}, u32[]{:S(2)}, u32[]{:S(2)}) %collective-permute-start.18) | collective-permute-done | bytes 262176 | tf_op jit(solution)/shard_map/ppermute | solution.py:42
  94.1 5.1 %collective-permute-done.13 = bf16[64,2048]{1,0:T(8,128)(2,1)S(1)} collective-permute-done((bf16[64,2048]{1,0:T(8,128)(2,1)S(1)}, bf16[64,2048]{1,0:T(8,128)(2,1)S(1)}, u32[]{:S(2)}, u32[]{:S(2)}) %collective-permute-start.13) | collective-permute-done | bytes 262176 | tf_op jit(solution)/shard_map/ppermute | solution.py:42
  99.2 0.4 collective-permute-start.21
  99.6 0.1 collective-permute-start.22
  99.7 0.4 collective-permute-start.23
  100.1 0.1 add_convert_fusion.8
  100.2 1.7 %collective-permute-start.20 = (bf16[64,2048]{1,0:T(8,128)(2,1)S(1)}, bf16[64,2048]{1,0:T(8,128)(2,1)S(1)}, u32[]{:S(2)}, u32[]{:S(2)}) collective-permute-start(bf16[64,2048]{1,0:T(8,128)(2,1)S(1)} %get-tuple-element.137), channel_id=1, source_target_pairs={{0,9},{2,8},{4,10},{6,12},{7,14},{5,15},{3,13},{1,11},{8,1},{10,0}... | collective-permute-start | bytes 786440 | tf_op jit(solution)/shard_map/ppermute | solution.py:42
  101.9 1.0 collective-permute-start.19
  102.9 1.8 %add_convert_fusion.2 = bf16[384,2048]{1,0:T(8,128)(2,1)} fusion(bf16[384,2048]{1,0:T(8,128)(2,1)S(1)} %collective-permute-done.21, bf16[384,2048]{1,0:T(8,128)(2,1)S(1)} %get-tuple-element.120), kind=kLoop, calls=%fused_computation.2 | loop fusion | flops 3145728 | bytes 4718592 | tf_op jit(solution)/shard_map/convert_element_type | solution.py:260
  104.7 0.1 collective-permute-done.22
  104.9 1.8 %add_convert_fusion.1 = bf16[384,2048]{1,0:T(8,128)(2,1)} fusion(bf16[384,2048]{1,0:T(8,128)(2,1)S(1)} %collective-permute-done.22, bf16[384,2048]{1,0:T(8,128)(2,1)S(1)} %get-tuple-element.122), kind=kLoop, calls=%fused_computation.1 | loop fusion | flops 3145728 | bytes 4718592 | tf_op jit(solution)/shard_map/convert_element_type | solution.py:260
  106.7 0.4 collective-permute-done.23
  107.1 1.7 %add_convert_fusion = bf16[384,2048]{1,0:T(8,128)(2,1)} fusion(bf16[384,2048]{1,0:T(8,128)(2,1)S(1)} %collective-permute-done.23, bf16[384,2048]{1,0:T(8,128)(2,1)S(1)} %get-tuple-element.124), kind=kLoop, calls=%fused_computation | loop fusion | flops 3145728 | bytes 4718592 | tf_op jit(solution)/shard_map/convert_element_type | solution.py:260
  108.9 1.5 %collective-permute-done.20 = bf16[64,2048]{1,0:T(8,128)(2,1)S(1)} collective-permute-done((bf16[64,2048]{1,0:T(8,128)(2,1)S(1)}, bf16[64,2048]{1,0:T(8,128)(2,1)S(1)}, u32[]{:S(2)}, u32[]{:S(2)}) %collective-permute-start.20) | collective-permute-done | bytes 262176 | tf_op jit(solution)/shard_map/ppermute | solution.py:42
  110.3 4.8 %collective-permute-done.19 = bf16[64,2048]{1,0:T(8,128)(2,1)S(1)} collective-permute-done((bf16[64,2048]{1,0:T(8,128)(2,1)S(1)}, bf16[64,2048]{1,0:T(8,128)(2,1)S(1)}, u32[]{:S(2)}, u32[]{:S(2)}) %collective-permute-start.19) | collective-permute-done | bytes 262176 | tf_op jit(solution)/shard_map/ppermute | solution.py:42
  115.1 1.0 fusion
  (9 shorter events, 0.0 us)
Async XLA Ops:
  0.6 36.5 %collective-permute-start.3 = (bf16[384,2048]{1,0:T(8,128)(2,1)}, bf16[384,2048]{1,0:T(8,128)(2,1)S(1)}, u32[]{:S(2)}, u32[]{:S(2)}) collective-permute-start(bf16[384,2048]{1,0:T(8,128)(2,1)} %bitcast.21), channel_id=1, source_target_pairs={{0,16},{16,0},{1,17},{17,1},{2,18},{18,2},{3,19},{19,3},{4,20},{20... | collective-permute-start | bytes 4718600 | tf_op jit(solution)/shard_map/ppermute | solution.py:47
  1.2 36.0 %collective-permute-start.4 = (bf16[384,2048]{1,0:T(8,128)(2,1)}, bf16[384,2048]{1,0:T(8,128)(2,1)S(1)}, u32[]{:S(2)}, u32[]{:S(2)}) collective-permute-start(bf16[384,2048]{1,0:T(8,128)(2,1)} %bitcast.23), channel_id=1, source_target_pairs={{0,16},{16,0},{1,17},{17,1},{2,18},{18,2},{3,19},{19,3},{4,20},{20... | collective-permute-start | bytes 4718600 | tf_op jit(solution)/shard_map/ppermute | solution.py:47
  1.2 35.9 %collective-permute-start.5 = (bf16[384,2048]{1,0:T(8,128)(2,1)}, bf16[384,2048]{1,0:T(8,128)(2,1)}, u32[]{:S(2)}, u32[]{:S(2)}) collective-permute-start(bf16[384,2048]{1,0:T(8,128)(2,1)} %bitcast.25), channel_id=1, source_target_pairs={{0,16},{16,0},{1,17},{17,1},{2,18},{18,2},{3,19},{19,3},{4,20},{20... | collective-permute-start | bytes 4718600 | tf_op jit(solution)/shard_map/ppermute | solution.py:47
  3.9 12.0 %collective-permute-start = (bf16[64,4224]{1,0:T(8,128)(2,1)}, bf16[64,4224]{1,0:T(8,128)(2,1)S(1)}, u32[]{:S(2)}, u32[]{:S(2)}) collective-permute-start(bf16[64,4224]{1,0:T(8,128)(2,1)} %pack_rows.1.refs_0_), channel_id=1, source_target_pairs={{0,2},{2,4},{4,6},{6,7},{7,5},{5,3},{3,1},{1,0},{8,10},{10,12},{12... | collective-permute-start | bytes 1622024 | tf_op jit(solution)/shard_map/ppermute | solution.py:42
  6.5 1.4 %copy-start.1 = (bf16[1,2,192,2048]{3,2,1,0:T(8,128)(2,1)S(1)}, bf16[1,2,192,2048]{3,2,1,0:T(8,128)(2,1)}, u32[]{:S(2)}) copy-start(bf16[1,2,192,2048]{3,2,1,0:T(8,128)(2,1)} %param.13) | copy-start | bytes 4718596
  7.9 1.4 %copy-start.2 = (bf16[1,2,192,2048]{3,2,1,0:T(8,128)(2,1)S(1)}, bf16[1,2,192,2048]{3,2,1,0:T(8,128)(2,1)}, u32[]{:S(2)}) copy-start(bf16[1,2,192,2048]{3,2,1,0:T(8,128)(2,1)} %param.14) | copy-start | bytes 4718596
  7.9 1.9 %copy-start.3 = (bf16[1,2,192,2048]{3,2,1,0:T(8,128)(2,1)S(1)}, bf16[1,2,192,2048]{3,2,1,0:T(8,128)(2,1)}, u32[]{:S(2)}) copy-start(bf16[1,2,192,2048]{3,2,1,0:T(8,128)(2,1)} %param.15) | copy-start | bytes 4718596
  9.8 1.0 copy-start
  10.9 12.7 %collective-permute-start.1 = (bf16[64,4224]{1,0:T(8,128)(2,1)S(1)}, bf16[64,4224]{1,0:T(8,128)(2,1)S(1)}, u32[]{:S(2)}, u32[]{:S(2)}) collective-permute-start(bf16[64,4224]{1,0:T(8,128)(2,1)S(1)} %copy-done), channel_id=1, source_target_pairs={{0,1},{2,0},{4,2},{6,4},{7,6},{5,7},{3,5},{1,3},{8,9},{10,8},{12,1... | collective-permute-start | bytes 1622024 | tf_op jit(solution)/shard_map/ppermute | solution.py:42
  15.8 12.3 %collective-permute-start.2 = (bf16[64,4224]{1,0:T(8,128)(2,1)S(1)}, bf16[64,4224]{1,0:T(8,128)(2,1)S(1)}, u32[]{:S(2)}, u32[]{:S(2)}) collective-permute-start(bf16[64,4224]{1,0:T(8,128)(2,1)S(1)} %collective-permute-done.refs_1_), channel_id=1, source_target_pairs={{0,2},{2,4},{4,6},{6,7},{7,5},{5,3},{3,1},{1,0},{8,10},{10,12},{12... | collective-permute-start | bytes 1622024 | tf_op jit(solution)/shard_map/ppermute | solution.py:42
  23.6 13.5 %collective-permute-start.8 = (bf16[64,4224]{1,0:T(8,128)(2,1)S(1)}, bf16[64,4224]{1,0:T(8,128)(2,1)S(1)}, u32[]{:S(2)}, u32[]{:S(2)}) collective-permute-start(bf16[64,4224]{1,0:T(8,128)(2,1)S(1)} %collective-permute-done.1.refs_2_), channel_id=1, source_target_pairs={{0,1},{2,0},{4,2},{6,4},{7,6},{5,7},{3,5},{1,3},{8,9},{10,8},{12,1... | collective-permute-start | bytes 1622024 | tf_op jit(solution)/shard_map/ppermute | solution.py:42
  28.2 16.7 %collective-permute-start.6 = (bf16[64,4224]{1,0:T(8,128)(2,1)S(1)}, bf16[64,4224]{1,0:T(8,128)(2,1)S(1)}, u32[]{:S(2)}, u32[]{:S(2)}) collective-permute-start(bf16[64,4224]{1,0:T(8,128)(2,1)S(1)} %collective-permute-done.2.refs_3_), channel_id=1, source_target_pairs={{0,2},{2,4},{4,6},{6,7},{7,5},{5,3},{3,1},{1,0},{8,10},{10,12},{12... | collective-permute-start | bytes 1622024 | tf_op jit(solution)/shard_map/ppermute | solution.py:42
  37.1 12.1 %collective-permute-start.9 = (bf16[64,4224]{1,0:T(8,128)(2,1)S(1)}, bf16[64,4224]{1,0:T(8,128)(2,1)S(1)}, u32[]{:S(2)}, u32[]{:S(2)}) collective-permute-start(bf16[64,4224]{1,0:T(8,128)(2,1)S(1)} %collective-permute-done.8.refs_0_.refs_4_), channel_id=1, source_target_pairs={{0,1},{2,0},{4,2},{6,4},{7,6},{5,7},{3,5},{1,3},{8,9},{10,8},{12,1... | collective-permute-start | bytes 1622024 | tf_op jit(solution)/shard_map/ppermute | solution.py:42
  44.9 12.5 %collective-permute-start.7 = (bf16[64,4224]{1,0:T(8,128)(2,1)S(1)}, bf16[64,4224]{1,0:T(8,128)(2,1)S(1)}, u32[]{:S(2)}, u32[]{:S(2)}) collective-permute-start(bf16[64,4224]{1,0:T(8,128)(2,1)S(1)} %collective-permute-done.6.refs_0_.refs_6_), channel_id=1, source_target_pairs={{0,2},{2,4},{4,6},{6,7},{7,5},{5,3},{3,1},{1,0},{8,10},{10,12},{12... | collective-permute-start | bytes 1622024 | tf_op jit(solution)/shard_map/ppermute | solution.py:42
  55.4 12.6 %collective-permute-start.11 = (bf16[64,4096]{1,0:T(8,128)(2,1)S(1)}, bf16[64,4096]{1,0:T(8,128)(2,1)S(1)}, u32[]{:S(2)}, u32[]{:S(2)}) collective-permute-start(bf16[64,4096]{1,0:T(8,128)(2,1)S(1)} %get-tuple-element.91), channel_id=1, source_target_pairs={{0,2},{2,4},{4,6},{6,7},{7,5},{5,3},{3,1},{1,0},{8,10},{10,12},{12... | collective-permute-start | bytes 1572872 | tf_op jit(solution)/shard_map/ppermute | solution.py:42
  63.6 10.5 %collective-permute-start.14 = (bf16[64,4096]{1,0:T(8,128)(2,1)S(1)}, bf16[64,4096]{1,0:T(8,128)(2,1)S(1)}, u32[]{:S(2)}, u32[]{:S(2)}) collective-permute-start(bf16[64,4096]{1,0:T(8,128)(2,1)S(1)} %get-tuple-element.94), channel_id=1, source_target_pairs={{0,1},{2,0},{4,2},{6,4},{7,6},{5,7},{3,5},{1,3},{8,9},{10,8},{12,1... | collective-permute-start | bytes 1572872 | tf_op jit(solution)/shard_map/ppermute | solution.py:42
  68.1 13.4 %collective-permute-start.12 = (bf16[64,4096]{1,0:T(8,128)(2,1)S(1)}, bf16[64,4096]{1,0:T(8,128)(2,1)S(1)}, u32[]{:S(2)}, u32[]{:S(2)}) collective-permute-start(bf16[64,4096]{1,0:T(8,128)(2,1)S(1)} %add_convert_fusion.5), channel_id=1, source_target_pairs={{0,2},{2,4},{4,6},{6,7},{7,5},{5,3},{3,1},{1,0},{8,10},{10,12},{12... | collective-permute-start | bytes 1572872 | tf_op jit(solution)/shard_map/ppermute | solution.py:42
  70.4 11.2 %collective-permute-start.16 = (bf16[64,2048]{1,0:T(8,128)(2,1)S(1)}, bf16[64,2048]{1,0:T(8,128)(2,1)S(1)}, u32[]{:S(2)}, u32[]{:S(2)}) collective-permute-start(bf16[64,2048]{1,0:T(8,128)(2,1)S(1)} %get-tuple-element.135), channel_id=1, source_target_pairs={{0,8},{8,0},{1,9},{9,1},{2,10},{10,2},{3,11},{11,3},{4,12},{12,4},... | collective-permute-start | bytes 786440 | tf_op jit(solution)/shard_map/ppermute | solution.py:47
  72.0 9.6 %collective-permute-start.10 = (bf16[64,2048]{1,0:T(8,128)(2,1)S(1)}, bf16[64,2048]{1,0:T(8,128)(2,1)S(1)}, u32[]{:S(2)}, u32[]{:S(2)}) collective-permute-start(bf16[64,2048]{1,0:T(8,128)(2,1)S(1)} %get-tuple-element.136), channel_id=1, source_target_pairs={{0,8},{8,0},{1,9},{9,1},{2,10},{10,2},{3,11},{11,3},{4,12},{12,4},... | collective-permute-start | bytes 786440 | tf_op jit(solution)/shard_map/ppermute | solution.py:47
  74.3 9.2 %collective-permute-start.15 = (bf16[64,4096]{1,0:T(8,128)(2,1)S(1)}, bf16[64,4096]{1,0:T(8,128)(2,1)S(1)}, u32[]{:S(2)}, u32[]{:S(2)}) collective-permute-start(bf16[64,4096]{1,0:T(8,128)(2,1)S(1)} %add_convert_fusion.4), channel_id=1, source_target_pairs={{0,1},{2,0},{4,2},{6,4},{7,6},{5,7},{3,5},{1,3},{8,9},{10,8},{12,1... | collective-permute-start | bytes 1572872 | tf_op jit(solution)/shard_map/ppermute | solution.py:42
  83.6 15.6 %collective-permute-start.17 = (bf16[64,4096]{1,0:T(8,128)(2,1)S(1)}, bf16[64,4096]{1,0:T(8,128)(2,1)S(1)}, u32[]{:S(2)}, u32[]{:S(2)}) collective-permute-start(bf16[64,4096]{1,0:T(8,128)(2,1)S(1)} %add_convert_fusion.3), channel_id=1, source_target_pairs={{0,1},{2,0},{4,2},{6,4},{7,6},{5,7},{3,5},{1,3},{8,9},{10,8},{12,1... | collective-permute-start | bytes 1572872 | tf_op jit(solution)/shard_map/ppermute | solution.py:42
  84.0 10.1 %collective-permute-start.18 = (bf16[64,2048]{1,0:T(8,128)(2,1)S(1)}, bf16[64,2048]{1,0:T(8,128)(2,1)S(1)}, u32[]{:S(2)}, u32[]{:S(2)}) collective-permute-start(bf16[64,2048]{1,0:T(8,128)(2,1)S(1)} %get-tuple-element.139), channel_id=1, source_target_pairs={{0,10},{2,12},{4,14},{6,15},{7,13},{5,11},{3,9},{1,8},{8,2},{10,4}... | collective-permute-start | bytes 786440 | tf_op jit(solution)/shard_map/ppermute | solution.py:42
  86.7 12.5 %collective-permute-start.13 = (bf16[64,2048]{1,0:T(8,128)(2,1)S(1)}, bf16[64,2048]{1,0:T(8,128)(2,1)S(1)}, u32[]{:S(2)}, u32[]{:S(2)}) collective-permute-start(bf16[64,2048]{1,0:T(8,128)(2,1)S(1)} %get-tuple-element.140), channel_id=1, source_target_pairs={{0,10},{2,12},{4,14},{6,15},{7,13},{5,11},{3,9},{1,8},{8,2},{10,4}... | collective-permute-start | bytes 786440 | tf_op jit(solution)/shard_map/ppermute | solution.py:42
  99.2 3.7 %collective-permute-start.21 = (bf16[384,2048]{1,0:T(8,128)(2,1)S(1)}, bf16[384,2048]{1,0:T(8,128)(2,1)S(1)}, u32[]{:S(2)}, u32[]{:S(2)}) collective-permute-start(bf16[384,2048]{1,0:T(8,128)(2,1)S(1)} %get-tuple-element.121), channel_id=1, source_target_pairs={{0,16},{16,0},{1,17},{17,1},{2,18},{18,2},{3,19},{19,3},{4,20},{20... | collective-permute-start | bytes 4718600 | tf_op jit(solution)/shard_map/ppermute | solution.py:47
  99.6 5.3 %collective-permute-start.22 = (bf16[384,2048]{1,0:T(8,128)(2,1)S(1)}, bf16[384,2048]{1,0:T(8,128)(2,1)S(1)}, u32[]{:S(2)}, u32[]{:S(2)}) collective-permute-start(bf16[384,2048]{1,0:T(8,128)(2,1)S(1)} %get-tuple-element.123), channel_id=1, source_target_pairs={{0,16},{16,0},{1,17},{17,1},{2,18},{18,2},{3,19},{19,3},{4,20},{20... | collective-permute-start | bytes 4718600 | tf_op jit(solution)/shard_map/ppermute | solution.py:47
  99.7 7.4 %collective-permute-start.23 = (bf16[384,2048]{1,0:T(8,128)(2,1)S(1)}, bf16[384,2048]{1,0:T(8,128)(2,1)S(1)}, u32[]{:S(2)}, u32[]{:S(2)}) collective-permute-start(bf16[384,2048]{1,0:T(8,128)(2,1)S(1)} %get-tuple-element.125), channel_id=1, source_target_pairs={{0,16},{16,0},{1,17},{17,1},{2,18},{18,2},{3,19},{19,3},{4,20},{20... | collective-permute-start | bytes 4718600 | tf_op jit(solution)/shard_map/ppermute | solution.py:47
  100.2 10.1 %collective-permute-start.20 = (bf16[64,2048]{1,0:T(8,128)(2,1)S(1)}, bf16[64,2048]{1,0:T(8,128)(2,1)S(1)}, u32[]{:S(2)}, u32[]{:S(2)}) collective-permute-start(bf16[64,2048]{1,0:T(8,128)(2,1)S(1)} %get-tuple-element.137), channel_id=1, source_target_pairs={{0,9},{2,8},{4,10},{6,12},{7,14},{5,15},{3,13},{1,11},{8,1},{10,0}... | collective-permute-start | bytes 786440 | tf_op jit(solution)/shard_map/ppermute | solution.py:42
  101.9 13.2 %collective-permute-start.19 = (bf16[64,2048]{1,0:T(8,128)(2,1)S(1)}, bf16[64,2048]{1,0:T(8,128)(2,1)S(1)}, u32[]{:S(2)}, u32[]{:S(2)}) collective-permute-start(bf16[64,2048]{1,0:T(8,128)(2,1)S(1)} %get-tuple-element.138), channel_id=1, source_target_pairs={{0,9},{2,8},{4,10},{6,12},{7,14},{5,15},{3,13},{1,11},{8,1},{10,0}... | collective-permute-start | bytes 786440 | tf_op jit(solution)/shard_map/ppermute | solution.py:42

commit v9 on v8

--- a/solution.py
+++ b/solution.py
@@ -334,18 +334,19 @@
             far_sum = ring_shift(add(far_sum, partial["far", left]), 1)
             near_sum, _ = tie((near_sum, far_done))
         if k == 3:
-            own_total, other_total = weight_call(blocks, kept, width, peers)
-            here = [final[0] for final in finals]
-            near_sum, own_total, other_total, _ = tie((near_sum, own_total, other_total, here))
             lasts = [add(far_sum[:, part], partial["far", 1][:, part]) for part in both]
             for final, last, step in zip(finals, lasts, steps):
                 final.append(ring_shift(last, 1, step))
-            near_sum, _ = tie((near_sum, lasts))
+            kept[-1], _ = tie((kept[-1], lasts))
+            own_total, other_total = weight_call(blocks, kept, width, peers)
+            here = [final[0] for final in finals] + finals[0][1:]
+            near_sum, own_total, other_total, _ = tie((near_sum, own_total, other_total, here))
             near_sum = add(near_sum, partial["near", 2])
+            near_sum, other_total = tie((near_sum, other_total))
+            received = [from_behind(g, "rep", 1) for g in other_total]
         elif k == 2:
             here = [final[1] for final in finals]
-            near_sum, other_total, _ = tie((near_sum, other_total, here))
-            received = [from_behind(g, "rep", 1) for g in other_total]
+            near_sum, _ = tie((near_sum, here))
         elif k > 2:
             near_sum = add(near_sum, partial["near", k - 1])
     lasts = [add(near_sum[:, part], partial["near", 1][:, part]) for part in both]

time: 116 us -> 119 us (1.026)
  waiting for transfers between devices: 50.3 us -> 53.8 us
    ppermute x16, waiting for transfers between devices: 49.7 us -> 53.8 us  [ring_shift(): return lax.ppermute(value, ('rep', 'section', 'exp'), pairs)]
  transfers between devices with their start and end apart: 24 -> 24, of which waited for: 15 -> 12; matrix products, arithmetic and copies ran while one was open for 5% -> 5% of each run, Pallas kernels for 25% -> 24%
where the time goes in v9:
time: 119 us
  waiting for transfers between devices  53.8 us (45%)
  Pallas kernels  28.6 us (24%)
  starting transfers between devices  24.4 us (21%)
  other arithmetic  7.15 us (6%)
  local copies, waits for them, and re-layouts  3.97 us (3%)
    ppermute x16, waiting for transfers between devices, ring_shift(): return lax.ppermute(value, ('rep', 'section', 'exp'), pairs)  53.8 us
    ppermute x16, starting transfers between devices, ring_shift(): return lax.ppermute(value, ('rep', 'section', 'exp'), pairs)  20.7 us
    pallas_call x3, Pallas kernels, expert_call(): pl.pallas_call(functools.partial(expert_kernel, count, experts, local_exp...  20.1 us
    convert_element_type x9, other arithmetic, add(): return (a.astype(F32) + b.astype(F32)).astype(BF16)  6.12 us
    pallas_call x1, Pallas kernels, weight_call(): pl.pallas_call(functools.partial(weight_kernel, len(kept), count), out_sh...  5.88 us
    unnamed x8, local copies, waits for them, and re-layouts  3.97 us
    ppermute x8, starting transfers between devices, from_behind(): lax.ppermute(value, axis, [(i, (i + by) % peers) for i in range(peers)])  3.69 us
  transfers between devices with their start and end apart: 24, of which 12 were waited for; matrix products, arithmetic and copies ran while one was open for 5% of the time, Pallas kernels for 24%

profile of v9, /device:TPU:0, one launch (start us, length us, event | category | flops | bytes accessed | tf_op | source)
XLA Modules:
  0.0 118.7 jit_solution(4056142529218640544)
XLA Ops:
  0.6 0.5 collective-permute-start.3
  1.2 0.1 collective-permute-start.4
  1.2 0.4 collective-permute-start.5
  1.7 2.2 %pack_rows.1.refs_0_ = bf16[64,4224]{1,0:T(8,128)(2,1)} custom-call(bf16[64,2048]{1,0:T(8,128)(2,1)} %bitcast.30, s32[16,64]{1,0:T(8,128)} %bitcast.32, s32[8,64]{1,0:T(8,128)} %bitcast.33, f32[8,64]{1,0:T(8,128)} %bitcast.34, bf16[64,2048]{1,0:T(8,128)(2,1)} %bitcast.31), custom_call_target="tpu_custom_call" | custom-call | tf_op jit(solution)/shard_map/pack_rows/pallas_call | solution.py:274
  3.9 2.7 %collective-permute-start = (bf16[64,4224]{1,0:T(8,128)(2,1)}, bf16[64,4224]{1,0:T(8,128)(2,1)S(1)}, u32[]{:S(2)}, u32[]{:S(2)}) collective-permute-start(bf16[64,4224]{1,0:T(8,128)(2,1)} %pack_rows.1.refs_0_), channel_id=1, source_target_pairs={{0,2},{2,4},{4,6},{6,7},{7,5},{5,3},{3,1},{1,0},{8,10},{10,12},{12... | collective-permute-start | bytes 1622024 | tf_op jit(solution)/shard_map/ppermute | solution.py:42
  6.5 1.4 %copy-done.1 = bf16[1,2,192,2048]{3,2,1,0:T(8,128)(2,1)S(1)} copy-done((bf16[1,2,192,2048]{3,2,1,0:T(8,128)(2,1)S(1)}, bf16[1,2,192,2048]{3,2,1,0:T(8,128)(2,1)}, u32[]{:S(2)}) %copy-start.1) | copy-done | bytes 1572888
  7.9 0.1 load_weights.2.refs_4_.refs_2_
  8.1 1.3 %copy-done.2 = bf16[1,2,192,2048]{3,2,1,0:T(8,128)(2,1)S(1)} copy-done((bf16[1,2,192,2048]{3,2,1,0:T(8,128)(2,1)S(1)}, bf16[1,2,192,2048]{3,2,1,0:T(8,128)(2,1)}, u32[]{:S(2)}) %copy-start.2) | copy-done | bytes 1572888
  9.3 0.5 copy-done.3
  9.8 0.2 load_weights.3
  10.1 0.8 copy-done
  10.9 0.0 collective-permute-start.1
  10.9 5.0 %collective-permute-done.refs_1_ = bf16[64,4224]{1,0:T(8,128)(2,1)S(1)} collective-permute-done((bf16[64,4224]{1,0:T(8,128)(2,1)}, bf16[64,4224]{1,0:T(8,128)(2,1)S(1)}, u32[]{:S(2)}, u32[]{:S(2)}) %collective-permute-start) | collective-permute-done | bytes 540704 | tf_op jit(solution)/shard_map/ppermute | solution.py:42
  15.8 2.4 %collective-permute-start.2 = (bf16[64,4224]{1,0:T(8,128)(2,1)S(1)}, bf16[64,4224]{1,0:T(8,128)(2,1)S(1)}, u32[]{:S(2)}, u32[]{:S(2)}) collective-permute-start(bf16[64,4224]{1,0:T(8,128)(2,1)S(1)} %collective-permute-done.refs_1_), channel_id=1, source_target_pairs={{0,2},{2,4},{4,6},{6,7},{7,5},{5,3},{3,1},{1,0},{8,10},{10,12},{12... | collective-permute-start | bytes 1622024 | tf_op jit(solution)/shard_map/ppermute | solution.py:42
  18.2 5.4 %collective-permute-done.1.refs_2_ = bf16[64,4224]{1,0:T(8,128)(2,1)S(1)} collective-permute-done((bf16[64,4224]{1,0:T(8,128)(2,1)S(1)}, bf16[64,4224]{1,0:T(8,128)(2,1)S(1)}, u32[]{:S(2)}, u32[]{:S(2)}) %collective-permute-start.1) | collective-permute-done | bytes 540704 | tf_op jit(solution)/shard_map/ppermute | solution.py:42
  23.6 0.0 collective-permute-start.8
  23.6 4.6 %collective-permute-done.2.refs_3_ = bf16[64,4224]{1,0:T(8,128)(2,1)S(1)} collective-permute-done((bf16[64,4224]{1,0:T(8,128)(2,1)S(1)}, bf16[64,4224]{1,0:T(8,128)(2,1)S(1)}, u32[]{:S(2)}, u32[]{:S(2)}) %collective-permute-start.2) | collective-permute-done | bytes 540704 | tf_op jit(solution)/shard_map/ppermute | solution.py:42
  28.2 2.5 %collective-permute-start.6 = (bf16[64,4224]{1,0:T(8,128)(2,1)S(1)}, bf16[64,4224]{1,0:T(8,128)(2,1)S(1)}, u32[]{:S(2)}, u32[]{:S(2)}) collective-permute-start(bf16[64,4224]{1,0:T(8,128)(2,1)S(1)} %collective-permute-done.2.refs_3_), channel_id=1, source_target_pairs={{0,2},{2,4},{4,6},{6,7},{7,5},{5,3},{3,1},{1,0},{8,10},{10,12},{12... | collective-permute-start | bytes 1622024 | tf_op jit(solution)/shard_map/ppermute | solution.py:42
  30.7 6.5 %collective-permute-done.8.refs_0_.refs_4_ = bf16[64,4224]{1,0:T(8,128)(2,1)S(1)} collective-permute-done((bf16[64,4224]{1,0:T(8,128)(2,1)S(1)}, bf16[64,4224]{1,0:T(8,128)(2,1)S(1)}, u32[]{:S(2)}, u32[]{:S(2)}) %collective-permute-start.8) | collective-permute-done | bytes 540704 | tf_op jit(solution)/shard_map/ppermute | solution.py:42
  37.1 0.0 collective-permute-start.9
  37.1 0.0 collective-permute-done.3.refs_7_.refs_5_
  37.1 7.7 %expert_rows.3 = (bf16[64,4096]{1,0:T(8,128)(2,1)S(1)}, bf16[64,4096]{1,0:T(8,128)(2,1)S(1)}, bf16[64,4096]{1,0:T(8,128)(2,1)S(1)}, bf16[64,4096]{1,0:T(8,128)(2...) custom-call(bf16[64,4224]{1,0:T(8,128)(2,1)S(1)} %copy-done, ...), custom_call_target="tpu_custom_call" | custom-call | flops 4831838208 | bytes 13631488 | tf_op jit(solution)/shard_map/expert_rows/pallas_call | solution.py:191
  44.9 0.0 collective-permute-done.6.refs_0_.refs_6_
  44.9 2.1 %collective-permute-start.7 = (bf16[64,4224]{1,0:T(8,128)(2,1)S(1)}, bf16[64,4224]{1,0:T(8,128)(2,1)S(1)}, u32[]{:S(2)}, u32[]{:S(2)}) collective-permute-start(bf16[64,4224]{1,0:T(8,128)(2,1)S(1)} %collective-permute-done.6.refs_0_.refs_6_), channel_id=1, source_target_pairs={{0,2},{2,4},{4,6},{6,7},{7,5},{5,3},{3,1},{1,0},{8,10},{10,12},{12... | collective-permute-start | bytes 1622024 | tf_op jit(solution)/shard_map/ppermute | solution.py:42
  46.9 2.3 %collective-permute-done.9.refs_1_.refs_5_ = bf16[64,4224]{1,0:T(8,128)(2,1)S(1)} collective-permute-done((bf16[64,4224]{1,0:T(8,128)(2,1)S(1)}, bf16[64,4224]{1,0:T(8,128)(2,1)S(1)}, u32[]{:S(2)}, u32[]{:S(2)}) %collective-permute-start.9) | collective-permute-done | bytes 540704 | tf_op jit(solution)/shard_map/ppermute | solution.py:42
  49.2 6.2 %expert_rows.4 = (bf16[64,4096]{1,0:T(8,128)(2,1)S(1)}, bf16[64,4096]{1,0:T(8,128)(2,1)S(1)}, bf16[768,128]{1,0:T(8,128)(2,1)S(1)}, bf16[768,128]{1,0:T(8,128)(2,1)S(1)}, bf16[768,128]{1,0:T(8,128)(2,1)S(1)}) custom-call(bf16[64,4224]{1,0:T(8,128)(2,1)S(1)} %collective-permute-done.8.refs_0_.refs_4_, ...), custom_call_target="tpu_custom_call" | custom-call | flops 2415919104 | bytes 11534336 | tf_op jit(solution)/shard_map/expert_rows/pallas_call | solution.py:191
  55.4 2.0 %collective-permute-start.11 = (bf16[64,4096]{1,0:T(8,128)(2,1)S(1)}, bf16[64,4096]{1,0:T(8,128)(2,1)S(1)}, u32[]{:S(2)}, u32[]{:S(2)}) collective-permute-start(bf16[64,4096]{1,0:T(8,128)(2,1)S(1)} %get-tuple-element.94), channel_id=1, source_target_pairs={{0,2},{2,4},{4,6},{6,7},{7,5},{5,3},{3,1},{1,0},{8,10},{10,12},{12... | collective-permute-start | bytes 1572872 | tf_op jit(solution)/shard_map/ppermute | solution.py:42
  57.4 6.2 %expert_rows.5 = (bf16[64,4096]{1,0:T(8,128)(2,1)S(1)}, bf16[64,4096]{1,0:T(8,128)(2,1)S(1)}, bf16[768,128]{1,0:T(8,128)(2,1)S(1)}, bf16[768,128]{1,0:T(8,128)(2,1)S(1)}, bf16[768,128]{1,0:T(8,128)(2,1)S(1)}) custom-call(bf16[64,4224]{1,0:T(8,128)(2,1)S(1)} %collective-permute-done.6.refs_0_.refs_6_, ...), custom_call_target="tpu_custom_call" | custom-call | flops 2415919104 | bytes 11534336 | tf_op jit(solution)/shard_map/expert_rows/pallas_call | solution.py:191
  63.6 0.2 collective-permute-start.14
  63.8 4.2 %collective-permute-done.11 = bf16[64,4096]{1,0:T(8,128)(2,1)S(1)} collective-permute-done((bf16[64,4096]{1,0:T(8,128)(2,1)S(1)}, bf16[64,4096]{1,0:T(8,128)(2,1)S(1)}, u32[]{:S(2)}, u32[]{:S(2)}) %collective-permute-start.11) | collective-permute-done | bytes 524320 | tf_op jit(solution)/shard_map/ppermute | solution.py:42
  68.0 0.1 add_convert_fusion.5
  68.1 2.1 %collective-permute-start.12 = (bf16[64,4096]{1,0:T(8,128)(2,1)S(1)}, bf16[64,4096]{1,0:T(8,128)(2,1)S(1)}, u32[]{:S(2)}, u32[]{:S(2)}) collective-permute-start(bf16[64,4096]{1,0:T(8,128)(2,1)S(1)} %add_convert_fusion.5), channel_id=1, source_target_pairs={{0,2},{2,4},{4,6},{6,7},{7,5},{5,3},{3,1},{1,0},{8,10},{10,12},{12... | collective-permute-start | bytes 1572872 | tf_op jit(solution)/shard_map/ppermute | solution.py:42
  70.3 0.1 add_convert_fusion.10
  70.4 1.6 %collective-permute-start.10 = (bf16[64,2048]{1,0:T(8,128)(2,1)S(1)}, bf16[64,2048]{1,0:T(8,128)(2,1)S(1)}, u32[]{:S(2)}, u32[]{:S(2)}) collective-permute-start(bf16[64,2048]{1,0:T(8,128)(2,1)S(1)} %get-tuple-element.142), channel_id=1, source_target_pairs={{0,8},{8,0},{1,9},{9,1},{2,10},{10,2},{3,11},{11,3},{4,12},{12,4},... | collective-permute-start | bytes 786440 | tf_op jit(solution)/shard_map/ppermute | solution.py:47
  72.0 0.5 collective-permute-start.16
  72.5 1.7 %collective-permute-done.14 = bf16[64,4096]{1,0:T(8,128)(2,1)S(1)} collective-permute-done((bf16[64,4096]{1,0:T(8,128)(2,1)S(1)}, bf16[64,4096]{1,0:T(8,128)(2,1)S(1)}, u32[]{:S(2)}, u32[]{:S(2)}) %collective-permute-start.14) | collective-permute-done | bytes 524320 | tf_op jit(solution)/shard_map/ppermute | solution.py:42
  74.1 0.1 add_convert_fusion.4
  74.3 0.3 collective-permute-start.15
  74.6 6.9 %collective-permute-done.12 = bf16[64,4096]{1,0:T(8,128)(2,1)S(1)} collective-permute-done((bf16[64,4096]{1,0:T(8,128)(2,1)S(1)}, bf16[64,4096]{1,0:T(8,128)(2,1)S(1)}, u32[]{:S(2)}, u32[]{:S(2)}) %collective-permute-start.12) | collective-permute-done | bytes 524320 | tf_op jit(solution)/shard_map/ppermute | solution.py:42
  81.5 0.1 add_convert_fusion.11
  81.6 3.3 %collective-permute-start.13 = (bf16[64,2048]{1,0:T(8,128)(2,1)S(1)}, bf16[64,2048]{1,0:T(8,128)(2,1)S(1)}, u32[]{:S(2)}, u32[]{:S(2)}) collective-permute-start(bf16[64,2048]{1,0:T(8,128)(2,1)S(1)} %get-tuple-element.146), channel_id=1, source_target_pairs={{0,10},{2,12},{4,14},{6,15},{7,13},{5,11},{3,9},{1,8},{8,2},{10,4}... | collective-permute-start | bytes 786440 | tf_op jit(solution)/shard_map/ppermute | solution.py:42
  84.9 5.9 %weight_grads.1 = (bf16[384,2048]{1,0:T(8,128)(2,1)S(1)}, bf16[384,2048]{1,0:T(8,128)(2,1)S(1)}, bf16[384,2048]{1,0:T(8,128)(2,1)S(1)}, bf16[384,2048]{1,0:T(8,1...) custom-call(bf16[64,4224]{1,0:T(8,128)(2,1)S(1)} %copy-done, ...), custom_call_target="tpu_custom_call" | custom-call | flops 4831838208 | bytes 13631488 | tf_op jit(solution)/shard_map/weight_grads/pallas_call | solution.py:242
  90.8 0.0 collective-permute-done.10
  90.8 0.0 collective-permute-done.16
  90.9 0.0 collective-permute-done.15
  90.9 0.1 add_convert_fusion.3
  91.0 0.1 collective-permute-start.23
  91.1 0.5 collective-permute-start.22
  91.6 0.3 collective-permute-start.17
  91.9 1.6 %collective-permute-start.18 = (bf16[64,2048]{1,0:T(8,128)(2,1)S(1)}, bf16[64,2048]{1,0:T(8,128)(2,1)S(1)}, u32[]{:S(2)}, u32[]{:S(2)}) collective-permute-start(bf16[64,2048]{1,0:T(8,128)(2,1)S(1)} %get-tuple-element.145), channel_id=1, source_target_pairs={{0,10},{2,12},{4,14},{6,15},{7,13},{5,11},{3,9},{1,8},{8,2},{10,4}... | collective-permute-start | bytes 786440 | tf_op jit(solution)/shard_map/ppermute | solution.py:42
  93.5 0.0 collective-permute-start.21
  93.5 8.5 %collective-permute-done.18 = bf16[64,2048]{1,0:T(8,128)(2,1)S(1)} collective-permute-done((bf16[64,2048]{1,0:T(8,128)(2,1)S(1)}, bf16[64,2048]{1,0:T(8,128)(2,1)S(1)}, u32[]{:S(2)}, u32[]{:S(2)}) %collective-permute-start.18) | collective-permute-done | bytes 262176 | tf_op jit(solution)/shard_map/ppermute | solution.py:42
  102.0 1.5 %collective-permute-done.17 = bf16[64,4096]{1,0:T(8,128)(2,1)S(1)} collective-permute-done((bf16[64,4096]{1,0:T(8,128)(2,1)S(1)}, bf16[64,4096]{1,0:T(8,128)(2,1)S(1)}, u32[]{:S(2)}, u32[]{:S(2)}) %collective-permute-start.17) | collective-permute-done | bytes 524320 | tf_op jit(solution)/shard_map/ppermute | solution.py:42
  103.6 0.1 add_convert_fusion.8
  103.7 0.1 collective-permute-start.19
  103.8 1.2 %collective-permute-start.20 = (bf16[64,2048]{1,0:T(8,128)(2,1)S(1)}, bf16[64,2048]{1,0:T(8,128)(2,1)S(1)}, u32[]{:S(2)}, u32[]{:S(2)}) collective-permute-start(bf16[64,2048]{1,0:T(8,128)(2,1)S(1)} %get-tuple-element.143), channel_id=1, source_target_pairs={{0,9},{2,8},{4,10},{6,12},{7,14},{5,15},{3,13},{1,11},{8,1},{10,0}... | collective-permute-start | bytes 786440 | tf_op jit(solution)/shard_map/ppermute | solution.py:42
  105.0 0.0 collective-permute-done.23
  105.0 1.8 %add_convert_fusion = bf16[384,2048]{1,0:T(8,128)(2,1)} fusion(bf16[384,2048]{1,0:T(8,128)(2,1)S(1)} %collective-permute-done.23, bf16[384,2048]{1,0:T(8,128)(2,1)S(1)} %get-tuple-element.130), kind=kLoop, calls=%fused_computation | loop fusion | flops 3145728 | bytes 4718592 | tf_op jit(solution)/shard_map/convert_element_type | solution.py:260
  106.8 0.0 collective-permute-done.22
  106.8 1.7 %add_convert_fusion.1 = bf16[384,2048]{1,0:T(8,128)(2,1)} fusion(bf16[384,2048]{1,0:T(8,128)(2,1)S(1)} %collective-permute-done.22, bf16[384,2048]{1,0:T(8,128)(2,1)S(1)} %get-tuple-element.128), kind=kLoop, calls=%fused_computation.1 | loop fusion | flops 3145728 | bytes 4718592 | tf_op jit(solution)/shard_map/convert_element_type | solution.py:260
  108.5 1.8 %add_convert_fusion.2 = bf16[384,2048]{1,0:T(8,128)(2,1)} fusion(bf16[384,2048]{1,0:T(8,128)(2,1)S(1)} %collective-permute-done.21, bf16[384,2048]{1,0:T(8,128)(2,1)S(1)} %get-tuple-element.126), kind=kLoop, calls=%fused_computation.2 | loop fusion | flops 3145728 | bytes 4718592 | tf_op jit(solution)/shard_map/convert_element_type | solution.py:260
  110.4 3.5 %collective-permute-done.19 = bf16[64,2048]{1,0:T(8,128)(2,1)S(1)} collective-permute-done((bf16[64,2048]{1,0:T(8,128)(2,1)S(1)}, bf16[64,2048]{1,0:T(8,128)(2,1)S(1)}, u32[]{:S(2)}, u32[]{:S(2)}) %collective-permute-start.19) | collective-permute-done | bytes 262176 | tf_op jit(solution)/shard_map/ppermute | solution.py:42
  113.8 3.9 %collective-permute-done.20 = bf16[64,2048]{1,0:T(8,128)(2,1)S(1)} collective-permute-done((bf16[64,2048]{1,0:T(8,128)(2,1)S(1)}, bf16[64,2048]{1,0:T(8,128)(2,1)S(1)}, u32[]{:S(2)}, u32[]{:S(2)}) %collective-permute-start.20) | collective-permute-done | bytes 262176 | tf_op jit(solution)/shard_map/ppermute | solution.py:42
  117.7 1.0 fusion
  (9 shorter events, 0.0 us)
Async XLA Ops:
  0.6 36.5 %collective-permute-start.3 = (bf16[384,2048]{1,0:T(8,128)(2,1)}, bf16[384,2048]{1,0:T(8,128)(2,1)S(1)}, u32[]{:S(2)}, u32[]{:S(2)}) collective-permute-start(bf16[384,2048]{1,0:T(8,128)(2,1)} %bitcast.21), channel_id=1, source_target_pairs={{0,16},{16,0},{1,17},{17,1},{2,18},{18,2},{3,19},{19,3},{4,20},{20... | collective-permute-start | bytes 4718600 | tf_op jit(solution)/shard_map/ppermute | solution.py:47
  1.2 36.0 %collective-permute-start.4 = (bf16[384,2048]{1,0:T(8,128)(2,1)}, bf16[384,2048]{1,0:T(8,128)(2,1)S(1)}, u32[]{:S(2)}, u32[]{:S(2)}) collective-permute-start(bf16[384,2048]{1,0:T(8,128)(2,1)} %bitcast.23), channel_id=1, source_target_pairs={{0,16},{16,0},{1,17},{17,1},{2,18},{18,2},{3,19},{19,3},{4,20},{20... | collective-permute-start | bytes 4718600 | tf_op jit(solution)/shard_map/ppermute | solution.py:47
  1.2 35.9 %collective-permute-start.5 = (bf16[384,2048]{1,0:T(8,128)(2,1)}, bf16[384,2048]{1,0:T(8,128)(2,1)}, u32[]{:S(2)}, u32[]{:S(2)}) collective-permute-start(bf16[384,2048]{1,0:T(8,128)(2,1)} %bitcast.25), channel_id=1, source_target_pairs={{0,16},{16,0},{1,17},{17,1},{2,18},{18,2},{3,19},{19,3},{4,20},{20... | collective-permute-start | bytes 4718600 | tf_op jit(solution)/shard_map/ppermute | solution.py:47
  3.9 12.0 %collective-permute-start = (bf16[64,4224]{1,0:T(8,128)(2,1)}, bf16[64,4224]{1,0:T(8,128)(2,1)S(1)}, u32[]{:S(2)}, u32[]{:S(2)}) collective-permute-start(bf16[64,4224]{1,0:T(8,128)(2,1)} %pack_rows.1.refs_0_), channel_id=1, source_target_pairs={{0,2},{2,4},{4,6},{6,7},{7,5},{5,3},{3,1},{1,0},{8,10},{10,12},{12... | collective-permute-start | bytes 1622024 | tf_op jit(solution)/shard_map/ppermute | solution.py:42
  6.5 1.4 %copy-start.1 = (bf16[1,2,192,2048]{3,2,1,0:T(8,128)(2,1)S(1)}, bf16[1,2,192,2048]{3,2,1,0:T(8,128)(2,1)}, u32[]{:S(2)}) copy-start(bf16[1,2,192,2048]{3,2,1,0:T(8,128)(2,1)} %param.13) | copy-start | bytes 4718596
  7.9 1.4 %copy-start.2 = (bf16[1,2,192,2048]{3,2,1,0:T(8,128)(2,1)S(1)}, bf16[1,2,192,2048]{3,2,1,0:T(8,128)(2,1)}, u32[]{:S(2)}) copy-start(bf16[1,2,192,2048]{3,2,1,0:T(8,128)(2,1)} %param.14) | copy-start | bytes 4718596
  7.9 1.9 %copy-start.3 = (bf16[1,2,192,2048]{3,2,1,0:T(8,128)(2,1)S(1)}, bf16[1,2,192,2048]{3,2,1,0:T(8,128)(2,1)}, u32[]{:S(2)}) copy-start(bf16[1,2,192,2048]{3,2,1,0:T(8,128)(2,1)} %param.15) | copy-start | bytes 4718596
  9.8 1.0 copy-start
  10.9 12.7 %collective-permute-start.1 = (bf16[64,4224]{1,0:T(8,128)(2,1)S(1)}, bf16[64,4224]{1,0:T(8,128)(2,1)S(1)}, u32[]{:S(2)}, u32[]{:S(2)}) collective-permute-start(bf16[64,4224]{1,0:T(8,128)(2,1)S(1)} %copy-done), channel_id=1, source_target_pairs={{0,1},{2,0},{4,2},{6,4},{7,6},{5,7},{3,5},{1,3},{8,9},{10,8},{12,1... | collective-permute-start | bytes 1622024 | tf_op jit(solution)/shard_map/ppermute | solution.py:42
  15.8 12.3 %collective-permute-start.2 = (bf16[64,4224]{1,0:T(8,128)(2,1)S(1)}, bf16[64,4224]{1,0:T(8,128)(2,1)S(1)}, u32[]{:S(2)}, u32[]{:S(2)}) collective-permute-start(bf16[64,4224]{1,0:T(8,128)(2,1)S(1)} %collective-permute-done.refs_1_), channel_id=1, source_target_pairs={{0,2},{2,4},{4,6},{6,7},{7,5},{5,3},{3,1},{1,0},{8,10},{10,12},{12... | collective-permute-start | bytes 1622024 | tf_op jit(solution)/shard_map/ppermute | solution.py:42
  23.6 13.5 %collective-permute-start.8 = (bf16[64,4224]{1,0:T(8,128)(2,1)S(1)}, bf16[64,4224]{1,0:T(8,128)(2,1)S(1)}, u32[]{:S(2)}, u32[]{:S(2)}) collective-permute-start(bf16[64,4224]{1,0:T(8,128)(2,1)S(1)} %collective-permute-done.1.refs_2_), channel_id=1, source_target_pairs={{0,1},{2,0},{4,2},{6,4},{7,6},{5,7},{3,5},{1,3},{8,9},{10,8},{12,1... | collective-permute-start | bytes 1622024 | tf_op jit(solution)/shard_map/ppermute | solution.py:42
  28.2 16.7 %collective-permute-start.6 = (bf16[64,4224]{1,0:T(8,128)(2,1)S(1)}, bf16[64,4224]{1,0:T(8,128)(2,1)S(1)}, u32[]{:S(2)}, u32[]{:S(2)}) collective-permute-start(bf16[64,4224]{1,0:T(8,128)(2,1)S(1)} %collective-permute-done.2.refs_3_), channel_id=1, source_target_pairs={{0,2},{2,4},{4,6},{6,7},{7,5},{5,3},{3,1},{1,0},{8,10},{10,12},{12... | collective-permute-start | bytes 1622024 | tf_op jit(solution)/shard_map/ppermute | solution.py:42
  37.1 12.1 %collective-permute-start.9 = (bf16[64,4224]{1,0:T(8,128)(2,1)S(1)}, bf16[64,4224]{1,0:T(8,128)(2,1)S(1)}, u32[]{:S(2)}, u32[]{:S(2)}) collective-permute-start(bf16[64,4224]{1,0:T(8,128)(2,1)S(1)} %collective-permute-done.8.refs_0_.refs_4_), channel_id=1, source_target_pairs={{0,1},{2,0},{4,2},{6,4},{7,6},{5,7},{3,5},{1,3},{8,9},{10,8},{12,1... | collective-permute-start | bytes 1622024 | tf_op jit(solution)/shard_map/ppermute | solution.py:42
  44.9 12.5 %collective-permute-start.7 = (bf16[64,4224]{1,0:T(8,128)(2,1)S(1)}, bf16[64,4224]{1,0:T(8,128)(2,1)S(1)}, u32[]{:S(2)}, u32[]{:S(2)}) collective-permute-start(bf16[64,4224]{1,0:T(8,128)(2,1)S(1)} %collective-permute-done.6.refs_0_.refs_6_), channel_id=1, source_target_pairs={{0,2},{2,4},{4,6},{6,7},{7,5},{5,3},{3,1},{1,0},{8,10},{10,12},{12... | collective-permute-start | bytes 1622024 | tf_op jit(solution)/shard_map/ppermute | solution.py:42
  55.4 12.6 %collective-permute-start.11 = (bf16[64,4096]{1,0:T(8,128)(2,1)S(1)}, bf16[64,4096]{1,0:T(8,128)(2,1)S(1)}, u32[]{:S(2)}, u32[]{:S(2)}) collective-permute-start(bf16[64,4096]{1,0:T(8,128)(2,1)S(1)} %get-tuple-element.94), channel_id=1, source_target_pairs={{0,2},{2,4},{4,6},{6,7},{7,5},{5,3},{3,1},{1,0},{8,10},{10,12},{12... | collective-permute-start | bytes 1572872 | tf_op jit(solution)/shard_map/ppermute | solution.py:42
  63.6 10.5 %collective-permute-start.14 = (bf16[64,4096]{1,0:T(8,128)(2,1)S(1)}, bf16[64,4096]{1,0:T(8,128)(2,1)S(1)}, u32[]{:S(2)}, u32[]{:S(2)}) collective-permute-start(bf16[64,4096]{1,0:T(8,128)(2,1)S(1)} %get-tuple-element.97), channel_id=1, source_target_pairs={{0,1},{2,0},{4,2},{6,4},{7,6},{5,7},{3,5},{1,3},{8,9},{10,8},{12,1... | collective-permute-start | bytes 1572872 | tf_op jit(solution)/shard_map/ppermute | solution.py:42
  68.1 13.4 %collective-permute-start.12 = (bf16[64,4096]{1,0:T(8,128)(2,1)S(1)}, bf16[64,4096]{1,0:T(8,128)(2,1)S(1)}, u32[]{:S(2)}, u32[]{:S(2)}) collective-permute-start(bf16[64,4096]{1,0:T(8,128)(2,1)S(1)} %add_convert_fusion.5), channel_id=1, source_target_pairs={{0,2},{2,4},{4,6},{6,7},{7,5},{5,3},{3,1},{1,0},{8,10},{10,12},{12... | collective-permute-start | bytes 1572872 | tf_op jit(solution)/shard_map/ppermute | solution.py:42
  70.4 20.4 %collective-permute-start.10 = (bf16[64,2048]{1,0:T(8,128)(2,1)S(1)}, bf16[64,2048]{1,0:T(8,128)(2,1)S(1)}, u32[]{:S(2)}, u32[]{:S(2)}) collective-permute-start(bf16[64,2048]{1,0:T(8,128)(2,1)S(1)} %get-tuple-element.142), channel_id=1, source_target_pairs={{0,8},{8,0},{1,9},{9,1},{2,10},{10,2},{3,11},{11,3},{4,12},{12,4},... | collective-permute-start | bytes 786440 | tf_op jit(solution)/shard_map/ppermute | solution.py:47
  72.0 18.8 %collective-permute-start.16 = (bf16[64,2048]{1,0:T(8,128)(2,1)S(1)}, bf16[64,2048]{1,0:T(8,128)(2,1)S(1)}, u32[]{:S(2)}, u32[]{:S(2)}) collective-permute-start(bf16[64,2048]{1,0:T(8,128)(2,1)S(1)} %get-tuple-element.141), channel_id=1, source_target_pairs={{0,8},{8,0},{1,9},{9,1},{2,10},{10,2},{3,11},{11,3},{4,12},{12,4},... | collective-permute-start | bytes 786440 | tf_op jit(solution)/shard_map/ppermute | solution.py:47
  74.3 16.6 %collective-permute-start.15 = (bf16[64,4096]{1,0:T(8,128)(2,1)S(1)}, bf16[64,4096]{1,0:T(8,128)(2,1)S(1)}, u32[]{:S(2)}, u32[]{:S(2)}) collective-permute-start(bf16[64,4096]{1,0:T(8,128)(2,1)S(1)} %add_convert_fusion.4), channel_id=1, source_target_pairs={{0,1},{2,0},{4,2},{6,4},{7,6},{5,7},{3,5},{1,3},{8,9},{10,8},{12,1... | collective-permute-start | bytes 1572872 | tf_op jit(solution)/shard_map/ppermute | solution.py:42
  81.6 9.2 %collective-permute-start.13 = (bf16[64,2048]{1,0:T(8,128)(2,1)S(1)}, bf16[64,2048]{1,0:T(8,128)(2,1)S(1)}, u32[]{:S(2)}, u32[]{:S(2)}) collective-permute-start(bf16[64,2048]{1,0:T(8,128)(2,1)S(1)} %get-tuple-element.146), channel_id=1, source_target_pairs={{0,10},{2,12},{4,14},{6,15},{7,13},{5,11},{3,9},{1,8},{8,2},{10,4}... | collective-permute-start | bytes 786440 | tf_op jit(solution)/shard_map/ppermute | solution.py:42
  91.0 14.0 %collective-permute-start.23 = (bf16[384,2048]{1,0:T(8,128)(2,1)S(1)}, bf16[384,2048]{1,0:T(8,128)(2,1)S(1)}, u32[]{:S(2)}, u32[]{:S(2)}) collective-permute-start(bf16[384,2048]{1,0:T(8,128)(2,1)S(1)} %get-tuple-element.131), channel_id=1, source_target_pairs={{0,16},{16,0},{1,17},{17,1},{2,18},{18,2},{3,19},{19,3},{4,20},{20... | collective-permute-start | bytes 4718600 | tf_op jit(solution)/shard_map/ppermute | solution.py:47
  91.1 15.7 %collective-permute-start.22 = (bf16[384,2048]{1,0:T(8,128)(2,1)S(1)}, bf16[384,2048]{1,0:T(8,128)(2,1)S(1)}, u32[]{:S(2)}, u32[]{:S(2)}) collective-permute-start(bf16[384,2048]{1,0:T(8,128)(2,1)S(1)} %get-tuple-element.129), channel_id=1, source_target_pairs={{0,16},{16,0},{1,17},{17,1},{2,18},{18,2},{3,19},{19,3},{4,20},{20... | collective-permute-start | bytes 4718600 | tf_op jit(solution)/shard_map/ppermute | solution.py:47
  91.6 12.0 %collective-permute-start.17 = (bf16[64,4096]{1,0:T(8,128)(2,1)S(1)}, bf16[64,4096]{1,0:T(8,128)(2,1)S(1)}, u32[]{:S(2)}, u32[]{:S(2)}) collective-permute-start(bf16[64,4096]{1,0:T(8,128)(2,1)S(1)} %add_convert_fusion.3), channel_id=1, source_target_pairs={{0,1},{2,0},{4,2},{6,4},{7,6},{5,7},{3,5},{1,3},{8,9},{10,8},{12,1... | collective-permute-start | bytes 1572872 | tf_op jit(solution)/shard_map/ppermute | solution.py:42
  91.9 10.1 %collective-permute-start.18 = (bf16[64,2048]{1,0:T(8,128)(2,1)S(1)}, bf16[64,2048]{1,0:T(8,128)(2,1)S(1)}, u32[]{:S(2)}, u32[]{:S(2)}) collective-permute-start(bf16[64,2048]{1,0:T(8,128)(2,1)S(1)} %get-tuple-element.145), channel_id=1, source_target_pairs={{0,10},{2,12},{4,14},{6,15},{7,13},{5,11},{3,9},{1,8},{8,2},{10,4}... | collective-permute-start | bytes 786440 | tf_op jit(solution)/shard_map/ppermute | solution.py:42
  93.5 15.0 %collective-permute-start.21 = (bf16[384,2048]{1,0:T(8,128)(2,1)S(1)}, bf16[384,2048]{1,0:T(8,128)(2,1)S(1)}, u32[]{:S(2)}, u32[]{:S(2)}) collective-permute-start(bf16[384,2048]{1,0:T(8,128)(2,1)S(1)} %get-tuple-element.127), channel_id=1, source_target_pairs={{0,16},{16,0},{1,17},{17,1},{2,18},{18,2},{3,19},{19,3},{4,20},{20... | collective-permute-start | bytes 4718600 | tf_op jit(solution)/shard_map/ppermute | solution.py:47
  103.7 10.1 %collective-permute-start.19 = (bf16[64,2048]{1,0:T(8,128)(2,1)S(1)}, bf16[64,2048]{1,0:T(8,128)(2,1)S(1)}, u32[]{:S(2)}, u32[]{:S(2)}) collective-permute-start(bf16[64,2048]{1,0:T(8,128)(2,1)S(1)} %get-tuple-element.144), channel_id=1, source_target_pairs={{0,9},{2,8},{4,10},{6,12},{7,14},{5,15},{3,13},{1,11},{8,1},{10,0}... | collective-permute-start | bytes 786440 | tf_op jit(solution)/shard_map/ppermute | solution.py:42
  103.8 13.9 %collective-permute-start.20 = (bf16[64,2048]{1,0:T(8,128)(2,1)S(1)}, bf16[64,2048]{1,0:T(8,128)(2,1)S(1)}, u32[]{:S(2)}, u32[]{:S(2)}) collective-permute-start(bf16[64,2048]{1,0:T(8,128)(2,1)S(1)} %get-tuple-element.143), channel_id=1, source_target_pairs={{0,9},{2,8},{4,10},{6,12},{7,14},{5,15},{3,13},{1,11},{8,1},{10,0}... | collective-permute-start | bytes 786440 | tf_op jit(solution)/shard_map/ppermute | solution.py:42

commit v10 on v8

--- a/solution.py
+++ b/solution.py
@@ -290,8 +290,7 @@
         names += [("near", k), ("far", k)]
     names = names[: 2 * ahead]
     groups = [names[i : i + 4] for i in range(0, len(names) - 4, 4)]
-    groups.append([name for name in names[-4:] if name[0] == "far"])
-    groups.append([name for name in names[-4:] if name[0] == "near"])
+    groups += [names[-4:-2], names[-2:]]
     held = {("near", 0): home, ("far", 0): tie((home, own))[0]}
     partial, kept = {}, []
 
@@ -304,18 +303,20 @@
 
     for k in range(1, ahead + 1):
         held["near", k] = ring_shift(held["near", k - 1], 1)
-        if k <= behind:
-            held["far", k] = ring_shift(held["far", k - 1], -1)
         if k == 1:
             held["near", 1], own = tie((held["near", 1], own))
             weights[:3] = own
         if k % 2 == 1 and k > 1:
             work(groups[(k - 3) // 2])
-            held["near", k], kept[-1] = tie((held["near", k], kept[-1]))
+            held["far", k - 1], kept[-1] = tie((held["far", k - 1], kept[-1]))
+        if k <= behind:
+            held["far", k] = ring_shift(held["far", k - 1], -1)
     work(groups[-2])
+    arrived = [held[name] for name in groups[-1]]
+    arrived, kept[-1] = tie((arrived, kept[-1]))
+    held.update(zip(groups[-1], arrived))
+    work(groups[-1])
     far_sum = ring_shift(partial["far", behind], 1)
-    held["near", ahead], kept[-1] = tie((held["near", ahead], kept[-1]))
-    work(groups[-1])
     both = (slice(0, width), slice(width, 2 * width))
     near_sum = partial["near", ahead]
     own_total = received = None

time: 116 us -> 122 us (1.052)
  waiting for transfers between devices: 50.3 us -> 57 us
    ppermute x8, waiting for transfers between devices: 0.6 us -> 7.36 us  [from_behind(): lax.ppermute(value, axis, [(i, (i + by) % peers) for i in range(peers)])]
  transfers between devices with their start and end apart: 24 -> 24, of which waited for: 15 -> 15; matrix products, arithmetic and copies ran while one was open for 5% -> 5% of each run, Pallas kernels for 25% -> 18%
where the time goes in v10:
time: 122 us
  waiting for transfers between devices  57 us (47%)
  Pallas kernels  28.5 us (23%)
  starting transfers between devices  24.6 us (20%)
  other arithmetic  7.09 us (6%)
  local copies, waits for them, and re-layouts  3.97 us (3%)
    ppermute x16, waiting for transfers between devices, ring_shift(): return lax.ppermute(value, ('rep', 'section', 'exp'), pairs)  49.7 us
    ppermute x16, starting transfers between devices, ring_shift(): return lax.ppermute(value, ('rep', 'section', 'exp'), pairs)  21 us
    pallas_call x3, Pallas kernels, expert_call(): pl.pallas_call(functools.partial(expert_kernel, count, experts, local_exp...  20.1 us
    ppermute x8, waiting for transfers between devices, from_behind(): lax.ppermute(value, axis, [(i, (i + by) % peers) for i in range(peers)])  7.36 us
    convert_element_type x9, other arithmetic, add(): return (a.astype(F32) + b.astype(F32)).astype(BF16)  6.05 us
    pallas_call x1, Pallas kernels, weight_call(): pl.pallas_call(functools.partial(weight_kernel, len(kept), count), out_sh...  5.88 us
    unnamed x8, local copies, waits for them, and re-layouts  3.97 us
    ppermute x8, starting transfers between devices, from_behind(): lax.ppermute(value, axis, [(i, (i + by) % peers) for i in range(peers)])  3.63 us
  transfers between devices with their start and end apart: 24, of which 15 were waited for; matrix products, arithmetic and copies ran while one was open for 5% of the time, Pallas kernels for 18%

profile of v10, /device:TPU:0, one launch (start us, length us, event | category | flops | bytes accessed | tf_op | source)
XLA Modules:
  0.0 122.1 jit_solution(10677830271667631298)
XLA Ops:
  0.6 0.5 collective-permute-start.3
  1.2 0.1 collective-permute-start.4
  1.2 0.4 collective-permute-start.5
  1.7 2.2 %pack_rows.1.refs_0_ = bf16[64,4224]{1,0:T(8,128)(2,1)} custom-call(bf16[64,2048]{1,0:T(8,128)(2,1)} %bitcast.30, s32[16,64]{1,0:T(8,128)} %bitcast.32, s32[8,64]{1,0:T(8,128)} %bitcast.33, f32[8,64]{1,0:T(8,128)} %bitcast.34, bf16[64,2048]{1,0:T(8,128)(2,1)} %bitcast.31), custom_call_target="tpu_custom_call" | custom-call | tf_op jit(solution)/shard_map/pack_rows/pallas_call | solution.py:274
  3.9 2.7 %collective-permute-start = (bf16[64,4224]{1,0:T(8,128)(2,1)}, bf16[64,4224]{1,0:T(8,128)(2,1)S(1)}, u32[]{:S(2)}, u32[]{:S(2)}) collective-permute-start(bf16[64,4224]{1,0:T(8,128)(2,1)} %pack_rows.1.refs_0_), channel_id=1, source_target_pairs={{0,2},{2,4},{4,6},{6,7},{7,5},{5,3},{3,1},{1,0},{8,10},{10,12},{12... | collective-permute-start | bytes 1622024 | tf_op jit(solution)/shard_map/ppermute | solution.py:42
  6.5 1.4 %copy-done.1 = bf16[1,2,192,2048]{3,2,1,0:T(8,128)(2,1)S(1)} copy-done((bf16[1,2,192,2048]{3,2,1,0:T(8,128)(2,1)S(1)}, bf16[1,2,192,2048]{3,2,1,0:T(8,128)(2,1)}, u32[]{:S(2)}) %copy-start.1) | copy-done | bytes 1572888
  7.9 0.1 load_weights.2.refs_4_.refs_2_
  8.1 1.3 %copy-done.2 = bf16[1,2,192,2048]{3,2,1,0:T(8,128)(2,1)S(1)} copy-done((bf16[1,2,192,2048]{3,2,1,0:T(8,128)(2,1)S(1)}, bf16[1,2,192,2048]{3,2,1,0:T(8,128)(2,1)}, u32[]{:S(2)}) %copy-start.2) | copy-done | bytes 1572888
  9.3 0.5 copy-done.3
  9.8 0.2 load_weights.3
  10.1 0.8 copy-done
  10.9 0.0 collective-permute-start.1
  10.9 5.0 %collective-permute-done.refs_1_ = bf16[64,4224]{1,0:T(8,128)(2,1)S(1)} collective-permute-done((bf16[64,4224]{1,0:T(8,128)(2,1)}, bf16[64,4224]{1,0:T(8,128)(2,1)S(1)}, u32[]{:S(2)}, u32[]{:S(2)}) %collective-permute-start) | collective-permute-done | bytes 540704 | tf_op jit(solution)/shard_map/ppermute | solution.py:42
  15.8 2.4 %collective-permute-start.2 = (bf16[64,4224]{1,0:T(8,128)(2,1)S(1)}, bf16[64,4224]{1,0:T(8,128)(2,1)S(1)}, u32[]{:S(2)}, u32[]{:S(2)}) collective-permute-start(bf16[64,4224]{1,0:T(8,128)(2,1)S(1)} %collective-permute-done.refs_1_), channel_id=1, source_target_pairs={{0,2},{2,4},{4,6},{6,7},{7,5},{5,3},{3,1},{1,0},{8,10},{10,12},{12... | collective-permute-start | bytes 1622024 | tf_op jit(solution)/shard_map/ppermute | solution.py:42
  18.2 5.4 %collective-permute-done.1.refs_2_ = bf16[64,4224]{1,0:T(8,128)(2,1)S(1)} collective-permute-done((bf16[64,4224]{1,0:T(8,128)(2,1)S(1)}, bf16[64,4224]{1,0:T(8,128)(2,1)S(1)}, u32[]{:S(2)}, u32[]{:S(2)}) %collective-permute-start.1) | collective-permute-done | bytes 540704 | tf_op jit(solution)/shard_map/ppermute | solution.py:42
  23.6 0.0 collective-permute-start.6
  23.6 4.6 %collective-permute-done.2.refs_3_ = bf16[64,4224]{1,0:T(8,128)(2,1)S(1)} collective-permute-done((bf16[64,4224]{1,0:T(8,128)(2,1)S(1)}, bf16[64,4224]{1,0:T(8,128)(2,1)S(1)}, u32[]{:S(2)}, u32[]{:S(2)}) %collective-permute-start.2) | collective-permute-done | bytes 540704 | tf_op jit(solution)/shard_map/ppermute | solution.py:42
  28.2 2.5 %collective-permute-start.8 = (bf16[64,4224]{1,0:T(8,128)(2,1)S(1)}, bf16[64,4224]{1,0:T(8,128)(2,1)S(1)}, u32[]{:S(2)}, u32[]{:S(2)}) collective-permute-start(bf16[64,4224]{1,0:T(8,128)(2,1)S(1)} %collective-permute-done.2.refs_3_), channel_id=1, source_target_pairs={{0,2},{2,4},{4,6},{6,7},{7,5},{5,3},{3,1},{1,0},{8,10},{10,12},{12... | collective-permute-start | bytes 1622024 | tf_op jit(solution)/shard_map/ppermute | solution.py:42
  30.7 0.0 collective-permute-done.3.refs_7_.refs_5_
  30.7 0.0 collective-permute-done.4.refs_8_.refs_6_
  30.7 7.7 %expert_rows.3 = (bf16[64,4096]{1,0:T(8,128)(2,1)S(1)}, bf16[64,4096]{1,0:T(8,128)(2,1)S(1)}, bf16[64,4096]{1,0:T(8,128)(2,1)S(1)}, bf16[64,4096]{1,0:T(8,128)(2...) custom-call(bf16[64,4224]{1,0:T(8,128)(2,1)S(1)} %copy-done, ...), custom_call_target="tpu_custom_call" | custom-call | flops 4831838208 | bytes 13631488 | tf_op jit(solution)/shard_map/expert_rows/pallas_call | solution.py:191
  38.4 0.0 collective-permute-done.6.refs_0_.refs_4_
  38.4 0.1 collective-permute-start.7
  38.5 0.8 collective-permute-done.8.refs_1_.refs_5_
  39.2 2.5 %collective-permute-start.9 = (bf16[64,4224]{1,0:T(8,128)(2,1)S(1)}, bf16[64,4224]{1,0:T(8,128)(2,1)S(1)}, u32[]{:S(2)}, u32[]{:S(2)}) collective-permute-start(bf16[64,4224]{1,0:T(8,128)(2,1)S(1)} %collective-permute-done.8.refs_1_.refs_5_), channel_id=1, source_target_pairs={{0,2},{2,4},{4,6},{6,7},{7,5},{5,3},{3,1},{1,0},{8,10},{10,12},{12... | collective-permute-start | bytes 1622024 | tf_op jit(solution)/shard_map/ppermute | solution.py:42
  41.7 6.2 %expert_rows.4 = (bf16[64,4096]{1,0:T(8,128)(2,1)S(1)}, bf16[64,4096]{1,0:T(8,128)(2,1)S(1)}, bf16[768,128]{1,0:T(8,128)(2,1)S(1)}, bf16[768,128]{1,0:T(8,128)(2,1)S(1)}, bf16[768,128]{1,0:T(8,128)(2,1)S(1)}) custom-call(bf16[64,4224]{1,0:T(8,128)(2,1)S(1)} %collective-permute-done.6.refs_0_.refs_4_, ...), custom_call_target="tpu_custom_call" | custom-call | flops 2415919104 | bytes 11534336 | tf_op jit(solution)/shard_map/expert_rows/pallas_call | solution.py:191
  47.9 5.0 %collective-permute-done.7.refs_0_.refs_6_ = bf16[64,4224]{1,0:T(8,128)(2,1)S(1)} collective-permute-done((bf16[64,4224]{1,0:T(8,128)(2,1)S(1)}, bf16[64,4224]{1,0:T(8,128)(2,1)S(1)}, u32[]{:S(2)}, u32[]{:S(2)}) %collective-permute-start.7) | collective-permute-done | bytes 540704 | tf_op jit(solution)/shard_map/ppermute | solution.py:42
  53.0 6.2 %expert_rows.5 = (bf16[64,4096]{1,0:T(8,128)(2,1)S(1)}, bf16[64,4096]{1,0:T(8,128)(2,1)S(1)}, bf16[768,128]{1,0:T(8,128)(2,1)S(1)}, bf16[768,128]{1,0:T(8,128)(2,1)S(1)}, bf16[768,128]{1,0:T(8,128)(2,1)S(1)}) custom-call(bf16[64,4224]{1,0:T(8,128)(2,1)S(1)} %collective-permute-done.7.refs_0_.refs_6_, ...), custom_call_target="tpu_custom_call" | custom-call | flops 2415919104 | bytes 11534336 | tf_op jit(solution)/shard_map/expert_rows/pallas_call | solution.py:191
  59.2 0.1 collective-permute-start.14
  59.3 1.9 %collective-permute-start.11 = (bf16[64,4096]{1,0:T(8,128)(2,1)S(1)}, bf16[64,4096]{1,0:T(8,128)(2,1)S(1)}, u32[]{:S(2)}, u32[]{:S(2)}) collective-permute-start(bf16[64,4096]{1,0:T(8,128)(2,1)S(1)} %get-tuple-element.93), channel_id=1, source_target_pairs={{0,2},{2,4},{4,6},{6,7},{7,5},{5,3},{3,1},{1,0},{8,10},{10,12},{12... | collective-permute-start | bytes 1572872 | tf_op jit(solution)/shard_map/ppermute | solution.py:42
  61.3 12.5 %collective-permute-done.14 = bf16[64,4096]{1,0:T(8,128)(2,1)S(1)} collective-permute-done((bf16[64,4096]{1,0:T(8,128)(2,1)S(1)}, bf16[64,4096]{1,0:T(8,128)(2,1)S(1)}, u32[]{:S(2)}, u32[]{:S(2)}) %collective-permute-start.14) | collective-permute-done | bytes 524320 | tf_op jit(solution)/shard_map/ppermute | solution.py:42
  73.7 0.1 add_convert_fusion.4
  73.9 0.1 collective-permute-start.15
  73.9 0.1 add_convert_fusion.5
  74.1 2.1 %collective-permute-start.12 = (bf16[64,4096]{1,0:T(8,128)(2,1)S(1)}, bf16[64,4096]{1,0:T(8,128)(2,1)S(1)}, u32[]{:S(2)}, u32[]{:S(2)}) collective-permute-start(bf16[64,4096]{1,0:T(8,128)(2,1)S(1)} %add_convert_fusion.5), channel_id=1, source_target_pairs={{0,2},{2,4},{4,6},{6,7},{7,5},{5,3},{3,1},{1,0},{8,10},{10,12},{12... | collective-permute-start | bytes 1572872 | tf_op jit(solution)/shard_map/ppermute | solution.py:42
  76.1 0.1 add_convert_fusion.11
  76.3 1.6 %collective-permute-start.16 = (bf16[64,2048]{1,0:T(8,128)(2,1)S(1)}, bf16[64,2048]{1,0:T(8,128)(2,1)S(1)}, u32[]{:S(2)}, u32[]{:S(2)}) collective-permute-start(bf16[64,2048]{1,0:T(8,128)(2,1)S(1)} %get-tuple-element.137), channel_id=1, source_target_pairs={{0,8},{8,0},{1,9},{9,1},{2,10},{10,2},{3,11},{11,3},{4,12},{12,4},... | collective-permute-start | bytes 786440 | tf_op jit(solution)/shard_map/ppermute | solution.py:47
  77.9 0.5 collective-permute-start.10
  78.3 5.9 %weight_grads.1 = (bf16[384,2048]{1,0:T(8,128)(2,1)S(1)}, bf16[384,2048]{1,0:T(8,128)(2,1)S(1)}, bf16[384,2048]{1,0:T(8,128)(2,1)S(1)}, bf16[384,2048]{1,0:T(8,1...) custom-call(bf16[64,4224]{1,0:T(8,128)(2,1)S(1)} %copy-done, ...), custom_call_target="tpu_custom_call" | custom-call | flops 4831838208 | bytes 13631488 | tf_op jit(solution)/shard_map/weight_grads/pallas_call | solution.py:242
  84.2 1.3 %collective-permute-done.16 = bf16[64,2048]{1,0:T(8,128)(2,1)S(1)} collective-permute-done((bf16[64,2048]{1,0:T(8,128)(2,1)S(1)}, bf16[64,2048]{1,0:T(8,128)(2,1)S(1)}, u32[]{:S(2)}, u32[]{:S(2)}) %collective-permute-start.16) | collective-permute-done | bytes 262176 | tf_op jit(solution)/shard_map/ppermute | solution.py:47
  85.5 4.3 %collective-permute-done.10 = bf16[64,2048]{1,0:T(8,128)(2,1)S(1)} collective-permute-done((bf16[64,2048]{1,0:T(8,128)(2,1)S(1)}, bf16[64,2048]{1,0:T(8,128)(2,1)S(1)}, u32[]{:S(2)}, u32[]{:S(2)}) %collective-permute-start.10) | collective-permute-done | bytes 262176 | tf_op jit(solution)/shard_map/ppermute | solution.py:47
  89.9 0.0 collective-permute-done.15
  89.9 0.0 collective-permute-done.12
  89.9 0.1 add_convert_fusion.10
  90.0 0.1 add_convert_fusion.3
  90.2 0.2 collective-permute-start.17
  90.3 2.9 %collective-permute-start.18 = (bf16[64,2048]{1,0:T(8,128)(2,1)S(1)}, bf16[64,2048]{1,0:T(8,128)(2,1)S(1)}, u32[]{:S(2)}, u32[]{:S(2)}) collective-permute-start(bf16[64,2048]{1,0:T(8,128)(2,1)S(1)} %get-tuple-element.141), channel_id=1, source_target_pairs={{0,10},{2,12},{4,14},{6,15},{7,13},{5,11},{3,9},{1,8},{8,2},{10,4}... | collective-permute-start | bytes 786440 | tf_op jit(solution)/shard_map/ppermute | solution.py:42
  93.2 1.7 %collective-permute-start.13 = (bf16[64,2048]{1,0:T(8,128)(2,1)S(1)}, bf16[64,2048]{1,0:T(8,128)(2,1)S(1)}, u32[]{:S(2)}, u32[]{:S(2)}) collective-permute-start(bf16[64,2048]{1,0:T(8,128)(2,1)S(1)} %get-tuple-element.142), channel_id=1, source_target_pairs={{0,10},{2,12},{4,14},{6,15},{7,13},{5,11},{3,9},{1,8},{8,2},{10,4}... | collective-permute-start | bytes 786440 | tf_op jit(solution)/shard_map/ppermute | solution.py:42
  94.9 5.6 %collective-permute-done.18 = bf16[64,2048]{1,0:T(8,128)(2,1)S(1)} collective-permute-done((bf16[64,2048]{1,0:T(8,128)(2,1)S(1)}, bf16[64,2048]{1,0:T(8,128)(2,1)S(1)}, u32[]{:S(2)}, u32[]{:S(2)}) %collective-permute-start.18) | collective-permute-done | bytes 262176 | tf_op jit(solution)/shard_map/ppermute | solution.py:42
  100.5 4.6 %collective-permute-done.13 = bf16[64,2048]{1,0:T(8,128)(2,1)S(1)} collective-permute-done((bf16[64,2048]{1,0:T(8,128)(2,1)S(1)}, bf16[64,2048]{1,0:T(8,128)(2,1)S(1)}, u32[]{:S(2)}, u32[]{:S(2)}) %collective-permute-start.13) | collective-permute-done | bytes 262176 | tf_op jit(solution)/shard_map/ppermute | solution.py:42
  105.1 0.5 collective-permute-start.22
  105.6 0.0 collective-permute-start.23
  105.6 0.1 add_convert_fusion.8
  105.7 2.0 %collective-permute-start.20 = (bf16[64,2048]{1,0:T(8,128)(2,1)S(1)}, bf16[64,2048]{1,0:T(8,128)(2,1)S(1)}, u32[]{:S(2)}, u32[]{:S(2)}) collective-permute-start(bf16[64,2048]{1,0:T(8,128)(2,1)S(1)} %get-tuple-element.139), channel_id=1, source_target_pairs={{0,9},{2,8},{4,10},{6,12},{7,14},{5,15},{3,13},{1,11},{8,1},{10,0}... | collective-permute-start | bytes 786440 | tf_op jit(solution)/shard_map/ppermute | solution.py:42
  107.7 0.1 collective-permute-start.19
  107.8 0.7 collective-permute-done.21
  108.5 1.7 %add_convert_fusion.2 = bf16[384,2048]{1,0:T(8,128)(2,1)} fusion(bf16[384,2048]{1,0:T(8,128)(2,1)S(1)} %collective-permute-done.21, bf16[384,2048]{1,0:T(8,128)(2,1)S(1)} %get-tuple-element.122), kind=kLoop, calls=%fused_computation.2 | loop fusion | flops 3145728 | bytes 4718592 | tf_op jit(solution)/shard_map/convert_element_type | solution.py:260
  110.3 0.5 collective-permute-done.22
  110.8 1.7 %add_convert_fusion.1 = bf16[384,2048]{1,0:T(8,128)(2,1)} fusion(bf16[384,2048]{1,0:T(8,128)(2,1)S(1)} %collective-permute-done.22, bf16[384,2048]{1,0:T(8,128)(2,1)S(1)} %get-tuple-element.124), kind=kLoop, calls=%fused_computation.1 | loop fusion | flops 3145728 | bytes 4718592 | tf_op jit(solution)/shard_map/convert_element_type | solution.py:260
  112.5 0.5 collective-permute-done.23
  113.0 1.8 %add_convert_fusion = bf16[384,2048]{1,0:T(8,128)(2,1)} fusion(bf16[384,2048]{1,0:T(8,128)(2,1)S(1)} %collective-permute-done.23, bf16[384,2048]{1,0:T(8,128)(2,1)S(1)} %get-tuple-element.126), kind=kLoop, calls=%fused_computation | loop fusion | flops 3145728 | bytes 4718592 | tf_op jit(solution)/shard_map/convert_element_type | solution.py:260
  114.8 1.1 collective-permute-done.20
  115.9 5.2 %collective-permute-done.19 = bf16[64,2048]{1,0:T(8,128)(2,1)S(1)} collective-permute-done((bf16[64,2048]{1,0:T(8,128)(2,1)S(1)}, bf16[64,2048]{1,0:T(8,128)(2,1)S(1)}, u32[]{:S(2)}, u32[]{:S(2)}) %collective-permute-start.19) | collective-permute-done | bytes 262176 | tf_op jit(solution)/shard_map/ppermute | solution.py:42
  121.0 1.0 fusion
  (9 shorter events, 0.0 us)
Async XLA Ops:
  0.6 30.0 %collective-permute-start.3 = (bf16[384,2048]{1,0:T(8,128)(2,1)}, bf16[384,2048]{1,0:T(8,128)(2,1)S(1)}, u32[]{:S(2)}, u32[]{:S(2)}) collective-permute-start(bf16[384,2048]{1,0:T(8,128)(2,1)} %bitcast.21), channel_id=1, source_target_pairs={{0,16},{16,0},{1,17},{17,1},{2,18},{18,2},{3,19},{19,3},{4,20},{20... | collective-permute-start | bytes 4718600 | tf_op jit(solution)/shard_map/ppermute | solution.py:47
  1.2 29.5 %collective-permute-start.4 = (bf16[384,2048]{1,0:T(8,128)(2,1)}, bf16[384,2048]{1,0:T(8,128)(2,1)S(1)}, u32[]{:S(2)}, u32[]{:S(2)}) collective-permute-start(bf16[384,2048]{1,0:T(8,128)(2,1)} %bitcast.23), channel_id=1, source_target_pairs={{0,16},{16,0},{1,17},{17,1},{2,18},{18,2},{3,19},{19,3},{4,20},{20... | collective-permute-start | bytes 4718600 | tf_op jit(solution)/shard_map/ppermute | solution.py:47
  1.2 29.4 %collective-permute-start.5 = (bf16[384,2048]{1,0:T(8,128)(2,1)}, bf16[384,2048]{1,0:T(8,128)(2,1)}, u32[]{:S(2)}, u32[]{:S(2)}) collective-permute-start(bf16[384,2048]{1,0:T(8,128)(2,1)} %bitcast.25), channel_id=1, source_target_pairs={{0,16},{16,0},{1,17},{17,1},{2,18},{18,2},{3,19},{19,3},{4,20},{20... | collective-permute-start | bytes 4718600 | tf_op jit(solution)/shard_map/ppermute | solution.py:47
  3.9 12.0 %collective-permute-start = (bf16[64,4224]{1,0:T(8,128)(2,1)}, bf16[64,4224]{1,0:T(8,128)(2,1)S(1)}, u32[]{:S(2)}, u32[]{:S(2)}) collective-permute-start(bf16[64,4224]{1,0:T(8,128)(2,1)} %pack_rows.1.refs_0_), channel_id=1, source_target_pairs={{0,2},{2,4},{4,6},{6,7},{7,5},{5,3},{3,1},{1,0},{8,10},{10,12},{12... | collective-permute-start | bytes 1622024 | tf_op jit(solution)/shard_map/ppermute | solution.py:42
  6.5 1.4 %copy-start.1 = (bf16[1,2,192,2048]{3,2,1,0:T(8,128)(2,1)S(1)}, bf16[1,2,192,2048]{3,2,1,0:T(8,128)(2,1)}, u32[]{:S(2)}) copy-start(bf16[1,2,192,2048]{3,2,1,0:T(8,128)(2,1)} %param.13) | copy-start | bytes 4718596
  7.9 1.4 %copy-start.2 = (bf16[1,2,192,2048]{3,2,1,0:T(8,128)(2,1)S(1)}, bf16[1,2,192,2048]{3,2,1,0:T(8,128)(2,1)}, u32[]{:S(2)}) copy-start(bf16[1,2,192,2048]{3,2,1,0:T(8,128)(2,1)} %param.14) | copy-start | bytes 4718596
  7.9 1.9 %copy-start.3 = (bf16[1,2,192,2048]{3,2,1,0:T(8,128)(2,1)S(1)}, bf16[1,2,192,2048]{3,2,1,0:T(8,128)(2,1)}, u32[]{:S(2)}) copy-start(bf16[1,2,192,2048]{3,2,1,0:T(8,128)(2,1)} %param.15) | copy-start | bytes 4718596
  9.8 1.0 copy-start
  10.9 12.7 %collective-permute-start.1 = (bf16[64,4224]{1,0:T(8,128)(2,1)S(1)}, bf16[64,4224]{1,0:T(8,128)(2,1)S(1)}, u32[]{:S(2)}, u32[]{:S(2)}) collective-permute-start(bf16[64,4224]{1,0:T(8,128)(2,1)S(1)} %copy-done), channel_id=1, source_target_pairs={{0,1},{2,0},{4,2},{6,4},{7,6},{5,7},{3,5},{1,3},{8,9},{10,8},{12,1... | collective-permute-start | bytes 1622024 | tf_op jit(solution)/shard_map/ppermute | solution.py:42
  15.8 12.3 %collective-permute-start.2 = (bf16[64,4224]{1,0:T(8,128)(2,1)S(1)}, bf16[64,4224]{1,0:T(8,128)(2,1)S(1)}, u32[]{:S(2)}, u32[]{:S(2)}) collective-permute-start(bf16[64,4224]{1,0:T(8,128)(2,1)S(1)} %collective-permute-done.refs_1_), channel_id=1, source_target_pairs={{0,2},{2,4},{4,6},{6,7},{7,5},{5,3},{3,1},{1,0},{8,10},{10,12},{12... | collective-permute-start | bytes 1622024 | tf_op jit(solution)/shard_map/ppermute | solution.py:42
  23.6 14.8 %collective-permute-start.6 = (bf16[64,4224]{1,0:T(8,128)(2,1)S(1)}, bf16[64,4224]{1,0:T(8,128)(2,1)S(1)}, u32[]{:S(2)}, u32[]{:S(2)}) collective-permute-start(bf16[64,4224]{1,0:T(8,128)(2,1)S(1)} %collective-permute-done.1.refs_2_), channel_id=1, source_target_pairs={{0,1},{2,0},{4,2},{6,4},{7,6},{5,7},{3,5},{1,3},{8,9},{10,8},{12,1... | collective-permute-start | bytes 1622024 | tf_op jit(solution)/shard_map/ppermute | solution.py:42
  28.2 11.1 %collective-permute-start.8 = (bf16[64,4224]{1,0:T(8,128)(2,1)S(1)}, bf16[64,4224]{1,0:T(8,128)(2,1)S(1)}, u32[]{:S(2)}, u32[]{:S(2)}) collective-permute-start(bf16[64,4224]{1,0:T(8,128)(2,1)S(1)} %collective-permute-done.2.refs_3_), channel_id=1, source_target_pairs={{0,2},{2,4},{4,6},{6,7},{7,5},{5,3},{3,1},{1,0},{8,10},{10,12},{12... | collective-permute-start | bytes 1622024 | tf_op jit(solution)/shard_map/ppermute | solution.py:42
  38.4 14.6 %collective-permute-start.7 = (bf16[64,4224]{1,0:T(8,128)(2,1)S(1)}, bf16[64,4224]{1,0:T(8,128)(2,1)S(1)}, u32[]{:S(2)}, u32[]{:S(2)}) collective-permute-start(bf16[64,4224]{1,0:T(8,128)(2,1)S(1)} %collective-permute-done.6.refs_0_.refs_4_), channel_id=1, source_target_pairs={{0,1},{2,0},{4,2},{6,4},{7,6},{5,7},{3,5},{1,3},{8,9},{10,8},{12,1... | collective-permute-start | bytes 1622024 | tf_op jit(solution)/shard_map/ppermute | solution.py:42
  39.2 13.7 %collective-permute-start.9 = (bf16[64,4224]{1,0:T(8,128)(2,1)S(1)}, bf16[64,4224]{1,0:T(8,128)(2,1)S(1)}, u32[]{:S(2)}, u32[]{:S(2)}) collective-permute-start(bf16[64,4224]{1,0:T(8,128)(2,1)S(1)} %collective-permute-done.8.refs_1_.refs_5_), channel_id=1, source_target_pairs={{0,2},{2,4},{4,6},{6,7},{7,5},{5,3},{3,1},{1,0},{8,10},{10,12},{12... | collective-permute-start | bytes 1622024 | tf_op jit(solution)/shard_map/ppermute | solution.py:42
  59.2 14.5 %collective-permute-start.14 = (bf16[64,4096]{1,0:T(8,128)(2,1)S(1)}, bf16[64,4096]{1,0:T(8,128)(2,1)S(1)}, u32[]{:S(2)}, u32[]{:S(2)}) collective-permute-start(bf16[64,4096]{1,0:T(8,128)(2,1)S(1)} %get-tuple-element.96), channel_id=1, source_target_pairs={{0,1},{2,0},{4,2},{6,4},{7,6},{5,7},{3,5},{1,3},{8,9},{10,8},{12,1... | collective-permute-start | bytes 1572872 | tf_op jit(solution)/shard_map/ppermute | solution.py:42
  59.3 14.4 %collective-permute-start.11 = (bf16[64,4096]{1,0:T(8,128)(2,1)S(1)}, bf16[64,4096]{1,0:T(8,128)(2,1)S(1)}, u32[]{:S(2)}, u32[]{:S(2)}) collective-permute-start(bf16[64,4096]{1,0:T(8,128)(2,1)S(1)} %get-tuple-element.93), channel_id=1, source_target_pairs={{0,2},{2,4},{4,6},{6,7},{7,5},{5,3},{3,1},{1,0},{8,10},{10,12},{12... | collective-permute-start | bytes 1572872 | tf_op jit(solution)/shard_map/ppermute | solution.py:42
  73.9 16.0 %collective-permute-start.15 = (bf16[64,4096]{1,0:T(8,128)(2,1)S(1)}, bf16[64,4096]{1,0:T(8,128)(2,1)S(1)}, u32[]{:S(2)}, u32[]{:S(2)}) collective-permute-start(bf16[64,4096]{1,0:T(8,128)(2,1)S(1)} %add_convert_fusion.4), channel_id=1, source_target_pairs={{0,1},{2,0},{4,2},{6,4},{7,6},{5,7},{3,5},{1,3},{8,9},{10,8},{12,1... | collective-permute-start | bytes 1572872 | tf_op jit(solution)/shard_map/ppermute | solution.py:42
  74.1 15.8 %collective-permute-start.12 = (bf16[64,4096]{1,0:T(8,128)(2,1)S(1)}, bf16[64,4096]{1,0:T(8,128)(2,1)S(1)}, u32[]{:S(2)}, u32[]{:S(2)}) collective-permute-start(bf16[64,4096]{1,0:T(8,128)(2,1)S(1)} %add_convert_fusion.5), channel_id=1, source_target_pairs={{0,2},{2,4},{4,6},{6,7},{7,5},{5,3},{3,1},{1,0},{8,10},{10,12},{12... | collective-permute-start | bytes 1572872 | tf_op jit(solution)/shard_map/ppermute | solution.py:42
  76.3 9.3 %collective-permute-start.16 = (bf16[64,2048]{1,0:T(8,128)(2,1)S(1)}, bf16[64,2048]{1,0:T(8,128)(2,1)S(1)}, u32[]{:S(2)}, u32[]{:S(2)}) collective-permute-start(bf16[64,2048]{1,0:T(8,128)(2,1)S(1)} %get-tuple-element.137), channel_id=1, source_target_pairs={{0,8},{8,0},{1,9},{9,1},{2,10},{10,2},{3,11},{11,3},{4,12},{12,4},... | collective-permute-start | bytes 786440 | tf_op jit(solution)/shard_map/ppermute | solution.py:47
  77.9 12.0 %collective-permute-start.10 = (bf16[64,2048]{1,0:T(8,128)(2,1)S(1)}, bf16[64,2048]{1,0:T(8,128)(2,1)S(1)}, u32[]{:S(2)}, u32[]{:S(2)}) collective-permute-start(bf16[64,2048]{1,0:T(8,128)(2,1)S(1)} %get-tuple-element.138), channel_id=1, source_target_pairs={{0,8},{8,0},{1,9},{9,1},{2,10},{10,2},{3,11},{11,3},{4,12},{12,4},... | collective-permute-start | bytes 786440 | tf_op jit(solution)/shard_map/ppermute | solution.py:47
  90.2 14.9 %collective-permute-start.17 = (bf16[64,4096]{1,0:T(8,128)(2,1)S(1)}, bf16[64,4096]{1,0:T(8,128)(2,1)S(1)}, u32[]{:S(2)}, u32[]{:S(2)}) collective-permute-start(bf16[64,4096]{1,0:T(8,128)(2,1)S(1)} %add_convert_fusion.3), channel_id=1, source_target_pairs={{0,1},{2,0},{4,2},{6,4},{7,6},{5,7},{3,5},{1,3},{8,9},{10,8},{12,1... | collective-permute-start | bytes 1572872 | tf_op jit(solution)/shard_map/ppermute | solution.py:42
  90.3 10.1 %collective-permute-start.18 = (bf16[64,2048]{1,0:T(8,128)(2,1)S(1)}, bf16[64,2048]{1,0:T(8,128)(2,1)S(1)}, u32[]{:S(2)}, u32[]{:S(2)}) collective-permute-start(bf16[64,2048]{1,0:T(8,128)(2,1)S(1)} %get-tuple-element.141), channel_id=1, source_target_pairs={{0,10},{2,12},{4,14},{6,15},{7,13},{5,11},{3,9},{1,8},{8,2},{10,4}... | collective-permute-start | bytes 786440 | tf_op jit(solution)/shard_map/ppermute | solution.py:42
  93.2 11.9 %collective-permute-start.13 = (bf16[64,2048]{1,0:T(8,128)(2,1)S(1)}, bf16[64,2048]{1,0:T(8,128)(2,1)S(1)}, u32[]{:S(2)}, u32[]{:S(2)}) collective-permute-start(bf16[64,2048]{1,0:T(8,128)(2,1)S(1)} %get-tuple-element.142), channel_id=1, source_target_pairs={{0,10},{2,12},{4,14},{6,15},{7,13},{5,11},{3,9},{1,8},{8,2},{10,4}... | collective-permute-start | bytes 786440 | tf_op jit(solution)/shard_map/ppermute | solution.py:42
  105.1 3.4 %collective-permute-start.21 = (bf16[384,2048]{1,0:T(8,128)(2,1)S(1)}, bf16[384,2048]{1,0:T(8,128)(2,1)S(1)}, u32[]{:S(2)}, u32[]{:S(2)}) collective-permute-start(bf16[384,2048]{1,0:T(8,128)(2,1)S(1)} %get-tuple-element.123), channel_id=1, source_target_pairs={{0,16},{16,0},{1,17},{17,1},{2,18},{18,2},{3,19},{19,3},{4,20},{20... | collective-permute-start | bytes 4718600 | tf_op jit(solution)/shard_map/ppermute | solution.py:47
  105.1 5.7 %collective-permute-start.22 = (bf16[384,2048]{1,0:T(8,128)(2,1)S(1)}, bf16[384,2048]{1,0:T(8,128)(2,1)S(1)}, u32[]{:S(2)}, u32[]{:S(2)}) collective-permute-start(bf16[384,2048]{1,0:T(8,128)(2,1)S(1)} %get-tuple-element.125), channel_id=1, source_target_pairs={{0,16},{16,0},{1,17},{17,1},{2,18},{18,2},{3,19},{19,3},{4,20},{20... | collective-permute-start | bytes 4718600 | tf_op jit(solution)/shard_map/ppermute | solution.py:47
  105.6 7.4 %collective-permute-start.23 = (bf16[384,2048]{1,0:T(8,128)(2,1)S(1)}, bf16[384,2048]{1,0:T(8,128)(2,1)S(1)}, u32[]{:S(2)}, u32[]{:S(2)}) collective-permute-start(bf16[384,2048]{1,0:T(8,128)(2,1)S(1)} %get-tuple-element.127), channel_id=1, source_target_pairs={{0,16},{16,0},{1,17},{17,1},{2,18},{18,2},{3,19},{19,3},{4,20},{20... | collective-permute-start | bytes 4718600 | tf_op jit(solution)/shard_map/ppermute | solution.py:47
  105.7 10.1 %collective-permute-start.20 = (bf16[64,2048]{1,0:T(8,128)(2,1)S(1)}, bf16[64,2048]{1,0:T(8,128)(2,1)S(1)}, u32[]{:S(2)}, u32[]{:S(2)}) collective-permute-start(bf16[64,2048]{1,0:T(8,128)(2,1)S(1)} %get-tuple-element.139), channel_id=1, source_target_pairs={{0,9},{2,8},{4,10},{6,12},{7,14},{5,15},{3,13},{1,11},{8,1},{10,0}... | collective-permute-start | bytes 786440 | tf_op jit(solution)/shard_map/ppermute | solution.py:42
  107.7 13.3 %collective-permute-start.19 = (bf16[64,2048]{1,0:T(8,128)(2,1)S(1)}, bf16[64,2048]{1,0:T(8,128)(2,1)S(1)}, u32[]{:S(2)}, u32[]{:S(2)}) collective-permute-start(bf16[64,2048]{1,0:T(8,128)(2,1)S(1)} %get-tuple-element.140), channel_id=1, source_target_pairs={{0,9},{2,8},{4,10},{6,12},{7,14},{5,15},{3,13},{1,11},{8,1},{10,0}... | collective-permute-start | bytes 786440 | tf_op jit(solution)/shard_map/ppermute | solution.py:42

commit v11 on v9

--- a/solution.py
+++ b/solution.py
@@ -290,8 +290,7 @@
         names += [("near", k), ("far", k)]
     names = names[: 2 * ahead]
     groups = [names[i : i + 4] for i in range(0, len(names) - 4, 4)]
-    groups.append([name for name in names[-4:] if name[0] == "far"])
-    groups.append([name for name in names[-4:] if name[0] == "near"])
+    groups += [[name for name in names[-4:] if name[0] == way] for way in ("far", "near")]
     held = {("near", 0): home, ("far", 0): tie((home, own))[0]}
     partial, kept = {}, []
 
@@ -304,14 +303,14 @@
 
     for k in range(1, ahead + 1):
         held["near", k] = ring_shift(held["near", k - 1], 1)
-        if k <= behind:
-            held["far", k] = ring_shift(held["far", k - 1], -1)
         if k == 1:
             held["near", 1], own = tie((held["near", 1], own))
             weights[:3] = own
         if k % 2 == 1 and k > 1:
             work(groups[(k - 3) // 2])
-            held["near", k], kept[-1] = tie((held["near", k], kept[-1]))
+            held["far", k - 1], kept[-1] = tie((held["far", k - 1], kept[-1]))
+        if k <= behind:
+            held["far", k] = ring_shift(held["far", k - 1], -1)
     work(groups[-2])
     far_sum = ring_shift(partial["far", behind], 1)
     held["near", ahead], kept[-1] = tie((held["near", ahead], kept[-1]))
@@ -322,7 +321,7 @@
     blocks = [held[name] for group in groups for name in group]
     steps = (1, -1)
     finals = []
-    here, near_sum = tie((partial["near", 0], near_sum))
+    here, far_sum = tie((partial["near", 0], far_sum))
     for part, step in zip(both, steps):
         kept_here = add(home[:, part], here[:, part])
         finals.append([from_behind(kept_here, "section", step)])
@@ -331,16 +330,19 @@
         left = k - 2
         if left > 1:
             far_done = far_sum
-            far_sum = ring_shift(add(far_sum, partial["far", left]), 1)
+            far_next = add(far_sum, partial["far", left])
+            far_sum = ring_shift(far_next, 1)
             near_sum, _ = tie((near_sum, far_done))
+        if k == 4:
+            kept[-1], _ = tie((kept[-1], far_next))
+            own_total, other_total = weight_call(blocks, kept, width, peers)
+            near_sum, own_total, other_total = tie((near_sum, own_total, other_total))
         if k == 3:
             lasts = [add(far_sum[:, part], partial["far", 1][:, part]) for part in both]
             for final, last, step in zip(finals, lasts, steps):
                 final.append(ring_shift(last, 1, step))
-            kept[-1], _ = tie((kept[-1], lasts))
-            own_total, other_total = weight_call(blocks, kept, width, peers)
             here = [final[0] for final in finals] + finals[0][1:]
-            near_sum, own_total, other_total, _ = tie((near_sum, own_total, other_total, here))
+            near_sum, _ = tie((near_sum, here))
             near_sum = add(near_sum, partial["near", 2])
             near_sum, other_total = tie((near_sum, other_total))
             received = [from_behind(g, "rep", 1) for g in other_total]

time: 119 us -> 122 us (1.025)
  starting transfers between devices: 24.4 us -> 26.8 us
    ppermute x16, starting transfers between devices: 20.7 us -> 23.2 us  [ring_shift(): return lax.ppermute(value, ('rep', 'section', 'exp'), pairs)]
  transfers between devices with their start and end apart: 24 -> 24, of which waited for: 12 -> 13; matrix products, arithmetic and copies ran while one was open for 5% -> 5% of each run, Pallas kernels for 24% -> 23%
where the time goes in v11:
time: 122 us
  waiting for transfers between devices  54.6 us (45%)
  Pallas kernels  28.6 us (23%)
  starting transfers between devices  26.8 us (22%)
  other arithmetic  7.15 us (6%)
  local copies, waits for them, and re-layouts  3.97 us (3%)
    ppermute x16, waiting for transfers between devices, ring_shift(): return lax.ppermute(value, ('rep', 'section', 'exp'), pairs)  54.5 us
    ppermute x16, starting transfers between devices, ring_shift(): return lax.ppermute(value, ('rep', 'section', 'exp'), pairs)  23.2 us
    pallas_call x3, Pallas kernels, expert_call(): pl.pallas_call(functools.partial(expert_kernel, count, experts, local_exp...  20.1 us
    convert_element_type x9, other arithmetic, add(): return (a.astype(F32) + b.astype(F32)).astype(BF16)  6.12 us
    pallas_call x1, Pallas kernels, weight_call(): pl.pallas_call(functools.partial(weight_kernel, len(kept), count), out_sh...  5.88 us
    unnamed x8, local copies, waits for them, and re-layouts  3.97 us
    ppermute x8, starting transfers between devices, from_behind(): lax.ppermute(value, axis, [(i, (i + by) % peers) for i in range(peers)])  3.62 us
  transfers between devices with their start and end apart: 24, of which 13 were waited for; matrix products, arithmetic and copies ran while one was open for 5% of the time, Pallas kernels for 23%

profile of v11, /device:TPU:0, one launch (start us, length us, event | category | flops | bytes accessed | tf_op | source)
XLA Modules:
  0.0 121.8 jit_solution(4910681600621449088)
XLA Ops:
  0.6 0.5 collective-permute-start.3
  1.2 0.1 collective-permute-start.4
  1.2 0.4 collective-permute-start.5
  1.7 2.2 %pack_rows.1.refs_0_ = bf16[64,4224]{1,0:T(8,128)(2,1)} custom-call(bf16[64,2048]{1,0:T(8,128)(2,1)} %bitcast.30, s32[16,64]{1,0:T(8,128)} %bitcast.32, s32[8,64]{1,0:T(8,128)} %bitcast.33, f32[8,64]{1,0:T(8,128)} %bitcast.34, bf16[64,2048]{1,0:T(8,128)(2,1)} %bitcast.31), custom_call_target="tpu_custom_call" | custom-call | tf_op jit(solution)/shard_map/pack_rows/pallas_call | solution.py:274
  3.9 2.7 %collective-permute-start = (bf16[64,4224]{1,0:T(8,128)(2,1)}, bf16[64,4224]{1,0:T(8,128)(2,1)S(1)}, u32[]{:S(2)}, u32[]{:S(2)}) collective-permute-start(bf16[64,4224]{1,0:T(8,128)(2,1)} %pack_rows.1.refs_0_), channel_id=1, source_target_pairs={{0,2},{2,4},{4,6},{6,7},{7,5},{5,3},{3,1},{1,0},{8,10},{10,12},{12... | collective-permute-start | bytes 1622024 | tf_op jit(solution)/shard_map/ppermute | solution.py:42
  6.5 1.4 %copy-done.1 = bf16[1,2,192,2048]{3,2,1,0:T(8,128)(2,1)S(1)} copy-done((bf16[1,2,192,2048]{3,2,1,0:T(8,128)(2,1)S(1)}, bf16[1,2,192,2048]{3,2,1,0:T(8,128)(2,1)}, u32[]{:S(2)}) %copy-start.1) | copy-done | bytes 1572888
  7.9 0.1 load_weights.2.refs_4_.refs_2_
  8.1 1.3 %copy-done.2 = bf16[1,2,192,2048]{3,2,1,0:T(8,128)(2,1)S(1)} copy-done((bf16[1,2,192,2048]{3,2,1,0:T(8,128)(2,1)S(1)}, bf16[1,2,192,2048]{3,2,1,0:T(8,128)(2,1)}, u32[]{:S(2)}) %copy-start.2) | copy-done | bytes 1572888
  9.3 0.5 copy-done.3
  9.8 0.2 load_weights.3
  10.1 0.8 copy-done
  10.9 0.0 collective-permute-start.1
  10.9 5.0 %collective-permute-done.refs_1_ = bf16[64,4224]{1,0:T(8,128)(2,1)S(1)} collective-permute-done((bf16[64,4224]{1,0:T(8,128)(2,1)}, bf16[64,4224]{1,0:T(8,128)(2,1)S(1)}, u32[]{:S(2)}, u32[]{:S(2)}) %collective-permute-start) | collective-permute-done | bytes 540704 | tf_op jit(solution)/shard_map/ppermute | solution.py:42
  15.8 2.4 %collective-permute-start.2 = (bf16[64,4224]{1,0:T(8,128)(2,1)S(1)}, bf16[64,4224]{1,0:T(8,128)(2,1)S(1)}, u32[]{:S(2)}, u32[]{:S(2)}) collective-permute-start(bf16[64,4224]{1,0:T(8,128)(2,1)S(1)} %collective-permute-done.refs_1_), channel_id=1, source_target_pairs={{0,2},{2,4},{4,6},{6,7},{7,5},{5,3},{3,1},{1,0},{8,10},{10,12},{12... | collective-permute-start | bytes 1622024 | tf_op jit(solution)/shard_map/ppermute | solution.py:42
  18.2 5.4 %collective-permute-done.1.refs_2_ = bf16[64,4224]{1,0:T(8,128)(2,1)S(1)} collective-permute-done((bf16[64,4224]{1,0:T(8,128)(2,1)S(1)}, bf16[64,4224]{1,0:T(8,128)(2,1)S(1)}, u32[]{:S(2)}, u32[]{:S(2)}) %collective-permute-start.1) | collective-permute-done | bytes 540704 | tf_op jit(solution)/shard_map/ppermute | solution.py:42
  23.6 0.0 collective-permute-start.6
  23.6 4.6 %collective-permute-done.2.refs_3_ = bf16[64,4224]{1,0:T(8,128)(2,1)S(1)} collective-permute-done((bf16[64,4224]{1,0:T(8,128)(2,1)S(1)}, bf16[64,4224]{1,0:T(8,128)(2,1)S(1)}, u32[]{:S(2)}, u32[]{:S(2)}) %collective-permute-start.2) | collective-permute-done | bytes 540704 | tf_op jit(solution)/shard_map/ppermute | solution.py:42
  28.2 2.5 %collective-permute-start.12 = (bf16[64,4224]{1,0:T(8,128)(2,1)S(1)}, bf16[64,4224]{1,0:T(8,128)(2,1)S(1)}, u32[]{:S(2)}, u32[]{:S(2)}) collective-permute-start(bf16[64,4224]{1,0:T(8,128)(2,1)S(1)} %collective-permute-done.2.refs_3_), channel_id=1, source_target_pairs={{0,2},{2,4},{4,6},{6,7},{7,5},{5,3},{3,1},{1,0},{8,10},{10,12},{12... | collective-permute-start | bytes 1622024 | tf_op jit(solution)/shard_map/ppermute | solution.py:42
  30.7 0.0 collective-permute-done.3.refs_7_.refs_5_
  30.7 0.0 collective-permute-done.4.refs_8_.refs_6_
  30.7 0.0 collective-permute-done.5.refs_9_.refs_7_
  30.7 7.7 %expert_rows.3 = (bf16[64,4096]{1,0:T(8,128)(2,1)S(1)}, bf16[64,4096]{1,0:T(8,128)(2,1)S(1)}, bf16[64,4096]{1,0:T(8,128)(2,1)S(1)}, bf16[64,4096]{1,0:T(8,128)(2...) custom-call(bf16[64,4224]{1,0:T(8,128)(2,1)S(1)} %copy-done, ...), custom_call_target="tpu_custom_call" | custom-call | flops 4831838208 | bytes 13631488 | tf_op jit(solution)/shard_map/expert_rows/pallas_call | solution.py:191
  38.4 0.0 collective-permute-done.6.refs_0_.refs_4_
  38.4 0.1 collective-permute-start.7
  38.5 0.8 collective-permute-done.12.refs_0_.refs_6_
  39.2 2.5 %collective-permute-start.13 = (bf16[64,4224]{1,0:T(8,128)(2,1)S(1)}, bf16[64,4224]{1,0:T(8,128)(2,1)S(1)}, u32[]{:S(2)}, u32[]{:S(2)}) collective-permute-start(bf16[64,4224]{1,0:T(8,128)(2,1)S(1)} %collective-permute-done.12.refs_0_.refs_6_), channel_id=1, source_target_pairs={{0,2},{2,4},{4,6},{6,7},{7,5},{5,3},{3,1},{1,0},{8,10},{10,12},{12... | collective-permute-start | bytes 1622024 | tf_op jit(solution)/shard_map/ppermute | solution.py:42
  41.7 11.2 %collective-permute-done.7.refs_1_.refs_5_ = bf16[64,4224]{1,0:T(8,128)(2,1)S(1)} collective-permute-done((bf16[64,4224]{1,0:T(8,128)(2,1)S(1)}, bf16[64,4224]{1,0:T(8,128)(2,1)S(1)}, u32[]{:S(2)}, u32[]{:S(2)}) %collective-permute-start.7) | collective-permute-done | bytes 540704 | tf_op jit(solution)/shard_map/ppermute | solution.py:42
  53.0 6.2 %expert_rows.4 = (bf16[64,4096]{1,0:T(8,128)(2,1)S(1)}, bf16[64,4096]{1,0:T(8,128)(2,1)S(1)}, bf16[768,128]{1,0:T(8,128)(2,1)S(1)}, bf16[768,128]{1,0:T(8,128)(2,1)S(1)}, bf16[768,128]{1,0:T(8,128)(2,1)S(1)}) custom-call(bf16[64,4224]{1,0:T(8,128)(2,1)S(1)} %collective-permute-done.6.refs_0_.refs_4_, ...), custom_call_target="tpu_custom_call" | custom-call | flops 2415919104 | bytes 11534336 | tf_op jit(solution)/shard_map/expert_rows/pallas_call | solution.py:191
  59.2 1.8 %collective-permute-start.8 = (bf16[64,4096]{1,0:T(8,128)(2,1)S(1)}, bf16[64,4096]{1,0:T(8,128)(2,1)S(1)}, u32[]{:S(2)}, u32[]{:S(2)}) collective-permute-start(bf16[64,4096]{1,0:T(8,128)(2,1)S(1)} %get-tuple-element.89), channel_id=1, source_target_pairs={{0,2},{2,4},{4,6},{6,7},{7,5},{5,3},{3,1},{1,0},{8,10},{10,12},{12... | collective-permute-start | bytes 1572872 | tf_op jit(solution)/shard_map/ppermute | solution.py:42
  61.0 0.0 collective-permute-done.13.refs_1_.refs_7_
  61.0 6.2 %expert_rows.5 = (bf16[64,4096]{1,0:T(8,128)(2,1)S(1)}, bf16[64,4096]{1,0:T(8,128)(2,1)S(1)}, bf16[768,128]{1,0:T(8,128)(2,1)S(1)}, bf16[768,128]{1,0:T(8,128)(2,1)S(1)}, bf16[768,128]{1,0:T(8,128)(2,1)S(1)}) custom-call(bf16[64,4224]{1,0:T(8,128)(2,1)S(1)} %collective-permute-done.12.refs_0_.refs_6_, ...), custom_call_target="tpu_custom_call" | custom-call | flops 2415919104 | bytes 11534336 | tf_op jit(solution)/shard_map/expert_rows/pallas_call | solution.py:191
  67.2 0.3 collective-permute-start.14
  67.5 5.6 %collective-permute-done.8 = bf16[64,4096]{1,0:T(8,128)(2,1)S(1)} collective-permute-done((bf16[64,4096]{1,0:T(8,128)(2,1)S(1)}, bf16[64,4096]{1,0:T(8,128)(2,1)S(1)}, u32[]{:S(2)}, u32[]{:S(2)}) %collective-permute-start.8) | collective-permute-done | bytes 524320 | tf_op jit(solution)/shard_map/ppermute | solution.py:42
  73.1 0.1 add_convert_fusion.5
  73.2 0.1 add_convert_fusion.11
  73.4 1.6 %collective-permute-start.10 = (bf16[64,4096]{1,0:T(8,128)(2,1)S(1)}, bf16[64,4096]{1,0:T(8,128)(2,1)S(1)}, u32[]{:S(2)}, u32[]{:S(2)}) collective-permute-start(bf16[64,4096]{1,0:T(8,128)(2,1)S(1)} %add_convert_fusion.5), channel_id=1, source_target_pairs={{0,2},{2,4},{4,6},{6,7},{7,5},{5,3},{3,1},{1,0},{8,10},{10,12},{12... | collective-permute-start | bytes 1572872 | tf_op jit(solution)/shard_map/ppermute | solution.py:42
  74.9 1.5 %collective-permute-start.16 = (bf16[64,2048]{1,0:T(8,128)(2,1)S(1)}, bf16[64,2048]{1,0:T(8,128)(2,1)S(1)}, u32[]{:S(2)}, u32[]{:S(2)}) collective-permute-start(bf16[64,2048]{1,0:T(8,128)(2,1)S(1)} %get-tuple-element.143), channel_id=1, source_target_pairs={{0,8},{8,0},{1,9},{9,1},{2,10},{10,2},{3,11},{11,3},{4,12},{12,4},... | collective-permute-start | bytes 786440 | tf_op jit(solution)/shard_map/ppermute | solution.py:47
  76.4 0.5 collective-permute-start.9
  77.0 5.9 %weight_grads.1 = (bf16[384,2048]{1,0:T(8,128)(2,1)S(1)}, bf16[384,2048]{1,0:T(8,128)(2,1)S(1)}, bf16[384,2048]{1,0:T(8,128)(2,1)S(1)}, bf16[384,2048]{1,0:T(8,1...) custom-call(bf16[64,4224]{1,0:T(8,128)(2,1)S(1)} %copy-done, ...), custom_call_target="tpu_custom_call" | custom-call | flops 4831838208 | bytes 13631488 | tf_op jit(solution)/shard_map/weight_grads/pallas_call | solution.py:242
  82.8 0.1 add_convert_fusion.4
  83.0 0.6 collective-permute-start.15
  83.6 3.0 %collective-permute-done.10 = bf16[64,4096]{1,0:T(8,128)(2,1)S(1)} collective-permute-done((bf16[64,4096]{1,0:T(8,128)(2,1)S(1)}, bf16[64,4096]{1,0:T(8,128)(2,1)S(1)}, u32[]{:S(2)}, u32[]{:S(2)}) %collective-permute-start.10) | collective-permute-done | bytes 524320 | tf_op jit(solution)/shard_map/ppermute | solution.py:42
  86.5 0.1 add_convert_fusion.10
  86.6 2.0 %collective-permute-start.11 = (bf16[64,2048]{1,0:T(8,128)(2,1)S(1)}, bf16[64,2048]{1,0:T(8,128)(2,1)S(1)}, u32[]{:S(2)}, u32[]{:S(2)}) collective-permute-start(bf16[64,2048]{1,0:T(8,128)(2,1)S(1)} %get-tuple-element.148), channel_id=1, source_target_pairs={{0,10},{2,12},{4,14},{6,15},{7,13},{5,11},{3,9},{1,8},{8,2},{10,4}... | collective-permute-start | bytes 786440 | tf_op jit(solution)/shard_map/ppermute | solution.py:42
  88.7 3.5 %collective-permute-done.15 = bf16[64,4096]{1,0:T(8,128)(2,1)S(1)} collective-permute-done((bf16[64,4096]{1,0:T(8,128)(2,1)S(1)}, bf16[64,4096]{1,0:T(8,128)(2,1)S(1)}, u32[]{:S(2)}, u32[]{:S(2)}) %collective-permute-start.15) | collective-permute-done | bytes 524320 | tf_op jit(solution)/shard_map/ppermute | solution.py:42
  92.2 1.8 %collective-permute-done.11 = bf16[64,2048]{1,0:T(8,128)(2,1)S(1)} collective-permute-done((bf16[64,2048]{1,0:T(8,128)(2,1)S(1)}, bf16[64,2048]{1,0:T(8,128)(2,1)S(1)}, u32[]{:S(2)}, u32[]{:S(2)}) %collective-permute-start.11) | collective-permute-done | bytes 262176 | tf_op jit(solution)/shard_map/ppermute | solution.py:42
  94.0 0.1 add_convert_fusion.3
  94.1 0.1 collective-permute-start.21
  94.2 0.5 collective-permute-start.22
  94.7 1.7 %collective-permute-start.17 = (bf16[64,4096]{1,0:T(8,128)(2,1)S(1)}, bf16[64,4096]{1,0:T(8,128)(2,1)S(1)}, u32[]{:S(2)}, u32[]{:S(2)}) collective-permute-start(bf16[64,4096]{1,0:T(8,128)(2,1)S(1)} %add_convert_fusion.3), channel_id=1, source_target_pairs={{0,1},{2,0},{4,2},{6,4},{7,6},{5,7},{3,5},{1,3},{8,9},{10,8},{12,1... | collective-permute-start | bytes 1572872 | tf_op jit(solution)/shard_map/ppermute | solution.py:42
  96.4 1.4 %collective-permute-start.18 = (bf16[64,2048]{1,0:T(8,128)(2,1)S(1)}, bf16[64,2048]{1,0:T(8,128)(2,1)S(1)}, u32[]{:S(2)}, u32[]{:S(2)}) collective-permute-start(bf16[64,2048]{1,0:T(8,128)(2,1)S(1)} %get-tuple-element.147), channel_id=1, source_target_pairs={{0,10},{2,12},{4,14},{6,15},{7,13},{5,11},{3,9},{1,8},{8,2},{10,4}... | collective-permute-start | bytes 786440 | tf_op jit(solution)/shard_map/ppermute | solution.py:42
  97.8 8.8 %collective-permute-done.18 = bf16[64,2048]{1,0:T(8,128)(2,1)S(1)} collective-permute-done((bf16[64,2048]{1,0:T(8,128)(2,1)S(1)}, bf16[64,2048]{1,0:T(8,128)(2,1)S(1)}, u32[]{:S(2)}, u32[]{:S(2)}) %collective-permute-start.18) | collective-permute-done | bytes 262176 | tf_op jit(solution)/shard_map/ppermute | solution.py:42
  106.5 0.1 collective-permute-done.17
  106.7 0.1 add_convert_fusion.8
  106.8 1.8 %collective-permute-start.20 = (bf16[64,2048]{1,0:T(8,128)(2,1)S(1)}, bf16[64,2048]{1,0:T(8,128)(2,1)S(1)}, u32[]{:S(2)}, u32[]{:S(2)}) collective-permute-start(bf16[64,2048]{1,0:T(8,128)(2,1)S(1)} %get-tuple-element.145), channel_id=1, source_target_pairs={{0,9},{2,8},{4,10},{6,12},{7,14},{5,15},{3,13},{1,11},{8,1},{10,0}... | collective-permute-start | bytes 786440 | tf_op jit(solution)/shard_map/ppermute | solution.py:42
  108.6 1.9 %collective-permute-start.19 = (bf16[64,2048]{1,0:T(8,128)(2,1)S(1)}, bf16[64,2048]{1,0:T(8,128)(2,1)S(1)}, u32[]{:S(2)}, u32[]{:S(2)}) collective-permute-start(bf16[64,2048]{1,0:T(8,128)(2,1)S(1)} %get-tuple-element.146), channel_id=1, source_target_pairs={{0,9},{2,8},{4,10},{6,12},{7,14},{5,15},{3,13},{1,11},{8,1},{10,0}... | collective-permute-start | bytes 786440 | tf_op jit(solution)/shard_map/ppermute | solution.py:42
  110.5 1.8 %add_convert_fusion.2 = bf16[384,2048]{1,0:T(8,128)(2,1)} fusion(bf16[384,2048]{1,0:T(8,128)(2,1)S(1)} %collective-permute-done.21, bf16[384,2048]{1,0:T(8,128)(2,1)S(1)} %get-tuple-element.128), kind=kLoop, calls=%fused_computation.2 | loop fusion | flops 3145728 | bytes 4718592 | tf_op jit(solution)/shard_map/convert_element_type | solution.py:260
  112.3 0.0 collective-permute-done.22
  112.3 1.7 %add_convert_fusion.1 = bf16[384,2048]{1,0:T(8,128)(2,1)} fusion(bf16[384,2048]{1,0:T(8,128)(2,1)S(1)} %collective-permute-done.22, bf16[384,2048]{1,0:T(8,128)(2,1)S(1)} %get-tuple-element.130), kind=kLoop, calls=%fused_computation.1 | loop fusion | flops 3145728 | bytes 4718592 | tf_op jit(solution)/shard_map/convert_element_type | solution.py:260
  114.1 0.0 collective-permute-done.23
  114.1 1.8 %add_convert_fusion = bf16[384,2048]{1,0:T(8,128)(2,1)} fusion(bf16[384,2048]{1,0:T(8,128)(2,1)S(1)} %collective-permute-done.23, bf16[384,2048]{1,0:T(8,128)(2,1)S(1)} %get-tuple-element.132), kind=kLoop, calls=%fused_computation | loop fusion | flops 3145728 | bytes 4718592 | tf_op jit(solution)/shard_map/convert_element_type | solution.py:260
  115.9 1.0 collective-permute-done.20
  116.9 3.9 %collective-permute-done.19 = bf16[64,2048]{1,0:T(8,128)(2,1)S(1)} collective-permute-done((bf16[64,2048]{1,0:T(8,128)(2,1)S(1)}, bf16[64,2048]{1,0:T(8,128)(2,1)S(1)}, u32[]{:S(2)}, u32[]{:S(2)}) %collective-permute-start.19) | collective-permute-done | bytes 262176 | tf_op jit(solution)/shard_map/ppermute | solution.py:42
  120.8 1.0 fusion
  (9 shorter events, 0.0 us)
Async XLA Ops:
  0.6 30.0 %collective-permute-start.3 = (bf16[384,2048]{1,0:T(8,128)(2,1)}, bf16[384,2048]{1,0:T(8,128)(2,1)S(1)}, u32[]{:S(2)}, u32[]{:S(2)}) collective-permute-start(bf16[384,2048]{1,0:T(8,128)(2,1)} %bitcast.21), channel_id=1, source_target_pairs={{0,16},{16,0},{1,17},{17,1},{2,18},{18,2},{3,19},{19,3},{4,20},{20... | collective-permute-start | bytes 4718600 | tf_op jit(solution)/shard_map/ppermute | solution.py:47
  1.2 29.5 %collective-permute-start.4 = (bf16[384,2048]{1,0:T(8,128)(2,1)}, bf16[384,2048]{1,0:T(8,128)(2,1)S(1)}, u32[]{:S(2)}, u32[]{:S(2)}) collective-permute-start(bf16[384,2048]{1,0:T(8,128)(2,1)} %bitcast.23), channel_id=1, source_target_pairs={{0,16},{16,0},{1,17},{17,1},{2,18},{18,2},{3,19},{19,3},{4,20},{20... | collective-permute-start | bytes 4718600 | tf_op jit(solution)/shard_map/ppermute | solution.py:47
  1.2 29.4 %collective-permute-start.5 = (bf16[384,2048]{1,0:T(8,128)(2,1)}, bf16[384,2048]{1,0:T(8,128)(2,1)}, u32[]{:S(2)}, u32[]{:S(2)}) collective-permute-start(bf16[384,2048]{1,0:T(8,128)(2,1)} %bitcast.25), channel_id=1, source_target_pairs={{0,16},{16,0},{1,17},{17,1},{2,18},{18,2},{3,19},{19,3},{4,20},{20... | collective-permute-start | bytes 4718600 | tf_op jit(solution)/shard_map/ppermute | solution.py:47
  3.9 12.0 %collective-permute-start = (bf16[64,4224]{1,0:T(8,128)(2,1)}, bf16[64,4224]{1,0:T(8,128)(2,1)S(1)}, u32[]{:S(2)}, u32[]{:S(2)}) collective-permute-start(bf16[64,4224]{1,0:T(8,128)(2,1)} %pack_rows.1.refs_0_), channel_id=1, source_target_pairs={{0,2},{2,4},{4,6},{6,7},{7,5},{5,3},{3,1},{1,0},{8,10},{10,12},{12... | collective-permute-start | bytes 1622024 | tf_op jit(solution)/shard_map/ppermute | solution.py:42
  6.5 1.4 %copy-start.1 = (bf16[1,2,192,2048]{3,2,1,0:T(8,128)(2,1)S(1)}, bf16[1,2,192,2048]{3,2,1,0:T(8,128)(2,1)}, u32[]{:S(2)}) copy-start(bf16[1,2,192,2048]{3,2,1,0:T(8,128)(2,1)} %param.13) | copy-start | bytes 4718596
  7.9 1.4 %copy-start.2 = (bf16[1,2,192,2048]{3,2,1,0:T(8,128)(2,1)S(1)}, bf16[1,2,192,2048]{3,2,1,0:T(8,128)(2,1)}, u32[]{:S(2)}) copy-start(bf16[1,2,192,2048]{3,2,1,0:T(8,128)(2,1)} %param.14) | copy-start | bytes 4718596
  7.9 1.9 %copy-start.3 = (bf16[1,2,192,2048]{3,2,1,0:T(8,128)(2,1)S(1)}, bf16[1,2,192,2048]{3,2,1,0:T(8,128)(2,1)}, u32[]{:S(2)}) copy-start(bf16[1,2,192,2048]{3,2,1,0:T(8,128)(2,1)} %param.15) | copy-start | bytes 4718596
  9.8 1.0 copy-start
  10.9 12.7 %collective-permute-start.1 = (bf16[64,4224]{1,0:T(8,128)(2,1)S(1)}, bf16[64,4224]{1,0:T(8,128)(2,1)S(1)}, u32[]{:S(2)}, u32[]{:S(2)}) collective-permute-start(bf16[64,4224]{1,0:T(8,128)(2,1)S(1)} %copy-done), channel_id=1, source_target_pairs={{0,1},{2,0},{4,2},{6,4},{7,6},{5,7},{3,5},{1,3},{8,9},{10,8},{12,1... | collective-permute-start | bytes 1622024 | tf_op jit(solution)/shard_map/ppermute | solution.py:42
  15.8 12.3 %collective-permute-start.2 = (bf16[64,4224]{1,0:T(8,128)(2,1)S(1)}, bf16[64,4224]{1,0:T(8,128)(2,1)S(1)}, u32[]{:S(2)}, u32[]{:S(2)}) collective-permute-start(bf16[64,4224]{1,0:T(8,128)(2,1)S(1)} %collective-permute-done.refs_1_), channel_id=1, source_target_pairs={{0,2},{2,4},{4,6},{6,7},{7,5},{5,3},{3,1},{1,0},{8,10},{10,12},{12... | collective-permute-start | bytes 1622024 | tf_op jit(solution)/shard_map/ppermute | solution.py:42
  23.6 14.8 %collective-permute-start.6 = (bf16[64,4224]{1,0:T(8,128)(2,1)S(1)}, bf16[64,4224]{1,0:T(8,128)(2,1)S(1)}, u32[]{:S(2)}, u32[]{:S(2)}) collective-permute-start(bf16[64,4224]{1,0:T(8,128)(2,1)S(1)} %collective-permute-done.1.refs_2_), channel_id=1, source_target_pairs={{0,1},{2,0},{4,2},{6,4},{7,6},{5,7},{3,5},{1,3},{8,9},{10,8},{12,1... | collective-permute-start | bytes 1622024 | tf_op jit(solution)/shard_map/ppermute | solution.py:42
  28.2 11.1 %collective-permute-start.12 = (bf16[64,4224]{1,0:T(8,128)(2,1)S(1)}, bf16[64,4224]{1,0:T(8,128)(2,1)S(1)}, u32[]{:S(2)}, u32[]{:S(2)}) collective-permute-start(bf16[64,4224]{1,0:T(8,128)(2,1)S(1)} %collective-permute-done.2.refs_3_), channel_id=1, source_target_pairs={{0,2},{2,4},{4,6},{6,7},{7,5},{5,3},{3,1},{1,0},{8,10},{10,12},{12... | collective-permute-start | bytes 1622024 | tf_op jit(solution)/shard_map/ppermute | solution.py:42
  38.4 14.6 %collective-permute-start.7 = (bf16[64,4224]{1,0:T(8,128)(2,1)S(1)}, bf16[64,4224]{1,0:T(8,128)(2,1)S(1)}, u32[]{:S(2)}, u32[]{:S(2)}) collective-permute-start(bf16[64,4224]{1,0:T(8,128)(2,1)S(1)} %collective-permute-done.6.refs_0_.refs_4_), channel_id=1, source_target_pairs={{0,1},{2,0},{4,2},{6,4},{7,6},{5,7},{3,5},{1,3},{8,9},{10,8},{12,1... | collective-permute-start | bytes 1622024 | tf_op jit(solution)/shard_map/ppermute | solution.py:42
  39.2 21.7 %collective-permute-start.13 = (bf16[64,4224]{1,0:T(8,128)(2,1)S(1)}, bf16[64,4224]{1,0:T(8,128)(2,1)S(1)}, u32[]{:S(2)}, u32[]{:S(2)}) collective-permute-start(bf16[64,4224]{1,0:T(8,128)(2,1)S(1)} %collective-permute-done.12.refs_0_.refs_6_), channel_id=1, source_target_pairs={{0,2},{2,4},{4,6},{6,7},{7,5},{5,3},{3,1},{1,0},{8,10},{10,12},{12... | collective-permute-start | bytes 1622024 | tf_op jit(solution)/shard_map/ppermute | solution.py:42
  59.2 13.9 %collective-permute-start.8 = (bf16[64,4096]{1,0:T(8,128)(2,1)S(1)}, bf16[64,4096]{1,0:T(8,128)(2,1)S(1)}, u32[]{:S(2)}, u32[]{:S(2)}) collective-permute-start(bf16[64,4096]{1,0:T(8,128)(2,1)S(1)} %get-tuple-element.89), channel_id=1, source_target_pairs={{0,2},{2,4},{4,6},{6,7},{7,5},{5,3},{3,1},{1,0},{8,10},{10,12},{12... | collective-permute-start | bytes 1572872 | tf_op jit(solution)/shard_map/ppermute | solution.py:42
  67.2 15.6 %collective-permute-start.14 = (bf16[64,4096]{1,0:T(8,128)(2,1)S(1)}, bf16[64,4096]{1,0:T(8,128)(2,1)S(1)}, u32[]{:S(2)}, u32[]{:S(2)}) collective-permute-start(bf16[64,4096]{1,0:T(8,128)(2,1)S(1)} %get-tuple-element.98), channel_id=1, source_target_pairs={{0,1},{2,0},{4,2},{6,4},{7,6},{5,7},{3,5},{1,3},{8,9},{10,8},{12,1... | collective-permute-start | bytes 1572872 | tf_op jit(solution)/shard_map/ppermute | solution.py:42
  73.4 13.1 %collective-permute-start.10 = (bf16[64,4096]{1,0:T(8,128)(2,1)S(1)}, bf16[64,4096]{1,0:T(8,128)(2,1)S(1)}, u32[]{:S(2)}, u32[]{:S(2)}) collective-permute-start(bf16[64,4096]{1,0:T(8,128)(2,1)S(1)} %add_convert_fusion.5), channel_id=1, source_target_pairs={{0,2},{2,4},{4,6},{6,7},{7,5},{5,3},{3,1},{1,0},{8,10},{10,12},{12... | collective-permute-start | bytes 1572872 | tf_op jit(solution)/shard_map/ppermute | solution.py:42
  74.9 13.7 %collective-permute-start.16 = (bf16[64,2048]{1,0:T(8,128)(2,1)S(1)}, bf16[64,2048]{1,0:T(8,128)(2,1)S(1)}, u32[]{:S(2)}, u32[]{:S(2)}) collective-permute-start(bf16[64,2048]{1,0:T(8,128)(2,1)S(1)} %get-tuple-element.143), channel_id=1, source_target_pairs={{0,8},{8,0},{1,9},{9,1},{2,10},{10,2},{3,11},{11,3},{4,12},{12,4},... | collective-permute-start | bytes 786440 | tf_op jit(solution)/shard_map/ppermute | solution.py:47
  76.4 12.2 %collective-permute-start.9 = (bf16[64,2048]{1,0:T(8,128)(2,1)S(1)}, bf16[64,2048]{1,0:T(8,128)(2,1)S(1)}, u32[]{:S(2)}, u32[]{:S(2)}) collective-permute-start(bf16[64,2048]{1,0:T(8,128)(2,1)S(1)} %get-tuple-element.144), channel_id=1, source_target_pairs={{0,8},{8,0},{1,9},{9,1},{2,10},{10,2},{3,11},{11,3},{4,12},{12,4},... | collective-permute-start | bytes 786440 | tf_op jit(solution)/shard_map/ppermute | solution.py:47
  83.0 9.2 %collective-permute-start.15 = (bf16[64,4096]{1,0:T(8,128)(2,1)S(1)}, bf16[64,4096]{1,0:T(8,128)(2,1)S(1)}, u32[]{:S(2)}, u32[]{:S(2)}) collective-permute-start(bf16[64,4096]{1,0:T(8,128)(2,1)S(1)} %add_convert_fusion.4), channel_id=1, source_target_pairs={{0,1},{2,0},{4,2},{6,4},{7,6},{5,7},{3,5},{1,3},{8,9},{10,8},{12,1... | collective-permute-start | bytes 1572872 | tf_op jit(solution)/shard_map/ppermute | solution.py:42
  86.6 7.3 %collective-permute-start.11 = (bf16[64,2048]{1,0:T(8,128)(2,1)S(1)}, bf16[64,2048]{1,0:T(8,128)(2,1)S(1)}, u32[]{:S(2)}, u32[]{:S(2)}) collective-permute-start(bf16[64,2048]{1,0:T(8,128)(2,1)S(1)} %get-tuple-element.148), channel_id=1, source_target_pairs={{0,10},{2,12},{4,14},{6,15},{7,13},{5,11},{3,9},{1,8},{8,2},{10,4}... | collective-permute-start | bytes 786440 | tf_op jit(solution)/shard_map/ppermute | solution.py:42
  94.1 16.4 %collective-permute-start.21 = (bf16[384,2048]{1,0:T(8,128)(2,1)S(1)}, bf16[384,2048]{1,0:T(8,128)(2,1)S(1)}, u32[]{:S(2)}, u32[]{:S(2)}) collective-permute-start(bf16[384,2048]{1,0:T(8,128)(2,1)S(1)} %get-tuple-element.129), channel_id=1, source_target_pairs={{0,16},{16,0},{1,17},{17,1},{2,18},{18,2},{3,19},{19,3},{4,20},{20... | collective-permute-start | bytes 4718600 | tf_op jit(solution)/shard_map/ppermute | solution.py:47
  94.2 18.2 %collective-permute-start.22 = (bf16[384,2048]{1,0:T(8,128)(2,1)S(1)}, bf16[384,2048]{1,0:T(8,128)(2,1)S(1)}, u32[]{:S(2)}, u32[]{:S(2)}) collective-permute-start(bf16[384,2048]{1,0:T(8,128)(2,1)S(1)} %get-tuple-element.131), channel_id=1, source_target_pairs={{0,16},{16,0},{1,17},{17,1},{2,18},{18,2},{3,19},{19,3},{4,20},{20... | collective-permute-start | bytes 4718600 | tf_op jit(solution)/shard_map/ppermute | solution.py:47
  94.7 12.0 %collective-permute-start.17 = (bf16[64,4096]{1,0:T(8,128)(2,1)S(1)}, bf16[64,4096]{1,0:T(8,128)(2,1)S(1)}, u32[]{:S(2)}, u32[]{:S(2)}) collective-permute-start(bf16[64,4096]{1,0:T(8,128)(2,1)S(1)} %add_convert_fusion.3), channel_id=1, source_target_pairs={{0,1},{2,0},{4,2},{6,4},{7,6},{5,7},{3,5},{1,3},{8,9},{10,8},{12,1... | collective-permute-start | bytes 1572872 | tf_op jit(solution)/shard_map/ppermute | solution.py:42
  96.4 10.1 %collective-permute-start.18 = (bf16[64,2048]{1,0:T(8,128)(2,1)S(1)}, bf16[64,2048]{1,0:T(8,128)(2,1)S(1)}, u32[]{:S(2)}, u32[]{:S(2)}) collective-permute-start(bf16[64,2048]{1,0:T(8,128)(2,1)S(1)} %get-tuple-element.147), channel_id=1, source_target_pairs={{0,10},{2,12},{4,14},{6,15},{7,13},{5,11},{3,9},{1,8},{8,2},{10,4}... | collective-permute-start | bytes 786440 | tf_op jit(solution)/shard_map/ppermute | solution.py:42
  97.8 16.3 %collective-permute-start.23 = (bf16[384,2048]{1,0:T(8,128)(2,1)S(1)}, bf16[384,2048]{1,0:T(8,128)(2,1)S(1)}, u32[]{:S(2)}, u32[]{:S(2)}) collective-permute-start(bf16[384,2048]{1,0:T(8,128)(2,1)S(1)} %get-tuple-element.133), channel_id=1, source_target_pairs={{0,16},{16,0},{1,17},{17,1},{2,18},{18,2},{3,19},{19,3},{4,20},{20... | collective-permute-start | bytes 4718600 | tf_op jit(solution)/shard_map/ppermute | solution.py:47
  106.8 10.1 %collective-permute-start.20 = (bf16[64,2048]{1,0:T(8,128)(2,1)S(1)}, bf16[64,2048]{1,0:T(8,128)(2,1)S(1)}, u32[]{:S(2)}, u32[]{:S(2)}) collective-permute-start(bf16[64,2048]{1,0:T(8,128)(2,1)S(1)} %get-tuple-element.145), channel_id=1, source_target_pairs={{0,9},{2,8},{4,10},{6,12},{7,14},{5,15},{3,13},{1,11},{8,1},{10,0}... | collective-permute-start | bytes 786440 | tf_op jit(solution)/shard_map/ppermute | solution.py:42
  108.6 12.2 %collective-permute-start.19 = (bf16[64,2048]{1,0:T(8,128)(2,1)S(1)}, bf16[64,2048]{1,0:T(8,128)(2,1)S(1)}, u32[]{:S(2)}, u32[]{:S(2)}) collective-permute-start(bf16[64,2048]{1,0:T(8,128)(2,1)S(1)} %get-tuple-element.146), channel_id=1, source_target_pairs={{0,9},{2,8},{4,10},{6,12},{7,14},{5,15},{3,13},{1,11},{8,1},{10,0}... | collective-permute-start | bytes 786440 | tf_op jit(solution)/shard_map/ppermute | solution.py:42

commit v12 on v8

--- a/solution.py
+++ b/solution.py
@@ -85,7 +85,6 @@
     out_ref[:, 2 * width :] = turned(jnp.concatenate(parts, axis=0)).astype(BF16)
 
 
-LAST = ((1,), (1,))
 PLAIN = ((1,), (0,))
 TILE = 256
 
@@ -137,9 +136,11 @@
     half, width = weights[0].shape
     tokens = blocks[0].shape[0]
     tables = []
-    for i, block in enumerate(blocks):
-        rows[0, i * tokens : (i + 1) * tokens] = block[:, :width]
-        rows[1, i * tokens : (i + 1) * tokens] = block[:, width : 2 * width]
+    for start in range(0, 2 * width, TILE):
+        part, at = divmod(start, width)
+        piece = jnp.concatenate([block[:, start : start + TILE] for block in blocks], axis=0)
+        rows[part, at : at + TILE] = piece.T
+    for block in blocks:
         tables.append(block[:, 2 * width :].astype(F32))
     table = jnp.concatenate(tables, axis=0).T
     expert_of = lax.rem(lax.broadcasted_iota(jnp.int32, table.shape, 0), experts)
@@ -154,9 +155,9 @@
         scale = jnp.where(unit >= e * (half // local_experts), scales[e], scale)
     for side in range(2):
         at = slice(side * half, (side + 1) * half)
-        gate = dot(weights[3 * side][...], rows[0], LAST)
-        up = dot(weights[3 * side + 1][...], rows[0], LAST)
-        back = dot(weights[3 * side + 2][...], rows[1], LAST) * scale
+        gate = dot(weights[3 * side][...], rows[0], PLAIN)
+        up = dot(weights[3 * side + 1][...], rows[0], PLAIN)
+        back = dot(weights[3 * side + 2][...], rows[1], PLAIN) * scale
         sig = 1.0 / (1.0 + jnp.exp(-gate))
         swish = gate * sig
         results = (
@@ -195,7 +196,7 @@
         in_specs=[whole()] * (count + 6),
         out_specs=[whole()] * (count + 3),
         scratch_shapes=[
-            pltpu.VMEM((2, rows, width), BF16),
+            pltpu.VMEM((2, width, rows), BF16),
             pltpu.VMEM((3, rows, units), BF16),
         ],
         compiler_params=pltpu.CompilerParams(vmem_limit_bytes=vmem(experts // local_experts)),

time: 116 us -> 117 us (level)
  no operation moved by 1% of the time
where the time goes in v12:
time: 117 us; the launch traced here: 116 us
  waiting for transfers between devices  50 us (43%)
  Pallas kernels  28.8 us (25%)
  starting transfers between devices  25.7 us (22%)
  other arithmetic  7.15 us (6%)
  local copies, waits for them, and re-layouts  3.97 us (3%)
    ppermute x16, waiting for transfers between devices, ring_shift(): return lax.ppermute(value, ('rep', 'section', 'exp'), pairs)  49.5 us
    ppermute x16, starting transfers between devices, ring_shift(): return lax.ppermute(value, ('rep', 'section', 'exp'), pairs)  21.7 us
    pallas_call x3, Pallas kernels, expert_call(): pl.pallas_call(functools.partial(expert_kernel, count, experts, local_exp...  20.4 us
    convert_element_type x9, other arithmetic, add(): return (a.astype(F32) + b.astype(F32)).astype(BF16)  6.11 us
    pallas_call x1, Pallas kernels, weight_call(): pl.pallas_call(functools.partial(weight_kernel, len(kept), count), out_sh...  5.88 us
    ppermute x8, starting transfers between devices, from_behind(): lax.ppermute(value, axis, [(i, (i + by) % peers) for i in range(peers)])  4 us
    unnamed x8, local copies, waits for them, and re-layouts  3.97 us
  transfers between devices with their start and end apart: 24, of which 15 were waited for; matrix products, arithmetic and copies ran while one was open for 5% of the time, Pallas kernels for 25%

profile of v12, /device:TPU:0, one launch (start us, length us, event | category | flops | bytes accessed | tf_op | source)
XLA Modules:
  0.0 116.4 jit_solution(11810859416028724201)
XLA Ops:
  0.6 0.5 collective-permute-start.3
  1.2 0.1 collective-permute-start.4
  1.2 0.4 collective-permute-start.5
  1.7 2.2 %pack_rows.1.refs_0_ = bf16[64,4224]{1,0:T(8,128)(2,1)} custom-call(bf16[64,2048]{1,0:T(8,128)(2,1)} %bitcast.30, s32[16,64]{1,0:T(8,128)} %bitcast.32, s32[8,64]{1,0:T(8,128)} %bitcast.33, f32[8,64]{1,0:T(8,128)} %bitcast.34, bf16[64,2048]{1,0:T(8,128)(2,1)} %bitcast.31), custom_call_target="tpu_custom_call" | custom-call | tf_op jit(solution)/shard_map/pack_rows/pallas_call | solution.py:275
  3.9 2.7 %collective-permute-start = (bf16[64,4224]{1,0:T(8,128)(2,1)}, bf16[64,4224]{1,0:T(8,128)(2,1)S(1)}, u32[]{:S(2)}, u32[]{:S(2)}) collective-permute-start(bf16[64,4224]{1,0:T(8,128)(2,1)} %pack_rows.1.refs_0_), channel_id=1, source_target_pairs={{0,2},{2,4},{4,6},{6,7},{7,5},{5,3},{3,1},{1,0},{8,10},{10,12},{12... | collective-permute-start | bytes 1622024 | tf_op jit(solution)/shard_map/ppermute | solution.py:42
  6.5 1.4 %copy-done.1 = bf16[1,2,192,2048]{3,2,1,0:T(8,128)(2,1)S(1)} copy-done((bf16[1,2,192,2048]{3,2,1,0:T(8,128)(2,1)S(1)}, bf16[1,2,192,2048]{3,2,1,0:T(8,128)(2,1)}, u32[]{:S(2)}) %copy-start.1) | copy-done | bytes 1572888
  7.9 0.1 load_weights.2.refs_4_.refs_2_
  8.1 1.3 %copy-done.2 = bf16[1,2,192,2048]{3,2,1,0:T(8,128)(2,1)S(1)} copy-done((bf16[1,2,192,2048]{3,2,1,0:T(8,128)(2,1)S(1)}, bf16[1,2,192,2048]{3,2,1,0:T(8,128)(2,1)}, u32[]{:S(2)}) %copy-start.2) | copy-done | bytes 1572888
  9.3 0.5 copy-done.3
  9.8 0.2 load_weights.3
  10.1 0.8 copy-done
  10.9 0.0 collective-permute-start.1
  10.9 5.0 %collective-permute-done.refs_1_ = bf16[64,4224]{1,0:T(8,128)(2,1)S(1)} collective-permute-done((bf16[64,4224]{1,0:T(8,128)(2,1)}, bf16[64,4224]{1,0:T(8,128)(2,1)S(1)}, u32[]{:S(2)}, u32[]{:S(2)}) %collective-permute-start) | collective-permute-done | bytes 540704 | tf_op jit(solution)/shard_map/ppermute | solution.py:42
  15.8 2.4 %collective-permute-start.2 = (bf16[64,4224]{1,0:T(8,128)(2,1)S(1)}, bf16[64,4224]{1,0:T(8,128)(2,1)S(1)}, u32[]{:S(2)}, u32[]{:S(2)}) collective-permute-start(bf16[64,4224]{1,0:T(8,128)(2,1)S(1)} %collective-permute-done.refs_1_), channel_id=1, source_target_pairs={{0,2},{2,4},{4,6},{6,7},{7,5},{5,3},{3,1},{1,0},{8,10},{10,12},{12... | collective-permute-start | bytes 1622024 | tf_op jit(solution)/shard_map/ppermute | solution.py:42
  18.2 5.4 %collective-permute-done.1.refs_2_ = bf16[64,4224]{1,0:T(8,128)(2,1)S(1)} collective-permute-done((bf16[64,4224]{1,0:T(8,128)(2,1)S(1)}, bf16[64,4224]{1,0:T(8,128)(2,1)S(1)}, u32[]{:S(2)}, u32[]{:S(2)}) %collective-permute-start.1) | collective-permute-done | bytes 540704 | tf_op jit(solution)/shard_map/ppermute | solution.py:42
  23.6 0.0 collective-permute-start.8
  23.6 4.6 %collective-permute-done.2.refs_3_ = bf16[64,4224]{1,0:T(8,128)(2,1)S(1)} collective-permute-done((bf16[64,4224]{1,0:T(8,128)(2,1)S(1)}, bf16[64,4224]{1,0:T(8,128)(2,1)S(1)}, u32[]{:S(2)}, u32[]{:S(2)}) %collective-permute-start.2) | collective-permute-done | bytes 540704 | tf_op jit(solution)/shard_map/ppermute | solution.py:42
  28.2 2.5 %collective-permute-start.6 = (bf16[64,4224]{1,0:T(8,128)(2,1)S(1)}, bf16[64,4224]{1,0:T(8,128)(2,1)S(1)}, u32[]{:S(2)}, u32[]{:S(2)}) collective-permute-start(bf16[64,4224]{1,0:T(8,128)(2,1)S(1)} %collective-permute-done.2.refs_3_), channel_id=1, source_target_pairs={{0,2},{2,4},{4,6},{6,7},{7,5},{5,3},{3,1},{1,0},{8,10},{10,12},{12... | collective-permute-start | bytes 1622024 | tf_op jit(solution)/shard_map/ppermute | solution.py:42
  30.7 6.5 %collective-permute-done.8.refs_0_.refs_4_ = bf16[64,4224]{1,0:T(8,128)(2,1)S(1)} collective-permute-done((bf16[64,4224]{1,0:T(8,128)(2,1)S(1)}, bf16[64,4224]{1,0:T(8,128)(2,1)S(1)}, u32[]{:S(2)}, u32[]{:S(2)}) %collective-permute-start.8) | collective-permute-done | bytes 540704 | tf_op jit(solution)/shard_map/ppermute | solution.py:42
  37.1 0.0 collective-permute-start.9
  37.1 0.0 collective-permute-done.5.refs_9_.refs_7_
  37.1 7.7 %expert_rows.3 = (bf16[64,4096]{1,0:T(8,128)(2,1)S(1)}, bf16[64,4096]{1,0:T(8,128)(2,1)S(1)}, bf16[64,4096]{1,0:T(8,128)(2,1)S(1)}, bf16[64,4096]{1,0:T(8,128)(2...) custom-call(bf16[64,4224]{1,0:T(8,128)(2,1)S(1)} %copy-done, ...), custom_call_target="tpu_custom_call" | custom-call | flops 4831838208 | bytes 13631488 | tf_op jit(solution)/shard_map/expert_rows/pallas_call | solution.py:192
  44.9 2.1 %collective-permute-start.7 = (bf16[64,4224]{1,0:T(8,128)(2,1)S(1)}, bf16[64,4224]{1,0:T(8,128)(2,1)S(1)}, u32[]{:S(2)}, u32[]{:S(2)}) collective-permute-start(bf16[64,4224]{1,0:T(8,128)(2,1)S(1)} %collective-permute-done.6.refs_0_.refs_6_), channel_id=1, source_target_pairs={{0,2},{2,4},{4,6},{6,7},{7,5},{5,3},{3,1},{1,0},{8,10},{10,12},{12... | collective-permute-start | bytes 1622024 | tf_op jit(solution)/shard_map/ppermute | solution.py:42
  47.0 2.2 %collective-permute-done.9.refs_1_.refs_5_ = bf16[64,4224]{1,0:T(8,128)(2,1)S(1)} collective-permute-done((bf16[64,4224]{1,0:T(8,128)(2,1)S(1)}, bf16[64,4224]{1,0:T(8,128)(2,1)S(1)}, u32[]{:S(2)}, u32[]{:S(2)}) %collective-permute-start.9) | collective-permute-done | bytes 540704 | tf_op jit(solution)/shard_map/ppermute | solution.py:42
  49.2 6.3 %expert_rows.4 = (bf16[64,4096]{1,0:T(8,128)(2,1)S(1)}, bf16[64,4096]{1,0:T(8,128)(2,1)S(1)}, bf16[768,128]{1,0:T(8,128)(2,1)S(1)}, bf16[768,128]{1,0:T(8,128)(2,1)S(1)}, bf16[768,128]{1,0:T(8,128)(2,1)S(1)}) custom-call(bf16[64,4224]{1,0:T(8,128)(2,1)S(1)} %collective-permute-done.8.refs_0_.refs_4_, ...), custom_call_target="tpu_custom_call" | custom-call | flops 2415919104 | bytes 11534336 | tf_op jit(solution)/shard_map/expert_rows/pallas_call | solution.py:192
  55.5 2.0 %collective-permute-start.11 = (bf16[64,4096]{1,0:T(8,128)(2,1)S(1)}, bf16[64,4096]{1,0:T(8,128)(2,1)S(1)}, u32[]{:S(2)}, u32[]{:S(2)}) collective-permute-start(bf16[64,4096]{1,0:T(8,128)(2,1)S(1)} %get-tuple-element.91), channel_id=1, source_target_pairs={{0,2},{2,4},{4,6},{6,7},{7,5},{5,3},{3,1},{1,0},{8,10},{10,12},{12... | collective-permute-start | bytes 1572872 | tf_op jit(solution)/shard_map/ppermute | solution.py:42
  57.5 0.0 collective-permute-done.7.refs_1_.refs_7_
  57.5 6.3 %expert_rows.5 = (bf16[64,4096]{1,0:T(8,128)(2,1)S(1)}, bf16[64,4096]{1,0:T(8,128)(2,1)S(1)}, bf16[768,128]{1,0:T(8,128)(2,1)S(1)}, bf16[768,128]{1,0:T(8,128)(2,1)S(1)}, bf16[768,128]{1,0:T(8,128)(2,1)S(1)}) custom-call(bf16[64,4224]{1,0:T(8,128)(2,1)S(1)} %collective-permute-done.6.refs_0_.refs_6_, ...), custom_call_target="tpu_custom_call" | custom-call | flops 2415919104 | bytes 11534336 | tf_op jit(solution)/shard_map/expert_rows/pallas_call | solution.py:192
  63.8 0.1 collective-permute-start.14
  64.0 4.1 %collective-permute-done.11 = bf16[64,4096]{1,0:T(8,128)(2,1)S(1)} collective-permute-done((bf16[64,4096]{1,0:T(8,128)(2,1)S(1)}, bf16[64,4096]{1,0:T(8,128)(2,1)S(1)}, u32[]{:S(2)}, u32[]{:S(2)}) %collective-permute-start.11) | collective-permute-done | bytes 524320 | tf_op jit(solution)/shard_map/ppermute | solution.py:42
  68.1 0.1 add_convert_fusion.5
  68.2 2.2 %collective-permute-start.12 = (bf16[64,4096]{1,0:T(8,128)(2,1)S(1)}, bf16[64,4096]{1,0:T(8,128)(2,1)S(1)}, u32[]{:S(2)}, u32[]{:S(2)}) collective-permute-start(bf16[64,4096]{1,0:T(8,128)(2,1)S(1)} %add_convert_fusion.5), channel_id=1, source_target_pairs={{0,2},{2,4},{4,6},{6,7},{7,5},{5,3},{3,1},{1,0},{8,10},{10,12},{12... | collective-permute-start | bytes 1572872 | tf_op jit(solution)/shard_map/ppermute | solution.py:42
  70.3 0.1 add_convert_fusion.11
  70.5 1.6 %collective-permute-start.16 = (bf16[64,2048]{1,0:T(8,128)(2,1)S(1)}, bf16[64,2048]{1,0:T(8,128)(2,1)S(1)}, u32[]{:S(2)}, u32[]{:S(2)}) collective-permute-start(bf16[64,2048]{1,0:T(8,128)(2,1)S(1)} %get-tuple-element.135), channel_id=1, source_target_pairs={{0,8},{8,0},{1,9},{9,1},{2,10},{10,2},{3,11},{11,3},{4,12},{12,4},... | collective-permute-start | bytes 786440 | tf_op jit(solution)/shard_map/ppermute | solution.py:47
  72.1 0.5 collective-permute-start.10
  72.6 1.7 %collective-permute-done.14 = bf16[64,4096]{1,0:T(8,128)(2,1)S(1)} collective-permute-done((bf16[64,4096]{1,0:T(8,128)(2,1)S(1)}, bf16[64,4096]{1,0:T(8,128)(2,1)S(1)}, u32[]{:S(2)}, u32[]{:S(2)}) %collective-permute-start.14) | collective-permute-done | bytes 524320 | tf_op jit(solution)/shard_map/ppermute | solution.py:42
  74.3 0.1 add_convert_fusion.4
  74.4 0.5 collective-permute-start.15
  74.9 5.9 %weight_grads.1 = (bf16[384,2048]{1,0:T(8,128)(2,1)S(1)}, bf16[384,2048]{1,0:T(8,128)(2,1)S(1)}, bf16[384,2048]{1,0:T(8,128)(2,1)S(1)}, bf16[384,2048]{1,0:T(8,1...) custom-call(bf16[64,4224]{1,0:T(8,128)(2,1)S(1)} %copy-done, ...), custom_call_target="tpu_custom_call" | custom-call | flops 4831838208 | bytes 13631488 | tf_op jit(solution)/shard_map/weight_grads/pallas_call | solution.py:243
  80.8 0.5 collective-permute-done.12
  81.3 0.1 add_convert_fusion.10
  81.5 0.0 collective-permute-done.16
  81.5 0.0 collective-permute-done.10
  81.5 2.3 %collective-permute-done.15 = bf16[64,4096]{1,0:T(8,128)(2,1)S(1)} collective-permute-done((bf16[64,4096]{1,0:T(8,128)(2,1)S(1)}, bf16[64,4096]{1,0:T(8,128)(2,1)S(1)}, u32[]{:S(2)}, u32[]{:S(2)}) %collective-permute-start.15) | collective-permute-done | bytes 524320 | tf_op jit(solution)/shard_map/ppermute | solution.py:42
  83.8 0.1 add_convert_fusion.3
  83.9 0.3 collective-permute-start.17
  84.3 2.7 %collective-permute-start.18 = (bf16[64,2048]{1,0:T(8,128)(2,1)S(1)}, bf16[64,2048]{1,0:T(8,128)(2,1)S(1)}, u32[]{:S(2)}, u32[]{:S(2)}) collective-permute-start(bf16[64,2048]{1,0:T(8,128)(2,1)S(1)} %get-tuple-element.139), channel_id=1, source_target_pairs={{0,10},{2,12},{4,14},{6,15},{7,13},{5,11},{3,9},{1,8},{8,2},{10,4}... | collective-permute-start | bytes 786440 | tf_op jit(solution)/shard_map/ppermute | solution.py:42
  86.9 1.5 %collective-permute-start.13 = (bf16[64,2048]{1,0:T(8,128)(2,1)S(1)}, bf16[64,2048]{1,0:T(8,128)(2,1)S(1)}, u32[]{:S(2)}, u32[]{:S(2)}) collective-permute-start(bf16[64,2048]{1,0:T(8,128)(2,1)S(1)} %get-tuple-element.140), channel_id=1, source_target_pairs={{0,10},{2,12},{4,14},{6,15},{7,13},{5,11},{3,9},{1,8},{8,2},{10,4}... | collective-permute-start | bytes 786440 | tf_op jit(solution)/shard_map/ppermute | solution.py:42
  88.5 5.9 %collective-permute-done.18 = bf16[64,2048]{1,0:T(8,128)(2,1)S(1)} collective-permute-done((bf16[64,2048]{1,0:T(8,128)(2,1)S(1)}, bf16[64,2048]{1,0:T(8,128)(2,1)S(1)}, u32[]{:S(2)}, u32[]{:S(2)}) %collective-permute-start.18) | collective-permute-done | bytes 262176 | tf_op jit(solution)/shard_map/ppermute | solution.py:42
  94.4 5.0 %collective-permute-done.13 = bf16[64,2048]{1,0:T(8,128)(2,1)S(1)} collective-permute-done((bf16[64,2048]{1,0:T(8,128)(2,1)S(1)}, bf16[64,2048]{1,0:T(8,128)(2,1)S(1)}, u32[]{:S(2)}, u32[]{:S(2)}) %collective-permute-start.13) | collective-permute-done | bytes 262176 | tf_op jit(solution)/shard_map/ppermute | solution.py:42
  99.4 0.4 collective-permute-start.21
  99.8 0.1 collective-permute-start.22
  99.9 0.4 collective-permute-start.23
  100.3 0.1 add_convert_fusion.8
  100.4 1.7 %collective-permute-start.20 = (bf16[64,2048]{1,0:T(8,128)(2,1)S(1)}, bf16[64,2048]{1,0:T(8,128)(2,1)S(1)}, u32[]{:S(2)}, u32[]{:S(2)}) collective-permute-start(bf16[64,2048]{1,0:T(8,128)(2,1)S(1)} %get-tuple-element.137), channel_id=1, source_target_pairs={{0,9},{2,8},{4,10},{6,12},{7,14},{5,15},{3,13},{1,11},{8,1},{10,0}... | collective-permute-start | bytes 786440 | tf_op jit(solution)/shard_map/ppermute | solution.py:42
  102.1 1.1 collective-permute-start.19
  103.2 1.8 %add_convert_fusion.2 = bf16[384,2048]{1,0:T(8,128)(2,1)} fusion(bf16[384,2048]{1,0:T(8,128)(2,1)S(1)} %collective-permute-done.21, bf16[384,2048]{1,0:T(8,128)(2,1)S(1)} %get-tuple-element.120), kind=kLoop, calls=%fused_computation.2 | loop fusion | flops 3145728 | bytes 4718592 | tf_op jit(solution)/shard_map/convert_element_type | solution.py:261
  105.0 0.1 collective-permute-done.22
  105.1 1.8 %add_convert_fusion.1 = bf16[384,2048]{1,0:T(8,128)(2,1)} fusion(bf16[384,2048]{1,0:T(8,128)(2,1)S(1)} %collective-permute-done.22, bf16[384,2048]{1,0:T(8,128)(2,1)S(1)} %get-tuple-element.122), kind=kLoop, calls=%fused_computation.1 | loop fusion | flops 3145728 | bytes 4718592 | tf_op jit(solution)/shard_map/convert_element_type | solution.py:261
  106.9 0.4 collective-permute-done.23
  107.3 1.7 %add_convert_fusion = bf16[384,2048]{1,0:T(8,128)(2,1)} fusion(bf16[384,2048]{1,0:T(8,128)(2,1)S(1)} %collective-permute-done.23, bf16[384,2048]{1,0:T(8,128)(2,1)S(1)} %get-tuple-element.124), kind=kLoop, calls=%fused_computation | loop fusion | flops 3145728 | bytes 4718592 | tf_op jit(solution)/shard_map/convert_element_type | solution.py:261
  109.1 1.5 %collective-permute-done.20 = bf16[64,2048]{1,0:T(8,128)(2,1)S(1)} collective-permute-done((bf16[64,2048]{1,0:T(8,128)(2,1)S(1)}, bf16[64,2048]{1,0:T(8,128)(2,1)S(1)}, u32[]{:S(2)}, u32[]{:S(2)}) %collective-permute-start.20) | collective-permute-done | bytes 262176 | tf_op jit(solution)/shard_map/ppermute | solution.py:42
  110.5 4.8 %collective-permute-done.19 = bf16[64,2048]{1,0:T(8,128)(2,1)S(1)} collective-permute-done((bf16[64,2048]{1,0:T(8,128)(2,1)S(1)}, bf16[64,2048]{1,0:T(8,128)(2,1)S(1)}, u32[]{:S(2)}, u32[]{:S(2)}) %collective-permute-start.19) | collective-permute-done | bytes 262176 | tf_op jit(solution)/shard_map/ppermute | solution.py:42
  115.3 1.0 fusion
  (9 shorter events, 0.0 us)
Async XLA Ops:
  0.6 36.5 %collective-permute-start.3 = (bf16[384,2048]{1,0:T(8,128)(2,1)}, bf16[384,2048]{1,0:T(8,128)(2,1)S(1)}, u32[]{:S(2)}, u32[]{:S(2)}) collective-permute-start(bf16[384,2048]{1,0:T(8,128)(2,1)} %bitcast.21), channel_id=1, source_target_pairs={{0,16},{16,0},{1,17},{17,1},{2,18},{18,2},{3,19},{19,3},{4,20},{20... | collective-permute-start | bytes 4718600 | tf_op jit(solution)/shard_map/ppermute | solution.py:47
  1.2 36.0 %collective-permute-start.4 = (bf16[384,2048]{1,0:T(8,128)(2,1)}, bf16[384,2048]{1,0:T(8,128)(2,1)S(1)}, u32[]{:S(2)}, u32[]{:S(2)}) collective-permute-start(bf16[384,2048]{1,0:T(8,128)(2,1)} %bitcast.23), channel_id=1, source_target_pairs={{0,16},{16,0},{1,17},{17,1},{2,18},{18,2},{3,19},{19,3},{4,20},{20... | collective-permute-start | bytes 4718600 | tf_op jit(solution)/shard_map/ppermute | solution.py:47
  1.2 35.9 %collective-permute-start.5 = (bf16[384,2048]{1,0:T(8,128)(2,1)}, bf16[384,2048]{1,0:T(8,128)(2,1)}, u32[]{:S(2)}, u32[]{:S(2)}) collective-permute-start(bf16[384,2048]{1,0:T(8,128)(2,1)} %bitcast.25), channel_id=1, source_target_pairs={{0,16},{16,0},{1,17},{17,1},{2,18},{18,2},{3,19},{19,3},{4,20},{20... | collective-permute-start | bytes 4718600 | tf_op jit(solution)/shard_map/ppermute | solution.py:47
  3.9 12.0 %collective-permute-start = (bf16[64,4224]{1,0:T(8,128)(2,1)}, bf16[64,4224]{1,0:T(8,128)(2,1)S(1)}, u32[]{:S(2)}, u32[]{:S(2)}) collective-permute-start(bf16[64,4224]{1,0:T(8,128)(2,1)} %pack_rows.1.refs_0_), channel_id=1, source_target_pairs={{0,2},{2,4},{4,6},{6,7},{7,5},{5,3},{3,1},{1,0},{8,10},{10,12},{12... | collective-permute-start | bytes 1622024 | tf_op jit(solution)/shard_map/ppermute | solution.py:42
  6.5 1.4 %copy-start.1 = (bf16[1,2,192,2048]{3,2,1,0:T(8,128)(2,1)S(1)}, bf16[1,2,192,2048]{3,2,1,0:T(8,128)(2,1)}, u32[]{:S(2)}) copy-start(bf16[1,2,192,2048]{3,2,1,0:T(8,128)(2,1)} %param.13) | copy-start | bytes 4718596
  7.9 1.4 %copy-start.2 = (bf16[1,2,192,2048]{3,2,1,0:T(8,128)(2,1)S(1)}, bf16[1,2,192,2048]{3,2,1,0:T(8,128)(2,1)}, u32[]{:S(2)}) copy-start(bf16[1,2,192,2048]{3,2,1,0:T(8,128)(2,1)} %param.14) | copy-start | bytes 4718596
  7.9 1.9 %copy-start.3 = (bf16[1,2,192,2048]{3,2,1,0:T(8,128)(2,1)S(1)}, bf16[1,2,192,2048]{3,2,1,0:T(8,128)(2,1)}, u32[]{:S(2)}) copy-start(bf16[1,2,192,2048]{3,2,1,0:T(8,128)(2,1)} %param.15) | copy-start | bytes 4718596
  9.8 1.0 copy-start
  10.9 12.7 %collective-permute-start.1 = (bf16[64,4224]{1,0:T(8,128)(2,1)S(1)}, bf16[64,4224]{1,0:T(8,128)(2,1)S(1)}, u32[]{:S(2)}, u32[]{:S(2)}) collective-permute-start(bf16[64,4224]{1,0:T(8,128)(2,1)S(1)} %copy-done), channel_id=1, source_target_pairs={{0,1},{2,0},{4,2},{6,4},{7,6},{5,7},{3,5},{1,3},{8,9},{10,8},{12,1... | collective-permute-start | bytes 1622024 | tf_op jit(solution)/shard_map/ppermute | solution.py:42
  15.8 12.3 %collective-permute-start.2 = (bf16[64,4224]{1,0:T(8,128)(2,1)S(1)}, bf16[64,4224]{1,0:T(8,128)(2,1)S(1)}, u32[]{:S(2)}, u32[]{:S(2)}) collective-permute-start(bf16[64,4224]{1,0:T(8,128)(2,1)S(1)} %collective-permute-done.refs_1_), channel_id=1, source_target_pairs={{0,2},{2,4},{4,6},{6,7},{7,5},{5,3},{3,1},{1,0},{8,10},{10,12},{12... | collective-permute-start | bytes 1622024 | tf_op jit(solution)/shard_map/ppermute | solution.py:42
  23.6 13.5 %collective-permute-start.8 = (bf16[64,4224]{1,0:T(8,128)(2,1)S(1)}, bf16[64,4224]{1,0:T(8,128)(2,1)S(1)}, u32[]{:S(2)}, u32[]{:S(2)}) collective-permute-start(bf16[64,4224]{1,0:T(8,128)(2,1)S(1)} %collective-permute-done.1.refs_2_), channel_id=1, source_target_pairs={{0,1},{2,0},{4,2},{6,4},{7,6},{5,7},{3,5},{1,3},{8,9},{10,8},{12,1... | collective-permute-start | bytes 1622024 | tf_op jit(solution)/shard_map/ppermute | solution.py:42
  28.2 16.7 %collective-permute-start.6 = (bf16[64,4224]{1,0:T(8,128)(2,1)S(1)}, bf16[64,4224]{1,0:T(8,128)(2,1)S(1)}, u32[]{:S(2)}, u32[]{:S(2)}) collective-permute-start(bf16[64,4224]{1,0:T(8,128)(2,1)S(1)} %collective-permute-done.2.refs_3_), channel_id=1, source_target_pairs={{0,2},{2,4},{4,6},{6,7},{7,5},{5,3},{3,1},{1,0},{8,10},{10,12},{12... | collective-permute-start | bytes 1622024 | tf_op jit(solution)/shard_map/ppermute | solution.py:42
  37.1 12.1 %collective-permute-start.9 = (bf16[64,4224]{1,0:T(8,128)(2,1)S(1)}, bf16[64,4224]{1,0:T(8,128)(2,1)S(1)}, u32[]{:S(2)}, u32[]{:S(2)}) collective-permute-start(bf16[64,4224]{1,0:T(8,128)(2,1)S(1)} %collective-permute-done.8.refs_0_.refs_4_), channel_id=1, source_target_pairs={{0,1},{2,0},{4,2},{6,4},{7,6},{5,7},{3,5},{1,3},{8,9},{10,8},{12,1... | collective-permute-start | bytes 1622024 | tf_op jit(solution)/shard_map/ppermute | solution.py:42
  44.9 12.6 %collective-permute-start.7 = (bf16[64,4224]{1,0:T(8,128)(2,1)S(1)}, bf16[64,4224]{1,0:T(8,128)(2,1)S(1)}, u32[]{:S(2)}, u32[]{:S(2)}) collective-permute-start(bf16[64,4224]{1,0:T(8,128)(2,1)S(1)} %collective-permute-done.6.refs_0_.refs_6_), channel_id=1, source_target_pairs={{0,2},{2,4},{4,6},{6,7},{7,5},{5,3},{3,1},{1,0},{8,10},{10,12},{12... | collective-permute-start | bytes 1622024 | tf_op jit(solution)/shard_map/ppermute | solution.py:42
  55.5 12.5 %collective-permute-start.11 = (bf16[64,4096]{1,0:T(8,128)(2,1)S(1)}, bf16[64,4096]{1,0:T(8,128)(2,1)S(1)}, u32[]{:S(2)}, u32[]{:S(2)}) collective-permute-start(bf16[64,4096]{1,0:T(8,128)(2,1)S(1)} %get-tuple-element.91), channel_id=1, source_target_pairs={{0,2},{2,4},{4,6},{6,7},{7,5},{5,3},{3,1},{1,0},{8,10},{10,12},{12... | collective-permute-start | bytes 1572872 | tf_op jit(solution)/shard_map/ppermute | solution.py:42
  63.8 10.4 %collective-permute-start.14 = (bf16[64,4096]{1,0:T(8,128)(2,1)S(1)}, bf16[64,4096]{1,0:T(8,128)(2,1)S(1)}, u32[]{:S(2)}, u32[]{:S(2)}) collective-permute-start(bf16[64,4096]{1,0:T(8,128)(2,1)S(1)} %get-tuple-element.94), channel_id=1, source_target_pairs={{0,1},{2,0},{4,2},{6,4},{7,6},{5,7},{3,5},{1,3},{8,9},{10,8},{12,1... | collective-permute-start | bytes 1572872 | tf_op jit(solution)/shard_map/ppermute | solution.py:42
  68.2 13.2 %collective-permute-start.12 = (bf16[64,4096]{1,0:T(8,128)(2,1)S(1)}, bf16[64,4096]{1,0:T(8,128)(2,1)S(1)}, u32[]{:S(2)}, u32[]{:S(2)}) collective-permute-start(bf16[64,4096]{1,0:T(8,128)(2,1)S(1)} %add_convert_fusion.5), channel_id=1, source_target_pairs={{0,2},{2,4},{4,6},{6,7},{7,5},{5,3},{3,1},{1,0},{8,10},{10,12},{12... | collective-permute-start | bytes 1572872 | tf_op jit(solution)/shard_map/ppermute | solution.py:42
  70.5 11.0 %collective-permute-start.16 = (bf16[64,2048]{1,0:T(8,128)(2,1)S(1)}, bf16[64,2048]{1,0:T(8,128)(2,1)S(1)}, u32[]{:S(2)}, u32[]{:S(2)}) collective-permute-start(bf16[64,2048]{1,0:T(8,128)(2,1)S(1)} %get-tuple-element.135), channel_id=1, source_target_pairs={{0,8},{8,0},{1,9},{9,1},{2,10},{10,2},{3,11},{11,3},{4,12},{12,4},... | collective-permute-start | bytes 786440 | tf_op jit(solution)/shard_map/ppermute | solution.py:47
  72.1 9.4 %collective-permute-start.10 = (bf16[64,2048]{1,0:T(8,128)(2,1)S(1)}, bf16[64,2048]{1,0:T(8,128)(2,1)S(1)}, u32[]{:S(2)}, u32[]{:S(2)}) collective-permute-start(bf16[64,2048]{1,0:T(8,128)(2,1)S(1)} %get-tuple-element.136), channel_id=1, source_target_pairs={{0,8},{8,0},{1,9},{9,1},{2,10},{10,2},{3,11},{11,3},{4,12},{12,4},... | collective-permute-start | bytes 786440 | tf_op jit(solution)/shard_map/ppermute | solution.py:47
  74.4 9.4 %collective-permute-start.15 = (bf16[64,4096]{1,0:T(8,128)(2,1)S(1)}, bf16[64,4096]{1,0:T(8,128)(2,1)S(1)}, u32[]{:S(2)}, u32[]{:S(2)}) collective-permute-start(bf16[64,4096]{1,0:T(8,128)(2,1)S(1)} %add_convert_fusion.4), channel_id=1, source_target_pairs={{0,1},{2,0},{4,2},{6,4},{7,6},{5,7},{3,5},{1,3},{8,9},{10,8},{12,1... | collective-permute-start | bytes 1572872 | tf_op jit(solution)/shard_map/ppermute | solution.py:42
  83.9 15.5 %collective-permute-start.17 = (bf16[64,4096]{1,0:T(8,128)(2,1)S(1)}, bf16[64,4096]{1,0:T(8,128)(2,1)S(1)}, u32[]{:S(2)}, u32[]{:S(2)}) collective-permute-start(bf16[64,4096]{1,0:T(8,128)(2,1)S(1)} %add_convert_fusion.3), channel_id=1, source_target_pairs={{0,1},{2,0},{4,2},{6,4},{7,6},{5,7},{3,5},{1,3},{8,9},{10,8},{12,1... | collective-permute-start | bytes 1572872 | tf_op jit(solution)/shard_map/ppermute | solution.py:42
  84.3 10.1 %collective-permute-start.18 = (bf16[64,2048]{1,0:T(8,128)(2,1)S(1)}, bf16[64,2048]{1,0:T(8,128)(2,1)S(1)}, u32[]{:S(2)}, u32[]{:S(2)}) collective-permute-start(bf16[64,2048]{1,0:T(8,128)(2,1)S(1)} %get-tuple-element.139), channel_id=1, source_target_pairs={{0,10},{2,12},{4,14},{6,15},{7,13},{5,11},{3,9},{1,8},{8,2},{10,4}... | collective-permute-start | bytes 786440 | tf_op jit(solution)/shard_map/ppermute | solution.py:42
  86.9 12.4 %collective-permute-start.13 = (bf16[64,2048]{1,0:T(8,128)(2,1)S(1)}, bf16[64,2048]{1,0:T(8,128)(2,1)S(1)}, u32[]{:S(2)}, u32[]{:S(2)}) collective-permute-start(bf16[64,2048]{1,0:T(8,128)(2,1)S(1)} %get-tuple-element.140), channel_id=1, source_target_pairs={{0,10},{2,12},{4,14},{6,15},{7,13},{5,11},{3,9},{1,8},{8,2},{10,4}... | collective-permute-start | bytes 786440 | tf_op jit(solution)/shard_map/ppermute | solution.py:42
  99.4 3.8 %collective-permute-start.21 = (bf16[384,2048]{1,0:T(8,128)(2,1)S(1)}, bf16[384,2048]{1,0:T(8,128)(2,1)S(1)}, u32[]{:S(2)}, u32[]{:S(2)}) collective-permute-start(bf16[384,2048]{1,0:T(8,128)(2,1)S(1)} %get-tuple-element.121), channel_id=1, source_target_pairs={{0,16},{16,0},{1,17},{17,1},{2,18},{18,2},{3,19},{19,3},{4,20},{20... | collective-permute-start | bytes 4718600 | tf_op jit(solution)/shard_map/ppermute | solution.py:47
  99.8 5.3 %collective-permute-start.22 = (bf16[384,2048]{1,0:T(8,128)(2,1)S(1)}, bf16[384,2048]{1,0:T(8,128)(2,1)S(1)}, u32[]{:S(2)}, u32[]{:S(2)}) collective-permute-start(bf16[384,2048]{1,0:T(8,128)(2,1)S(1)} %get-tuple-element.123), channel_id=1, source_target_pairs={{0,16},{16,0},{1,17},{17,1},{2,18},{18,2},{3,19},{19,3},{4,20},{20... | collective-permute-start | bytes 4718600 | tf_op jit(solution)/shard_map/ppermute | solution.py:47
  99.9 7.4 %collective-permute-start.23 = (bf16[384,2048]{1,0:T(8,128)(2,1)S(1)}, bf16[384,2048]{1,0:T(8,128)(2,1)S(1)}, u32[]{:S(2)}, u32[]{:S(2)}) collective-permute-start(bf16[384,2048]{1,0:T(8,128)(2,1)S(1)} %get-tuple-element.125), channel_id=1, source_target_pairs={{0,16},{16,0},{1,17},{17,1},{2,18},{18,2},{3,19},{19,3},{4,20},{20... | collective-permute-start | bytes 4718600 | tf_op jit(solution)/shard_map/ppermute | solution.py:47
  100.4 10.1 %collective-permute-start.20 = (bf16[64,2048]{1,0:T(8,128)(2,1)S(1)}, bf16[64,2048]{1,0:T(8,128)(2,1)S(1)}, u32[]{:S(2)}, u32[]{:S(2)}) collective-permute-start(bf16[64,2048]{1,0:T(8,128)(2,1)S(1)} %get-tuple-element.137), channel_id=1, source_target_pairs={{0,9},{2,8},{4,10},{6,12},{7,14},{5,15},{3,13},{1,11},{8,1},{10,0}... | collective-permute-start | bytes 786440 | tf_op jit(solution)/shard_map/ppermute | solution.py:42
  102.1 13.2 %collective-permute-start.19 = (bf16[64,2048]{1,0:T(8,128)(2,1)S(1)}, bf16[64,2048]{1,0:T(8,128)(2,1)S(1)}, u32[]{:S(2)}, u32[]{:S(2)}) collective-permute-start(bf16[64,2048]{1,0:T(8,128)(2,1)S(1)} %get-tuple-element.138), channel_id=1, source_target_pairs={{0,9},{2,8},{4,10},{6,12},{7,14},{5,15},{3,13},{1,11},{8,1},{10,0}... | collective-permute-start | bytes 786440 | tf_op jit(solution)/shard_map/ppermute | solution.py:42

commit v13 on v10

--- a/solution.py
+++ b/solution.py
@@ -312,49 +312,54 @@
         if k <= behind:
             held["far", k] = ring_shift(held["far", k - 1], -1)
     work(groups[-2])
+    outs, back = slice(0, width), slice(width, 2 * width)
+    early_far = from_behind(partial["far", 1][:, back], "section", -1)
     arrived = [held[name] for name in groups[-1]]
-    arrived, kept[-1] = tie((arrived, kept[-1]))
+    arrived, kept[-1], early_far = tie((arrived, kept[-1], early_far))
     held.update(zip(groups[-1], arrived))
     work(groups[-1])
+    blocks = [held[name] for group in groups for name in group]
+
+    near_sum = partial["near", ahead]
     far_sum = ring_shift(partial["far", behind], 1)
-    both = (slice(0, width), slice(width, 2 * width))
-    near_sum = partial["near", ahead]
-    own_total = received = None
-    blocks = [held[name] for group in groups for name in group]
-    steps = (1, -1)
-    finals = []
-    here, near_sum = tie((partial["near", 0], near_sum))
-    for part, step in zip(both, steps):
-        kept_here = add(home[:, part], here[:, part])
-        finals.append([from_behind(kept_here, "section", step)])
-    for k in range(ahead, 1, -1):
-        near_sum = ring_shift(near_sum, -1)
-        left = k - 2
-        if left > 1:
-            far_done = far_sum
-            far_sum = ring_shift(add(far_sum, partial["far", left]), 1)
-            near_sum, _ = tie((near_sum, far_done))
-        if k == 3:
-            own_total, other_total = weight_call(blocks, kept, width, peers)
-            here = [final[0] for final in finals]
-            near_sum, own_total, other_total, _ = tie((near_sum, own_total, other_total, here))
-            lasts = [add(far_sum[:, part], partial["far", 1][:, part]) for part in both]
-            for final, last, step in zip(finals, lasts, steps):
-                final.append(ring_shift(last, 1, step))
-            near_sum, _ = tie((near_sum, lasts))
-            near_sum = add(near_sum, partial["near", 2])
-        elif k == 2:
-            here = [final[1] for final in finals]
-            near_sum, other_total, _ = tie((near_sum, other_total, here))
-            received = [from_behind(g, "rep", 1) for g in other_total]
-        elif k > 2:
-            near_sum = add(near_sum, partial["near", k - 1])
-    lasts = [add(near_sum[:, part], partial["near", 1][:, part]) for part in both]
-    for final, last, step in zip(finals, lasts, steps):
-        final.append(ring_shift(last, -1, step))
+    for k in range(ahead, 4, -1):
+        near_sum, far_sum = tie((ring_shift(near_sum, -1), far_sum))
+        near_sum = add(near_sum, partial["near", k - 1])
+        far_sum = ring_shift(add(far_sum, partial["far", k - 2]), 1)
+
+    near_sum = ring_shift(near_sum, -1)
+    here = partial["near", 0]
+    early_near = from_behind(partial["near", 1][:, back], "section", -1)
+    home_back = from_behind(add(home[:, back], here[:, back]), "section", -1)
+    own_total, other_total = weight_call(blocks, kept, width, peers)
+    near_sum, far_sum, early_near, home_back, own_total, other_total, here = tie(
+        (near_sum, far_sum, early_near, home_back, own_total, other_total, here)
+    )
+
+    near_sum = ring_shift(add(near_sum, partial["near", 3]), -1)
+    far_outs = ring_shift(add(far_sum[:, outs], partial["far", 2][:, outs]), 1)
+    far_back = ring_shift(add(far_sum[:, back], partial["far", 2][:, back]), 1, -1)
+    home_outs = from_behind(add(home[:, outs], here[:, outs]), "section", 1)
+    near_sum, far_outs, far_back, home_outs = tie((near_sum, far_outs, far_back, home_outs))
+
+    near_outs = add(near_sum[:, outs], partial["near", 2][:, outs])
+    near_back = add(near_sum[:, back], partial["near", 2][:, back])
+    far_outs = add(far_outs, partial["far", 1][:, outs])
+    far_back = add(far_back, early_far)
+    near_outs, near_back, other_total = tie((near_outs, near_back, other_total))
+    received = [from_behind(g, "rep", 1) for g in other_total]
+    near_outs, near_back = ring_shift(near_outs, -1), ring_shift(near_back, -1, -1)
+    far_outs, far_back = ring_shift(far_outs, 1, 1), ring_shift(far_back, 1)
+    near_outs, near_back, far_outs, far_back = tie((near_outs, near_back, far_outs, far_back))
+
+    near_outs = ring_shift(add(near_outs, partial["near", 1][:, outs]), -1, 1)
+    near_back = ring_shift(add(near_back, early_near), -1)
     totals = [add(a, b) for a, b in zip(own_total, received)]
-    finals, totals = tie((finals, totals))
-    results = [sum(f.astype(F32) for f in final).astype(BF16)[None] for final in finals]
+    near_outs, near_back, totals = tie((near_outs, near_back, totals))
+    results = [
+        sum(f.astype(F32) for f in final).astype(BF16)[None]
+        for final in ((home_outs, near_outs, far_outs), (home_back, near_back, far_back))
+    ]
     shape = (1, local_experts, half_units, width)
     return tuple(results) + tuple(t.reshape(shape) for t in totals)
 

time: 122 us -> 123 us (level)
  starting transfers between devices: 24.6 us -> 29.8 us
  waiting for transfers between devices: 57 us -> 52.2 us
    ppermute x16 -> x18, waiting for transfers between devices: 49.7 us -> 45.6 us  [ring_shift(): return lax.ppermute(value, ('rep', 'section', 'exp'), pairs)]
    ppermute x16 -> x18, starting transfers between devices: 21 us -> 24.7 us  [ring_shift(): return lax.ppermute(value, ('rep', 'section', 'exp'), pairs)]
    ppermute x8 -> x10, starting transfers between devices: 3.63 us -> 5.1 us  [from_behind(): lax.ppermute(value, axis, [(i, (i + by) % peers) for i in range(peers)])]
    ppermute x8 -> x10, waiting for transfers between devices: 7.36 us -> 6.62 us  [from_behind(): lax.ppermute(value, axis, [(i, (i + by) % peers) for i in range(peers)])]
    convert_element_type x9 -> x12, other arithmetic: 6.05 us -> 6.13 us  [add(): return (a.astype(F32) + b.astype(F32)).astype(BF16)]
  transfers between devices with their start and end apart: 24 -> 28, of which waited for: 15 -> 13; matrix products, arithmetic and copies ran while one was open for 5% -> 5% of each run, Pallas kernels for 18% -> 18%
where the time goes in v13:
time: 123 us; the launch traced here: 122 us
  waiting for transfers between devices  52.2 us (42%)
  starting transfers between devices  29.8 us (24%)
  Pallas kernels  28.6 us (23%)
  other arithmetic  7.16 us (6%)
  local copies, waits for them, and re-layouts  4.01 us (3%)
    ppermute x18, waiting for transfers between devices, ring_shift(): return lax.ppermute(value, ('rep', 'section', 'exp'), pairs)  45.6 us
    ppermute x18, starting transfers between devices, ring_shift(): return lax.ppermute(value, ('rep', 'section', 'exp'), pairs)  24.7 us
    pallas_call x3, Pallas kernels, expert_call(): pl.pallas_call(functools.partial(expert_kernel, count, experts, local_exp...  20.1 us
    ppermute x10, waiting for transfers between devices, from_behind(): lax.ppermute(value, axis, [(i, (i + by) % peers) for i in range(peers)])  6.62 us
    convert_element_type x12, other arithmetic, add(): return (a.astype(F32) + b.astype(F32)).astype(BF16)  6.13 us
    pallas_call x1, Pallas kernels, weight_call(): pl.pallas_call(functools.partial(weight_kernel, len(kept), count), out_sh...  5.88 us
    ppermute x10, starting transfers between devices, from_behind(): lax.ppermute(value, axis, [(i, (i + by) % peers) for i in range(peers)])  5.1 us
    unnamed x8, local copies, waits for them, and re-layouts  3.97 us
  transfers between devices with their start and end apart: 28, of which 13 were waited for; matrix products, arithmetic and copies ran while one was open for 5% of the time, Pallas kernels for 18%

profile of v13, /device:TPU:0, one launch (start us, length us, event | category | flops | bytes accessed | tf_op | source)
XLA Modules:
  0.0 122.5 jit_solution(18356262101256910501)
XLA Ops:
  0.6 0.5 collective-permute-start.4
  1.2 0.1 collective-permute-start.5
  1.2 0.4 collective-permute-start.6
  1.7 2.2 %pack_rows.1.refs_0_ = bf16[64,4224]{1,0:T(8,128)(2,1)} custom-call(bf16[64,2048]{1,0:T(8,128)(2,1)} %bitcast.30, s32[16,64]{1,0:T(8,128)} %bitcast.32, s32[8,64]{1,0:T(8,128)} %bitcast.33, f32[8,64]{1,0:T(8,128)} %bitcast.34, bf16[64,2048]{1,0:T(8,128)(2,1)} %bitcast.31), custom_call_target="tpu_custom_call" | custom-call | tf_op jit(solution)/shard_map/pack_rows/pallas_call | solution.py:274
  3.9 2.7 %collective-permute-start.2 = (bf16[64,4224]{1,0:T(8,128)(2,1)}, bf16[64,4224]{1,0:T(8,128)(2,1)S(1)}, u32[]{:S(2)}, u32[]{:S(2)}) collective-permute-start(bf16[64,4224]{1,0:T(8,128)(2,1)} %pack_rows.1.refs_0_), channel_id=1, source_target_pairs={{0,2},{2,4},{4,6},{6,7},{7,5},{5,3},{3,1},{1,0},{8,10},{10,12},{12... | collective-permute-start | bytes 1622024 | tf_op jit(solution)/shard_map/ppermute | solution.py:42
  6.5 1.4 %copy-done.1 = bf16[1,2,192,2048]{3,2,1,0:T(8,128)(2,1)S(1)} copy-done((bf16[1,2,192,2048]{3,2,1,0:T(8,128)(2,1)S(1)}, bf16[1,2,192,2048]{3,2,1,0:T(8,128)(2,1)}, u32[]{:S(2)}) %copy-start.1) | copy-done | bytes 1572888
  7.9 0.1 load_weights.2.refs_4_.refs_2_
  8.1 1.3 %copy-done.2 = bf16[1,2,192,2048]{3,2,1,0:T(8,128)(2,1)S(1)} copy-done((bf16[1,2,192,2048]{3,2,1,0:T(8,128)(2,1)S(1)}, bf16[1,2,192,2048]{3,2,1,0:T(8,128)(2,1)}, u32[]{:S(2)}) %copy-start.2) | copy-done | bytes 1572888
  9.3 0.5 copy-done.3
  9.8 0.2 load_weights.3
  10.1 0.8 copy-done
  10.9 0.0 collective-permute-start
  10.9 5.0 %collective-permute-done.2.refs_1_ = bf16[64,4224]{1,0:T(8,128)(2,1)S(1)} collective-permute-done((bf16[64,4224]{1,0:T(8,128)(2,1)}, bf16[64,4224]{1,0:T(8,128)(2,1)S(1)}, u32[]{:S(2)}, u32[]{:S(2)}) %collective-permute-start.2) | collective-permute-done | bytes 540704 | tf_op jit(solution)/shard_map/ppermute | solution.py:42
  15.8 2.4 %collective-permute-start.3 = (bf16[64,4224]{1,0:T(8,128)(2,1)S(1)}, bf16[64,4224]{1,0:T(8,128)(2,1)S(1)}, u32[]{:S(2)}, u32[]{:S(2)}) collective-permute-start(bf16[64,4224]{1,0:T(8,128)(2,1)S(1)} %collective-permute-done.2.refs_1_), channel_id=1, source_target_pairs={{0,2},{2,4},{4,6},{6,7},{7,5},{5,3},{3,1},{1,0},{8,10},{10,12},{12... | collective-permute-start | bytes 1622024 | tf_op jit(solution)/shard_map/ppermute | solution.py:42
  18.2 5.4 %collective-permute-done.refs_2_ = bf16[64,4224]{1,0:T(8,128)(2,1)S(1)} collective-permute-done((bf16[64,4224]{1,0:T(8,128)(2,1)S(1)}, bf16[64,4224]{1,0:T(8,128)(2,1)S(1)}, u32[]{:S(2)}, u32[]{:S(2)}) %collective-permute-start) | collective-permute-done | bytes 540704 | tf_op jit(solution)/shard_map/ppermute | solution.py:42
  23.6 0.0 collective-permute-start.1
  23.6 4.6 %collective-permute-done.3.refs_3_ = bf16[64,4224]{1,0:T(8,128)(2,1)S(1)} collective-permute-done((bf16[64,4224]{1,0:T(8,128)(2,1)S(1)}, bf16[64,4224]{1,0:T(8,128)(2,1)S(1)}, u32[]{:S(2)}, u32[]{:S(2)}) %collective-permute-start.3) | collective-permute-done | bytes 540704 | tf_op jit(solution)/shard_map/ppermute | solution.py:42
  28.2 2.5 %collective-permute-start.8 = (bf16[64,4224]{1,0:T(8,128)(2,1)S(1)}, bf16[64,4224]{1,0:T(8,128)(2,1)S(1)}, u32[]{:S(2)}, u32[]{:S(2)}) collective-permute-start(bf16[64,4224]{1,0:T(8,128)(2,1)S(1)} %collective-permute-done.3.refs_3_), channel_id=1, source_target_pairs={{0,2},{2,4},{4,6},{6,7},{7,5},{5,3},{3,1},{1,0},{8,10},{10,12},{12... | collective-permute-start | bytes 1622024 | tf_op jit(solution)/shard_map/ppermute | solution.py:42
  30.7 7.7 %expert_rows.3 = (bf16[64,4096]{1,0:T(8,128)(2,1)S(1)}, bf16[64,4096]{1,0:T(8,128)(2,1)S(1)}, bf16[64,4096]{1,0:T(8,128)(2,1)S(1)}, bf16[64,4096]{1,0:T(8,128)(2...) custom-call(bf16[64,4224]{1,0:T(8,128)(2,1)S(1)} %copy-done, ...), custom_call_target="tpu_custom_call" | custom-call | flops 4831838208 | bytes 13631488 | tf_op jit(solution)/shard_map/expert_rows/pallas_call | solution.py:191
  38.4 0.1 collective-permute-start.7
  38.5 0.8 collective-permute-done.8.refs_1_.refs_5_
  39.2 2.5 %collective-permute-start.9 = (bf16[64,4224]{1,0:T(8,128)(2,1)S(1)}, bf16[64,4224]{1,0:T(8,128)(2,1)S(1)}, u32[]{:S(2)}, u32[]{:S(2)}) collective-permute-start(bf16[64,4224]{1,0:T(8,128)(2,1)S(1)} %collective-permute-done.8.refs_1_.refs_5_), channel_id=1, source_target_pairs={{0,2},{2,4},{4,6},{6,7},{7,5},{5,3},{3,1},{1,0},{8,10},{10,12},{12... | collective-permute-start | bytes 1622024 | tf_op jit(solution)/shard_map/ppermute | solution.py:42
  41.8 1.2 %collective-permute-start.10 = (bf16[64,2048]{1,0:T(8,128)(2,1)S(1)}, bf16[64,2048]{1,0:T(8,128)(2,1)S(1)}, u32[]{:S(2)}, u32[]{:S(2)}) collective-permute-start(bf16[64,2048]{1,0:T(8,128)(2,1)S(1)} %slice.48), channel_id=1, source_target_pairs={{0,8},{8,0},{1,9},{9,1},{2,10},{10,2},{3,11},{11,3},{4,12},{12,4},... | collective-permute-start | bytes 786440 | tf_op jit(solution)/shard_map/ppermute | solution.py:47
  43.0 6.2 %expert_rows.4 = (bf16[64,4096]{1,0:T(8,128)(2,1)S(1)}, bf16[64,4096]{1,0:T(8,128)(2,1)S(1)}, bf16[768,128]{1,0:T(8,128)(2,1)S(1)}, bf16[768,128]{1,0:T(8,128)(2,1)S(1)}, bf16[768,128]{1,0:T(8,128)(2,1)S(1)}) custom-call(bf16[64,4224]{1,0:T(8,128)(2,1)S(1)} %collective-permute-done.1.refs_0_.refs_4_, ...), custom_call_target="tpu_custom_call" | custom-call | flops 2415919104 | bytes 11534336 | tf_op jit(solution)/shard_map/expert_rows/pallas_call | solution.py:191
  49.2 3.7 %collective-permute-done.7.refs_0_.refs_6_ = bf16[64,4224]{1,0:T(8,128)(2,1)S(1)} collective-permute-done((bf16[64,4224]{1,0:T(8,128)(2,1)S(1)}, bf16[64,4224]{1,0:T(8,128)(2,1)S(1)}, u32[]{:S(2)}, u32[]{:S(2)}) %collective-permute-start.7) | collective-permute-done | bytes 540704 | tf_op jit(solution)/shard_map/ppermute | solution.py:42
  53.0 6.2 %expert_rows.5 = (bf16[64,4096]{1,0:T(8,128)(2,1)S(1)}, bf16[64,4096]{1,0:T(8,128)(2,1)S(1)}, bf16[768,128]{1,0:T(8,128)(2,1)S(1)}, bf16[768,128]{1,0:T(8,128)(2,1)S(1)}, bf16[768,128]{1,0:T(8,128)(2,1)S(1)}) custom-call(bf16[64,4224]{1,0:T(8,128)(2,1)S(1)} %collective-permute-done.7.refs_0_.refs_6_, ...), custom_call_target="tpu_custom_call" | custom-call | flops 2415919104 | bytes 11534336 | tf_op jit(solution)/shard_map/expert_rows/pallas_call | solution.py:191
  59.2 0.1 collective-permute-start.11
  59.3 1.9 %collective-permute-start.12 = (bf16[64,4096]{1,0:T(8,128)(2,1)S(1)}, bf16[64,4096]{1,0:T(8,128)(2,1)S(1)}, u32[]{:S(2)}, u32[]{:S(2)}) collective-permute-start(bf16[64,4096]{1,0:T(8,128)(2,1)S(1)} %get-tuple-element.98), channel_id=1, source_target_pairs={{0,2},{2,4},{4,6},{6,7},{7,5},{5,3},{3,1},{1,0},{8,10},{10,12},{12... | collective-permute-start | bytes 1572872 | tf_op jit(solution)/shard_map/ppermute | solution.py:42
  61.3 0.1 add_convert_fusion.15
  61.3 1.6 %collective-permute-start.14 = (bf16[64,2048]{1,0:T(8,128)(2,1)S(1)}, bf16[64,2048]{1,0:T(8,128)(2,1)S(1)}, u32[]{:S(2)}, u32[]{:S(2)}) collective-permute-start(bf16[64,2048]{1,0:T(8,128)(2,1)S(1)} %add_convert_fusion.15), channel_id=1, source_target_pairs={{0,8},{8,0},{1,9},{9,1},{2,10},{10,2},{3,11},{11,3},{4,12},{12,4},... | collective-permute-start | bytes 786440 | tf_op jit(solution)/shard_map/ppermute | solution.py:47
  62.9 0.6 collective-permute-start.13
  63.5 5.9 %weight_grads.1 = (bf16[384,2048]{1,0:T(8,128)(2,1)S(1)}, bf16[384,2048]{1,0:T(8,128)(2,1)S(1)}, bf16[384,2048]{1,0:T(8,128)(2,1)S(1)}, bf16[384,2048]{1,0:T(8,1...) custom-call(bf16[64,4224]{1,0:T(8,128)(2,1)S(1)} %copy-done, ...), custom_call_target="tpu_custom_call" | custom-call | flops 4831838208 | bytes 13631488 | tf_op jit(solution)/shard_map/weight_grads/pallas_call | solution.py:242
  69.4 1.2 %collective-permute-done.14 = bf16[64,2048]{1,0:T(8,128)(2,1)S(1)} collective-permute-done((bf16[64,2048]{1,0:T(8,128)(2,1)S(1)}, bf16[64,2048]{1,0:T(8,128)(2,1)S(1)}, u32[]{:S(2)}, u32[]{:S(2)}) %collective-permute-start.14) | collective-permute-done | bytes 262176 | tf_op jit(solution)/shard_map/ppermute | solution.py:47
  70.6 3.9 %collective-permute-done.13 = bf16[64,2048]{1,0:T(8,128)(2,1)S(1)} collective-permute-done((bf16[64,2048]{1,0:T(8,128)(2,1)S(1)}, bf16[64,2048]{1,0:T(8,128)(2,1)S(1)}, u32[]{:S(2)}, u32[]{:S(2)}) %collective-permute-start.13) | collective-permute-done | bytes 262176 | tf_op jit(solution)/shard_map/ppermute | solution.py:47
  74.5 0.0 collective-permute-done.11
  74.5 0.1 add_convert_fusion.13
  74.6 1.8 %collective-permute-start.16 = (bf16[64,2048]{1,0:T(8,128)(2,1)S(1)}, bf16[64,2048]{1,0:T(8,128)(2,1)S(1)}, u32[]{:S(2)}, u32[]{:S(2)}) collective-permute-start(bf16[64,2048]{1,0:T(8,128)(2,1)S(1)} %get-tuple-element.152), channel_id=1, source_target_pairs={{0,2},{2,4},{4,6},{6,7},{7,5},{5,3},{3,1},{1,0},{8,10},{10,12},{12... | collective-permute-start | bytes 786440 | tf_op jit(solution)/shard_map/ppermute | solution.py:42
  76.4 2.5 %collective-permute-start.17 = (bf16[64,2048]{1,0:T(8,128)(2,1)S(1)}, bf16[64,2048]{1,0:T(8,128)(2,1)S(1)}, u32[]{:S(2)}, u32[]{:S(2)}) collective-permute-start(bf16[64,2048]{1,0:T(8,128)(2,1)S(1)} %get-tuple-element.151), channel_id=1, source_target_pairs={{0,10},{2,12},{4,14},{6,15},{7,13},{5,11},{3,9},{1,8},{8,2},{10,4}... | collective-permute-start | bytes 786440 | tf_op jit(solution)/shard_map/ppermute | solution.py:42
  79.0 0.1 add_convert_fusion.3
  79.1 0.5 collective-permute-start.15
  79.6 0.1 add_convert_fusion.12
  79.6 0.6 collective-permute-start.18
  80.2 3.6 %collective-permute-done.16 = bf16[64,2048]{1,0:T(8,128)(2,1)S(1)} collective-permute-done((bf16[64,2048]{1,0:T(8,128)(2,1)S(1)}, bf16[64,2048]{1,0:T(8,128)(2,1)S(1)}, u32[]{:S(2)}, u32[]{:S(2)}) %collective-permute-start.16) | collective-permute-done | bytes 262176 | tf_op jit(solution)/shard_map/ppermute | solution.py:42
  83.8 5.7 %collective-permute-done.17 = bf16[64,2048]{1,0:T(8,128)(2,1)S(1)} collective-permute-done((bf16[64,2048]{1,0:T(8,128)(2,1)S(1)}, bf16[64,2048]{1,0:T(8,128)(2,1)S(1)}, u32[]{:S(2)}, u32[]{:S(2)}) %collective-permute-start.17) | collective-permute-done | bytes 262176 | tf_op jit(solution)/shard_map/ppermute | solution.py:42
  89.5 1.5 %collective-permute-done.18 = bf16[64,2048]{1,0:T(8,128)(2,1)S(1)} collective-permute-done((bf16[64,2048]{1,0:T(8,128)(2,1)S(1)}, bf16[64,2048]{1,0:T(8,128)(2,1)S(1)}, u32[]{:S(2)}, u32[]{:S(2)}) %collective-permute-start.18) | collective-permute-done | bytes 262176 | tf_op jit(solution)/shard_map/ppermute | solution.py:47
  91.0 0.1 add_convert_fusion.10
  91.1 0.1 collective-permute-start.27
  91.2 0.1 add_convert_fusion.8
  91.3 2.0 %collective-permute-start.22 = (bf16[64,2048]{1,0:T(8,128)(2,1)S(1)}, bf16[64,2048]{1,0:T(8,128)(2,1)S(1)}, u32[]{:S(2)}, u32[]{:S(2)}) collective-permute-start(bf16[64,2048]{1,0:T(8,128)(2,1)S(1)} %add_convert_fusion.8), channel_id=1, source_target_pairs={{0,2},{2,4},{4,6},{6,7},{7,5},{5,3},{3,1},{1,0},{8,10},{10,12},{12... | collective-permute-start | bytes 786440 | tf_op jit(solution)/shard_map/ppermute | solution.py:42
  93.2 0.1 add_convert_fusion.9
  93.3 1.2 collective-permute-start.21
  94.5 0.8 collective-permute-start.19
  95.3 1.2 %collective-permute-start.20 = (bf16[64,2048]{1,0:T(8,128)(2,1)S(1)}, bf16[64,2048]{1,0:T(8,128)(2,1)S(1)}, u32[]{:S(2)}, u32[]{:S(2)}) collective-permute-start(bf16[64,2048]{1,0:T(8,128)(2,1)S(1)} %get-tuple-element.128), channel_id=1, source_target_pairs={{0,9},{2,8},{4,10},{6,12},{7,14},{5,15},{3,13},{1,11},{8,1},{10,0}... | collective-permute-start | bytes 786440 | tf_op jit(solution)/shard_map/ppermute | solution.py:42
  96.6 3.4 %collective-permute-done.22 = bf16[64,2048]{1,0:T(8,128)(2,1)S(1)} collective-permute-done((bf16[64,2048]{1,0:T(8,128)(2,1)S(1)}, bf16[64,2048]{1,0:T(8,128)(2,1)S(1)}, u32[]{:S(2)}, u32[]{:S(2)}) %collective-permute-start.22) | collective-permute-done | bytes 262176 | tf_op jit(solution)/shard_map/ppermute | solution.py:42
  100.0 8.9 %collective-permute-done.21 = bf16[64,2048]{1,0:T(8,128)(2,1)S(1)} collective-permute-done((bf16[64,2048]{1,0:T(8,128)(2,1)S(1)}, bf16[64,2048]{1,0:T(8,128)(2,1)S(1)}, u32[]{:S(2)}, u32[]{:S(2)}) %collective-permute-start.21) | collective-permute-done | bytes 262176 | tf_op jit(solution)/shard_map/ppermute | solution.py:42
  109.0 0.1 add_convert_fusion.6
  109.0 0.2 collective-permute-start.24
  109.3 0.1 add_convert_fusion.7
  109.4 2.2 %collective-permute-start.23 = (bf16[64,2048]{1,0:T(8,128)(2,1)S(1)}, bf16[64,2048]{1,0:T(8,128)(2,1)S(1)}, u32[]{:S(2)}, u32[]{:S(2)}) collective-permute-start(bf16[64,2048]{1,0:T(8,128)(2,1)S(1)} %add_convert_fusion.7), channel_id=1, source_target_pairs={{0,9},{2,8},{4,10},{6,12},{7,14},{5,15},{3,13},{1,11},{8,1},{10,0}... | collective-permute-start | bytes 786440 | tf_op jit(solution)/shard_map/ppermute | solution.py:42
  111.6 1.7 %add_convert_fusion = bf16[384,2048]{1,0:T(8,128)(2,1)} fusion(bf16[384,2048]{1,0:T(8,128)(2,1)S(1)} %collective-permute-done.27, bf16[384,2048]{1,0:T(8,128)(2,1)S(1)} %get-tuple-element.139), kind=kLoop, calls=%fused_computation | loop fusion | flops 3145728 | bytes 4718592 | tf_op jit(solution)/shard_map/convert_element_type | solution.py:260
  113.3 1.8 %add_convert_fusion.1 = bf16[384,2048]{1,0:T(8,128)(2,1)} fusion(bf16[384,2048]{1,0:T(8,128)(2,1)S(1)} %collective-permute-done.26, bf16[384,2048]{1,0:T(8,128)(2,1)S(1)} %get-tuple-element.137), kind=kLoop, calls=%fused_computation.1 | loop fusion | flops 3145728 | bytes 4718592 | tf_op jit(solution)/shard_map/convert_element_type | solution.py:260
  115.2 1.8 %add_convert_fusion.2 = bf16[384,2048]{1,0:T(8,128)(2,1)} fusion(bf16[384,2048]{1,0:T(8,128)(2,1)S(1)} %collective-permute-done.25, bf16[384,2048]{1,0:T(8,128)(2,1)S(1)} %get-tuple-element.135), kind=kLoop, calls=%fused_computation.2 | loop fusion | flops 3145728 | bytes 4718592 | tf_op jit(solution)/shard_map/convert_element_type | solution.py:260
  117.0 4.5 %collective-permute-done.23 = bf16[64,2048]{1,0:T(8,128)(2,1)S(1)} collective-permute-done((bf16[64,2048]{1,0:T(8,128)(2,1)S(1)}, bf16[64,2048]{1,0:T(8,128)(2,1)S(1)}, u32[]{:S(2)}, u32[]{:S(2)}) %collective-permute-start.23) | collective-permute-done | bytes 262176 | tf_op jit(solution)/shard_map/ppermute | solution.py:42
  121.5 1.0 fusion
  (22 shorter events, 0.1 us)
Async XLA Ops:
  0.6 30.0 %collective-permute-start.4 = (bf16[384,2048]{1,0:T(8,128)(2,1)}, bf16[384,2048]{1,0:T(8,128)(2,1)S(1)}, u32[]{:S(2)}, u32[]{:S(2)}) collective-permute-start(bf16[384,2048]{1,0:T(8,128)(2,1)} %bitcast.21), channel_id=1, source_target_pairs={{0,16},{16,0},{1,17},{17,1},{2,18},{18,2},{3,19},{19,3},{4,20},{20... | collective-permute-start | bytes 4718600 | tf_op jit(solution)/shard_map/ppermute | solution.py:47
  1.2 29.5 %collective-permute-start.5 = (bf16[384,2048]{1,0:T(8,128)(2,1)}, bf16[384,2048]{1,0:T(8,128)(2,1)S(1)}, u32[]{:S(2)}, u32[]{:S(2)}) collective-permute-start(bf16[384,2048]{1,0:T(8,128)(2,1)} %bitcast.23), channel_id=1, source_target_pairs={{0,16},{16,0},{1,17},{17,1},{2,18},{18,2},{3,19},{19,3},{4,20},{20... | collective-permute-start | bytes 4718600 | tf_op jit(solution)/shard_map/ppermute | solution.py:47
  1.2 29.4 %collective-permute-start.6 = (bf16[384,2048]{1,0:T(8,128)(2,1)}, bf16[384,2048]{1,0:T(8,128)(2,1)}, u32[]{:S(2)}, u32[]{:S(2)}) collective-permute-start(bf16[384,2048]{1,0:T(8,128)(2,1)} %bitcast.25), channel_id=1, source_target_pairs={{0,16},{16,0},{1,17},{17,1},{2,18},{18,2},{3,19},{19,3},{4,20},{20... | collective-permute-start | bytes 4718600 | tf_op jit(solution)/shard_map/ppermute | solution.py:47
  3.9 12.0 %collective-permute-start.2 = (bf16[64,4224]{1,0:T(8,128)(2,1)}, bf16[64,4224]{1,0:T(8,128)(2,1)S(1)}, u32[]{:S(2)}, u32[]{:S(2)}) collective-permute-start(bf16[64,4224]{1,0:T(8,128)(2,1)} %pack_rows.1.refs_0_), channel_id=1, source_target_pairs={{0,2},{2,4},{4,6},{6,7},{7,5},{5,3},{3,1},{1,0},{8,10},{10,12},{12... | collective-permute-start | bytes 1622024 | tf_op jit(solution)/shard_map/ppermute | solution.py:42
  6.5 1.4 %copy-start.1 = (bf16[1,2,192,2048]{3,2,1,0:T(8,128)(2,1)S(1)}, bf16[1,2,192,2048]{3,2,1,0:T(8,128)(2,1)}, u32[]{:S(2)}) copy-start(bf16[1,2,192,2048]{3,2,1,0:T(8,128)(2,1)} %param.13) | copy-start | bytes 4718596
  7.9 1.4 %copy-start.2 = (bf16[1,2,192,2048]{3,2,1,0:T(8,128)(2,1)S(1)}, bf16[1,2,192,2048]{3,2,1,0:T(8,128)(2,1)}, u32[]{:S(2)}) copy-start(bf16[1,2,192,2048]{3,2,1,0:T(8,128)(2,1)} %param.14) | copy-start | bytes 4718596
  7.9 1.9 %copy-start.3 = (bf16[1,2,192,2048]{3,2,1,0:T(8,128)(2,1)S(1)}, bf16[1,2,192,2048]{3,2,1,0:T(8,128)(2,1)}, u32[]{:S(2)}) copy-start(bf16[1,2,192,2048]{3,2,1,0:T(8,128)(2,1)} %param.15) | copy-start | bytes 4718596
  9.8 1.0 copy-start
  10.9 12.7 %collective-permute-start = (bf16[64,4224]{1,0:T(8,128)(2,1)S(1)}, bf16[64,4224]{1,0:T(8,128)(2,1)S(1)}, u32[]{:S(2)}, u32[]{:S(2)}) collective-permute-start(bf16[64,4224]{1,0:T(8,128)(2,1)S(1)} %copy-done), channel_id=1, source_target_pairs={{0,1},{2,0},{4,2},{6,4},{7,6},{5,7},{3,5},{1,3},{8,9},{10,8},{12,1... | collective-permute-start | bytes 1622024 | tf_op jit(solution)/shard_map/ppermute | solution.py:42
  15.8 12.3 %collective-permute-start.3 = (bf16[64,4224]{1,0:T(8,128)(2,1)S(1)}, bf16[64,4224]{1,0:T(8,128)(2,1)S(1)}, u32[]{:S(2)}, u32[]{:S(2)}) collective-permute-start(bf16[64,4224]{1,0:T(8,128)(2,1)S(1)} %collective-permute-done.2.refs_1_), channel_id=1, source_target_pairs={{0,2},{2,4},{4,6},{6,7},{7,5},{5,3},{3,1},{1,0},{8,10},{10,12},{12... | collective-permute-start | bytes 1622024 | tf_op jit(solution)/shard_map/ppermute | solution.py:42
  23.6 14.8 %collective-permute-start.1 = (bf16[64,4224]{1,0:T(8,128)(2,1)S(1)}, bf16[64,4224]{1,0:T(8,128)(2,1)S(1)}, u32[]{:S(2)}, u32[]{:S(2)}) collective-permute-start(bf16[64,4224]{1,0:T(8,128)(2,1)S(1)} %collective-permute-done.refs_2_), channel_id=1, source_target_pairs={{0,1},{2,0},{4,2},{6,4},{7,6},{5,7},{3,5},{1,3},{8,9},{10,8},{12,1... | collective-permute-start | bytes 1622024 | tf_op jit(solution)/shard_map/ppermute | solution.py:42
  28.2 11.1 %collective-permute-start.8 = (bf16[64,4224]{1,0:T(8,128)(2,1)S(1)}, bf16[64,4224]{1,0:T(8,128)(2,1)S(1)}, u32[]{:S(2)}, u32[]{:S(2)}) collective-permute-start(bf16[64,4224]{1,0:T(8,128)(2,1)S(1)} %collective-permute-done.3.refs_3_), channel_id=1, source_target_pairs={{0,2},{2,4},{4,6},{6,7},{7,5},{5,3},{3,1},{1,0},{8,10},{10,12},{12... | collective-permute-start | bytes 1622024 | tf_op jit(solution)/shard_map/ppermute | solution.py:42
  38.4 14.6 %collective-permute-start.7 = (bf16[64,4224]{1,0:T(8,128)(2,1)S(1)}, bf16[64,4224]{1,0:T(8,128)(2,1)S(1)}, u32[]{:S(2)}, u32[]{:S(2)}) collective-permute-start(bf16[64,4224]{1,0:T(8,128)(2,1)S(1)} %collective-permute-done.1.refs_0_.refs_4_), channel_id=1, source_target_pairs={{0,1},{2,0},{4,2},{6,4},{7,6},{5,7},{3,5},{1,3},{8,9},{10,8},{12,1... | collective-permute-start | bytes 1622024 | tf_op jit(solution)/shard_map/ppermute | solution.py:42
  39.2 13.7 %collective-permute-start.9 = (bf16[64,4224]{1,0:T(8,128)(2,1)S(1)}, bf16[64,4224]{1,0:T(8,128)(2,1)S(1)}, u32[]{:S(2)}, u32[]{:S(2)}) collective-permute-start(bf16[64,4224]{1,0:T(8,128)(2,1)S(1)} %collective-permute-done.8.refs_1_.refs_5_), channel_id=1, source_target_pairs={{0,2},{2,4},{4,6},{6,7},{7,5},{5,3},{3,1},{1,0},{8,10},{10,12},{12... | collective-permute-start | bytes 1622024 | tf_op jit(solution)/shard_map/ppermute | solution.py:42
  41.8 7.5 %collective-permute-start.10 = (bf16[64,2048]{1,0:T(8,128)(2,1)S(1)}, bf16[64,2048]{1,0:T(8,128)(2,1)S(1)}, u32[]{:S(2)}, u32[]{:S(2)}) collective-permute-start(bf16[64,2048]{1,0:T(8,128)(2,1)S(1)} %slice.48), channel_id=1, source_target_pairs={{0,8},{8,0},{1,9},{9,1},{2,10},{10,2},{3,11},{11,3},{4,12},{12,4},... | collective-permute-start | bytes 786440 | tf_op jit(solution)/shard_map/ppermute | solution.py:47
  59.2 15.3 %collective-permute-start.11 = (bf16[64,4096]{1,0:T(8,128)(2,1)S(1)}, bf16[64,4096]{1,0:T(8,128)(2,1)S(1)}, u32[]{:S(2)}, u32[]{:S(2)}) collective-permute-start(bf16[64,4096]{1,0:T(8,128)(2,1)S(1)} %get-tuple-element.97), channel_id=1, source_target_pairs={{0,1},{2,0},{4,2},{6,4},{7,6},{5,7},{3,5},{1,3},{8,9},{10,8},{12,1... | collective-permute-start | bytes 1572872 | tf_op jit(solution)/shard_map/ppermute | solution.py:42
  59.3 15.2 %collective-permute-start.12 = (bf16[64,4096]{1,0:T(8,128)(2,1)S(1)}, bf16[64,4096]{1,0:T(8,128)(2,1)S(1)}, u32[]{:S(2)}, u32[]{:S(2)}) collective-permute-start(bf16[64,4096]{1,0:T(8,128)(2,1)S(1)} %get-tuple-element.98), channel_id=1, source_target_pairs={{0,2},{2,4},{4,6},{6,7},{7,5},{5,3},{3,1},{1,0},{8,10},{10,12},{12... | collective-permute-start | bytes 1572872 | tf_op jit(solution)/shard_map/ppermute | solution.py:42
  61.3 9.3 %collective-permute-start.14 = (bf16[64,2048]{1,0:T(8,128)(2,1)S(1)}, bf16[64,2048]{1,0:T(8,128)(2,1)S(1)}, u32[]{:S(2)}, u32[]{:S(2)}) collective-permute-start(bf16[64,2048]{1,0:T(8,128)(2,1)S(1)} %add_convert_fusion.15), channel_id=1, source_target_pairs={{0,8},{8,0},{1,9},{9,1},{2,10},{10,2},{3,11},{11,3},{4,12},{12,4},... | collective-permute-start | bytes 786440 | tf_op jit(solution)/shard_map/ppermute | solution.py:47
  62.9 11.5 %collective-permute-start.13 = (bf16[64,2048]{1,0:T(8,128)(2,1)S(1)}, bf16[64,2048]{1,0:T(8,128)(2,1)S(1)}, u32[]{:S(2)}, u32[]{:S(2)}) collective-permute-start(bf16[64,2048]{1,0:T(8,128)(2,1)S(1)} %slice.49), channel_id=1, source_target_pairs={{0,8},{8,0},{1,9},{9,1},{2,10},{10,2},{3,11},{11,3},{4,12},{12,4},... | collective-permute-start | bytes 786440 | tf_op jit(solution)/shard_map/ppermute | solution.py:47
  74.6 9.2 %collective-permute-start.16 = (bf16[64,2048]{1,0:T(8,128)(2,1)S(1)}, bf16[64,2048]{1,0:T(8,128)(2,1)S(1)}, u32[]{:S(2)}, u32[]{:S(2)}) collective-permute-start(bf16[64,2048]{1,0:T(8,128)(2,1)S(1)} %get-tuple-element.152), channel_id=1, source_target_pairs={{0,2},{2,4},{4,6},{6,7},{7,5},{5,3},{3,1},{1,0},{8,10},{10,12},{12... | collective-permute-start | bytes 786440 | tf_op jit(solution)/shard_map/ppermute | solution.py:42
  76.4 13.0 %collective-permute-start.17 = (bf16[64,2048]{1,0:T(8,128)(2,1)S(1)}, bf16[64,2048]{1,0:T(8,128)(2,1)S(1)}, u32[]{:S(2)}, u32[]{:S(2)}) collective-permute-start(bf16[64,2048]{1,0:T(8,128)(2,1)S(1)} %get-tuple-element.151), channel_id=1, source_target_pairs={{0,10},{2,12},{4,14},{6,15},{7,13},{5,11},{3,9},{1,8},{8,2},{10,4}... | collective-permute-start | bytes 786440 | tf_op jit(solution)/shard_map/ppermute | solution.py:42
  79.1 11.9 %collective-permute-start.15 = (bf16[64,4096]{1,0:T(8,128)(2,1)S(1)}, bf16[64,4096]{1,0:T(8,128)(2,1)S(1)}, u32[]{:S(2)}, u32[]{:S(2)}) collective-permute-start(bf16[64,4096]{1,0:T(8,128)(2,1)S(1)} %add_convert_fusion.3), channel_id=1, source_target_pairs={{0,1},{2,0},{4,2},{6,4},{7,6},{5,7},{3,5},{1,3},{8,9},{10,8},{12,1... | collective-permute-start | bytes 1572872 | tf_op jit(solution)/shard_map/ppermute | solution.py:42
  79.6 11.3 %collective-permute-start.18 = (bf16[64,2048]{1,0:T(8,128)(2,1)S(1)}, bf16[64,2048]{1,0:T(8,128)(2,1)S(1)}, u32[]{:S(2)}, u32[]{:S(2)}) collective-permute-start(bf16[64,2048]{1,0:T(8,128)(2,1)S(1)} %add_convert_fusion.12), channel_id=1, source_target_pairs={{0,8},{8,0},{1,9},{9,1},{2,10},{10,2},{3,11},{11,3},{4,12},{12,4},... | collective-permute-start | bytes 786440 | tf_op jit(solution)/shard_map/ppermute | solution.py:47
  91.1 20.5 %collective-permute-start.27 = (bf16[384,2048]{1,0:T(8,128)(2,1)S(1)}, bf16[384,2048]{1,0:T(8,128)(2,1)S(1)}, u32[]{:S(2)}, u32[]{:S(2)}) collective-permute-start(bf16[384,2048]{1,0:T(8,128)(2,1)S(1)} %get-tuple-element.140), channel_id=1, source_target_pairs={{0,16},{16,0},{1,17},{17,1},{2,18},{18,2},{3,19},{19,3},{4,20},{20... | collective-permute-start | bytes 4718600 | tf_op jit(solution)/shard_map/ppermute | solution.py:47
  91.3 8.8 %collective-permute-start.22 = (bf16[64,2048]{1,0:T(8,128)(2,1)S(1)}, bf16[64,2048]{1,0:T(8,128)(2,1)S(1)}, u32[]{:S(2)}, u32[]{:S(2)}) collective-permute-start(bf16[64,2048]{1,0:T(8,128)(2,1)S(1)} %add_convert_fusion.8), channel_id=1, source_target_pairs={{0,2},{2,4},{4,6},{6,7},{7,5},{5,3},{3,1},{1,0},{8,10},{10,12},{12... | collective-permute-start | bytes 786440 | tf_op jit(solution)/shard_map/ppermute | solution.py:42
  93.3 15.7 %collective-permute-start.21 = (bf16[64,2048]{1,0:T(8,128)(2,1)S(1)}, bf16[64,2048]{1,0:T(8,128)(2,1)S(1)}, u32[]{:S(2)}, u32[]{:S(2)}) collective-permute-start(bf16[64,2048]{1,0:T(8,128)(2,1)S(1)} %add_convert_fusion.9), channel_id=1, source_target_pairs={{0,10},{2,12},{4,14},{6,15},{7,13},{5,11},{3,9},{1,8},{8,2},{10,4}... | collective-permute-start | bytes 786440 | tf_op jit(solution)/shard_map/ppermute | solution.py:42
  94.5 14.4 %collective-permute-start.19 = (bf16[64,2048]{1,0:T(8,128)(2,1)S(1)}, bf16[64,2048]{1,0:T(8,128)(2,1)S(1)}, u32[]{:S(2)}, u32[]{:S(2)}) collective-permute-start(bf16[64,2048]{1,0:T(8,128)(2,1)S(1)} %get-tuple-element.127), channel_id=1, source_target_pairs={{0,1},{2,0},{4,2},{6,4},{7,6},{5,7},{3,5},{1,3},{8,9},{10,8},{12,1... | collective-permute-start | bytes 786440 | tf_op jit(solution)/shard_map/ppermute | solution.py:42
  95.3 13.6 %collective-permute-start.20 = (bf16[64,2048]{1,0:T(8,128)(2,1)S(1)}, bf16[64,2048]{1,0:T(8,128)(2,1)S(1)}, u32[]{:S(2)}, u32[]{:S(2)}) collective-permute-start(bf16[64,2048]{1,0:T(8,128)(2,1)S(1)} %get-tuple-element.128), channel_id=1, source_target_pairs={{0,9},{2,8},{4,10},{6,12},{7,14},{5,15},{3,13},{1,11},{8,1},{10,0}... | collective-permute-start | bytes 786440 | tf_op jit(solution)/shard_map/ppermute | solution.py:42
  100.0 13.3 %collective-permute-start.26 = (bf16[384,2048]{1,0:T(8,128)(2,1)S(1)}, bf16[384,2048]{1,0:T(8,128)(2,1)S(1)}, u32[]{:S(2)}, u32[]{:S(2)}) collective-permute-start(bf16[384,2048]{1,0:T(8,128)(2,1)S(1)} %get-tuple-element.138), channel_id=1, source_target_pairs={{0,16},{16,0},{1,17},{17,1},{2,18},{18,2},{3,19},{19,3},{4,20},{20... | collective-permute-start | bytes 4718600 | tf_op jit(solution)/shard_map/ppermute | solution.py:47
  109.0 6.2 %collective-permute-start.25 = (bf16[384,2048]{1,0:T(8,128)(2,1)S(1)}, bf16[384,2048]{1,0:T(8,128)(2,1)S(1)}, u32[]{:S(2)}, u32[]{:S(2)}) collective-permute-start(bf16[384,2048]{1,0:T(8,128)(2,1)S(1)} %get-tuple-element.136), channel_id=1, source_target_pairs={{0,16},{16,0},{1,17},{17,1},{2,18},{18,2},{3,19},{19,3},{4,20},{20... | collective-permute-start | bytes 4718600 | tf_op jit(solution)/shard_map/ppermute | solution.py:47
  109.0 7.9 %collective-permute-start.24 = (bf16[64,2048]{1,0:T(8,128)(2,1)S(1)}, bf16[64,2048]{1,0:T(8,128)(2,1)S(1)}, u32[]{:S(2)}, u32[]{:S(2)}) collective-permute-start(bf16[64,2048]{1,0:T(8,128)(2,1)S(1)} %add_convert_fusion.6), channel_id=1, source_target_pairs={{0,1},{2,0},{4,2},{6,4},{7,6},{5,7},{3,5},{1,3},{8,9},{10,8},{12,1... | collective-permute-start | bytes 786440 | tf_op jit(solution)/shard_map/ppermute | solution.py:42
  109.4 12.1 %collective-permute-start.23 = (bf16[64,2048]{1,0:T(8,128)(2,1)S(1)}, bf16[64,2048]{1,0:T(8,128)(2,1)S(1)}, u32[]{:S(2)}, u32[]{:S(2)}) collective-permute-start(bf16[64,2048]{1,0:T(8,128)(2,1)S(1)} %add_convert_fusion.7), channel_id=1, source_target_pairs={{0,9},{2,8},{4,10},{6,12},{7,14},{5,15},{3,13},{1,11},{8,1},{10,0}... | collective-permute-start | bytes 786440 | tf_op jit(solution)/shard_map/ppermute | solution.py:42

commit v14 on v11

--- a/solution.py
+++ b/solution.py
@@ -289,8 +289,9 @@
     for k in range(1, ahead + 1):
         names += [("near", k), ("far", k)]
     names = names[: 2 * ahead]
-    groups = [names[i : i + 4] for i in range(0, len(names) - 4, 4)]
-    groups += [[name for name in names[-4:] if name[0] == way] for way in ("far", "near")]
+    groups = [names[i : i + 2] for i in range(0, len(names) - 4, 2)]
+    groups.append([name for name in names[-4:] if name[0] == "far"])
+    groups.append([name for name in names[-4:] if name[0] == "near"])
     held = {("near", 0): home, ("far", 0): tie((home, own))[0]}
     partial, kept = {}, []
 
@@ -306,8 +307,8 @@
         if k == 1:
             held["near", 1], own = tie((held["near", 1], own))
             weights[:3] = own
-        if k % 2 == 1 and k > 1:
-            work(groups[(k - 3) // 2])
+        elif k <= behind:
+            work(groups[k - 2])
             held["far", k - 1], kept[-1] = tie((held["far", k - 1], kept[-1]))
         if k <= behind:
             held["far", k] = ring_shift(held["far", k - 1], -1)
@@ -316,12 +317,12 @@
     held["near", ahead], kept[-1] = tie((held["near", ahead], kept[-1]))
     work(groups[-1])
     both = (slice(0, width), slice(width, 2 * width))
-    near_sum = partial["near", ahead]
+    near_sum, far_sum = tie((partial["near", ahead], far_sum))
     own_total = received = None
     blocks = [held[name] for group in groups for name in group]
     steps = (1, -1)
     finals = []
-    here, far_sum = tie((partial["near", 0], far_sum))
+    here, near_sum = tie((partial["near", 0], near_sum))
     for part, step in zip(both, steps):
         kept_here = add(home[:, part], here[:, part])
         finals.append([from_behind(kept_here, "section", step)])
@@ -329,8 +330,7 @@
         near_sum = ring_shift(near_sum, -1)
         left = k - 2
         if left > 1:
-            far_done = far_sum
-            far_next = add(far_sum, partial["far", left])
+            far_done, far_next = far_sum, add(far_sum, partial["far", left])
             far_sum = ring_shift(far_next, 1)
             near_sum, _ = tie((near_sum, far_done))
         if k == 4:
@@ -344,11 +344,10 @@
             here = [final[0] for final in finals] + finals[0][1:]
             near_sum, _ = tie((near_sum, here))
             near_sum = add(near_sum, partial["near", 2])
-            near_sum, other_total = tie((near_sum, other_total))
-            received = [from_behind(g, "rep", 1) for g in other_total]
         elif k == 2:
             here = [final[1] for final in finals]
-            near_sum, _ = tie((near_sum, here))
+            near_sum, other_total, _ = tie((near_sum, other_total, here))
+            received = [from_behind(g, "rep", 1) for g in other_total]
         elif k > 2:
             near_sum = add(near_sum, partial["near", k - 1])
     lasts = [add(near_sum[:, part], partial["near", 1][:, part]) for part in both]

time: 122 us -> 124 us (1.016)
  Pallas kernels: 28.6 us -> 33.4 us
  waiting for transfers between devices: 54.6 us -> 53 us
    pallas_call x3 -> x4, Pallas kernels: 20.1 us -> 24.8 us  [expert_call(): pl.pallas_call(functools.partial(expert_kernel, count, experts, local_exp...]
    ppermute x16, waiting for transfers between devices: 54.5 us -> 50.8 us  [ring_shift(): return lax.ppermute(value, ('rep', 'section', 'exp'), pairs)]
    ppermute x8, waiting for transfers between devices: 0.02 us -> 2.21 us  [from_behind(): lax.ppermute(value, axis, [(i, (i + by) % peers) for i in range(peers)])]
  transfers between devices with their start and end apart: 24 -> 24, of which waited for: 13 -> 17; matrix products, arithmetic and copies ran while one was open for 5% -> 5% of each run, Pallas kernels for 23% -> 27%
where the time goes in v14:
time: 124 us
  waiting for transfers between devices  53 us (43%)
  Pallas kernels  33.4 us (27%)
  starting transfers between devices  25.7 us (21%)
  other arithmetic  7.15 us (6%)
  local copies, waits for them, and re-layouts  3.97 us (3%)
    ppermute x16, waiting for transfers between devices, ring_shift(): return lax.ppermute(value, ('rep', 'section', 'exp'), pairs)  50.8 us
    pallas_call x4, Pallas kernels, expert_call(): pl.pallas_call(functools.partial(expert_kernel, count, experts, local_exp...  24.8 us
    ppermute x16, starting transfers between devices, ring_shift(): return lax.ppermute(value, ('rep', 'section', 'exp'), pairs)  22.1 us
    convert_element_type x9, other arithmetic, add(): return (a.astype(F32) + b.astype(F32)).astype(BF16)  6.11 us
    pallas_call x1, Pallas kernels, weight_call(): pl.pallas_call(functools.partial(weight_kernel, len(kept), count), out_sh...  5.99 us
    unnamed x8, local copies, waits for them, and re-layouts  3.97 us
    ppermute x8, starting transfers between devices, from_behind(): lax.ppermute(value, axis, [(i, (i + by) % peers) for i in range(peers)])  3.57 us
  transfers between devices with their start and end apart: 24, of which 17 were waited for; matrix products, arithmetic and copies ran while one was open for 5% of the time, Pallas kernels for 27%

profile of v14, /device:TPU:0, one launch (start us, length us, event | category | flops | bytes accessed | tf_op | source)
XLA Modules:
  0.0 124.0 jit_solution(6586623129426956502)
XLA Ops:
  0.6 0.5 collective-permute-start.1
  1.2 0.1 collective-permute-start.2
  1.2 0.4 collective-permute-start.3
  1.7 2.2 %pack_rows.1.refs_0_ = bf16[64,4224]{1,0:T(8,128)(2,1)} custom-call(bf16[64,2048]{1,0:T(8,128)(2,1)} %bitcast.30, s32[16,64]{1,0:T(8,128)} %bitcast.32, s32[8,64]{1,0:T(8,128)} %bitcast.33, f32[8,64]{1,0:T(8,128)} %bitcast.34, bf16[64,2048]{1,0:T(8,128)(2,1)} %bitcast.31), custom_call_target="tpu_custom_call" | custom-call | tf_op jit(solution)/shard_map/pack_rows/pallas_call | solution.py:274
  3.9 2.7 %collective-permute-start = (bf16[64,4224]{1,0:T(8,128)(2,1)}, bf16[64,4224]{1,0:T(8,128)(2,1)S(1)}, u32[]{:S(2)}, u32[]{:S(2)}) collective-permute-start(bf16[64,4224]{1,0:T(8,128)(2,1)} %pack_rows.1.refs_0_), channel_id=1, source_target_pairs={{0,2},{2,4},{4,6},{6,7},{7,5},{5,3},{3,1},{1,0},{8,10},{10,12},{12... | collective-permute-start | bytes 1622024 | tf_op jit(solution)/shard_map/ppermute | solution.py:42
  6.5 1.4 %copy-done.1 = bf16[1,2,192,2048]{3,2,1,0:T(8,128)(2,1)S(1)} copy-done((bf16[1,2,192,2048]{3,2,1,0:T(8,128)(2,1)S(1)}, bf16[1,2,192,2048]{3,2,1,0:T(8,128)(2,1)}, u32[]{:S(2)}) %copy-start.1) | copy-done | bytes 1572888
  7.9 0.1 load_weights.2.refs_2_
  8.1 1.3 %copy-done.2 = bf16[1,2,192,2048]{3,2,1,0:T(8,128)(2,1)S(1)} copy-done((bf16[1,2,192,2048]{3,2,1,0:T(8,128)(2,1)S(1)}, bf16[1,2,192,2048]{3,2,1,0:T(8,128)(2,1)}, u32[]{:S(2)}) %copy-start.2) | copy-done | bytes 1572888
  9.3 0.5 copy-done.3
  9.8 0.2 load_weights.3
  10.1 0.8 copy-done
  10.9 0.0 collective-permute-start.7
  10.9 5.0 %collective-permute-done.refs_1_ = bf16[64,4224]{1,0:T(8,128)(2,1)S(1)} collective-permute-done((bf16[64,4224]{1,0:T(8,128)(2,1)}, bf16[64,4224]{1,0:T(8,128)(2,1)S(1)}, u32[]{:S(2)}, u32[]{:S(2)}) %collective-permute-start) | collective-permute-done | bytes 540704 | tf_op jit(solution)/shard_map/ppermute | solution.py:42
  15.8 2.4 %collective-permute-start.4 = (bf16[64,4224]{1,0:T(8,128)(2,1)S(1)}, bf16[64,4224]{1,0:T(8,128)(2,1)S(1)}, u32[]{:S(2)}, u32[]{:S(2)}) collective-permute-start(bf16[64,4224]{1,0:T(8,128)(2,1)S(1)} %collective-permute-done.refs_1_), channel_id=1, source_target_pairs={{0,2},{2,4},{4,6},{6,7},{7,5},{5,3},{3,1},{1,0},{8,10},{10,12},{12... | collective-permute-start | bytes 1622024 | tf_op jit(solution)/shard_map/ppermute | solution.py:42
  18.2 0.0 collective-permute-done.1.refs_5_
  18.2 6.2 %expert_rows.4 = (bf16[64,4096]{1,0:T(8,128)(2,1)S(1)}, bf16[64,4096]{1,0:T(8,128)(2,1)S(1)}, bf16[768,128]{1,0:T(8,128)(2,1)S(1)}, bf16[768,128]{1,0:T(8,128)(2,1)S(1)}, bf16[768,128]{1,0:T(8,128)(2,1)S(1)}) custom-call(bf16[64,4224]{1,0:T(8,128)(2,1)S(1)} %copy-done, bf16[64,4224]{1,0:T(8,128)(2,1)S(1)} %collective-permute-done.refs_1_, ...), custom_call_target="tpu_custom_call" | custom-call | flops 2415919104 | bytes 11534336 | tf_op jit(solution)/shard_map/expert_rows/pallas_call | solution.py:191
  24.5 0.1 collective-permute-start.8
  24.5 2.8 %collective-permute-done.4.refs_1_.refs_3_ = bf16[64,4224]{1,0:T(8,128)(2,1)S(1)} collective-permute-done((bf16[64,4224]{1,0:T(8,128)(2,1)S(1)}, bf16[64,4224]{1,0:T(8,128)(2,1)S(1)}, u32[]{:S(2)}, u32[]{:S(2)}) %collective-permute-start.4) | collective-permute-done | bytes 540704 | tf_op jit(solution)/shard_map/ppermute | solution.py:42
  27.4 2.5 %collective-permute-start.5 = (bf16[64,4224]{1,0:T(8,128)(2,1)S(1)}, bf16[64,4224]{1,0:T(8,128)(2,1)S(1)}, u32[]{:S(2)}, u32[]{:S(2)}) collective-permute-start(bf16[64,4224]{1,0:T(8,128)(2,1)S(1)} %collective-permute-done.4.refs_1_.refs_3_), channel_id=1, source_target_pairs={{0,2},{2,4},{4,6},{6,7},{7,5},{5,3},{3,1},{1,0},{8,10},{10,12},{12... | collective-permute-start | bytes 1622024 | tf_op jit(solution)/shard_map/ppermute | solution.py:42
  29.8 6.2 %expert_rows.5 = (bf16[64,4096]{1,0:T(8,128)(2,1)S(1)}, bf16[64,4096]{1,0:T(8,128)(2,1)S(1)}, bf16[768,128]{1,0:T(8,128)(2,1)S(1)}, bf16[768,128]{1,0:T(8,128)(2,1)S(1)}, bf16[768,128]{1,0:T(8,128)(2,1)S(1)}) custom-call(bf16[64,4224]{1,0:T(8,128)(2,1)S(1)} %collective-permute-done.7.refs_0_.refs_2_, ...), custom_call_target="tpu_custom_call" | custom-call | flops 2415919104 | bytes 11534336 | tf_op jit(solution)/shard_map/expert_rows/pallas_call | solution.py:191
  36.1 3.1 %collective-permute-done.8.refs_0_.refs_4_ = bf16[64,4224]{1,0:T(8,128)(2,1)S(1)} collective-permute-done((bf16[64,4224]{1,0:T(8,128)(2,1)S(1)}, bf16[64,4224]{1,0:T(8,128)(2,1)S(1)}, u32[]{:S(2)}, u32[]{:S(2)}) %collective-permute-start.8) | collective-permute-done | bytes 540704 | tf_op jit(solution)/shard_map/ppermute | solution.py:42
  39.2 0.1 collective-permute-done.5.refs_0_.refs_6_
  39.3 2.7 %collective-permute-start.6 = (bf16[64,4224]{1,0:T(8,128)(2,1)S(1)}, bf16[64,4224]{1,0:T(8,128)(2,1)S(1)}, u32[]{:S(2)}, u32[]{:S(2)}) collective-permute-start(bf16[64,4224]{1,0:T(8,128)(2,1)S(1)} %collective-permute-done.5.refs_0_.refs_6_), channel_id=1, source_target_pairs={{0,2},{2,4},{4,6},{6,7},{7,5},{5,3},{3,1},{1,0},{8,10},{10,12},{12... | collective-permute-start | bytes 1622024 | tf_op jit(solution)/shard_map/ppermute | solution.py:42
  42.0 12.3 %collective-permute-done.9.refs_1_.refs_5_ = bf16[64,4224]{1,0:T(8,128)(2,1)S(1)} collective-permute-done((bf16[64,4224]{1,0:T(8,128)(2,1)S(1)}, bf16[64,4224]{1,0:T(8,128)(2,1)S(1)}, u32[]{:S(2)}, u32[]{:S(2)}) %collective-permute-start.9) | collective-permute-done | bytes 540704 | tf_op jit(solution)/shard_map/ppermute | solution.py:42
  54.3 6.2 %expert_rows.6 = (bf16[64,4096]{1,0:T(8,128)(2,1)S(1)}, bf16[64,4096]{1,0:T(8,128)(2,1)S(1)}, bf16[768,128]{1,0:T(8,128)(2,1)S(1)}, bf16[768,128]{1,0:T(8,128)(2,1)S(1)}, bf16[768,128]{1,0:T(8,128)(2,1)S(1)}) custom-call(bf16[64,4224]{1,0:T(8,128)(2,1)S(1)} %collective-permute-done.8.refs_0_.refs_4_, ...), custom_call_target="tpu_custom_call" | custom-call | flops 2415919104 | bytes 11534336 | tf_op jit(solution)/shard_map/expert_rows/pallas_call | solution.py:191
  60.5 1.2 collective-permute-start.10
  61.7 0.0 collective-permute-done.6.refs_1_.refs_7_
  61.7 6.2 %expert_rows.7 = (bf16[64,4096]{1,0:T(8,128)(2,1)S(1)}, bf16[64,4096]{1,0:T(8,128)(2,1)S(1)}, bf16[768,128]{1,0:T(8,128)(2,1)S(1)}, bf16[768,128]{1,0:T(8,128)(2,1)S(1)}, bf16[768,128]{1,0:T(8,128)(2,1)S(1)}) custom-call(bf16[64,4224]{1,0:T(8,128)(2,1)S(1)} %collective-permute-done.5.refs_0_.refs_6_, ...), custom_call_target="tpu_custom_call" | custom-call | flops 2415919104 | bytes 11534336 | tf_op jit(solution)/shard_map/expert_rows/pallas_call | solution.py:191
  67.9 5.3 %collective-permute-done.10 = bf16[64,4096]{1,0:T(8,128)(2,1)S(1)} collective-permute-done((bf16[64,4096]{1,0:T(8,128)(2,1)S(1)}, bf16[64,4096]{1,0:T(8,128)(2,1)S(1)}, u32[]{:S(2)}, u32[]{:S(2)}) %collective-permute-start.10) | collective-permute-done | bytes 524320 | tf_op jit(solution)/shard_map/ppermute | solution.py:42
  73.3 0.6 collective-permute-start.14
  73.9 0.1 add_convert_fusion.5
  74.0 0.1 add_convert_fusion.11
  74.2 1.8 %collective-permute-start.12 = (bf16[64,4096]{1,0:T(8,128)(2,1)S(1)}, bf16[64,4096]{1,0:T(8,128)(2,1)S(1)}, u32[]{:S(2)}, u32[]{:S(2)}) collective-permute-start(bf16[64,4096]{1,0:T(8,128)(2,1)S(1)} %add_convert_fusion.5), channel_id=1, source_target_pairs={{0,2},{2,4},{4,6},{6,7},{7,5},{5,3},{3,1},{1,0},{8,10},{10,12},{12... | collective-permute-start | bytes 1572872 | tf_op jit(solution)/shard_map/ppermute | solution.py:42
  76.0 2.0 %collective-permute-start.16 = (bf16[64,2048]{1,0:T(8,128)(2,1)S(1)}, bf16[64,2048]{1,0:T(8,128)(2,1)S(1)}, u32[]{:S(2)}, u32[]{:S(2)}) collective-permute-start(bf16[64,2048]{1,0:T(8,128)(2,1)S(1)} %get-tuple-element.159), channel_id=1, source_target_pairs={{0,8},{8,0},{1,9},{9,1},{2,10},{10,2},{3,11},{11,3},{4,12},{12,4},... | collective-permute-start | bytes 786440 | tf_op jit(solution)/shard_map/ppermute | solution.py:47
  78.0 0.1 collective-permute-start.11
  78.0 6.0 %weight_grads.1 = (bf16[384,2048]{1,0:T(8,128)(2,1)S(1)}, bf16[384,2048]{1,0:T(8,128)(2,1)S(1)}, bf16[384,2048]{1,0:T(8,128)(2,1)S(1)}, bf16[384,2048]{1,0:T(8,1...) custom-call(bf16[64,4224]{1,0:T(8,128)(2,1)S(1)} %copy-done, ...), custom_call_target="tpu_custom_call" | custom-call | flops 4831838208 | bytes 13631488 | tf_op jit(solution)/shard_map/weight_grads/pallas_call | solution.py:242
  84.0 1.4 %collective-permute-done.14 = bf16[64,4096]{1,0:T(8,128)(2,1)S(1)} collective-permute-done((bf16[64,4096]{1,0:T(8,128)(2,1)S(1)}, bf16[64,4096]{1,0:T(8,128)(2,1)S(1)}, u32[]{:S(2)}, u32[]{:S(2)}) %collective-permute-start.14) | collective-permute-done | bytes 524320 | tf_op jit(solution)/shard_map/ppermute | solution.py:42
  85.5 0.1 add_convert_fusion.4
  85.6 0.5 collective-permute-start.15
  86.1 0.1 collective-permute-done.12
  86.2 0.1 add_convert_fusion.10
  86.3 3.5 %collective-permute-start.13 = (bf16[64,2048]{1,0:T(8,128)(2,1)S(1)}, bf16[64,2048]{1,0:T(8,128)(2,1)S(1)}, u32[]{:S(2)}, u32[]{:S(2)}) collective-permute-start(bf16[64,2048]{1,0:T(8,128)(2,1)S(1)} %get-tuple-element.164), channel_id=1, source_target_pairs={{0,10},{2,12},{4,14},{6,15},{7,13},{5,11},{3,9},{1,8},{8,2},{10,4}... | collective-permute-start | bytes 786440 | tf_op jit(solution)/shard_map/ppermute | solution.py:42
  89.8 6.7 %collective-permute-done.13 = bf16[64,2048]{1,0:T(8,128)(2,1)S(1)} collective-permute-done((bf16[64,2048]{1,0:T(8,128)(2,1)S(1)}, bf16[64,2048]{1,0:T(8,128)(2,1)S(1)}, u32[]{:S(2)}, u32[]{:S(2)}) %collective-permute-start.13) | collective-permute-done | bytes 262176 | tf_op jit(solution)/shard_map/ppermute | solution.py:42
  96.5 1.2 collective-permute-done.15
  97.7 0.1 add_convert_fusion.3
  97.8 0.5 collective-permute-start.17
  98.2 2.3 %collective-permute-start.18 = (bf16[64,2048]{1,0:T(8,128)(2,1)S(1)}, bf16[64,2048]{1,0:T(8,128)(2,1)S(1)}, u32[]{:S(2)}, u32[]{:S(2)}) collective-permute-start(bf16[64,2048]{1,0:T(8,128)(2,1)S(1)} %get-tuple-element.163), channel_id=1, source_target_pairs={{0,10},{2,12},{4,14},{6,15},{7,13},{5,11},{3,9},{1,8},{8,2},{10,4}... | collective-permute-start | bytes 786440 | tf_op jit(solution)/shard_map/ppermute | solution.py:42
  100.6 5.0 %collective-permute-done.18 = bf16[64,2048]{1,0:T(8,128)(2,1)S(1)} collective-permute-done((bf16[64,2048]{1,0:T(8,128)(2,1)S(1)}, bf16[64,2048]{1,0:T(8,128)(2,1)S(1)}, u32[]{:S(2)}, u32[]{:S(2)}) %collective-permute-start.18) | collective-permute-done | bytes 262176 | tf_op jit(solution)/shard_map/ppermute | solution.py:42
  105.5 1.5 %collective-permute-done.17 = bf16[64,4096]{1,0:T(8,128)(2,1)S(1)} collective-permute-done((bf16[64,4096]{1,0:T(8,128)(2,1)S(1)}, bf16[64,4096]{1,0:T(8,128)(2,1)S(1)}, u32[]{:S(2)}, u32[]{:S(2)}) %collective-permute-start.17) | collective-permute-done | bytes 524320 | tf_op jit(solution)/shard_map/ppermute | solution.py:42
  107.0 0.0 collective-permute-start.21
  107.0 0.5 collective-permute-start.22
  107.5 0.0 collective-permute-start.23
  107.5 0.1 add_convert_fusion.8
  107.7 0.7 collective-permute-start.20
  108.4 0.8 collective-permute-start.19
  109.2 1.3 %collective-permute-done.21 = bf16[384,2048]{1,0:T(8,128)(2,1)S(1)} collective-permute-done((bf16[384,2048]{1,0:T(8,128)(2,1)S(1)}, bf16[384,2048]{1,0:T(8,128)(2,1)S(1)}, u32[]{:S(2)}, u32[]{:S(2)}) %collective-permute-start.21) | collective-permute-done | bytes 1572896 | tf_op jit(solution)/shard_map/ppermute | solution.py:47
  110.4 1.8 %add_convert_fusion.2 = bf16[384,2048]{1,0:T(8,128)(2,1)} fusion(bf16[384,2048]{1,0:T(8,128)(2,1)S(1)} %collective-permute-done.21, bf16[384,2048]{1,0:T(8,128)(2,1)S(1)} %get-tuple-element.144), kind=kLoop, calls=%fused_computation.2 | loop fusion | flops 3145728 | bytes 4718592 | tf_op jit(solution)/shard_map/convert_element_type | solution.py:260
  112.2 0.4 collective-permute-done.22
  112.7 1.7 %add_convert_fusion.1 = bf16[384,2048]{1,0:T(8,128)(2,1)} fusion(bf16[384,2048]{1,0:T(8,128)(2,1)S(1)} %collective-permute-done.22, bf16[384,2048]{1,0:T(8,128)(2,1)S(1)} %get-tuple-element.146), kind=kLoop, calls=%fused_computation.1 | loop fusion | flops 3145728 | bytes 4718592 | tf_op jit(solution)/shard_map/convert_element_type | solution.py:260
  114.4 0.5 collective-permute-done.23
  114.9 1.8 %add_convert_fusion = bf16[384,2048]{1,0:T(8,128)(2,1)} fusion(bf16[384,2048]{1,0:T(8,128)(2,1)S(1)} %collective-permute-done.23, bf16[384,2048]{1,0:T(8,128)(2,1)S(1)} %get-tuple-element.148), kind=kLoop, calls=%fused_computation | loop fusion | flops 3145728 | bytes 4718592 | tf_op jit(solution)/shard_map/convert_element_type | solution.py:260
  116.7 1.1 collective-permute-done.20
  117.8 5.2 %collective-permute-done.19 = bf16[64,2048]{1,0:T(8,128)(2,1)S(1)} collective-permute-done((bf16[64,2048]{1,0:T(8,128)(2,1)S(1)}, bf16[64,2048]{1,0:T(8,128)(2,1)S(1)}, u32[]{:S(2)}, u32[]{:S(2)}) %collective-permute-start.19) | collective-permute-done | bytes 262176 | tf_op jit(solution)/shard_map/ppermute | solution.py:42
  123.0 1.0 fusion
  (10 shorter events, 0.0 us)
Async XLA Ops:
  0.6 17.6 %collective-permute-start.1 = (bf16[384,2048]{1,0:T(8,128)(2,1)}, bf16[384,2048]{1,0:T(8,128)(2,1)S(1)}, u32[]{:S(2)}, u32[]{:S(2)}) collective-permute-start(bf16[384,2048]{1,0:T(8,128)(2,1)} %bitcast.21), channel_id=1, source_target_pairs={{0,16},{16,0},{1,17},{17,1},{2,18},{18,2},{3,19},{19,3},{4,20},{20... | collective-permute-start | bytes 4718600 | tf_op jit(solution)/shard_map/ppermute | solution.py:47
  1.2 17.1 %collective-permute-start.2 = (bf16[384,2048]{1,0:T(8,128)(2,1)}, bf16[384,2048]{1,0:T(8,128)(2,1)S(1)}, u32[]{:S(2)}, u32[]{:S(2)}) collective-permute-start(bf16[384,2048]{1,0:T(8,128)(2,1)} %bitcast.23), channel_id=1, source_target_pairs={{0,16},{16,0},{1,17},{17,1},{2,18},{18,2},{3,19},{19,3},{4,20},{20... | collective-permute-start | bytes 4718600 | tf_op jit(solution)/shard_map/ppermute | solution.py:47
  1.2 17.0 %collective-permute-start.3 = (bf16[384,2048]{1,0:T(8,128)(2,1)}, bf16[384,2048]{1,0:T(8,128)(2,1)}, u32[]{:S(2)}, u32[]{:S(2)}) collective-permute-start(bf16[384,2048]{1,0:T(8,128)(2,1)} %bitcast.25), channel_id=1, source_target_pairs={{0,16},{16,0},{1,17},{17,1},{2,18},{18,2},{3,19},{19,3},{4,20},{20... | collective-permute-start | bytes 4718600 | tf_op jit(solution)/shard_map/ppermute | solution.py:47
  3.9 12.0 %collective-permute-start = (bf16[64,4224]{1,0:T(8,128)(2,1)}, bf16[64,4224]{1,0:T(8,128)(2,1)S(1)}, u32[]{:S(2)}, u32[]{:S(2)}) collective-permute-start(bf16[64,4224]{1,0:T(8,128)(2,1)} %pack_rows.1.refs_0_), channel_id=1, source_target_pairs={{0,2},{2,4},{4,6},{6,7},{7,5},{5,3},{3,1},{1,0},{8,10},{10,12},{12... | collective-permute-start | bytes 1622024 | tf_op jit(solution)/shard_map/ppermute | solution.py:42
  6.5 1.4 %copy-start.1 = (bf16[1,2,192,2048]{3,2,1,0:T(8,128)(2,1)S(1)}, bf16[1,2,192,2048]{3,2,1,0:T(8,128)(2,1)}, u32[]{:S(2)}) copy-start(bf16[1,2,192,2048]{3,2,1,0:T(8,128)(2,1)} %param.13) | copy-start | bytes 4718596
  7.9 1.4 %copy-start.2 = (bf16[1,2,192,2048]{3,2,1,0:T(8,128)(2,1)S(1)}, bf16[1,2,192,2048]{3,2,1,0:T(8,128)(2,1)}, u32[]{:S(2)}) copy-start(bf16[1,2,192,2048]{3,2,1,0:T(8,128)(2,1)} %param.14) | copy-start | bytes 4718596
  7.9 1.9 %copy-start.3 = (bf16[1,2,192,2048]{3,2,1,0:T(8,128)(2,1)S(1)}, bf16[1,2,192,2048]{3,2,1,0:T(8,128)(2,1)}, u32[]{:S(2)}) copy-start(bf16[1,2,192,2048]{3,2,1,0:T(8,128)(2,1)} %param.15) | copy-start | bytes 4718596
  9.8 1.0 copy-start
  10.9 13.6 %collective-permute-start.7 = (bf16[64,4224]{1,0:T(8,128)(2,1)S(1)}, bf16[64,4224]{1,0:T(8,128)(2,1)S(1)}, u32[]{:S(2)}, u32[]{:S(2)}) collective-permute-start(bf16[64,4224]{1,0:T(8,128)(2,1)S(1)} %copy-done), channel_id=1, source_target_pairs={{0,1},{2,0},{4,2},{6,4},{7,6},{5,7},{3,5},{1,3},{8,9},{10,8},{12,1... | collective-permute-start | bytes 1622024 | tf_op jit(solution)/shard_map/ppermute | solution.py:42
  15.8 11.5 %collective-permute-start.4 = (bf16[64,4224]{1,0:T(8,128)(2,1)S(1)}, bf16[64,4224]{1,0:T(8,128)(2,1)S(1)}, u32[]{:S(2)}, u32[]{:S(2)}) collective-permute-start(bf16[64,4224]{1,0:T(8,128)(2,1)S(1)} %collective-permute-done.refs_1_), channel_id=1, source_target_pairs={{0,2},{2,4},{4,6},{6,7},{7,5},{5,3},{3,1},{1,0},{8,10},{10,12},{12... | collective-permute-start | bytes 1622024 | tf_op jit(solution)/shard_map/ppermute | solution.py:42
  24.5 14.7 %collective-permute-start.8 = (bf16[64,4224]{1,0:T(8,128)(2,1)S(1)}, bf16[64,4224]{1,0:T(8,128)(2,1)S(1)}, u32[]{:S(2)}, u32[]{:S(2)}) collective-permute-start(bf16[64,4224]{1,0:T(8,128)(2,1)S(1)} %collective-permute-done.7.refs_0_.refs_2_), channel_id=1, source_target_pairs={{0,1},{2,0},{4,2},{6,4},{7,6},{5,7},{3,5},{1,3},{8,9},{10,8},{12,1... | collective-permute-start | bytes 1622024 | tf_op jit(solution)/shard_map/ppermute | solution.py:42
  27.4 12.0 %collective-permute-start.5 = (bf16[64,4224]{1,0:T(8,128)(2,1)S(1)}, bf16[64,4224]{1,0:T(8,128)(2,1)S(1)}, u32[]{:S(2)}, u32[]{:S(2)}) collective-permute-start(bf16[64,4224]{1,0:T(8,128)(2,1)S(1)} %collective-permute-done.4.refs_1_.refs_3_), channel_id=1, source_target_pairs={{0,2},{2,4},{4,6},{6,7},{7,5},{5,3},{3,1},{1,0},{8,10},{10,12},{12... | collective-permute-start | bytes 1622024 | tf_op jit(solution)/shard_map/ppermute | solution.py:42
  39.2 15.1 %collective-permute-start.9 = (bf16[64,4224]{1,0:T(8,128)(2,1)S(1)}, bf16[64,4224]{1,0:T(8,128)(2,1)S(1)}, u32[]{:S(2)}, u32[]{:S(2)}) collective-permute-start(bf16[64,4224]{1,0:T(8,128)(2,1)S(1)} %collective-permute-done.8.refs_0_.refs_4_), channel_id=1, source_target_pairs={{0,1},{2,0},{4,2},{6,4},{7,6},{5,7},{3,5},{1,3},{8,9},{10,8},{12,1... | collective-permute-start | bytes 1622024 | tf_op jit(solution)/shard_map/ppermute | solution.py:42
  39.3 22.4 %collective-permute-start.6 = (bf16[64,4224]{1,0:T(8,128)(2,1)S(1)}, bf16[64,4224]{1,0:T(8,128)(2,1)S(1)}, u32[]{:S(2)}, u32[]{:S(2)}) collective-permute-start(bf16[64,4224]{1,0:T(8,128)(2,1)S(1)} %collective-permute-done.5.refs_0_.refs_6_), channel_id=1, source_target_pairs={{0,2},{2,4},{4,6},{6,7},{7,5},{5,3},{3,1},{1,0},{8,10},{10,12},{12... | collective-permute-start | bytes 1622024 | tf_op jit(solution)/shard_map/ppermute | solution.py:42
  60.5 12.7 %collective-permute-start.10 = (bf16[64,4096]{1,0:T(8,128)(2,1)S(1)}, bf16[64,4096]{1,0:T(8,128)(2,1)S(1)}, u32[]{:S(2)}, u32[]{:S(2)}) collective-permute-start(bf16[64,4096]{1,0:T(8,128)(2,1)S(1)} %get-tuple-element.106), channel_id=1, source_target_pairs={{0,2},{2,4},{4,6},{6,7},{7,5},{5,3},{3,1},{1,0},{8,10},{10,12},{12... | collective-permute-start | bytes 1572872 | tf_op jit(solution)/shard_map/ppermute | solution.py:42
  73.3 12.2 %collective-permute-start.14 = (bf16[64,4096]{1,0:T(8,128)(2,1)S(1)}, bf16[64,4096]{1,0:T(8,128)(2,1)S(1)}, u32[]{:S(2)}, u32[]{:S(2)}) collective-permute-start(bf16[64,4096]{1,0:T(8,128)(2,1)S(1)} %get-tuple-element.112), channel_id=1, source_target_pairs={{0,1},{2,0},{4,2},{6,4},{7,6},{5,7},{3,5},{1,3},{8,9},{10,8},{12,1... | collective-permute-start | bytes 1572872 | tf_op jit(solution)/shard_map/ppermute | solution.py:42
  74.2 12.0 %collective-permute-start.12 = (bf16[64,4096]{1,0:T(8,128)(2,1)S(1)}, bf16[64,4096]{1,0:T(8,128)(2,1)S(1)}, u32[]{:S(2)}, u32[]{:S(2)}) collective-permute-start(bf16[64,4096]{1,0:T(8,128)(2,1)S(1)} %add_convert_fusion.5), channel_id=1, source_target_pairs={{0,2},{2,4},{4,6},{6,7},{7,5},{5,3},{3,1},{1,0},{8,10},{10,12},{12... | collective-permute-start | bytes 1572872 | tf_op jit(solution)/shard_map/ppermute | solution.py:42
  76.0 13.7 %collective-permute-start.16 = (bf16[64,2048]{1,0:T(8,128)(2,1)S(1)}, bf16[64,2048]{1,0:T(8,128)(2,1)S(1)}, u32[]{:S(2)}, u32[]{:S(2)}) collective-permute-start(bf16[64,2048]{1,0:T(8,128)(2,1)S(1)} %get-tuple-element.159), channel_id=1, source_target_pairs={{0,8},{8,0},{1,9},{9,1},{2,10},{10,2},{3,11},{11,3},{4,12},{12,4},... | collective-permute-start | bytes 786440 | tf_op jit(solution)/shard_map/ppermute | solution.py:47
  78.0 11.8 %collective-permute-start.11 = (bf16[64,2048]{1,0:T(8,128)(2,1)S(1)}, bf16[64,2048]{1,0:T(8,128)(2,1)S(1)}, u32[]{:S(2)}, u32[]{:S(2)}) collective-permute-start(bf16[64,2048]{1,0:T(8,128)(2,1)S(1)} %get-tuple-element.160), channel_id=1, source_target_pairs={{0,8},{8,0},{1,9},{9,1},{2,10},{10,2},{3,11},{11,3},{4,12},{12,4},... | collective-permute-start | bytes 786440 | tf_op jit(solution)/shard_map/ppermute | solution.py:47
  85.6 12.0 %collective-permute-start.15 = (bf16[64,4096]{1,0:T(8,128)(2,1)S(1)}, bf16[64,4096]{1,0:T(8,128)(2,1)S(1)}, u32[]{:S(2)}, u32[]{:S(2)}) collective-permute-start(bf16[64,4096]{1,0:T(8,128)(2,1)S(1)} %add_convert_fusion.4), channel_id=1, source_target_pairs={{0,1},{2,0},{4,2},{6,4},{7,6},{5,7},{3,5},{1,3},{8,9},{10,8},{12,1... | collective-permute-start | bytes 1572872 | tf_op jit(solution)/shard_map/ppermute | solution.py:42
  86.3 10.2 %collective-permute-start.13 = (bf16[64,2048]{1,0:T(8,128)(2,1)S(1)}, bf16[64,2048]{1,0:T(8,128)(2,1)S(1)}, u32[]{:S(2)}, u32[]{:S(2)}) collective-permute-start(bf16[64,2048]{1,0:T(8,128)(2,1)S(1)} %get-tuple-element.164), channel_id=1, source_target_pairs={{0,10},{2,12},{4,14},{6,15},{7,13},{5,11},{3,9},{1,8},{8,2},{10,4}... | collective-permute-start | bytes 786440 | tf_op jit(solution)/shard_map/ppermute | solution.py:42
  97.8 9.2 %collective-permute-start.17 = (bf16[64,4096]{1,0:T(8,128)(2,1)S(1)}, bf16[64,4096]{1,0:T(8,128)(2,1)S(1)}, u32[]{:S(2)}, u32[]{:S(2)}) collective-permute-start(bf16[64,4096]{1,0:T(8,128)(2,1)S(1)} %add_convert_fusion.3), channel_id=1, source_target_pairs={{0,1},{2,0},{4,2},{6,4},{7,6},{5,7},{3,5},{1,3},{8,9},{10,8},{12,1... | collective-permute-start | bytes 1572872 | tf_op jit(solution)/shard_map/ppermute | solution.py:42
  98.2 7.3 %collective-permute-start.18 = (bf16[64,2048]{1,0:T(8,128)(2,1)S(1)}, bf16[64,2048]{1,0:T(8,128)(2,1)S(1)}, u32[]{:S(2)}, u32[]{:S(2)}) collective-permute-start(bf16[64,2048]{1,0:T(8,128)(2,1)S(1)} %get-tuple-element.163), channel_id=1, source_target_pairs={{0,10},{2,12},{4,14},{6,15},{7,13},{5,11},{3,9},{1,8},{8,2},{10,4}... | collective-permute-start | bytes 786440 | tf_op jit(solution)/shard_map/ppermute | solution.py:42
  107.0 3.4 %collective-permute-start.21 = (bf16[384,2048]{1,0:T(8,128)(2,1)S(1)}, bf16[384,2048]{1,0:T(8,128)(2,1)S(1)}, u32[]{:S(2)}, u32[]{:S(2)}) collective-permute-start(bf16[384,2048]{1,0:T(8,128)(2,1)S(1)} %get-tuple-element.145), channel_id=1, source_target_pairs={{0,16},{16,0},{1,17},{17,1},{2,18},{18,2},{3,19},{19,3},{4,20},{20... | collective-permute-start | bytes 4718600 | tf_op jit(solution)/shard_map/ppermute | solution.py:47
  107.0 5.7 %collective-permute-start.22 = (bf16[384,2048]{1,0:T(8,128)(2,1)S(1)}, bf16[384,2048]{1,0:T(8,128)(2,1)S(1)}, u32[]{:S(2)}, u32[]{:S(2)}) collective-permute-start(bf16[384,2048]{1,0:T(8,128)(2,1)S(1)} %get-tuple-element.147), channel_id=1, source_target_pairs={{0,16},{16,0},{1,17},{17,1},{2,18},{18,2},{3,19},{19,3},{4,20},{20... | collective-permute-start | bytes 4718600 | tf_op jit(solution)/shard_map/ppermute | solution.py:47
  107.5 7.4 %collective-permute-start.23 = (bf16[384,2048]{1,0:T(8,128)(2,1)S(1)}, bf16[384,2048]{1,0:T(8,128)(2,1)S(1)}, u32[]{:S(2)}, u32[]{:S(2)}) collective-permute-start(bf16[384,2048]{1,0:T(8,128)(2,1)S(1)} %get-tuple-element.149), channel_id=1, source_target_pairs={{0,16},{16,0},{1,17},{17,1},{2,18},{18,2},{3,19},{19,3},{4,20},{20... | collective-permute-start | bytes 4718600 | tf_op jit(solution)/shard_map/ppermute | solution.py:47
  107.7 10.1 %collective-permute-start.20 = (bf16[64,2048]{1,0:T(8,128)(2,1)S(1)}, bf16[64,2048]{1,0:T(8,128)(2,1)S(1)}, u32[]{:S(2)}, u32[]{:S(2)}) collective-permute-start(bf16[64,2048]{1,0:T(8,128)(2,1)S(1)} %get-tuple-element.161), channel_id=1, source_target_pairs={{0,9},{2,8},{4,10},{6,12},{7,14},{5,15},{3,13},{1,11},{8,1},{10,0}... | collective-permute-start | bytes 786440 | tf_op jit(solution)/shard_map/ppermute | solution.py:42
  108.4 14.5 %collective-permute-start.19 = (bf16[64,2048]{1,0:T(8,128)(2,1)S(1)}, bf16[64,2048]{1,0:T(8,128)(2,1)S(1)}, u32[]{:S(2)}, u32[]{:S(2)}) collective-permute-start(bf16[64,2048]{1,0:T(8,128)(2,1)S(1)} %get-tuple-element.162), channel_id=1, source_target_pairs={{0,9},{2,8},{4,10},{6,12},{7,14},{5,15},{3,13},{1,11},{8,1},{10,0}... | collective-permute-start | bytes 786440 | tf_op jit(solution)/shard_map/ppermute | solution.py:42

commit v15 on v8

--- a/solution.py
+++ b/solution.py
@@ -322,9 +322,8 @@
     blocks = [held[name] for group in groups for name in group]
     steps = (1, -1)
     finals = []
-    here, near_sum = tie((partial["near", 0], near_sum))
     for part, step in zip(both, steps):
-        kept_here = add(home[:, part], here[:, part])
+        kept_here = add(home[:, part], partial["near", 0][:, part])
         finals.append([from_behind(kept_here, "section", step)])
     for k in range(ahead, 1, -1):
         near_sum = ring_shift(near_sum, -1)
@@ -342,10 +341,11 @@
                 final.append(ring_shift(last, 1, step))
             near_sum, _ = tie((near_sum, lasts))
             near_sum = add(near_sum, partial["near", 2])
+            near_sum, other_total = tie((near_sum, other_total))
+            received = [from_behind(g, "rep", 1) for g in other_total]
         elif k == 2:
             here = [final[1] for final in finals]
-            near_sum, other_total, _ = tie((near_sum, other_total, here))
-            received = [from_behind(g, "rep", 1) for g in other_total]
+            near_sum, _ = tie((near_sum, here))
         elif k > 2:
             near_sum = add(near_sum, partial["near", k - 1])
     lasts = [add(near_sum[:, part], partial["near", 1][:, part]) for part in both]

time: 116 us -> 117 us (level)
  transfers between devices with their start and end apart: 24 -> 24, of which waited for: 15 -> 12; matrix products, arithmetic and copies ran while one was open for 5% -> 5% of each run, Pallas kernels for 25% -> 24%
where the time goes in v15:
time: 117 us
  waiting for transfers between devices  49.9 us (43%)
  Pallas kernels  28.6 us (24%)
  starting transfers between devices  26.5 us (23%)
  other arithmetic  7.15 us (6%)
  local copies, waits for them, and re-layouts  3.97 us (3%)
    ppermute x16, waiting for transfers between devices, ring_shift(): return lax.ppermute(value, ('rep', 'section', 'exp'), pairs)  49.9 us
    ppermute x16, starting transfers between devices, ring_shift(): return lax.ppermute(value, ('rep', 'section', 'exp'), pairs)  22.4 us
    pallas_call x3, Pallas kernels, expert_call(): pl.pallas_call(functools.partial(expert_kernel, count, experts, local_exp...  20.1 us
    convert_element_type x9, other arithmetic, add(): return (a.astype(F32) + b.astype(F32)).astype(BF16)  6.12 us
    pallas_call x1, Pallas kernels, weight_call(): pl.pallas_call(functools.partial(weight_kernel, len(kept), count), out_sh...  5.88 us
    ppermute x8, starting transfers between devices, from_behind(): lax.ppermute(value, axis, [(i, (i + by) % peers) for i in range(peers)])  4.11 us
    unnamed x8, local copies, waits for them, and re-layouts  3.97 us
  transfers between devices with their start and end apart: 24, of which 12 were waited for; matrix products, arithmetic and copies ran while one was open for 5% of the time, Pallas kernels for 24%

profile of v15, /device:TPU:0, one launch (start us, length us, event | category | flops | bytes accessed | tf_op | source)
XLA Modules:
  0.0 116.9 jit_solution(12556968239495278283)
XLA Ops:
  0.6 0.5 collective-permute-start.3
  1.2 0.1 collective-permute-start.4
  1.2 0.4 collective-permute-start.5
  1.7 2.2 %pack_rows.1.refs_0_ = bf16[64,4224]{1,0:T(8,128)(2,1)} custom-call(bf16[64,2048]{1,0:T(8,128)(2,1)} %bitcast.30, s32[16,64]{1,0:T(8,128)} %bitcast.32, s32[8,64]{1,0:T(8,128)} %bitcast.33, f32[8,64]{1,0:T(8,128)} %bitcast.34, bf16[64,2048]{1,0:T(8,128)(2,1)} %bitcast.31), custom_call_target="tpu_custom_call" | custom-call | tf_op jit(solution)/shard_map/pack_rows/pallas_call | solution.py:274
  3.9 2.7 %collective-permute-start = (bf16[64,4224]{1,0:T(8,128)(2,1)}, bf16[64,4224]{1,0:T(8,128)(2,1)S(1)}, u32[]{:S(2)}, u32[]{:S(2)}) collective-permute-start(bf16[64,4224]{1,0:T(8,128)(2,1)} %pack_rows.1.refs_0_), channel_id=1, source_target_pairs={{0,2},{2,4},{4,6},{6,7},{7,5},{5,3},{3,1},{1,0},{8,10},{10,12},{12... | collective-permute-start | bytes 1622024 | tf_op jit(solution)/shard_map/ppermute | solution.py:42
  6.5 1.4 %copy-done.1 = bf16[1,2,192,2048]{3,2,1,0:T(8,128)(2,1)S(1)} copy-done((bf16[1,2,192,2048]{3,2,1,0:T(8,128)(2,1)S(1)}, bf16[1,2,192,2048]{3,2,1,0:T(8,128)(2,1)}, u32[]{:S(2)}) %copy-start.1) | copy-done | bytes 1572888
  7.9 0.1 load_weights.2.refs_4_.refs_2_
  8.1 1.3 %copy-done.2 = bf16[1,2,192,2048]{3,2,1,0:T(8,128)(2,1)S(1)} copy-done((bf16[1,2,192,2048]{3,2,1,0:T(8,128)(2,1)S(1)}, bf16[1,2,192,2048]{3,2,1,0:T(8,128)(2,1)}, u32[]{:S(2)}) %copy-start.2) | copy-done | bytes 1572888
  9.3 0.5 copy-done.3
  9.8 0.2 load_weights.3
  10.1 0.8 copy-done
  10.9 0.0 collective-permute-start.1
  10.9 5.0 %collective-permute-done.refs_1_ = bf16[64,4224]{1,0:T(8,128)(2,1)S(1)} collective-permute-done((bf16[64,4224]{1,0:T(8,128)(2,1)}, bf16[64,4224]{1,0:T(8,128)(2,1)S(1)}, u32[]{:S(2)}, u32[]{:S(2)}) %collective-permute-start) | collective-permute-done | bytes 540704 | tf_op jit(solution)/shard_map/ppermute | solution.py:42
  15.8 2.4 %collective-permute-start.2 = (bf16[64,4224]{1,0:T(8,128)(2,1)S(1)}, bf16[64,4224]{1,0:T(8,128)(2,1)S(1)}, u32[]{:S(2)}, u32[]{:S(2)}) collective-permute-start(bf16[64,4224]{1,0:T(8,128)(2,1)S(1)} %collective-permute-done.refs_1_), channel_id=1, source_target_pairs={{0,2},{2,4},{4,6},{6,7},{7,5},{5,3},{3,1},{1,0},{8,10},{10,12},{12... | collective-permute-start | bytes 1622024 | tf_op jit(solution)/shard_map/ppermute | solution.py:42
  18.2 5.4 %collective-permute-done.1.refs_2_ = bf16[64,4224]{1,0:T(8,128)(2,1)S(1)} collective-permute-done((bf16[64,4224]{1,0:T(8,128)(2,1)S(1)}, bf16[64,4224]{1,0:T(8,128)(2,1)S(1)}, u32[]{:S(2)}, u32[]{:S(2)}) %collective-permute-start.1) | collective-permute-done | bytes 540704 | tf_op jit(solution)/shard_map/ppermute | solution.py:42
  23.6 0.0 collective-permute-start.7
  23.6 4.6 %collective-permute-done.2.refs_3_ = bf16[64,4224]{1,0:T(8,128)(2,1)S(1)} collective-permute-done((bf16[64,4224]{1,0:T(8,128)(2,1)S(1)}, bf16[64,4224]{1,0:T(8,128)(2,1)S(1)}, u32[]{:S(2)}, u32[]{:S(2)}) %collective-permute-start.2) | collective-permute-done | bytes 540704 | tf_op jit(solution)/shard_map/ppermute | solution.py:42
  28.2 2.5 %collective-permute-start.12 = (bf16[64,4224]{1,0:T(8,128)(2,1)S(1)}, bf16[64,4224]{1,0:T(8,128)(2,1)S(1)}, u32[]{:S(2)}, u32[]{:S(2)}) collective-permute-start(bf16[64,4224]{1,0:T(8,128)(2,1)S(1)} %collective-permute-done.2.refs_3_), channel_id=1, source_target_pairs={{0,2},{2,4},{4,6},{6,7},{7,5},{5,3},{3,1},{1,0},{8,10},{10,12},{12... | collective-permute-start | bytes 1622024 | tf_op jit(solution)/shard_map/ppermute | solution.py:42
  30.7 6.5 %collective-permute-done.7.refs_0_.refs_4_ = bf16[64,4224]{1,0:T(8,128)(2,1)S(1)} collective-permute-done((bf16[64,4224]{1,0:T(8,128)(2,1)S(1)}, bf16[64,4224]{1,0:T(8,128)(2,1)S(1)}, u32[]{:S(2)}, u32[]{:S(2)}) %collective-permute-start.7) | collective-permute-done | bytes 540704 | tf_op jit(solution)/shard_map/ppermute | solution.py:42
  37.1 0.0 collective-permute-start.8
  37.1 0.0 collective-permute-done.3.refs_7_.refs_5_
  37.1 0.0 collective-permute-done.5.refs_9_.refs_7_
  37.1 7.7 %expert_rows.3 = (bf16[64,4096]{1,0:T(8,128)(2,1)S(1)}, bf16[64,4096]{1,0:T(8,128)(2,1)S(1)}, bf16[64,4096]{1,0:T(8,128)(2,1)S(1)}, bf16[64,4096]{1,0:T(8,128)(2...) custom-call(bf16[64,4224]{1,0:T(8,128)(2,1)S(1)} %copy-done, ...), custom_call_target="tpu_custom_call" | custom-call | flops 4831838208 | bytes 13631488 | tf_op jit(solution)/shard_map/expert_rows/pallas_call | solution.py:191
  44.9 0.0 collective-permute-done.12.refs_0_.refs_6_
  44.9 2.1 %collective-permute-start.13 = (bf16[64,4224]{1,0:T(8,128)(2,1)S(1)}, bf16[64,4224]{1,0:T(8,128)(2,1)S(1)}, u32[]{:S(2)}, u32[]{:S(2)}) collective-permute-start(bf16[64,4224]{1,0:T(8,128)(2,1)S(1)} %collective-permute-done.12.refs_0_.refs_6_), channel_id=1, source_target_pairs={{0,2},{2,4},{4,6},{6,7},{7,5},{5,3},{3,1},{1,0},{8,10},{10,12},{12... | collective-permute-start | bytes 1622024 | tf_op jit(solution)/shard_map/ppermute | solution.py:42
  46.9 2.3 %collective-permute-done.8.refs_1_.refs_5_ = bf16[64,4224]{1,0:T(8,128)(2,1)S(1)} collective-permute-done((bf16[64,4224]{1,0:T(8,128)(2,1)S(1)}, bf16[64,4224]{1,0:T(8,128)(2,1)S(1)}, u32[]{:S(2)}, u32[]{:S(2)}) %collective-permute-start.8) | collective-permute-done | bytes 540704 | tf_op jit(solution)/shard_map/ppermute | solution.py:42
  49.2 6.2 %expert_rows.4 = (bf16[64,4096]{1,0:T(8,128)(2,1)S(1)}, bf16[64,4096]{1,0:T(8,128)(2,1)S(1)}, bf16[768,128]{1,0:T(8,128)(2,1)S(1)}, bf16[768,128]{1,0:T(8,128)(2,1)S(1)}, bf16[768,128]{1,0:T(8,128)(2,1)S(1)}) custom-call(bf16[64,4224]{1,0:T(8,128)(2,1)S(1)} %collective-permute-done.7.refs_0_.refs_4_, ...), custom_call_target="tpu_custom_call" | custom-call | flops 2415919104 | bytes 11534336 | tf_op jit(solution)/shard_map/expert_rows/pallas_call | solution.py:191
  55.4 2.0 %collective-permute-start.9 = (bf16[64,4096]{1,0:T(8,128)(2,1)S(1)}, bf16[64,4096]{1,0:T(8,128)(2,1)S(1)}, u32[]{:S(2)}, u32[]{:S(2)}) collective-permute-start(bf16[64,4096]{1,0:T(8,128)(2,1)S(1)} %get-tuple-element.80), channel_id=1, source_target_pairs={{0,2},{2,4},{4,6},{6,7},{7,5},{5,3},{3,1},{1,0},{8,10},{10,12},{12... | collective-permute-start | bytes 1572872 | tf_op jit(solution)/shard_map/ppermute | solution.py:42
  57.4 0.1 add_convert_fusion.11
  57.5 1.6 %collective-permute-start.6 = (bf16[64,2048]{1,0:T(8,128)(2,1)S(1)}, bf16[64,2048]{1,0:T(8,128)(2,1)S(1)}, u32[]{:S(2)}, u32[]{:S(2)}) collective-permute-start(bf16[64,2048]{1,0:T(8,128)(2,1)S(1)} %get-tuple-element.134), channel_id=1, source_target_pairs={{0,8},{8,0},{1,9},{9,1},{2,10},{10,2},{3,11},{11,3},{4,12},{12,4},... | collective-permute-start | bytes 786440 | tf_op jit(solution)/shard_map/ppermute | solution.py:47
  59.1 0.5 collective-permute-start.16
  59.6 6.2 %expert_rows.5 = (bf16[64,4096]{1,0:T(8,128)(2,1)S(1)}, bf16[64,4096]{1,0:T(8,128)(2,1)S(1)}, bf16[768,128]{1,0:T(8,128)(2,1)S(1)}, bf16[768,128]{1,0:T(8,128)(2,1)S(1)}, bf16[768,128]{1,0:T(8,128)(2,1)S(1)}) custom-call(bf16[64,4224]{1,0:T(8,128)(2,1)S(1)} %collective-permute-done.12.refs_0_.refs_6_, ...), custom_call_target="tpu_custom_call" | custom-call | flops 2415919104 | bytes 11534336 | tf_op jit(solution)/shard_map/expert_rows/pallas_call | solution.py:191
  65.8 0.2 collective-permute-start.14
  66.0 1.6 %collective-permute-done.9 = bf16[64,4096]{1,0:T(8,128)(2,1)S(1)} collective-permute-done((bf16[64,4096]{1,0:T(8,128)(2,1)S(1)}, bf16[64,4096]{1,0:T(8,128)(2,1)S(1)}, u32[]{:S(2)}, u32[]{:S(2)}) %collective-permute-start.9) | collective-permute-done | bytes 524320 | tf_op jit(solution)/shard_map/ppermute | solution.py:42
  67.6 0.1 add_convert_fusion.5
  67.8 2.5 %collective-permute-start.10 = (bf16[64,4096]{1,0:T(8,128)(2,1)S(1)}, bf16[64,4096]{1,0:T(8,128)(2,1)S(1)}, u32[]{:S(2)}, u32[]{:S(2)}) collective-permute-start(bf16[64,4096]{1,0:T(8,128)(2,1)S(1)} %add_convert_fusion.5), channel_id=1, source_target_pairs={{0,2},{2,4},{4,6},{6,7},{7,5},{5,3},{3,1},{1,0},{8,10},{10,12},{12... | collective-permute-start | bytes 1572872 | tf_op jit(solution)/shard_map/ppermute | solution.py:42
  70.3 4.8 %collective-permute-done.14 = bf16[64,4096]{1,0:T(8,128)(2,1)S(1)} collective-permute-done((bf16[64,4096]{1,0:T(8,128)(2,1)S(1)}, bf16[64,4096]{1,0:T(8,128)(2,1)S(1)}, u32[]{:S(2)}, u32[]{:S(2)}) %collective-permute-start.14) | collective-permute-done | bytes 524320 | tf_op jit(solution)/shard_map/ppermute | solution.py:42
  75.1 0.1 add_convert_fusion.4
  75.2 0.2 collective-permute-start.15
  75.4 5.9 %weight_grads.1 = (bf16[384,2048]{1,0:T(8,128)(2,1)S(1)}, bf16[384,2048]{1,0:T(8,128)(2,1)S(1)}, bf16[384,2048]{1,0:T(8,128)(2,1)S(1)}, bf16[384,2048]{1,0:T(8,1...) custom-call(bf16[64,4224]{1,0:T(8,128)(2,1)S(1)} %copy-done, ...), custom_call_target="tpu_custom_call" | custom-call | flops 4831838208 | bytes 13631488 | tf_op jit(solution)/shard_map/weight_grads/pallas_call | solution.py:242
  81.2 0.0 collective-permute-done.10
  81.3 0.1 add_convert_fusion.10
  81.4 0.0 collective-permute-done.16
  81.4 3.0 %collective-permute-done.15 = bf16[64,4096]{1,0:T(8,128)(2,1)S(1)} collective-permute-done((bf16[64,4096]{1,0:T(8,128)(2,1)S(1)}, bf16[64,4096]{1,0:T(8,128)(2,1)S(1)}, u32[]{:S(2)}, u32[]{:S(2)}) %collective-permute-start.15) | collective-permute-done | bytes 524320 | tf_op jit(solution)/shard_map/ppermute | solution.py:42
  84.4 0.1 add_convert_fusion.3
  84.6 0.1 collective-permute-start.21
  84.7 0.5 collective-permute-start.22
  85.1 0.1 collective-permute-start.17
  85.2 2.9 %collective-permute-start.11 = (bf16[64,2048]{1,0:T(8,128)(2,1)S(1)}, bf16[64,2048]{1,0:T(8,128)(2,1)S(1)}, u32[]{:S(2)}, u32[]{:S(2)}) collective-permute-start(bf16[64,2048]{1,0:T(8,128)(2,1)S(1)} %get-tuple-element.138), channel_id=1, source_target_pairs={{0,10},{2,12},{4,14},{6,15},{7,13},{5,11},{3,9},{1,8},{8,2},{10,4}... | collective-permute-start | bytes 786440 | tf_op jit(solution)/shard_map/ppermute | solution.py:42
  88.1 1.5 %collective-permute-start.18 = (bf16[64,2048]{1,0:T(8,128)(2,1)S(1)}, bf16[64,2048]{1,0:T(8,128)(2,1)S(1)}, u32[]{:S(2)}, u32[]{:S(2)}) collective-permute-start(bf16[64,2048]{1,0:T(8,128)(2,1)S(1)} %get-tuple-element.137), channel_id=1, source_target_pairs={{0,10},{2,12},{4,14},{6,15},{7,13},{5,11},{3,9},{1,8},{8,2},{10,4}... | collective-permute-start | bytes 786440 | tf_op jit(solution)/shard_map/ppermute | solution.py:42
  89.7 5.7 %collective-permute-done.11 = bf16[64,2048]{1,0:T(8,128)(2,1)S(1)} collective-permute-done((bf16[64,2048]{1,0:T(8,128)(2,1)S(1)}, bf16[64,2048]{1,0:T(8,128)(2,1)S(1)}, u32[]{:S(2)}, u32[]{:S(2)}) %collective-permute-start.11) | collective-permute-done | bytes 262176 | tf_op jit(solution)/shard_map/ppermute | solution.py:42
  95.3 0.4 collective-permute-start.23
  95.7 4.7 %collective-permute-done.18 = bf16[64,2048]{1,0:T(8,128)(2,1)S(1)} collective-permute-done((bf16[64,2048]{1,0:T(8,128)(2,1)S(1)}, bf16[64,2048]{1,0:T(8,128)(2,1)S(1)}, u32[]{:S(2)}, u32[]{:S(2)}) %collective-permute-start.18) | collective-permute-done | bytes 262176 | tf_op jit(solution)/shard_map/ppermute | solution.py:42
  100.5 0.0 collective-permute-done.17
  100.5 0.1 add_convert_fusion.8
  100.6 2.2 %collective-permute-start.19 = (bf16[64,2048]{1,0:T(8,128)(2,1)S(1)}, bf16[64,2048]{1,0:T(8,128)(2,1)S(1)}, u32[]{:S(2)}, u32[]{:S(2)}) collective-permute-start(bf16[64,2048]{1,0:T(8,128)(2,1)S(1)} %get-tuple-element.136), channel_id=1, source_target_pairs={{0,9},{2,8},{4,10},{6,12},{7,14},{5,15},{3,13},{1,11},{8,1},{10,0}... | collective-permute-start | bytes 786440 | tf_op jit(solution)/shard_map/ppermute | solution.py:42
  102.8 1.3 %collective-permute-start.20 = (bf16[64,2048]{1,0:T(8,128)(2,1)S(1)}, bf16[64,2048]{1,0:T(8,128)(2,1)S(1)}, u32[]{:S(2)}, u32[]{:S(2)}) collective-permute-start(bf16[64,2048]{1,0:T(8,128)(2,1)S(1)} %get-tuple-element.135), channel_id=1, source_target_pairs={{0,9},{2,8},{4,10},{6,12},{7,14},{5,15},{3,13},{1,11},{8,1},{10,0}... | collective-permute-start | bytes 786440 | tf_op jit(solution)/shard_map/ppermute | solution.py:42
  104.1 1.8 %add_convert_fusion.2 = bf16[384,2048]{1,0:T(8,128)(2,1)} fusion(bf16[384,2048]{1,0:T(8,128)(2,1)S(1)} %collective-permute-done.21, bf16[384,2048]{1,0:T(8,128)(2,1)S(1)} %get-tuple-element.118), kind=kLoop, calls=%fused_computation.2 | loop fusion | flops 3145728 | bytes 4718592 | tf_op jit(solution)/shard_map/convert_element_type | solution.py:260
  105.9 1.7 %add_convert_fusion.1 = bf16[384,2048]{1,0:T(8,128)(2,1)} fusion(bf16[384,2048]{1,0:T(8,128)(2,1)S(1)} %collective-permute-done.22, bf16[384,2048]{1,0:T(8,128)(2,1)S(1)} %get-tuple-element.120), kind=kLoop, calls=%fused_computation.1 | loop fusion | flops 3145728 | bytes 4718592 | tf_op jit(solution)/shard_map/convert_element_type | solution.py:260
  107.7 0.0 collective-permute-done.23
  107.7 1.8 %add_convert_fusion = bf16[384,2048]{1,0:T(8,128)(2,1)} fusion(bf16[384,2048]{1,0:T(8,128)(2,1)S(1)} %collective-permute-done.23, bf16[384,2048]{1,0:T(8,128)(2,1)S(1)} %get-tuple-element.122), kind=kLoop, calls=%fused_computation | loop fusion | flops 3145728 | bytes 4718592 | tf_op jit(solution)/shard_map/convert_element_type | solution.py:260
  109.5 1.2 %collective-permute-done.19 = bf16[64,2048]{1,0:T(8,128)(2,1)S(1)} collective-permute-done((bf16[64,2048]{1,0:T(8,128)(2,1)S(1)}, bf16[64,2048]{1,0:T(8,128)(2,1)S(1)}, u32[]{:S(2)}, u32[]{:S(2)}) %collective-permute-start.19) | collective-permute-done | bytes 262176 | tf_op jit(solution)/shard_map/ppermute | solution.py:42
  110.7 5.1 %collective-permute-done.20 = bf16[64,2048]{1,0:T(8,128)(2,1)S(1)} collective-permute-done((bf16[64,2048]{1,0:T(8,128)(2,1)S(1)}, bf16[64,2048]{1,0:T(8,128)(2,1)S(1)}, u32[]{:S(2)}, u32[]{:S(2)}) %collective-permute-start.20) | collective-permute-done | bytes 262176 | tf_op jit(solution)/shard_map/ppermute | solution.py:42
  115.8 1.0 fusion
  (9 shorter events, 0.0 us)
Async XLA Ops:
  0.6 36.5 %collective-permute-start.3 = (bf16[384,2048]{1,0:T(8,128)(2,1)}, bf16[384,2048]{1,0:T(8,128)(2,1)S(1)}, u32[]{:S(2)}, u32[]{:S(2)}) collective-permute-start(bf16[384,2048]{1,0:T(8,128)(2,1)} %bitcast.21), channel_id=1, source_target_pairs={{0,16},{16,0},{1,17},{17,1},{2,18},{18,2},{3,19},{19,3},{4,20},{20... | collective-permute-start | bytes 4718600 | tf_op jit(solution)/shard_map/ppermute | solution.py:47
  1.2 36.0 %collective-permute-start.4 = (bf16[384,2048]{1,0:T(8,128)(2,1)}, bf16[384,2048]{1,0:T(8,128)(2,1)S(1)}, u32[]{:S(2)}, u32[]{:S(2)}) collective-permute-start(bf16[384,2048]{1,0:T(8,128)(2,1)} %bitcast.23), channel_id=1, source_target_pairs={{0,16},{16,0},{1,17},{17,1},{2,18},{18,2},{3,19},{19,3},{4,20},{20... | collective-permute-start | bytes 4718600 | tf_op jit(solution)/shard_map/ppermute | solution.py:47
  1.2 35.9 %collective-permute-start.5 = (bf16[384,2048]{1,0:T(8,128)(2,1)}, bf16[384,2048]{1,0:T(8,128)(2,1)}, u32[]{:S(2)}, u32[]{:S(2)}) collective-permute-start(bf16[384,2048]{1,0:T(8,128)(2,1)} %bitcast.25), channel_id=1, source_target_pairs={{0,16},{16,0},{1,17},{17,1},{2,18},{18,2},{3,19},{19,3},{4,20},{20... | collective-permute-start | bytes 4718600 | tf_op jit(solution)/shard_map/ppermute | solution.py:47
  3.9 12.0 %collective-permute-start = (bf16[64,4224]{1,0:T(8,128)(2,1)}, bf16[64,4224]{1,0:T(8,128)(2,1)S(1)}, u32[]{:S(2)}, u32[]{:S(2)}) collective-permute-start(bf16[64,4224]{1,0:T(8,128)(2,1)} %pack_rows.1.refs_0_), channel_id=1, source_target_pairs={{0,2},{2,4},{4,6},{6,7},{7,5},{5,3},{3,1},{1,0},{8,10},{10,12},{12... | collective-permute-start | bytes 1622024 | tf_op jit(solution)/shard_map/ppermute | solution.py:42
  6.5 1.4 %copy-start.1 = (bf16[1,2,192,2048]{3,2,1,0:T(8,128)(2,1)S(1)}, bf16[1,2,192,2048]{3,2,1,0:T(8,128)(2,1)}, u32[]{:S(2)}) copy-start(bf16[1,2,192,2048]{3,2,1,0:T(8,128)(2,1)} %param.13) | copy-start | bytes 4718596
  7.9 1.4 %copy-start.2 = (bf16[1,2,192,2048]{3,2,1,0:T(8,128)(2,1)S(1)}, bf16[1,2,192,2048]{3,2,1,0:T(8,128)(2,1)}, u32[]{:S(2)}) copy-start(bf16[1,2,192,2048]{3,2,1,0:T(8,128)(2,1)} %param.14) | copy-start | bytes 4718596
  7.9 1.9 %copy-start.3 = (bf16[1,2,192,2048]{3,2,1,0:T(8,128)(2,1)S(1)}, bf16[1,2,192,2048]{3,2,1,0:T(8,128)(2,1)}, u32[]{:S(2)}) copy-start(bf16[1,2,192,2048]{3,2,1,0:T(8,128)(2,1)} %param.15) | copy-start | bytes 4718596
  9.8 1.0 copy-start
  10.9 12.7 %collective-permute-start.1 = (bf16[64,4224]{1,0:T(8,128)(2,1)S(1)}, bf16[64,4224]{1,0:T(8,128)(2,1)S(1)}, u32[]{:S(2)}, u32[]{:S(2)}) collective-permute-start(bf16[64,4224]{1,0:T(8,128)(2,1)S(1)} %copy-done), channel_id=1, source_target_pairs={{0,1},{2,0},{4,2},{6,4},{7,6},{5,7},{3,5},{1,3},{8,9},{10,8},{12,1... | collective-permute-start | bytes 1622024 | tf_op jit(solution)/shard_map/ppermute | solution.py:42
  15.8 12.3 %collective-permute-start.2 = (bf16[64,4224]{1,0:T(8,128)(2,1)S(1)}, bf16[64,4224]{1,0:T(8,128)(2,1)S(1)}, u32[]{:S(2)}, u32[]{:S(2)}) collective-permute-start(bf16[64,4224]{1,0:T(8,128)(2,1)S(1)} %collective-permute-done.refs_1_), channel_id=1, source_target_pairs={{0,2},{2,4},{4,6},{6,7},{7,5},{5,3},{3,1},{1,0},{8,10},{10,12},{12... | collective-permute-start | bytes 1622024 | tf_op jit(solution)/shard_map/ppermute | solution.py:42
  23.6 13.5 %collective-permute-start.7 = (bf16[64,4224]{1,0:T(8,128)(2,1)S(1)}, bf16[64,4224]{1,0:T(8,128)(2,1)S(1)}, u32[]{:S(2)}, u32[]{:S(2)}) collective-permute-start(bf16[64,4224]{1,0:T(8,128)(2,1)S(1)} %collective-permute-done.1.refs_2_), channel_id=1, source_target_pairs={{0,1},{2,0},{4,2},{6,4},{7,6},{5,7},{3,5},{1,3},{8,9},{10,8},{12,1... | collective-permute-start | bytes 1622024 | tf_op jit(solution)/shard_map/ppermute | solution.py:42
  28.2 16.7 %collective-permute-start.12 = (bf16[64,4224]{1,0:T(8,128)(2,1)S(1)}, bf16[64,4224]{1,0:T(8,128)(2,1)S(1)}, u32[]{:S(2)}, u32[]{:S(2)}) collective-permute-start(bf16[64,4224]{1,0:T(8,128)(2,1)S(1)} %collective-permute-done.2.refs_3_), channel_id=1, source_target_pairs={{0,2},{2,4},{4,6},{6,7},{7,5},{5,3},{3,1},{1,0},{8,10},{10,12},{12... | collective-permute-start | bytes 1622024 | tf_op jit(solution)/shard_map/ppermute | solution.py:42
  37.1 12.1 %collective-permute-start.8 = (bf16[64,4224]{1,0:T(8,128)(2,1)S(1)}, bf16[64,4224]{1,0:T(8,128)(2,1)S(1)}, u32[]{:S(2)}, u32[]{:S(2)}) collective-permute-start(bf16[64,4224]{1,0:T(8,128)(2,1)S(1)} %collective-permute-done.7.refs_0_.refs_4_), channel_id=1, source_target_pairs={{0,1},{2,0},{4,2},{6,4},{7,6},{5,7},{3,5},{1,3},{8,9},{10,8},{12,1... | collective-permute-start | bytes 1622024 | tf_op jit(solution)/shard_map/ppermute | solution.py:42
  44.9 14.7 %collective-permute-start.13 = (bf16[64,4224]{1,0:T(8,128)(2,1)S(1)}, bf16[64,4224]{1,0:T(8,128)(2,1)S(1)}, u32[]{:S(2)}, u32[]{:S(2)}) collective-permute-start(bf16[64,4224]{1,0:T(8,128)(2,1)S(1)} %collective-permute-done.12.refs_0_.refs_6_), channel_id=1, source_target_pairs={{0,2},{2,4},{4,6},{6,7},{7,5},{5,3},{3,1},{1,0},{8,10},{10,12},{12... | collective-permute-start | bytes 1622024 | tf_op jit(solution)/shard_map/ppermute | solution.py:42
  55.4 12.2 %collective-permute-start.9 = (bf16[64,4096]{1,0:T(8,128)(2,1)S(1)}, bf16[64,4096]{1,0:T(8,128)(2,1)S(1)}, u32[]{:S(2)}, u32[]{:S(2)}) collective-permute-start(bf16[64,4096]{1,0:T(8,128)(2,1)S(1)} %get-tuple-element.80), channel_id=1, source_target_pairs={{0,2},{2,4},{4,6},{6,7},{7,5},{5,3},{3,1},{1,0},{8,10},{10,12},{12... | collective-permute-start | bytes 1572872 | tf_op jit(solution)/shard_map/ppermute | solution.py:42
  57.5 23.9 %collective-permute-start.6 = (bf16[64,2048]{1,0:T(8,128)(2,1)S(1)}, bf16[64,2048]{1,0:T(8,128)(2,1)S(1)}, u32[]{:S(2)}, u32[]{:S(2)}) collective-permute-start(bf16[64,2048]{1,0:T(8,128)(2,1)S(1)} %get-tuple-element.134), channel_id=1, source_target_pairs={{0,8},{8,0},{1,9},{9,1},{2,10},{10,2},{3,11},{11,3},{4,12},{12,4},... | collective-permute-start | bytes 786440 | tf_op jit(solution)/shard_map/ppermute | solution.py:47
  59.1 22.3 %collective-permute-start.16 = (bf16[64,2048]{1,0:T(8,128)(2,1)S(1)}, bf16[64,2048]{1,0:T(8,128)(2,1)S(1)}, u32[]{:S(2)}, u32[]{:S(2)}) collective-permute-start(bf16[64,2048]{1,0:T(8,128)(2,1)S(1)} %get-tuple-element.133), channel_id=1, source_target_pairs={{0,8},{8,0},{1,9},{9,1},{2,10},{10,2},{3,11},{11,3},{4,12},{12,4},... | collective-permute-start | bytes 786440 | tf_op jit(solution)/shard_map/ppermute | solution.py:47
  65.8 9.2 %collective-permute-start.14 = (bf16[64,4096]{1,0:T(8,128)(2,1)S(1)}, bf16[64,4096]{1,0:T(8,128)(2,1)S(1)}, u32[]{:S(2)}, u32[]{:S(2)}) collective-permute-start(bf16[64,4096]{1,0:T(8,128)(2,1)S(1)} %get-tuple-element.91), channel_id=1, source_target_pairs={{0,1},{2,0},{4,2},{6,4},{7,6},{5,7},{3,5},{1,3},{8,9},{10,8},{12,1... | collective-permute-start | bytes 1572872 | tf_op jit(solution)/shard_map/ppermute | solution.py:42
  67.8 13.5 %collective-permute-start.10 = (bf16[64,4096]{1,0:T(8,128)(2,1)S(1)}, bf16[64,4096]{1,0:T(8,128)(2,1)S(1)}, u32[]{:S(2)}, u32[]{:S(2)}) collective-permute-start(bf16[64,4096]{1,0:T(8,128)(2,1)S(1)} %add_convert_fusion.5), channel_id=1, source_target_pairs={{0,2},{2,4},{4,6},{6,7},{7,5},{5,3},{3,1},{1,0},{8,10},{10,12},{12... | collective-permute-start | bytes 1572872 | tf_op jit(solution)/shard_map/ppermute | solution.py:42
  75.2 9.2 %collective-permute-start.15 = (bf16[64,4096]{1,0:T(8,128)(2,1)S(1)}, bf16[64,4096]{1,0:T(8,128)(2,1)S(1)}, u32[]{:S(2)}, u32[]{:S(2)}) collective-permute-start(bf16[64,4096]{1,0:T(8,128)(2,1)S(1)} %add_convert_fusion.4), channel_id=1, source_target_pairs={{0,1},{2,0},{4,2},{6,4},{7,6},{5,7},{3,5},{1,3},{8,9},{10,8},{12,1... | collective-permute-start | bytes 1572872 | tf_op jit(solution)/shard_map/ppermute | solution.py:42
  84.6 19.5 %collective-permute-start.21 = (bf16[384,2048]{1,0:T(8,128)(2,1)S(1)}, bf16[384,2048]{1,0:T(8,128)(2,1)S(1)}, u32[]{:S(2)}, u32[]{:S(2)}) collective-permute-start(bf16[384,2048]{1,0:T(8,128)(2,1)S(1)} %get-tuple-element.119), channel_id=1, source_target_pairs={{0,16},{16,0},{1,17},{17,1},{2,18},{18,2},{3,19},{19,3},{4,20},{20... | collective-permute-start | bytes 4718600 | tf_op jit(solution)/shard_map/ppermute | solution.py:47
  84.7 21.3 %collective-permute-start.22 = (bf16[384,2048]{1,0:T(8,128)(2,1)S(1)}, bf16[384,2048]{1,0:T(8,128)(2,1)S(1)}, u32[]{:S(2)}, u32[]{:S(2)}) collective-permute-start(bf16[384,2048]{1,0:T(8,128)(2,1)S(1)} %get-tuple-element.121), channel_id=1, source_target_pairs={{0,16},{16,0},{1,17},{17,1},{2,18},{18,2},{3,19},{19,3},{4,20},{20... | collective-permute-start | bytes 4718600 | tf_op jit(solution)/shard_map/ppermute | solution.py:47
  85.1 15.3 %collective-permute-start.17 = (bf16[64,4096]{1,0:T(8,128)(2,1)S(1)}, bf16[64,4096]{1,0:T(8,128)(2,1)S(1)}, u32[]{:S(2)}, u32[]{:S(2)}) collective-permute-start(bf16[64,4096]{1,0:T(8,128)(2,1)S(1)} %add_convert_fusion.3), channel_id=1, source_target_pairs={{0,1},{2,0},{4,2},{6,4},{7,6},{5,7},{3,5},{1,3},{8,9},{10,8},{12,1... | collective-permute-start | bytes 1572872 | tf_op jit(solution)/shard_map/ppermute | solution.py:42
  85.2 10.1 %collective-permute-start.11 = (bf16[64,2048]{1,0:T(8,128)(2,1)S(1)}, bf16[64,2048]{1,0:T(8,128)(2,1)S(1)}, u32[]{:S(2)}, u32[]{:S(2)}) collective-permute-start(bf16[64,2048]{1,0:T(8,128)(2,1)S(1)} %get-tuple-element.138), channel_id=1, source_target_pairs={{0,10},{2,12},{4,14},{6,15},{7,13},{5,11},{3,9},{1,8},{8,2},{10,4}... | collective-permute-start | bytes 786440 | tf_op jit(solution)/shard_map/ppermute | solution.py:42
  88.1 12.3 %collective-permute-start.18 = (bf16[64,2048]{1,0:T(8,128)(2,1)S(1)}, bf16[64,2048]{1,0:T(8,128)(2,1)S(1)}, u32[]{:S(2)}, u32[]{:S(2)}) collective-permute-start(bf16[64,2048]{1,0:T(8,128)(2,1)S(1)} %get-tuple-element.137), channel_id=1, source_target_pairs={{0,10},{2,12},{4,14},{6,15},{7,13},{5,11},{3,9},{1,8},{8,2},{10,4}... | collective-permute-start | bytes 786440 | tf_op jit(solution)/shard_map/ppermute | solution.py:42
  95.3 12.4 %collective-permute-start.23 = (bf16[384,2048]{1,0:T(8,128)(2,1)S(1)}, bf16[384,2048]{1,0:T(8,128)(2,1)S(1)}, u32[]{:S(2)}, u32[]{:S(2)}) collective-permute-start(bf16[384,2048]{1,0:T(8,128)(2,1)S(1)} %get-tuple-element.123), channel_id=1, source_target_pairs={{0,16},{16,0},{1,17},{17,1},{2,18},{18,2},{3,19},{19,3},{4,20},{20... | collective-permute-start | bytes 4718600 | tf_op jit(solution)/shard_map/ppermute | solution.py:47
  100.6 10.1 %collective-permute-start.19 = (bf16[64,2048]{1,0:T(8,128)(2,1)S(1)}, bf16[64,2048]{1,0:T(8,128)(2,1)S(1)}, u32[]{:S(2)}, u32[]{:S(2)}) collective-permute-start(bf16[64,2048]{1,0:T(8,128)(2,1)S(1)} %get-tuple-element.136), channel_id=1, source_target_pairs={{0,9},{2,8},{4,10},{6,12},{7,14},{5,15},{3,13},{1,11},{8,1},{10,0}... | collective-permute-start | bytes 786440 | tf_op jit(solution)/shard_map/ppermute | solution.py:42
  102.8 13.1 %collective-permute-start.20 = (bf16[64,2048]{1,0:T(8,128)(2,1)S(1)}, bf16[64,2048]{1,0:T(8,128)(2,1)S(1)}, u32[]{:S(2)}, u32[]{:S(2)}) collective-permute-start(bf16[64,2048]{1,0:T(8,128)(2,1)S(1)} %get-tuple-element.135), channel_id=1, source_target_pairs={{0,9},{2,8},{4,10},{6,12},{7,14},{5,15},{3,13},{1,11},{8,1},{10,0}... | collective-permute-start | bytes 786440 | tf_op jit(solution)/shard_map/ppermute | solution.py:42

commit v16 on v10

--- a/solution.py
+++ b/solution.py
@@ -212,7 +212,7 @@
 def weight_kernel(groups, count, *refs):
     blocks = refs[:count]
     kept = [refs[count + g * 3 : count + g * 3 + 3] for g in range(groups)]
-    outs, across = refs[-7:-1], refs[-1]
+    outs, other, across = refs[-5:-2], refs[-2], refs[-1]
     half, width = outs[0].shape
     for kind in range(3):
         start = 0
@@ -230,7 +230,7 @@
         for kind in range(3):
             total = dot(across[kind], right[kind // 2], PLAIN).astype(BF16)
             outs[kind][:, at] = total[:half]
-            outs[3 + kind][:, at] = total[half:]
+            other[kind, :, at] = total[half:]
 
     columns_of(width, column)
 
@@ -241,9 +241,10 @@
     half, total = units // 2, count * blocks[0].shape[0]
     results = pl.pallas_call(
         functools.partial(weight_kernel, len(kept), count),
-        out_shape=[jax.ShapeDtypeStruct((half, width), BF16)] * 6,
+        out_shape=[jax.ShapeDtypeStruct((half, width), BF16)] * 3
+        + [jax.ShapeDtypeStruct((3, half, width), BF16)],
         in_specs=[whole()] * (count + 3 * len(kept)),
-        out_specs=[whole()] * 6,
+        out_specs=[whole()] * 4,
         scratch_shapes=[pltpu.VMEM((3, units, total), BF16)],
         compiler_params=pltpu.CompilerParams(vmem_limit_bytes=vmem(peers)),
         cost_estimate=pl.CostEstimate(
@@ -253,7 +254,7 @@
         ),
         name="weight_grads",
     )(*blocks, *[k for group in kept for k in group])
-    return results[:3], results[3:]
+    return results[:3], results[3]
 
 
 def add(a, b):
@@ -317,44 +318,46 @@
     held.update(zip(groups[-1], arrived))
     work(groups[-1])
     far_sum = ring_shift(partial["far", behind], 1)
-    both = (slice(0, width), slice(width, 2 * width))
+    both, steps = (slice(0, width), slice(width, 2 * width)), (1, -1)
+    if lax.axis_size("section") == 2:
+        both, steps = (slice(0, 2 * width),), (1,)
     near_sum = partial["near", ahead]
     own_total = received = None
     blocks = [held[name] for group in groups for name in group]
-    steps = (1, -1)
     finals = []
-    here, near_sum = tie((partial["near", 0], near_sum))
     for part, step in zip(both, steps):
-        kept_here = add(home[:, part], here[:, part])
+        kept_here = add(home[:, part], partial["near", 0][:, part])
         finals.append([from_behind(kept_here, "section", step)])
+    here = [final[0] for final in finals]
     for k in range(ahead, 1, -1):
         near_sum = ring_shift(near_sum, -1)
-        left = k - 2
-        if left > 1:
-            far_done = far_sum
-            far_sum = ring_shift(add(far_sum, partial["far", left]), 1)
-            near_sum, _ = tie((near_sum, far_done))
+        near_sum, far_sum = tie((near_sum, far_sum))
+        if k == 4:
+            near_sum, far_sum, _ = tie((near_sum, far_sum, here))
         if k == 3:
             own_total, other_total = weight_call(blocks, kept, width, peers)
-            here = [final[0] for final in finals]
-            near_sum, own_total, other_total, _ = tie((near_sum, own_total, other_total, here))
+            near_sum, far_sum, own_total, other_total = tie(
+                (near_sum, far_sum, own_total, other_total)
+            )
+        if k > 2:
+            near_sum = add(near_sum, partial["near", k - 1])
+        if k > 3:
+            far_sum = ring_shift(add(far_sum, partial["far", k - 2]), 1)
+        elif k == 3:
             lasts = [add(far_sum[:, part], partial["far", 1][:, part]) for part in both]
+            near_sum, lasts, other_total = tie((near_sum, lasts, other_total))
             for final, last, step in zip(finals, lasts, steps):
                 final.append(ring_shift(last, 1, step))
-            near_sum, _ = tie((near_sum, lasts))
-            near_sum = add(near_sum, partial["near", 2])
-        elif k == 2:
-            here = [final[1] for final in finals]
-            near_sum, other_total, _ = tie((near_sum, other_total, here))
-            received = [from_behind(g, "rep", 1) for g in other_total]
-        elif k > 2:
-            near_sum = add(near_sum, partial["near", k - 1])
+            far_sum = [final[1] for final in finals]
+            received = from_behind(other_total, "rep", 1)
     lasts = [add(near_sum[:, part], partial["near", 1][:, part]) for part in both]
     for final, last, step in zip(finals, lasts, steps):
         final.append(ring_shift(last, -1, step))
     totals = [add(a, b) for a, b in zip(own_total, received)]
     finals, totals = tie((finals, totals))
     results = [sum(f.astype(F32) for f in final).astype(BF16)[None] for final in finals]
+    if len(results) == 1:
+        results = [results[0][:, :, :width], results[0][:, :, width:]]
     shape = (1, local_experts, half_units, width)
     return tuple(results) + tuple(t.reshape(shape) for t in totals)
 

time: 122 us -> 120 us (0.984)
  starting transfers between devices: 24.6 us -> 21.2 us
  waiting for transfers between devices: 57 us -> 59.9 us
  other arithmetic: 7.09 us -> 4.57 us
    ppermute x16 -> x14, waiting for transfers between devices: 49.7 us -> 59.1 us  [ring_shift(): return lax.ppermute(value, ('rep', 'section', 'exp'), pairs)]
    ppermute x8 -> x5, waiting for transfers between devices: 7.36 us -> 0.8 us  [from_behind(): lax.ppermute(value, axis, [(i, (i + by) % peers) for i in range(peers)])]
    ppermute x16 -> x14, starting transfers between devices: 21 us -> 18.5 us  [ring_shift(): return lax.ppermute(value, ('rep', 'section', 'exp'), pairs)]
    convert_element_type x9 -> x6, other arithmetic: 6.05 us -> 4.38 us  [add(): return (a.astype(F32) + b.astype(F32)).astype(BF16)]
    ppermute x8 -> x5, starting transfers between devices: 3.63 us -> 2.67 us  [from_behind(): lax.ppermute(value, axis, [(i, (i + by) % peers) for i in range(peers)])]
  transfers between devices with their start and end apart: 24 -> 19, of which waited for: 15 -> 11; matrix products, arithmetic and copies ran while one was open for 5% -> 3% of each run, Pallas kernels for 18% -> 19%
where the time goes in v16:
time: 120 us
  waiting for transfers between devices  59.9 us (50%)
  Pallas kernels  28.7 us (24%)
  starting transfers between devices  21.2 us (18%)
  local copies, waits for them, and re-layouts  4.8 us (4%)
  other arithmetic  4.57 us (4%)
    ppermute x14, waiting for transfers between devices, ring_shift(): return lax.ppermute(value, ('rep', 'section', 'exp'), pairs)  59.1 us
    pallas_call x3, Pallas kernels, expert_call(): pl.pallas_call(functools.partial(expert_kernel, count, experts, local_exp...  20.1 us
    ppermute x14, starting transfers between devices, ring_shift(): return lax.ppermute(value, ('rep', 'section', 'exp'), pairs)  18.5 us
    pallas_call x1, Pallas kernels, weight_call(): pl.pallas_call(functools.partial(weight_kernel, len(kept), count), out_sh...  6.05 us
    convert_element_type x6, other arithmetic, add(): return (a.astype(F32) + b.astype(F32)).astype(BF16)  4.38 us
    unnamed x8, local copies, waits for them, and re-layouts  3.97 us
    ppermute x5, starting transfers between devices, from_behind(): lax.ppermute(value, axis, [(i, (i + by) % peers) for i in range(peers)])  2.67 us
  transfers between devices with their start and end apart: 19, of which 11 were waited for; matrix products, arithmetic and copies ran while one was open for 3% of the time, Pallas kernels for 19%

profile of v16, /device:TPU:0, one launch (start us, length us, event | category | flops | bytes accessed | tf_op | source)
XLA Modules:
  0.0 120.0 jit_solution(4190644968580839203)
XLA Ops:
  0.6 0.5 collective-permute-start.3
  1.2 0.1 collective-permute-start.4
  1.2 0.4 collective-permute-start.5
  1.7 2.2 %pack_rows.1.refs_0_ = bf16[64,4224]{1,0:T(8,128)(2,1)} custom-call(bf16[64,2048]{1,0:T(8,128)(2,1)} %bitcast.43, s32[16,64]{1,0:T(8,128)} %bitcast.45, s32[8,64]{1,0:T(8,128)} %bitcast.46, f32[8,64]{1,0:T(8,128)} %bitcast.47, bf16[64,2048]{1,0:T(8,128)(2,1)} %bitcast.44), custom_call_target="tpu_custom_call" | custom-call | tf_op jit(solution)/shard_map/pack_rows/pallas_call | solution.py:275
  3.9 2.7 %collective-permute-start = (bf16[64,4224]{1,0:T(8,128)(2,1)}, bf16[64,4224]{1,0:T(8,128)(2,1)S(1)}, u32[]{:S(2)}, u32[]{:S(2)}) collective-permute-start(bf16[64,4224]{1,0:T(8,128)(2,1)} %pack_rows.1.refs_0_), channel_id=1, source_target_pairs={{0,2},{2,4},{4,6},{6,7},{7,5},{5,3},{3,1},{1,0},{8,10},{10,12},{12... | collective-permute-start | bytes 1622024 | tf_op jit(solution)/shard_map/ppermute | solution.py:42
  6.5 0.0 copy-start.1
  6.5 1.4 %copy-done.1 = bf16[1,2,192,2048]{3,2,1,0:T(8,128)(2,1)S(1)} copy-done((bf16[1,2,192,2048]{3,2,1,0:T(8,128)(2,1)S(1)}, bf16[1,2,192,2048]{3,2,1,0:T(8,128)(2,1)}, u32[]{:S(2)}) %copy-start.1) | copy-done | bytes 1572888
  7.9 0.0 copy-start.2
  7.9 0.0 copy-start.3
  7.9 0.1 load_weights.2.refs_4_.refs_2_
  8.1 1.3 %copy-done.2 = bf16[1,2,192,2048]{3,2,1,0:T(8,128)(2,1)S(1)} copy-done((bf16[1,2,192,2048]{3,2,1,0:T(8,128)(2,1)S(1)}, bf16[1,2,192,2048]{3,2,1,0:T(8,128)(2,1)}, u32[]{:S(2)}) %copy-start.2) | copy-done | bytes 1572888
  9.3 0.5 copy-done.3
  9.8 0.0 copy-start
  9.8 0.2 load_weights.3
  10.1 0.8 copy-done
  10.9 0.0 collective-permute-start.1
  10.9 5.0 %collective-permute-done.refs_1_ = bf16[64,4224]{1,0:T(8,128)(2,1)S(1)} collective-permute-done((bf16[64,4224]{1,0:T(8,128)(2,1)}, bf16[64,4224]{1,0:T(8,128)(2,1)S(1)}, u32[]{:S(2)}, u32[]{:S(2)}) %collective-permute-start) | collective-permute-done | bytes 540704 | tf_op jit(solution)/shard_map/ppermute | solution.py:42
  15.8 2.4 %collective-permute-start.2 = (bf16[64,4224]{1,0:T(8,128)(2,1)S(1)}, bf16[64,4224]{1,0:T(8,128)(2,1)S(1)}, u32[]{:S(2)}, u32[]{:S(2)}) collective-permute-start(bf16[64,4224]{1,0:T(8,128)(2,1)S(1)} %collective-permute-done.refs_1_), channel_id=1, source_target_pairs={{0,2},{2,4},{4,6},{6,7},{7,5},{5,3},{3,1},{1,0},{8,10},{10,12},{12... | collective-permute-start | bytes 1622024 | tf_op jit(solution)/shard_map/ppermute | solution.py:42
  18.2 5.4 %collective-permute-done.1.refs_2_ = bf16[64,4224]{1,0:T(8,128)(2,1)S(1)} collective-permute-done((bf16[64,4224]{1,0:T(8,128)(2,1)S(1)}, bf16[64,4224]{1,0:T(8,128)(2,1)S(1)}, u32[]{:S(2)}, u32[]{:S(2)}) %collective-permute-start.1) | collective-permute-done | bytes 540704 | tf_op jit(solution)/shard_map/ppermute | solution.py:42
  23.6 0.0 collective-permute-start.7
  23.6 4.6 %collective-permute-done.2.refs_3_ = bf16[64,4224]{1,0:T(8,128)(2,1)S(1)} collective-permute-done((bf16[64,4224]{1,0:T(8,128)(2,1)S(1)}, bf16[64,4224]{1,0:T(8,128)(2,1)S(1)}, u32[]{:S(2)}, u32[]{:S(2)}) %collective-permute-start.2) | collective-permute-done | bytes 540704 | tf_op jit(solution)/shard_map/ppermute | solution.py:42
  28.2 2.5 %collective-permute-start.9 = (bf16[64,4224]{1,0:T(8,128)(2,1)S(1)}, bf16[64,4224]{1,0:T(8,128)(2,1)S(1)}, u32[]{:S(2)}, u32[]{:S(2)}) collective-permute-start(bf16[64,4224]{1,0:T(8,128)(2,1)S(1)} %collective-permute-done.2.refs_3_), channel_id=1, source_target_pairs={{0,2},{2,4},{4,6},{6,7},{7,5},{5,3},{3,1},{1,0},{8,10},{10,12},{12... | collective-permute-start | bytes 1622024 | tf_op jit(solution)/shard_map/ppermute | solution.py:42
  30.7 0.0 collective-permute-done.3.refs_7_.refs_5_
  30.7 0.0 collective-permute-done.4.refs_8_.refs_6_
  30.7 0.0 collective-permute-done.5.refs_9_.refs_7_
  30.7 7.7 %expert_rows.3 = (bf16[64,4096]{1,0:T(8,128)(2,1)S(1)}, bf16[64,4096]{1,0:T(8,128)(2,1)S(1)}, bf16[64,4096]{1,0:T(8,128)(2,1)S(1)}, bf16[64,4096]{1,0:T(8,128)(2...) custom-call(bf16[64,4224]{1,0:T(8,128)(2,1)S(1)} %copy-done, ...), custom_call_target="tpu_custom_call" | custom-call | flops 4831838208 | bytes 13631488 | tf_op jit(solution)/shard_map/expert_rows/pallas_call | solution.py:191
  38.4 0.0 collective-permute-done.7.refs_0_.refs_4_
  38.4 0.1 collective-permute-start.8
  38.5 0.8 collective-permute-done.9.refs_1_.refs_5_
  39.2 2.5 %collective-permute-start.10 = (bf16[64,4224]{1,0:T(8,128)(2,1)S(1)}, bf16[64,4224]{1,0:T(8,128)(2,1)S(1)}, u32[]{:S(2)}, u32[]{:S(2)}) collective-permute-start(bf16[64,4224]{1,0:T(8,128)(2,1)S(1)} %collective-permute-done.9.refs_1_.refs_5_), channel_id=1, source_target_pairs={{0,2},{2,4},{4,6},{6,7},{7,5},{5,3},{3,1},{1,0},{8,10},{10,12},{12... | collective-permute-start | bytes 1622024 | tf_op jit(solution)/shard_map/ppermute | solution.py:42
  41.7 6.2 %expert_rows.4 = (bf16[64,4096]{1,0:T(8,128)(2,1)S(1)}, bf16[64,4096]{1,0:T(8,128)(2,1)S(1)}, bf16[768,128]{1,0:T(8,128)(2,1)S(1)}, bf16[768,128]{1,0:T(8,128)(2,1)S(1)}, bf16[768,128]{1,0:T(8,128)(2,1)S(1)}) custom-call(bf16[64,4224]{1,0:T(8,128)(2,1)S(1)} %collective-permute-done.7.refs_0_.refs_4_, ...), custom_call_target="tpu_custom_call" | custom-call | flops 2415919104 | bytes 11534336 | tf_op jit(solution)/shard_map/expert_rows/pallas_call | solution.py:191
  47.9 5.0 %collective-permute-done.8.refs_0_.refs_6_ = bf16[64,4224]{1,0:T(8,128)(2,1)S(1)} collective-permute-done((bf16[64,4224]{1,0:T(8,128)(2,1)S(1)}, bf16[64,4224]{1,0:T(8,128)(2,1)S(1)}, u32[]{:S(2)}, u32[]{:S(2)}) %collective-permute-start.8) | collective-permute-done | bytes 540704 | tf_op jit(solution)/shard_map/ppermute | solution.py:42
  53.0 0.0 collective-permute-done.10.refs_1_.refs_7_
  53.0 6.2 %expert_rows.5 = (bf16[64,4096]{1,0:T(8,128)(2,1)S(1)}, bf16[64,4096]{1,0:T(8,128)(2,1)S(1)}, bf16[768,128]{1,0:T(8,128)(2,1)S(1)}, bf16[768,128]{1,0:T(8,128)(2,1)S(1)}, bf16[768,128]{1,0:T(8,128)(2,1)S(1)}) custom-call(bf16[64,4224]{1,0:T(8,128)(2,1)S(1)} %collective-permute-done.8.refs_0_.refs_6_, ...), custom_call_target="tpu_custom_call" | custom-call | flops 2415919104 | bytes 11534336 | tf_op jit(solution)/shard_map/expert_rows/pallas_call | solution.py:191
  59.2 0.1 collective-permute-start.11
  59.3 1.9 %collective-permute-start.12 = (bf16[64,4096]{1,0:T(8,128)(2,1)S(1)}, bf16[64,4096]{1,0:T(8,128)(2,1)S(1)}, u32[]{:S(2)}, u32[]{:S(2)}) collective-permute-start(bf16[64,4096]{1,0:T(8,128)(2,1)S(1)} %get-tuple-element.88), channel_id=1, source_target_pairs={{0,2},{2,4},{4,6},{6,7},{7,5},{5,3},{3,1},{1,0},{8,10},{10,12},{12... | collective-permute-start | bytes 1572872 | tf_op jit(solution)/shard_map/ppermute | solution.py:42
  61.3 0.1 add_convert_fusion.6
  61.4 1.6 %collective-permute-start.6 = (bf16[64,4096]{1,0:T(8,128)(2,1)S(1)}, bf16[64,4096]{1,0:T(8,128)(2,1)S(1)}, u32[]{:S(2)}, u32[]{:S(2)}) collective-permute-start(bf16[64,4096]{1,0:T(8,128)(2,1)S(1)} %add_convert_fusion.6), channel_id=1, source_target_pairs={{0,8},{8,0},{1,9},{9,1},{2,10},{10,2},{3,11},{11,3},{4,12},{12,4},... | collective-permute-start | bytes 1572872 | tf_op jit(solution)/shard_map/ppermute | solution.py:47
  63.0 10.8 %collective-permute-done.11 = bf16[64,4096]{1,0:T(8,128)(2,1)S(1)} collective-permute-done((bf16[64,4096]{1,0:T(8,128)(2,1)S(1)}, bf16[64,4096]{1,0:T(8,128)(2,1)S(1)}, u32[]{:S(2)}, u32[]{:S(2)}) %collective-permute-start.11) | collective-permute-done | bytes 524320 | tf_op jit(solution)/shard_map/ppermute | solution.py:42
  73.7 0.0 collective-permute-done.12
  73.7 0.8 collective-permute-done.6
  74.5 0.1 add_convert_fusion.4
  74.7 1.8 %collective-permute-start.14 = (bf16[64,4096]{1,0:T(8,128)(2,1)S(1)}, bf16[64,4096]{1,0:T(8,128)(2,1)S(1)}, u32[]{:S(2)}, u32[]{:S(2)}) collective-permute-start(bf16[64,4096]{1,0:T(8,128)(2,1)S(1)} %add_convert_fusion.4), channel_id=1, source_target_pairs={{0,2},{2,4},{4,6},{6,7},{7,5},{5,3},{3,1},{1,0},{8,10},{10,12},{12... | collective-permute-start | bytes 1572872 | tf_op jit(solution)/shard_map/ppermute | solution.py:42
  76.5 0.1 add_convert_fusion.5
  76.6 0.3 collective-permute-start.13
  76.9 6.1 %weight_grads.1 = (bf16[384,2048]{1,0:T(8,128)(2,1)S(1)}, bf16[384,2048]{1,0:T(8,128)(2,1)S(1)}, bf16[384,2048]{1,0:T(8,128)(2,1)S(1)}, bf16[3,384,2048]{2,1,0:T(8,128)(2,1)S(1)}) custom-call(bf16[64,4224]{1,0:T(8,128)(2,1)S(1)} %copy-done, bf16[64,4224]{1,0:T(8,128)(2,1)S(1)} %collective-permute-done.refs_1_, ...), custom_call_target="tpu_custom_call" | custom-call | flops 4831838208 | bytes 13631488 | tf_op jit(solution)/shard_map/weight_grads/pallas_call | solution.py:242
  83.0 5.4 %collective-permute-done.14 = bf16[64,4096]{1,0:T(8,128)(2,1)S(1)} collective-permute-done((bf16[64,4096]{1,0:T(8,128)(2,1)S(1)}, bf16[64,4096]{1,0:T(8,128)(2,1)S(1)}, u32[]{:S(2)}, u32[]{:S(2)}) %collective-permute-start.14) | collective-permute-done | bytes 524320 | tf_op jit(solution)/shard_map/ppermute | solution.py:42
  88.4 0.0 collective-permute-done.13
  88.4 0.2 add_convert_fusion.2
  88.6 0.1 collective-permute-start.18
  88.7 2.8 %collective-permute-start.15 = (bf16[64,4096]{1,0:T(8,128)(2,1)S(1)}, bf16[64,4096]{1,0:T(8,128)(2,1)S(1)}, u32[]{:S(2)}, u32[]{:S(2)}) collective-permute-start(bf16[64,4096]{1,0:T(8,128)(2,1)S(1)} %get-tuple-element.115), channel_id=1, source_target_pairs={{0,10},{2,12},{4,14},{6,15},{7,13},{5,11},{3,9},{1,8},{8,2},{10,4}... | collective-permute-start | bytes 1572872 | tf_op jit(solution)/shard_map/ppermute | solution.py:42
  91.5 0.3 collective-permute-start.16
  91.7 12.4 %collective-permute-done.15 = bf16[64,4096]{1,0:T(8,128)(2,1)S(1)} collective-permute-done((bf16[64,4096]{1,0:T(8,128)(2,1)S(1)}, bf16[64,4096]{1,0:T(8,128)(2,1)S(1)}, u32[]{:S(2)}, u32[]{:S(2)}) %collective-permute-start.15) | collective-permute-done | bytes 524320 | tf_op jit(solution)/shard_map/ppermute | solution.py:42
  104.2 0.1 collective-permute-done.16
  104.2 0.1 add_convert_fusion.1
  104.4 1.2 %collective-permute-start.17 = (bf16[64,4096]{1,0:T(8,128)(2,1)S(1)}, bf16[64,4096]{1,0:T(8,128)(2,1)S(1)}, u32[]{:S(2)}, u32[]{:S(2)}) collective-permute-start(bf16[64,4096]{1,0:T(8,128)(2,1)S(1)} %add_convert_fusion.1), channel_id=1, source_target_pairs={{0,9},{2,8},{4,10},{6,12},{7,14},{5,15},{3,13},{1,11},{8,1},{10,0}... | collective-permute-start | bytes 1572872 | tf_op jit(solution)/shard_map/ppermute | solution.py:42
  105.6 0.0 collective-permute-done.18
  105.6 3.6 %fusion = (bf16[384,2048]{1,0:T(8,128)(2,1)}, bf16[384,2048]{1,0:T(8,128)(2,1)}, bf16[384,2048]{1,0:T(8,128)(2,1)}) fusion(bf16[384,2048]{1,0:T(8,128)(2,1)S(1)} %get-tuple-element.122, bf16[3,384,2048]{2,1,0:T(8,128)(2,1)S(1)} %collective-permute-done.18, bf16[384,2048]{1,0:T(8,128)(2,1)S(1)} %get-tuple-element.121, bf16[384,2048]{1,0:T(8,128)(2,1)S(1)} %get-tuple-element.119), kind=kLoop, calls=%fused_computation.1 | loop fusion | flops 9437184 | bytes 14155776 | tf_op jit(solution)/shard_map/convert_element_type | solution.py:261
  109.2 9.7 %collective-permute-done.17 = bf16[64,4096]{1,0:T(8,128)(2,1)S(1)} collective-permute-done((bf16[64,4096]{1,0:T(8,128)(2,1)S(1)}, bf16[64,4096]{1,0:T(8,128)(2,1)S(1)}, u32[]{:S(2)}, u32[]{:S(2)}) %collective-permute-start.17) | collective-permute-done | bytes 524320 | tf_op jit(solution)/shard_map/ppermute | solution.py:42
  119.0 0.2 fusion.3
  119.2 0.8 fusion.4
Async XLA Ops:
  0.6 30.0 %collective-permute-start.3 = (bf16[384,2048]{1,0:T(8,128)(2,1)}, bf16[384,2048]{1,0:T(8,128)(2,1)S(1)}, u32[]{:S(2)}, u32[]{:S(2)}) collective-permute-start(bf16[384,2048]{1,0:T(8,128)(2,1)} %bitcast.34), channel_id=1, source_target_pairs={{0,16},{16,0},{1,17},{17,1},{2,18},{18,2},{3,19},{19,3},{4,20},{20... | collective-permute-start | bytes 4718600 | tf_op jit(solution)/shard_map/ppermute | solution.py:47
  1.2 29.5 %collective-permute-start.4 = (bf16[384,2048]{1,0:T(8,128)(2,1)}, bf16[384,2048]{1,0:T(8,128)(2,1)S(1)}, u32[]{:S(2)}, u32[]{:S(2)}) collective-permute-start(bf16[384,2048]{1,0:T(8,128)(2,1)} %bitcast.36), channel_id=1, source_target_pairs={{0,16},{16,0},{1,17},{17,1},{2,18},{18,2},{3,19},{19,3},{4,20},{20... | collective-permute-start | bytes 4718600 | tf_op jit(solution)/shard_map/ppermute | solution.py:47
  1.2 29.4 %collective-permute-start.5 = (bf16[384,2048]{1,0:T(8,128)(2,1)}, bf16[384,2048]{1,0:T(8,128)(2,1)}, u32[]{:S(2)}, u32[]{:S(2)}) collective-permute-start(bf16[384,2048]{1,0:T(8,128)(2,1)} %bitcast.38), channel_id=1, source_target_pairs={{0,16},{16,0},{1,17},{17,1},{2,18},{18,2},{3,19},{19,3},{4,20},{20... | collective-permute-start | bytes 4718600 | tf_op jit(solution)/shard_map/ppermute | solution.py:47
  3.9 12.0 %collective-permute-start = (bf16[64,4224]{1,0:T(8,128)(2,1)}, bf16[64,4224]{1,0:T(8,128)(2,1)S(1)}, u32[]{:S(2)}, u32[]{:S(2)}) collective-permute-start(bf16[64,4224]{1,0:T(8,128)(2,1)} %pack_rows.1.refs_0_), channel_id=1, source_target_pairs={{0,2},{2,4},{4,6},{6,7},{7,5},{5,3},{3,1},{1,0},{8,10},{10,12},{12... | collective-permute-start | bytes 1622024 | tf_op jit(solution)/shard_map/ppermute | solution.py:42
  6.5 1.4 %copy-start.1 = (bf16[1,2,192,2048]{3,2,1,0:T(8,128)(2,1)S(1)}, bf16[1,2,192,2048]{3,2,1,0:T(8,128)(2,1)}, u32[]{:S(2)}) copy-start(bf16[1,2,192,2048]{3,2,1,0:T(8,128)(2,1)} %param.13) | copy-start | bytes 4718596
  7.9 1.4 %copy-start.2 = (bf16[1,2,192,2048]{3,2,1,0:T(8,128)(2,1)S(1)}, bf16[1,2,192,2048]{3,2,1,0:T(8,128)(2,1)}, u32[]{:S(2)}) copy-start(bf16[1,2,192,2048]{3,2,1,0:T(8,128)(2,1)} %param.14) | copy-start | bytes 4718596
  7.9 1.9 %copy-start.3 = (bf16[1,2,192,2048]{3,2,1,0:T(8,128)(2,1)S(1)}, bf16[1,2,192,2048]{3,2,1,0:T(8,128)(2,1)}, u32[]{:S(2)}) copy-start(bf16[1,2,192,2048]{3,2,1,0:T(8,128)(2,1)} %param.15) | copy-start | bytes 4718596
  9.8 1.0 copy-start
  10.9 12.7 %collective-permute-start.1 = (bf16[64,4224]{1,0:T(8,128)(2,1)S(1)}, bf16[64,4224]{1,0:T(8,128)(2,1)S(1)}, u32[]{:S(2)}, u32[]{:S(2)}) collective-permute-start(bf16[64,4224]{1,0:T(8,128)(2,1)S(1)} %copy-done), channel_id=1, source_target_pairs={{0,1},{2,0},{4,2},{6,4},{7,6},{5,7},{3,5},{1,3},{8,9},{10,8},{12,1... | collective-permute-start | bytes 1622024 | tf_op jit(solution)/shard_map/ppermute | solution.py:42
  15.8 12.3 %collective-permute-start.2 = (bf16[64,4224]{1,0:T(8,128)(2,1)S(1)}, bf16[64,4224]{1,0:T(8,128)(2,1)S(1)}, u32[]{:S(2)}, u32[]{:S(2)}) collective-permute-start(bf16[64,4224]{1,0:T(8,128)(2,1)S(1)} %collective-permute-done.refs_1_), channel_id=1, source_target_pairs={{0,2},{2,4},{4,6},{6,7},{7,5},{5,3},{3,1},{1,0},{8,10},{10,12},{12... | collective-permute-start | bytes 1622024 | tf_op jit(solution)/shard_map/ppermute | solution.py:42
  23.6 14.8 %collective-permute-start.7 = (bf16[64,4224]{1,0:T(8,128)(2,1)S(1)}, bf16[64,4224]{1,0:T(8,128)(2,1)S(1)}, u32[]{:S(2)}, u32[]{:S(2)}) collective-permute-start(bf16[64,4224]{1,0:T(8,128)(2,1)S(1)} %collective-permute-done.1.refs_2_), channel_id=1, source_target_pairs={{0,1},{2,0},{4,2},{6,4},{7,6},{5,7},{3,5},{1,3},{8,9},{10,8},{12,1... | collective-permute-start | bytes 1622024 | tf_op jit(solution)/shard_map/ppermute | solution.py:42
  28.2 11.1 %collective-permute-start.9 = (bf16[64,4224]{1,0:T(8,128)(2,1)S(1)}, bf16[64,4224]{1,0:T(8,128)(2,1)S(1)}, u32[]{:S(2)}, u32[]{:S(2)}) collective-permute-start(bf16[64,4224]{1,0:T(8,128)(2,1)S(1)} %collective-permute-done.2.refs_3_), channel_id=1, source_target_pairs={{0,2},{2,4},{4,6},{6,7},{7,5},{5,3},{3,1},{1,0},{8,10},{10,12},{12... | collective-permute-start | bytes 1622024 | tf_op jit(solution)/shard_map/ppermute | solution.py:42
  38.4 14.6 %collective-permute-start.8 = (bf16[64,4224]{1,0:T(8,128)(2,1)S(1)}, bf16[64,4224]{1,0:T(8,128)(2,1)S(1)}, u32[]{:S(2)}, u32[]{:S(2)}) collective-permute-start(bf16[64,4224]{1,0:T(8,128)(2,1)S(1)} %collective-permute-done.7.refs_0_.refs_4_), channel_id=1, source_target_pairs={{0,1},{2,0},{4,2},{6,4},{7,6},{5,7},{3,5},{1,3},{8,9},{10,8},{12,1... | collective-permute-start | bytes 1622024 | tf_op jit(solution)/shard_map/ppermute | solution.py:42
  39.2 13.7 %collective-permute-start.10 = (bf16[64,4224]{1,0:T(8,128)(2,1)S(1)}, bf16[64,4224]{1,0:T(8,128)(2,1)S(1)}, u32[]{:S(2)}, u32[]{:S(2)}) collective-permute-start(bf16[64,4224]{1,0:T(8,128)(2,1)S(1)} %collective-permute-done.9.refs_1_.refs_5_), channel_id=1, source_target_pairs={{0,2},{2,4},{4,6},{6,7},{7,5},{5,3},{3,1},{1,0},{8,10},{10,12},{12... | collective-permute-start | bytes 1622024 | tf_op jit(solution)/shard_map/ppermute | solution.py:42
  59.2 14.5 %collective-permute-start.11 = (bf16[64,4096]{1,0:T(8,128)(2,1)S(1)}, bf16[64,4096]{1,0:T(8,128)(2,1)S(1)}, u32[]{:S(2)}, u32[]{:S(2)}) collective-permute-start(bf16[64,4096]{1,0:T(8,128)(2,1)S(1)} %get-tuple-element.87), channel_id=1, source_target_pairs={{0,1},{2,0},{4,2},{6,4},{7,6},{5,7},{3,5},{1,3},{8,9},{10,8},{12,1... | collective-permute-start | bytes 1572872 | tf_op jit(solution)/shard_map/ppermute | solution.py:42
  59.3 14.4 %collective-permute-start.12 = (bf16[64,4096]{1,0:T(8,128)(2,1)S(1)}, bf16[64,4096]{1,0:T(8,128)(2,1)S(1)}, u32[]{:S(2)}, u32[]{:S(2)}) collective-permute-start(bf16[64,4096]{1,0:T(8,128)(2,1)S(1)} %get-tuple-element.88), channel_id=1, source_target_pairs={{0,2},{2,4},{4,6},{6,7},{7,5},{5,3},{3,1},{1,0},{8,10},{10,12},{12... | collective-permute-start | bytes 1572872 | tf_op jit(solution)/shard_map/ppermute | solution.py:42
  61.4 13.1 %collective-permute-start.6 = (bf16[64,4096]{1,0:T(8,128)(2,1)S(1)}, bf16[64,4096]{1,0:T(8,128)(2,1)S(1)}, u32[]{:S(2)}, u32[]{:S(2)}) collective-permute-start(bf16[64,4096]{1,0:T(8,128)(2,1)S(1)} %add_convert_fusion.6), channel_id=1, source_target_pairs={{0,8},{8,0},{1,9},{9,1},{2,10},{10,2},{3,11},{11,3},{4,12},{12,4},... | collective-permute-start | bytes 1572872 | tf_op jit(solution)/shard_map/ppermute | solution.py:47
  74.7 13.7 %collective-permute-start.14 = (bf16[64,4096]{1,0:T(8,128)(2,1)S(1)}, bf16[64,4096]{1,0:T(8,128)(2,1)S(1)}, u32[]{:S(2)}, u32[]{:S(2)}) collective-permute-start(bf16[64,4096]{1,0:T(8,128)(2,1)S(1)} %add_convert_fusion.4), channel_id=1, source_target_pairs={{0,2},{2,4},{4,6},{6,7},{7,5},{5,3},{3,1},{1,0},{8,10},{10,12},{12... | collective-permute-start | bytes 1572872 | tf_op jit(solution)/shard_map/ppermute | solution.py:42
  76.6 11.8 %collective-permute-start.13 = (bf16[64,4096]{1,0:T(8,128)(2,1)S(1)}, bf16[64,4096]{1,0:T(8,128)(2,1)S(1)}, u32[]{:S(2)}, u32[]{:S(2)}) collective-permute-start(bf16[64,4096]{1,0:T(8,128)(2,1)S(1)} %add_convert_fusion.5), channel_id=1, source_target_pairs={{0,1},{2,0},{4,2},{6,4},{7,6},{5,7},{3,5},{1,3},{8,9},{10,8},{12,1... | collective-permute-start | bytes 1572872 | tf_op jit(solution)/shard_map/ppermute | solution.py:42
  88.6 17.0 %collective-permute-start.18 = (bf16[3,384,2048]{2,1,0:T(8,128)(2,1)S(1)}, bf16[3,384,2048]{2,1,0:T(8,128)(2,1)S(1)}, u32[]{:S(2)}, u32[]{:S(2)}) collective-permute-start(bf16[3,384,2048]{2,1,0:T(8,128)(2,1)S(1)} %get-tuple-element.120), channel_id=1, source_target_pairs={{0,16},{16,0},{1,17},{17,1},{2,18},{18,2},{3,19},{19,3},{4,20},{20... | collective-permute-start | bytes 14155784 | tf_op jit(solution)/shard_map/ppermute | solution.py:47
  88.7 15.5 %collective-permute-start.15 = (bf16[64,4096]{1,0:T(8,128)(2,1)S(1)}, bf16[64,4096]{1,0:T(8,128)(2,1)S(1)}, u32[]{:S(2)}, u32[]{:S(2)}) collective-permute-start(bf16[64,4096]{1,0:T(8,128)(2,1)S(1)} %get-tuple-element.115), channel_id=1, source_target_pairs={{0,10},{2,12},{4,14},{6,15},{7,13},{5,11},{3,9},{1,8},{8,2},{10,4}... | collective-permute-start | bytes 1572872 | tf_op jit(solution)/shard_map/ppermute | solution.py:42
  91.5 12.8 %collective-permute-start.16 = (bf16[64,4096]{1,0:T(8,128)(2,1)S(1)}, bf16[64,4096]{1,0:T(8,128)(2,1)S(1)}, u32[]{:S(2)}, u32[]{:S(2)}) collective-permute-start(bf16[64,4096]{1,0:T(8,128)(2,1)S(1)} %get-tuple-element.116), channel_id=1, source_target_pairs={{0,1},{2,0},{4,2},{6,4},{7,6},{5,7},{3,5},{1,3},{8,9},{10,8},{12,1... | collective-permute-start | bytes 1572872 | tf_op jit(solution)/shard_map/ppermute | solution.py:42
  104.4 14.6 %collective-permute-start.17 = (bf16[64,4096]{1,0:T(8,128)(2,1)S(1)}, bf16[64,4096]{1,0:T(8,128)(2,1)S(1)}, u32[]{:S(2)}, u32[]{:S(2)}) collective-permute-start(bf16[64,4096]{1,0:T(8,128)(2,1)S(1)} %add_convert_fusion.1), channel_id=1, source_target_pairs={{0,9},{2,8},{4,10},{6,12},{7,14},{5,15},{3,13},{1,11},{8,1},{10,0}... | collective-permute-start | bytes 1572872 | tf_op jit(solution)/shard_map/ppermute | solution.py:42

commit v17 on v15

--- a/solution.py
+++ b/solution.py
@@ -212,7 +212,7 @@
 def weight_kernel(groups, count, *refs):
     blocks = refs[:count]
     kept = [refs[count + g * 3 : count + g * 3 + 3] for g in range(groups)]
-    outs, across = refs[-7:-1], refs[-1]
+    outs, other, across = refs[-5:-2], refs[-2], refs[-1]
     half, width = outs[0].shape
     for kind in range(3):
         start = 0
@@ -230,7 +230,7 @@
         for kind in range(3):
             total = dot(across[kind], right[kind // 2], PLAIN).astype(BF16)
             outs[kind][:, at] = total[:half]
-            outs[3 + kind][:, at] = total[half:]
+            other[kind, :, at] = total[half:]
 
     columns_of(width, column)
 
@@ -241,9 +241,10 @@
     half, total = units // 2, count * blocks[0].shape[0]
     results = pl.pallas_call(
         functools.partial(weight_kernel, len(kept), count),
-        out_shape=[jax.ShapeDtypeStruct((half, width), BF16)] * 6,
+        out_shape=[jax.ShapeDtypeStruct((half, width), BF16)] * 3
+        + [jax.ShapeDtypeStruct((3, half, width), BF16)],
         in_specs=[whole()] * (count + 3 * len(kept)),
-        out_specs=[whole()] * 6,
+        out_specs=[whole()] * 4,
         scratch_shapes=[pltpu.VMEM((3, units, total), BF16)],
         compiler_params=pltpu.CompilerParams(vmem_limit_bytes=vmem(peers)),
         cost_estimate=pl.CostEstimate(
@@ -253,7 +254,7 @@
         ),
         name="weight_grads",
     )(*blocks, *[k for group in kept for k in group])
-    return results[:3], results[3:]
+    return results[:3], results[3]
 
 
 def add(a, b):
@@ -270,7 +271,6 @@
     experts = peers * local_experts
     lanes = -(-3 * experts // 128) * 128
     shards_of = [w.reshape(half, width) for w in (gate_weight, up_weight, down_weight)]
-    other = [from_behind(w, "rep", 1) for w in shards_of]
     home = pl.pallas_call(
         functools.partial(pack_kernel, experts),
         out_shape=jax.ShapeDtypeStruct((tokens, 2 * width + lanes), BF16),
@@ -281,6 +281,7 @@
     )(row_codes[0], block_exponents[0].T, routes[0].T, route_weight[0].T, out_grad[0])
 
     tie = lax.optimization_barrier
+    other = [from_behind(w, "rep", 1) for w in shards_of]
     shards_of = tie((home, shards_of))[1]
     own = load_call(shards_of[:1]) + load_call(shards_of[1:])
     weights = list(own) + other
@@ -321,10 +322,18 @@
     own_total = received = None
     blocks = [held[name] for group in groups for name in group]
     steps = (1, -1)
-    finals = []
-    for part, step in zip(both, steps):
-        kept_here = add(home[:, part], partial["near", 0][:, part])
-        finals.append([from_behind(kept_here, "section", step)])
+    home_terms = [
+        from_behind(add(home[:, part], partial["near", 0][:, part]), "section", step)
+        for part, step in zip(both, steps)
+    ]
+    joined = [slice(0, 2 * width)] if lax.axis_size("section") == 2 else both
+
+    def crossing(value, by):
+        return [ring_shift(value[:, part], by, step) for part, step in zip(joined, steps)]
+
+    def part_of(sent, i):
+        return sent[i] if len(sent) == 2 else sent[0][:, both[i]]
+
     for k in range(ahead, 1, -1):
         near_sum = ring_shift(near_sum, -1)
         left = k - 2
@@ -334,26 +343,27 @@
             near_sum, _ = tie((near_sum, far_done))
         if k == 3:
             own_total, other_total = weight_call(blocks, kept, width, peers)
-            here = [final[0] for final in finals]
-            near_sum, own_total, other_total, _ = tie((near_sum, own_total, other_total, here))
-            lasts = [add(far_sum[:, part], partial["far", 1][:, part]) for part in both]
-            for final, last, step in zip(finals, lasts, steps):
-                final.append(ring_shift(last, 1, step))
-            near_sum, _ = tie((near_sum, lasts))
+            near_sum, own_total, other_total, home_terms = tie(
+                (near_sum, own_total, other_total, home_terms)
+            )
+            last = add(far_sum, partial["far", 1])
+            far_last = crossing(last, 1)
+            near_sum, _ = tie((near_sum, last))
             near_sum = add(near_sum, partial["near", 2])
             near_sum, other_total = tie((near_sum, other_total))
-            received = [from_behind(g, "rep", 1) for g in other_total]
+            received = from_behind(other_total, "rep", 1)
         elif k == 2:
-            here = [final[1] for final in finals]
-            near_sum, _ = tie((near_sum, here))
+            near_sum, far_last = tie((near_sum, far_last))
         elif k > 2:
             near_sum = add(near_sum, partial["near", k - 1])
-    lasts = [add(near_sum[:, part], partial["near", 1][:, part]) for part in both]
-    for final, last, step in zip(finals, lasts, steps):
-        final.append(ring_shift(last, -1, step))
+    near_last = crossing(add(near_sum, partial["near", 1]), -1)
     totals = [add(a, b) for a, b in zip(own_total, received)]
-    finals, totals = tie((finals, totals))
-    results = [sum(f.astype(F32) for f in final).astype(BF16)[None] for final in finals]
+    near_last, totals = tie((near_last, totals))
+    results = []
+    for i in range(2):
+        total = home_terms[i].astype(F32) + part_of(far_last, i).astype(F32)
+        total = total + part_of(near_last, i).astype(F32)
+        results.append(total.astype(BF16)[None])
     shape = (1, local_experts, half_units, width)
     return tuple(results) + tuple(t.reshape(shape) for t in totals)
 

time: 117 us -> 117 us (level)
  waiting for transfers between devices: 49.9 us -> 56.4 us
  starting transfers between devices: 26.5 us -> 21.5 us
  other arithmetic: 7.15 us -> 5.37 us
    ppermute x16 -> x14, waiting for transfers between devices: 49.9 us -> 56.4 us  [ring_shift(): return lax.ppermute(value, ('rep', 'section', 'exp'), pairs)]
    ppermute x16 -> x14, starting transfers between devices: 22.4 us -> 18.3 us  [ring_shift(): return lax.ppermute(value, ('rep', 'section', 'exp'), pairs)]
    convert_element_type x9 -> x7, other arithmetic: 6.12 us -> 4.34 us  [add(): return (a.astype(F32) + b.astype(F32)).astype(BF16)]
    ppermute x8 -> x6, starting transfers between devices: 4.11 us -> 3.19 us  [from_behind(): lax.ppermute(value, axis, [(i, (i + by) % peers) for i in range(peers)])]
  transfers between devices with their start and end apart: 24 -> 20, of which waited for: 12 -> 11; matrix products, arithmetic and copies ran while one was open for 5% -> 4% of each run, Pallas kernels for 24% -> 25%
where the time goes in v17:
time: 117 us
  waiting for transfers between devices  56.4 us (48%)
  Pallas kernels  28.7 us (25%)
  starting transfers between devices  21.5 us (18%)
  other arithmetic  5.37 us (5%)
  local copies, waits for them, and re-layouts  3.97 us (3%)
    ppermute x14, waiting for transfers between devices, ring_shift(): return lax.ppermute(value, ('rep', 'section', 'exp'), pairs)  56.4 us
    pallas_call x3, Pallas kernels, expert_call(): pl.pallas_call(functools.partial(expert_kernel, count, experts, local_exp...  20.1 us
    ppermute x14, starting transfers between devices, ring_shift(): return lax.ppermute(value, ('rep', 'section', 'exp'), pairs)  18.3 us
    pallas_call x1, Pallas kernels, weight_call(): pl.pallas_call(functools.partial(weight_kernel, len(kept), count), out_sh...  6.06 us
    convert_element_type x7, other arithmetic, add(): return (a.astype(F32) + b.astype(F32)).astype(BF16)  4.34 us
    unnamed x8, local copies, waits for them, and re-layouts  3.97 us
    ppermute x6, starting transfers between devices, from_behind(): lax.ppermute(value, axis, [(i, (i + by) % peers) for i in range(peers)])  3.19 us
  transfers between devices with their start and end apart: 20, of which 11 were waited for; matrix products, arithmetic and copies ran while one was open for 4% of the time, Pallas kernels for 25%

profile of v17, /device:TPU:0, one launch (start us, length us, event | category | flops | bytes accessed | tf_op | source)
XLA Modules:
  0.0 116.8 jit_solution(799548075779100093)
XLA Ops:
  0.6 0.5 collective-permute-start.4
  1.2 0.1 collective-permute-start.5
  1.2 0.4 collective-permute-start.6
  1.7 2.2 %pack_rows.1.refs_0_ = bf16[64,4224]{1,0:T(8,128)(2,1)} custom-call(bf16[64,2048]{1,0:T(8,128)(2,1)} %bitcast.45, s32[16,64]{1,0:T(8,128)} %bitcast.47, s32[8,64]{1,0:T(8,128)} %bitcast.48, f32[8,64]{1,0:T(8,128)} %bitcast.49, bf16[64,2048]{1,0:T(8,128)(2,1)} %bitcast.46), custom_call_target="tpu_custom_call" | custom-call | tf_op jit(solution)/shard_map/pack_rows/pallas_call | solution.py:274
  3.9 2.7 %collective-permute-start = (bf16[64,4224]{1,0:T(8,128)(2,1)}, bf16[64,4224]{1,0:T(8,128)(2,1)S(1)}, u32[]{:S(2)}, u32[]{:S(2)}) collective-permute-start(bf16[64,4224]{1,0:T(8,128)(2,1)} %pack_rows.1.refs_0_), channel_id=1, source_target_pairs={{0,2},{2,4},{4,6},{6,7},{7,5},{5,3},{3,1},{1,0},{8,10},{10,12},{12... | collective-permute-start | bytes 1622024 | tf_op jit(solution)/shard_map/ppermute | solution.py:42
  6.5 0.0 copy-start.1
  6.5 1.4 %copy-done.1 = bf16[1,2,192,2048]{3,2,1,0:T(8,128)(2,1)S(1)} copy-done((bf16[1,2,192,2048]{3,2,1,0:T(8,128)(2,1)S(1)}, bf16[1,2,192,2048]{3,2,1,0:T(8,128)(2,1)}, u32[]{:S(2)}) %copy-start.1) | copy-done | bytes 1572888
  7.9 0.0 copy-start.2
  7.9 0.0 copy-start.3
  7.9 0.1 load_weights.2.refs_4_.refs_2_
  8.1 1.3 %copy-done.2 = bf16[1,2,192,2048]{3,2,1,0:T(8,128)(2,1)S(1)} copy-done((bf16[1,2,192,2048]{3,2,1,0:T(8,128)(2,1)S(1)}, bf16[1,2,192,2048]{3,2,1,0:T(8,128)(2,1)}, u32[]{:S(2)}) %copy-start.2) | copy-done | bytes 1572888
  9.3 0.5 copy-done.3
  9.8 0.0 copy-start
  9.8 0.2 load_weights.3
  10.1 0.8 copy-done
  10.9 0.0 collective-permute-start.3
  10.9 5.0 %collective-permute-done.refs_1_ = bf16[64,4224]{1,0:T(8,128)(2,1)S(1)} collective-permute-done((bf16[64,4224]{1,0:T(8,128)(2,1)}, bf16[64,4224]{1,0:T(8,128)(2,1)S(1)}, u32[]{:S(2)}, u32[]{:S(2)}) %collective-permute-start) | collective-permute-done | bytes 540704 | tf_op jit(solution)/shard_map/ppermute | solution.py:42
  15.8 2.4 %collective-permute-start.1 = (bf16[64,4224]{1,0:T(8,128)(2,1)S(1)}, bf16[64,4224]{1,0:T(8,128)(2,1)S(1)}, u32[]{:S(2)}, u32[]{:S(2)}) collective-permute-start(bf16[64,4224]{1,0:T(8,128)(2,1)S(1)} %collective-permute-done.refs_1_), channel_id=1, source_target_pairs={{0,2},{2,4},{4,6},{6,7},{7,5},{5,3},{3,1},{1,0},{8,10},{10,12},{12... | collective-permute-start | bytes 1622024 | tf_op jit(solution)/shard_map/ppermute | solution.py:42
  18.2 5.4 %collective-permute-done.3.refs_2_ = bf16[64,4224]{1,0:T(8,128)(2,1)S(1)} collective-permute-done((bf16[64,4224]{1,0:T(8,128)(2,1)S(1)}, bf16[64,4224]{1,0:T(8,128)(2,1)S(1)}, u32[]{:S(2)}, u32[]{:S(2)}) %collective-permute-start.3) | collective-permute-done | bytes 540704 | tf_op jit(solution)/shard_map/ppermute | solution.py:42
  23.6 0.0 collective-permute-start.8
  23.6 4.6 %collective-permute-done.1.refs_3_ = bf16[64,4224]{1,0:T(8,128)(2,1)S(1)} collective-permute-done((bf16[64,4224]{1,0:T(8,128)(2,1)S(1)}, bf16[64,4224]{1,0:T(8,128)(2,1)S(1)}, u32[]{:S(2)}, u32[]{:S(2)}) %collective-permute-start.1) | collective-permute-done | bytes 540704 | tf_op jit(solution)/shard_map/ppermute | solution.py:42
  28.2 2.5 %collective-permute-start.2 = (bf16[64,4224]{1,0:T(8,128)(2,1)S(1)}, bf16[64,4224]{1,0:T(8,128)(2,1)S(1)}, u32[]{:S(2)}, u32[]{:S(2)}) collective-permute-start(bf16[64,4224]{1,0:T(8,128)(2,1)S(1)} %collective-permute-done.1.refs_3_), channel_id=1, source_target_pairs={{0,2},{2,4},{4,6},{6,7},{7,5},{5,3},{3,1},{1,0},{8,10},{10,12},{12... | collective-permute-start | bytes 1622024 | tf_op jit(solution)/shard_map/ppermute | solution.py:42
  30.7 6.5 %collective-permute-done.8.refs_0_.refs_4_ = bf16[64,4224]{1,0:T(8,128)(2,1)S(1)} collective-permute-done((bf16[64,4224]{1,0:T(8,128)(2,1)S(1)}, bf16[64,4224]{1,0:T(8,128)(2,1)S(1)}, u32[]{:S(2)}, u32[]{:S(2)}) %collective-permute-start.8) | collective-permute-done | bytes 540704 | tf_op jit(solution)/shard_map/ppermute | solution.py:42
  37.1 0.0 collective-permute-start.9
  37.1 0.0 collective-permute-done.4.refs_7_.refs_5_
  37.1 0.0 collective-permute-done.5.refs_8_.refs_6_
  37.1 0.0 collective-permute-done.6.refs_9_.refs_7_
  37.1 7.7 %expert_rows.3 = (bf16[64,4096]{1,0:T(8,128)(2,1)S(1)}, bf16[64,4096]{1,0:T(8,128)(2,1)S(1)}, bf16[64,4096]{1,0:T(8,128)(2,1)S(1)}, bf16[64,4096]{1,0:T(8,128)(2...) custom-call(bf16[64,4224]{1,0:T(8,128)(2,1)S(1)} %copy-done, ...), custom_call_target="tpu_custom_call" | custom-call | flops 4831838208 | bytes 13631488 | tf_op jit(solution)/shard_map/expert_rows/pallas_call | solution.py:191
  44.8 0.0 collective-permute-done.2.refs_0_.refs_6_
  44.9 2.1 %collective-permute-start.7 = (bf16[64,4224]{1,0:T(8,128)(2,1)S(1)}, bf16[64,4224]{1,0:T(8,128)(2,1)S(1)}, u32[]{:S(2)}, u32[]{:S(2)}) collective-permute-start(bf16[64,4224]{1,0:T(8,128)(2,1)S(1)} %collective-permute-done.2.refs_0_.refs_6_), channel_id=1, source_target_pairs={{0,2},{2,4},{4,6},{6,7},{7,5},{5,3},{3,1},{1,0},{8,10},{10,12},{12... | collective-permute-start | bytes 1622024 | tf_op jit(solution)/shard_map/ppermute | solution.py:42
  46.9 2.3 %collective-permute-done.9.refs_1_.refs_5_ = bf16[64,4224]{1,0:T(8,128)(2,1)S(1)} collective-permute-done((bf16[64,4224]{1,0:T(8,128)(2,1)S(1)}, bf16[64,4224]{1,0:T(8,128)(2,1)S(1)}, u32[]{:S(2)}, u32[]{:S(2)}) %collective-permute-start.9) | collective-permute-done | bytes 540704 | tf_op jit(solution)/shard_map/ppermute | solution.py:42
  49.2 6.2 %expert_rows.4 = (bf16[64,4096]{1,0:T(8,128)(2,1)S(1)}, bf16[64,4096]{1,0:T(8,128)(2,1)S(1)}, bf16[768,128]{1,0:T(8,128)(2,1)S(1)}, bf16[768,128]{1,0:T(8,128)(2,1)S(1)}, bf16[768,128]{1,0:T(8,128)(2,1)S(1)}) custom-call(bf16[64,4224]{1,0:T(8,128)(2,1)S(1)} %collective-permute-done.8.refs_0_.refs_4_, ...), custom_call_target="tpu_custom_call" | custom-call | flops 2415919104 | bytes 11534336 | tf_op jit(solution)/shard_map/expert_rows/pallas_call | solution.py:191
  55.4 2.0 %collective-permute-start.11 = (bf16[64,4096]{1,0:T(8,128)(2,1)S(1)}, bf16[64,4096]{1,0:T(8,128)(2,1)S(1)}, u32[]{:S(2)}, u32[]{:S(2)}) collective-permute-start(bf16[64,4096]{1,0:T(8,128)(2,1)S(1)} %get-tuple-element.80), channel_id=1, source_target_pairs={{0,2},{2,4},{4,6},{6,7},{7,5},{5,3},{3,1},{1,0},{8,10},{10,12},{12... | collective-permute-start | bytes 1572872 | tf_op jit(solution)/shard_map/ppermute | solution.py:42
  57.4 0.1 add_convert_fusion.7
  57.5 1.6 %collective-permute-start.13 = (bf16[64,2048]{1,0:T(8,128)(2,1)S(1)}, bf16[64,2048]{1,0:T(8,128)(2,1)S(1)}, u32[]{:S(2)}, u32[]{:S(2)}) collective-permute-start(bf16[64,2048]{1,0:T(8,128)(2,1)S(1)} %get-tuple-element.121), channel_id=1, source_target_pairs={{0,8},{8,0},{1,9},{9,1},{2,10},{10,2},{3,11},{11,3},{4,12},{12,4},... | collective-permute-start | bytes 786440 | tf_op jit(solution)/shard_map/ppermute | solution.py:47
  59.1 0.5 collective-permute-start.14
  59.6 0.0 collective-permute-done.7.refs_1_.refs_7_
  59.6 6.2 %expert_rows.5 = (bf16[64,4096]{1,0:T(8,128)(2,1)S(1)}, bf16[64,4096]{1,0:T(8,128)(2,1)S(1)}, bf16[768,128]{1,0:T(8,128)(2,1)S(1)}, bf16[768,128]{1,0:T(8,128)(2,1)S(1)}, bf16[768,128]{1,0:T(8,128)(2,1)S(1)}) custom-call(bf16[64,4224]{1,0:T(8,128)(2,1)S(1)} %collective-permute-done.2.refs_0_.refs_6_, ...), custom_call_target="tpu_custom_call" | custom-call | flops 2415919104 | bytes 11534336 | tf_op jit(solution)/shard_map/expert_rows/pallas_call | solution.py:191
  65.8 0.1 collective-permute-start.10
  66.0 1.6 %collective-permute-done.11 = bf16[64,4096]{1,0:T(8,128)(2,1)S(1)} collective-permute-done((bf16[64,4096]{1,0:T(8,128)(2,1)S(1)}, bf16[64,4096]{1,0:T(8,128)(2,1)S(1)}, u32[]{:S(2)}, u32[]{:S(2)}) %collective-permute-start.11) | collective-permute-done | bytes 524320 | tf_op jit(solution)/shard_map/ppermute | solution.py:42
  67.6 0.1 add_convert_fusion.3
  67.7 2.5 %collective-permute-start.15 = (bf16[64,4096]{1,0:T(8,128)(2,1)S(1)}, bf16[64,4096]{1,0:T(8,128)(2,1)S(1)}, u32[]{:S(2)}, u32[]{:S(2)}) collective-permute-start(bf16[64,4096]{1,0:T(8,128)(2,1)S(1)} %add_convert_fusion.3), channel_id=1, source_target_pairs={{0,2},{2,4},{4,6},{6,7},{7,5},{5,3},{3,1},{1,0},{8,10},{10,12},{12... | collective-permute-start | bytes 1572872 | tf_op jit(solution)/shard_map/ppermute | solution.py:42
  70.3 6.1 %weight_grads.1 = (bf16[384,2048]{1,0:T(8,128)(2,1)S(1)}, bf16[384,2048]{1,0:T(8,128)(2,1)S(1)}, bf16[384,2048]{1,0:T(8,128)(2,1)S(1)}, bf16[3,384,2048]{2,1,0:T(8,128)(2,1)S(1)}) custom-call(bf16[64,4224]{1,0:T(8,128)(2,1)S(1)} %copy-done, bf16[64,4224]{1,0:T(8,128)(2,1)S(1)} %collective-permute-done.refs_1_, ...), custom_call_target="tpu_custom_call" | custom-call | flops 4831838208 | bytes 13631488 | tf_op jit(solution)/shard_map/weight_grads/pallas_call | solution.py:242
  76.3 0.0 collective-permute-done.10
  76.3 0.1 add_convert_fusion.4
  76.5 0.1 collective-permute-start.12
  76.5 4.7 %collective-permute-done.15 = bf16[64,4096]{1,0:T(8,128)(2,1)S(1)} collective-permute-done((bf16[64,4096]{1,0:T(8,128)(2,1)S(1)}, bf16[64,4096]{1,0:T(8,128)(2,1)S(1)}, u32[]{:S(2)}, u32[]{:S(2)}) %collective-permute-start.15) | collective-permute-done | bytes 524320 | tf_op jit(solution)/shard_map/ppermute | solution.py:42
  81.3 0.1 add_convert_fusion.2
  81.4 0.0 collective-permute-done.13
  81.4 0.0 collective-permute-done.14
  81.4 4.3 %collective-permute-done.12 = bf16[64,4096]{1,0:T(8,128)(2,1)S(1)} collective-permute-done((bf16[64,4096]{1,0:T(8,128)(2,1)S(1)}, bf16[64,4096]{1,0:T(8,128)(2,1)S(1)}, u32[]{:S(2)}, u32[]{:S(2)}) %collective-permute-start.12) | collective-permute-done | bytes 524320 | tf_op jit(solution)/shard_map/ppermute | solution.py:42
  85.7 0.1 add_convert_fusion.1
  85.8 0.1 collective-permute-start.19
  85.9 2.6 %collective-permute-start.17 = (bf16[64,4096]{1,0:T(8,128)(2,1)S(1)}, bf16[64,4096]{1,0:T(8,128)(2,1)S(1)}, u32[]{:S(2)}, u32[]{:S(2)}) collective-permute-start(bf16[64,4096]{1,0:T(8,128)(2,1)S(1)} %add_convert_fusion.2), channel_id=1, source_target_pairs={{0,10},{2,12},{4,14},{6,15},{7,13},{5,11},{3,9},{1,8},{8,2},{10,4}... | collective-permute-start | bytes 1572872 | tf_op jit(solution)/shard_map/ppermute | solution.py:42
  88.5 0.4 collective-permute-start.16
  88.9 12.2 %collective-permute-done.17 = bf16[64,4096]{1,0:T(8,128)(2,1)S(1)} collective-permute-done((bf16[64,4096]{1,0:T(8,128)(2,1)S(1)}, bf16[64,4096]{1,0:T(8,128)(2,1)S(1)}, u32[]{:S(2)}, u32[]{:S(2)}) %collective-permute-start.17) | collective-permute-done | bytes 524320 | tf_op jit(solution)/shard_map/ppermute | solution.py:42
  101.2 0.2 collective-permute-done.16
  101.4 0.1 add_convert_fusion
  101.5 1.0 collective-permute-start.18
  102.5 0.0 collective-permute-done.19
  102.5 3.6 %fusion = (bf16[384,2048]{1,0:T(8,128)(2,1)}, bf16[384,2048]{1,0:T(8,128)(2,1)}, bf16[384,2048]{1,0:T(8,128)(2,1)}) fusion(bf16[384,2048]{1,0:T(8,128)(2,1)S(1)} %get-tuple-element.111, bf16[3,384,2048]{2,1,0:T(8,128)(2,1)S(1)} %collective-permute-done.19, bf16[384,2048]{1,0:T(8,128)(2,1)S(1)} %get-tuple-element.110, bf16[384,2048]{1,0:T(8,128)(2,1)S(1)} %get-tuple-element.108), kind=kLoop, calls=%fused_computation.1 | loop fusion | flops 9437184 | bytes 14155776 | tf_op jit(solution)/shard_map/convert_element_type | solution.py:261
  106.1 9.6 %collective-permute-done.18 = bf16[64,4096]{1,0:T(8,128)(2,1)S(1)} collective-permute-done((bf16[64,4096]{1,0:T(8,128)(2,1)S(1)}, bf16[64,4096]{1,0:T(8,128)(2,1)S(1)}, u32[]{:S(2)}, u32[]{:S(2)}) %collective-permute-start.18) | collective-permute-done | bytes 524320 | tf_op jit(solution)/shard_map/ppermute | solution.py:42
  115.7 1.0 fusion.4
Async XLA Ops:
  0.6 36.5 %collective-permute-start.4 = (bf16[384,2048]{1,0:T(8,128)(2,1)}, bf16[384,2048]{1,0:T(8,128)(2,1)S(1)}, u32[]{:S(2)}, u32[]{:S(2)}) collective-permute-start(bf16[384,2048]{1,0:T(8,128)(2,1)} %bitcast.36), channel_id=1, source_target_pairs={{0,16},{16,0},{1,17},{17,1},{2,18},{18,2},{3,19},{19,3},{4,20},{20... | collective-permute-start | bytes 4718600 | tf_op jit(solution)/shard_map/ppermute | solution.py:47
  1.2 36.0 %collective-permute-start.5 = (bf16[384,2048]{1,0:T(8,128)(2,1)}, bf16[384,2048]{1,0:T(8,128)(2,1)S(1)}, u32[]{:S(2)}, u32[]{:S(2)}) collective-permute-start(bf16[384,2048]{1,0:T(8,128)(2,1)} %bitcast.38), channel_id=1, source_target_pairs={{0,16},{16,0},{1,17},{17,1},{2,18},{18,2},{3,19},{19,3},{4,20},{20... | collective-permute-start | bytes 4718600 | tf_op jit(solution)/shard_map/ppermute | solution.py:47
  1.2 35.9 %collective-permute-start.6 = (bf16[384,2048]{1,0:T(8,128)(2,1)}, bf16[384,2048]{1,0:T(8,128)(2,1)}, u32[]{:S(2)}, u32[]{:S(2)}) collective-permute-start(bf16[384,2048]{1,0:T(8,128)(2,1)} %bitcast.40), channel_id=1, source_target_pairs={{0,16},{16,0},{1,17},{17,1},{2,18},{18,2},{3,19},{19,3},{4,20},{20... | collective-permute-start | bytes 4718600 | tf_op jit(solution)/shard_map/ppermute | solution.py:47
  3.9 12.0 %collective-permute-start = (bf16[64,4224]{1,0:T(8,128)(2,1)}, bf16[64,4224]{1,0:T(8,128)(2,1)S(1)}, u32[]{:S(2)}, u32[]{:S(2)}) collective-permute-start(bf16[64,4224]{1,0:T(8,128)(2,1)} %pack_rows.1.refs_0_), channel_id=1, source_target_pairs={{0,2},{2,4},{4,6},{6,7},{7,5},{5,3},{3,1},{1,0},{8,10},{10,12},{12... | collective-permute-start | bytes 1622024 | tf_op jit(solution)/shard_map/ppermute | solution.py:42
  6.5 1.4 %copy-start.1 = (bf16[1,2,192,2048]{3,2,1,0:T(8,128)(2,1)S(1)}, bf16[1,2,192,2048]{3,2,1,0:T(8,128)(2,1)}, u32[]{:S(2)}) copy-start(bf16[1,2,192,2048]{3,2,1,0:T(8,128)(2,1)} %param.13) | copy-start | bytes 4718596
  7.9 1.4 %copy-start.2 = (bf16[1,2,192,2048]{3,2,1,0:T(8,128)(2,1)S(1)}, bf16[1,2,192,2048]{3,2,1,0:T(8,128)(2,1)}, u32[]{:S(2)}) copy-start(bf16[1,2,192,2048]{3,2,1,0:T(8,128)(2,1)} %param.14) | copy-start | bytes 4718596
  7.9 1.9 %copy-start.3 = (bf16[1,2,192,2048]{3,2,1,0:T(8,128)(2,1)S(1)}, bf16[1,2,192,2048]{3,2,1,0:T(8,128)(2,1)}, u32[]{:S(2)}) copy-start(bf16[1,2,192,2048]{3,2,1,0:T(8,128)(2,1)} %param.15) | copy-start | bytes 4718596
  9.8 1.0 copy-start
  10.9 12.7 %collective-permute-start.3 = (bf16[64,4224]{1,0:T(8,128)(2,1)S(1)}, bf16[64,4224]{1,0:T(8,128)(2,1)S(1)}, u32[]{:S(2)}, u32[]{:S(2)}) collective-permute-start(bf16[64,4224]{1,0:T(8,128)(2,1)S(1)} %copy-done), channel_id=1, source_target_pairs={{0,1},{2,0},{4,2},{6,4},{7,6},{5,7},{3,5},{1,3},{8,9},{10,8},{12,1... | collective-permute-start | bytes 1622024 | tf_op jit(solution)/shard_map/ppermute | solution.py:42
  15.8 12.3 %collective-permute-start.1 = (bf16[64,4224]{1,0:T(8,128)(2,1)S(1)}, bf16[64,4224]{1,0:T(8,128)(2,1)S(1)}, u32[]{:S(2)}, u32[]{:S(2)}) collective-permute-start(bf16[64,4224]{1,0:T(8,128)(2,1)S(1)} %collective-permute-done.refs_1_), channel_id=1, source_target_pairs={{0,2},{2,4},{4,6},{6,7},{7,5},{5,3},{3,1},{1,0},{8,10},{10,12},{12... | collective-permute-start | bytes 1622024 | tf_op jit(solution)/shard_map/ppermute | solution.py:42
  23.6 13.5 %collective-permute-start.8 = (bf16[64,4224]{1,0:T(8,128)(2,1)S(1)}, bf16[64,4224]{1,0:T(8,128)(2,1)S(1)}, u32[]{:S(2)}, u32[]{:S(2)}) collective-permute-start(bf16[64,4224]{1,0:T(8,128)(2,1)S(1)} %collective-permute-done.3.refs_2_), channel_id=1, source_target_pairs={{0,1},{2,0},{4,2},{6,4},{7,6},{5,7},{3,5},{1,3},{8,9},{10,8},{12,1... | collective-permute-start | bytes 1622024 | tf_op jit(solution)/shard_map/ppermute | solution.py:42
  28.2 16.7 %collective-permute-start.2 = (bf16[64,4224]{1,0:T(8,128)(2,1)S(1)}, bf16[64,4224]{1,0:T(8,128)(2,1)S(1)}, u32[]{:S(2)}, u32[]{:S(2)}) collective-permute-start(bf16[64,4224]{1,0:T(8,128)(2,1)S(1)} %collective-permute-done.1.refs_3_), channel_id=1, source_target_pairs={{0,2},{2,4},{4,6},{6,7},{7,5},{5,3},{3,1},{1,0},{8,10},{10,12},{12... | collective-permute-start | bytes 1622024 | tf_op jit(solution)/shard_map/ppermute | solution.py:42
  37.1 12.1 %collective-permute-start.9 = (bf16[64,4224]{1,0:T(8,128)(2,1)S(1)}, bf16[64,4224]{1,0:T(8,128)(2,1)S(1)}, u32[]{:S(2)}, u32[]{:S(2)}) collective-permute-start(bf16[64,4224]{1,0:T(8,128)(2,1)S(1)} %collective-permute-done.8.refs_0_.refs_4_), channel_id=1, source_target_pairs={{0,1},{2,0},{4,2},{6,4},{7,6},{5,7},{3,5},{1,3},{8,9},{10,8},{12,1... | collective-permute-start | bytes 1622024 | tf_op jit(solution)/shard_map/ppermute | solution.py:42
  44.9 14.8 %collective-permute-start.7 = (bf16[64,4224]{1,0:T(8,128)(2,1)S(1)}, bf16[64,4224]{1,0:T(8,128)(2,1)S(1)}, u32[]{:S(2)}, u32[]{:S(2)}) collective-permute-start(bf16[64,4224]{1,0:T(8,128)(2,1)S(1)} %collective-permute-done.2.refs_0_.refs_6_), channel_id=1, source_target_pairs={{0,2},{2,4},{4,6},{6,7},{7,5},{5,3},{3,1},{1,0},{8,10},{10,12},{12... | collective-permute-start | bytes 1622024 | tf_op jit(solution)/shard_map/ppermute | solution.py:42
  55.4 12.2 %collective-permute-start.11 = (bf16[64,4096]{1,0:T(8,128)(2,1)S(1)}, bf16[64,4096]{1,0:T(8,128)(2,1)S(1)}, u32[]{:S(2)}, u32[]{:S(2)}) collective-permute-start(bf16[64,4096]{1,0:T(8,128)(2,1)S(1)} %get-tuple-element.80), channel_id=1, source_target_pairs={{0,2},{2,4},{4,6},{6,7},{7,5},{5,3},{3,1},{1,0},{8,10},{10,12},{12... | collective-permute-start | bytes 1572872 | tf_op jit(solution)/shard_map/ppermute | solution.py:42
  57.5 23.9 %collective-permute-start.13 = (bf16[64,2048]{1,0:T(8,128)(2,1)S(1)}, bf16[64,2048]{1,0:T(8,128)(2,1)S(1)}, u32[]{:S(2)}, u32[]{:S(2)}) collective-permute-start(bf16[64,2048]{1,0:T(8,128)(2,1)S(1)} %get-tuple-element.121), channel_id=1, source_target_pairs={{0,8},{8,0},{1,9},{9,1},{2,10},{10,2},{3,11},{11,3},{4,12},{12,4},... | collective-permute-start | bytes 786440 | tf_op jit(solution)/shard_map/ppermute | solution.py:47
  59.1 22.3 %collective-permute-start.14 = (bf16[64,2048]{1,0:T(8,128)(2,1)S(1)}, bf16[64,2048]{1,0:T(8,128)(2,1)S(1)}, u32[]{:S(2)}, u32[]{:S(2)}) collective-permute-start(bf16[64,2048]{1,0:T(8,128)(2,1)S(1)} %get-tuple-element.120), channel_id=1, source_target_pairs={{0,8},{8,0},{1,9},{9,1},{2,10},{10,2},{3,11},{11,3},{4,12},{12,4},... | collective-permute-start | bytes 786440 | tf_op jit(solution)/shard_map/ppermute | solution.py:47
  65.8 10.5 %collective-permute-start.10 = (bf16[64,4096]{1,0:T(8,128)(2,1)S(1)}, bf16[64,4096]{1,0:T(8,128)(2,1)S(1)}, u32[]{:S(2)}, u32[]{:S(2)}) collective-permute-start(bf16[64,4096]{1,0:T(8,128)(2,1)S(1)} %get-tuple-element.79), channel_id=1, source_target_pairs={{0,1},{2,0},{4,2},{6,4},{7,6},{5,7},{3,5},{1,3},{8,9},{10,8},{12,1... | collective-permute-start | bytes 1572872 | tf_op jit(solution)/shard_map/ppermute | solution.py:42
  67.7 13.6 %collective-permute-start.15 = (bf16[64,4096]{1,0:T(8,128)(2,1)S(1)}, bf16[64,4096]{1,0:T(8,128)(2,1)S(1)}, u32[]{:S(2)}, u32[]{:S(2)}) collective-permute-start(bf16[64,4096]{1,0:T(8,128)(2,1)S(1)} %add_convert_fusion.3), channel_id=1, source_target_pairs={{0,2},{2,4},{4,6},{6,7},{7,5},{5,3},{3,1},{1,0},{8,10},{10,12},{12... | collective-permute-start | bytes 1572872 | tf_op jit(solution)/shard_map/ppermute | solution.py:42
  76.5 9.2 %collective-permute-start.12 = (bf16[64,4096]{1,0:T(8,128)(2,1)S(1)}, bf16[64,4096]{1,0:T(8,128)(2,1)S(1)}, u32[]{:S(2)}, u32[]{:S(2)}) collective-permute-start(bf16[64,4096]{1,0:T(8,128)(2,1)S(1)} %add_convert_fusion.4), channel_id=1, source_target_pairs={{0,1},{2,0},{4,2},{6,4},{7,6},{5,7},{3,5},{1,3},{8,9},{10,8},{12,1... | collective-permute-start | bytes 1572872 | tf_op jit(solution)/shard_map/ppermute | solution.py:42
  85.8 16.7 %collective-permute-start.19 = (bf16[3,384,2048]{2,1,0:T(8,128)(2,1)S(1)}, bf16[3,384,2048]{2,1,0:T(8,128)(2,1)S(1)}, u32[]{:S(2)}, u32[]{:S(2)}) collective-permute-start(bf16[3,384,2048]{2,1,0:T(8,128)(2,1)S(1)} %get-tuple-element.109), channel_id=1, source_target_pairs={{0,16},{16,0},{1,17},{17,1},{2,18},{18,2},{3,19},{19,3},{4,20},{20... | collective-permute-start | bytes 14155784 | tf_op jit(solution)/shard_map/ppermute | solution.py:47
  85.9 15.3 %collective-permute-start.17 = (bf16[64,4096]{1,0:T(8,128)(2,1)S(1)}, bf16[64,4096]{1,0:T(8,128)(2,1)S(1)}, u32[]{:S(2)}, u32[]{:S(2)}) collective-permute-start(bf16[64,4096]{1,0:T(8,128)(2,1)S(1)} %add_convert_fusion.2), channel_id=1, source_target_pairs={{0,10},{2,12},{4,14},{6,15},{7,13},{5,11},{3,9},{1,8},{8,2},{10,4}... | collective-permute-start | bytes 1572872 | tf_op jit(solution)/shard_map/ppermute | solution.py:42
  88.5 12.9 %collective-permute-start.16 = (bf16[64,4096]{1,0:T(8,128)(2,1)S(1)}, bf16[64,4096]{1,0:T(8,128)(2,1)S(1)}, u32[]{:S(2)}, u32[]{:S(2)}) collective-permute-start(bf16[64,4096]{1,0:T(8,128)(2,1)S(1)} %add_convert_fusion.1), channel_id=1, source_target_pairs={{0,1},{2,0},{4,2},{6,4},{7,6},{5,7},{3,5},{1,3},{8,9},{10,8},{12,1... | collective-permute-start | bytes 1572872 | tf_op jit(solution)/shard_map/ppermute | solution.py:42
  101.5 14.2 %collective-permute-start.18 = (bf16[64,4096]{1,0:T(8,128)(2,1)S(1)}, bf16[64,4096]{1,0:T(8,128)(2,1)S(1)}, u32[]{:S(2)}, u32[]{:S(2)}) collective-permute-start(bf16[64,4096]{1,0:T(8,128)(2,1)S(1)} %add_convert_fusion), channel_id=1, source_target_pairs={{0,9},{2,8},{4,10},{6,12},{7,14},{5,15},{3,13},{1,11},{8,1},{10,0}... | collective-permute-start | bytes 1572872 | tf_op jit(solution)/shard_map/ppermute | solution.py:42

commit v18 on v17

--- a/solution.py
+++ b/solution.py
@@ -321,18 +321,14 @@
     near_sum = partial["near", ahead]
     own_total = received = None
     blocks = [held[name] for group in groups for name in group]
-    steps = (1, -1)
-    home_terms = [
-        from_behind(add(home[:, part], partial["near", 0][:, part]), "section", step)
-        for part, step in zip(both, steps)
-    ]
-    joined = [slice(0, 2 * width)] if lax.axis_size("section") == 2 else both
-
-    def crossing(value, by):
-        return [ring_shift(value[:, part], by, step) for part, step in zip(joined, steps)]
-
-    def part_of(sent, i):
-        return sent[i] if len(sent) == 2 else sent[0][:, both[i]]
+    outs, back = both
+    home_outs = from_behind(add(home[:, outs], partial["near", 0][:, outs]), "section", 1)
+
+    def last_sums(value, term):
+        return add(value[:, back], term[:, back]), add(value[:, outs], term[:, outs])
+
+    def last_step(sums, by):
+        return ring_shift(sums[0], by), ring_shift(sums[1], by, 1)
 
     for k in range(ahead, 1, -1):
         near_sum = ring_shift(near_sum, -1)
@@ -343,12 +339,12 @@
             near_sum, _ = tie((near_sum, far_done))
         if k == 3:
             own_total, other_total = weight_call(blocks, kept, width, peers)
-            near_sum, own_total, other_total, home_terms = tie(
-                (near_sum, own_total, other_total, home_terms)
+            near_sum, own_total, other_total, home_outs = tie(
+                (near_sum, own_total, other_total, home_outs)
             )
-            last = add(far_sum, partial["far", 1])
-            far_last = crossing(last, 1)
-            near_sum, _ = tie((near_sum, last))
+            sums = last_sums(far_sum, partial["far", 1])
+            far_last = last_step(sums, 1)
+            near_sum, _ = tie((near_sum, sums))
             near_sum = add(near_sum, partial["near", 2])
             near_sum, other_total = tie((near_sum, other_total))
             received = from_behind(other_total, "rep", 1)
@@ -356,14 +352,18 @@
             near_sum, far_last = tie((near_sum, far_last))
         elif k > 2:
             near_sum = add(near_sum, partial["near", k - 1])
-    near_last = crossing(add(near_sum, partial["near", 1]), -1)
+    near_back, near_outs = last_step(last_sums(near_sum, partial["near", 1]), -1)
     totals = [add(a, b) for a, b in zip(own_total, received)]
-    near_last, totals = tie((near_last, totals))
-    results = []
-    for i in range(2):
-        total = home_terms[i].astype(F32) + part_of(far_last, i).astype(F32)
-        total = total + part_of(near_last, i).astype(F32)
-        results.append(total.astype(BF16)[None])
+    near_back, totals = tie((near_back, totals))
+
+    def total(*terms):
+        return sum(term.astype(F32) for term in terms).astype(BF16)[None]
+
+    back_sum = total(home[:, back], partial["near", 0][:, back], far_last[0], near_back)
+    results = [
+        total(home_outs, far_last[1], near_outs),
+        from_behind(back_sum, "section", -1),
+    ]
     shape = (1, local_experts, half_units, width)
     return tuple(results) + tuple(t.reshape(shape) for t in totals)
 

time: 117 us -> 118 us (level)
  starting transfers between devices: 21.5 us -> 25.5 us
  waiting for transfers between devices: 56.4 us -> 52.9 us
    ppermute x14 -> x16, waiting for transfers between devices: 56.4 us -> 48.1 us  [ring_shift(): return lax.ppermute(value, ('rep', 'section', 'exp'), pairs)]
    ppermute x6, waiting for transfers between devices: 0.02 us -> 4.73 us  [from_behind(): lax.ppermute(value, axis, [(i, (i + by) % peers) for i in range(peers)])]
    ppermute x14 -> x16, starting transfers between devices: 18.3 us -> 21.9 us  [ring_shift(): return lax.ppermute(value, ('rep', 'section', 'exp'), pairs)]
    unnamed x8 -> x9, local copies, waits for them, and re-layouts: 3.97 us -> 4.67 us
  transfers between devices with their start and end apart: 20 -> 22, of which waited for: 11 -> 13; matrix products, arithmetic and copies ran while one was open for 4% -> 4% of each run, Pallas kernels for 25% -> 24%
where the time goes in v18:
time: 118 us
  waiting for transfers between devices  52.9 us (45%)
  Pallas kernels  28.8 us (24%)
  starting transfers between devices  25.5 us (22%)
  other arithmetic  5.22 us (4%)
  local copies, waits for them, and re-layouts  4.67 us (4%)
    ppermute x16, waiting for transfers between devices, ring_shift(): return lax.ppermute(value, ('rep', 'section', 'exp'), pairs)  48.1 us
    ppermute x16, starting transfers between devices, ring_shift(): return lax.ppermute(value, ('rep', 'section', 'exp'), pairs)  21.9 us
    pallas_call x3, Pallas kernels, expert_call(): pl.pallas_call(functools.partial(expert_kernel, count, experts, local_exp...  20.1 us
    pallas_call x1, Pallas kernels, weight_call(): pl.pallas_call(functools.partial(weight_kernel, len(kept), count), out_sh...  6.05 us
    ppermute x6, waiting for transfers between devices, from_behind(): lax.ppermute(value, axis, [(i, (i + by) % peers) for i in range(peers)])  4.73 us
    unnamed x9, local copies, waits for them, and re-layouts  4.67 us
    convert_element_type x7, other arithmetic, add(): return (a.astype(F32) + b.astype(F32)).astype(BF16)  4.29 us
    ppermute x6, starting transfers between devices, from_behind(): lax.ppermute(value, axis, [(i, (i + by) % peers) for i in range(peers)])  3.58 us
  transfers between devices with their start and end apart: 22, of which 13 were waited for; matrix products, arithmetic and copies ran while one was open for 4% of the time, Pallas kernels for 24%

profile of v18, /device:TPU:0, one launch (start us, length us, event | category | flops | bytes accessed | tf_op | source)
XLA Modules:
  0.0 117.7 jit_solution(8499312915722234280)
XLA Ops:
  0.6 0.5 collective-permute-start.4
  1.2 0.1 collective-permute-start.5
  1.2 0.4 collective-permute-start.6
  1.7 2.2 %pack_rows.1.refs_0_ = bf16[64,4224]{1,0:T(8,128)(2,1)} custom-call(bf16[64,2048]{1,0:T(8,128)(2,1)} %bitcast.45, s32[16,64]{1,0:T(8,128)} %bitcast.47, s32[8,64]{1,0:T(8,128)} %bitcast.48, f32[8,64]{1,0:T(8,128)} %bitcast.49, bf16[64,2048]{1,0:T(8,128)(2,1)} %bitcast.46), custom_call_target="tpu_custom_call" | custom-call | tf_op jit(solution)/shard_map/pack_rows/pallas_call | solution.py:274
  3.9 2.7 %collective-permute-start = (bf16[64,4224]{1,0:T(8,128)(2,1)}, bf16[64,4224]{1,0:T(8,128)(2,1)S(1)}, u32[]{:S(2)}, u32[]{:S(2)}) collective-permute-start(bf16[64,4224]{1,0:T(8,128)(2,1)} %pack_rows.1.refs_0_), channel_id=1, source_target_pairs={{0,2},{2,4},{4,6},{6,7},{7,5},{5,3},{3,1},{1,0},{8,10},{10,12},{12... | collective-permute-start | bytes 1622024 | tf_op jit(solution)/shard_map/ppermute | solution.py:42
  6.5 1.4 %copy-done.1 = bf16[1,2,192,2048]{3,2,1,0:T(8,128)(2,1)S(1)} copy-done((bf16[1,2,192,2048]{3,2,1,0:T(8,128)(2,1)S(1)}, bf16[1,2,192,2048]{3,2,1,0:T(8,128)(2,1)}, u32[]{:S(2)}) %copy-start.1) | copy-done | bytes 1572888
  7.9 0.1 load_weights.2.refs_4_.refs_2_
  8.1 1.3 %copy-done.2 = bf16[1,2,192,2048]{3,2,1,0:T(8,128)(2,1)S(1)} copy-done((bf16[1,2,192,2048]{3,2,1,0:T(8,128)(2,1)S(1)}, bf16[1,2,192,2048]{3,2,1,0:T(8,128)(2,1)}, u32[]{:S(2)}) %copy-start.2) | copy-done | bytes 1572888
  9.3 0.5 copy-done.3
  9.8 0.2 load_weights.3
  10.1 0.8 copy-done
  10.9 0.0 collective-permute-start.3
  10.9 5.0 %collective-permute-done.refs_1_ = bf16[64,4224]{1,0:T(8,128)(2,1)S(1)} collective-permute-done((bf16[64,4224]{1,0:T(8,128)(2,1)}, bf16[64,4224]{1,0:T(8,128)(2,1)S(1)}, u32[]{:S(2)}, u32[]{:S(2)}) %collective-permute-start) | collective-permute-done | bytes 540704 | tf_op jit(solution)/shard_map/ppermute | solution.py:42
  15.8 2.4 %collective-permute-start.1 = (bf16[64,4224]{1,0:T(8,128)(2,1)S(1)}, bf16[64,4224]{1,0:T(8,128)(2,1)S(1)}, u32[]{:S(2)}, u32[]{:S(2)}) collective-permute-start(bf16[64,4224]{1,0:T(8,128)(2,1)S(1)} %collective-permute-done.refs_1_), channel_id=1, source_target_pairs={{0,2},{2,4},{4,6},{6,7},{7,5},{5,3},{3,1},{1,0},{8,10},{10,12},{12... | collective-permute-start | bytes 1622024 | tf_op jit(solution)/shard_map/ppermute | solution.py:42
  18.2 5.4 %collective-permute-done.3.refs_2_ = bf16[64,4224]{1,0:T(8,128)(2,1)S(1)} collective-permute-done((bf16[64,4224]{1,0:T(8,128)(2,1)S(1)}, bf16[64,4224]{1,0:T(8,128)(2,1)S(1)}, u32[]{:S(2)}, u32[]{:S(2)}) %collective-permute-start.3) | collective-permute-done | bytes 540704 | tf_op jit(solution)/shard_map/ppermute | solution.py:42
  23.6 0.0 collective-permute-start.8
  23.6 4.6 %collective-permute-done.1.refs_3_ = bf16[64,4224]{1,0:T(8,128)(2,1)S(1)} collective-permute-done((bf16[64,4224]{1,0:T(8,128)(2,1)S(1)}, bf16[64,4224]{1,0:T(8,128)(2,1)S(1)}, u32[]{:S(2)}, u32[]{:S(2)}) %collective-permute-start.1) | collective-permute-done | bytes 540704 | tf_op jit(solution)/shard_map/ppermute | solution.py:42
  28.2 2.5 %collective-permute-start.2 = (bf16[64,4224]{1,0:T(8,128)(2,1)S(1)}, bf16[64,4224]{1,0:T(8,128)(2,1)S(1)}, u32[]{:S(2)}, u32[]{:S(2)}) collective-permute-start(bf16[64,4224]{1,0:T(8,128)(2,1)S(1)} %collective-permute-done.1.refs_3_), channel_id=1, source_target_pairs={{0,2},{2,4},{4,6},{6,7},{7,5},{5,3},{3,1},{1,0},{8,10},{10,12},{12... | collective-permute-start | bytes 1622024 | tf_op jit(solution)/shard_map/ppermute | solution.py:42
  30.7 6.5 %collective-permute-done.8.refs_0_.refs_4_ = bf16[64,4224]{1,0:T(8,128)(2,1)S(1)} collective-permute-done((bf16[64,4224]{1,0:T(8,128)(2,1)S(1)}, bf16[64,4224]{1,0:T(8,128)(2,1)S(1)}, u32[]{:S(2)}, u32[]{:S(2)}) %collective-permute-start.8) | collective-permute-done | bytes 540704 | tf_op jit(solution)/shard_map/ppermute | solution.py:42
  37.1 0.0 collective-permute-start.9
  37.1 0.0 collective-permute-done.4.refs_7_.refs_5_
  37.1 0.0 collective-permute-done.5.refs_8_.refs_6_
  37.1 0.0 collective-permute-done.6.refs_9_.refs_7_
  37.1 7.7 %expert_rows.3 = (bf16[64,4096]{1,0:T(8,128)(2,1)S(1)}, bf16[64,4096]{1,0:T(8,128)(2,1)S(1)}, bf16[64,4096]{1,0:T(8,128)(2,1)S(1)}, bf16[64,4096]{1,0:T(8,128)(2...) custom-call(bf16[64,4224]{1,0:T(8,128)(2,1)S(1)} %copy-done, ...), custom_call_target="tpu_custom_call" | custom-call | flops 4831838208 | bytes 13631488 | tf_op jit(solution)/shard_map/expert_rows/pallas_call | solution.py:191
  44.9 0.0 collective-permute-done.2.refs_0_.refs_6_
  44.9 2.1 %collective-permute-start.7 = (bf16[64,4224]{1,0:T(8,128)(2,1)S(1)}, bf16[64,4224]{1,0:T(8,128)(2,1)S(1)}, u32[]{:S(2)}, u32[]{:S(2)}) collective-permute-start(bf16[64,4224]{1,0:T(8,128)(2,1)S(1)} %collective-permute-done.2.refs_0_.refs_6_), channel_id=1, source_target_pairs={{0,2},{2,4},{4,6},{6,7},{7,5},{5,3},{3,1},{1,0},{8,10},{10,12},{12... | collective-permute-start | bytes 1622024 | tf_op jit(solution)/shard_map/ppermute | solution.py:42
  46.9 2.3 %collective-permute-done.9.refs_1_.refs_5_ = bf16[64,4224]{1,0:T(8,128)(2,1)S(1)} collective-permute-done((bf16[64,4224]{1,0:T(8,128)(2,1)S(1)}, bf16[64,4224]{1,0:T(8,128)(2,1)S(1)}, u32[]{:S(2)}, u32[]{:S(2)}) %collective-permute-start.9) | collective-permute-done | bytes 540704 | tf_op jit(solution)/shard_map/ppermute | solution.py:42
  49.2 6.2 %expert_rows.4 = (bf16[64,4096]{1,0:T(8,128)(2,1)S(1)}, bf16[64,4096]{1,0:T(8,128)(2,1)S(1)}, bf16[768,128]{1,0:T(8,128)(2,1)S(1)}, bf16[768,128]{1,0:T(8,128)(2,1)S(1)}, bf16[768,128]{1,0:T(8,128)(2,1)S(1)}) custom-call(bf16[64,4224]{1,0:T(8,128)(2,1)S(1)} %collective-permute-done.8.refs_0_.refs_4_, ...), custom_call_target="tpu_custom_call" | custom-call | flops 2415919104 | bytes 11534336 | tf_op jit(solution)/shard_map/expert_rows/pallas_call | solution.py:191
  55.4 2.0 %collective-permute-start.11 = (bf16[64,4096]{1,0:T(8,128)(2,1)S(1)}, bf16[64,4096]{1,0:T(8,128)(2,1)S(1)}, u32[]{:S(2)}, u32[]{:S(2)}) collective-permute-start(bf16[64,4096]{1,0:T(8,128)(2,1)S(1)} %get-tuple-element.80), channel_id=1, source_target_pairs={{0,2},{2,4},{4,6},{6,7},{7,5},{5,3},{3,1},{1,0},{8,10},{10,12},{12... | collective-permute-start | bytes 1572872 | tf_op jit(solution)/shard_map/ppermute | solution.py:42
  57.4 0.1 add_convert_fusion.9
  57.5 1.6 %collective-permute-start.13 = (bf16[64,2048]{1,0:T(8,128)(2,1)S(1)}, bf16[64,2048]{1,0:T(8,128)(2,1)S(1)}, u32[]{:S(2)}, u32[]{:S(2)}) collective-permute-start(bf16[64,2048]{1,0:T(8,128)(2,1)S(1)} %add_convert_fusion.9), channel_id=1, source_target_pairs={{0,8},{8,0},{1,9},{9,1},{2,10},{10,2},{3,11},{11,3},{4,12},{12,4},... | collective-permute-start | bytes 786440 | tf_op jit(solution)/shard_map/ppermute | solution.py:47
  59.1 0.0 collective-permute-done.7.refs_1_.refs_7_
  59.1 6.2 %expert_rows.5 = (bf16[64,4096]{1,0:T(8,128)(2,1)S(1)}, bf16[64,4096]{1,0:T(8,128)(2,1)S(1)}, bf16[768,128]{1,0:T(8,128)(2,1)S(1)}, bf16[768,128]{1,0:T(8,128)(2,1)S(1)}, bf16[768,128]{1,0:T(8,128)(2,1)S(1)}) custom-call(bf16[64,4224]{1,0:T(8,128)(2,1)S(1)} %collective-permute-done.2.refs_0_.refs_6_, ...), custom_call_target="tpu_custom_call" | custom-call | flops 2415919104 | bytes 11534336 | tf_op jit(solution)/shard_map/expert_rows/pallas_call | solution.py:191
  65.3 0.5 collective-permute-start.10
  65.7 2.2 %collective-permute-done.11 = bf16[64,4096]{1,0:T(8,128)(2,1)S(1)} collective-permute-done((bf16[64,4096]{1,0:T(8,128)(2,1)S(1)}, bf16[64,4096]{1,0:T(8,128)(2,1)S(1)}, u32[]{:S(2)}, u32[]{:S(2)}) %collective-permute-start.11) | collective-permute-done | bytes 524320 | tf_op jit(solution)/shard_map/ppermute | solution.py:42
  67.9 0.1 add_convert_fusion.1
  68.0 2.2 %collective-permute-start.14 = (bf16[64,4096]{1,0:T(8,128)(2,1)S(1)}, bf16[64,4096]{1,0:T(8,128)(2,1)S(1)}, u32[]{:S(2)}, u32[]{:S(2)}) collective-permute-start(bf16[64,4096]{1,0:T(8,128)(2,1)S(1)} %add_convert_fusion.1), channel_id=1, source_target_pairs={{0,2},{2,4},{4,6},{6,7},{7,5},{5,3},{3,1},{1,0},{8,10},{10,12},{12... | collective-permute-start | bytes 1572872 | tf_op jit(solution)/shard_map/ppermute | solution.py:42
  70.3 4.3 %collective-permute-done.10 = bf16[64,4096]{1,0:T(8,128)(2,1)S(1)} collective-permute-done((bf16[64,4096]{1,0:T(8,128)(2,1)S(1)}, bf16[64,4096]{1,0:T(8,128)(2,1)S(1)}, u32[]{:S(2)}, u32[]{:S(2)}) %collective-permute-start.10) | collective-permute-done | bytes 524320 | tf_op jit(solution)/shard_map/ppermute | solution.py:42
  74.5 0.1 add_convert_fusion.2
  74.6 0.5 collective-permute-start.12
  75.1 6.1 %weight_grads.1 = (bf16[384,2048]{1,0:T(8,128)(2,1)S(1)}, bf16[384,2048]{1,0:T(8,128)(2,1)S(1)}, bf16[384,2048]{1,0:T(8,128)(2,1)S(1)}, bf16[3,384,2048]{2,1,0:T(8,128)(2,1)S(1)}) custom-call(bf16[64,4224]{1,0:T(8,128)(2,1)S(1)} %copy-done, bf16[64,4224]{1,0:T(8,128)(2,1)S(1)} %collective-permute-done.refs_1_, ...), custom_call_target="tpu_custom_call" | custom-call | flops 4831838208 | bytes 13631488 | tf_op jit(solution)/shard_map/weight_grads/pallas_call | solution.py:242
  81.2 0.1 collective-permute-done.14
  81.3 0.1 add_convert_fusion.7
  81.4 2.4 %collective-permute-done.12 = bf16[64,4096]{1,0:T(8,128)(2,1)S(1)} collective-permute-done((bf16[64,4096]{1,0:T(8,128)(2,1)S(1)}, bf16[64,4096]{1,0:T(8,128)(2,1)S(1)}, u32[]{:S(2)}, u32[]{:S(2)}) %collective-permute-start.12) | collective-permute-done | bytes 524320 | tf_op jit(solution)/shard_map/ppermute | solution.py:42
  83.9 0.1 add_convert_fusion
  84.0 0.1 collective-permute-start.20
  84.1 0.5 collective-permute-start.15
  84.5 1.6 %collective-permute-start.16 = (bf16[64,2048]{1,0:T(8,128)(2,1)S(1)}, bf16[64,2048]{1,0:T(8,128)(2,1)S(1)}, u32[]{:S(2)}, u32[]{:S(2)}) collective-permute-start(bf16[64,2048]{1,0:T(8,128)(2,1)S(1)} %get-tuple-element.123), channel_id=1, source_target_pairs={{0,2},{2,4},{4,6},{6,7},{7,5},{5,3},{3,1},{1,0},{8,10},{10,12},{12... | collective-permute-start | bytes 786440 | tf_op jit(solution)/shard_map/ppermute | solution.py:42
  86.2 2.2 %collective-permute-start.17 = (bf16[64,2048]{1,0:T(8,128)(2,1)S(1)}, bf16[64,2048]{1,0:T(8,128)(2,1)S(1)}, u32[]{:S(2)}, u32[]{:S(2)}) collective-permute-start(bf16[64,2048]{1,0:T(8,128)(2,1)S(1)} %get-tuple-element.122), channel_id=1, source_target_pairs={{0,10},{2,12},{4,14},{6,15},{7,13},{5,11},{3,9},{1,8},{8,2},{10,4}... | collective-permute-start | bytes 786440 | tf_op jit(solution)/shard_map/ppermute | solution.py:42
  88.4 5.3 %collective-permute-done.16 = bf16[64,2048]{1,0:T(8,128)(2,1)S(1)} collective-permute-done((bf16[64,2048]{1,0:T(8,128)(2,1)S(1)}, bf16[64,2048]{1,0:T(8,128)(2,1)S(1)}, u32[]{:S(2)}, u32[]{:S(2)}) %collective-permute-start.16) | collective-permute-done | bytes 262176 | tf_op jit(solution)/shard_map/ppermute | solution.py:42
  93.7 5.9 %collective-permute-done.17 = bf16[64,2048]{1,0:T(8,128)(2,1)S(1)} collective-permute-done((bf16[64,2048]{1,0:T(8,128)(2,1)S(1)}, bf16[64,2048]{1,0:T(8,128)(2,1)S(1)}, u32[]{:S(2)}, u32[]{:S(2)}) %collective-permute-start.17) | collective-permute-done | bytes 262176 | tf_op jit(solution)/shard_map/ppermute | solution.py:42
  99.6 0.0 collective-permute-done.15
  99.6 0.1 add_convert_fusion.4
  99.7 0.7 collective-permute-start.19
  100.4 2.2 %collective-permute-start.18 = (bf16[64,2048]{1,0:T(8,128)(2,1)S(1)}, bf16[64,2048]{1,0:T(8,128)(2,1)S(1)}, u32[]{:S(2)}, u32[]{:S(2)}) collective-permute-start(bf16[64,2048]{1,0:T(8,128)(2,1)S(1)} %get-tuple-element.121), channel_id=1, source_target_pairs={{0,9},{2,8},{4,10},{6,12},{7,14},{5,15},{3,13},{1,11},{8,1},{10,0}... | collective-permute-start | bytes 786440 | tf_op jit(solution)/shard_map/ppermute | solution.py:42
  102.6 0.0 collective-permute-done.20
  102.6 3.6 %fusion = (bf16[384,2048]{1,0:T(8,128)(2,1)}, bf16[384,2048]{1,0:T(8,128)(2,1)}, bf16[384,2048]{1,0:T(8,128)(2,1)}) fusion(bf16[384,2048]{1,0:T(8,128)(2,1)S(1)} %get-tuple-element.112, bf16[3,384,2048]{2,1,0:T(8,128)(2,1)S(1)} %collective-permute-done.20, bf16[384,2048]{1,0:T(8,128)(2,1)S(1)} %get-tuple-element.111, bf16[384,2048]{1,0:T(8,128)(2,1)S(1)} %get-tuple-element.109), kind=kLoop, calls=%fused_computation.1 | loop fusion | flops 9437184 | bytes 14155776 | tf_op jit(solution)/shard_map/convert_element_type | solution.py:261
  106.2 0.0 collective-permute-done.19
  106.2 0.1 fusion.4
  106.4 0.9 collective-permute-start.21
  107.3 4.3 %collective-permute-done.18 = bf16[64,2048]{1,0:T(8,128)(2,1)S(1)} collective-permute-done((bf16[64,2048]{1,0:T(8,128)(2,1)S(1)}, bf16[64,2048]{1,0:T(8,128)(2,1)S(1)}, u32[]{:S(2)}, u32[]{:S(2)}) %collective-permute-start.18) | collective-permute-done | bytes 262176 | tf_op jit(solution)/shard_map/ppermute | solution.py:42
  111.5 0.8 fusion.3
  112.3 4.7 %collective-permute-done.21 = bf16[1,64,2048]{2,1,0:T(8,128)(2,1)S(1)} collective-permute-done((bf16[1,64,2048]{2,1,0:T(8,128)(2,1)S(1)}, bf16[1,64,2048]{2,1,0:T(8,128)(2,1)S(1)}, u32[]{:S(2)}, u32[]{:S(2)}) %collective-permute-start.21) | collective-permute-done | bytes 262176 | tf_op jit(solution)/shard_map/ppermute | solution.py:47
  117.0 0.7 copy.14
  (5 shorter events, 0.0 us)
Async XLA Ops:
  0.6 36.5 %collective-permute-start.4 = (bf16[384,2048]{1,0:T(8,128)(2,1)}, bf16[384,2048]{1,0:T(8,128)(2,1)S(1)}, u32[]{:S(2)}, u32[]{:S(2)}) collective-permute-start(bf16[384,2048]{1,0:T(8,128)(2,1)} %bitcast.36), channel_id=1, source_target_pairs={{0,16},{16,0},{1,17},{17,1},{2,18},{18,2},{3,19},{19,3},{4,20},{20... | collective-permute-start | bytes 4718600 | tf_op jit(solution)/shard_map/ppermute | solution.py:47
  1.2 36.0 %collective-permute-start.5 = (bf16[384,2048]{1,0:T(8,128)(2,1)}, bf16[384,2048]{1,0:T(8,128)(2,1)S(1)}, u32[]{:S(2)}, u32[]{:S(2)}) collective-permute-start(bf16[384,2048]{1,0:T(8,128)(2,1)} %bitcast.38), channel_id=1, source_target_pairs={{0,16},{16,0},{1,17},{17,1},{2,18},{18,2},{3,19},{19,3},{4,20},{20... | collective-permute-start | bytes 4718600 | tf_op jit(solution)/shard_map/ppermute | solution.py:47
  1.2 35.9 %collective-permute-start.6 = (bf16[384,2048]{1,0:T(8,128)(2,1)}, bf16[384,2048]{1,0:T(8,128)(2,1)}, u32[]{:S(2)}, u32[]{:S(2)}) collective-permute-start(bf16[384,2048]{1,0:T(8,128)(2,1)} %bitcast.40), channel_id=1, source_target_pairs={{0,16},{16,0},{1,17},{17,1},{2,18},{18,2},{3,19},{19,3},{4,20},{20... | collective-permute-start | bytes 4718600 | tf_op jit(solution)/shard_map/ppermute | solution.py:47
  3.9 12.0 %collective-permute-start = (bf16[64,4224]{1,0:T(8,128)(2,1)}, bf16[64,4224]{1,0:T(8,128)(2,1)S(1)}, u32[]{:S(2)}, u32[]{:S(2)}) collective-permute-start(bf16[64,4224]{1,0:T(8,128)(2,1)} %pack_rows.1.refs_0_), channel_id=1, source_target_pairs={{0,2},{2,4},{4,6},{6,7},{7,5},{5,3},{3,1},{1,0},{8,10},{10,12},{12... | collective-permute-start | bytes 1622024 | tf_op jit(solution)/shard_map/ppermute | solution.py:42
  6.5 1.4 %copy-start.1 = (bf16[1,2,192,2048]{3,2,1,0:T(8,128)(2,1)S(1)}, bf16[1,2,192,2048]{3,2,1,0:T(8,128)(2,1)}, u32[]{:S(2)}) copy-start(bf16[1,2,192,2048]{3,2,1,0:T(8,128)(2,1)} %param.13) | copy-start | bytes 4718596
  7.9 1.4 %copy-start.2 = (bf16[1,2,192,2048]{3,2,1,0:T(8,128)(2,1)S(1)}, bf16[1,2,192,2048]{3,2,1,0:T(8,128)(2,1)}, u32[]{:S(2)}) copy-start(bf16[1,2,192,2048]{3,2,1,0:T(8,128)(2,1)} %param.14) | copy-start | bytes 4718596
  7.9 1.9 %copy-start.3 = (bf16[1,2,192,2048]{3,2,1,0:T(8,128)(2,1)S(1)}, bf16[1,2,192,2048]{3,2,1,0:T(8,128)(2,1)}, u32[]{:S(2)}) copy-start(bf16[1,2,192,2048]{3,2,1,0:T(8,128)(2,1)} %param.15) | copy-start | bytes 4718596
  9.8 1.0 copy-start
  10.9 12.7 %collective-permute-start.3 = (bf16[64,4224]{1,0:T(8,128)(2,1)S(1)}, bf16[64,4224]{1,0:T(8,128)(2,1)S(1)}, u32[]{:S(2)}, u32[]{:S(2)}) collective-permute-start(bf16[64,4224]{1,0:T(8,128)(2,1)S(1)} %copy-done), channel_id=1, source_target_pairs={{0,1},{2,0},{4,2},{6,4},{7,6},{5,7},{3,5},{1,3},{8,9},{10,8},{12,1... | collective-permute-start | bytes 1622024 | tf_op jit(solution)/shard_map/ppermute | solution.py:42
  15.8 12.3 %collective-permute-start.1 = (bf16[64,4224]{1,0:T(8,128)(2,1)S(1)}, bf16[64,4224]{1,0:T(8,128)(2,1)S(1)}, u32[]{:S(2)}, u32[]{:S(2)}) collective-permute-start(bf16[64,4224]{1,0:T(8,128)(2,1)S(1)} %collective-permute-done.refs_1_), channel_id=1, source_target_pairs={{0,2},{2,4},{4,6},{6,7},{7,5},{5,3},{3,1},{1,0},{8,10},{10,12},{12... | collective-permute-start | bytes 1622024 | tf_op jit(solution)/shard_map/ppermute | solution.py:42
  23.6 13.5 %collective-permute-start.8 = (bf16[64,4224]{1,0:T(8,128)(2,1)S(1)}, bf16[64,4224]{1,0:T(8,128)(2,1)S(1)}, u32[]{:S(2)}, u32[]{:S(2)}) collective-permute-start(bf16[64,4224]{1,0:T(8,128)(2,1)S(1)} %collective-permute-done.3.refs_2_), channel_id=1, source_target_pairs={{0,1},{2,0},{4,2},{6,4},{7,6},{5,7},{3,5},{1,3},{8,9},{10,8},{12,1... | collective-permute-start | bytes 1622024 | tf_op jit(solution)/shard_map/ppermute | solution.py:42
  28.2 16.7 %collective-permute-start.2 = (bf16[64,4224]{1,0:T(8,128)(2,1)S(1)}, bf16[64,4224]{1,0:T(8,128)(2,1)S(1)}, u32[]{:S(2)}, u32[]{:S(2)}) collective-permute-start(bf16[64,4224]{1,0:T(8,128)(2,1)S(1)} %collective-permute-done.1.refs_3_), channel_id=1, source_target_pairs={{0,2},{2,4},{4,6},{6,7},{7,5},{5,3},{3,1},{1,0},{8,10},{10,12},{12... | collective-permute-start | bytes 1622024 | tf_op jit(solution)/shard_map/ppermute | solution.py:42
  37.1 12.1 %collective-permute-start.9 = (bf16[64,4224]{1,0:T(8,128)(2,1)S(1)}, bf16[64,4224]{1,0:T(8,128)(2,1)S(1)}, u32[]{:S(2)}, u32[]{:S(2)}) collective-permute-start(bf16[64,4224]{1,0:T(8,128)(2,1)S(1)} %collective-permute-done.8.refs_0_.refs_4_), channel_id=1, source_target_pairs={{0,1},{2,0},{4,2},{6,4},{7,6},{5,7},{3,5},{1,3},{8,9},{10,8},{12,1... | collective-permute-start | bytes 1622024 | tf_op jit(solution)/shard_map/ppermute | solution.py:42
  44.9 14.2 %collective-permute-start.7 = (bf16[64,4224]{1,0:T(8,128)(2,1)S(1)}, bf16[64,4224]{1,0:T(8,128)(2,1)S(1)}, u32[]{:S(2)}, u32[]{:S(2)}) collective-permute-start(bf16[64,4224]{1,0:T(8,128)(2,1)S(1)} %collective-permute-done.2.refs_0_.refs_6_), channel_id=1, source_target_pairs={{0,2},{2,4},{4,6},{6,7},{7,5},{5,3},{3,1},{1,0},{8,10},{10,12},{12... | collective-permute-start | bytes 1622024 | tf_op jit(solution)/shard_map/ppermute | solution.py:42
  55.4 12.5 %collective-permute-start.11 = (bf16[64,4096]{1,0:T(8,128)(2,1)S(1)}, bf16[64,4096]{1,0:T(8,128)(2,1)S(1)}, u32[]{:S(2)}, u32[]{:S(2)}) collective-permute-start(bf16[64,4096]{1,0:T(8,128)(2,1)S(1)} %get-tuple-element.80), channel_id=1, source_target_pairs={{0,2},{2,4},{4,6},{6,7},{7,5},{5,3},{3,1},{1,0},{8,10},{10,12},{12... | collective-permute-start | bytes 1572872 | tf_op jit(solution)/shard_map/ppermute | solution.py:42
  57.5 24.0 %collective-permute-start.13 = (bf16[64,2048]{1,0:T(8,128)(2,1)S(1)}, bf16[64,2048]{1,0:T(8,128)(2,1)S(1)}, u32[]{:S(2)}, u32[]{:S(2)}) collective-permute-start(bf16[64,2048]{1,0:T(8,128)(2,1)S(1)} %add_convert_fusion.9), channel_id=1, source_target_pairs={{0,8},{8,0},{1,9},{9,1},{2,10},{10,2},{3,11},{11,3},{4,12},{12,4},... | collective-permute-start | bytes 786440 | tf_op jit(solution)/shard_map/ppermute | solution.py:47
  65.3 9.2 %collective-permute-start.10 = (bf16[64,4096]{1,0:T(8,128)(2,1)S(1)}, bf16[64,4096]{1,0:T(8,128)(2,1)S(1)}, u32[]{:S(2)}, u32[]{:S(2)}) collective-permute-start(bf16[64,4096]{1,0:T(8,128)(2,1)S(1)} %get-tuple-element.79), channel_id=1, source_target_pairs={{0,1},{2,0},{4,2},{6,4},{7,6},{5,7},{3,5},{1,3},{8,9},{10,8},{12,1... | collective-permute-start | bytes 1572872 | tf_op jit(solution)/shard_map/ppermute | solution.py:42
  68.0 13.3 %collective-permute-start.14 = (bf16[64,4096]{1,0:T(8,128)(2,1)S(1)}, bf16[64,4096]{1,0:T(8,128)(2,1)S(1)}, u32[]{:S(2)}, u32[]{:S(2)}) collective-permute-start(bf16[64,4096]{1,0:T(8,128)(2,1)S(1)} %add_convert_fusion.1), channel_id=1, source_target_pairs={{0,2},{2,4},{4,6},{6,7},{7,5},{5,3},{3,1},{1,0},{8,10},{10,12},{12... | collective-permute-start | bytes 1572872 | tf_op jit(solution)/shard_map/ppermute | solution.py:42
  74.6 9.2 %collective-permute-start.12 = (bf16[64,4096]{1,0:T(8,128)(2,1)S(1)}, bf16[64,4096]{1,0:T(8,128)(2,1)S(1)}, u32[]{:S(2)}, u32[]{:S(2)}) collective-permute-start(bf16[64,4096]{1,0:T(8,128)(2,1)S(1)} %add_convert_fusion.2), channel_id=1, source_target_pairs={{0,1},{2,0},{4,2},{6,4},{7,6},{5,7},{3,5},{1,3},{8,9},{10,8},{12,1... | collective-permute-start | bytes 1572872 | tf_op jit(solution)/shard_map/ppermute | solution.py:42
  84.0 18.6 %collective-permute-start.20 = (bf16[3,384,2048]{2,1,0:T(8,128)(2,1)S(1)}, bf16[3,384,2048]{2,1,0:T(8,128)(2,1)S(1)}, u32[]{:S(2)}, u32[]{:S(2)}) collective-permute-start(bf16[3,384,2048]{2,1,0:T(8,128)(2,1)S(1)} %get-tuple-element.110), channel_id=1, source_target_pairs={{0,16},{16,0},{1,17},{17,1},{2,18},{18,2},{3,19},{19,3},{4,20},{20... | collective-permute-start | bytes 14155784 | tf_op jit(solution)/shard_map/ppermute | solution.py:47
  84.1 15.5 %collective-permute-start.15 = (bf16[64,4096]{1,0:T(8,128)(2,1)S(1)}, bf16[64,4096]{1,0:T(8,128)(2,1)S(1)}, u32[]{:S(2)}, u32[]{:S(2)}) collective-permute-start(bf16[64,4096]{1,0:T(8,128)(2,1)S(1)} %add_convert_fusion), channel_id=1, source_target_pairs={{0,1},{2,0},{4,2},{6,4},{7,6},{5,7},{3,5},{1,3},{8,9},{10,8},{12,1... | collective-permute-start | bytes 1572872 | tf_op jit(solution)/shard_map/ppermute | solution.py:42
  84.5 9.2 %collective-permute-start.16 = (bf16[64,2048]{1,0:T(8,128)(2,1)S(1)}, bf16[64,2048]{1,0:T(8,128)(2,1)S(1)}, u32[]{:S(2)}, u32[]{:S(2)}) collective-permute-start(bf16[64,2048]{1,0:T(8,128)(2,1)S(1)} %get-tuple-element.123), channel_id=1, source_target_pairs={{0,2},{2,4},{4,6},{6,7},{7,5},{5,3},{3,1},{1,0},{8,10},{10,12},{12... | collective-permute-start | bytes 786440 | tf_op jit(solution)/shard_map/ppermute | solution.py:42
  86.2 13.4 %collective-permute-start.17 = (bf16[64,2048]{1,0:T(8,128)(2,1)S(1)}, bf16[64,2048]{1,0:T(8,128)(2,1)S(1)}, u32[]{:S(2)}, u32[]{:S(2)}) collective-permute-start(bf16[64,2048]{1,0:T(8,128)(2,1)S(1)} %get-tuple-element.122), channel_id=1, source_target_pairs={{0,10},{2,12},{4,14},{6,15},{7,13},{5,11},{3,9},{1,8},{8,2},{10,4}... | collective-permute-start | bytes 786440 | tf_op jit(solution)/shard_map/ppermute | solution.py:42
  99.7 6.5 %collective-permute-start.19 = (bf16[64,2048]{1,0:T(8,128)(2,1)S(1)}, bf16[64,2048]{1,0:T(8,128)(2,1)S(1)}, u32[]{:S(2)}, u32[]{:S(2)}) collective-permute-start(bf16[64,2048]{1,0:T(8,128)(2,1)S(1)} %get-tuple-element.120), channel_id=1, source_target_pairs={{0,1},{2,0},{4,2},{6,4},{7,6},{5,7},{3,5},{1,3},{8,9},{10,8},{12,1... | collective-permute-start | bytes 786440 | tf_op jit(solution)/shard_map/ppermute | solution.py:42
  100.4 11.1 %collective-permute-start.18 = (bf16[64,2048]{1,0:T(8,128)(2,1)S(1)}, bf16[64,2048]{1,0:T(8,128)(2,1)S(1)}, u32[]{:S(2)}, u32[]{:S(2)}) collective-permute-start(bf16[64,2048]{1,0:T(8,128)(2,1)S(1)} %get-tuple-element.121), channel_id=1, source_target_pairs={{0,9},{2,8},{4,10},{6,12},{7,14},{5,15},{3,13},{1,11},{8,1},{10,0}... | collective-permute-start | bytes 786440 | tf_op jit(solution)/shard_map/ppermute | solution.py:42
  106.4 10.7 %collective-permute-start.21 = (bf16[1,64,2048]{2,1,0:T(8,128)(2,1)S(1)}, bf16[1,64,2048]{2,1,0:T(8,128)(2,1)S(1)}, u32[]{:S(2)}, u32[]{:S(2)}) collective-permute-start(bf16[1,64,2048]{2,1,0:T(8,128)(2,1)S(1)} %fusion.4), channel_id=1, source_target_pairs={{0,8},{8,0},{1,9},{9,1},{2,10},{10,2},{3,11},{11,3},{4,12},{12,4},... | collective-permute-start | bytes 786440 | tf_op jit(solution)/shard_map/ppermute | solution.py:47

commit v19 on v8

--- a/solution.py
+++ b/solution.py
@@ -212,7 +212,7 @@
 def weight_kernel(groups, count, *refs):
     blocks = refs[:count]
     kept = [refs[count + g * 3 : count + g * 3 + 3] for g in range(groups)]
-    outs, across = refs[-7:-1], refs[-1]
+    outs, other, across = refs[-5:-2], refs[-2], refs[-1]
     half, width = outs[0].shape
     for kind in range(3):
         start = 0
@@ -230,7 +230,7 @@
         for kind in range(3):
             total = dot(across[kind], right[kind // 2], PLAIN).astype(BF16)
             outs[kind][:, at] = total[:half]
-            outs[3 + kind][:, at] = total[half:]
+            other[kind, :, at] = total[half:]
 
     columns_of(width, column)
 
@@ -241,9 +241,10 @@
     half, total = units // 2, count * blocks[0].shape[0]
     results = pl.pallas_call(
         functools.partial(weight_kernel, len(kept), count),
-        out_shape=[jax.ShapeDtypeStruct((half, width), BF16)] * 6,
+        out_shape=[jax.ShapeDtypeStruct((half, width), BF16)] * 3
+        + [jax.ShapeDtypeStruct((3, half, width), BF16)],
         in_specs=[whole()] * (count + 3 * len(kept)),
-        out_specs=[whole()] * 6,
+        out_specs=[whole()] * 4,
         scratch_shapes=[pltpu.VMEM((3, units, total), BF16)],
         compiler_params=pltpu.CompilerParams(vmem_limit_bytes=vmem(peers)),
         cost_estimate=pl.CostEstimate(
@@ -253,7 +254,7 @@
         ),
         name="weight_grads",
     )(*blocks, *[k for group in kept for k in group])
-    return results[:3], results[3:]
+    return results[:3], results[3]
 
 
 def add(a, b):
@@ -345,15 +346,22 @@
         elif k == 2:
             here = [final[1] for final in finals]
             near_sum, other_total, _ = tie((near_sum, other_total, here))
-            received = [from_behind(g, "rep", 1) for g in other_total]
+            received = from_behind(other_total, "rep", 1)
         elif k > 2:
             near_sum = add(near_sum, partial["near", k - 1])
-    lasts = [add(near_sum[:, part], partial["near", 1][:, part]) for part in both]
-    for final, last, step in zip(finals, lasts, steps):
-        final.append(ring_shift(last, -1, step))
+    joined = [slice(0, 2 * width)] if lax.axis_size("section") == 2 else both
+    near_last = [
+        ring_shift(add(near_sum[:, part], partial["near", 1][:, part]), -1, step)
+        for part, step in zip(joined, steps)
+    ]
     totals = [add(a, b) for a, b in zip(own_total, received)]
-    finals, totals = tie((finals, totals))
-    results = [sum(f.astype(F32) for f in final).astype(BF16)[None] for final in finals]
+    near_last, totals = tie((near_last, totals))
+    if len(near_last) == 1:
+        near_last = [near_last[0][:, part] for part in both]
+    results = [
+        sum(f.astype(F32) for f in final + [last]).astype(BF16)[None]
+        for final, last in zip(finals, near_last)
+    ]
     shape = (1, local_experts, half_units, width)
     return tuple(results) + tuple(t.reshape(shape) for t in totals)
 

time: 116 us -> 116 us (level)
  waiting for transfers between devices: 50.3 us -> 52.8 us
  other arithmetic: 7.15 us -> 5.41 us
  starting transfers between devices: 25.4 us -> 23.9 us
    ppermute x8 -> x6, waiting for transfers between devices: 0.6 us -> 5.75 us  [from_behind(): lax.ppermute(value, axis, [(i, (i + by) % peers) for i in range(peers)])]
    ppermute x16 -> x15, waiting for transfers between devices: 49.7 us -> 47.1 us  [ring_shift(): return lax.ppermute(value, ('rep', 'section', 'exp'), pairs)]
    convert_element_type x9 -> x7, other arithmetic: 6.11 us -> 4.38 us  [add(): return (a.astype(F32) + b.astype(F32)).astype(BF16)]
    ppermute x16 -> x15, starting transfers between devices: 21.4 us -> 20.4 us  [ring_shift(): return lax.ppermute(value, ('rep', 'section', 'exp'), pairs)]
    ppermute x8 -> x6, starting transfers between devices: 4 us -> 3.49 us  [from_behind(): lax.ppermute(value, axis, [(i, (i + by) % peers) for i in range(peers)])]
  transfers between devices with their start and end apart: 24 -> 21, of which waited for: 15 -> 13; matrix products, arithmetic and copies ran while one was open for 5% -> 4% of each run, Pallas kernels for 25% -> 25%
where the time goes in v19:
time: 116 us
  waiting for transfers between devices  52.8 us (46%)
  Pallas kernels  28.7 us (25%)
  starting transfers between devices  23.9 us (21%)
  other arithmetic  5.41 us (5%)
  local copies, waits for them, and re-layouts  3.97 us (3%)
    ppermute x15, waiting for transfers between devices, ring_shift(): return lax.ppermute(value, ('rep', 'section', 'exp'), pairs)  47.1 us
    ppermute x15, starting transfers between devices, ring_shift(): return lax.ppermute(value, ('rep', 'section', 'exp'), pairs)  20.4 us
    pallas_call x3, Pallas kernels, expert_call(): pl.pallas_call(functools.partial(expert_kernel, count, experts, local_exp...  20.1 us
    pallas_call x1, Pallas kernels, weight_call(): pl.pallas_call(functools.partial(weight_kernel, len(kept), count), out_sh...  6.05 us
    ppermute x6, waiting for transfers between devices, from_behind(): lax.ppermute(value, axis, [(i, (i + by) % peers) for i in range(peers)])  5.75 us
    convert_element_type x7, other arithmetic, add(): return (a.astype(F32) + b.astype(F32)).astype(BF16)  4.38 us
    unnamed x8, local copies, waits for them, and re-layouts  3.97 us
    ppermute x6, starting transfers between devices, from_behind(): lax.ppermute(value, axis, [(i, (i + by) % peers) for i in range(peers)])  3.49 us
  transfers between devices with their start and end apart: 21, of which 13 were waited for; matrix products, arithmetic and copies ran while one was open for 4% of the time, Pallas kernels for 25%

profile of v19, /device:TPU:0, one launch (start us, length us, event | category | flops | bytes accessed | tf_op | source)
XLA Modules:
  0.0 115.7 jit_solution(12707063203691566012)
XLA Ops:
  0.6 0.5 collective-permute-start.3
  1.2 0.1 collective-permute-start.4
  1.2 0.4 collective-permute-start.5
  1.7 2.2 %pack_rows.1.refs_0_ = bf16[64,4224]{1,0:T(8,128)(2,1)} custom-call(bf16[64,2048]{1,0:T(8,128)(2,1)} %bitcast.45, s32[16,64]{1,0:T(8,128)} %bitcast.47, s32[8,64]{1,0:T(8,128)} %bitcast.48, f32[8,64]{1,0:T(8,128)} %bitcast.49, bf16[64,2048]{1,0:T(8,128)(2,1)} %bitcast.46), custom_call_target="tpu_custom_call" | custom-call | tf_op jit(solution)/shard_map/pack_rows/pallas_call | solution.py:275
  3.9 2.7 %collective-permute-start = (bf16[64,4224]{1,0:T(8,128)(2,1)}, bf16[64,4224]{1,0:T(8,128)(2,1)S(1)}, u32[]{:S(2)}, u32[]{:S(2)}) collective-permute-start(bf16[64,4224]{1,0:T(8,128)(2,1)} %pack_rows.1.refs_0_), channel_id=1, source_target_pairs={{0,2},{2,4},{4,6},{6,7},{7,5},{5,3},{3,1},{1,0},{8,10},{10,12},{12... | collective-permute-start | bytes 1622024 | tf_op jit(solution)/shard_map/ppermute | solution.py:42
  6.5 0.0 copy-start.1
  6.5 1.4 %copy-done.1 = bf16[1,2,192,2048]{3,2,1,0:T(8,128)(2,1)S(1)} copy-done((bf16[1,2,192,2048]{3,2,1,0:T(8,128)(2,1)S(1)}, bf16[1,2,192,2048]{3,2,1,0:T(8,128)(2,1)}, u32[]{:S(2)}) %copy-start.1) | copy-done | bytes 1572888
  7.9 0.0 copy-start.2
  7.9 0.0 copy-start.3
  7.9 0.1 load_weights.2.refs_4_.refs_2_
  8.1 1.3 %copy-done.2 = bf16[1,2,192,2048]{3,2,1,0:T(8,128)(2,1)S(1)} copy-done((bf16[1,2,192,2048]{3,2,1,0:T(8,128)(2,1)S(1)}, bf16[1,2,192,2048]{3,2,1,0:T(8,128)(2,1)}, u32[]{:S(2)}) %copy-start.2) | copy-done | bytes 1572888
  9.3 0.5 copy-done.3
  9.8 0.2 load_weights.3
  10.1 0.8 copy-done
  10.9 0.0 collective-permute-start.1
  10.9 5.0 %collective-permute-done.refs_1_ = bf16[64,4224]{1,0:T(8,128)(2,1)S(1)} collective-permute-done((bf16[64,4224]{1,0:T(8,128)(2,1)}, bf16[64,4224]{1,0:T(8,128)(2,1)S(1)}, u32[]{:S(2)}, u32[]{:S(2)}) %collective-permute-start) | collective-permute-done | bytes 540704 | tf_op jit(solution)/shard_map/ppermute | solution.py:42
  15.8 2.4 %collective-permute-start.2 = (bf16[64,4224]{1,0:T(8,128)(2,1)S(1)}, bf16[64,4224]{1,0:T(8,128)(2,1)S(1)}, u32[]{:S(2)}, u32[]{:S(2)}) collective-permute-start(bf16[64,4224]{1,0:T(8,128)(2,1)S(1)} %collective-permute-done.refs_1_), channel_id=1, source_target_pairs={{0,2},{2,4},{4,6},{6,7},{7,5},{5,3},{3,1},{1,0},{8,10},{10,12},{12... | collective-permute-start | bytes 1622024 | tf_op jit(solution)/shard_map/ppermute | solution.py:42
  18.2 5.4 %collective-permute-done.1.refs_2_ = bf16[64,4224]{1,0:T(8,128)(2,1)S(1)} collective-permute-done((bf16[64,4224]{1,0:T(8,128)(2,1)S(1)}, bf16[64,4224]{1,0:T(8,128)(2,1)S(1)}, u32[]{:S(2)}, u32[]{:S(2)}) %collective-permute-start.1) | collective-permute-done | bytes 540704 | tf_op jit(solution)/shard_map/ppermute | solution.py:42
  23.6 0.0 collective-permute-start.8
  23.6 4.6 %collective-permute-done.2.refs_3_ = bf16[64,4224]{1,0:T(8,128)(2,1)S(1)} collective-permute-done((bf16[64,4224]{1,0:T(8,128)(2,1)S(1)}, bf16[64,4224]{1,0:T(8,128)(2,1)S(1)}, u32[]{:S(2)}, u32[]{:S(2)}) %collective-permute-start.2) | collective-permute-done | bytes 540704 | tf_op jit(solution)/shard_map/ppermute | solution.py:42
  28.2 2.5 %collective-permute-start.6 = (bf16[64,4224]{1,0:T(8,128)(2,1)S(1)}, bf16[64,4224]{1,0:T(8,128)(2,1)S(1)}, u32[]{:S(2)}, u32[]{:S(2)}) collective-permute-start(bf16[64,4224]{1,0:T(8,128)(2,1)S(1)} %collective-permute-done.2.refs_3_), channel_id=1, source_target_pairs={{0,2},{2,4},{4,6},{6,7},{7,5},{5,3},{3,1},{1,0},{8,10},{10,12},{12... | collective-permute-start | bytes 1622024 | tf_op jit(solution)/shard_map/ppermute | solution.py:42
  30.7 6.5 %collective-permute-done.8.refs_0_.refs_4_ = bf16[64,4224]{1,0:T(8,128)(2,1)S(1)} collective-permute-done((bf16[64,4224]{1,0:T(8,128)(2,1)S(1)}, bf16[64,4224]{1,0:T(8,128)(2,1)S(1)}, u32[]{:S(2)}, u32[]{:S(2)}) %collective-permute-start.8) | collective-permute-done | bytes 540704 | tf_op jit(solution)/shard_map/ppermute | solution.py:42
  37.1 0.0 collective-permute-start.9
  37.1 0.0 collective-permute-done.3.refs_7_.refs_5_
  37.1 0.0 collective-permute-done.4.refs_8_.refs_6_
  37.1 0.0 collective-permute-done.5.refs_9_.refs_7_
  37.1 7.7 %expert_rows.3 = (bf16[64,4096]{1,0:T(8,128)(2,1)S(1)}, bf16[64,4096]{1,0:T(8,128)(2,1)S(1)}, bf16[64,4096]{1,0:T(8,128)(2,1)S(1)}, bf16[64,4096]{1,0:T(8,128)(2...) custom-call(bf16[64,4224]{1,0:T(8,128)(2,1)S(1)} %copy-done, ...), custom_call_target="tpu_custom_call" | custom-call | flops 4831838208 | bytes 13631488 | tf_op jit(solution)/shard_map/expert_rows/pallas_call | solution.py:191
  44.9 0.0 collective-permute-done.6.refs_0_.refs_6_
  44.9 2.1 %collective-permute-start.7 = (bf16[64,4224]{1,0:T(8,128)(2,1)S(1)}, bf16[64,4224]{1,0:T(8,128)(2,1)S(1)}, u32[]{:S(2)}, u32[]{:S(2)}) collective-permute-start(bf16[64,4224]{1,0:T(8,128)(2,1)S(1)} %collective-permute-done.6.refs_0_.refs_6_), channel_id=1, source_target_pairs={{0,2},{2,4},{4,6},{6,7},{7,5},{5,3},{3,1},{1,0},{8,10},{10,12},{12... | collective-permute-start | bytes 1622024 | tf_op jit(solution)/shard_map/ppermute | solution.py:42
  46.9 2.3 %collective-permute-done.9.refs_1_.refs_5_ = bf16[64,4224]{1,0:T(8,128)(2,1)S(1)} collective-permute-done((bf16[64,4224]{1,0:T(8,128)(2,1)S(1)}, bf16[64,4224]{1,0:T(8,128)(2,1)S(1)}, u32[]{:S(2)}, u32[]{:S(2)}) %collective-permute-start.9) | collective-permute-done | bytes 540704 | tf_op jit(solution)/shard_map/ppermute | solution.py:42
  49.2 6.2 %expert_rows.4 = (bf16[64,4096]{1,0:T(8,128)(2,1)S(1)}, bf16[64,4096]{1,0:T(8,128)(2,1)S(1)}, bf16[768,128]{1,0:T(8,128)(2,1)S(1)}, bf16[768,128]{1,0:T(8,128)(2,1)S(1)}, bf16[768,128]{1,0:T(8,128)(2,1)S(1)}) custom-call(bf16[64,4224]{1,0:T(8,128)(2,1)S(1)} %collective-permute-done.8.refs_0_.refs_4_, ...), custom_call_target="tpu_custom_call" | custom-call | flops 2415919104 | bytes 11534336 | tf_op jit(solution)/shard_map/expert_rows/pallas_call | solution.py:191
  55.4 2.0 %collective-permute-start.11 = (bf16[64,4096]{1,0:T(8,128)(2,1)S(1)}, bf16[64,4096]{1,0:T(8,128)(2,1)S(1)}, u32[]{:S(2)}, u32[]{:S(2)}) collective-permute-start(bf16[64,4096]{1,0:T(8,128)(2,1)S(1)} %get-tuple-element.80), channel_id=1, source_target_pairs={{0,2},{2,4},{4,6},{6,7},{7,5},{5,3},{3,1},{1,0},{8,10},{10,12},{12... | collective-permute-start | bytes 1572872 | tf_op jit(solution)/shard_map/ppermute | solution.py:42
  57.4 0.0 collective-permute-done.7.refs_1_.refs_7_
  57.4 6.2 %expert_rows.5 = (bf16[64,4096]{1,0:T(8,128)(2,1)S(1)}, bf16[64,4096]{1,0:T(8,128)(2,1)S(1)}, bf16[768,128]{1,0:T(8,128)(2,1)S(1)}, bf16[768,128]{1,0:T(8,128)(2,1)S(1)}, bf16[768,128]{1,0:T(8,128)(2,1)S(1)}) custom-call(bf16[64,4224]{1,0:T(8,128)(2,1)S(1)} %collective-permute-done.6.refs_0_.refs_6_, ...), custom_call_target="tpu_custom_call" | custom-call | flops 2415919104 | bytes 11534336 | tf_op jit(solution)/shard_map/expert_rows/pallas_call | solution.py:191
  63.6 0.2 collective-permute-start.14
  63.8 4.2 %collective-permute-done.11 = bf16[64,4096]{1,0:T(8,128)(2,1)S(1)} collective-permute-done((bf16[64,4096]{1,0:T(8,128)(2,1)S(1)}, bf16[64,4096]{1,0:T(8,128)(2,1)S(1)}, u32[]{:S(2)}, u32[]{:S(2)}) %collective-permute-start.11) | collective-permute-done | bytes 524320 | tf_op jit(solution)/shard_map/ppermute | solution.py:42
  68.0 0.1 add_convert_fusion.3
  68.1 2.1 %collective-permute-start.12 = (bf16[64,4096]{1,0:T(8,128)(2,1)S(1)}, bf16[64,4096]{1,0:T(8,128)(2,1)S(1)}, u32[]{:S(2)}, u32[]{:S(2)}) collective-permute-start(bf16[64,4096]{1,0:T(8,128)(2,1)S(1)} %add_convert_fusion.3), channel_id=1, source_target_pairs={{0,2},{2,4},{4,6},{6,7},{7,5},{5,3},{3,1},{1,0},{8,10},{10,12},{12... | collective-permute-start | bytes 1572872 | tf_op jit(solution)/shard_map/ppermute | solution.py:42
  70.3 0.1 add_convert_fusion.7
  70.4 1.6 %collective-permute-start.16 = (bf16[64,2048]{1,0:T(8,128)(2,1)S(1)}, bf16[64,2048]{1,0:T(8,128)(2,1)S(1)}, u32[]{:S(2)}, u32[]{:S(2)}) collective-permute-start(bf16[64,2048]{1,0:T(8,128)(2,1)S(1)} %get-tuple-element.116), channel_id=1, source_target_pairs={{0,8},{8,0},{1,9},{9,1},{2,10},{10,2},{3,11},{11,3},{4,12},{12,4},... | collective-permute-start | bytes 786440 | tf_op jit(solution)/shard_map/ppermute | solution.py:47
  72.0 0.5 collective-permute-start.10
  72.5 1.7 %collective-permute-done.14 = bf16[64,4096]{1,0:T(8,128)(2,1)S(1)} collective-permute-done((bf16[64,4096]{1,0:T(8,128)(2,1)S(1)}, bf16[64,4096]{1,0:T(8,128)(2,1)S(1)}, u32[]{:S(2)}, u32[]{:S(2)}) %collective-permute-start.14) | collective-permute-done | bytes 524320 | tf_op jit(solution)/shard_map/ppermute | solution.py:42
  74.1 0.1 add_convert_fusion.2
  74.3 0.3 collective-permute-start.15
  74.6 6.0 %weight_grads.1 = (bf16[384,2048]{1,0:T(8,128)(2,1)S(1)}, bf16[384,2048]{1,0:T(8,128)(2,1)S(1)}, bf16[384,2048]{1,0:T(8,128)(2,1)S(1)}, bf16[3,384,2048]{2,1,0:T(8,128)(2,1)S(1)}) custom-call(bf16[64,4224]{1,0:T(8,128)(2,1)S(1)} %copy-done, bf16[64,4224]{1,0:T(8,128)(2,1)S(1)} %collective-permute-done.refs_1_, ...), custom_call_target="tpu_custom_call" | custom-call | flops 4831838208 | bytes 13631488 | tf_op jit(solution)/shard_map/weight_grads/pallas_call | solution.py:242
  80.7 0.8 collective-permute-done.12
  81.5 0.1 add_convert_fusion.6
  81.6 0.0 collective-permute-done.16
  81.6 0.0 collective-permute-done.10
  81.6 1.9 %collective-permute-done.15 = bf16[64,4096]{1,0:T(8,128)(2,1)S(1)} collective-permute-done((bf16[64,4096]{1,0:T(8,128)(2,1)S(1)}, bf16[64,4096]{1,0:T(8,128)(2,1)S(1)}, u32[]{:S(2)}, u32[]{:S(2)}) %collective-permute-start.15) | collective-permute-done | bytes 524320 | tf_op jit(solution)/shard_map/ppermute | solution.py:42
  83.5 0.1 add_convert_fusion.1
  83.6 0.3 collective-permute-start.17
  84.0 2.7 %collective-permute-start.18 = (bf16[64,2048]{1,0:T(8,128)(2,1)S(1)}, bf16[64,2048]{1,0:T(8,128)(2,1)S(1)}, u32[]{:S(2)}, u32[]{:S(2)}) collective-permute-start(bf16[64,2048]{1,0:T(8,128)(2,1)S(1)} %get-tuple-element.118), channel_id=1, source_target_pairs={{0,10},{2,12},{4,14},{6,15},{7,13},{5,11},{3,9},{1,8},{8,2},{10,4}... | collective-permute-start | bytes 786440 | tf_op jit(solution)/shard_map/ppermute | solution.py:42
  86.7 1.5 %collective-permute-start.13 = (bf16[64,2048]{1,0:T(8,128)(2,1)S(1)}, bf16[64,2048]{1,0:T(8,128)(2,1)S(1)}, u32[]{:S(2)}, u32[]{:S(2)}) collective-permute-start(bf16[64,2048]{1,0:T(8,128)(2,1)S(1)} %get-tuple-element.119), channel_id=1, source_target_pairs={{0,10},{2,12},{4,14},{6,15},{7,13},{5,11},{3,9},{1,8},{8,2},{10,4}... | collective-permute-start | bytes 786440 | tf_op jit(solution)/shard_map/ppermute | solution.py:42
  88.2 5.9 %collective-permute-done.18 = bf16[64,2048]{1,0:T(8,128)(2,1)S(1)} collective-permute-done((bf16[64,2048]{1,0:T(8,128)(2,1)S(1)}, bf16[64,2048]{1,0:T(8,128)(2,1)S(1)}, u32[]{:S(2)}, u32[]{:S(2)}) %collective-permute-start.18) | collective-permute-done | bytes 262176 | tf_op jit(solution)/shard_map/ppermute | solution.py:42
  94.1 5.1 %collective-permute-done.13 = bf16[64,2048]{1,0:T(8,128)(2,1)S(1)} collective-permute-done((bf16[64,2048]{1,0:T(8,128)(2,1)S(1)}, bf16[64,2048]{1,0:T(8,128)(2,1)S(1)}, u32[]{:S(2)}, u32[]{:S(2)}) %collective-permute-start.13) | collective-permute-done | bytes 262176 | tf_op jit(solution)/shard_map/ppermute | solution.py:42
  99.2 0.0 collective-permute-done.17
  99.2 0.4 collective-permute-start.20
  99.6 0.1 add_convert_fusion
  99.7 1.7 %collective-permute-start.19 = (bf16[64,4096]{1,0:T(8,128)(2,1)S(1)}, bf16[64,4096]{1,0:T(8,128)(2,1)S(1)}, u32[]{:S(2)}, u32[]{:S(2)}) collective-permute-start(bf16[64,4096]{1,0:T(8,128)(2,1)S(1)} %add_convert_fusion), channel_id=1, source_target_pairs={{0,9},{2,8},{4,10},{6,12},{7,14},{5,15},{3,13},{1,11},{8,1},{10,0}... | collective-permute-start | bytes 1572872 | tf_op jit(solution)/shard_map/ppermute | solution.py:42
  101.4 5.7 %collective-permute-done.20 = bf16[3,384,2048]{2,1,0:T(8,128)(2,1)S(1)} collective-permute-done((bf16[3,384,2048]{2,1,0:T(8,128)(2,1)S(1)}, bf16[3,384,2048]{2,1,0:T(8,128)(2,1)S(1)}, u32[]{:S(2)}, u32[]{:S(2)}) %collective-permute-start.20) | collective-permute-done | bytes 4718624 | tf_op jit(solution)/shard_map/ppermute | solution.py:47
  107.1 3.6 %fusion = (bf16[384,2048]{1,0:T(8,128)(2,1)}, bf16[384,2048]{1,0:T(8,128)(2,1)}, bf16[384,2048]{1,0:T(8,128)(2,1)}) fusion(bf16[384,2048]{1,0:T(8,128)(2,1)S(1)} %get-tuple-element.108, bf16[3,384,2048]{2,1,0:T(8,128)(2,1)S(1)} %collective-permute-done.20, bf16[384,2048]{1,0:T(8,128)(2,1)S(1)} %get-tuple-element.107, bf16[384,2048]{1,0:T(8,128)(2,1)S(1)} %get-tuple-element.105), kind=kLoop, calls=%fused_computation.1 | loop fusion | flops 9437184 | bytes 14155776 | tf_op jit(solution)/shard_map/convert_element_type | solution.py:261
  110.7 3.9 %collective-permute-done.19 = bf16[64,4096]{1,0:T(8,128)(2,1)S(1)} collective-permute-done((bf16[64,4096]{1,0:T(8,128)(2,1)S(1)}, bf16[64,4096]{1,0:T(8,128)(2,1)S(1)}, u32[]{:S(2)}, u32[]{:S(2)}) %collective-permute-start.19) | collective-permute-done | bytes 524320 | tf_op jit(solution)/shard_map/ppermute | solution.py:42
  114.6 1.0 fusion.4
  (1 shorter events, 0.0 us)
Async XLA Ops:
  0.6 36.5 %collective-permute-start.3 = (bf16[384,2048]{1,0:T(8,128)(2,1)}, bf16[384,2048]{1,0:T(8,128)(2,1)S(1)}, u32[]{:S(2)}, u32[]{:S(2)}) collective-permute-start(bf16[384,2048]{1,0:T(8,128)(2,1)} %bitcast.36), channel_id=1, source_target_pairs={{0,16},{16,0},{1,17},{17,1},{2,18},{18,2},{3,19},{19,3},{4,20},{20... | collective-permute-start | bytes 4718600 | tf_op jit(solution)/shard_map/ppermute | solution.py:47
  1.2 36.0 %collective-permute-start.4 = (bf16[384,2048]{1,0:T(8,128)(2,1)}, bf16[384,2048]{1,0:T(8,128)(2,1)S(1)}, u32[]{:S(2)}, u32[]{:S(2)}) collective-permute-start(bf16[384,2048]{1,0:T(8,128)(2,1)} %bitcast.38), channel_id=1, source_target_pairs={{0,16},{16,0},{1,17},{17,1},{2,18},{18,2},{3,19},{19,3},{4,20},{20... | collective-permute-start | bytes 4718600 | tf_op jit(solution)/shard_map/ppermute | solution.py:47
  1.2 35.9 %collective-permute-start.5 = (bf16[384,2048]{1,0:T(8,128)(2,1)}, bf16[384,2048]{1,0:T(8,128)(2,1)}, u32[]{:S(2)}, u32[]{:S(2)}) collective-permute-start(bf16[384,2048]{1,0:T(8,128)(2,1)} %bitcast.40), channel_id=1, source_target_pairs={{0,16},{16,0},{1,17},{17,1},{2,18},{18,2},{3,19},{19,3},{4,20},{20... | collective-permute-start | bytes 4718600 | tf_op jit(solution)/shard_map/ppermute | solution.py:47
  3.9 12.0 %collective-permute-start = (bf16[64,4224]{1,0:T(8,128)(2,1)}, bf16[64,4224]{1,0:T(8,128)(2,1)S(1)}, u32[]{:S(2)}, u32[]{:S(2)}) collective-permute-start(bf16[64,4224]{1,0:T(8,128)(2,1)} %pack_rows.1.refs_0_), channel_id=1, source_target_pairs={{0,2},{2,4},{4,6},{6,7},{7,5},{5,3},{3,1},{1,0},{8,10},{10,12},{12... | collective-permute-start | bytes 1622024 | tf_op jit(solution)/shard_map/ppermute | solution.py:42
  6.5 1.4 %copy-start.1 = (bf16[1,2,192,2048]{3,2,1,0:T(8,128)(2,1)S(1)}, bf16[1,2,192,2048]{3,2,1,0:T(8,128)(2,1)}, u32[]{:S(2)}) copy-start(bf16[1,2,192,2048]{3,2,1,0:T(8,128)(2,1)} %param.13) | copy-start | bytes 4718596
  7.9 1.4 %copy-start.2 = (bf16[1,2,192,2048]{3,2,1,0:T(8,128)(2,1)S(1)}, bf16[1,2,192,2048]{3,2,1,0:T(8,128)(2,1)}, u32[]{:S(2)}) copy-start(bf16[1,2,192,2048]{3,2,1,0:T(8,128)(2,1)} %param.14) | copy-start | bytes 4718596
  7.9 1.9 %copy-start.3 = (bf16[1,2,192,2048]{3,2,1,0:T(8,128)(2,1)S(1)}, bf16[1,2,192,2048]{3,2,1,0:T(8,128)(2,1)}, u32[]{:S(2)}) copy-start(bf16[1,2,192,2048]{3,2,1,0:T(8,128)(2,1)} %param.15) | copy-start | bytes 4718596
  9.8 1.0 copy-start
  10.9 12.7 %collective-permute-start.1 = (bf16[64,4224]{1,0:T(8,128)(2,1)S(1)}, bf16[64,4224]{1,0:T(8,128)(2,1)S(1)}, u32[]{:S(2)}, u32[]{:S(2)}) collective-permute-start(bf16[64,4224]{1,0:T(8,128)(2,1)S(1)} %copy-done), channel_id=1, source_target_pairs={{0,1},{2,0},{4,2},{6,4},{7,6},{5,7},{3,5},{1,3},{8,9},{10,8},{12,1... | collective-permute-start | bytes 1622024 | tf_op jit(solution)/shard_map/ppermute | solution.py:42
  15.8 12.3 %collective-permute-start.2 = (bf16[64,4224]{1,0:T(8,128)(2,1)S(1)}, bf16[64,4224]{1,0:T(8,128)(2,1)S(1)}, u32[]{:S(2)}, u32[]{:S(2)}) collective-permute-start(bf16[64,4224]{1,0:T(8,128)(2,1)S(1)} %collective-permute-done.refs_1_), channel_id=1, source_target_pairs={{0,2},{2,4},{4,6},{6,7},{7,5},{5,3},{3,1},{1,0},{8,10},{10,12},{12... | collective-permute-start | bytes 1622024 | tf_op jit(solution)/shard_map/ppermute | solution.py:42
  23.6 13.5 %collective-permute-start.8 = (bf16[64,4224]{1,0:T(8,128)(2,1)S(1)}, bf16[64,4224]{1,0:T(8,128)(2,1)S(1)}, u32[]{:S(2)}, u32[]{:S(2)}) collective-permute-start(bf16[64,4224]{1,0:T(8,128)(2,1)S(1)} %collective-permute-done.1.refs_2_), channel_id=1, source_target_pairs={{0,1},{2,0},{4,2},{6,4},{7,6},{5,7},{3,5},{1,3},{8,9},{10,8},{12,1... | collective-permute-start | bytes 1622024 | tf_op jit(solution)/shard_map/ppermute | solution.py:42
  28.2 16.7 %collective-permute-start.6 = (bf16[64,4224]{1,0:T(8,128)(2,1)S(1)}, bf16[64,4224]{1,0:T(8,128)(2,1)S(1)}, u32[]{:S(2)}, u32[]{:S(2)}) collective-permute-start(bf16[64,4224]{1,0:T(8,128)(2,1)S(1)} %collective-permute-done.2.refs_3_), channel_id=1, source_target_pairs={{0,2},{2,4},{4,6},{6,7},{7,5},{5,3},{3,1},{1,0},{8,10},{10,12},{12... | collective-permute-start | bytes 1622024 | tf_op jit(solution)/shard_map/ppermute | solution.py:42
  37.1 12.1 %collective-permute-start.9 = (bf16[64,4224]{1,0:T(8,128)(2,1)S(1)}, bf16[64,4224]{1,0:T(8,128)(2,1)S(1)}, u32[]{:S(2)}, u32[]{:S(2)}) collective-permute-start(bf16[64,4224]{1,0:T(8,128)(2,1)S(1)} %collective-permute-done.8.refs_0_.refs_4_), channel_id=1, source_target_pairs={{0,1},{2,0},{4,2},{6,4},{7,6},{5,7},{3,5},{1,3},{8,9},{10,8},{12,1... | collective-permute-start | bytes 1622024 | tf_op jit(solution)/shard_map/ppermute | solution.py:42
  44.9 12.5 %collective-permute-start.7 = (bf16[64,4224]{1,0:T(8,128)(2,1)S(1)}, bf16[64,4224]{1,0:T(8,128)(2,1)S(1)}, u32[]{:S(2)}, u32[]{:S(2)}) collective-permute-start(bf16[64,4224]{1,0:T(8,128)(2,1)S(1)} %collective-permute-done.6.refs_0_.refs_6_), channel_id=1, source_target_pairs={{0,2},{2,4},{4,6},{6,7},{7,5},{5,3},{3,1},{1,0},{8,10},{10,12},{12... | collective-permute-start | bytes 1622024 | tf_op jit(solution)/shard_map/ppermute | solution.py:42
  55.4 12.6 %collective-permute-start.11 = (bf16[64,4096]{1,0:T(8,128)(2,1)S(1)}, bf16[64,4096]{1,0:T(8,128)(2,1)S(1)}, u32[]{:S(2)}, u32[]{:S(2)}) collective-permute-start(bf16[64,4096]{1,0:T(8,128)(2,1)S(1)} %get-tuple-element.80), channel_id=1, source_target_pairs={{0,2},{2,4},{4,6},{6,7},{7,5},{5,3},{3,1},{1,0},{8,10},{10,12},{12... | collective-permute-start | bytes 1572872 | tf_op jit(solution)/shard_map/ppermute | solution.py:42
  63.6 10.5 %collective-permute-start.14 = (bf16[64,4096]{1,0:T(8,128)(2,1)S(1)}, bf16[64,4096]{1,0:T(8,128)(2,1)S(1)}, u32[]{:S(2)}, u32[]{:S(2)}) collective-permute-start(bf16[64,4096]{1,0:T(8,128)(2,1)S(1)} %get-tuple-element.83), channel_id=1, source_target_pairs={{0,1},{2,0},{4,2},{6,4},{7,6},{5,7},{3,5},{1,3},{8,9},{10,8},{12,1... | collective-permute-start | bytes 1572872 | tf_op jit(solution)/shard_map/ppermute | solution.py:42
  68.1 13.4 %collective-permute-start.12 = (bf16[64,4096]{1,0:T(8,128)(2,1)S(1)}, bf16[64,4096]{1,0:T(8,128)(2,1)S(1)}, u32[]{:S(2)}, u32[]{:S(2)}) collective-permute-start(bf16[64,4096]{1,0:T(8,128)(2,1)S(1)} %add_convert_fusion.3), channel_id=1, source_target_pairs={{0,2},{2,4},{4,6},{6,7},{7,5},{5,3},{3,1},{1,0},{8,10},{10,12},{12... | collective-permute-start | bytes 1572872 | tf_op jit(solution)/shard_map/ppermute | solution.py:42
  70.4 11.2 %collective-permute-start.16 = (bf16[64,2048]{1,0:T(8,128)(2,1)S(1)}, bf16[64,2048]{1,0:T(8,128)(2,1)S(1)}, u32[]{:S(2)}, u32[]{:S(2)}) collective-permute-start(bf16[64,2048]{1,0:T(8,128)(2,1)S(1)} %get-tuple-element.116), channel_id=1, source_target_pairs={{0,8},{8,0},{1,9},{9,1},{2,10},{10,2},{3,11},{11,3},{4,12},{12,4},... | collective-permute-start | bytes 786440 | tf_op jit(solution)/shard_map/ppermute | solution.py:47
  72.0 9.6 %collective-permute-start.10 = (bf16[64,2048]{1,0:T(8,128)(2,1)S(1)}, bf16[64,2048]{1,0:T(8,128)(2,1)S(1)}, u32[]{:S(2)}, u32[]{:S(2)}) collective-permute-start(bf16[64,2048]{1,0:T(8,128)(2,1)S(1)} %get-tuple-element.117), channel_id=1, source_target_pairs={{0,8},{8,0},{1,9},{9,1},{2,10},{10,2},{3,11},{11,3},{4,12},{12,4},... | collective-permute-start | bytes 786440 | tf_op jit(solution)/shard_map/ppermute | solution.py:47
  74.3 9.2 %collective-permute-start.15 = (bf16[64,4096]{1,0:T(8,128)(2,1)S(1)}, bf16[64,4096]{1,0:T(8,128)(2,1)S(1)}, u32[]{:S(2)}, u32[]{:S(2)}) collective-permute-start(bf16[64,4096]{1,0:T(8,128)(2,1)S(1)} %add_convert_fusion.2), channel_id=1, source_target_pairs={{0,1},{2,0},{4,2},{6,4},{7,6},{5,7},{3,5},{1,3},{8,9},{10,8},{12,1... | collective-permute-start | bytes 1572872 | tf_op jit(solution)/shard_map/ppermute | solution.py:42
  83.6 15.6 %collective-permute-start.17 = (bf16[64,4096]{1,0:T(8,128)(2,1)S(1)}, bf16[64,4096]{1,0:T(8,128)(2,1)S(1)}, u32[]{:S(2)}, u32[]{:S(2)}) collective-permute-start(bf16[64,4096]{1,0:T(8,128)(2,1)S(1)} %add_convert_fusion.1), channel_id=1, source_target_pairs={{0,1},{2,0},{4,2},{6,4},{7,6},{5,7},{3,5},{1,3},{8,9},{10,8},{12,1... | collective-permute-start | bytes 1572872 | tf_op jit(solution)/shard_map/ppermute | solution.py:42
  84.0 10.1 %collective-permute-start.18 = (bf16[64,2048]{1,0:T(8,128)(2,1)S(1)}, bf16[64,2048]{1,0:T(8,128)(2,1)S(1)}, u32[]{:S(2)}, u32[]{:S(2)}) collective-permute-start(bf16[64,2048]{1,0:T(8,128)(2,1)S(1)} %get-tuple-element.118), channel_id=1, source_target_pairs={{0,10},{2,12},{4,14},{6,15},{7,13},{5,11},{3,9},{1,8},{8,2},{10,4}... | collective-permute-start | bytes 786440 | tf_op jit(solution)/shard_map/ppermute | solution.py:42
  86.7 12.5 %collective-permute-start.13 = (bf16[64,2048]{1,0:T(8,128)(2,1)S(1)}, bf16[64,2048]{1,0:T(8,128)(2,1)S(1)}, u32[]{:S(2)}, u32[]{:S(2)}) collective-permute-start(bf16[64,2048]{1,0:T(8,128)(2,1)S(1)} %get-tuple-element.119), channel_id=1, source_target_pairs={{0,10},{2,12},{4,14},{6,15},{7,13},{5,11},{3,9},{1,8},{8,2},{10,4}... | collective-permute-start | bytes 786440 | tf_op jit(solution)/shard_map/ppermute | solution.py:42
  99.2 7.9 %collective-permute-start.20 = (bf16[3,384,2048]{2,1,0:T(8,128)(2,1)S(1)}, bf16[3,384,2048]{2,1,0:T(8,128)(2,1)S(1)}, u32[]{:S(2)}, u32[]{:S(2)}) collective-permute-start(bf16[3,384,2048]{2,1,0:T(8,128)(2,1)S(1)} %get-tuple-element.106), channel_id=1, source_target_pairs={{0,16},{16,0},{1,17},{17,1},{2,18},{18,2},{3,19},{19,3},{4,20},{20... | collective-permute-start | bytes 14155784 | tf_op jit(solution)/shard_map/ppermute | solution.py:47
  99.7 14.9 %collective-permute-start.19 = (bf16[64,4096]{1,0:T(8,128)(2,1)S(1)}, bf16[64,4096]{1,0:T(8,128)(2,1)S(1)}, u32[]{:S(2)}, u32[]{:S(2)}) collective-permute-start(bf16[64,4096]{1,0:T(8,128)(2,1)S(1)} %add_convert_fusion), channel_id=1, source_target_pairs={{0,9},{2,8},{4,10},{6,12},{7,14},{5,15},{3,13},{1,11},{8,1},{10,0}... | collective-permute-start | bytes 1572872 | tf_op jit(solution)/shard_map/ppermute | solution.py:42

commit v20 on v19

--- a/solution.py
+++ b/solution.py
@@ -313,15 +313,19 @@
         if k % 2 == 1 and k > 1:
             work(groups[(k - 3) // 2])
             held["near", k], kept[-1] = tie((held["near", k], kept[-1]))
+            if k <= behind:
+                held["far", k], kept[-1] = tie((held["far", k], kept[-1]))
     work(groups[-2])
     far_sum = ring_shift(partial["far", behind], 1)
     held["near", ahead], kept[-1] = tie((held["near", ahead], kept[-1]))
     work(groups[-1])
     both = (slice(0, width), slice(width, 2 * width))
     near_sum = partial["near", ahead]
+    far_sum, _ = tie((far_sum, near_sum))
     own_total = received = None
     blocks = [held[name] for group in groups for name in group]
     steps = (1, -1)
+    joined = [slice(0, 2 * width)] if lax.axis_size("section") == 2 else both
     finals = []
     here, near_sum = tie((partial["near", 0], near_sum))
     for part, step in zip(both, steps):
@@ -338,18 +342,15 @@
             own_total, other_total = weight_call(blocks, kept, width, peers)
             here = [final[0] for final in finals]
             near_sum, own_total, other_total, _ = tie((near_sum, own_total, other_total, here))
-            lasts = [add(far_sum[:, part], partial["far", 1][:, part]) for part in both]
-            for final, last, step in zip(finals, lasts, steps):
-                final.append(ring_shift(last, 1, step))
+            lasts = [add(far_sum[:, part], partial["far", 1][:, part]) for part in joined]
+            far_last = [ring_shift(last, 1, step) for last, step in zip(lasts, steps)]
             near_sum, _ = tie((near_sum, lasts))
             near_sum = add(near_sum, partial["near", 2])
         elif k == 2:
-            here = [final[1] for final in finals]
-            near_sum, other_total, _ = tie((near_sum, other_total, here))
+            near_sum, other_total, far_last = tie((near_sum, other_total, far_last))
             received = from_behind(other_total, "rep", 1)
         elif k > 2:
             near_sum = add(near_sum, partial["near", k - 1])
-    joined = [slice(0, 2 * width)] if lax.axis_size("section") == 2 else both
     near_last = [
         ring_shift(add(near_sum[:, part], partial["near", 1][:, part]), -1, step)
         for part, step in zip(joined, steps)
@@ -358,9 +359,10 @@
     near_last, totals = tie((near_last, totals))
     if len(near_last) == 1:
         near_last = [near_last[0][:, part] for part in both]
+        far_last = [far_last[0][:, part] for part in both]
     results = [
-        sum(f.astype(F32) for f in final + [last]).astype(BF16)[None]
-        for final, last in zip(finals, near_last)
+        sum(f.astype(F32) for f in (final[0], far, last)).astype(BF16)[None]
+        for final, far, last in zip(finals, far_last, near_last)
     ]
     shape = (1, local_experts, half_units, width)
     return tuple(results) + tuple(t.reshape(shape) for t in totals)

time: 116 us -> 113 us (0.974)
  starting transfers between devices: 23.9 us -> 22.3 us
    ppermute x15 -> x14, waiting for transfers between devices: 47.1 us -> 45.4 us  [ring_shift(): return lax.ppermute(value, ('rep', 'section', 'exp'), pairs)]
    ppermute x15 -> x14, starting transfers between devices: 20.4 us -> 19.2 us  [ring_shift(): return lax.ppermute(value, ('rep', 'section', 'exp'), pairs)]
  transfers between devices with their start and end apart: 21 -> 20, of which waited for: 13 -> 13; matrix products, arithmetic and copies ran while one was open for 4% -> 4% of each run, Pallas kernels for 25% -> 25%
where the time goes in v20:
time: 113 us
  waiting for transfers between devices  51.9 us (46%)
  Pallas kernels  28.7 us (25%)
  starting transfers between devices  22.3 us (20%)
  other arithmetic  5.41 us (5%)
  local copies, waits for them, and re-layouts  3.97 us (4%)
    ppermute x14, waiting for transfers between devices, ring_shift(): return lax.ppermute(value, ('rep', 'section', 'exp'), pairs)  45.4 us
    pallas_call x3, Pallas kernels, expert_call(): pl.pallas_call(functools.partial(expert_kernel, count, experts, local_exp...  20.1 us
    ppermute x14, starting transfers between devices, ring_shift(): return lax.ppermute(value, ('rep', 'section', 'exp'), pairs)  19.2 us
    ppermute x6, waiting for transfers between devices, from_behind(): lax.ppermute(value, axis, [(i, (i + by) % peers) for i in range(peers)])  6.52 us
    pallas_call x1, Pallas kernels, weight_call(): pl.pallas_call(functools.partial(weight_kernel, len(kept), count), out_sh...  6.06 us
    convert_element_type x7, other arithmetic, add(): return (a.astype(F32) + b.astype(F32)).astype(BF16)  4.38 us
    unnamed x8, local copies, waits for them, and re-layouts  3.97 us
    ppermute x6, starting transfers between devices, from_behind(): lax.ppermute(value, axis, [(i, (i + by) % peers) for i in range(peers)])  3.12 us
  transfers between devices with their start and end apart: 20, of which 13 were waited for; matrix products, arithmetic and copies ran while one was open for 4% of the time, Pallas kernels for 25%

profile of v20, /device:TPU:0, one launch (start us, length us, event | category | flops | bytes accessed | tf_op | source)
XLA Modules:
  0.0 113.2 jit_solution(12899526669699314074)
XLA Ops:
  0.6 0.5 collective-permute-start.3
  1.2 0.1 collective-permute-start.4
  1.2 0.4 collective-permute-start.5
  1.7 2.2 %pack_rows.1.refs_0_ = bf16[64,4224]{1,0:T(8,128)(2,1)} custom-call(bf16[64,2048]{1,0:T(8,128)(2,1)} %bitcast.45, s32[16,64]{1,0:T(8,128)} %bitcast.47, s32[8,64]{1,0:T(8,128)} %bitcast.48, f32[8,64]{1,0:T(8,128)} %bitcast.49, bf16[64,2048]{1,0:T(8,128)(2,1)} %bitcast.46), custom_call_target="tpu_custom_call" | custom-call | tf_op jit(solution)/shard_map/pack_rows/pallas_call | solution.py:275
  3.9 2.7 %collective-permute-start = (bf16[64,4224]{1,0:T(8,128)(2,1)}, bf16[64,4224]{1,0:T(8,128)(2,1)S(1)}, u32[]{:S(2)}, u32[]{:S(2)}) collective-permute-start(bf16[64,4224]{1,0:T(8,128)(2,1)} %pack_rows.1.refs_0_), channel_id=1, source_target_pairs={{0,2},{2,4},{4,6},{6,7},{7,5},{5,3},{3,1},{1,0},{8,10},{10,12},{12... | collective-permute-start | bytes 1622024 | tf_op jit(solution)/shard_map/ppermute | solution.py:42
  6.5 0.0 copy-start.1
  6.5 1.4 %copy-done.1 = bf16[1,2,192,2048]{3,2,1,0:T(8,128)(2,1)S(1)} copy-done((bf16[1,2,192,2048]{3,2,1,0:T(8,128)(2,1)S(1)}, bf16[1,2,192,2048]{3,2,1,0:T(8,128)(2,1)}, u32[]{:S(2)}) %copy-start.1) | copy-done | bytes 1572888
  7.9 0.0 copy-start.2
  7.9 0.0 copy-start.3
  7.9 0.1 load_weights.2.refs_4_.refs_2_
  8.1 1.3 %copy-done.2 = bf16[1,2,192,2048]{3,2,1,0:T(8,128)(2,1)S(1)} copy-done((bf16[1,2,192,2048]{3,2,1,0:T(8,128)(2,1)S(1)}, bf16[1,2,192,2048]{3,2,1,0:T(8,128)(2,1)}, u32[]{:S(2)}) %copy-start.2) | copy-done | bytes 1572888
  9.3 0.5 copy-done.3
  9.8 0.0 copy-start
  9.8 0.2 load_weights.3
  10.1 0.8 copy-done
  10.9 0.0 collective-permute-start.1
  10.9 5.0 %collective-permute-done.refs_1_ = bf16[64,4224]{1,0:T(8,128)(2,1)S(1)} collective-permute-done((bf16[64,4224]{1,0:T(8,128)(2,1)}, bf16[64,4224]{1,0:T(8,128)(2,1)S(1)}, u32[]{:S(2)}, u32[]{:S(2)}) %collective-permute-start) | collective-permute-done | bytes 540704 | tf_op jit(solution)/shard_map/ppermute | solution.py:42
  15.8 2.4 %collective-permute-start.2 = (bf16[64,4224]{1,0:T(8,128)(2,1)S(1)}, bf16[64,4224]{1,0:T(8,128)(2,1)S(1)}, u32[]{:S(2)}, u32[]{:S(2)}) collective-permute-start(bf16[64,4224]{1,0:T(8,128)(2,1)S(1)} %collective-permute-done.refs_1_), channel_id=1, source_target_pairs={{0,2},{2,4},{4,6},{6,7},{7,5},{5,3},{3,1},{1,0},{8,10},{10,12},{12... | collective-permute-start | bytes 1622024 | tf_op jit(solution)/shard_map/ppermute | solution.py:42
  18.2 5.4 %collective-permute-done.1.refs_2_ = bf16[64,4224]{1,0:T(8,128)(2,1)S(1)} collective-permute-done((bf16[64,4224]{1,0:T(8,128)(2,1)S(1)}, bf16[64,4224]{1,0:T(8,128)(2,1)S(1)}, u32[]{:S(2)}, u32[]{:S(2)}) %collective-permute-start.1) | collective-permute-done | bytes 540704 | tf_op jit(solution)/shard_map/ppermute | solution.py:42
  23.6 0.0 collective-permute-start.8
  23.6 4.6 %collective-permute-done.2.refs_3_ = bf16[64,4224]{1,0:T(8,128)(2,1)S(1)} collective-permute-done((bf16[64,4224]{1,0:T(8,128)(2,1)S(1)}, bf16[64,4224]{1,0:T(8,128)(2,1)S(1)}, u32[]{:S(2)}, u32[]{:S(2)}) %collective-permute-start.2) | collective-permute-done | bytes 540704 | tf_op jit(solution)/shard_map/ppermute | solution.py:42
  28.2 2.5 %collective-permute-start.6 = (bf16[64,4224]{1,0:T(8,128)(2,1)S(1)}, bf16[64,4224]{1,0:T(8,128)(2,1)S(1)}, u32[]{:S(2)}, u32[]{:S(2)}) collective-permute-start(bf16[64,4224]{1,0:T(8,128)(2,1)S(1)} %collective-permute-done.2.refs_3_), channel_id=1, source_target_pairs={{0,2},{2,4},{4,6},{6,7},{7,5},{5,3},{3,1},{1,0},{8,10},{10,12},{12... | collective-permute-start | bytes 1622024 | tf_op jit(solution)/shard_map/ppermute | solution.py:42
  30.7 6.5 %collective-permute-done.8.refs_0_.refs_4_ = bf16[64,4224]{1,0:T(8,128)(2,1)S(1)} collective-permute-done((bf16[64,4224]{1,0:T(8,128)(2,1)S(1)}, bf16[64,4224]{1,0:T(8,128)(2,1)S(1)}, u32[]{:S(2)}, u32[]{:S(2)}) %collective-permute-start.8) | collective-permute-done | bytes 540704 | tf_op jit(solution)/shard_map/ppermute | solution.py:42
  37.1 0.0 collective-permute-start.9
  37.1 0.0 collective-permute-done.3.refs_7_.refs_5_
  37.1 0.0 collective-permute-done.4.refs_8_.refs_6_
  37.1 0.0 collective-permute-done.5.refs_9_.refs_7_
  37.1 7.7 %expert_rows.3 = (bf16[64,4096]{1,0:T(8,128)(2,1)S(1)}, bf16[64,4096]{1,0:T(8,128)(2,1)S(1)}, bf16[64,4096]{1,0:T(8,128)(2,1)S(1)}, bf16[64,4096]{1,0:T(8,128)(2...) custom-call(bf16[64,4224]{1,0:T(8,128)(2,1)S(1)} %copy-done, ...), custom_call_target="tpu_custom_call" | custom-call | flops 4831838208 | bytes 13631488 | tf_op jit(solution)/shard_map/expert_rows/pallas_call | solution.py:191
  44.9 0.0 collective-permute-done.6.refs_0_.refs_6_
  44.9 2.1 %collective-permute-start.7 = (bf16[64,4224]{1,0:T(8,128)(2,1)S(1)}, bf16[64,4224]{1,0:T(8,128)(2,1)S(1)}, u32[]{:S(2)}, u32[]{:S(2)}) collective-permute-start(bf16[64,4224]{1,0:T(8,128)(2,1)S(1)} %collective-permute-done.6.refs_0_.refs_6_), channel_id=1, source_target_pairs={{0,2},{2,4},{4,6},{6,7},{7,5},{5,3},{3,1},{1,0},{8,10},{10,12},{12... | collective-permute-start | bytes 1622024 | tf_op jit(solution)/shard_map/ppermute | solution.py:42
  46.9 2.3 %collective-permute-done.9.refs_1_.refs_5_ = bf16[64,4224]{1,0:T(8,128)(2,1)S(1)} collective-permute-done((bf16[64,4224]{1,0:T(8,128)(2,1)S(1)}, bf16[64,4224]{1,0:T(8,128)(2,1)S(1)}, u32[]{:S(2)}, u32[]{:S(2)}) %collective-permute-start.9) | collective-permute-done | bytes 540704 | tf_op jit(solution)/shard_map/ppermute | solution.py:42
  49.2 6.2 %expert_rows.4 = (bf16[64,4096]{1,0:T(8,128)(2,1)S(1)}, bf16[64,4096]{1,0:T(8,128)(2,1)S(1)}, bf16[768,128]{1,0:T(8,128)(2,1)S(1)}, bf16[768,128]{1,0:T(8,128)(2,1)S(1)}, bf16[768,128]{1,0:T(8,128)(2,1)S(1)}) custom-call(bf16[64,4224]{1,0:T(8,128)(2,1)S(1)} %collective-permute-done.8.refs_0_.refs_4_, ...), custom_call_target="tpu_custom_call" | custom-call | flops 2415919104 | bytes 11534336 | tf_op jit(solution)/shard_map/expert_rows/pallas_call | solution.py:191
  55.4 2.0 %collective-permute-start.12 = (bf16[64,4096]{1,0:T(8,128)(2,1)S(1)}, bf16[64,4096]{1,0:T(8,128)(2,1)S(1)}, u32[]{:S(2)}, u32[]{:S(2)}) collective-permute-start(bf16[64,4096]{1,0:T(8,128)(2,1)S(1)} %get-tuple-element.91), channel_id=1, source_target_pairs={{0,2},{2,4},{4,6},{6,7},{7,5},{5,3},{3,1},{1,0},{8,10},{10,12},{12... | collective-permute-start | bytes 1572872 | tf_op jit(solution)/shard_map/ppermute | solution.py:42
  57.4 0.0 collective-permute-done.7.refs_1_.refs_7_
  57.4 6.2 %expert_rows.5 = (bf16[64,4096]{1,0:T(8,128)(2,1)S(1)}, bf16[64,4096]{1,0:T(8,128)(2,1)S(1)}, bf16[768,128]{1,0:T(8,128)(2,1)S(1)}, bf16[768,128]{1,0:T(8,128)(2,1)S(1)}, bf16[768,128]{1,0:T(8,128)(2,1)S(1)}) custom-call(bf16[64,4224]{1,0:T(8,128)(2,1)S(1)} %collective-permute-done.6.refs_0_.refs_6_, ...), custom_call_target="tpu_custom_call" | custom-call | flops 2415919104 | bytes 11534336 | tf_op jit(solution)/shard_map/expert_rows/pallas_call | solution.py:191
  63.6 0.1 add_convert_fusion.7
  63.7 1.6 %collective-permute-start.14 = (bf16[64,2048]{1,0:T(8,128)(2,1)S(1)}, bf16[64,2048]{1,0:T(8,128)(2,1)S(1)}, u32[]{:S(2)}, u32[]{:S(2)}) collective-permute-start(bf16[64,2048]{1,0:T(8,128)(2,1)S(1)} %get-tuple-element.128), channel_id=1, source_target_pairs={{0,8},{8,0},{1,9},{9,1},{2,10},{10,2},{3,11},{11,3},{4,12},{12,4},... | collective-permute-start | bytes 786440 | tf_op jit(solution)/shard_map/ppermute | solution.py:47
  65.3 0.5 collective-permute-start.10
  65.8 0.1 collective-permute-start.11
  66.0 0.4 collective-permute-done.12
  66.3 0.1 add_convert_fusion.3
  66.5 2.2 %collective-permute-start.15 = (bf16[64,4096]{1,0:T(8,128)(2,1)S(1)}, bf16[64,4096]{1,0:T(8,128)(2,1)S(1)}, u32[]{:S(2)}, u32[]{:S(2)}) collective-permute-start(bf16[64,4096]{1,0:T(8,128)(2,1)S(1)} %add_convert_fusion.3), channel_id=1, source_target_pairs={{0,2},{2,4},{4,6},{6,7},{7,5},{5,3},{3,1},{1,0},{8,10},{10,12},{12... | collective-permute-start | bytes 1572872 | tf_op jit(solution)/shard_map/ppermute | solution.py:42
  68.6 6.1 %weight_grads.1 = (bf16[384,2048]{1,0:T(8,128)(2,1)S(1)}, bf16[384,2048]{1,0:T(8,128)(2,1)S(1)}, bf16[384,2048]{1,0:T(8,128)(2,1)S(1)}, bf16[3,384,2048]{2,1,0:T(8,128)(2,1)S(1)}) custom-call(bf16[64,4224]{1,0:T(8,128)(2,1)S(1)} %copy-done, bf16[64,4224]{1,0:T(8,128)(2,1)S(1)} %collective-permute-done.refs_1_, ...), custom_call_target="tpu_custom_call" | custom-call | flops 4831838208 | bytes 13631488 | tf_op jit(solution)/shard_map/weight_grads/pallas_call | solution.py:242
  74.7 1.1 collective-permute-done.11
  75.8 0.1 add_convert_fusion.4
  75.9 0.4 collective-permute-start.13
  76.2 2.2 %collective-permute-done.15 = bf16[64,4096]{1,0:T(8,128)(2,1)S(1)} collective-permute-done((bf16[64,4096]{1,0:T(8,128)(2,1)S(1)}, bf16[64,4096]{1,0:T(8,128)(2,1)S(1)}, u32[]{:S(2)}, u32[]{:S(2)}) %collective-permute-start.15) | collective-permute-done | bytes 524320 | tf_op jit(solution)/shard_map/ppermute | solution.py:42
  78.4 0.1 add_convert_fusion.2
  78.6 3.1 %collective-permute-start.17 = (bf16[64,4096]{1,0:T(8,128)(2,1)S(1)}, bf16[64,4096]{1,0:T(8,128)(2,1)S(1)}, u32[]{:S(2)}, u32[]{:S(2)}) collective-permute-start(bf16[64,4096]{1,0:T(8,128)(2,1)S(1)} %add_convert_fusion.2), channel_id=1, source_target_pairs={{0,10},{2,12},{4,14},{6,15},{7,13},{5,11},{3,9},{1,8},{8,2},{10,4}... | collective-permute-start | bytes 1572872 | tf_op jit(solution)/shard_map/ppermute | solution.py:42
  81.7 0.0 collective-permute-done.14
  81.7 0.0 collective-permute-done.10
  81.7 5.5 %collective-permute-done.13 = bf16[64,4096]{1,0:T(8,128)(2,1)S(1)} collective-permute-done((bf16[64,4096]{1,0:T(8,128)(2,1)S(1)}, bf16[64,4096]{1,0:T(8,128)(2,1)S(1)}, u32[]{:S(2)}, u32[]{:S(2)}) %collective-permute-start.13) | collective-permute-done | bytes 524320 | tf_op jit(solution)/shard_map/ppermute | solution.py:42
  87.2 0.1 add_convert_fusion.1
  87.3 0.6 collective-permute-start.16
  88.0 4.7 %collective-permute-done.17 = bf16[64,4096]{1,0:T(8,128)(2,1)S(1)} collective-permute-done((bf16[64,4096]{1,0:T(8,128)(2,1)S(1)}, bf16[64,4096]{1,0:T(8,128)(2,1)S(1)}, u32[]{:S(2)}, u32[]{:S(2)}) %collective-permute-start.17) | collective-permute-done | bytes 524320 | tf_op jit(solution)/shard_map/ppermute | solution.py:42
  92.7 4.1 %collective-permute-done.16 = bf16[64,4096]{1,0:T(8,128)(2,1)S(1)} collective-permute-done((bf16[64,4096]{1,0:T(8,128)(2,1)S(1)}, bf16[64,4096]{1,0:T(8,128)(2,1)S(1)}, u32[]{:S(2)}, u32[]{:S(2)}) %collective-permute-start.16) | collective-permute-done | bytes 524320 | tf_op jit(solution)/shard_map/ppermute | solution.py:42
  96.7 0.0 collective-permute-start.19
  96.7 0.1 add_convert_fusion
  96.9 1.3 %collective-permute-start.18 = (bf16[64,4096]{1,0:T(8,128)(2,1)S(1)}, bf16[64,4096]{1,0:T(8,128)(2,1)S(1)}, u32[]{:S(2)}, u32[]{:S(2)}) collective-permute-start(bf16[64,4096]{1,0:T(8,128)(2,1)S(1)} %add_convert_fusion), channel_id=1, source_target_pairs={{0,9},{2,8},{4,10},{6,12},{7,14},{5,15},{3,13},{1,11},{8,1},{10,0}... | collective-permute-start | bytes 1572872 | tf_op jit(solution)/shard_map/ppermute | solution.py:42
  98.1 6.5 %collective-permute-done.19 = bf16[3,384,2048]{2,1,0:T(8,128)(2,1)S(1)} collective-permute-done((bf16[3,384,2048]{2,1,0:T(8,128)(2,1)S(1)}, bf16[3,384,2048]{2,1,0:T(8,128)(2,1)S(1)}, u32[]{:S(2)}, u32[]{:S(2)}) %collective-permute-start.19) | collective-permute-done | bytes 4718624 | tf_op jit(solution)/shard_map/ppermute | solution.py:47
  104.6 3.6 %fusion = (bf16[384,2048]{1,0:T(8,128)(2,1)}, bf16[384,2048]{1,0:T(8,128)(2,1)}, bf16[384,2048]{1,0:T(8,128)(2,1)}) fusion(bf16[384,2048]{1,0:T(8,128)(2,1)S(1)} %get-tuple-element.120, bf16[3,384,2048]{2,1,0:T(8,128)(2,1)S(1)} %collective-permute-done.19, bf16[384,2048]{1,0:T(8,128)(2,1)S(1)} %get-tuple-element.119, bf16[384,2048]{1,0:T(8,128)(2,1)S(1)} %get-tuple-element.117), kind=kLoop, calls=%fused_computation.1 | loop fusion | flops 9437184 | bytes 14155776 | tf_op jit(solution)/shard_map/convert_element_type | solution.py:261
  108.3 3.9 %collective-permute-done.18 = bf16[64,4096]{1,0:T(8,128)(2,1)S(1)} collective-permute-done((bf16[64,4096]{1,0:T(8,128)(2,1)S(1)}, bf16[64,4096]{1,0:T(8,128)(2,1)S(1)}, u32[]{:S(2)}, u32[]{:S(2)}) %collective-permute-start.18) | collective-permute-done | bytes 524320 | tf_op jit(solution)/shard_map/ppermute | solution.py:42
  112.1 1.0 fusion.4
Async XLA Ops:
  0.6 36.5 %collective-permute-start.3 = (bf16[384,2048]{1,0:T(8,128)(2,1)}, bf16[384,2048]{1,0:T(8,128)(2,1)S(1)}, u32[]{:S(2)}, u32[]{:S(2)}) collective-permute-start(bf16[384,2048]{1,0:T(8,128)(2,1)} %bitcast.36), channel_id=1, source_target_pairs={{0,16},{16,0},{1,17},{17,1},{2,18},{18,2},{3,19},{19,3},{4,20},{20... | collective-permute-start | bytes 4718600 | tf_op jit(solution)/shard_map/ppermute | solution.py:47
  1.2 36.0 %collective-permute-start.4 = (bf16[384,2048]{1,0:T(8,128)(2,1)}, bf16[384,2048]{1,0:T(8,128)(2,1)S(1)}, u32[]{:S(2)}, u32[]{:S(2)}) collective-permute-start(bf16[384,2048]{1,0:T(8,128)(2,1)} %bitcast.38), channel_id=1, source_target_pairs={{0,16},{16,0},{1,17},{17,1},{2,18},{18,2},{3,19},{19,3},{4,20},{20... | collective-permute-start | bytes 4718600 | tf_op jit(solution)/shard_map/ppermute | solution.py:47
  1.2 35.9 %collective-permute-start.5 = (bf16[384,2048]{1,0:T(8,128)(2,1)}, bf16[384,2048]{1,0:T(8,128)(2,1)}, u32[]{:S(2)}, u32[]{:S(2)}) collective-permute-start(bf16[384,2048]{1,0:T(8,128)(2,1)} %bitcast.40), channel_id=1, source_target_pairs={{0,16},{16,0},{1,17},{17,1},{2,18},{18,2},{3,19},{19,3},{4,20},{20... | collective-permute-start | bytes 4718600 | tf_op jit(solution)/shard_map/ppermute | solution.py:47
  3.9 12.0 %collective-permute-start = (bf16[64,4224]{1,0:T(8,128)(2,1)}, bf16[64,4224]{1,0:T(8,128)(2,1)S(1)}, u32[]{:S(2)}, u32[]{:S(2)}) collective-permute-start(bf16[64,4224]{1,0:T(8,128)(2,1)} %pack_rows.1.refs_0_), channel_id=1, source_target_pairs={{0,2},{2,4},{4,6},{6,7},{7,5},{5,3},{3,1},{1,0},{8,10},{10,12},{12... | collective-permute-start | bytes 1622024 | tf_op jit(solution)/shard_map/ppermute | solution.py:42
  6.5 1.4 %copy-start.1 = (bf16[1,2,192,2048]{3,2,1,0:T(8,128)(2,1)S(1)}, bf16[1,2,192,2048]{3,2,1,0:T(8,128)(2,1)}, u32[]{:S(2)}) copy-start(bf16[1,2,192,2048]{3,2,1,0:T(8,128)(2,1)} %param.13) | copy-start | bytes 4718596
  7.9 1.4 %copy-start.2 = (bf16[1,2,192,2048]{3,2,1,0:T(8,128)(2,1)S(1)}, bf16[1,2,192,2048]{3,2,1,0:T(8,128)(2,1)}, u32[]{:S(2)}) copy-start(bf16[1,2,192,2048]{3,2,1,0:T(8,128)(2,1)} %param.14) | copy-start | bytes 4718596
  7.9 1.9 %copy-start.3 = (bf16[1,2,192,2048]{3,2,1,0:T(8,128)(2,1)S(1)}, bf16[1,2,192,2048]{3,2,1,0:T(8,128)(2,1)}, u32[]{:S(2)}) copy-start(bf16[1,2,192,2048]{3,2,1,0:T(8,128)(2,1)} %param.15) | copy-start | bytes 4718596
  9.8 1.0 copy-start
  10.9 12.7 %collective-permute-start.1 = (bf16[64,4224]{1,0:T(8,128)(2,1)S(1)}, bf16[64,4224]{1,0:T(8,128)(2,1)S(1)}, u32[]{:S(2)}, u32[]{:S(2)}) collective-permute-start(bf16[64,4224]{1,0:T(8,128)(2,1)S(1)} %copy-done), channel_id=1, source_target_pairs={{0,1},{2,0},{4,2},{6,4},{7,6},{5,7},{3,5},{1,3},{8,9},{10,8},{12,1... | collective-permute-start | bytes 1622024 | tf_op jit(solution)/shard_map/ppermute | solution.py:42
  15.8 12.3 %collective-permute-start.2 = (bf16[64,4224]{1,0:T(8,128)(2,1)S(1)}, bf16[64,4224]{1,0:T(8,128)(2,1)S(1)}, u32[]{:S(2)}, u32[]{:S(2)}) collective-permute-start(bf16[64,4224]{1,0:T(8,128)(2,1)S(1)} %collective-permute-done.refs_1_), channel_id=1, source_target_pairs={{0,2},{2,4},{4,6},{6,7},{7,5},{5,3},{3,1},{1,0},{8,10},{10,12},{12... | collective-permute-start | bytes 1622024 | tf_op jit(solution)/shard_map/ppermute | solution.py:42
  23.6 13.5 %collective-permute-start.8 = (bf16[64,4224]{1,0:T(8,128)(2,1)S(1)}, bf16[64,4224]{1,0:T(8,128)(2,1)S(1)}, u32[]{:S(2)}, u32[]{:S(2)}) collective-permute-start(bf16[64,4224]{1,0:T(8,128)(2,1)S(1)} %collective-permute-done.1.refs_2_), channel_id=1, source_target_pairs={{0,1},{2,0},{4,2},{6,4},{7,6},{5,7},{3,5},{1,3},{8,9},{10,8},{12,1... | collective-permute-start | bytes 1622024 | tf_op jit(solution)/shard_map/ppermute | solution.py:42
  28.2 16.7 %collective-permute-start.6 = (bf16[64,4224]{1,0:T(8,128)(2,1)S(1)}, bf16[64,4224]{1,0:T(8,128)(2,1)S(1)}, u32[]{:S(2)}, u32[]{:S(2)}) collective-permute-start(bf16[64,4224]{1,0:T(8,128)(2,1)S(1)} %collective-permute-done.2.refs_3_), channel_id=1, source_target_pairs={{0,2},{2,4},{4,6},{6,7},{7,5},{5,3},{3,1},{1,0},{8,10},{10,12},{12... | collective-permute-start | bytes 1622024 | tf_op jit(solution)/shard_map/ppermute | solution.py:42
  37.1 12.1 %collective-permute-start.9 = (bf16[64,4224]{1,0:T(8,128)(2,1)S(1)}, bf16[64,4224]{1,0:T(8,128)(2,1)S(1)}, u32[]{:S(2)}, u32[]{:S(2)}) collective-permute-start(bf16[64,4224]{1,0:T(8,128)(2,1)S(1)} %collective-permute-done.8.refs_0_.refs_4_), channel_id=1, source_target_pairs={{0,1},{2,0},{4,2},{6,4},{7,6},{5,7},{3,5},{1,3},{8,9},{10,8},{12,1... | collective-permute-start | bytes 1622024 | tf_op jit(solution)/shard_map/ppermute | solution.py:42
  44.9 12.5 %collective-permute-start.7 = (bf16[64,4224]{1,0:T(8,128)(2,1)S(1)}, bf16[64,4224]{1,0:T(8,128)(2,1)S(1)}, u32[]{:S(2)}, u32[]{:S(2)}) collective-permute-start(bf16[64,4224]{1,0:T(8,128)(2,1)S(1)} %collective-permute-done.6.refs_0_.refs_6_), channel_id=1, source_target_pairs={{0,2},{2,4},{4,6},{6,7},{7,5},{5,3},{3,1},{1,0},{8,10},{10,12},{12... | collective-permute-start | bytes 1622024 | tf_op jit(solution)/shard_map/ppermute | solution.py:42
  55.4 10.9 %collective-permute-start.12 = (bf16[64,4096]{1,0:T(8,128)(2,1)S(1)}, bf16[64,4096]{1,0:T(8,128)(2,1)S(1)}, u32[]{:S(2)}, u32[]{:S(2)}) collective-permute-start(bf16[64,4096]{1,0:T(8,128)(2,1)S(1)} %get-tuple-element.91), channel_id=1, source_target_pairs={{0,2},{2,4},{4,6},{6,7},{7,5},{5,3},{3,1},{1,0},{8,10},{10,12},{12... | collective-permute-start | bytes 1572872 | tf_op jit(solution)/shard_map/ppermute | solution.py:42
  63.7 17.9 %collective-permute-start.14 = (bf16[64,2048]{1,0:T(8,128)(2,1)S(1)}, bf16[64,2048]{1,0:T(8,128)(2,1)S(1)}, u32[]{:S(2)}, u32[]{:S(2)}) collective-permute-start(bf16[64,2048]{1,0:T(8,128)(2,1)S(1)} %get-tuple-element.128), channel_id=1, source_target_pairs={{0,8},{8,0},{1,9},{9,1},{2,10},{10,2},{3,11},{11,3},{4,12},{12,4},... | collective-permute-start | bytes 786440 | tf_op jit(solution)/shard_map/ppermute | solution.py:47
  65.3 16.3 %collective-permute-start.10 = (bf16[64,2048]{1,0:T(8,128)(2,1)S(1)}, bf16[64,2048]{1,0:T(8,128)(2,1)S(1)}, u32[]{:S(2)}, u32[]{:S(2)}) collective-permute-start(bf16[64,2048]{1,0:T(8,128)(2,1)S(1)} %get-tuple-element.129), channel_id=1, source_target_pairs={{0,8},{8,0},{1,9},{9,1},{2,10},{10,2},{3,11},{11,3},{4,12},{12,4},... | collective-permute-start | bytes 786440 | tf_op jit(solution)/shard_map/ppermute | solution.py:47
  65.8 9.9 %collective-permute-start.11 = (bf16[64,4096]{1,0:T(8,128)(2,1)S(1)}, bf16[64,4096]{1,0:T(8,128)(2,1)S(1)}, u32[]{:S(2)}, u32[]{:S(2)}) collective-permute-start(bf16[64,4096]{1,0:T(8,128)(2,1)S(1)} %get-tuple-element.90), channel_id=1, source_target_pairs={{0,1},{2,0},{4,2},{6,4},{7,6},{5,7},{3,5},{1,3},{8,9},{10,8},{12,1... | collective-permute-start | bytes 1572872 | tf_op jit(solution)/shard_map/ppermute | solution.py:42
  66.5 12.0 %collective-permute-start.15 = (bf16[64,4096]{1,0:T(8,128)(2,1)S(1)}, bf16[64,4096]{1,0:T(8,128)(2,1)S(1)}, u32[]{:S(2)}, u32[]{:S(2)}) collective-permute-start(bf16[64,4096]{1,0:T(8,128)(2,1)S(1)} %add_convert_fusion.3), channel_id=1, source_target_pairs={{0,2},{2,4},{4,6},{6,7},{7,5},{5,3},{3,1},{1,0},{8,10},{10,12},{12... | collective-permute-start | bytes 1572872 | tf_op jit(solution)/shard_map/ppermute | solution.py:42
  75.9 11.3 %collective-permute-start.13 = (bf16[64,4096]{1,0:T(8,128)(2,1)S(1)}, bf16[64,4096]{1,0:T(8,128)(2,1)S(1)}, u32[]{:S(2)}, u32[]{:S(2)}) collective-permute-start(bf16[64,4096]{1,0:T(8,128)(2,1)S(1)} %add_convert_fusion.4), channel_id=1, source_target_pairs={{0,1},{2,0},{4,2},{6,4},{7,6},{5,7},{3,5},{1,3},{8,9},{10,8},{12,1... | collective-permute-start | bytes 1572872 | tf_op jit(solution)/shard_map/ppermute | solution.py:42
  78.6 14.1 %collective-permute-start.17 = (bf16[64,4096]{1,0:T(8,128)(2,1)S(1)}, bf16[64,4096]{1,0:T(8,128)(2,1)S(1)}, u32[]{:S(2)}, u32[]{:S(2)}) collective-permute-start(bf16[64,4096]{1,0:T(8,128)(2,1)S(1)} %add_convert_fusion.2), channel_id=1, source_target_pairs={{0,10},{2,12},{4,14},{6,15},{7,13},{5,11},{3,9},{1,8},{8,2},{10,4}... | collective-permute-start | bytes 1572872 | tf_op jit(solution)/shard_map/ppermute | solution.py:42
  87.3 9.4 %collective-permute-start.16 = (bf16[64,4096]{1,0:T(8,128)(2,1)S(1)}, bf16[64,4096]{1,0:T(8,128)(2,1)S(1)}, u32[]{:S(2)}, u32[]{:S(2)}) collective-permute-start(bf16[64,4096]{1,0:T(8,128)(2,1)S(1)} %add_convert_fusion.1), channel_id=1, source_target_pairs={{0,1},{2,0},{4,2},{6,4},{7,6},{5,7},{3,5},{1,3},{8,9},{10,8},{12,1... | collective-permute-start | bytes 1572872 | tf_op jit(solution)/shard_map/ppermute | solution.py:42
  96.7 7.9 %collective-permute-start.19 = (bf16[3,384,2048]{2,1,0:T(8,128)(2,1)S(1)}, bf16[3,384,2048]{2,1,0:T(8,128)(2,1)S(1)}, u32[]{:S(2)}, u32[]{:S(2)}) collective-permute-start(bf16[3,384,2048]{2,1,0:T(8,128)(2,1)S(1)} %get-tuple-element.118), channel_id=1, source_target_pairs={{0,16},{16,0},{1,17},{17,1},{2,18},{18,2},{3,19},{19,3},{4,20},{20... | collective-permute-start | bytes 14155784 | tf_op jit(solution)/shard_map/ppermute | solution.py:47
  96.9 15.3 %collective-permute-start.18 = (bf16[64,4096]{1,0:T(8,128)(2,1)S(1)}, bf16[64,4096]{1,0:T(8,128)(2,1)S(1)}, u32[]{:S(2)}, u32[]{:S(2)}) collective-permute-start(bf16[64,4096]{1,0:T(8,128)(2,1)S(1)} %add_convert_fusion), channel_id=1, source_target_pairs={{0,9},{2,8},{4,10},{6,12},{7,14},{5,15},{3,13},{1,11},{8,1},{10,0}... | collective-permute-start | bytes 1572872 | tf_op jit(solution)/shard_map/ppermute | solution.py:42
